TPU v7x, 32 devices: a whole 2x2x4 slice. The times are simulated.
32 devices in a mesh: ctx: 32 (over z, y, x, core).
Axes of the slice: x: 2, y: 2, z: 4, core: 2. Of those that a mesh axis runs over, the one named last changes fastest.
Arguments:
- tiles: bfloat16 [8192, 768], P('ctx'), may hold values from -6 to 6
- w_qkv: bfloat16 [768, 2304], replicated, may hold values from -1 to 1
- w_out: bfloat16 [768, 768], replicated, may hold values from -0.21875 to 0.21875
- cotangent: bfloat16 [8192, 768], P('ctx'), may hold values from -6 to 6
- offsets: int32 [2, 12], replicated, may hold values from 0 to 31, as said below
- pad_count: int32 [1], replicated, may hold values from 0 to 127
Outputs:
- out_rows: bfloat16 [8192, 768], P('ctx')
- grad_tiles: bfloat16 [8192, 768], P('ctx')
- grad_wqkv: float32 [768, 2304], P('ctx')
- grad_wout: float32 [768, 768], P('ctx')
Inputs may be any that keep to these rules, and one draw needn't show every extreme that they name: offsets[0, h] is below 8; offsets[1, h] is below 32.
All inputs are finite; a program needn't handle non-finite values.
Results may differ from a plain program's by a relative error of at most 0.033.
Values may be sent and summed in bfloat16 or wider, within the bound.
No kernel may reach another device: no remote copies, remote signals or barrier semaphores. Data moves between devices by JAX's collectives and lax.ppermute only.
A program may use at most 128 MiB of HBM per device.

v0:
```python
import jax
import jax.numpy as jnp
from jax import lax
from jax.sharding import PartitionSpec as P

D = 768
HEADS = 12
HEAD_DIM = 64
GROUP = 8


scale_factor = 0.125
block_rows = 512


def from_partner(value, axis, apart):
    mask = 2**apart
    pairs = [(source, source ^ mask) for source in range(lax.axis_size(axis))]
    return lax.ppermute(value, axis, pairs)


def pick_rows(array_in, stride, offsets_row):
    row_count = array_in.shape[0]
    blocked = array_in.reshape((row_count // stride, stride) + array_in.shape[1:])
    chosen = jnp.arange(stride, dtype=jnp.int32)[:, None] == offsets_row[None, :]
    chosen = chosen.reshape((1, stride, offsets_row.shape[0]) + (1,) * (array_in.ndim - 2))
    return jnp.sum(jnp.where(chosen, blocked, jnp.zeros((), array_in.dtype)), axis=1)


def spread_rows(array_in, stride, offsets_row, fill):
    chosen = jnp.arange(stride, dtype=jnp.int32)[:, None] == offsets_row[None, :]
    chosen = chosen.reshape((1, stride, offsets_row.shape[0]) + (1,) * (array_in.ndim - 2))
    widened = jnp.where(chosen, array_in[:, None], jnp.asarray(fill, array_in.dtype))
    return widened.reshape((array_in.shape[0] * stride,) + array_in.shape[1:])


def masked_scores(queries, key_rows, key_valid):
    scores = (
        jnp.einsum("nhe,mhe->hnm", queries, key_rows, preferred_element_type=jnp.float32)
        * scale_factor
    )
    return jnp.where(key_valid[:, None, :], scores, -jnp.inf)


def level_forward(queries, key_rows, value_rows, key_valid):
    scores = masked_scores(queries, key_rows, key_valid)
    peak = jnp.max(scores, axis=-1, keepdims=True)
    log_total = peak[..., 0] + jnp.log(jnp.sum(jnp.exp(scores - peak), axis=-1))
    weights = jnp.exp(scores - log_total[..., None]).astype(jnp.bfloat16)
    mixed = jnp.einsum("hnm,mhe->nhe", weights, value_rows, preferred_element_type=jnp.float32)
    return (mixed, log_total.T)


def level_grads(
    queries,
    key_rows,
    value_rows,
    key_valid,
    log_total,
    grad_out,
    delta_rows,
    want_queries,
    want_keys,
):
    scores = masked_scores(queries, key_rows, key_valid)
    probs = jnp.exp(scores - log_total.T[:, :, None])
    grad_probs = jnp.einsum(
        "nhe,mhe->hnm", grad_out, value_rows, preferred_element_type=jnp.float32
    )
    grad_scores = (probs * (grad_probs - delta_rows.T[:, :, None])).astype(jnp.bfloat16)
    results = []
    if want_queries:
        results.append(
            scale_factor
            * jnp.einsum("hnm,mhe->nhe", grad_scores, key_rows, preferred_element_type=jnp.float32)
        )
    if want_keys:
        results.append(
            scale_factor
            * jnp.einsum("hnm,nhe->mhe", grad_scores, queries, preferred_element_type=jnp.float32)
        )
        results.append(
            jnp.einsum(
                "hnm,nhe->mhe",
                probs.astype(jnp.bfloat16),
                grad_out,
                preferred_element_type=jnp.float32,
            )
        )
    return tuple(results)


def forward_blocks(queries, key_rows, value_rows, key_valid):
    count = queries.shape[0]
    size = min(count, block_rows)
    return level_forward(queries, key_rows, value_rows, key_valid)


def grads_blocks(queries, key_rows, value_rows, key_valid, log_total, grad_out, delta_rows):
    count = queries.shape[0]
    size = min(count, block_rows)
    return level_grads(
        queries, key_rows, value_rows, key_valid, log_total, grad_out, delta_rows, True, True
    )


def per_device(tiles, w_qkv, w_out, cotangent, offsets, pad_count):
    row_count = tiles.shape[0]
    dev_count = lax.axis_size("ctx")
    own_index = lax.axis_index("ctx")
    shaped = (row_count, HEADS, HEAD_DIM)
    packed = jnp.dot(tiles, w_qkv, preferred_element_type=jnp.float32).astype(jnp.bfloat16)
    queries = packed[:, :D].reshape(shaped)
    key_all = packed[:, D : 2 * D].reshape(shaped)
    value_all = packed[:, 2 * D :].reshape(shaped)
    limit = row_count * dev_count - pad_count[0]
    base_pos = own_index * row_count + jnp.arange(row_count, dtype=jnp.int32)
    valid_near = jnp.broadcast_to((base_pos < limit)[None, :], (HEADS, row_count))
    mixed_near, lse_near = forward_blocks(queries, key_all, value_all, valid_near)
    offs_mid = offsets[0]
    mid_rows = row_count // GROUP
    query_mid = pick_rows(queries, GROUP, offs_mid)
    key_mid = pick_rows(key_all, GROUP, offs_mid)
    value_mid = pick_rows(value_all, GROUP, offs_mid)
    gathered = jnp.stack([key_mid.reshape(mid_rows, D), value_mid.reshape(mid_rows, D)])
    bit_total = GROUP.bit_length() - 1
    for bit_index in range(bit_total):
        partner = from_partner(gathered, "ctx", bit_index)
        upper = own_index // 2**bit_index % 2 == 1
        gathered = jnp.where(
            upper,
            jnp.concatenate([partner, gathered], axis=1),
            jnp.concatenate([gathered, partner], axis=1),
        )
    keys_group = gathered[0].reshape(shaped)
    values_group = gathered[1].reshape(shaped)
    group_start = own_index // GROUP * GROUP * row_count
    mid_pos = (
        group_start + jnp.arange(row_count, dtype=jnp.int32)[:, None] * GROUP + offs_mid[None, :]
    )
    valid_mid = (mid_pos < limit).T
    mixed_mid, lse_mid = level_forward(query_mid, keys_group, values_group, valid_mid)
    offs_far = offsets[1]
    far_rows = row_count // dev_count
    query_far = pick_rows(queries, dev_count, offs_far)
    key_far = pick_rows(key_all, dev_count, offs_far)
    value_far = pick_rows(value_all, dev_count, offs_far)
    far_all = lax.all_gather(
        jnp.stack([key_far.reshape(far_rows, D), value_far.reshape(far_rows, D)]),
        "ctx",
        axis=1,
        tiled=True,
    )
    keys_far_all = far_all[0].reshape(shaped)
    values_far_all = far_all[1].reshape(shaped)
    far_pos = jnp.arange(row_count, dtype=jnp.int32)[:, None] * dev_count + offs_far[None, :]
    valid_far = (far_pos < limit).T
    mixed_far, lse_far = level_forward(query_far, keys_far_all, values_far_all, valid_far)
    lse_mid_all = spread_rows(lse_mid, GROUP, offs_mid, -jnp.inf)
    lse_far_all = spread_rows(lse_far, dev_count, offs_far, -jnp.inf)
    log_total = jnp.logaddexp(jnp.logaddexp(lse_near, lse_mid_all), lse_far_all)
    combined = jnp.exp(lse_near - log_total)[..., None] * mixed_near
    combined = combined + jnp.exp(lse_mid_all - log_total)[..., None] * spread_rows(
        mixed_mid, GROUP, offs_mid, 0.0
    )
    combined = combined + jnp.exp(lse_far_all - log_total)[..., None] * spread_rows(
        mixed_far, dev_count, offs_far, 0.0
    )
    attn = combined.astype(jnp.bfloat16).reshape(row_count, D)
    out_rows = (
        tiles.astype(jnp.float32) + jnp.dot(attn, w_out, preferred_element_type=jnp.float32)
    ).astype(jnp.bfloat16)
    grad_attn = jnp.dot(cotangent, w_out.T, preferred_element_type=jnp.float32).astype(jnp.bfloat16)
    grad_wout_part = lax.dot_general(
        attn, cotangent, (((0,), (0,)), ((), ())), preferred_element_type=jnp.float32
    )
    grad_heads = grad_attn.reshape(shaped)
    delta_rows = jnp.sum(
        grad_heads.astype(jnp.float32) * attn.reshape(shaped).astype(jnp.float32), axis=-1
    )
    grad_query_near, grad_key_near, grad_value_near = grads_blocks(
        queries, key_all, value_all, valid_near, log_total, grad_heads, delta_rows
    )
    lse_mid_rows = pick_rows(log_total, GROUP, offs_mid)
    grad_mid_rows = pick_rows(grad_heads, GROUP, offs_mid)
    delta_mid_rows = pick_rows(delta_rows, GROUP, offs_mid)
    grad_query_mid, grad_key_group, grad_value_group = level_grads(
        query_mid,
        keys_group,
        values_group,
        valid_mid,
        lse_mid_rows,
        grad_mid_rows,
        delta_mid_rows,
        True,
        True,
    )
    summed = jnp.stack(
        [grad_key_group.reshape(row_count, D), grad_value_group.reshape(row_count, D)]
    )
    for bit_index in reversed(range(bit_total)):
        half = summed.shape[1] // 2
        lower = summed[:, :half]
        higher = summed[:, half:]
        upper = own_index // 2**bit_index % 2 == 1
        outgoing = jnp.where(upper, lower, higher)
        summed = jnp.where(upper, higher, lower) + from_partner(outgoing, "ctx", bit_index)
    grad_key_mid = summed[0].reshape(mid_rows, HEADS, HEAD_DIM)
    grad_value_mid = summed[1].reshape(mid_rows, HEADS, HEAD_DIM)
    lse_far_rows = pick_rows(log_total, dev_count, offs_far)
    grad_far_rows = pick_rows(grad_heads, dev_count, offs_far)
    delta_far_rows = pick_rows(delta_rows, dev_count, offs_far)
    row_block = jnp.stack(
        [query_far.reshape(far_rows, D), grad_far_rows.reshape(far_rows, D)]
    ).astype(jnp.float32)
    stat_block = jnp.stack([lse_far_rows, delta_far_rows])
    rows_all, stats_all = (
        lax.all_gather(row_block, "ctx", axis=1, tiled=True),
        lax.all_gather(stat_block, "ctx", axis=1, tiled=True),
    )
    query_all = rows_all[0].astype(jnp.bfloat16).reshape(shaped)
    grad_all = rows_all[1].astype(jnp.bfloat16).reshape(shaped)
    (grad_query_far,) = level_grads(
        query_far,
        keys_far_all,
        values_far_all,
        valid_far,
        lse_far_rows,
        grad_far_rows,
        delta_far_rows,
        True,
        False,
    )
    own_pos = (own_index * far_rows + jnp.arange(far_rows, dtype=jnp.int32))[
        :, None
    ] * dev_count + offs_far[None, :]
    grad_key_far, grad_value_far = level_grads(
        query_all,
        key_far,
        value_far,
        (own_pos < limit).T,
        stats_all[0],
        grad_all,
        stats_all[1],
        False,
        True,
    )
    grad_query = (
        grad_query_near
        + spread_rows(grad_query_mid, GROUP, offs_mid, 0.0)
        + spread_rows(grad_query_far, dev_count, offs_far, 0.0)
    )
    grad_key = (
        grad_key_near
        + spread_rows(grad_key_mid, GROUP, offs_mid, 0.0)
        + spread_rows(grad_key_far, dev_count, offs_far, 0.0)
    )
    grad_value = (
        grad_value_near
        + spread_rows(grad_value_mid, GROUP, offs_mid, 0.0)
        + spread_rows(grad_value_far, dev_count, offs_far, 0.0)
    )
    grad_packed = jnp.concatenate(
        [
            grad_query.reshape(row_count, D),
            grad_key.reshape(row_count, D),
            grad_value.reshape(row_count, D),
        ],
        axis=1,
    ).astype(jnp.bfloat16)
    grad_tiles = jnp.dot(grad_packed, w_qkv.T, preferred_element_type=jnp.float32).astype(
        jnp.bfloat16
    )
    grad_wqkv_part = lax.dot_general(
        tiles, grad_packed, (((0,), (0,)), ((), ())), preferred_element_type=jnp.float32
    )
    grad_wqkv, grad_wout = (
        lax.psum_scatter(grad_wqkv_part, "ctx", scatter_dimension=0, tiled=True),
        lax.psum_scatter(grad_wout_part, "ctx", scatter_dimension=0, tiled=True),
    )
    return (out_rows, grad_tiles, grad_wqkv, grad_wout)


def solution(mesh):
    return jax.shard_map(
        per_device,
        mesh=mesh,
        in_specs=(P("ctx", None), P(), P(), P("ctx", None), P(), P()),
        out_specs=(P("ctx", None), P("ctx", None), P("ctx", None), P("ctx", None)),
        check_vma=False,
    )
```

profile of v0, /device:TPU:0, one launch (start us, length us, event | category | flops | bytes accessed | tf_op | source)
XLA Modules:
  0.0 557.5 jit_solution(5915493366938448926)
XLA Ops:
  8.1 2.8 convolution_convert_fusion.2
  10.9 2.4 reshape_reshape.30
  13.3 2.1 convolution_convert_fusion
  16.5 2.5 reshape_reshape.25
  19.0 2.4 reshape_reshape.26
  21.4 2.4 reshape_reshape.24
  23.8 4.6 select_reduce_fusion.1
  35.7 2.4 reshape_reshape.31
  41.9 2.5 reshape_reshape.28
  44.4 2.4 reshape_reshape.29
  46.9 2.4 reshape_reshape.27
  50.6 4.1 select_reduce_fusion
  60.6 45.0 %all_gather.10 = bf16[2,256,768]{2,1,0:T(8,128)(2,1)S(1)} all-gather(bf16[2,8,768]{2,1,0:T(8,128)(2,1)S(1)} %maximum_convert_fusion), channel_id=1, replica_groups=mesh['ctx'=32] {'ctx'}, dimensions={1}, use_global_device_ids=true | all-gather | bytes 811008 | tf_op jit(solution)/shard_map/all_gather | solution.py:218
  106.6 39.1 %all_gather.9 = bf16[2,256,768]{2,1,0:T(8,128)(2,1)S(1)} all-gather(bf16[2,8,768]{2,1,0:T(8,128)(2,1)S(1)} %pad_maximum_fusion.4), channel_id=1, replica_groups=mesh['ctx'=32] {'ctx'}, dimensions={1}, use_global_device_ids=true | all-gather | bytes 811008 | tf_op jit(solution)/shard_map/all_gather | solution.py:148
  151.3 3.5 fusion.85
  181.5 2.0 broadcast_in_dim.374
  183.6 2.8 copy.156
  189.1 2.9 exponential_reduce_fusion
  192.0 6.8 %collective-permute-done.2 = bf16[2,128,768]{2,1,0:T(8,128)(2,1)S(1)} collective-permute-done((bf16[2,128,768]{2,1,0:T(8,128)(2,1)S(1)}, bf16[2,128,768]{2,1,0:T(8,128)(2,1)S(1)}, u32[]{:S(2)}, u32[]{:S(2)}) %collective-permute-start.2) | collective-permute-done | bytes 393248 | tf_op jit(solution)/shard_map/ppermute | solution.py:19
  215.5 2.8 copy.154
  218.2 4.7 multiply_reduce_fusion
  232.2 2.3 fusion.52
  235.4 2.3 copy.168
  238.4 37.4 %all_gather.11 = f32[2,256,12]{2,1,0:T(8,128)S(1)} all-gather(f32[2,8,12]{2,1,0:T(8,128)S(1)} %pad_maximum_fusion.5), channel_id=1, replica_groups=mesh['ctx'=32] {'ctx'}, dimensions={1}, use_global_device_ids=true | all-gather | bytes 25344 | tf_op jit(solution)/shard_map/all_gather | solution.py:219
  279.7 2.2 convolution_multiply_fusion.2
  281.9 2.3 copy.167
  284.2 2.3 broadcast_select_fusion
  286.5 2.1 fusion.49
  290.5 2.1 fusion.46
  297.1 9.6 %collective-permute-done.3 = f32[2,128,768]{2,1,0:T(8,128)} collective-permute-done((f32[2,128,768]{2,1,0:T(8,128)}, f32[2,128,768]{2,1,0:T(8,128)}, u32[]{:S(2)}, u32[]{:S(2)}) %collective-permute-start.3) | collective-permute-done | bytes 786464 | tf_op jit(solution)/shard_map/ppermute | solution.py:19
  312.5 2.8 copy.161
  315.3 2.0 broadcast_in_dim.392
  317.3 2.7 copy.183
  320.1 2.0 broadcast_in_dim.387
  322.1 2.7 copy.179
  324.9 2.0 broadcast_in_dim.380
  326.9 2.8 copy.163
  330.0 3.1 multiply_convert_fusion
  344.6 2.9 copy.182
  347.5 2.2 broadcast_bitcast_fusion.1
  349.7 2.8 copy.170
  352.6 2.8 fusion.30
  355.7 2.3 fusion.27
  358.7 4.0 convolution_bitcast_fusion
  362.7 8.0 %copy.190 = f32[768,2304]{1,0:T(8,128)} copy(f32[768,2304]{0,1:T(8,128)} %convolution_bitcast_fusion) | data formatting | bytes 14155776
  370.8 2.8 fusion.25
  375.6 49.7 %reduce-scatter.5.cloned.1.call-done = f32[24,768]{1,0:T(8,128)} async-done(((f32[768,768]{1,0:T(8,128)}), f32[24,768]{1,0:T(8,128)}) %reduce-scatter.5.cloned.1.call-update) | async-done | bytes 73744 | tf_op jit(solution)/shard_map/reduce_scatter | solution.py:279
  425.2 125.5 %reduce-scatter.7.cloned.1.call-done = f32[24,2304]{1,0:T(8,128)} async-done(((f32[768,2304]{1,0:T(8,128)}), f32[24,2304]{1,0:T(8,128)}) %reduce-scatter.7.cloned.1.call-update) | async-done | bytes 221200
  (182 shorter events, 113.8 us)
Async XLA Ops:
  7.2 6.2 %copy-start = (bf16[768,2304]{1,0:T(8,128)(2,1)S(1)}, bf16[768,2304]{1,0:T(8,128)(2,1)}, u32[]{:S(2)}) copy-start(bf16[768,2304]{1,0:T(8,128)(2,1)} %param.7) | copy-start | bytes 10616836
  7.2 418.0 %reduce-scatter.5.cloned.1.call-start = ((), (), s32[]{:S(2)}) async-start(), calls=%async_computation.2 | async-start | bytes 2433024 | tf_op jit(solution)/shard_map/reduce_scatter | solution.py:279
  8.1 5.3 copy-start.36
  8.1 140.5 %copy-start.34 = (s32[12]{0:T(128)}, s32[12]{0:T(128)S(1)}, u32[]{:S(2)}) copy-start(s32[12]{0:T(128)S(1)} %get-tuple-element.55) | copy-start | bytes 148
  8.1 15.8 %copy-start.35 = (pred[8,12]{1,0:T(8,128)(4,1)}, pred[8,12]{1,0:T(8,128)(4,1)S(1)}, u32[]{:S(2)}) copy-start(pred[8,12]{1,0:T(8,128)(4,1)S(1)} %iota_compare_fusion.1) | copy-start | bytes 292
  34.6 122.8 %collective-permute-start = (bf16[2,32,768]{2,1,0:T(8,128)(2,1)}, bf16[2,32,768]{2,1,0:T(8,128)(2,1)}, u32[]{:S(2)}, u32[]{:S(2)}) collective-permute-start(bf16[2,32,768]{2,1,0:T(8,128)(2,1)} %constant_dynamic-update-slice_fusion), channel_id=1, source_target_pairs={{0,1},{1,0},{2,3},{3,2},{4,5},{5,4},{6,7},{7,6},{8,9},{9,8},{10,11... | collective-permute-start | bytes 294920 | tf_op jit(solution)/shard_map/ppermute | solution.py:19
  50.6 4.2 copy-start.32
  59.9 46.7 %copy-start.31 = (bf16[1,8,768]{2,1,0:T(8,128)(2,1)S(1)}, bf16[1,8,768]{2,1,0:T(8,128)(2,1)}, u32[]{:S(2)}) copy-start(bf16[1,8,768]{2,1,0:T(8,128)(2,1)} %stack_reshape.27) | copy-start | bytes 36868
  106.6 42.0 %copy-start.37 = (s32[12]{0:T(128)S(1)}, s32[12]{0:T(128)}, u32[]{:S(2)}) copy-start(s32[12]{0:T(128)} %copy-done.36) | copy-start | bytes 148
  106.6 42.0 %copy-start.38 = (s32[256]{0:T(256)S(1)}, s32[256]{0:T(256)}, u32[]{:S(2)}) copy-start(s32[256]{0:T(256)} %iota_multiply_fusion) | copy-start | bytes 3076
  106.6 42.0 %copy-start.39 = (s32[256]{0:T(256)S(1)}, s32[256]{0:T(256)}, u32[]{:S(2)}) copy-start(s32[256]{0:T(256)} %multiply_add_fusion) | copy-start | bytes 3076
  150.5 0.6 copy-start.20
  154.8 34.2 %copy-start.29 = (f32[12,256]{1,0:T(8,128)}, f32[12,256]{1,0:T(8,128)S(1)}, u32[]{:S(2)}) copy-start(f32[12,256]{1,0:T(8,128)S(1)} %get-tuple-element.60) | copy-start | bytes 36868
  159.1 27.2 %collective-permute-start.1 = (bf16[2,64,768]{2,1,0:T(8,128)(2,1)}, bf16[2,64,768]{2,1,0:T(8,128)(2,1)}, u32[]{:S(2)}, u32[]{:S(2)}) collective-permute-start(bf16[2,64,768]{2,1,0:T(8,128)(2,1)} %maximum_select_fusion.2), channel_id=1, source_target_pairs={{0,2},{1,3},{2,0},{3,1},{4,6},{5,7},{6,4},{7,5},{8,10},{9,11},{10,... | collective-permute-start | bytes 589832 | tf_op jit(solution)/shard_map/ppermute | solution.py:19
  187.7 11.1 %collective-permute-start.2 = (bf16[2,128,768]{2,1,0:T(8,128)(2,1)S(1)}, bf16[2,128,768]{2,1,0:T(8,128)(2,1)S(1)}, u32[]{:S(2)}, u32[]{:S(2)}) collective-permute-start(bf16[2,128,768]{2,1,0:T(8,128)(2,1)S(1)} %maximum_select_fusion.1), channel_id=1, source_target_pairs={{0,4},{1,5},{2,6},{3,7},{4,0},{5,1},{6,2},{7,3},{8,12},{9,13},{10,... | collective-permute-start | bytes 1179656 | tf_op jit(solution)/shard_map/ppermute | solution.py:19
  199.1 2.9 copy-start.33
  203.3 0.7 copy-start.3
  204.3 0.6 copy-start.30
  230.9 3.6 copy-start.4
  230.9 3.6 copy-start.9
  230.9 3.6 copy-start.23
  286.5 20.1 %collective-permute-start.3 = (f32[2,128,768]{2,1,0:T(8,128)}, f32[2,128,768]{2,1,0:T(8,128)}, u32[]{:S(2)}, u32[]{:S(2)}) collective-permute-start(f32[2,128,768]{2,1,0:T(8,128)} %broadcast_select_fusion), channel_id=1, source_target_pairs={{0,4},{1,5},{2,6},{3,7},{4,0},{5,1},{6,2},{7,3},{8,12},{9,13},{10,... | collective-permute-start | bytes 2359304 | tf_op jit(solution)/shard_map/ppermute | solution.py:19
  292.6 2.6 copy-start.13
  292.6 2.6 copy-start.21
  297.1 14.6 %copy-start.8 = (bf16[1,256,768]{1,2,0:T(8,128)(2,1)S(1)}, bf16[1,256,768]{1,2,0:T(8,128)(2,1)}, u32[]{:S(2)}) copy-start(bf16[1,256,768]{1,2,0:T(8,128)(2,1)} %copy.176) | copy-start | bytes 1179652
  297.1 14.6 %copy-start.22 = (f32[12,256,8]{1,2,0:T(8,128)S(1)}, f32[12,256,8]{1,2,0:T(8,128)}, u32[]{:S(2)}) copy-start(f32[12,256,8]{1,2,0:T(8,128)} %fusion.41) | copy-start | bytes 294916
  308.4 0.9 copy-start.5
  310.1 23.1 %collective-permute-start.4 = (f32[2,64,768]{2,1,0:T(8,128)}, f32[2,64,768]{2,1,0:T(8,128)}, u32[]{:S(2)}, u32[]{:S(2)}) collective-permute-start(f32[2,64,768]{2,1,0:T(8,128)} %slice_select_fusion), channel_id=1, source_target_pairs={{0,2},{1,3},{2,0},{3,1},{4,6},{5,7},{6,4},{7,5},{8,10},{9,11},{10,... | collective-permute-start | bytes 1179656 | tf_op jit(solution)/shard_map/ppermute | solution.py:19
  329.8 220.9 %reduce-scatter.7.cloned.1.call-start = ((), (), s32[]{:S(2)}) async-start(), calls=%async_computation.3 | async-start | bytes 7299072
  330.0 3.1 copy-start.6
  333.1 3.4 copy-start.2
  333.1 1.9 copy-start.10
  333.1 1.9 copy-start.11
  333.1 2.2 copy-start.12
  333.1 2.2 copy-start.25
  333.2 2.2 copy-start.27
  334.9 1.6 collective-permute-start.5
  352.5 3.1 copy-start.1
  352.6 3.1 copy-start.7
  352.6 3.1 copy-start.26
  352.6 3.1 copy-start.28
  355.7 2.3 copy-start.16
  355.7 3.0 copy-start.14
  355.7 3.0 copy-start.24
  357.9 0.8 copy-start.18
  370.8 2.8 copy-start.15
  370.8 2.8 copy-start.17
  370.8 2.8 copy-start.19
Sparse Core Ops, SparseCore 0:
  329.9 95.2 reduce-scatter.4
  432.4 118.2 reduce-scatter.6
where the time goes:
time: 561 us; the launch traced here: 558 us
  waiting for transfers between devices  192 us (34%)
  local copies, waits for them, and re-layouts  140 us (25%)
  blocking collectives  121 us (22%)
  matrix products  52.5 us (9%)
  other arithmetic  32.9 us (6%)
  between operations  15.1 us (3%)
    unnamed x3, waiting for transfers between devices  126 us
    broadcast_in_dim x28, local copies, waits for them, and re-layouts, spread_rows(): jnp.where(chosen, array_in[:, None], jnp.asarray(fill, array_in.dtype))  53.5 us
    reduce_scatter x1, waiting for transfers between devices, per_device(): lax.psum_scatter(grad_wout_part, 'ctx', scatter_dimension=0, tiled=True)  49.7 us
    all_gather x1, blocking collectives, per_device(): lax.all_gather(row_block, 'ctx', axis=1, tiled=True)  45 us
    all_gather x1, blocking collectives, per_device(): lax.all_gather(jnp.stack([key_far.reshape(far_rows, D), value_far.reshape...  39.1 us
    all_gather x1, blocking collectives, per_device(): lax.all_gather(stat_block, 'ctx', axis=1, tiled=True)  37.4 us
    another operation x8, local copies, waits for them, and re-layouts, pick_rows(): array_in.reshape((row_count // stride, stride) + array_in.shape[1:])  19.6 us
    ppermute x6, waiting for transfers between devices, from_partner(): return lax.ppermute(value, axis, pairs)  16.4 us
  transfers between devices with their start and end apart: 8, of which 4 were waited for; matrix products, arithmetic and copies ran while one was open for 25% of the time, Pallas kernels for 0%

commit v1 on v0

v1 whole, which is shorter than its diff:
```python
import functools

import jax
import jax.numpy as jnp
import numpy as np
from jax import lax
from jax.experimental import pallas as pl
from jax.experimental.pallas import tpu as pltpu
from jax.sharding import PartitionSpec as P

HEAD_DIM = 64
GROUP = 8
PAIR = 2 * HEAD_DIM
LANES = 128
SECOND = 16
SCALE = 0.125
BF = jnp.bfloat16
F32 = jnp.float32
NT = (((1,), (1,)), ((), ()))
NN = (((1,), (0,)), ((), ()))
TN = (((0,), (0,)), ((), ()))
VMEM_BYTES = 40 * 1024 * 1024


def dot(a, b, dims=NN):
    return lax.dot_general(a, b, dims, preferred_element_type=F32)


def dot_exact(a, b):
    return lax.dot_general(a, b, NN, preferred_element_type=F32, precision=lax.Precision.HIGHEST)


def iota(shape, dim):
    return lax.broadcasted_iota(jnp.int32, shape, dim)


def low_half(shape):
    return iota(shape, len(shape) - 1) % PAIR < HEAD_DIM


def halves(x):
    low = low_half(x.shape)
    zero = jnp.zeros((), x.dtype)
    return jnp.where(low, x, zero), jnp.where(low, zero, x)


def by_head(first, second, rows):
    return jnp.where(low_half((rows, PAIR)), first, second)


class Sizes:
    def __init__(self, rows, width, dev_count):
        self.rows = rows
        self.width = width
        self.devs = dev_count
        self.heads = width // HEAD_DIM
        self.pairs = self.heads // 2
        self.mid = rows // GROUP
        self.far = rows // dev_count
        self.sel = 2 * self.mid
        self.upper = dev_count // GROUP
        self.strip = width // dev_count
        self.half = width // 2


def chosen_row(z, index, off_mid, off_far):
    row = jnp.where(index < z.mid, index * GROUP + off_mid, (index - z.mid) * z.devs + off_far)
    return jnp.where(index < z.mid + z.far, row, -1)


def spread(z, offs_ref, pair, picked):
    lane = iota((1, 4 * z.sel), 1)
    second = (lane // z.sel) % 2 == 1
    off_mid = jnp.where(second, offs_ref[0, 2 * pair + 1], offs_ref[0, 2 * pair])
    off_far = jnp.where(second, offs_ref[1, 2 * pair + 1], offs_ref[1, 2 * pair])
    target = chosen_row(z, lane % z.sel, off_mid, off_far)
    place = (iota((z.rows, 4 * z.sel), 0) == target).astype(F32).astype(BF)
    high = picked.astype(BF)
    rest = (picked - high.astype(F32)).astype(BF)
    first_high, second_high = halves(high)
    first_rest, second_rest = halves(rest)
    stacked = jnp.concatenate([first_high, second_high, first_rest, second_rest], axis=0)
    return dot(place, stacked)


def lane_offsets(z, offs_ref):
    lane = iota((1, LANES), 1)
    off_mid = jnp.full((1, LANES), -1, jnp.int32)
    off_far = jnp.full((1, LANES), -1, jnp.int32)
    for head in range(z.heads):
        here = (lane == head) | (lane == SECOND + head)
        off_mid = jnp.where(here, offs_ref[0, head], off_mid)
        off_far = jnp.where(here, offs_ref[1, head], off_far)
    return off_mid, off_far


def stat_masks(z, offs_ref):
    off_mid, off_far = lane_offsets(z, offs_ref)
    row = iota((z.rows, LANES), 0)
    return row % GROUP == off_mid, row % z.devs == off_far


def pick_stats(z, masks, stats):
    entry = iota((z.sel, z.rows), 0)
    row = iota((z.sel, z.rows), 1)
    take_mid = ((entry < z.mid) & (row // GROUP == entry)).astype(F32)
    take_far = (row // z.devs == entry - z.mid).astype(F32)
    return dot_exact(take_mid, jnp.where(masks[0], stats, 0.0)) + dot_exact(
        take_far, jnp.where(masks[1], stats, 0.0)
    )


def spread_stats(z, masks, picked):
    row = iota((z.rows, z.sel), 0)
    entry = iota((z.rows, z.sel), 1)
    give_mid = ((entry < z.mid) & (row // GROUP == entry)).astype(F32)
    give_far = (row // z.devs == entry - z.mid).astype(F32)
    return (
        jnp.where(masks[0], dot_exact(give_mid, picked), -jnp.inf),
        jnp.where(masks[1], dot_exact(give_far, picked), -jnp.inf),
    )


def gathered_place(z, own):
    index = iota((1, 2 * z.rows), 1)
    core = index // z.rows
    plane = (index % z.rows) // z.sel
    inner = index % z.sel
    is_mid = inner < z.mid
    upper = jnp.where(is_mid, 0, (inner - z.mid) // z.far)
    step = jnp.where(is_mid, inner * GROUP, ((inner - z.mid) % z.far) * z.devs)
    dev = own ^ (core + 2 * plane + GROUP * upper)
    return dev * z.rows + step, is_mid


def project_kernel(z, offs_ref, tiles, w_qkv, cot, w_out, q, k, v, g, sel, far):
    width = z.width
    own = tiles[...]
    k[...] = dot(own, w_qkv[:, width : 2 * width]).astype(BF)
    v[...] = dot(own, w_qkv[:, 2 * width :]).astype(BF)
    q[...] = dot(own, w_qkv[:, :width]).astype(BF) * jnp.asarray(SCALE, BF)
    g[...] = dot(cot[...], w_out[...], NT).astype(BF)
    entry = iota((2 * z.sel, z.rows), 0)
    column = iota((2 * z.sel, z.rows), 1)
    second = entry >= z.sel
    for pair in range(z.pairs):
        lanes = slice(pair * PAIR, (pair + 1) * PAIR)
        off_mid = jnp.where(second, offs_ref[0, 2 * pair + 1], offs_ref[0, 2 * pair])
        off_far = jnp.where(second, offs_ref[1, 2 * pair + 1], offs_ref[1, 2 * pair])
        target = chosen_row(z, entry % z.sel, off_mid, off_far)
        take = (column == target).astype(F32).astype(BF)
        every = jnp.concatenate([k[:, lanes], v[:, lanes], q[:, lanes], g[:, lanes]], axis=1)
        both = dot(take, every)
        picked = jnp.where(low_half((z.sel, 4 * PAIR)), both[: z.sel], both[z.sel :]).astype(BF)
        far_part = jnp.where(
            low_half((z.far, 4 * PAIR)),
            both[z.mid : z.mid + z.far],
            both[z.sel + z.mid : z.sel + z.mid + z.far],
        ).astype(BF)
        for part in range(4):
            to = slice(part * width + pair * PAIR, part * width + (pair + 1) * PAIR)
            sel[:, to] = picked[:, part * PAIR : (part + 1) * PAIR]
            far[:, to] = far_part[:, part * PAIR : (part + 1) * PAIR]


def near_kernel(z, pad_ref, q, k, v, tiles, order, mixed, lse, turned, turned_out):
    own = lax.axis_index("ctx")
    limit = z.rows * z.devs - pad_ref[0] - own * z.rows
    valid = iota((1, z.rows), 1) < limit
    lane = iota((z.rows, LANES), 1)
    lse_all = jnp.zeros((z.rows, LANES), F32)
    for pair in range(z.pairs):
        lanes = slice(pair * PAIR, (pair + 1) * PAIR)
        query = q[:, lanes]
        keys = halves(k[:, lanes])
        values = halves(v[:, lanes])
        total = None
        for side in range(2):
            scores = jnp.where(valid, dot(query, keys[side], NT), -jnp.inf)
            peak = jnp.max(scores, axis=1, keepdims=True)
            powers = jnp.exp(scores - peak)
            summed = jnp.sum(powers, axis=1, keepdims=True)
            part = dot(powers.astype(BF), values[side]) * (1.0 / summed)
            total = part if total is None else total + part
            lse_all = jnp.where(lane == 2 * pair + side, peak + jnp.log(summed), lse_all)
        mixed[:, lanes] = total
    lse[...] = lse_all
    count = 2 * z.width
    for start in range(0, count, 256):
        rows = slice(start, start + 256)
        place = (iota((256, z.width), 1) == order[rows, :]).astype(F32).astype(BF)
        result = dot(place, tiles[...], NT).astype(BF)
        if start < z.width:
            turned[rows, :] = result
        else:
            turned_out[start - z.width : start - z.width + 256, :] = result


def join_kernel(z, offs_ref, pad_ref, sel, first, second, mixed, lse, g, attn, stats, picked, held):
    own = lax.axis_index("ctx")
    limit = z.rows * z.devs - pad_ref[0]
    place, is_mid = gathered_place(z, own)
    lane = iota((z.sel, LANES), 1)
    same = (iota((z.sel, 1), 0) < z.mid) == is_mid
    lse_sel = jnp.zeros((z.sel, LANES), F32)
    width = z.width
    for pair in range(z.pairs):
        lanes = slice(pair * PAIR, (pair + 1) * PAIR)
        value_lanes = slice(width + pair * PAIR, width + (pair + 1) * PAIR)
        query = sel[:, 2 * width + pair * PAIR : 2 * width + (pair + 1) * PAIR]
        keys = halves(jnp.concatenate([first[:, lanes], second[:, lanes]], axis=0))
        values = halves(jnp.concatenate([first[:, value_lanes], second[:, value_lanes]], axis=0))
        total = None
        for side in range(2):
            head = 2 * pair + side
            valid = place + jnp.where(is_mid, offs_ref[0, head], offs_ref[1, head]) < limit
            scores = jnp.where(same & valid, dot(query, keys[side], NT), -jnp.inf)
            peak = jnp.max(scores, axis=1, keepdims=True)
            powers = jnp.exp(scores - peak)
            summed = jnp.sum(powers, axis=1, keepdims=True)
            part = dot(powers.astype(BF), values[side]) * (1.0 / summed)
            total = part if total is None else total + part
            lse_sel = jnp.where(lane == head, peak + jnp.log(summed), lse_sel)
        held[:, lanes] = total
    masks = stat_masks(z, offs_ref)
    lse_near = lse[...]
    lse_mid, lse_far = spread_stats(z, masks, lse_sel)
    top = jnp.maximum(lse_near, jnp.maximum(lse_mid, lse_far))
    total_lse = top + jnp.log(
        jnp.exp(lse_near - top) + jnp.exp(lse_mid - top) + jnp.exp(lse_far - top)
    )
    near_share = jnp.exp(lse_near - total_lse)
    sel_share = jnp.exp(lse_sel - pick_stats(z, masks, total_lse))
    lane = iota((z.rows, LANES), 1)
    both = total_lse
    for pair in range(z.pairs):
        lanes = slice(pair * PAIR, (pair + 1) * PAIR)
        share = by_head(
            sel_share[:, 2 * pair : 2 * pair + 1], sel_share[:, 2 * pair + 1 : 2 * pair + 2], z.sel
        )
        near = by_head(
            near_share[:, 2 * pair : 2 * pair + 1],
            near_share[:, 2 * pair + 1 : 2 * pair + 2],
            z.rows,
        )
        combined = near * mixed[:, lanes] + spread(z, offs_ref, pair, share * held[:, lanes])
        rounded = combined.astype(BF)
        attn[:, lanes] = rounded
        product = g[:, lanes].astype(F32) * rounded.astype(F32)
        parts = halves(product)
        for side in range(2):
            delta = jnp.sum(parts[side], axis=1, keepdims=True)
            both = jnp.where(lane == SECOND + 2 * pair + side, delta, both)
    stats[...] = both
    picked[...] = pick_stats(z, masks, both)


def output_kernel(z, attn, tiles, w_out, order, rows_out, turned, turned_out):
    rows_out[...] = (tiles[...].astype(F32) + dot(attn[...], w_out[...])).astype(BF)
    for start in range(0, z.width, z.half):
        source = order[2 * start : 2 * start + z.half, :]
        place = (iota((z.half, z.width), 1) == source).astype(F32).astype(BF)
        result = dot(place, attn[...], NT).astype(BF)
        if start == 0:
            turned[...] = result
        else:
            turned_out[...] = result


def near_grads_kernel(
    z, offs_ref, pad_ref, q, k, v, g, stats, sel, first, second, picked, dq, dk, dv
):
    own = lax.axis_index("ctx")
    limit = z.rows * z.devs - pad_ref[0]
    place, is_mid = gathered_place(z, own)
    same = (iota((z.sel, 1), 0) < z.mid) == is_mid
    valid_near = iota((z.rows, 1), 0) < limit - own * z.rows
    across = jnp.transpose(stats[...])
    width = z.width
    for pair in range(z.pairs):
        lanes = slice(pair * PAIR, (pair + 1) * PAIR)
        value_lanes = slice(width + pair * PAIR, width + (pair + 1) * PAIR)
        query, grad = q[:, lanes], g[:, lanes]
        queries, grads = halves(query), halves(grad)
        keys, values = halves(k[:, lanes]), halves(v[:, lanes])
        query_sel = sel[:, 2 * width + pair * PAIR : 2 * width + (pair + 1) * PAIR]
        grad_sel = sel[:, 3 * width + pair * PAIR : 3 * width + (pair + 1) * PAIR]
        keys_all = halves(jnp.concatenate([first[:, lanes], second[:, lanes]], axis=0))
        values_all = halves(
            jnp.concatenate([first[:, value_lanes], second[:, value_lanes]], axis=0)
        )
        sum_q = sum_k = sum_v = sum_sel = None
        for side in range(2):
            head = 2 * pair + side
            scores = jnp.where(valid_near, dot(keys[side], query, NT), -jnp.inf)
            probs = jnp.exp(scores - across[head : head + 1, :])
            grad_probs = dot(values[side], grad, NT)
            grad_scores = probs * (grad_probs - across[SECOND + head : SECOND + head + 1, :])
            grad_scores = grad_scores.astype(BF)
            part_k = dot(grad_scores, queries[side])
            part_v = dot(probs.astype(BF), grads[side])
            part_q = dot(grad_scores, keys[side], TN)
            valid = place + jnp.where(is_mid, offs_ref[0, head], offs_ref[1, head]) < limit
            scores = jnp.where(same & valid, dot(query_sel, keys_all[side], NT), -jnp.inf)
            probs = jnp.exp(scores - picked[:, head : head + 1])
            grad_probs = dot(grad_sel, values_all[side], NT)
            grad_scores = probs * (grad_probs - picked[:, SECOND + head : SECOND + head + 1])
            part_sel = dot(grad_scores.astype(BF), keys_all[side])
            if side == 0:
                sum_q, sum_k, sum_v, sum_sel = part_q, part_k, part_v, part_sel
            else:
                sum_q, sum_k, sum_v = sum_q + part_q, sum_k + part_k, sum_v + part_v
                sum_sel = sum_sel + part_sel
        dk[:, lanes] = sum_k
        dv[:, lanes] = sum_v
        dq[:, lanes] = (SCALE * (sum_q + spread(z, offs_ref, pair, sum_sel))).astype(BF)


def key_grads_kernel(
    z, offs_ref, pad_ref, sel, first, second, first_stats, second_stats, dk_near, dv_near, dk, dv
):
    own = lax.axis_index("ctx")
    limit = z.rows * z.devs - pad_ref[0] - own * z.rows
    _, is_mid = gathered_place(z, own)
    entry = iota((z.sel, 1), 0)
    same = (entry < z.mid) == is_mid
    across = jnp.transpose(jnp.concatenate([first_stats[...], second_stats[...]], axis=0))
    width = z.width
    for pair in range(z.pairs):
        lanes = slice(pair * PAIR, (pair + 1) * PAIR)
        value_lanes = slice(width + pair * PAIR, width + (pair + 1) * PAIR)
        keys, values = sel[:, lanes], sel[:, value_lanes]
        queries = halves(jnp.concatenate([first[:, lanes], second[:, lanes]], axis=0))
        grads = halves(jnp.concatenate([first[:, value_lanes], second[:, value_lanes]], axis=0))
        sum_k = sum_v = None
        for side in range(2):
            head = 2 * pair + side
            at = chosen_row(z, entry, offs_ref[0, head], offs_ref[1, head])
            valid = (at >= 0) & (at < limit)
            scores = jnp.where(same & valid, dot(keys, queries[side], NT), -jnp.inf)
            probs = jnp.exp(scores - across[head : head + 1, :])
            grad_probs = dot(values, grads[side], NT)
            grad_scores = probs * (grad_probs - across[SECOND + head : SECOND + head + 1, :])
            part_k = dot(grad_scores.astype(BF), queries[side])
            part_v = dot(probs.astype(BF), grads[side])
            sum_k = part_k if side == 0 else sum_k + part_k
            sum_v = part_v if side == 0 else sum_v + part_v
        dk[:, lanes] = (dk_near[:, lanes] + spread(z, offs_ref, pair, sum_k)).astype(BF)
        dv[:, lanes] = (dv_near[:, lanes] + spread(z, offs_ref, pair, sum_v)).astype(BF)


def weight_kernel(count, *refs):
    left_own, left_other = refs[0], refs[1]
    out = refs[-1]
    width = refs[2].shape[1]
    for i in range(count):
        out[:, i * width : (i + 1) * width] = (
            dot(left_own[...], refs[2 + i][...]) + dot(left_other[...], refs[2 + count + i][...])
        ).astype(BF)


def tiles_kernel(z, dq, dk, dv, w_qkv, out):
    width = z.width
    out[...] = (
        dot(dq[...], w_qkv[:, :width], NT)
        + dot(dk[...], w_qkv[:, width : 2 * width], NT)
        + dot(dv[...], w_qkv[:, 2 * width :], NT)
    ).astype(BF)


def call(kernel, outs, flops, scratch=(), smem=0):
    def run(*args):
        moved = sum(int(np.prod(a.shape)) * a.dtype.itemsize for a in args)
        moved += sum(int(np.prod(s)) * jnp.dtype(t).itemsize for s, t in outs)
        specs = [
            pl.BlockSpec(memory_space=pltpu.SMEM if i < smem else pltpu.VMEM)
            for i in range(len(args))
        ]
        return pl.pallas_call(
            kernel,
            out_shape=tuple(jax.ShapeDtypeStruct(s, t) for s, t in outs),
            in_specs=specs,
            out_specs=tuple(pl.BlockSpec(memory_space=pltpu.VMEM) for _ in outs),
            scratch_shapes=list(scratch),
            compiler_params=pltpu.CompilerParams(vmem_limit_bytes=VMEM_BYTES),
            cost_estimate=pl.CostEstimate(
                flops=int(flops), bytes_accessed=int(moved), transcendentals=0
            ),
        )(*args)

    return run


def swap(value, mask, dev_count):
    return lax.ppermute(value, "ctx", [(d, d ^ mask) for d in range(dev_count)])


def upper_steps(dev_count):
    steps, base = [], GROUP
    while base < dev_count:
        count = 4 if base * 4 <= dev_count else 2
        steps.append((base, count))
        base *= count
    return steps


PLANE = (2, 4)


def collect(value, step, dev_count):
    base, count = step
    return jnp.concatenate(
        [value] + [swap(value, base * i, dev_count) for i in range(1, count)], axis=0
    )


def reduce_step(value, step, dev_count, dtype):
    base, count = step
    size = value.shape[0] // count
    total = value[:size].astype(F32)
    for i in range(1, count):
        total = total + swap(value[i * size : (i + 1) * size], base * i, dev_count).astype(F32)
    return total.astype(dtype)


def reduce_all(value, steps, dev_count):
    for i, step in enumerate(steps):
        value = reduce_step(value, step, dev_count, F32 if i == len(steps) - 1 else BF)
    return value


def strip_order(z, own):
    entries = []
    for core in range(2):
        for first_plane in (True, False):
            outer, inner = (4, z.upper) if first_plane else (z.upper, 4)
            a, b, r = np.meshgrid(
                np.arange(outer), np.arange(inner), np.arange(z.strip), indexing="ij"
            )
            plane, upper = (a, b) if first_plane else (b, a)
            entries.append(
                np.stack([(core + 2 * plane + GROUP * upper).ravel(), r.ravel()], axis=1)
            )
    table = np.concatenate(entries, axis=0).astype(np.int32)
    return (own ^ table[:, :1]) * z.strip + table[:, 1:]


def per_device(tiles, w_qkv, w_out, cotangent, offsets, pad_count):
    n = lax.axis_size("ctx")
    z = Sizes(tiles.shape[0], tiles.shape[1], n)
    own = lax.axis_index("ctx")
    rows, width = z.rows, z.width
    ups = upper_steps(n)
    order = strip_order(z, own)
    base_flops = 2 * rows * rows * width

    q, k, v, g, sel, far = call(
        functools.partial(project_kernel, z),
        [((rows, width), BF)] * 4 + [((z.sel, 4 * width), BF), ((z.far, 4 * width), BF)],
        2 * rows * width * 4 * width,
        smem=1,
    )(offsets, tiles, w_qkv, cotangent, w_out)

    far_up = far
    for step in ups:
        far_up = collect(far_up, step, n)
    mixed, lse, turned, turned_out = call(
        functools.partial(near_kernel, z),
        [
            ((rows, width), F32),
            ((rows, LANES), F32),
            ((width, rows), BF),
            ((width, rows), BF),
        ],
        8 * base_flops,
        smem=1,
    )(pad_count, q, k, v, tiles, order)
    kv_first = collect(
        jnp.concatenate([sel[: z.mid, : 2 * width], far_up[:, : 2 * width]], axis=0), PLANE, n
    )
    kv_second = swap(kv_first, 1, n)
    qg_first = collect(
        jnp.concatenate([sel[: z.mid, 2 * width :], far_up[:, 2 * width :]], axis=0), PLANE, n
    )
    qg_second = swap(qg_first, 1, n)
    turned_other = swap(turned_out, 1, n)
    cot_other = swap(cotangent, 1, n)

    attn, stats, picked = call(
        functools.partial(join_kernel, z),
        [((rows, width), BF), ((rows, LANES), F32), ((z.sel, LANES), F32)],
        3 * base_flops,
        scratch=[pltpu.VMEM((z.sel, width), F32)],
        smem=2,
    )(offsets, pad_count, sel, kv_first, kv_second, mixed, lse, g)

    stats_up = picked[z.mid : z.mid + z.far]
    for step in ups:
        stats_up = collect(stats_up, step, n)
    stats_first = collect(jnp.concatenate([picked[: z.mid], stats_up], axis=0), PLANE, n)
    stats_second = swap(stats_first, 1, n)

    out_rows, attn_turned, attn_turned_out = call(
        functools.partial(output_kernel, z),
        [((rows, width), BF), ((z.half, rows), BF), ((z.half, rows), BF)],
        4 * rows * width * width,
    )(attn, tiles, w_out, order)
    attn_other = swap(attn_turned_out, 1, n)

    dq, dk_near, dv_near = call(
        functools.partial(near_grads_kernel, z),
        [((rows, width), BF), ((rows, width), F32), ((rows, width), F32)],
        8 * base_flops,
        smem=2,
    )(offsets, pad_count, q, k, v, g, stats, sel, kv_first, kv_second, picked)
    dq_other = swap(dq, 1, n)

    (wout_half,) = call(
        functools.partial(weight_kernel, 1), [((z.half, width), BF)], 2 * rows * width * width
    )(attn_turned, attn_other, cotangent, cot_other)
    grad_wout = reduce_all(wout_half, [PLANE] + ups[::-1], n)

    (wq_half,) = call(
        functools.partial(weight_kernel, 1), [((z.half, width), BF)], 2 * rows * width * width
    )(turned[z.half :], turned_other[z.half :], dq, dq_other)
    grad_wq = reduce_all(wq_half, ups[::-1] + [PLANE], n)

    dk, dv = call(
        functools.partial(key_grads_kernel, z),
        [((rows, width), BF), ((rows, width), BF)],
        3 * base_flops,
        smem=2,
    )(offsets, pad_count, sel, qg_first, qg_second, stats_first, stats_second, dk_near, dv_near)
    dk_other = swap(dk, 1, n)
    dv_other = swap(dv, 1, n)
    (wkv_half,) = call(
        functools.partial(weight_kernel, 2), [((z.half, 2 * width), BF)], 4 * rows * width * width
    )(turned[: z.half], turned_other[: z.half], dk, dv, dk_other, dv_other)
    grad_wkv = reduce_all(wkv_half, [PLANE] + ups[::-1], n)

    (grad_tiles,) = call(
        functools.partial(tiles_kernel, z), [((rows, width), BF)], 6 * rows * width * width
    )(dq, dk, dv, w_qkv)
    grad_wqkv = jnp.concatenate([grad_wq, grad_wkv], axis=1)
    return out_rows, grad_tiles, grad_wqkv, grad_wout


def solution(mesh):
    return jax.shard_map(
        per_device,
        mesh=mesh,
        in_specs=(P("ctx", None), P(), P(), P("ctx", None), P(), P()),
        out_specs=(P("ctx", None), P("ctx", None), P("ctx", None), P("ctx", None)),
        check_vma=False,
    )
```

time: 561 us -> 129 us (0.23)
  waiting for transfers between devices: 192 us -> 43 us
  local copies, waits for them, and re-layouts: 140 us -> 5.37 us
  blocking collectives: 121 us -> 0 us
  matrix products: 52.5 us -> 0 us
  starting transfers between devices: 4.06 us -> 47.9 us
  other arithmetic: 32.9 us -> 3.02 us
  Pallas kernels: 0 us -> 27.3 us
  between operations: 15.1 us -> 1.72 us
    unnamed x3 -> x0, waiting for transfers between devices: 126 us -> none
    all_gather x3 -> x0, blocking collectives: 121 us -> none  [the longest x1 45 us: per_device(): lax.all_gather(row_block, 'ctx', axis=1, tiled=True)]
    broadcast_in_dim x28 -> x0, local copies, waits for them, and re-layouts: 53.5 us -> none  [spread_rows(): jnp.where(chosen, array_in[:, None], jnp.asarray(fill, array_in.dtype))]
    dot_general x24 -> x0, matrix products: 52.5 us -> none  [the longest x3 8.03 us: level_forward(): jnp.einsum('hnm,mhe->nhe', weights, value_rows, preferred_element_type=jn...]
    reduce_scatter x1 -> x0, waiting for transfers between devices: 49.7 us -> none  [per_device(): lax.psum_scatter(grad_wout_part, 'ctx', scatter_dimension=0, tiled=True)]
    ppermute x6 -> x42, starting transfers between devices: 3.76 us -> 47.9 us  [swap(): return lax.ppermute(value, 'ctx', [(d, d ^ mask) for d in range(dev_count)])]
    another operation x17 -> x0, local copies, waits for them, and re-layouts: 34.1 us -> none  [the longest x8 19.6 us: pick_rows(): array_in.reshape((row_count // stride, stride) + array_in.shape[1:])]
    pallas_call x0 -> x10, Pallas kernels: none -> 27.3 us  [run(): pl.pallas_call(kernel, out_shape=tuple((jax.ShapeDtypeStruct(s, t) for s,...]
  transfers between devices with their start and end apart: 8 -> 42, of which waited for: 4 -> 16; matrix products, arithmetic and copies ran while one was open for 25% -> 2% of each run, Pallas kernels for 0% -> 19%
where the time goes in v1:
time: 129 us; the launch traced here: 128 us
  starting transfers between devices  47.9 us (37%)
  waiting for transfers between devices  43 us (33%)
  Pallas kernels  27.3 us (21%)
  local copies, waits for them, and re-layouts  5.37 us (4%)
  other arithmetic  3.02 us (2%)
  between operations  1.72 us (1%)
    ppermute x42, starting transfers between devices, swap(): return lax.ppermute(value, 'ctx', [(d, d ^ mask) for d in range(dev_count)])  47.9 us
    ppermute x42, waiting for transfers between devices, swap(): return lax.ppermute(value, 'ctx', [(d, d ^ mask) for d in range(dev_count)])  43 us
    pallas_call x10, Pallas kernels, run(): pl.pallas_call(kernel, out_shape=tuple((jax.ShapeDtypeStruct(s, t) for s,...  27.3 us
    unnamed x30, local copies, waits for them, and re-layouts  5.05 us
  transfers between devices with their start and end apart: 42, of which 16 were waited for; matrix products, arithmetic and copies ran while one was open for 2% of the time, Pallas kernels for 19%

profile of v1, /device:TPU:0, one launch (start us, length us, event | category | flops | bytes accessed | tf_op | source)
XLA Modules:
  0.0 128.3 jit_solution(4779947407092451911)
XLA Ops:
  0.6 2.0 %copy-done = bf16[768,2304]{1,0:T(8,128)(2,1)S(1)} copy-done((bf16[768,2304]{1,0:T(8,128)(2,1)S(1)}, bf16[768,2304]{1,0:T(8,128)(2,1)}, u32[]{:S(2)}) %copy-start) | copy-done | bytes 3538968
  2.6 1.3 copy-done.2
  3.9 1.0 copy-done.4
  5.6 2.8 %shard_map.111 = (bf16[256,768]{1,0:T(8,128)(2,1)S(1)}, bf16[256,768]{1,0:T(8,128)(2,1)S(1)}, bf16[256,768]{1,0:T(8,128)(2,1)S(1)}, bf16[256,768]{1,0:T(8,128)(2...) custom-call(s32[2,12]{1,0:T(2,128)S(1)} %copy-done.6, bf16[256,768]{1,0:T(8,128)(2,1)S(1)} %copy-done.4, ...), custom_call_target="tpu_custom_call" | custom-call | flops 1207959552 | bytes 7520352 | tf_op jit(solution)/shard_map/pallas_call | solution.py:379
  8.3 3.1 %collective-permute-start = (bf16[8,3072]{1,0:T(8,128)(2,1)S(1)}, bf16[8,3072]{1,0:T(8,128)(2,1)S(1)}, u32[]{:S(2)}, u32[]{:S(2)}) collective-permute-start(bf16[8,3072]{1,0:T(8,128)(2,1)S(1)} %get-tuple-element.26), channel_id=1, source_target_pairs={{0,8},{1,9},{2,10},{3,11},{4,12},{5,13},{6,14},{7,15},{8,0},{9,1},... | collective-permute-start | bytes 147464 | tf_op jit(solution)/shard_map/ppermute | solution.py:395
  11.4 2.6 %collective-permute-start.1 = (bf16[8,3072]{1,0:T(8,128)(2,1)S(1)}, bf16[8,3072]{1,0:T(8,128)(2,1)S(1)}, u32[]{:S(2)}, u32[]{:S(2)}) collective-permute-start(bf16[8,3072]{1,0:T(8,128)(2,1)S(1)} %get-tuple-element.26), channel_id=1, source_target_pairs={{0,16},{1,17},{2,18},{3,19},{4,20},{5,21},{6,22},{7,23},{8,24},{9,... | collective-permute-start | bytes 147464 | tf_op jit(solution)/shard_map/ppermute | solution.py:395
  14.7 1.3 multiply_add_fusion.order
  16.0 2.4 %shard_map.112 = (f32[256,768]{1,0:T(8,128)S(1)}, f32[256,128]{1,0:T(8,128)S(1)}, bf16[768,256]{1,0:T(8,128)(2,1)S(1)}, bf16[768,256]{1,0:T(8,128)(2,1)S(1)}) custom-call(s32[1]{0:T(128)S(6)} %copy.30.pad_ref, bf16[256,768]{1,0:T(8,128)(2,1)S(1)} %get-tuple-element.27.q, bf16[256,768]{1,0:T(8,128)(2,1)S(1)} %get-tuple-element.28.k, ...), custom_call_target="tpu_custom_call" | custom-call | flops 805306368 | bytes 3282948 | tf_op jit(solution)/shard_map/pallas_call | solution.py:379
  19.0 0.9 collective-permute-done.2
  20.0 1.6 %collective-permute-start.3 = (bf16[64,1536]{1,0:T(8,128)(2,1)S(1)}, bf16[64,1536]{1,0:T(8,128)(2,1)S(1)}, u32[]{:S(2)}, u32[]{:S(2)}) collective-permute-start(bf16[64,1536]{1,0:T(8,128)(2,1)S(1)} %pad_maximum_fusion.1), channel_id=1, source_target_pairs={{0,2},{1,3},{2,0},{3,1},{4,6},{5,7},{6,4},{7,5},{8,10},{9,11},{10,... | collective-permute-start | bytes 589832 | tf_op jit(solution)/shard_map/ppermute | solution.py:395
  21.5 1.5 %collective-permute-start.4 = (bf16[64,1536]{1,0:T(8,128)(2,1)S(1)}, bf16[64,1536]{1,0:T(8,128)(2,1)S(1)}, u32[]{:S(2)}, u32[]{:S(2)}) collective-permute-start(bf16[64,1536]{1,0:T(8,128)(2,1)S(1)} %pad_maximum_fusion.1), channel_id=1, source_target_pairs={{0,4},{1,5},{2,6},{3,7},{4,0},{5,1},{6,2},{7,3},{8,12},{9,13},{10,... | collective-permute-start | bytes 589832 | tf_op jit(solution)/shard_map/ppermute | solution.py:395
  23.5 4.1 %collective-permute-done.3 = bf16[64,1536]{1,0:T(8,128)(2,1)S(1)} collective-permute-done((bf16[64,1536]{1,0:T(8,128)(2,1)S(1)}, bf16[64,1536]{1,0:T(8,128)(2,1)S(1)}, u32[]{:S(2)}, u32[]{:S(2)}) %collective-permute-start.3) | collective-permute-done | bytes 196640 | tf_op jit(solution)/shard_map/ppermute | solution.py:395
  27.6 1.7 %collective-permute-start.7 = (bf16[64,1536]{1,0:T(8,128)(2,1)S(1)}, bf16[64,1536]{1,0:T(8,128)(2,1)S(1)}, u32[]{:S(2)}, u32[]{:S(2)}) collective-permute-start(bf16[64,1536]{1,0:T(8,128)(2,1)S(1)} %pad_maximum_fusion.2), channel_id=1, source_target_pairs={{0,2},{1,3},{2,0},{3,1},{4,6},{5,7},{6,4},{7,5},{8,10},{9,11},{10,... | collective-permute-start | bytes 589832 | tf_op jit(solution)/shard_map/ppermute | solution.py:395
  29.4 1.0 collective-permute-done.4
  30.5 2.6 %collective-permute-done.5 = bf16[64,1536]{1,0:T(8,128)(2,1)S(1)} collective-permute-done((bf16[64,1536]{1,0:T(8,128)(2,1)S(1)}, bf16[64,1536]{1,0:T(8,128)(2,1)S(1)}, u32[]{:S(2)}, u32[]{:S(2)}) %collective-permute-start.5) | collective-permute-done | bytes 196640 | tf_op jit(solution)/shard_map/ppermute | solution.py:395
  33.5 0.9 collective-permute-done.7
  34.4 2.7 %collective-permute-start.9 = (bf16[64,1536]{1,0:T(8,128)(2,1)S(1)}, bf16[64,1536]{1,0:T(8,128)(2,1)S(1)}, u32[]{:S(2)}, u32[]{:S(2)}) collective-permute-start(bf16[64,1536]{1,0:T(8,128)(2,1)S(1)} %pad_maximum_fusion.2), channel_id=1, source_target_pairs={{0,6},{1,7},{2,4},{3,5},{4,2},{5,3},{6,0},{7,1},{8,14},{9,15},{10,... | collective-permute-start | bytes 589832 | tf_op jit(solution)/shard_map/ppermute | solution.py:395
  37.1 7.6 %collective-permute-done.8 = bf16[64,1536]{1,0:T(8,128)(2,1)S(1)} collective-permute-done((bf16[64,1536]{1,0:T(8,128)(2,1)S(1)}, bf16[64,1536]{1,0:T(8,128)(2,1)S(1)}, u32[]{:S(2)}, u32[]{:S(2)}) %collective-permute-start.8) | collective-permute-done | bytes 196640 | tf_op jit(solution)/shard_map/ppermute | solution.py:395
  44.9 5.9 %shard_map.113 = (bf16[256,768]{1,0:T(8,128)(2,1)S(1)}, f32[256,128]{1,0:T(8,128)S(1)}, f32[64,128]{1,0:T(8,128)S(1)}) custom-call(s32[2,12]{1,0:T(2,128)S(1)} %copy-done.7, s32[1]{0:T(128)S(6)} %copy.30.pad_ref, bf16[64,3072]{1,0:T(8,128)(2,1)S(1)} %get-tuple-element.25.sel, bf16[256,1536]{1,0:T(8,128)(2,1)S(1)} %constant_dynamic-update-slice_fusion.4.first, ...), custom_call_target="tpu_custom_call" | custom-call | flops 301989888 | bytes 3833956 | tf_op jit(solution)/shard_map/pallas_call | solution.py:379
  50.9 3.5 %collective-permute-start.12 = (f32[8,128]{1,0:T(8,128)S(1)}, f32[8,128]{1,0:T(8,128)S(1)}, u32[]{:S(2)}, u32[]{:S(2)}) collective-permute-start(f32[8,128]{1,0:T(8,128)S(1)} %slice.109), channel_id=1, source_target_pairs={{0,16},{1,17},{2,18},{3,19},{4,20},{5,21},{6,22},{7,23},{8,24},{9,... | collective-permute-start | bytes 12296 | tf_op jit(solution)/shard_map/ppermute | solution.py:395
  54.4 0.9 collective-permute-start.13
  55.3 1.4 %shard_map.114 = (bf16[256,768]{1,0:T(8,128)(2,1)}, bf16[384,256]{1,0:T(8,128)(2,1)S(1)}, bf16[384,256]{1,0:T(8,128)(2,1)S(1)}) custom-call(bf16[256,768]{1,0:T(8,128)(2,1)S(1)} %get-tuple-element.33.attn, bf16[256,768]{1,0:T(8,128)(2,1)S(1)} %copy-done.5, bf16[768,768]{1,0:T(8,128)(2,1)S(1)} %copy-done.3, s32[1536,1]{1,0:T(8,128)S(1)} %multiply_add_fusion.order), custom_call_target="tpu_custom_call" | custom-call | flops 603979776 | bytes 2758656 | tf_op jit(solution)/shard_map/pallas_call | solution.py:379
  57.2 2.6 %collective-permute-done.13 = f32[8,128]{1,0:T(8,128)S(1)} collective-permute-done((f32[8,128]{1,0:T(8,128)S(1)}, f32[8,128]{1,0:T(8,128)S(1)}, u32[]{:S(2)}, u32[]{:S(2)}) %collective-permute-start.13) | collective-permute-done | bytes 4128 | tf_op jit(solution)/shard_map/ppermute | solution.py:395
  59.8 1.4 %collective-permute-start.14 = (f32[64,128]{1,0:T(8,128)S(1)}, f32[64,128]{1,0:T(8,128)S(1)}, u32[]{:S(2)}, u32[]{:S(2)}) collective-permute-start(f32[64,128]{1,0:T(8,128)S(1)} %pad_maximum_fusion.3), channel_id=1, source_target_pairs={{0,2},{1,3},{2,0},{3,1},{4,6},{5,7},{6,4},{7,5},{8,10},{9,11},{10,... | collective-permute-start | bytes 98312 | tf_op jit(solution)/shard_map/ppermute | solution.py:395
  61.3 2.5 %collective-permute-done.14 = f32[64,128]{1,0:T(8,128)S(1)} collective-permute-done((f32[64,128]{1,0:T(8,128)S(1)}, f32[64,128]{1,0:T(8,128)S(1)}, u32[]{:S(2)}, u32[]{:S(2)}) %collective-permute-start.14) | collective-permute-done | bytes 32800 | tf_op jit(solution)/shard_map/ppermute | solution.py:395
  63.7 0.8 collective-permute-start.15
  64.6 3.3 %collective-permute-done.15 = f32[64,128]{1,0:T(8,128)S(1)} collective-permute-done((f32[64,128]{1,0:T(8,128)S(1)}, f32[64,128]{1,0:T(8,128)S(1)}, u32[]{:S(2)}, u32[]{:S(2)}) %collective-permute-start.15) | collective-permute-done | bytes 32800 | tf_op jit(solution)/shard_map/ppermute | solution.py:395
  67.8 1.4 %collective-permute-start.16 = (f32[64,128]{1,0:T(8,128)S(1)}, f32[64,128]{1,0:T(8,128)S(1)}, u32[]{:S(2)}, u32[]{:S(2)}) collective-permute-start(f32[64,128]{1,0:T(8,128)S(1)} %pad_maximum_fusion.3), channel_id=1, source_target_pairs={{0,6},{1,7},{2,4},{3,5},{4,2},{5,3},{6,0},{7,1},{8,14},{9,15},{10,... | collective-permute-start | bytes 98312 | tf_op jit(solution)/shard_map/ppermute | solution.py:395
  69.3 3.4 %collective-permute-done.16 = f32[64,128]{1,0:T(8,128)S(1)} collective-permute-done((f32[64,128]{1,0:T(8,128)S(1)}, f32[64,128]{1,0:T(8,128)S(1)}, u32[]{:S(2)}, u32[]{:S(2)}) %collective-permute-start.16) | collective-permute-done | bytes 32800 | tf_op jit(solution)/shard_map/ppermute | solution.py:395
  72.7 1.5 %shard_map.120 = bf16[384,768]{1,0:T(8,128)(2,1)S(1)} custom-call(bf16[384,256]{1,0:T(8,128)(2,1)S(1)} %get-tuple-element.44.refs_0_, bf16[384,256]{1,0:T(8,128)(2,1)S(1)} %collective-permute-done.34.refs_1_, bf16[256,768]{1,0:T(8,128)(2,1)} %refs_2_.1, bf16[256,768]{1,0:T(8,128)(2,1)S(1)} %collective-permute-done.35.refs_3_), custom_call_target="tpu_custom_call" | custom-call | flops 301989888 | bytes 1769472 | tf_op jit(solution)/shard_map/pallas_call | solution.py:379
  74.2 1.5 %collective-permute-start.36 = (bf16[96,768]{1,0:T(8,128)(2,1)S(1)}, bf16[96,768]{1,0:T(8,128)(2,1)S(1)}, u32[]{:S(2)}, u32[]{:S(2)}) collective-permute-start(bf16[96,768]{1,0:T(8,128)(2,1)S(1)} %get-tuple-element.49), channel_id=1, source_target_pairs={{0,2},{1,3},{2,0},{3,1},{4,6},{5,7},{6,4},{7,5},{8,10},{9,11},{10,... | collective-permute-start | bytes 442376 | tf_op jit(solution)/shard_map/ppermute | solution.py:395
  76.2 1.5 %collective-permute-start.38 = (bf16[96,768]{1,0:T(8,128)(2,1)S(1)}, bf16[96,768]{1,0:T(8,128)(2,1)S(1)}, u32[]{:S(2)}, u32[]{:S(2)}) collective-permute-start(bf16[96,768]{1,0:T(8,128)(2,1)S(1)} %get-tuple-element.50), channel_id=1, source_target_pairs={{0,6},{1,7},{2,4},{3,5},{4,2},{5,3},{6,0},{7,1},{8,14},{9,15},{10,... | collective-permute-start | bytes 442376 | tf_op jit(solution)/shard_map/ppermute | solution.py:395
  77.8 6.3 %shard_map.115 = (bf16[256,768]{1,0:T(8,128)(2,1)S(1)}, f32[256,768]{1,0:T(8,128)S(1)}, f32[256,768]{1,0:T(8,128)S(1)}) custom-call(s32[2,12]{1,0:T(2,128)S(1)} %copy-done.7, s32[1]{0:T(128)S(6)} %copy.30.pad_ref, bf16[256,768]{1,0:T(8,128)(2,1)S(1)} %get-tuple-element.27.q, bf16[256,768]{1,0:T(8,128)(2,1)S(1)} %get-tuple-element.28.k, ...), custom_call_target="tpu_custom_call" | custom-call | flops 805306368 | bytes 5668964 | tf_op jit(solution)/shard_map/pallas_call | solution.py:379
  84.2 3.8 %shard_map.116 = (bf16[256,768]{1,0:T(8,128)(2,1)S(1)}, bf16[256,768]{1,0:T(8,128)(2,1)S(1)}) custom-call(s32[2,12]{1,0:T(2,128)S(1)} %copy-done.7, s32[1]{0:T(128)S(6)} %copy.30.pad_ref, bf16[64,3072]{1,0:T(8,128)(2,1)S(1)} %get-tuple-element.25.sel, bf16[256,1536]{1,0:T(8,128)(2,1)S(1)} %constant_dynamic-update-slice_fusion.9.first, ...), custom_call_target="tpu_custom_call" | custom-call | flops 301989888 | bytes 4587620 | tf_op jit(solution)/shard_map/pallas_call | solution.py:379
  88.8 1.2 collective-permute-start.40
  90.0 3.1 %collective-permute-start.41 = (bf16[24,768]{1,0:T(8,128)(2,1)S(1)}, bf16[24,768]{1,0:T(8,128)(2,1)S(1)}, u32[]{:S(2)}, u32[]{:S(2)}) collective-permute-start(bf16[24,768]{1,0:T(8,128)(2,1)S(1)} %get-tuple-element.71), channel_id=1, source_target_pairs={{0,24},{1,25},{2,26},{3,27},{4,28},{5,29},{6,30},{7,31},{8,16},{9,... | collective-permute-start | bytes 110600 | tf_op jit(solution)/shard_map/ppermute | solution.py:395
  93.2 1.9 %shard_map.117 = bf16[256,768]{1,0:T(8,128)(2,1)} custom-call(bf16[256,768]{1,0:T(8,128)(2,1)S(1)} %get-tuple-element.37.dq.refs_2_, bf16[256,768]{1,0:T(8,128)(2,1)S(1)} %get-tuple-element.40.dk.refs_2_, bf16[256,768]{1,0:T(8,128)(2,1)S(1)} %get-tuple-element.41.dv.refs_3_, bf16[768,2304]{1,0:T(8,128)(2,1)S(1)} %copy-done.1), custom_call_target="tpu_custom_call" | custom-call | flops 905969664 | bytes 5111808 | tf_op jit(solution)/shard_map/pallas_call | solution.py:379
  97.1 3.6 %collective-permute-start.21 = (bf16[96,768]{1,0:T(8,128)(2,1)S(1)}, bf16[96,768]{1,0:T(8,128)(2,1)S(1)}, u32[]{:S(2)}, u32[]{:S(2)}) collective-permute-start(bf16[96,768]{1,0:T(8,128)(2,1)S(1)} %get-tuple-element.54), channel_id=1, source_target_pairs={{0,16},{1,17},{2,18},{3,19},{4,20},{5,21},{6,22},{7,23},{8,24},{9,... | collective-permute-start | bytes 442376 | tf_op jit(solution)/shard_map/ppermute | solution.py:395
  102.3 1.6 %collective-permute-start.28 = (bf16[96,1536]{1,0:T(8,128)(2,1)S(1)}, bf16[96,1536]{1,0:T(8,128)(2,1)S(1)}, u32[]{:S(2)}, u32[]{:S(2)}) collective-permute-start(bf16[96,1536]{1,0:T(8,128)(2,1)S(1)} %get-tuple-element.46), channel_id=1, source_target_pairs={{0,2},{1,3},{2,0},{3,1},{4,6},{5,7},{6,4},{7,5},{8,10},{9,11},{10,... | collective-permute-start | bytes 884744 | tf_op jit(solution)/shard_map/ppermute | solution.py:395
  105.1 1.4 %collective-permute-start.30 = (bf16[96,1536]{1,0:T(8,128)(2,1)S(1)}, bf16[96,1536]{1,0:T(8,128)(2,1)S(1)}, u32[]{:S(2)}, u32[]{:S(2)}) collective-permute-start(bf16[96,1536]{1,0:T(8,128)(2,1)S(1)} %get-tuple-element.47), channel_id=1, source_target_pairs={{0,6},{1,7},{2,4},{3,5},{4,2},{5,3},{6,0},{7,1},{8,14},{9,15},{10,... | collective-permute-start | bytes 884744 | tf_op jit(solution)/shard_map/ppermute | solution.py:395
  106.5 4.8 %collective-permute-done.21 = bf16[96,768]{1,0:T(8,128)(2,1)S(1)} collective-permute-done((bf16[96,768]{1,0:T(8,128)(2,1)S(1)}, bf16[96,768]{1,0:T(8,128)(2,1)S(1)}, u32[]{:S(2)}, u32[]{:S(2)}) %collective-permute-start.21) | collective-permute-done | bytes 147488 | tf_op jit(solution)/shard_map/ppermute | solution.py:395
  111.4 1.5 %collective-permute-start.23 = (bf16[24,768]{1,0:T(8,128)(2,1)S(1)}, bf16[24,768]{1,0:T(8,128)(2,1)S(1)}, u32[]{:S(2)}, u32[]{:S(2)}) collective-permute-start(bf16[24,768]{1,0:T(8,128)(2,1)S(1)} %get-tuple-element.73), channel_id=1, source_target_pairs={{0,2},{1,3},{2,0},{3,1},{4,6},{5,7},{6,4},{7,5},{8,10},{9,11},{10,... | collective-permute-start | bytes 110600 | tf_op jit(solution)/shard_map/ppermute | solution.py:395
  113.5 1.5 %collective-permute-start.25 = (bf16[24,768]{1,0:T(8,128)(2,1)S(1)}, bf16[24,768]{1,0:T(8,128)(2,1)S(1)}, u32[]{:S(2)}, u32[]{:S(2)}) collective-permute-start(bf16[24,768]{1,0:T(8,128)(2,1)S(1)} %get-tuple-element.74), channel_id=1, source_target_pairs={{0,6},{1,7},{2,4},{3,5},{4,2},{5,3},{6,0},{7,1},{8,14},{9,15},{10,... | collective-permute-start | bytes 110600 | tf_op jit(solution)/shard_map/ppermute | solution.py:395
  115.0 3.9 %collective-permute-done.29 = bf16[96,1536]{1,0:T(8,128)(2,1)S(1)} collective-permute-done((bf16[96,1536]{1,0:T(8,128)(2,1)S(1)}, bf16[96,1536]{1,0:T(8,128)(2,1)S(1)}, u32[]{:S(2)}, u32[]{:S(2)}) %collective-permute-start.29) | collective-permute-done | bytes 294944 | tf_op jit(solution)/shard_map/ppermute | solution.py:395
  119.1 2.2 %collective-permute-start.32 = (bf16[24,1536]{1,0:T(8,128)(2,1)S(1)}, bf16[24,1536]{1,0:T(8,128)(2,1)S(1)}, u32[]{:S(2)}, u32[]{:S(2)}) collective-permute-start(bf16[24,1536]{1,0:T(8,128)(2,1)S(1)} %get-tuple-element.65), channel_id=1, source_target_pairs={{0,16},{1,17},{2,18},{3,19},{4,20},{5,21},{6,22},{7,23},{8,24},{9,... | collective-permute-start | bytes 221192 | tf_op jit(solution)/shard_map/ppermute | solution.py:395
  121.4 2.1 %collective-permute-start.33 = (bf16[24,1536]{1,0:T(8,128)(2,1)S(1)}, bf16[24,1536]{1,0:T(8,128)(2,1)S(1)}, u32[]{:S(2)}, u32[]{:S(2)}) collective-permute-start(bf16[24,1536]{1,0:T(8,128)(2,1)S(1)} %get-tuple-element.64), channel_id=1, source_target_pairs={{0,24},{1,25},{2,26},{3,27},{4,28},{5,29},{6,30},{7,31},{8,16},{9,... | collective-permute-start | bytes 221192 | tf_op jit(solution)/shard_map/ppermute | solution.py:395
  123.5 0.9 collective-permute-done.32
  124.4 3.1 %collective-permute-done.33 = bf16[24,1536]{1,0:T(8,128)(2,1)S(1)} collective-permute-done((bf16[24,1536]{1,0:T(8,128)(2,1)S(1)}, bf16[24,1536]{1,0:T(8,128)(2,1)S(1)}, u32[]{:S(2)}, u32[]{:S(2)}) %collective-permute-start.33) | collective-permute-done | bytes 73760 | tf_op jit(solution)/shard_map/ppermute | solution.py:395
  (103 shorter events, 10.9 us)
Async XLA Ops:
  0.6 2.0 %copy-start = (bf16[768,2304]{1,0:T(8,128)(2,1)S(1)}, bf16[768,2304]{1,0:T(8,128)(2,1)}, u32[]{:S(2)}) copy-start(bf16[768,2304]{1,0:T(8,128)(2,1)} %w_qkv.3) | copy-start | bytes 10616836
  5.6 9.1 %copy-start.8 = (s32[1536,1]{1,0:T(8,128)S(1)}, s32[1536,1]{1,0:T(8,128)}, u32[]{:S(2)}) copy-start(s32[1536,1]{1,0:T(8,128)} %constant.10.clone) | copy-start | bytes 18436
  8.3 10.7 %collective-permute-start = (bf16[8,3072]{1,0:T(8,128)(2,1)S(1)}, bf16[8,3072]{1,0:T(8,128)(2,1)S(1)}, u32[]{:S(2)}, u32[]{:S(2)}) collective-permute-start(bf16[8,3072]{1,0:T(8,128)(2,1)S(1)} %get-tuple-element.26), channel_id=1, source_target_pairs={{0,8},{1,9},{2,10},{3,11},{4,12},{5,13},{6,14},{7,15},{8,0},{9,1},... | collective-permute-start | bytes 147464 | tf_op jit(solution)/shard_map/ppermute | solution.py:395
  11.4 7.6 %collective-permute-start.1 = (bf16[8,3072]{1,0:T(8,128)(2,1)S(1)}, bf16[8,3072]{1,0:T(8,128)(2,1)S(1)}, u32[]{:S(2)}, u32[]{:S(2)}) collective-permute-start(bf16[8,3072]{1,0:T(8,128)(2,1)S(1)} %get-tuple-element.26), channel_id=1, source_target_pairs={{0,16},{1,17},{2,18},{3,19},{4,20},{5,21},{6,22},{7,23},{8,24},{9,... | collective-permute-start | bytes 147464 | tf_op jit(solution)/shard_map/ppermute | solution.py:395
  14.0 5.9 %collective-permute-start.2 = (bf16[8,3072]{1,0:T(8,128)(2,1)S(1)}, bf16[8,3072]{1,0:T(8,128)(2,1)S(1)}, u32[]{:S(2)}, u32[]{:S(2)}) collective-permute-start(bf16[8,3072]{1,0:T(8,128)(2,1)S(1)} %get-tuple-element.26), channel_id=1, source_target_pairs={{0,24},{1,25},{2,26},{3,27},{4,28},{5,29},{6,30},{7,31},{8,16},{9,... | collective-permute-start | bytes 147464 | tf_op jit(solution)/shard_map/ppermute | solution.py:395
  14.0 58.6 %collective-permute-start.35 = (bf16[256,768]{1,0:T(8,128)(2,1)}, bf16[256,768]{1,0:T(8,128)(2,1)S(1)}, u32[]{:S(2)}, u32[]{:S(2)}) collective-permute-start(bf16[256,768]{1,0:T(8,128)(2,1)} %refs_2_.1), channel_id=1, source_target_pairs={{0,1},{1,0},{2,3},{3,2},{4,5},{5,4},{6,7},{7,6},{8,9},{9,8},{10,11... | collective-permute-start | bytes 1179656 | tf_op jit(solution)/shard_map/ppermute | solution.py:395
  14.7 1.3 %copy-start.5 = (bf16[256,768]{1,0:T(8,128)(2,1)S(1)}, bf16[256,768]{1,0:T(8,128)(2,1)}, u32[]{:S(2)}) copy-start(bf16[256,768]{1,0:T(8,128)(2,1)} %tiles.5) | copy-start | bytes 1179652
  18.4 57.9 %collective-permute-start.18 = (bf16[768,256]{1,0:T(8,128)(2,1)S(1)}, bf16[768,256]{1,0:T(8,128)(2,1)S(1)}, u32[]{:S(2)}, u32[]{:S(2)}) collective-permute-start(bf16[768,256]{1,0:T(8,128)(2,1)S(1)} %get-tuple-element.43), channel_id=1, source_target_pairs={{0,1},{1,0},{2,3},{3,2},{4,5},{5,4},{6,7},{7,6},{8,9},{9,8},{10,11... | collective-permute-start | bytes 1179656 | tf_op jit(solution)/shard_map/ppermute | solution.py:395
  20.0 7.7 %collective-permute-start.3 = (bf16[64,1536]{1,0:T(8,128)(2,1)S(1)}, bf16[64,1536]{1,0:T(8,128)(2,1)S(1)}, u32[]{:S(2)}, u32[]{:S(2)}) collective-permute-start(bf16[64,1536]{1,0:T(8,128)(2,1)S(1)} %pad_maximum_fusion.1), channel_id=1, source_target_pairs={{0,2},{1,3},{2,0},{3,1},{4,6},{5,7},{6,4},{7,5},{8,10},{9,11},{10,... | collective-permute-start | bytes 589832 | tf_op jit(solution)/shard_map/ppermute | solution.py:395
  21.5 8.9 %collective-permute-start.4 = (bf16[64,1536]{1,0:T(8,128)(2,1)S(1)}, bf16[64,1536]{1,0:T(8,128)(2,1)S(1)}, u32[]{:S(2)}, u32[]{:S(2)}) collective-permute-start(bf16[64,1536]{1,0:T(8,128)(2,1)S(1)} %pad_maximum_fusion.1), channel_id=1, source_target_pairs={{0,4},{1,5},{2,6},{3,7},{4,0},{5,1},{6,2},{7,3},{8,12},{9,13},{10,... | collective-permute-start | bytes 589832 | tf_op jit(solution)/shard_map/ppermute | solution.py:395
  23.0 10.0 %collective-permute-start.5 = (bf16[64,1536]{1,0:T(8,128)(2,1)S(1)}, bf16[64,1536]{1,0:T(8,128)(2,1)S(1)}, u32[]{:S(2)}, u32[]{:S(2)}) collective-permute-start(bf16[64,1536]{1,0:T(8,128)(2,1)S(1)} %pad_maximum_fusion.1), channel_id=1, source_target_pairs={{0,6},{1,7},{2,4},{3,5},{4,2},{5,3},{6,0},{7,1},{8,14},{9,15},{10,... | collective-permute-start | bytes 589832 | tf_op jit(solution)/shard_map/ppermute | solution.py:395
  27.6 6.8 %collective-permute-start.7 = (bf16[64,1536]{1,0:T(8,128)(2,1)S(1)}, bf16[64,1536]{1,0:T(8,128)(2,1)S(1)}, u32[]{:S(2)}, u32[]{:S(2)}) collective-permute-start(bf16[64,1536]{1,0:T(8,128)(2,1)S(1)} %pad_maximum_fusion.2), channel_id=1, source_target_pairs={{0,2},{1,3},{2,0},{3,1},{4,6},{5,7},{6,4},{7,5},{8,10},{9,11},{10,... | collective-permute-start | bytes 589832 | tf_op jit(solution)/shard_map/ppermute | solution.py:395
  30.4 14.4 %copy-start.7 = (s32[2,12]{1,0:T(2,128)S(1)}, s32[2,12]{1,0:T(2,128)}, u32[]{:S(2)}) copy-start(s32[2,12]{1,0:T(2,128)} %offs_ref.7) | copy-start | bytes 292
  33.1 11.7 %collective-permute-start.6 = (bf16[256,1536]{1,0:T(8,128)(2,1)S(1)}, bf16[256,1536]{1,0:T(8,128)(2,1)S(1)}, u32[]{:S(2)}, u32[]{:S(2)}) collective-permute-start(bf16[256,1536]{1,0:T(8,128)(2,1)S(1)} %constant_dynamic-update-slice_fusion.4.first), channel_id=1, source_target_pairs={{0,1},{1,0},{2,3},{3,2},{4,5},{5,4},{6,7},{7,6},{8,9},{9,8},{10,11... | collective-permute-start | bytes 2359304 | tf_op jit(solution)/shard_map/ppermute | solution.py:395
  33.2 11.6 %collective-permute-start.8 = (bf16[64,1536]{1,0:T(8,128)(2,1)S(1)}, bf16[64,1536]{1,0:T(8,128)(2,1)S(1)}, u32[]{:S(2)}, u32[]{:S(2)}) collective-permute-start(bf16[64,1536]{1,0:T(8,128)(2,1)S(1)} %pad_maximum_fusion.2), channel_id=1, source_target_pairs={{0,4},{1,5},{2,6},{3,7},{4,0},{5,1},{6,2},{7,3},{8,12},{9,13},{10,... | collective-permute-start | bytes 589832 | tf_op jit(solution)/shard_map/ppermute | solution.py:395
  34.4 10.3 %collective-permute-start.9 = (bf16[64,1536]{1,0:T(8,128)(2,1)S(1)}, bf16[64,1536]{1,0:T(8,128)(2,1)S(1)}, u32[]{:S(2)}, u32[]{:S(2)}) collective-permute-start(bf16[64,1536]{1,0:T(8,128)(2,1)S(1)} %pad_maximum_fusion.2), channel_id=1, source_target_pairs={{0,6},{1,7},{2,4},{3,5},{4,2},{5,3},{6,0},{7,1},{8,14},{9,15},{10,... | collective-permute-start | bytes 589832 | tf_op jit(solution)/shard_map/ppermute | solution.py:395
  44.8 10.4 %copy-start.3 = (bf16[768,768]{1,0:T(8,128)(2,1)S(1)}, bf16[768,768]{1,0:T(8,128)(2,1)}, u32[]{:S(2)}) copy-start(bf16[768,768]{1,0:T(8,128)(2,1)} %w_out.3) | copy-start | bytes 3538948
  50.8 5.9 %collective-permute-start.11 = (f32[8,128]{1,0:T(8,128)S(1)}, f32[8,128]{1,0:T(8,128)S(1)}, u32[]{:S(2)}, u32[]{:S(2)}) collective-permute-start(f32[8,128]{1,0:T(8,128)S(1)} %slice.109), channel_id=1, source_target_pairs={{0,8},{1,9},{2,10},{3,11},{4,12},{5,13},{6,14},{7,15},{8,0},{9,1},... | collective-permute-start | bytes 12296 | tf_op jit(solution)/shard_map/ppermute | solution.py:395
  50.9 5.8 %collective-permute-start.12 = (f32[8,128]{1,0:T(8,128)S(1)}, f32[8,128]{1,0:T(8,128)S(1)}, u32[]{:S(2)}, u32[]{:S(2)}) collective-permute-start(f32[8,128]{1,0:T(8,128)S(1)} %slice.109), channel_id=1, source_target_pairs={{0,16},{1,17},{2,18},{3,19},{4,20},{5,21},{6,22},{7,23},{8,24},{9,... | collective-permute-start | bytes 12296 | tf_op jit(solution)/shard_map/ppermute | solution.py:395
  54.4 5.4 %collective-permute-start.13 = (f32[8,128]{1,0:T(8,128)S(1)}, f32[8,128]{1,0:T(8,128)S(1)}, u32[]{:S(2)}, u32[]{:S(2)}) collective-permute-start(f32[8,128]{1,0:T(8,128)S(1)} %slice.109), channel_id=1, source_target_pairs={{0,24},{1,25},{2,26},{3,27},{4,28},{5,29},{6,30},{7,31},{8,16},{9,... | collective-permute-start | bytes 12296 | tf_op jit(solution)/shard_map/ppermute | solution.py:395
  56.7 27.4 %collective-permute-start.10 = (bf16[256,1536]{1,0:T(8,128)(2,1)S(1)}, bf16[256,1536]{1,0:T(8,128)(2,1)S(1)}, u32[]{:S(2)}, u32[]{:S(2)}) collective-permute-start(bf16[256,1536]{1,0:T(8,128)(2,1)S(1)} %constant_dynamic-update-slice_fusion.9.first), channel_id=1, source_target_pairs={{0,1},{1,0},{2,3},{3,2},{4,5},{5,4},{6,7},{7,6},{8,9},{9,8},{10,11... | collective-permute-start | bytes 2359304 | tf_op jit(solution)/shard_map/ppermute | solution.py:395
  56.7 15.9 %collective-permute-start.34 = (bf16[384,256]{1,0:T(8,128)(2,1)S(1)}, bf16[384,256]{1,0:T(8,128)(2,1)S(1)}, u32[]{:S(2)}, u32[]{:S(2)}) collective-permute-start(bf16[384,256]{1,0:T(8,128)(2,1)S(1)} %get-tuple-element.45), channel_id=1, source_target_pairs={{0,1},{1,0},{2,3},{3,2},{4,5},{5,4},{6,7},{7,6},{8,9},{9,8},{10,11... | collective-permute-start | bytes 589832 | tf_op jit(solution)/shard_map/ppermute | solution.py:395
  59.8 3.9 %collective-permute-start.14 = (f32[64,128]{1,0:T(8,128)S(1)}, f32[64,128]{1,0:T(8,128)S(1)}, u32[]{:S(2)}, u32[]{:S(2)}) collective-permute-start(f32[64,128]{1,0:T(8,128)S(1)} %pad_maximum_fusion.3), channel_id=1, source_target_pairs={{0,2},{1,3},{2,0},{3,1},{4,6},{5,7},{6,4},{7,5},{8,10},{9,11},{10,... | collective-permute-start | bytes 98312 | tf_op jit(solution)/shard_map/ppermute | solution.py:395
  63.7 4.1 %collective-permute-start.15 = (f32[64,128]{1,0:T(8,128)S(1)}, f32[64,128]{1,0:T(8,128)S(1)}, u32[]{:S(2)}, u32[]{:S(2)}) collective-permute-start(f32[64,128]{1,0:T(8,128)S(1)} %pad_maximum_fusion.3), channel_id=1, source_target_pairs={{0,4},{1,5},{2,6},{3,7},{4,0},{5,1},{6,2},{7,3},{8,12},{9,13},{10,... | collective-permute-start | bytes 98312 | tf_op jit(solution)/shard_map/ppermute | solution.py:395
  67.8 4.8 %collective-permute-start.16 = (f32[64,128]{1,0:T(8,128)S(1)}, f32[64,128]{1,0:T(8,128)S(1)}, u32[]{:S(2)}, u32[]{:S(2)}) collective-permute-start(f32[64,128]{1,0:T(8,128)S(1)} %pad_maximum_fusion.3), channel_id=1, source_target_pairs={{0,6},{1,7},{2,4},{3,5},{4,2},{5,3},{6,0},{7,1},{8,14},{9,15},{10,... | collective-permute-start | bytes 98312 | tf_op jit(solution)/shard_map/ppermute | solution.py:395
  72.6 11.6 %collective-permute-start.17 = (f32[256,128]{1,0:T(8,128)S(1)}, f32[256,128]{1,0:T(8,128)S(1)}, u32[]{:S(2)}, u32[]{:S(2)}) collective-permute-start(f32[256,128]{1,0:T(8,128)S(1)} %constant_dynamic-update-slice_fusion.14.first_stats), channel_id=1, source_target_pairs={{0,1},{1,0},{2,3},{3,2},{4,5},{5,4},{6,7},{7,6},{8,9},{9,8},{10,11... | collective-permute-start | bytes 393224 | tf_op jit(solution)/shard_map/ppermute | solution.py:395
  74.2 14.4 %collective-permute-start.36 = (bf16[96,768]{1,0:T(8,128)(2,1)S(1)}, bf16[96,768]{1,0:T(8,128)(2,1)S(1)}, u32[]{:S(2)}, u32[]{:S(2)}) collective-permute-start(bf16[96,768]{1,0:T(8,128)(2,1)S(1)} %get-tuple-element.49), channel_id=1, source_target_pairs={{0,2},{1,3},{2,0},{3,1},{4,6},{5,7},{6,4},{7,5},{8,10},{9,11},{10,... | collective-permute-start | bytes 442376 | tf_op jit(solution)/shard_map/ppermute | solution.py:395
  75.7 12.9 %collective-permute-start.37 = (bf16[96,768]{1,0:T(8,128)(2,1)S(1)}, bf16[96,768]{1,0:T(8,128)(2,1)S(1)}, u32[]{:S(2)}, u32[]{:S(2)}) collective-permute-start(bf16[96,768]{1,0:T(8,128)(2,1)S(1)} %get-tuple-element.51), channel_id=1, source_target_pairs={{0,4},{1,5},{2,6},{3,7},{4,0},{5,1},{6,2},{7,3},{8,12},{9,13},{10,... | collective-permute-start | bytes 442376 | tf_op jit(solution)/shard_map/ppermute | solution.py:395
  76.2 12.4 %collective-permute-start.38 = (bf16[96,768]{1,0:T(8,128)(2,1)S(1)}, bf16[96,768]{1,0:T(8,128)(2,1)S(1)}, u32[]{:S(2)}, u32[]{:S(2)}) collective-permute-start(bf16[96,768]{1,0:T(8,128)(2,1)S(1)} %get-tuple-element.50), channel_id=1, source_target_pairs={{0,6},{1,7},{2,4},{3,5},{4,2},{5,3},{6,0},{7,1},{8,14},{9,15},{10,... | collective-permute-start | bytes 442376 | tf_op jit(solution)/shard_map/ppermute | solution.py:395
  84.1 12.3 %collective-permute-start.19 = (bf16[256,768]{1,0:T(8,128)(2,1)S(1)}, bf16[256,768]{1,0:T(8,128)(2,1)S(1)}, u32[]{:S(2)}, u32[]{:S(2)}) collective-permute-start(bf16[256,768]{1,0:T(8,128)(2,1)S(1)} %get-tuple-element.37.dq.refs_2_), channel_id=1, source_target_pairs={{0,1},{1,0},{2,3},{3,2},{4,5},{5,4},{6,7},{7,6},{8,9},{9,8},{10,11... | collective-permute-start | bytes 1179656 | tf_op jit(solution)/shard_map/ppermute | solution.py:395
  84.2 9.0 %copy-start.1 = (bf16[768,2304]{1,0:T(8,128)(2,1)S(1)}, bf16[768,2304]{1,0:T(8,128)(2,1)}, u32[]{:S(2)}) copy-start(bf16[768,2304]{1,0:T(8,128)(2,1)} %w_qkv.3) | copy-start | bytes 10616836
  88.1 13.4 %collective-permute-start.26 = (bf16[256,768]{1,0:T(8,128)(2,1)S(1)}, bf16[256,768]{1,0:T(8,128)(2,1)S(1)}, u32[]{:S(2)}, u32[]{:S(2)}) collective-permute-start(bf16[256,768]{1,0:T(8,128)(2,1)S(1)} %get-tuple-element.40.dk.refs_2_), channel_id=1, source_target_pairs={{0,1},{1,0},{2,3},{3,2},{4,5},{5,4},{6,7},{7,6},{8,9},{9,8},{10,11... | collective-permute-start | bytes 1179656 | tf_op jit(solution)/shard_map/ppermute | solution.py:395
  88.7 6.3 %collective-permute-start.39 = (bf16[24,768]{1,0:T(8,128)(2,1)S(1)}, bf16[24,768]{1,0:T(8,128)(2,1)S(1)}, u32[]{:S(2)}, u32[]{:S(2)}) collective-permute-start(bf16[24,768]{1,0:T(8,128)(2,1)S(1)} %get-tuple-element.70), channel_id=1, source_target_pairs={{0,8},{1,9},{2,10},{3,11},{4,12},{5,13},{6,14},{7,15},{8,0},{9,1},... | collective-permute-start | bytes 110600 | tf_op jit(solution)/shard_map/ppermute | solution.py:395
  88.8 6.2 %collective-permute-start.40 = (bf16[24,768]{1,0:T(8,128)(2,1)S(1)}, bf16[24,768]{1,0:T(8,128)(2,1)S(1)}, u32[]{:S(2)}, u32[]{:S(2)}) collective-permute-start(bf16[24,768]{1,0:T(8,128)(2,1)S(1)} %get-tuple-element.72), channel_id=1, source_target_pairs={{0,16},{1,17},{2,18},{3,19},{4,20},{5,21},{6,22},{7,23},{8,24},{9,... | collective-permute-start | bytes 110600 | tf_op jit(solution)/shard_map/ppermute | solution.py:395
  90.0 5.8 %collective-permute-start.41 = (bf16[24,768]{1,0:T(8,128)(2,1)S(1)}, bf16[24,768]{1,0:T(8,128)(2,1)S(1)}, u32[]{:S(2)}, u32[]{:S(2)}) collective-permute-start(bf16[24,768]{1,0:T(8,128)(2,1)S(1)} %get-tuple-element.71), channel_id=1, source_target_pairs={{0,24},{1,25},{2,26},{3,27},{4,28},{5,29},{6,30},{7,31},{8,16},{9,... | collective-permute-start | bytes 110600 | tf_op jit(solution)/shard_map/ppermute | solution.py:395
  95.0 6.4 %collective-permute-start.27 = (bf16[256,768]{1,0:T(8,128)(2,1)S(1)}, bf16[256,768]{1,0:T(8,128)(2,1)S(1)}, u32[]{:S(2)}, u32[]{:S(2)}) collective-permute-start(bf16[256,768]{1,0:T(8,128)(2,1)S(1)} %get-tuple-element.41.dv.refs_3_), channel_id=1, source_target_pairs={{0,1},{1,0},{2,3},{3,2},{4,5},{5,4},{6,7},{7,6},{8,9},{9,8},{10,11... | collective-permute-start | bytes 1179656 | tf_op jit(solution)/shard_map/ppermute | solution.py:395
  97.0 8.1 %collective-permute-start.20 = (bf16[96,768]{1,0:T(8,128)(2,1)S(1)}, bf16[96,768]{1,0:T(8,128)(2,1)S(1)}, u32[]{:S(2)}, u32[]{:S(2)}) collective-permute-start(bf16[96,768]{1,0:T(8,128)(2,1)S(1)} %get-tuple-element.52), channel_id=1, source_target_pairs={{0,8},{1,9},{2,10},{3,11},{4,12},{5,13},{6,14},{7,15},{8,0},{9,1},... | collective-permute-start | bytes 442376 | tf_op jit(solution)/shard_map/ppermute | solution.py:395
  97.1 14.2 %collective-permute-start.21 = (bf16[96,768]{1,0:T(8,128)(2,1)S(1)}, bf16[96,768]{1,0:T(8,128)(2,1)S(1)}, u32[]{:S(2)}, u32[]{:S(2)}) collective-permute-start(bf16[96,768]{1,0:T(8,128)(2,1)S(1)} %get-tuple-element.54), channel_id=1, source_target_pairs={{0,16},{1,17},{2,18},{3,19},{4,20},{5,21},{6,22},{7,23},{8,24},{9,... | collective-permute-start | bytes 442376 | tf_op jit(solution)/shard_map/ppermute | solution.py:395
  100.7 10.6 %collective-permute-start.22 = (bf16[96,768]{1,0:T(8,128)(2,1)S(1)}, bf16[96,768]{1,0:T(8,128)(2,1)S(1)}, u32[]{:S(2)}, u32[]{:S(2)}) collective-permute-start(bf16[96,768]{1,0:T(8,128)(2,1)S(1)} %get-tuple-element.53), channel_id=1, source_target_pairs={{0,24},{1,25},{2,26},{3,27},{4,28},{5,29},{6,30},{7,31},{8,16},{9,... | collective-permute-start | bytes 442376 | tf_op jit(solution)/shard_map/ppermute | solution.py:395
  102.3 11.2 %collective-permute-start.28 = (bf16[96,1536]{1,0:T(8,128)(2,1)S(1)}, bf16[96,1536]{1,0:T(8,128)(2,1)S(1)}, u32[]{:S(2)}, u32[]{:S(2)}) collective-permute-start(bf16[96,1536]{1,0:T(8,128)(2,1)S(1)} %get-tuple-element.46), channel_id=1, source_target_pairs={{0,2},{1,3},{2,0},{3,1},{4,6},{5,7},{6,4},{7,5},{8,10},{9,11},{10,... | collective-permute-start | bytes 884744 | tf_op jit(solution)/shard_map/ppermute | solution.py:395
  103.9 15.0 %collective-permute-start.29 = (bf16[96,1536]{1,0:T(8,128)(2,1)S(1)}, bf16[96,1536]{1,0:T(8,128)(2,1)S(1)}, u32[]{:S(2)}, u32[]{:S(2)}) collective-permute-start(bf16[96,1536]{1,0:T(8,128)(2,1)S(1)} %get-tuple-element.48), channel_id=1, source_target_pairs={{0,4},{1,5},{2,6},{3,7},{4,0},{5,1},{6,2},{7,3},{8,12},{9,13},{10,... | collective-permute-start | bytes 884744 | tf_op jit(solution)/shard_map/ppermute | solution.py:395
  105.1 13.8 %collective-permute-start.30 = (bf16[96,1536]{1,0:T(8,128)(2,1)S(1)}, bf16[96,1536]{1,0:T(8,128)(2,1)S(1)}, u32[]{:S(2)}, u32[]{:S(2)}) collective-permute-start(bf16[96,1536]{1,0:T(8,128)(2,1)S(1)} %get-tuple-element.47), channel_id=1, source_target_pairs={{0,6},{1,7},{2,4},{3,5},{4,2},{5,3},{6,0},{7,1},{8,14},{9,15},{10,... | collective-permute-start | bytes 884744 | tf_op jit(solution)/shard_map/ppermute | solution.py:395
  111.4 10.0 %collective-permute-start.23 = (bf16[24,768]{1,0:T(8,128)(2,1)S(1)}, bf16[24,768]{1,0:T(8,128)(2,1)S(1)}, u32[]{:S(2)}, u32[]{:S(2)}) collective-permute-start(bf16[24,768]{1,0:T(8,128)(2,1)S(1)} %get-tuple-element.73), channel_id=1, source_target_pairs={{0,2},{1,3},{2,0},{3,1},{4,6},{5,7},{6,4},{7,5},{8,10},{9,11},{10,... | collective-permute-start | bytes 110600 | tf_op jit(solution)/shard_map/ppermute | solution.py:395
  112.9 10.6 %collective-permute-start.24 = (bf16[24,768]{1,0:T(8,128)(2,1)S(1)}, bf16[24,768]{1,0:T(8,128)(2,1)S(1)}, u32[]{:S(2)}, u32[]{:S(2)}) collective-permute-start(bf16[24,768]{1,0:T(8,128)(2,1)S(1)} %get-tuple-element.75), channel_id=1, source_target_pairs={{0,4},{1,5},{2,6},{3,7},{4,0},{5,1},{6,2},{7,3},{8,12},{9,13},{10,... | collective-permute-start | bytes 110600 | tf_op jit(solution)/shard_map/ppermute | solution.py:395
  113.5 10.0 %collective-permute-start.25 = (bf16[24,768]{1,0:T(8,128)(2,1)S(1)}, bf16[24,768]{1,0:T(8,128)(2,1)S(1)}, u32[]{:S(2)}, u32[]{:S(2)}) collective-permute-start(bf16[24,768]{1,0:T(8,128)(2,1)S(1)} %get-tuple-element.74), channel_id=1, source_target_pairs={{0,6},{1,7},{2,4},{3,5},{4,2},{5,3},{6,0},{7,1},{8,14},{9,15},{10,... | collective-permute-start | bytes 110600 | tf_op jit(solution)/shard_map/ppermute | solution.py:395
  119.0 4.5 %collective-permute-start.31 = (bf16[24,1536]{1,0:T(8,128)(2,1)S(1)}, bf16[24,1536]{1,0:T(8,128)(2,1)S(1)}, u32[]{:S(2)}, u32[]{:S(2)}) collective-permute-start(bf16[24,1536]{1,0:T(8,128)(2,1)S(1)} %get-tuple-element.63), channel_id=1, source_target_pairs={{0,8},{1,9},{2,10},{3,11},{4,12},{5,13},{6,14},{7,15},{8,0},{9,1},... | collective-permute-start | bytes 221192 | tf_op jit(solution)/shard_map/ppermute | solution.py:395
  119.1 5.3 %collective-permute-start.32 = (bf16[24,1536]{1,0:T(8,128)(2,1)S(1)}, bf16[24,1536]{1,0:T(8,128)(2,1)S(1)}, u32[]{:S(2)}, u32[]{:S(2)}) collective-permute-start(bf16[24,1536]{1,0:T(8,128)(2,1)S(1)} %get-tuple-element.65), channel_id=1, source_target_pairs={{0,16},{1,17},{2,18},{3,19},{4,20},{5,21},{6,22},{7,23},{8,24},{9,... | collective-permute-start | bytes 221192 | tf_op jit(solution)/shard_map/ppermute | solution.py:395
  121.4 6.2 %collective-permute-start.33 = (bf16[24,1536]{1,0:T(8,128)(2,1)S(1)}, bf16[24,1536]{1,0:T(8,128)(2,1)S(1)}, u32[]{:S(2)}, u32[]{:S(2)}) collective-permute-start(bf16[24,1536]{1,0:T(8,128)(2,1)S(1)} %get-tuple-element.64), channel_id=1, source_target_pairs={{0,24},{1,25},{2,26},{3,27},{4,28},{5,29},{6,30},{7,31},{8,16},{9,... | collective-permute-start | bytes 221192 | tf_op jit(solution)/shard_map/ppermute | solution.py:395
  (3 other events, 2.9 us)

commit v2 on v1

v2 whole, which is shorter than its diff:
```python
import functools

import jax
import jax.numpy as jnp
import numpy as np
from jax import lax
from jax.experimental import pallas as pl
from jax.experimental.pallas import tpu as pltpu
from jax.sharding import PartitionSpec as P

HEAD_DIM = 64
GROUP = 8
PAIR = 2 * HEAD_DIM
LANES = 128
SECOND = 16
SCALE = 0.125
BF = jnp.bfloat16
F32 = jnp.float32
NT = (((1,), (1,)), ((), ()))
NN = (((1,), (0,)), ((), ()))
TN = (((0,), (0,)), ((), ()))
LARGE = 1e30
VMEM_BYTES = 40 * 1024 * 1024


def dot(a, b, dims=NN):
    return lax.dot_general(a, b, dims, preferred_element_type=F32)


def dot_exact(a, b):
    return lax.dot_general(a, b, NN, preferred_element_type=F32, precision=lax.Precision.HIGHEST)


def iota(shape, dim):
    return lax.broadcasted_iota(jnp.int32, shape, dim)


def low_half(shape):
    return iota(shape, len(shape) - 1) % PAIR < HEAD_DIM


def halves(x):
    low = low_half(x.shape)
    zero = jnp.zeros((), x.dtype)
    return jnp.where(low, x, zero), jnp.where(low, zero, x)


def by_head(first, second, rows):
    return jnp.where(low_half((rows, PAIR)), first, second)


class Sizes:
    def __init__(self, rows, width, dev_count):
        self.rows = rows
        self.width = width
        self.devs = dev_count
        self.heads = width // HEAD_DIM
        self.pairs = self.heads // 2
        self.mid = rows // GROUP
        self.far = rows // dev_count
        self.sel = 2 * self.mid
        self.far_held = -(-self.far // 16) * 16
        self.upper = dev_count // GROUP
        self.strip = width // dev_count
        self.half = width // 2


def chosen_row(z, index, off_mid, off_far):
    row = jnp.where(index < z.mid, index * GROUP + off_mid, (index - z.mid) * z.devs + off_far)
    return jnp.where(index < z.mid + z.far, row, -1)


def spread(z, offs_ref, pair, picked):
    lane = iota((1, 4 * z.sel), 1)
    second = (lane // z.sel) % 2 == 1
    off_mid = jnp.where(second, offs_ref[0, 2 * pair + 1], offs_ref[0, 2 * pair])
    off_far = jnp.where(second, offs_ref[1, 2 * pair + 1], offs_ref[1, 2 * pair])
    target = chosen_row(z, lane % z.sel, off_mid, off_far)
    place = (iota((z.rows, 4 * z.sel), 0) == target).astype(F32).astype(BF)
    high = picked.astype(BF)
    rest = (picked - high.astype(F32)).astype(BF)
    first_high, second_high = halves(high)
    first_rest, second_rest = halves(rest)
    stacked = jnp.concatenate([first_high, second_high, first_rest, second_rest], axis=0)
    return dot(place, stacked)


def lane_offsets(z, offs_ref):
    lane = iota((1, LANES), 1)
    off_mid = jnp.full((1, LANES), -1, jnp.int32)
    off_far = jnp.full((1, LANES), -1, jnp.int32)
    for head in range(z.heads):
        here = (lane == head) | (lane == SECOND + head)
        off_mid = jnp.where(here, offs_ref[0, head], off_mid)
        off_far = jnp.where(here, offs_ref[1, head], off_far)
    return off_mid, off_far


def stat_masks(z, offs_ref):
    off_mid, off_far = lane_offsets(z, offs_ref)
    row = iota((z.rows, LANES), 0)
    return row % GROUP == off_mid, row % z.devs == off_far


def pick_stats(z, masks, stats):
    entry = iota((z.sel, z.rows), 0)
    row = iota((z.sel, z.rows), 1)
    take_mid = ((entry < z.mid) & (row // GROUP == entry)).astype(F32)
    take_far = (row // z.devs == entry - z.mid).astype(F32)
    return dot_exact(take_mid, jnp.where(masks[0], stats, 0.0)) + dot_exact(
        take_far, jnp.where(masks[1], stats, 0.0)
    )


def spread_stats(z, masks, picked):
    row = iota((z.rows, z.sel), 0)
    entry = iota((z.rows, z.sel), 1)
    give_mid = ((entry < z.mid) & (row // GROUP == entry)).astype(F32)
    give_far = (row // z.devs == entry - z.mid).astype(F32)
    fill = jnp.where(iota((z.rows, LANES), 1) < SECOND, -jnp.inf, 0.0)
    return (
        jnp.where(masks[0], dot_exact(give_mid, picked), fill),
        jnp.where(masks[1], dot_exact(give_far, picked), fill),
    )


def gathered_place(z, own, level):
    index = iota((1, z.rows), 1)
    core = index // (4 * z.mid)
    plane = (index // z.mid) % 4
    inner = index % z.mid
    if level == 0:
        return (own ^ (core + 2 * plane)) * z.rows + inner * GROUP
    dev = own ^ (core + 2 * plane + GROUP * (inner // z.far))
    return dev * z.rows + (inner % z.far) * z.devs


def level_parts(z):
    return ((0, z.mid), (z.mid, z.mid + z.far_held))


def project_kernel(z, offs_ref, tiles, w_qkv, cot, w_out, q, k, v, g, sel, far):
    width = z.width
    own = tiles[...]
    k[...] = dot(own, w_qkv[:, width : 2 * width]).astype(BF)
    v[...] = dot(own, w_qkv[:, 2 * width :]).astype(BF)
    q[...] = dot(own, w_qkv[:, :width]).astype(BF) * jnp.asarray(SCALE, BF)
    g[...] = dot(cot[...], w_out[...], NT).astype(BF)
    entry = iota((2 * z.sel, z.rows), 0)
    column = iota((2 * z.sel, z.rows), 1)
    second = entry >= z.sel
    for pair in range(z.pairs):
        lanes = slice(pair * PAIR, (pair + 1) * PAIR)
        off_mid = jnp.where(second, offs_ref[0, 2 * pair + 1], offs_ref[0, 2 * pair])
        off_far = jnp.where(second, offs_ref[1, 2 * pair + 1], offs_ref[1, 2 * pair])
        target = chosen_row(z, entry % z.sel, off_mid, off_far)
        take = (column == target).astype(F32).astype(BF)
        every = jnp.concatenate([k[:, lanes], v[:, lanes], q[:, lanes], g[:, lanes]], axis=1)
        both = dot(take, every)
        picked = jnp.where(low_half((z.sel, 4 * PAIR)), both[: z.sel], both[z.sel :]).astype(BF)
        far_part = jnp.where(
            low_half((z.far, 4 * PAIR)),
            both[z.mid : z.mid + z.far],
            both[z.sel + z.mid : z.sel + z.mid + z.far],
        ).astype(BF)
        for part in range(4):
            to = slice(part * width + pair * PAIR, part * width + (pair + 1) * PAIR)
            sel[:, to] = picked[:, part * PAIR : (part + 1) * PAIR]
            far[:, to] = far_part[:, part * PAIR : (part + 1) * PAIR]


def near_kernel(z, pad_ref, q, k, v, g, tiles, order, mixed, stats, turned, turned_out):
    own = lax.axis_index("ctx")
    limit = z.rows * z.devs - pad_ref[0] - own * z.rows
    valid = iota((1, z.rows), 1) < limit
    lane = iota((z.rows, LANES), 1)
    both = jnp.zeros((z.rows, LANES), F32)
    for pair in range(z.pairs):
        lanes = slice(pair * PAIR, (pair + 1) * PAIR)
        query = q[:, lanes]
        grad = g[:, lanes].astype(F32)
        keys = halves(k[:, lanes])
        values = halves(v[:, lanes])
        total = None
        for side in range(2):
            head = 2 * pair + side
            scores = jnp.where(valid, dot(query, keys[side], NT), -jnp.inf)
            peak = jnp.max(scores, axis=1, keepdims=True)
            powers = jnp.exp(scores - peak)
            summed = jnp.sum(powers, axis=1, keepdims=True)
            part = dot(powers.astype(BF), values[side]) * (1.0 / summed)
            total = part if total is None else total + part
            both = jnp.where(lane == head, peak + jnp.log(summed), both)
            meets = jnp.sum(grad * part, axis=1, keepdims=True)
            both = jnp.where(lane == SECOND + head, meets, both)
        mixed[:, lanes] = total
    stats[...] = both
    count = 2 * z.width
    for start in range(0, count, 256):
        rows = slice(start, start + 256)
        place = (iota((256, z.width), 1) == order[rows, :]).astype(F32).astype(BF)
        result = dot(place, tiles[...], NT).astype(BF)
        if start < z.width:
            turned[rows, :] = result
        else:
            turned_out[start - z.width : start - z.width + 256, :] = result


def gathered(pieces, lanes):
    return jnp.concatenate([piece[:, lanes] for piece in pieces], axis=0)


def join_kernel(
    z, offs_ref, pad_ref, sel, mid_0, mid_1, far_0, far_1, near_stats, stats, picked, held
):
    own = lax.axis_index("ctx")
    limit = z.rows * z.devs - pad_ref[0]
    places = [gathered_place(z, own, level) for level in range(2)]
    width = z.width
    pieces = ((mid_0, mid_1), (far_0, far_1))
    parts = level_parts(z)
    sel_stats = [jnp.zeros((stop - start, LANES), F32) for start, stop in parts]
    held_tail = z.sel - parts[1][1]
    for pair in range(z.pairs):
        lanes = slice(pair * PAIR, (pair + 1) * PAIR)
        value_lanes = slice(width + pair * PAIR, width + (pair + 1) * PAIR)
        query_lanes = slice(2 * width + pair * PAIR, 2 * width + (pair + 1) * PAIR)
        grad_lanes = slice(3 * width + pair * PAIR, 3 * width + (pair + 1) * PAIR)
        totals = []
        for level, (start, stop) in enumerate(parts):
            lane = iota((stop - start, LANES), 1)
            query = sel[start:stop, query_lanes]
            grad = sel[start:stop, grad_lanes].astype(F32)
            keys = halves(gathered(pieces[level], lanes))
            values = halves(gathered(pieces[level], value_lanes))
            total = None
            for side in range(2):
                head = 2 * pair + side
                valid = places[level] + offs_ref[level, head] < limit
                scores = jnp.where(valid, dot(query, keys[side], NT), -jnp.inf)
                peak = jnp.max(scores, axis=1, keepdims=True)
                powers = jnp.exp(scores - peak)
                summed = jnp.sum(powers, axis=1, keepdims=True)
                part = dot(powers.astype(BF), values[side]) * (1.0 / summed)
                total = part if total is None else total + part
                meets = jnp.sum(grad * part, axis=1, keepdims=True)
                here = jnp.where(lane == head, peak + jnp.log(summed), sel_stats[level])
                sel_stats[level] = jnp.where(lane == SECOND + head, meets, here)
            totals.append(total)
        totals.append(jnp.zeros((held_tail, PAIR), F32))
        held[:, lanes] = jnp.concatenate(totals, axis=0)
    sel_both = jnp.concatenate(sel_stats + [jnp.zeros((held_tail, LANES), F32)], axis=0)
    masks = stat_masks(z, offs_ref)
    near = near_stats[...]
    mid, far = spread_stats(z, masks, sel_both)
    top = jnp.maximum(near, jnp.maximum(mid, far))
    total_lse = top + jnp.log(jnp.exp(near - top) + jnp.exp(mid - top) + jnp.exp(far - top))
    delta = sum(
        pltpu.roll(jnp.exp(value - total_lse), SECOND, 1) * value
        for value in (
            near,
            jnp.where(masks[0], mid, -LARGE),
            jnp.where(masks[1], far, -LARGE),
        )
    )
    both = jnp.where(iota((z.rows, LANES), 1) < SECOND, total_lse, delta)
    stats[...] = both
    both_sel = pick_stats(z, masks, both)
    picked[...] = both_sel
    share = jnp.exp(sel_both - both_sel)
    for pair in range(z.pairs):
        lanes = slice(pair * PAIR, (pair + 1) * PAIR)
        held[:, lanes] = held[:, lanes] * by_head(
            share[:, 2 * pair : 2 * pair + 1], share[:, 2 * pair + 1 : 2 * pair + 2], z.sel
        )


def output_kernel(
    z, offs_ref, near_stats, stats, mixed, held, tiles, w_out, order, rows_out, turned, turned_out, attn
):
    near_share = jnp.exp(near_stats[...] - stats[...])
    for pair in range(z.pairs):
        lanes = slice(pair * PAIR, (pair + 1) * PAIR)
        near = by_head(
            near_share[:, 2 * pair : 2 * pair + 1],
            near_share[:, 2 * pair + 1 : 2 * pair + 2],
            z.rows,
        )
        combined = near * mixed[:, lanes] + spread(z, offs_ref, pair, held[:, lanes])
        attn[:, lanes] = combined.astype(BF)
    rows_out[...] = (tiles[...].astype(F32) + dot(attn[...], w_out[...])).astype(BF)
    for start in range(0, z.width, z.half):
        source = order[2 * start : 2 * start + z.half, :]
        place = (iota((z.half, z.width), 1) == source).astype(F32).astype(BF)
        result = dot(place, attn[...], NT).astype(BF)
        if start == 0:
            turned[...] = result
        else:
            turned_out[...] = result


def near_grads_kernel(
    z, offs_ref, pad_ref, q, k, v, g, stats, sel, mid_0, mid_1, far_0, far_1, picked, dq, dk, dv
):
    own = lax.axis_index("ctx")
    limit = z.rows * z.devs - pad_ref[0]
    places = [gathered_place(z, own, level) for level in range(2)]
    pieces = ((mid_0, mid_1), (far_0, far_1))
    parts = level_parts(z)
    held_tail = z.sel - parts[1][1]
    valid_near = iota((z.rows, 1), 0) < limit - own * z.rows
    across = jnp.transpose(stats[...])
    width = z.width
    for pair in range(z.pairs):
        lanes = slice(pair * PAIR, (pair + 1) * PAIR)
        value_lanes = slice(width + pair * PAIR, width + (pair + 1) * PAIR)
        query_lanes = slice(2 * width + pair * PAIR, 2 * width + (pair + 1) * PAIR)
        grad_lanes = slice(3 * width + pair * PAIR, 3 * width + (pair + 1) * PAIR)
        query, grad = q[:, lanes], g[:, lanes]
        queries, grads = halves(query), halves(grad)
        keys, values = halves(k[:, lanes]), halves(v[:, lanes])
        sum_q = sum_k = sum_v = None
        for side in range(2):
            head = 2 * pair + side
            scores = jnp.where(valid_near, dot(keys[side], query, NT), -jnp.inf)
            probs = jnp.exp(scores - across[head : head + 1, :])
            grad_probs = dot(values[side], grad, NT)
            grad_scores = probs * (grad_probs - across[SECOND + head : SECOND + head + 1, :])
            grad_scores = grad_scores.astype(BF)
            part_k = dot(grad_scores, queries[side])
            part_v = dot(probs.astype(BF), grads[side])
            part_q = dot(grad_scores, keys[side], TN)
            if side == 0:
                sum_q, sum_k, sum_v = part_q, part_k, part_v
            else:
                sum_q, sum_k, sum_v = sum_q + part_q, sum_k + part_k, sum_v + part_v
        sums = []
        for level, (start, stop) in enumerate(parts):
            rows = slice(start, stop)
            keys = halves(gathered(pieces[level], lanes))
            values = halves(gathered(pieces[level], value_lanes))
            total = None
            for side in range(2):
                head = 2 * pair + side
                valid = places[level] + offs_ref[level, head] < limit
                scores = dot(sel[rows, query_lanes], keys[side], NT)
                scores = jnp.where(valid, scores, -jnp.inf)
                probs = jnp.exp(scores - picked[rows, head : head + 1])
                grad_probs = dot(sel[rows, grad_lanes], values[side], NT)
                grad_probs = grad_probs - picked[rows, SECOND + head : SECOND + head + 1]
                part = dot((probs * grad_probs).astype(BF), keys[side])
                total = part if total is None else total + part
            sums.append(total)
        sums.append(jnp.zeros((held_tail, PAIR), F32))
        dk[:, lanes] = sum_k
        dv[:, lanes] = sum_v
        sum_sel = jnp.concatenate(sums, axis=0)
        dq[:, lanes] = (SCALE * (sum_q + spread(z, offs_ref, pair, sum_sel))).astype(BF)


def key_grads_kernel(
    z, offs_ref, pad_ref, sel, first, second, first_stats, second_stats, dk_near, dv_near, dk, dv
):
    own = lax.axis_index("ctx")
    limit = z.rows * z.devs - pad_ref[0] - own * z.rows
    width = z.width
    parts = level_parts(z)
    held_tail = z.sel - parts[1][1]

    def of_level(level, refs, lanes):
        return jnp.concatenate(
            [
                ref[p * z.sel + level * z.mid : p * z.sel + (level + 1) * z.mid, lanes]
                for ref in refs
                for p in range(4)
            ],
            axis=0,
        )

    across = [
        jnp.transpose(of_level(level, (first_stats, second_stats), slice(0, LANES)))
        for level in range(2)
    ]
    for pair in range(z.pairs):
        lanes = slice(pair * PAIR, (pair + 1) * PAIR)
        value_lanes = slice(width + pair * PAIR, width + (pair + 1) * PAIR)
        sums_k, sums_v = [], []
        for level, (start, stop) in enumerate(parts):
            entry = iota((stop - start, 1), 0) + start
            keys, values = sel[start:stop, lanes], sel[start:stop, value_lanes]
            queries = halves(of_level(level, (first, second), lanes))
            grads = halves(of_level(level, (first, second), value_lanes))
            sum_k = sum_v = None
            for side in range(2):
                head = 2 * pair + side
                at = chosen_row(z, entry, offs_ref[0, head], offs_ref[1, head])
                valid = (at >= 0) & (at < limit)
                scores = jnp.where(valid, dot(keys, queries[side], NT), -jnp.inf)
                probs = jnp.exp(scores - across[level][head : head + 1, :])
                grad_probs = dot(values, grads[side], NT)
                grad_probs = grad_probs - across[level][SECOND + head : SECOND + head + 1, :]
                part_k = dot((probs * grad_probs).astype(BF), queries[side])
                part_v = dot(probs.astype(BF), grads[side])
                sum_k = part_k if side == 0 else sum_k + part_k
                sum_v = part_v if side == 0 else sum_v + part_v
            sums_k.append(sum_k)
            sums_v.append(sum_v)
        tail = [jnp.zeros((held_tail, PAIR), F32)]
        sum_k = jnp.concatenate(sums_k + tail, axis=0)
        sum_v = jnp.concatenate(sums_v + tail, axis=0)
        dk[:, lanes] = (dk_near[:, lanes] + spread(z, offs_ref, pair, sum_k)).astype(BF)
        dv[:, lanes] = (dv_near[:, lanes] + spread(z, offs_ref, pair, sum_v)).astype(BF)


def early_weights_kernel(z, turned, turned_other, attn, attn_other, dq, dq_other, cot, cot_other, out):
    width = z.width
    out[:, :width] = (dot(attn[...], cot[...]) + dot(attn_other[...], cot_other[...])).astype(BF)
    out[:, width:] = (
        dot(turned[: z.half, :], dq[...]) + dot(turned_other[: z.half, :], dq_other[...])
    ).astype(BF)


def late_weights_kernel(z, turned, turned_other, dk, dv, dk_other, dv_other, out_a, out_b):
    width = z.width
    cut = out_a.shape[1] - width
    left, left_other = turned[: z.half, :], turned_other[: z.half, :]
    out_b[...] = (
        dot(turned[z.half :, :], dv[:, cut:]) + dot(turned_other[z.half :, :], dv_other[:, cut:])
    ).astype(BF)
    out_a[:, :width] = (dot(left, dk[...]) + dot(left_other, dk_other[...])).astype(BF)
    out_a[:, width:] = (dot(left, dv[:, :cut]) + dot(left_other, dv_other[:, :cut])).astype(BF)


def tiles_kernel(z, dq, dk, dv, w_qkv, out):
    width = z.width
    out[...] = (
        dot(dq[...], w_qkv[:, :width], NT)
        + dot(dk[...], w_qkv[:, width : 2 * width], NT)
        + dot(dv[...], w_qkv[:, 2 * width :], NT)
    ).astype(BF)


def call(kernel, outs, flops, scratch=(), smem=0):
    def run(*args):
        moved = sum(int(np.prod(a.shape)) * a.dtype.itemsize for a in args)
        moved += sum(int(np.prod(s)) * jnp.dtype(t).itemsize for s, t in outs)
        specs = [
            pl.BlockSpec(memory_space=pltpu.SMEM if i < smem else pltpu.VMEM)
            for i in range(len(args))
        ]
        return pl.pallas_call(
            kernel,
            out_shape=tuple(jax.ShapeDtypeStruct(s, t) for s, t in outs),
            in_specs=specs,
            out_specs=tuple(pl.BlockSpec(memory_space=pltpu.VMEM) for _ in outs),
            scratch_shapes=list(scratch),
            compiler_params=pltpu.CompilerParams(vmem_limit_bytes=VMEM_BYTES),
            cost_estimate=pl.CostEstimate(
                flops=int(flops), bytes_accessed=int(moved), transcendentals=0
            ),
        )(*args)

    return run


def swap(value, mask, dev_count):
    return lax.ppermute(value, "ctx", [(d, d ^ mask) for d in range(dev_count)])


def upper_steps(dev_count):
    steps, base = [], GROUP
    while base < dev_count:
        count = 4 if base * 4 <= dev_count else 2
        steps.append((base, count))
        base *= count
    return steps


PLANE = (2, 4)


def collect(value, step, dev_count, first=()):
    base, count = step
    parts = [value] + [swap(value, base * i, dev_count) for i in range(1, count)]
    if first:
        parts = lax.optimization_barrier((*parts, *first))[:count]
    return jnp.concatenate(parts, axis=0)


def reduce_step(value, step, dev_count, dtype):
    base, count = step
    size = value.shape[0] // count
    total = value[:size].astype(F32)
    for i in range(1, count):
        total = total + swap(value[i * size : (i + 1) * size], base * i, dev_count).astype(F32)
    return total.astype(dtype)


def reduce_all(value, steps, dev_count):
    for i, step in enumerate(steps):
        value = reduce_step(value, step, dev_count, F32 if i == len(steps) - 1 else BF)
    return value


def strip_order(z, own):
    entries = []
    for core in range(2):
        for first_plane in (True, False):
            outer, inner = (4, z.upper) if first_plane else (z.upper, 4)
            a, b, r = np.meshgrid(
                np.arange(outer), np.arange(inner), np.arange(z.strip), indexing="ij"
            )
            plane, upper = (a, b) if first_plane else (b, a)
            entries.append(
                np.stack([(core + 2 * plane + GROUP * upper).ravel(), r.ravel()], axis=1)
            )
    table = np.concatenate(entries, axis=0).astype(np.int32)
    return (own ^ table[:, :1]) * z.strip + table[:, 1:]


def after(value, *others):
    return lax.optimization_barrier((value, *others))[0]


def per_device(tiles, w_qkv, w_out, cotangent, offsets, pad_count):
    n = lax.axis_size("ctx")
    z = Sizes(tiles.shape[0], tiles.shape[1], n)
    own = lax.axis_index("ctx")
    rows, width = z.rows, z.width
    ups = upper_steps(n)
    order = strip_order(z, own)
    base_flops = 2 * rows * rows * width

    q, k, v, g, sel, far = call(
        functools.partial(project_kernel, z),
        [((rows, width), BF)] * 4 + [((z.sel, 4 * width), BF), ((z.far, 4 * width), BF)],
        2 * rows * width * 4 * width,
        smem=1,
    )(offsets, tiles, w_qkv, cotangent, w_out)

    mixed, near_stats, turned, turned_out = call(
        functools.partial(near_kernel, z),
        [
            ((rows, width), F32),
            ((rows, LANES), F32),
            ((width, rows), BF),
            ((width, rows), BF),
        ],
        8 * base_flops,
        smem=1,
    )(pad_count, q, k, v, g, tiles, order)

    far_up = far
    for i, step in enumerate(ups):
        far_up = collect(far_up, step, n, (near_stats,) if i == 0 else ())
    mid_0 = collect(sel[: z.mid, : 2 * width], PLANE, n)
    mid_1 = swap(mid_0, 1, n)
    far_0 = collect(far_up[:, : 2 * width], PLANE, n)
    far_1 = swap(far_0, 1, n)
    qg = jnp.concatenate([sel[: z.mid, 2 * width :], far_up[:, 2 * width :]], axis=0)
    qg_first = collect(after(qg, far_0), PLANE, n)
    qg_second = swap(qg_first, 1, n)
    turned_other = swap(turned_out, 1, n)
    cot_other = swap(cotangent, 1, n)

    stats, picked, held = call(
        functools.partial(join_kernel, z),
        [((rows, LANES), F32), ((z.sel, LANES), F32), ((z.sel, width), F32)],
        3 * base_flops,
        smem=2,
    )(offsets, pad_count, sel, mid_0, mid_1, far_0, far_1, near_stats)

    out_rows, attn_turned, attn_turned_out = call(
        functools.partial(output_kernel, z),
        [((rows, width), BF), ((z.half, rows), BF), ((z.half, rows), BF)],
        6 * rows * width * width,
        scratch=[pltpu.VMEM((rows, width), BF)],
        smem=1,
    )(offsets, near_stats, stats, mixed, held, tiles, w_out, order)
    attn_other = swap(attn_turned_out, 1, n)

    dq, dk_near, dv_near = call(
        functools.partial(near_grads_kernel, z),
        [((rows, width), BF), ((rows, width), F32), ((rows, width), F32)],
        8 * base_flops,
        smem=2,
    )(offsets, pad_count, q, k, v, g, stats, sel, mid_0, mid_1, far_0, far_1, picked)
    dq_other = swap(dq, 1, n)

    stats_up = picked[z.mid : z.mid + z.far]
    for i, step in enumerate(ups):
        stats_up = collect(stats_up, step, n, (out_rows,) if i == 0 else ())
    stats_first = collect(
        jnp.concatenate([picked[: z.mid], stats_up], axis=0), PLANE, n, (dk_near,)
    )
    stats_second = swap(stats_first, 1, n)

    (early_half,) = call(
        functools.partial(early_weights_kernel, z),
        [((z.half, 2 * width), BF)],
        4 * rows * width * width,
    )(turned, turned_other, attn_turned, attn_other, dq, dq_other, cotangent, cot_other)
    early = reduce_all(early_half, [PLANE] + ups[::-1], n)

    dk, dv = call(
        functools.partial(key_grads_kernel, z),
        [((rows, width), BF), ((rows, width), BF)],
        3 * base_flops,
        smem=2,
    )(offsets, pad_count, sel, qg_first, qg_second, stats_first, stats_second, dk_near, dv_near)
    dk_other = swap(dk, 1, n)
    dv_other = swap(dv, 1, n)
    cut = width // 3
    late_a, late_b = call(
        functools.partial(late_weights_kernel, z),
        [((z.half, width + cut), BF), ((z.half, width - cut), BF)],
        4 * rows * width * width,
    )(turned, turned_other, dk, dv, dk_other, dv_other)
    grad_a = reduce_all(late_a, [PLANE] + ups[::-1], n)
    grad_b = reduce_all(late_b, ups[::-1] + [PLANE], n)

    (grad_tiles,) = call(
        functools.partial(tiles_kernel, z), [((rows, width), BF)], 6 * rows * width * width
    )(dq, dk, dv, w_qkv)
    grad_wqkv = jnp.concatenate([early[:, width:], grad_a, grad_b], axis=1)
    return out_rows, grad_tiles, grad_wqkv, early[:, :width]


def solution(mesh):
    return jax.shard_map(
        per_device,
        mesh=mesh,
        in_specs=(P("ctx", None), P(), P(), P("ctx", None), P(), P()),
        out_specs=(P("ctx", None), P("ctx", None), P("ctx", None), P("ctx", None)),
        check_vma=False,
    )
```

time: 129 us -> 132 us (1.023)
  Pallas kernels: 27.3 us -> 29.8 us
  local copies, waits for them, and re-layouts: 5.37 us -> 6.9 us
    pallas_call x10 -> x9, Pallas kernels: 27.3 us -> 29.8 us  [run(): pl.pallas_call(kernel, out_shape=tuple((jax.ShapeDtypeStruct(s, t) for s,...]
    unnamed x30 -> x35, local copies, waits for them, and re-layouts: 5.05 us -> 6.04 us
    ppermute x42 -> x46, waiting for transfers between devices: 43 us -> 42.9 us  [swap(): return lax.ppermute(value, 'ctx', [(d, d ^ mask) for d in range(dev_count)])]
    ppermute x42 -> x46, starting transfers between devices: 47.9 us -> 47.8 us  [swap(): return lax.ppermute(value, 'ctx', [(d, d ^ mask) for d in range(dev_count)])]
  transfers between devices with their start and end apart: 42 -> 46, of which waited for: 16 -> 20; matrix products, arithmetic and copies ran while one was open for 2% -> 2% of each run, Pallas kernels for 19% -> 20%
where the time goes in v2:
time: 132 us
  starting transfers between devices  47.8 us (36%)
  waiting for transfers between devices  42.9 us (32%)
  Pallas kernels  29.8 us (23%)
  local copies, waits for them, and re-layouts  6.9 us (5%)
  other arithmetic  2.44 us (2%)
  between operations  1.69 us (1%)
    ppermute x46, starting transfers between devices, swap(): return lax.ppermute(value, 'ctx', [(d, d ^ mask) for d in range(dev_count)])  47.8 us
    ppermute x46, waiting for transfers between devices, swap(): return lax.ppermute(value, 'ctx', [(d, d ^ mask) for d in range(dev_count)])  42.9 us
    pallas_call x9, Pallas kernels, run(): pl.pallas_call(kernel, out_shape=tuple((jax.ShapeDtypeStruct(s, t) for s,...  29.8 us
    unnamed x35, local copies, waits for them, and re-layouts  6.04 us
  transfers between devices with their start and end apart: 46, of which 20 were waited for; matrix products, arithmetic and copies ran while one was open for 2% of the time, Pallas kernels for 20%

profile of v2, /device:TPU:0, one launch (start us, length us, event | category | flops | bytes accessed | tf_op | source)
XLA Modules:
  0.0 131.5 jit_solution(2356885728201885501)
XLA Ops:
  0.6 2.0 %copy-done = bf16[768,2304]{1,0:T(8,128)(2,1)S(1)} copy-done((bf16[768,2304]{1,0:T(8,128)(2,1)S(1)}, bf16[768,2304]{1,0:T(8,128)(2,1)}, u32[]{:S(2)}) %copy-start) | copy-done | bytes 3538968
  2.6 1.3 copy-done.2
  3.9 1.0 copy-done.4
  4.9 1.0 copy-done.6
  6.6 2.2 %shard_map.111 = (bf16[256,768]{1,0:T(8,128)(2,1)S(1)}, bf16[256,768]{1,0:T(8,128)(2,1)S(1)}, bf16[256,768]{1,0:T(8,128)(2,1)S(1)}, bf16[256,768]{1,0:T(8,128)(2...) custom-call(s32[2,12]{1,0:T(2,128)S(1)} %copy-done.8, bf16[256,768]{1,0:T(8,128)(2,1)S(1)} %copy-done.4, ...), custom_call_target="tpu_custom_call" | custom-call | flops 1207959552 | bytes 7520352 | tf_op jit(solution)/shard_map/pallas_call | solution.py:451
  8.8 4.0 %collective-permute-start.2 = (bf16[32,1536]{1,0:T(8,128)(2,1)S(1)}, bf16[32,1536]{1,0:T(8,128)(2,1)S(1)}, u32[]{:S(2)}, u32[]{:S(2)}) collective-permute-start(bf16[32,1536]{1,0:T(8,128)(2,1)S(1)} %get-tuple-element.86), channel_id=1, source_target_pairs={{0,6},{1,7},{2,4},{3,5},{4,2},{5,3},{6,0},{7,1},{8,14},{9,15},{10,... | collective-permute-start | bytes 294920 | tf_op jit(solution)/shard_map/ppermute | solution.py:467
  13.3 1.6 %collective-permute-start.4 = (bf16[8,3072]{1,0:T(8,128)(2,1)S(1)}, bf16[8,3072]{1,0:T(8,128)(2,1)S(1)}, u32[]{:S(2)}, u32[]{:S(2)}) collective-permute-start(bf16[8,3072]{1,0:T(8,128)(2,1)S(1)} %get-tuple-element.47), channel_id=1, source_target_pairs={{0,8},{1,9},{2,10},{3,11},{4,12},{5,13},{6,14},{7,15},{8,0},{9,1},... | collective-permute-start | bytes 147464 | tf_op jit(solution)/shard_map/ppermute | solution.py:467
  14.9 2.6 %collective-permute-start.5 = (bf16[8,3072]{1,0:T(8,128)(2,1)S(1)}, bf16[8,3072]{1,0:T(8,128)(2,1)S(1)}, u32[]{:S(2)}, u32[]{:S(2)}) collective-permute-start(bf16[8,3072]{1,0:T(8,128)(2,1)S(1)} %get-tuple-element.47), channel_id=1, source_target_pairs={{0,16},{1,17},{2,18},{3,19},{4,20},{5,21},{6,22},{7,23},{8,24},{9,... | collective-permute-start | bytes 147464 | tf_op jit(solution)/shard_map/ppermute | solution.py:467
  18.4 1.3 multiply_add_fusion.order
  19.7 2.6 %shard_map.112 = (f32[256,768]{1,0:T(8,128)S(1)}, f32[256,128]{1,0:T(8,128)S(1)}, bf16[768,256]{1,0:T(8,128)(2,1)S(1)}, bf16[768,256]{1,0:T(8,128)(2,1)S(1)}) custom-call(s32[1]{0:T(128)S(6)} %copy.26.pad_ref, bf16[256,768]{1,0:T(8,128)(2,1)S(1)} %get-tuple-element.40.q, bf16[256,768]{1,0:T(8,128)(2,1)S(1)} %get-tuple-element.41.k, ...), custom_call_target="tpu_custom_call" | custom-call | flops 805306368 | bytes 3676164 | tf_op jit(solution)/shard_map/pallas_call | solution.py:451
  23.5 2.5 %collective-permute-start.9 = (bf16[32,1536]{1,0:T(8,128)(2,1)S(1)}, bf16[32,1536]{1,0:T(8,128)(2,1)S(1)}, u32[]{:S(2)}, u32[]{:S(2)}) collective-permute-start(bf16[32,1536]{1,0:T(8,128)(2,1)S(1)} %get-tuple-element.94), channel_id=1, source_target_pairs={{0,6},{1,7},{2,4},{3,5},{4,2},{5,3},{6,0},{7,1},{8,14},{9,15},{10,... | collective-permute-start | bytes 294920 | tf_op jit(solution)/shard_map/ppermute | solution.py:467
  27.3 3.1 %collective-permute-done.9 = bf16[32,1536]{1,0:T(8,128)(2,1)S(1)} collective-permute-done((bf16[32,1536]{1,0:T(8,128)(2,1)S(1)}, bf16[32,1536]{1,0:T(8,128)(2,1)S(1)}, u32[]{:S(2)}, u32[]{:S(2)}) %collective-permute-start.9) | collective-permute-done | bytes 98336 | tf_op jit(solution)/shard_map/ppermute | solution.py:467
  30.4 1.7 %collective-permute-done.8 = bf16[32,1536]{1,0:T(8,128)(2,1)S(1)} collective-permute-done((bf16[32,1536]{1,0:T(8,128)(2,1)S(1)}, bf16[32,1536]{1,0:T(8,128)(2,1)S(1)}, u32[]{:S(2)}, u32[]{:S(2)}) %collective-permute-start.8) | collective-permute-done | bytes 98336 | tf_op jit(solution)/shard_map/ppermute | solution.py:467
  33.1 6.4 %collective-permute-done.11 = bf16[64,1536]{1,0:T(8,128)(2,1)S(1)} collective-permute-done((bf16[64,1536]{1,0:T(8,128)(2,1)S(1)}, bf16[64,1536]{1,0:T(8,128)(2,1)S(1)}, u32[]{:S(2)}, u32[]{:S(2)}) %collective-permute-start.11) | collective-permute-done | bytes 196640 | tf_op jit(solution)/shard_map/ppermute | solution.py:467
  39.5 1.4 %collective-permute-start.12 = (bf16[64,1536]{1,0:T(8,128)(2,1)S(1)}, bf16[64,1536]{1,0:T(8,128)(2,1)S(1)}, u32[]{:S(2)}, u32[]{:S(2)}) collective-permute-start(bf16[64,1536]{1,0:T(8,128)(2,1)S(1)} %pad_maximum_fusion.3), channel_id=1, source_target_pairs={{0,4},{1,5},{2,6},{3,7},{4,0},{5,1},{6,2},{7,3},{8,12},{9,13},{10,... | collective-permute-start | bytes 589832 | tf_op jit(solution)/shard_map/ppermute | solution.py:467
  40.9 5.1 %collective-permute-done.12 = bf16[64,1536]{1,0:T(8,128)(2,1)S(1)} collective-permute-done((bf16[64,1536]{1,0:T(8,128)(2,1)S(1)}, bf16[64,1536]{1,0:T(8,128)(2,1)S(1)}, u32[]{:S(2)}, u32[]{:S(2)}) %collective-permute-start.12) | collective-permute-done | bytes 196640 | tf_op jit(solution)/shard_map/ppermute | solution.py:467
  46.0 7.4 %shard_map.113 = (f32[256,128]{1,0:T(8,128)S(1)}, f32[64,128]{1,0:T(8,128)S(1)}, f32[64,768]{1,0:T(8,128)S(1)}) custom-call(s32[2,12]{1,0:T(2,128)S(1)} %copy-done.9, s32[1]{0:T(128)S(6)} %copy.26.pad_ref, bf16[64,3072]{1,0:T(8,128)(2,1)S(1)} %get-tuple-element.45.sel, bf16[128,1536]{1,0:T(8,128)(2,1)S(1)} %pad_maximum_fusion.mid_0, ...), custom_call_target="tpu_custom_call" | custom-call | flops 301989888 | bytes 2457700 | tf_op jit(solution)/shard_map/pallas_call | solution.py:451
  54.2 3.5 %collective-permute-start.16 = (f32[8,128]{1,0:T(8,128)S(1)}, f32[8,128]{1,0:T(8,128)S(1)}, u32[]{:S(2)}, u32[]{:S(2)}) collective-permute-start(f32[8,128]{1,0:T(8,128)S(1)} %slice.101), channel_id=1, source_target_pairs={{0,16},{1,17},{2,18},{3,19},{4,20},{5,21},{6,22},{7,23},{8,24},{9,... | collective-permute-start | bytes 12296 | tf_op jit(solution)/shard_map/ppermute | solution.py:467
  57.9 2.4 %shard_map.114 = (bf16[256,768]{1,0:T(8,128)(2,1)}, bf16[384,256]{1,0:T(8,128)(2,1)S(1)}, bf16[384,256]{1,0:T(8,128)(2,1)S(1)}) custom-call(s32[2,12]{1,0:T(2,128)S(1)} %copy-done.9, f32[256,128]{1,0:T(8,128)S(1)} %get-tuple-element.44.near_stats, f32[256,128]{1,0:T(8,128)S(1)} %get-tuple-element.51.stats, f32[256,768]{1,0:T(8,128)S(1)} %get-tuple-element.52.mixed, ...), custom_call_target="tpu_custom_call" | custom-call | flops 905969664 | bytes 3610720 | tf_op jit(solution)/shard_map/pallas_call | solution.py:451
  60.4 1.4 %collective-permute-start.13 = (bf16[64,1536]{1,0:T(8,128)(2,1)S(1)}, bf16[64,1536]{1,0:T(8,128)(2,1)S(1)}, u32[]{:S(2)}, u32[]{:S(2)}) collective-permute-start(bf16[64,1536]{1,0:T(8,128)(2,1)S(1)} %pad_maximum_fusion.3), channel_id=1, source_target_pairs={{0,6},{1,7},{2,4},{3,5},{4,2},{5,3},{6,0},{7,1},{8,14},{9,15},{10,... | collective-permute-start | bytes 589832 | tf_op jit(solution)/shard_map/ppermute | solution.py:467
  61.8 1.3 collective-permute-done.17
  64.0 7.2 %shard_map.115 = (bf16[256,768]{1,0:T(8,128)(2,1)S(1)}, f32[256,768]{1,0:T(8,128)S(1)}, f32[256,768]{1,0:T(8,128)S(1)}) custom-call(s32[2,12]{1,0:T(2,128)S(1)} %copy-done.9, s32[1]{0:T(128)S(6)} %copy.26.pad_ref, bf16[256,768]{1,0:T(8,128)(2,1)S(1)} %get-tuple-element.40.q, bf16[256,768]{1,0:T(8,128)(2,1)S(1)} %get-tuple-element.41.k, ...), custom_call_target="tpu_custom_call" | custom-call | flops 805306368 | bytes 5668964 | tf_op jit(solution)/shard_map/pallas_call | solution.py:451
  71.3 1.5 %collective-permute-start.19 = (f32[64,128]{1,0:T(8,128)S(1)}, f32[64,128]{1,0:T(8,128)S(1)}, u32[]{:S(2)}, u32[]{:S(2)}) collective-permute-start(f32[64,128]{1,0:T(8,128)S(1)} %constant_dynamic-update-slice_fusion.8), channel_id=1, source_target_pairs={{0,4},{1,5},{2,6},{3,7},{4,0},{5,1},{6,2},{7,3},{8,12},{9,13},{10,... | collective-permute-start | bytes 98312 | tf_op jit(solution)/shard_map/ppermute | solution.py:467
  72.8 1.3 collective-permute-start.20
  74.1 1.2 collective-permute-done.19
  75.3 2.3 %collective-permute-done.20 = f32[64,128]{1,0:T(8,128)S(1)} collective-permute-done((f32[64,128]{1,0:T(8,128)S(1)}, f32[64,128]{1,0:T(8,128)S(1)}, u32[]{:S(2)}, u32[]{:S(2)}) %collective-permute-start.20) | collective-permute-done | bytes 32800 | tf_op jit(solution)/shard_map/ppermute | solution.py:467
  77.6 1.4 %collective-permute-done.23.attn_other = bf16[384,256]{1,0:T(8,128)(2,1)S(1)} collective-permute-done((bf16[384,256]{1,0:T(8,128)(2,1)S(1)}, bf16[384,256]{1,0:T(8,128)(2,1)S(1)}, u32[]{:S(2)}, u32[]{:S(2)}) %collective-permute-start.23) | collective-permute-done | bytes 196640 | tf_op jit(solution)/shard_map/ppermute | solution.py:467
  79.9 1.3 %collective-permute-start.28 = (bf16[96,1536]{1,0:T(8,128)(2,1)S(1)}, bf16[96,1536]{1,0:T(8,128)(2,1)S(1)}, u32[]{:S(2)}, u32[]{:S(2)}) collective-permute-start(bf16[96,1536]{1,0:T(8,128)(2,1)S(1)} %get-tuple-element.77), channel_id=1, source_target_pairs={{0,6},{1,7},{2,4},{3,5},{4,2},{5,3},{6,0},{7,1},{8,14},{9,15},{10,... | collective-permute-start | bytes 884744 | tf_op jit(solution)/shard_map/ppermute | solution.py:467
  81.2 1.7 %collective-permute-start.27 = (bf16[96,1536]{1,0:T(8,128)(2,1)S(1)}, bf16[96,1536]{1,0:T(8,128)(2,1)S(1)}, u32[]{:S(2)}, u32[]{:S(2)}) collective-permute-start(bf16[96,1536]{1,0:T(8,128)(2,1)S(1)} %get-tuple-element.78), channel_id=1, source_target_pairs={{0,4},{1,5},{2,6},{3,7},{4,0},{5,1},{6,2},{7,3},{8,12},{9,13},{10,... | collective-permute-start | bytes 884744 | tf_op jit(solution)/shard_map/ppermute | solution.py:467
  83.5 1.3 %collective-permute-done.21.second_stats = f32[256,128]{1,0:T(8,128)S(1)} collective-permute-done((f32[256,128]{1,0:T(8,128)S(1)}, f32[256,128]{1,0:T(8,128)S(1)}, u32[]{:S(2)}, u32[]{:S(2)}) %collective-permute-start.21) | collective-permute-done | bytes 131104 | tf_op jit(solution)/shard_map/ppermute | solution.py:467
  84.9 4.5 %shard_map.116 = (bf16[256,768]{1,0:T(8,128)(2,1)S(1)}, bf16[256,768]{1,0:T(8,128)(2,1)S(1)}) custom-call(s32[2,12]{1,0:T(2,128)S(1)} %copy-done.9, s32[1]{0:T(128)S(6)} %copy.26.pad_ref, bf16[64,3072]{1,0:T(8,128)(2,1)S(1)} %get-tuple-element.45.sel, bf16[256,1536]{1,0:T(8,128)(2,1)S(1)} %constant_dynamic-update-slice_fusion.4.first, ...), custom_call_target="tpu_custom_call" | custom-call | flops 301989888 | bytes 4587620 | tf_op jit(solution)/shard_map/pallas_call | solution.py:451
  90.7 5.5 %collective-permute-done.27 = bf16[96,1536]{1,0:T(8,128)(2,1)S(1)} collective-permute-done((bf16[96,1536]{1,0:T(8,128)(2,1)S(1)}, bf16[96,1536]{1,0:T(8,128)(2,1)S(1)}, u32[]{:S(2)}, u32[]{:S(2)}) %collective-permute-start.27) | collective-permute-done | bytes 294944 | tf_op jit(solution)/shard_map/ppermute | solution.py:467
  96.4 2.6 %collective-permute-start.31 = (bf16[24,1536]{1,0:T(8,128)(2,1)S(1)}, bf16[24,1536]{1,0:T(8,128)(2,1)S(1)}, u32[]{:S(2)}, u32[]{:S(2)}) collective-permute-start(bf16[24,1536]{1,0:T(8,128)(2,1)S(1)} %get-tuple-element.88), channel_id=1, source_target_pairs={{0,24},{1,25},{2,26},{3,27},{4,28},{5,29},{6,30},{7,31},{8,16},{9,... | collective-permute-start | bytes 221192 | tf_op jit(solution)/shard_map/ppermute | solution.py:467
  99.0 1.9 %collective-permute-start.29 = (bf16[24,1536]{1,0:T(8,128)(2,1)S(1)}, bf16[24,1536]{1,0:T(8,128)(2,1)S(1)}, u32[]{:S(2)}, u32[]{:S(2)}) collective-permute-start(bf16[24,1536]{1,0:T(8,128)(2,1)S(1)} %get-tuple-element.87), channel_id=1, source_target_pairs={{0,8},{1,9},{2,10},{3,11},{4,12},{5,13},{6,14},{7,15},{8,0},{9,1},... | collective-permute-start | bytes 221192 | tf_op jit(solution)/shard_map/ppermute | solution.py:467
  100.9 1.9 %shard_map.117 = bf16[256,768]{1,0:T(8,128)(2,1)} custom-call(bf16[256,768]{1,0:T(8,128)(2,1)S(1)} %get-tuple-element.56.dq, bf16[256,768]{1,0:T(8,128)(2,1)S(1)} %get-tuple-element.68.dk, bf16[256,768]{1,0:T(8,128)(2,1)S(1)} %get-tuple-element.69.dv, bf16[768,2304]{1,0:T(8,128)(2,1)S(1)} %copy-done.1), custom_call_target="tpu_custom_call" | custom-call | flops 905969664 | bytes 5111808 | tf_op jit(solution)/shard_map/pallas_call | solution.py:451
  103.4 2.2 %collective-permute-done.30 = bf16[24,1536]{1,0:T(8,128)(2,1)S(1)} collective-permute-done((bf16[24,1536]{1,0:T(8,128)(2,1)S(1)}, bf16[24,1536]{1,0:T(8,128)(2,1)S(1)}, u32[]{:S(2)}, u32[]{:S(2)}) %collective-permute-start.30) | collective-permute-done | bytes 73760 | tf_op jit(solution)/shard_map/ppermute | solution.py:467
  107.1 2.3 %collective-permute-start.42 = (bf16[96,512]{1,0:T(8,128)(2,1)S(1)}, bf16[96,512]{1,0:T(8,128)(2,1)S(1)}, u32[]{:S(2)}, u32[]{:S(2)}) collective-permute-start(bf16[96,512]{1,0:T(8,128)(2,1)S(1)} %get-tuple-element.83), channel_id=1, source_target_pairs={{0,24},{1,25},{2,26},{3,27},{4,28},{5,29},{6,30},{7,31},{8,16},{9,... | collective-permute-start | bytes 294920 | tf_op jit(solution)/shard_map/ppermute | solution.py:467
  109.4 2.2 %collective-permute-start.40 = (bf16[96,512]{1,0:T(8,128)(2,1)S(1)}, bf16[96,512]{1,0:T(8,128)(2,1)S(1)}, u32[]{:S(2)}, u32[]{:S(2)}) collective-permute-start(bf16[96,512]{1,0:T(8,128)(2,1)S(1)} %get-tuple-element.82), channel_id=1, source_target_pairs={{0,8},{1,9},{2,10},{3,11},{4,12},{5,13},{6,14},{7,15},{8,0},{9,1},... | collective-permute-start | bytes 294920 | tf_op jit(solution)/shard_map/ppermute | solution.py:467
  111.6 1.3 %collective-permute-start.36 = (bf16[96,1024]{1,0:T(8,128)(2,1)S(1)}, bf16[96,1024]{1,0:T(8,128)(2,1)S(1)}, u32[]{:S(2)}, u32[]{:S(2)}) collective-permute-start(bf16[96,1024]{1,0:T(8,128)(2,1)S(1)} %get-tuple-element.80), channel_id=1, source_target_pairs={{0,6},{1,7},{2,4},{3,5},{4,2},{5,3},{6,0},{7,1},{8,14},{9,15},{10,... | collective-permute-start | bytes 589832 | tf_op jit(solution)/shard_map/ppermute | solution.py:467
  113.4 1.3 collective-permute-done.42
  115.2 2.7 %collective-permute-done.41 = bf16[96,512]{1,0:T(8,128)(2,1)S(1)} collective-permute-done((bf16[96,512]{1,0:T(8,128)(2,1)S(1)}, bf16[96,512]{1,0:T(8,128)(2,1)S(1)}, u32[]{:S(2)}, u32[]{:S(2)}) %collective-permute-start.41) | collective-permute-done | bytes 98336 | tf_op jit(solution)/shard_map/ppermute | solution.py:467
  118.0 1.8 %collective-permute-start.45 = (bf16[24,512]{1,0:T(8,128)(2,1)S(1)}, bf16[24,512]{1,0:T(8,128)(2,1)S(1)}, u32[]{:S(2)}, u32[]{:S(2)}) collective-permute-start(bf16[24,512]{1,0:T(8,128)(2,1)S(1)} %get-tuple-element.98), channel_id=1, source_target_pairs={{0,6},{1,7},{2,4},{3,5},{4,2},{5,3},{6,0},{7,1},{8,14},{9,15},{10,... | collective-permute-start | bytes 73736 | tf_op jit(solution)/shard_map/ppermute | solution.py:467
  120.5 1.1 collective-permute-start.43
  121.5 1.6 %collective-permute-done.35 = bf16[96,1024]{1,0:T(8,128)(2,1)S(1)} collective-permute-done((bf16[96,1024]{1,0:T(8,128)(2,1)S(1)}, bf16[96,1024]{1,0:T(8,128)(2,1)S(1)}, u32[]{:S(2)}, u32[]{:S(2)}) %collective-permute-start.35) | collective-permute-done | bytes 196640 | tf_op jit(solution)/shard_map/ppermute | solution.py:467
  123.2 2.3 %collective-permute-start.39 = (bf16[24,1024]{1,0:T(8,128)(2,1)S(1)}, bf16[24,1024]{1,0:T(8,128)(2,1)S(1)}, u32[]{:S(2)}, u32[]{:S(2)}) collective-permute-start(bf16[24,1024]{1,0:T(8,128)(2,1)S(1)} %get-tuple-element.91), channel_id=1, source_target_pairs={{0,24},{1,25},{2,26},{3,27},{4,28},{5,29},{6,30},{7,31},{8,16},{9,... | collective-permute-start | bytes 147464 | tf_op jit(solution)/shard_map/ppermute | solution.py:467
  125.6 2.1 %collective-permute-start.37 = (bf16[24,1024]{1,0:T(8,128)(2,1)S(1)}, bf16[24,1024]{1,0:T(8,128)(2,1)S(1)}, u32[]{:S(2)}, u32[]{:S(2)}) collective-permute-start(bf16[24,1024]{1,0:T(8,128)(2,1)S(1)} %get-tuple-element.90), channel_id=1, source_target_pairs={{0,8},{1,9},{2,10},{3,11},{4,12},{5,13},{6,14},{7,15},{8,0},{9,1},... | collective-permute-start | bytes 147464 | tf_op jit(solution)/shard_map/ppermute | solution.py:467
  127.7 1.5 %collective-permute-done.39 = bf16[24,1024]{1,0:T(8,128)(2,1)S(1)} collective-permute-done((bf16[24,1024]{1,0:T(8,128)(2,1)S(1)}, bf16[24,1024]{1,0:T(8,128)(2,1)S(1)}, u32[]{:S(2)}, u32[]{:S(2)}) %collective-permute-start.39) | collective-permute-done | bytes 49184 | tf_op jit(solution)/shard_map/ppermute | solution.py:467
  129.2 1.5 %collective-permute-done.38 = bf16[24,1024]{1,0:T(8,128)(2,1)S(1)} collective-permute-done((bf16[24,1024]{1,0:T(8,128)(2,1)S(1)}, bf16[24,1024]{1,0:T(8,128)(2,1)S(1)}, u32[]{:S(2)}, u32[]{:S(2)}) %collective-permute-start.38) | collective-permute-done | bytes 49184 | tf_op jit(solution)/shard_map/ppermute | solution.py:467
  (113 shorter events, 14.6 us)
Async XLA Ops:
  8.8 14.6 %collective-permute-start.2 = (bf16[32,1536]{1,0:T(8,128)(2,1)S(1)}, bf16[32,1536]{1,0:T(8,128)(2,1)S(1)}, u32[]{:S(2)}, u32[]{:S(2)}) collective-permute-start(bf16[32,1536]{1,0:T(8,128)(2,1)S(1)} %get-tuple-element.86), channel_id=1, source_target_pairs={{0,6},{1,7},{2,4},{3,5},{4,2},{5,3},{6,0},{7,1},{8,14},{9,15},{10,... | collective-permute-start | bytes 294920 | tf_op jit(solution)/shard_map/ppermute | solution.py:467
  12.8 13.2 %collective-permute-start.1 = (bf16[32,1536]{1,0:T(8,128)(2,1)S(1)}, bf16[32,1536]{1,0:T(8,128)(2,1)S(1)}, u32[]{:S(2)}, u32[]{:S(2)}) collective-permute-start(bf16[32,1536]{1,0:T(8,128)(2,1)S(1)} %get-tuple-element.86), channel_id=1, source_target_pairs={{0,4},{1,5},{2,6},{3,7},{4,0},{5,1},{6,2},{7,3},{8,12},{9,13},{10,... | collective-permute-start | bytes 294920 | tf_op jit(solution)/shard_map/ppermute | solution.py:467
  13.3 8.9 %collective-permute-start.4 = (bf16[8,3072]{1,0:T(8,128)(2,1)S(1)}, bf16[8,3072]{1,0:T(8,128)(2,1)S(1)}, u32[]{:S(2)}, u32[]{:S(2)}) collective-permute-start(bf16[8,3072]{1,0:T(8,128)(2,1)S(1)} %get-tuple-element.47), channel_id=1, source_target_pairs={{0,8},{1,9},{2,10},{3,11},{4,12},{5,13},{6,14},{7,15},{8,0},{9,1},... | collective-permute-start | bytes 147464 | tf_op jit(solution)/shard_map/ppermute | solution.py:467
  14.9 7.8 %collective-permute-start.5 = (bf16[8,3072]{1,0:T(8,128)(2,1)S(1)}, bf16[8,3072]{1,0:T(8,128)(2,1)S(1)}, u32[]{:S(2)}, u32[]{:S(2)}) collective-permute-start(bf16[8,3072]{1,0:T(8,128)(2,1)S(1)} %get-tuple-element.47), channel_id=1, source_target_pairs={{0,16},{1,17},{2,18},{3,19},{4,20},{5,21},{6,22},{7,23},{8,24},{9,... | collective-permute-start | bytes 147464 | tf_op jit(solution)/shard_map/ppermute | solution.py:467
  17.5 5.9 %collective-permute-start.6 = (bf16[8,3072]{1,0:T(8,128)(2,1)S(1)}, bf16[8,3072]{1,0:T(8,128)(2,1)S(1)}, u32[]{:S(2)}, u32[]{:S(2)}) collective-permute-start(bf16[8,3072]{1,0:T(8,128)(2,1)S(1)} %get-tuple-element.47), channel_id=1, source_target_pairs={{0,24},{1,25},{2,26},{3,27},{4,28},{5,29},{6,30},{7,31},{8,16},{9,... | collective-permute-start | bytes 147464 | tf_op jit(solution)/shard_map/ppermute | solution.py:467
  22.2 4.7 %collective-permute-start = (bf16[32,1536]{1,0:T(8,128)(2,1)S(1)}, bf16[32,1536]{1,0:T(8,128)(2,1)S(1)}, u32[]{:S(2)}, u32[]{:S(2)}) collective-permute-start(bf16[32,1536]{1,0:T(8,128)(2,1)S(1)} %get-tuple-element.86), channel_id=1, source_target_pairs={{0,2},{1,3},{2,0},{3,1},{4,6},{5,7},{6,4},{7,5},{8,10},{9,11},{10,... | collective-permute-start | bytes 294920 | tf_op jit(solution)/shard_map/ppermute | solution.py:467
  22.6 55.0 %collective-permute-start.25 = (bf16[256,768]{1,0:T(8,128)(2,1)S(1)}, bf16[256,768]{1,0:T(8,128)(2,1)S(1)}, u32[]{:S(2)}, u32[]{:S(2)}) collective-permute-start(bf16[256,768]{1,0:T(8,128)(2,1)S(1)} %copy-done.7), channel_id=1, source_target_pairs={{0,1},{1,0},{2,3},{3,2},{4,5},{5,4},{6,7},{7,6},{8,9},{9,8},{10,11... | collective-permute-start | bytes 1179656 | tf_op jit(solution)/shard_map/ppermute | solution.py:467
  23.4 54.2 %collective-permute-start.22 = (bf16[768,256]{1,0:T(8,128)(2,1)S(1)}, bf16[768,256]{1,0:T(8,128)(2,1)S(1)}, u32[]{:S(2)}, u32[]{:S(2)}) collective-permute-start(bf16[768,256]{1,0:T(8,128)(2,1)S(1)} %get-tuple-element.71), channel_id=1, source_target_pairs={{0,1},{1,0},{2,3},{3,2},{4,5},{5,4},{6,7},{7,6},{8,9},{9,8},{10,11... | collective-permute-start | bytes 1179656 | tf_op jit(solution)/shard_map/ppermute | solution.py:467
  23.5 6.9 %collective-permute-start.9 = (bf16[32,1536]{1,0:T(8,128)(2,1)S(1)}, bf16[32,1536]{1,0:T(8,128)(2,1)S(1)}, u32[]{:S(2)}, u32[]{:S(2)}) collective-permute-start(bf16[32,1536]{1,0:T(8,128)(2,1)S(1)} %get-tuple-element.94), channel_id=1, source_target_pairs={{0,6},{1,7},{2,4},{3,5},{4,2},{5,3},{6,0},{7,1},{8,14},{9,15},{10,... | collective-permute-start | bytes 294920 | tf_op jit(solution)/shard_map/ppermute | solution.py:467
  26.0 6.1 %collective-permute-start.8 = (bf16[32,1536]{1,0:T(8,128)(2,1)S(1)}, bf16[32,1536]{1,0:T(8,128)(2,1)S(1)}, u32[]{:S(2)}, u32[]{:S(2)}) collective-permute-start(bf16[32,1536]{1,0:T(8,128)(2,1)S(1)} %get-tuple-element.94), channel_id=1, source_target_pairs={{0,4},{1,5},{2,6},{3,7},{4,0},{5,1},{6,2},{7,3},{8,12},{9,13},{10,... | collective-permute-start | bytes 294920 | tf_op jit(solution)/shard_map/ppermute | solution.py:467
  26.9 5.2 %collective-permute-start.7 = (bf16[32,1536]{1,0:T(8,128)(2,1)S(1)}, bf16[32,1536]{1,0:T(8,128)(2,1)S(1)}, u32[]{:S(2)}, u32[]{:S(2)}) collective-permute-start(bf16[32,1536]{1,0:T(8,128)(2,1)S(1)} %get-tuple-element.94), channel_id=1, source_target_pairs={{0,2},{1,3},{2,0},{3,1},{4,6},{5,7},{6,4},{7,5},{8,10},{9,11},{10,... | collective-permute-start | bytes 294920 | tf_op jit(solution)/shard_map/ppermute | solution.py:467
  27.3 18.8 %copy-start.9 = (s32[2,12]{1,0:T(2,128)S(1)}, s32[2,12]{1,0:T(2,128)}, u32[]{:S(2)}) copy-start(s32[2,12]{1,0:T(2,128)} %offs_ref.9) | copy-start | bytes 292
  30.4 15.6 %collective-permute-start.3 = (bf16[128,1536]{1,0:T(8,128)(2,1)S(1)}, bf16[128,1536]{1,0:T(8,128)(2,1)S(1)}, u32[]{:S(2)}, u32[]{:S(2)}) collective-permute-start(bf16[128,1536]{1,0:T(8,128)(2,1)S(1)} %pad_maximum_fusion.mid_0), channel_id=1, source_target_pairs={{0,1},{1,0},{2,3},{3,2},{4,5},{5,4},{6,7},{7,6},{8,9},{9,8},{10,11... | collective-permute-start | bytes 1179656 | tf_op jit(solution)/shard_map/ppermute | solution.py:467
  32.1 13.9 %collective-permute-start.10 = (bf16[128,1536]{1,0:T(8,128)(2,1)S(1)}, bf16[128,1536]{1,0:T(8,128)(2,1)S(1)}, u32[]{:S(2)}, u32[]{:S(2)}) collective-permute-start(bf16[128,1536]{1,0:T(8,128)(2,1)S(1)} %pad_maximum_fusion.1.far_0), channel_id=1, source_target_pairs={{0,1},{1,0},{2,3},{3,2},{4,5},{5,4},{6,7},{7,6},{8,9},{9,8},{10,11... | collective-permute-start | bytes 1179656 | tf_op jit(solution)/shard_map/ppermute | solution.py:467
  32.2 7.3 %collective-permute-start.11 = (bf16[64,1536]{1,0:T(8,128)(2,1)S(1)}, bf16[64,1536]{1,0:T(8,128)(2,1)S(1)}, u32[]{:S(2)}, u32[]{:S(2)}) collective-permute-start(bf16[64,1536]{1,0:T(8,128)(2,1)S(1)} %pad_maximum_fusion.3), channel_id=1, source_target_pairs={{0,2},{1,3},{2,0},{3,1},{4,6},{5,7},{6,4},{7,5},{8,10},{9,11},{10,... | collective-permute-start | bytes 589832 | tf_op jit(solution)/shard_map/ppermute | solution.py:467
  39.5 6.5 %collective-permute-start.12 = (bf16[64,1536]{1,0:T(8,128)(2,1)S(1)}, bf16[64,1536]{1,0:T(8,128)(2,1)S(1)}, u32[]{:S(2)}, u32[]{:S(2)}) collective-permute-start(bf16[64,1536]{1,0:T(8,128)(2,1)S(1)} %pad_maximum_fusion.3), channel_id=1, source_target_pairs={{0,4},{1,5},{2,6},{3,7},{4,0},{5,1},{6,2},{7,3},{8,12},{9,13},{10,... | collective-permute-start | bytes 589832 | tf_op jit(solution)/shard_map/ppermute | solution.py:467
  40.9 17.0 %copy-start.3 = (bf16[768,768]{1,0:T(8,128)(2,1)S(1)}, bf16[768,768]{1,0:T(8,128)(2,1)}, u32[]{:S(2)}) copy-start(bf16[768,768]{1,0:T(8,128)(2,1)} %w_out.3) | copy-start | bytes 3538948
  53.5 6.9 %collective-permute-start.15 = (f32[8,128]{1,0:T(8,128)S(1)}, f32[8,128]{1,0:T(8,128)S(1)}, u32[]{:S(2)}, u32[]{:S(2)}) collective-permute-start(f32[8,128]{1,0:T(8,128)S(1)} %slice.101), channel_id=1, source_target_pairs={{0,8},{1,9},{2,10},{3,11},{4,12},{5,13},{6,14},{7,15},{8,0},{9,1},... | collective-permute-start | bytes 12296 | tf_op jit(solution)/shard_map/ppermute | solution.py:467
  54.2 7.6 %collective-permute-start.16 = (f32[8,128]{1,0:T(8,128)S(1)}, f32[8,128]{1,0:T(8,128)S(1)}, u32[]{:S(2)}, u32[]{:S(2)}) collective-permute-start(f32[8,128]{1,0:T(8,128)S(1)} %slice.101), channel_id=1, source_target_pairs={{0,16},{1,17},{2,18},{3,19},{4,20},{5,21},{6,22},{7,23},{8,24},{9,... | collective-permute-start | bytes 12296 | tf_op jit(solution)/shard_map/ppermute | solution.py:467
  57.7 5.4 %collective-permute-start.17 = (f32[8,128]{1,0:T(8,128)S(1)}, f32[8,128]{1,0:T(8,128)S(1)}, u32[]{:S(2)}, u32[]{:S(2)}) collective-permute-start(f32[8,128]{1,0:T(8,128)S(1)} %slice.101), channel_id=1, source_target_pairs={{0,24},{1,25},{2,26},{3,27},{4,28},{5,29},{6,30},{7,31},{8,16},{9,... | collective-permute-start | bytes 12296 | tf_op jit(solution)/shard_map/ppermute | solution.py:467
  60.4 10.9 %collective-permute-start.13 = (bf16[64,1536]{1,0:T(8,128)(2,1)S(1)}, bf16[64,1536]{1,0:T(8,128)(2,1)S(1)}, u32[]{:S(2)}, u32[]{:S(2)}) collective-permute-start(bf16[64,1536]{1,0:T(8,128)(2,1)S(1)} %pad_maximum_fusion.3), channel_id=1, source_target_pairs={{0,6},{1,7},{2,4},{3,5},{4,2},{5,3},{6,0},{7,1},{8,14},{9,15},{10,... | collective-permute-start | bytes 589832 | tf_op jit(solution)/shard_map/ppermute | solution.py:467
  63.1 9.6 %collective-permute-start.18 = (f32[64,128]{1,0:T(8,128)S(1)}, f32[64,128]{1,0:T(8,128)S(1)}, u32[]{:S(2)}, u32[]{:S(2)}) collective-permute-start(f32[64,128]{1,0:T(8,128)S(1)} %constant_dynamic-update-slice_fusion.8), channel_id=1, source_target_pairs={{0,2},{1,3},{2,0},{3,1},{4,6},{5,7},{6,4},{7,5},{8,10},{9,11},{10,... | collective-permute-start | bytes 98312 | tf_op jit(solution)/shard_map/ppermute | solution.py:467
  71.2 7.8 %collective-permute-start.24 = (bf16[256,768]{1,0:T(8,128)(2,1)S(1)}, bf16[256,768]{1,0:T(8,128)(2,1)S(1)}, u32[]{:S(2)}, u32[]{:S(2)}) collective-permute-start(bf16[256,768]{1,0:T(8,128)(2,1)S(1)} %get-tuple-element.56.dq), channel_id=1, source_target_pairs={{0,1},{1,0},{2,3},{3,2},{4,5},{5,4},{6,7},{7,6},{8,9},{9,8},{10,11... | collective-permute-start | bytes 1179656 | tf_op jit(solution)/shard_map/ppermute | solution.py:467
  71.3 4.0 %collective-permute-start.19 = (f32[64,128]{1,0:T(8,128)S(1)}, f32[64,128]{1,0:T(8,128)S(1)}, u32[]{:S(2)}, u32[]{:S(2)}) collective-permute-start(f32[64,128]{1,0:T(8,128)S(1)} %constant_dynamic-update-slice_fusion.8), channel_id=1, source_target_pairs={{0,4},{1,5},{2,6},{3,7},{4,0},{5,1},{6,2},{7,3},{8,12},{9,13},{10,... | collective-permute-start | bytes 98312 | tf_op jit(solution)/shard_map/ppermute | solution.py:467
  72.8 4.8 %collective-permute-start.20 = (f32[64,128]{1,0:T(8,128)S(1)}, f32[64,128]{1,0:T(8,128)S(1)}, u32[]{:S(2)}, u32[]{:S(2)}) collective-permute-start(f32[64,128]{1,0:T(8,128)S(1)} %constant_dynamic-update-slice_fusion.8), channel_id=1, source_target_pairs={{0,6},{1,7},{2,4},{3,5},{4,2},{5,3},{6,0},{7,1},{8,14},{9,15},{10,... | collective-permute-start | bytes 98312 | tf_op jit(solution)/shard_map/ppermute | solution.py:467
  75.3 9.6 %collective-permute-start.14 = (bf16[256,1536]{1,0:T(8,128)(2,1)S(1)}, bf16[256,1536]{1,0:T(8,128)(2,1)S(1)}, u32[]{:S(2)}, u32[]{:S(2)}) collective-permute-start(bf16[256,1536]{1,0:T(8,128)(2,1)S(1)} %constant_dynamic-update-slice_fusion.4.first), channel_id=1, source_target_pairs={{0,1},{1,0},{2,3},{3,2},{4,5},{5,4},{6,7},{7,6},{8,9},{9,8},{10,11... | collective-permute-start | bytes 2359304 | tf_op jit(solution)/shard_map/ppermute | solution.py:467
  77.6 1.4 %collective-permute-start.23 = (bf16[384,256]{1,0:T(8,128)(2,1)S(1)}, bf16[384,256]{1,0:T(8,128)(2,1)S(1)}, u32[]{:S(2)}, u32[]{:S(2)}) collective-permute-start(bf16[384,256]{1,0:T(8,128)(2,1)S(1)} %get-tuple-element.73), channel_id=1, source_target_pairs={{0,1},{1,0},{2,3},{3,2},{4,5},{5,4},{6,7},{7,6},{8,9},{9,8},{10,11... | collective-permute-start | bytes 589832 | tf_op jit(solution)/shard_map/ppermute | solution.py:467
  79.9 10.9 %collective-permute-start.28 = (bf16[96,1536]{1,0:T(8,128)(2,1)S(1)}, bf16[96,1536]{1,0:T(8,128)(2,1)S(1)}, u32[]{:S(2)}, u32[]{:S(2)}) collective-permute-start(bf16[96,1536]{1,0:T(8,128)(2,1)S(1)} %get-tuple-element.77), channel_id=1, source_target_pairs={{0,6},{1,7},{2,4},{3,5},{4,2},{5,3},{6,0},{7,1},{8,14},{9,15},{10,... | collective-permute-start | bytes 884744 | tf_op jit(solution)/shard_map/ppermute | solution.py:467
  81.2 15.0 %collective-permute-start.27 = (bf16[96,1536]{1,0:T(8,128)(2,1)S(1)}, bf16[96,1536]{1,0:T(8,128)(2,1)S(1)}, u32[]{:S(2)}, u32[]{:S(2)}) collective-permute-start(bf16[96,1536]{1,0:T(8,128)(2,1)S(1)} %get-tuple-element.78), channel_id=1, source_target_pairs={{0,4},{1,5},{2,6},{3,7},{4,0},{5,1},{6,2},{7,3},{8,12},{9,13},{10,... | collective-permute-start | bytes 884744 | tf_op jit(solution)/shard_map/ppermute | solution.py:467
  83.0 13.3 %collective-permute-start.26 = (bf16[96,1536]{1,0:T(8,128)(2,1)S(1)}, bf16[96,1536]{1,0:T(8,128)(2,1)S(1)}, u32[]{:S(2)}, u32[]{:S(2)}) collective-permute-start(bf16[96,1536]{1,0:T(8,128)(2,1)S(1)} %get-tuple-element.76), channel_id=1, source_target_pairs={{0,2},{1,3},{2,0},{3,1},{4,6},{5,7},{6,4},{7,5},{8,10},{9,11},{10,... | collective-permute-start | bytes 884744 | tf_op jit(solution)/shard_map/ppermute | solution.py:467
  83.4 1.4 %collective-permute-start.21 = (f32[256,128]{1,0:T(8,128)S(1)}, f32[256,128]{1,0:T(8,128)S(1)}, u32[]{:S(2)}, u32[]{:S(2)}) collective-permute-start(f32[256,128]{1,0:T(8,128)S(1)} %constant_dynamic-update-slice_fusion.13.first_stats), channel_id=1, source_target_pairs={{0,1},{1,0},{2,3},{3,2},{4,5},{5,4},{6,7},{7,6},{8,9},{9,8},{10,11... | collective-permute-start | bytes 393224 | tf_op jit(solution)/shard_map/ppermute | solution.py:467
  89.4 16.9 %collective-permute-start.32 = (bf16[256,768]{1,0:T(8,128)(2,1)S(1)}, bf16[256,768]{1,0:T(8,128)(2,1)S(1)}, u32[]{:S(2)}, u32[]{:S(2)}) collective-permute-start(bf16[256,768]{1,0:T(8,128)(2,1)S(1)} %get-tuple-element.68.dk), channel_id=1, source_target_pairs={{0,1},{1,0},{2,3},{3,2},{4,5},{5,4},{6,7},{7,6},{8,9},{9,8},{10,11... | collective-permute-start | bytes 1179656 | tf_op jit(solution)/shard_map/ppermute | solution.py:467
  89.6 16.7 %collective-permute-start.33 = (bf16[256,768]{1,0:T(8,128)(2,1)S(1)}, bf16[256,768]{1,0:T(8,128)(2,1)S(1)}, u32[]{:S(2)}, u32[]{:S(2)}) collective-permute-start(bf16[256,768]{1,0:T(8,128)(2,1)S(1)} %get-tuple-element.69.dv), channel_id=1, source_target_pairs={{0,1},{1,0},{2,3},{3,2},{4,5},{5,4},{6,7},{7,6},{8,9},{9,8},{10,11... | collective-permute-start | bytes 1179656 | tf_op jit(solution)/shard_map/ppermute | solution.py:467
  96.4 7.0 %collective-permute-start.31 = (bf16[24,1536]{1,0:T(8,128)(2,1)S(1)}, bf16[24,1536]{1,0:T(8,128)(2,1)S(1)}, u32[]{:S(2)}, u32[]{:S(2)}) collective-permute-start(bf16[24,1536]{1,0:T(8,128)(2,1)S(1)} %get-tuple-element.88), channel_id=1, source_target_pairs={{0,24},{1,25},{2,26},{3,27},{4,28},{5,29},{6,30},{7,31},{8,16},{9,... | collective-permute-start | bytes 221192 | tf_op jit(solution)/shard_map/ppermute | solution.py:467
  99.0 6.6 %collective-permute-start.30 = (bf16[24,1536]{1,0:T(8,128)(2,1)S(1)}, bf16[24,1536]{1,0:T(8,128)(2,1)S(1)}, u32[]{:S(2)}, u32[]{:S(2)}) collective-permute-start(bf16[24,1536]{1,0:T(8,128)(2,1)S(1)} %get-tuple-element.89), channel_id=1, source_target_pairs={{0,16},{1,17},{2,18},{3,19},{4,20},{5,21},{6,22},{7,23},{8,24},{9,... | collective-permute-start | bytes 221192 | tf_op jit(solution)/shard_map/ppermute | solution.py:467
  99.0 6.6 %collective-permute-start.29 = (bf16[24,1536]{1,0:T(8,128)(2,1)S(1)}, bf16[24,1536]{1,0:T(8,128)(2,1)S(1)}, u32[]{:S(2)}, u32[]{:S(2)}) collective-permute-start(bf16[24,1536]{1,0:T(8,128)(2,1)S(1)} %get-tuple-element.87), channel_id=1, source_target_pairs={{0,8},{1,9},{2,10},{3,11},{4,12},{5,13},{6,14},{7,15},{8,0},{9,1},... | collective-permute-start | bytes 221192 | tf_op jit(solution)/shard_map/ppermute | solution.py:467
  107.1 7.6 %collective-permute-start.42 = (bf16[96,512]{1,0:T(8,128)(2,1)S(1)}, bf16[96,512]{1,0:T(8,128)(2,1)S(1)}, u32[]{:S(2)}, u32[]{:S(2)}) collective-permute-start(bf16[96,512]{1,0:T(8,128)(2,1)S(1)} %get-tuple-element.83), channel_id=1, source_target_pairs={{0,24},{1,25},{2,26},{3,27},{4,28},{5,29},{6,30},{7,31},{8,16},{9,... | collective-permute-start | bytes 294920 | tf_op jit(solution)/shard_map/ppermute | solution.py:467
  109.4 8.5 %collective-permute-start.41 = (bf16[96,512]{1,0:T(8,128)(2,1)S(1)}, bf16[96,512]{1,0:T(8,128)(2,1)S(1)}, u32[]{:S(2)}, u32[]{:S(2)}) collective-permute-start(bf16[96,512]{1,0:T(8,128)(2,1)S(1)} %get-tuple-element.84), channel_id=1, source_target_pairs={{0,16},{1,17},{2,18},{3,19},{4,20},{5,21},{6,22},{7,23},{8,24},{9,... | collective-permute-start | bytes 294920 | tf_op jit(solution)/shard_map/ppermute | solution.py:467
  109.4 8.5 %collective-permute-start.40 = (bf16[96,512]{1,0:T(8,128)(2,1)S(1)}, bf16[96,512]{1,0:T(8,128)(2,1)S(1)}, u32[]{:S(2)}, u32[]{:S(2)}) collective-permute-start(bf16[96,512]{1,0:T(8,128)(2,1)S(1)} %get-tuple-element.82), channel_id=1, source_target_pairs={{0,8},{1,9},{2,10},{3,11},{4,12},{5,13},{6,14},{7,15},{8,0},{9,1},... | collective-permute-start | bytes 294920 | tf_op jit(solution)/shard_map/ppermute | solution.py:467
  111.6 8.8 %collective-permute-start.36 = (bf16[96,1024]{1,0:T(8,128)(2,1)S(1)}, bf16[96,1024]{1,0:T(8,128)(2,1)S(1)}, u32[]{:S(2)}, u32[]{:S(2)}) collective-permute-start(bf16[96,1024]{1,0:T(8,128)(2,1)S(1)} %get-tuple-element.80), channel_id=1, source_target_pairs={{0,6},{1,7},{2,4},{3,5},{4,2},{5,3},{6,0},{7,1},{8,14},{9,15},{10,... | collective-permute-start | bytes 589832 | tf_op jit(solution)/shard_map/ppermute | solution.py:467
  113.0 10.1 %collective-permute-start.35 = (bf16[96,1024]{1,0:T(8,128)(2,1)S(1)}, bf16[96,1024]{1,0:T(8,128)(2,1)S(1)}, u32[]{:S(2)}, u32[]{:S(2)}) collective-permute-start(bf16[96,1024]{1,0:T(8,128)(2,1)S(1)} %get-tuple-element.81), channel_id=1, source_target_pairs={{0,4},{1,5},{2,6},{3,7},{4,0},{5,1},{6,2},{7,3},{8,12},{9,13},{10,... | collective-permute-start | bytes 589832 | tf_op jit(solution)/shard_map/ppermute | solution.py:467
  114.7 8.4 %collective-permute-start.34 = (bf16[96,1024]{1,0:T(8,128)(2,1)S(1)}, bf16[96,1024]{1,0:T(8,128)(2,1)S(1)}, u32[]{:S(2)}, u32[]{:S(2)}) collective-permute-start(bf16[96,1024]{1,0:T(8,128)(2,1)S(1)} %get-tuple-element.79), channel_id=1, source_target_pairs={{0,2},{1,3},{2,0},{3,1},{4,6},{5,7},{6,4},{7,5},{8,10},{9,11},{10,... | collective-permute-start | bytes 589832 | tf_op jit(solution)/shard_map/ppermute | solution.py:467
  118.0 7.6 %collective-permute-start.45 = (bf16[24,512]{1,0:T(8,128)(2,1)S(1)}, bf16[24,512]{1,0:T(8,128)(2,1)S(1)}, u32[]{:S(2)}, u32[]{:S(2)}) collective-permute-start(bf16[24,512]{1,0:T(8,128)(2,1)S(1)} %get-tuple-element.98), channel_id=1, source_target_pairs={{0,6},{1,7},{2,4},{3,5},{4,2},{5,3},{6,0},{7,1},{8,14},{9,15},{10,... | collective-permute-start | bytes 73736 | tf_op jit(solution)/shard_map/ppermute | solution.py:467
  119.8 7.9 %collective-permute-start.44 = (bf16[24,512]{1,0:T(8,128)(2,1)S(1)}, bf16[24,512]{1,0:T(8,128)(2,1)S(1)}, u32[]{:S(2)}, u32[]{:S(2)}) collective-permute-start(bf16[24,512]{1,0:T(8,128)(2,1)S(1)} %get-tuple-element.99), channel_id=1, source_target_pairs={{0,4},{1,5},{2,6},{3,7},{4,0},{5,1},{6,2},{7,3},{8,12},{9,13},{10,... | collective-permute-start | bytes 73736 | tf_op jit(solution)/shard_map/ppermute | solution.py:467
  120.5 7.2 %collective-permute-start.43 = (bf16[24,512]{1,0:T(8,128)(2,1)S(1)}, bf16[24,512]{1,0:T(8,128)(2,1)S(1)}, u32[]{:S(2)}, u32[]{:S(2)}) collective-permute-start(bf16[24,512]{1,0:T(8,128)(2,1)S(1)} %get-tuple-element.97), channel_id=1, source_target_pairs={{0,2},{1,3},{2,0},{3,1},{4,6},{5,7},{6,4},{7,5},{8,10},{9,11},{10,... | collective-permute-start | bytes 73736 | tf_op jit(solution)/shard_map/ppermute | solution.py:467
  123.2 6.0 %collective-permute-start.39 = (bf16[24,1024]{1,0:T(8,128)(2,1)S(1)}, bf16[24,1024]{1,0:T(8,128)(2,1)S(1)}, u32[]{:S(2)}, u32[]{:S(2)}) collective-permute-start(bf16[24,1024]{1,0:T(8,128)(2,1)S(1)} %get-tuple-element.91), channel_id=1, source_target_pairs={{0,24},{1,25},{2,26},{3,27},{4,28},{5,29},{6,30},{7,31},{8,16},{9,... | collective-permute-start | bytes 147464 | tf_op jit(solution)/shard_map/ppermute | solution.py:467
  125.6 5.2 %collective-permute-start.38 = (bf16[24,1024]{1,0:T(8,128)(2,1)S(1)}, bf16[24,1024]{1,0:T(8,128)(2,1)S(1)}, u32[]{:S(2)}, u32[]{:S(2)}) collective-permute-start(bf16[24,1024]{1,0:T(8,128)(2,1)S(1)} %get-tuple-element.92), channel_id=1, source_target_pairs={{0,16},{1,17},{2,18},{3,19},{4,20},{5,21},{6,22},{7,23},{8,24},{9,... | collective-permute-start | bytes 147464 | tf_op jit(solution)/shard_map/ppermute | solution.py:467
  125.6 5.2 %collective-permute-start.37 = (bf16[24,1024]{1,0:T(8,128)(2,1)S(1)}, bf16[24,1024]{1,0:T(8,128)(2,1)S(1)}, u32[]{:S(2)}, u32[]{:S(2)}) collective-permute-start(bf16[24,1024]{1,0:T(8,128)(2,1)S(1)} %get-tuple-element.90), channel_id=1, source_target_pairs={{0,8},{1,9},{2,10},{3,11},{4,12},{5,13},{6,14},{7,15},{8,0},{9,1},... | collective-permute-start | bytes 147464 | tf_op jit(solution)/shard_map/ppermute | solution.py:467
  (9 other events, 38.0 us)

commit v3 on v2

v3 whole, which is shorter than its diff:
```python
import functools

import jax
import jax.numpy as jnp
import numpy as np
from jax import lax
from jax.experimental import pallas as pl
from jax.experimental.pallas import tpu as pltpu
from jax.sharding import PartitionSpec as P

HEAD_DIM = 64
GROUP = 8
PAIR = 2 * HEAD_DIM
LANES = 128
SECOND = 16
SCALE = 0.125
BF = jnp.bfloat16
F32 = jnp.float32
NT = (((1,), (1,)), ((), ()))
NN = (((1,), (0,)), ((), ()))
TN = (((0,), (0,)), ((), ()))
LARGE = 1e30
LOAD_CUTS = 4
VMEM_BYTES = 40 * 1024 * 1024


def dot(a, b, dims=NN):
    return lax.dot_general(a, b, dims, preferred_element_type=F32)


def dot_exact(a, b):
    return lax.dot_general(a, b, NN, preferred_element_type=F32, precision=lax.Precision.HIGHEST)


def iota(shape, dim):
    return lax.broadcasted_iota(jnp.int32, shape, dim)


def low_half(shape):
    return iota(shape, len(shape) - 1) % PAIR < HEAD_DIM


def halves(x):
    low = low_half(x.shape)
    zero = jnp.zeros((), x.dtype)
    return jnp.where(low, x, zero), jnp.where(low, zero, x)


def by_head(first, second, rows):
    return jnp.where(low_half((rows, PAIR)), first, second)


class Sizes:
    def __init__(self, rows, width, dev_count):
        self.rows = rows
        self.width = width
        self.devs = dev_count
        self.heads = width // HEAD_DIM
        self.pairs = self.heads // 2
        self.mid = rows // GROUP
        self.far = rows // dev_count
        self.sel = 2 * self.mid
        self.far_held = -(-self.far // 16) * 16
        self.upper = dev_count // GROUP
        self.strip = width // dev_count
        self.half = width // 2


def chosen_row(z, index, off_mid, off_far):
    row = jnp.where(index < z.mid, index * GROUP + off_mid, (index - z.mid) * z.devs + off_far)
    return jnp.where(index < z.mid + z.far, row, -1)


def spread(z, offs_ref, pair, picked):
    lane = iota((1, 4 * z.sel), 1)
    second = (lane // z.sel) % 2 == 1
    off_mid = jnp.where(second, offs_ref[0, 2 * pair + 1], offs_ref[0, 2 * pair])
    off_far = jnp.where(second, offs_ref[1, 2 * pair + 1], offs_ref[1, 2 * pair])
    target = chosen_row(z, lane % z.sel, off_mid, off_far)
    place = (iota((z.rows, 4 * z.sel), 0) == target).astype(F32).astype(BF)
    high = picked.astype(BF)
    rest = (picked - high.astype(F32)).astype(BF)
    first_high, second_high = halves(high)
    first_rest, second_rest = halves(rest)
    stacked = jnp.concatenate([first_high, second_high, first_rest, second_rest], axis=0)
    return dot(place, stacked)


def lane_offsets(z, offs_ref):
    lane = iota((1, LANES), 1)
    off_mid = jnp.full((1, LANES), -1, jnp.int32)
    off_far = jnp.full((1, LANES), -1, jnp.int32)
    for head in range(z.heads):
        here = (lane == head) | (lane == SECOND + head)
        off_mid = jnp.where(here, offs_ref[0, head], off_mid)
        off_far = jnp.where(here, offs_ref[1, head], off_far)
    return off_mid, off_far


def stat_masks(z, offs_ref):
    off_mid, off_far = lane_offsets(z, offs_ref)
    row = iota((z.rows, LANES), 0)
    return row % GROUP == off_mid, row % z.devs == off_far


def pick_stats(z, masks, stats):
    entry = iota((z.sel, z.rows), 0)
    row = iota((z.sel, z.rows), 1)
    take_mid = ((entry < z.mid) & (row // GROUP == entry)).astype(F32)
    take_far = (row // z.devs == entry - z.mid).astype(F32)
    return dot_exact(take_mid, jnp.where(masks[0], stats, 0.0)) + dot_exact(
        take_far, jnp.where(masks[1], stats, 0.0)
    )


def spread_stats(z, masks, picked):
    row = iota((z.rows, z.sel), 0)
    entry = iota((z.rows, z.sel), 1)
    give_mid = ((entry < z.mid) & (row // GROUP == entry)).astype(F32)
    give_far = (row // z.devs == entry - z.mid).astype(F32)
    fill = jnp.where(iota((z.rows, LANES), 1) < SECOND, -jnp.inf, 0.0)
    return (
        jnp.where(masks[0], dot_exact(give_mid, picked), fill),
        jnp.where(masks[1], dot_exact(give_far, picked), fill),
    )


def gathered_place(z, own, level):
    index = iota((1, z.rows), 1)
    core = index // (4 * z.mid)
    plane = (index // z.mid) % 4
    inner = index % z.mid
    if level == 0:
        return (own ^ (core + 2 * plane)) * z.rows + inner * GROUP
    dev = own ^ (core + 2 * plane + GROUP * (inner // z.far))
    return dev * z.rows + (inner % z.far) * z.devs


def level_parts(z):
    return ((0, z.mid), (z.mid, z.mid + z.far_held))


def project_kernel(
    z, offs_hbm, tiles_hbm, w_qkv_hbm, cot_hbm, w_out_hbm, q, k, v, g, sel, far,
    offs_ref, tiles, w_qkv, cot, w_out, sems,
):
    width = z.width
    step = width // LOAD_CUTS

    def column_block(block):
        return [
            (
                w_qkv_hbm.at[pl.ds(i * step, step), pl.ds(block * width, width)],
                w_qkv.at[pl.ds(i * step, step), pl.ds(block * width, width)],
            )
            for i in range(LOAD_CUTS)
        ]

    groups = [
        [(tiles_hbm, tiles)] + column_block(1),
        column_block(2),
        column_block(0),
        [(cot_hbm, cot)]
        + [
            (w_out_hbm.at[pl.ds(i * step, step), :], w_out.at[pl.ds(i * step, step), :])
            for i in range(LOAD_CUTS)
        ],
        [(offs_hbm, offs_ref)],
    ]
    copies, index = [], 0
    for group in groups:
        made = []
        for source, target in group:
            copy = pltpu.make_async_copy(source, target, sems.at[index])
            copy.start()
            made.append(copy)
            index += 1
        copies.append(made)

    def arrived(group):
        for copy in copies[group]:
            copy.wait()

    arrived(0)
    own = tiles[...]
    k[...] = dot(own, w_qkv[:, width : 2 * width]).astype(BF)
    arrived(1)
    v[...] = dot(own, w_qkv[:, 2 * width :]).astype(BF)
    arrived(2)
    q[...] = dot(own, w_qkv[:, :width]).astype(BF) * jnp.asarray(SCALE, BF)
    arrived(3)
    g[...] = dot(cot[...], w_out[...], NT).astype(BF)
    arrived(4)
    entry = iota((2 * z.sel, z.rows), 0)
    column = iota((2 * z.sel, z.rows), 1)
    second = entry >= z.sel
    for pair in range(z.pairs):
        lanes = slice(pair * PAIR, (pair + 1) * PAIR)
        off_mid = jnp.where(second, offs_ref[0, 2 * pair + 1], offs_ref[0, 2 * pair])
        off_far = jnp.where(second, offs_ref[1, 2 * pair + 1], offs_ref[1, 2 * pair])
        target = chosen_row(z, entry % z.sel, off_mid, off_far)
        take = (column == target).astype(F32).astype(BF)
        every = jnp.concatenate([k[:, lanes], v[:, lanes], q[:, lanes], g[:, lanes]], axis=1)
        both = dot(take, every)
        picked = jnp.where(low_half((z.sel, 4 * PAIR)), both[: z.sel], both[z.sel :]).astype(BF)
        far_part = jnp.where(
            low_half((z.far, 4 * PAIR)),
            both[z.mid : z.mid + z.far],
            both[z.sel + z.mid : z.sel + z.mid + z.far],
        ).astype(BF)
        for part in range(4):
            to = slice(part * width + pair * PAIR, part * width + (pair + 1) * PAIR)
            sel[:, to] = picked[:, part * PAIR : (part + 1) * PAIR]
            far[:, to] = far_part[:, part * PAIR : (part + 1) * PAIR]


def near_kernel(z, pad_ref, q, k, v, g, tiles, order, mixed, stats, turned, turned_out):
    own = lax.axis_index("ctx")
    limit = z.rows * z.devs - pad_ref[0] - own * z.rows
    valid = iota((1, z.rows), 1) < limit
    lane = iota((z.rows, LANES), 1)
    both = jnp.zeros((z.rows, LANES), F32)
    for pair in range(z.pairs):
        lanes = slice(pair * PAIR, (pair + 1) * PAIR)
        query = q[:, lanes]
        grad = g[:, lanes].astype(F32)
        keys = halves(k[:, lanes])
        values = halves(v[:, lanes])
        total = None
        for side in range(2):
            head = 2 * pair + side
            scores = jnp.where(valid, dot(query, keys[side], NT), -jnp.inf)
            peak = jnp.max(scores, axis=1, keepdims=True)
            powers = jnp.exp(scores - peak)
            summed = jnp.sum(powers, axis=1, keepdims=True)
            part = dot(powers.astype(BF), values[side]) * (1.0 / summed)
            total = part if total is None else total + part
            both = jnp.where(lane == head, peak + jnp.log(summed), both)
            meets = jnp.sum(grad * part, axis=1, keepdims=True)
            both = jnp.where(lane == SECOND + head, meets, both)
        mixed[:, lanes] = total
    stats[...] = both
    for part, target in enumerate((turned, turned_out)):
        source = order[part * z.half : (part + 1) * z.half, :]
        place = (iota((z.half, z.width), 1) == source).astype(F32).astype(BF)
        target[...] = dot(place, tiles[...], NT).astype(BF)


def of_level(level, refs, lanes):
    return jnp.concatenate([ref[:, lanes] for ref in refs[level]], axis=0)


def part_lanes(z, part, pair):
    return slice(part * z.width + pair * PAIR, part * z.width + (pair + 1) * PAIR)


def own_scores(z, limit, offs_ref, sel, refs):
    own = lax.axis_index("ctx")
    scores, places = [], []
    for level, (start, stop) in enumerate(level_parts(z)):
        place = gathered_place(z, own, level)
        for pair in range(z.pairs):
            query = sel[start:stop, part_lanes(z, 2, pair)]
            keys = halves(of_level(level, refs, part_lanes(z, 0, pair)))
            for side in range(2):
                valid = place + offs_ref[level, 2 * pair + side] < limit
                scores.append(jnp.where(valid, dot(query, keys[side], NT), -jnp.inf))
                places.append((level, 2 * pair + side, start, stop))
    spots, at = [], 0
    for level, head, start, stop in places:
        spots.append((level, head, at, at + stop - start))
        at += stop - start
    return jnp.concatenate(scores, axis=0), spots


def to_lanes(z, spots, columns):
    parts = []
    for level, (start, stop) in enumerate(level_parts(z)):
        lane = iota((stop - start, LANES), 1)
        part = jnp.zeros((stop - start, LANES), F32)
        for found, head, first, last in spots:
            if found == level:
                for shift, column in columns:
                    part = jnp.where(lane == shift + head, column[first:last], part)
        parts.append(part)
    parts.append(jnp.zeros((z.sel - level_parts(z)[1][1], LANES), F32))
    return jnp.concatenate(parts, axis=0)


def from_lanes(spots, array, shift):
    return lambda z: jnp.concatenate(
        [
            array[level_parts(z)[level][0] : level_parts(z)[level][1], shift + head : shift + head + 1]
            for level, head, _, _ in spots
        ],
        axis=0,
    )


def spot_of(spots, level, head):
    return next((first, last) for found, at, first, last in spots if (found, at) == (level, head))


def join_kernel(
    z, offs_ref, pad_ref, sel, mid_0, mid_1, far_0, far_1, near_stats, stats, picked, raw, held
):
    refs = ((mid_0, mid_1), (far_0, far_1))
    scores, spots = own_scores(z, z.rows * z.devs - pad_ref[0], offs_ref, sel, refs)
    peak = jnp.max(scores, axis=1, keepdims=True)
    powers = jnp.exp(scores - peak)
    summed = jnp.sum(powers, axis=1, keepdims=True)
    lse = peak + jnp.log(summed)
    scale = 1.0 / summed
    powers = powers.astype(BF)
    products = []
    tail = jnp.zeros((z.sel - level_parts(z)[1][1], PAIR), F32)
    for pair in range(z.pairs):
        totals = []
        for level, (start, stop) in enumerate(level_parts(z)):
            values = halves(of_level(level, refs, part_lanes(z, 1, pair)))
            parts = []
            for side in range(2):
                at, to = spot_of(spots, level, 2 * pair + side)
                parts.append(dot(powers[at:to], values[side]) * scale[at:to])
            totals.append(parts[0] + parts[1])
            grad = sel[start:stop, part_lanes(z, 3, pair)].astype(F32)
            products.append((level, pair, [grad * part for part in parts]))
        held[:, pair * PAIR : (pair + 1) * PAIR] = jnp.concatenate(totals + [tail], axis=0)
    products.sort(key=lambda entry: entry[:2])
    stacked = jnp.concatenate([part for _, _, both in products for part in both], axis=0)
    meets = jnp.sum(stacked, axis=1, keepdims=True)
    sel_both = to_lanes(z, spots, ((0, lse), (SECOND, meets)))
    raw[...] = sel_both
    masks = stat_masks(z, offs_ref)
    near = near_stats[...]
    mid, far = spread_stats(z, masks, sel_both)
    top = jnp.maximum(near, jnp.maximum(mid, far))
    total_lse = top + jnp.log(jnp.exp(near - top) + jnp.exp(mid - top) + jnp.exp(far - top))
    delta = sum(
        pltpu.roll(jnp.exp(value - total_lse), SECOND, 1) * value
        for value in (
            near,
            jnp.where(masks[0], mid, -LARGE),
            jnp.where(masks[1], far, -LARGE),
        )
    )
    both = jnp.where(iota((z.rows, LANES), 1) < SECOND, total_lse, delta)
    stats[...] = both
    picked[...] = pick_stats(z, masks, both)


def output_kernel(
    z, offs_ref, near_stats, stats, picked, raw, mixed, held, tiles, w_out, order,
    rows_out, turned, turned_out, attn,
):
    near_share = jnp.exp(near_stats[...] - stats[...])
    share = jnp.exp(raw[...] - picked[...])
    for pair in range(z.pairs):
        lanes = slice(pair * PAIR, (pair + 1) * PAIR)
        near = by_head(
            near_share[:, 2 * pair : 2 * pair + 1],
            near_share[:, 2 * pair + 1 : 2 * pair + 2],
            z.rows,
        )
        own = by_head(share[:, 2 * pair : 2 * pair + 1], share[:, 2 * pair + 1 : 2 * pair + 2], z.sel)
        combined = near * mixed[:, lanes] + spread(z, offs_ref, pair, own * held[:, lanes])
        attn[:, lanes] = combined.astype(BF)
    rows_out[...] = (tiles[...].astype(F32) + dot(attn[...], w_out[...])).astype(BF)
    for part, target in enumerate((turned, turned_out)):
        source = order[part * z.half : (part + 1) * z.half, :]
        place = (iota((z.half, z.width), 1) == source).astype(F32).astype(BF)
        target[...] = dot(place, attn[...], NT).astype(BF)


def near_grads_kernel(
    z, offs_ref, pad_ref, q, k, v, g, stats, sel, mid_0, mid_1, far_0, far_1, picked,
    dq, dk, dv, dq_sel,
):
    own = lax.axis_index("ctx")
    limit = z.rows * z.devs - pad_ref[0]
    refs = ((mid_0, mid_1), (far_0, far_1))
    scores, spots = own_scores(z, limit, offs_ref, sel, refs)
    probs = jnp.exp(scores - from_lanes(spots, picked, 0)(z))
    grad_probs = []
    for level, (start, stop) in enumerate(level_parts(z)):
        for pair in range(z.pairs):
            grad = sel[start:stop, part_lanes(z, 3, pair)]
            values = halves(of_level(level, refs, part_lanes(z, 1, pair)))
            grad_probs += [dot(grad, values[side], NT) for side in range(2)]
    grad_probs = jnp.concatenate(grad_probs, axis=0) - from_lanes(spots, picked, SECOND)(z)
    grad_scores = (probs * grad_probs).astype(BF)
    tail = jnp.zeros((z.sel - level_parts(z)[1][1], PAIR), F32)
    for pair in range(z.pairs):
        sums = []
        for level in range(2):
            keys = halves(of_level(level, refs, part_lanes(z, 0, pair)))
            at, to = spot_of(spots, level, 2 * pair)
            low = dot(grad_scores[at:to], keys[0])
            at, to = spot_of(spots, level, 2 * pair + 1)
            sums.append(low + dot(grad_scores[at:to], keys[1]))
        dq_sel[:, pair * PAIR : (pair + 1) * PAIR] = jnp.concatenate(sums + [tail], axis=0)
    valid_near = iota((z.rows, 1), 0) < limit - own * z.rows
    across = jnp.transpose(stats[...])
    for pair in range(z.pairs):
        lanes = slice(pair * PAIR, (pair + 1) * PAIR)
        query, grad = q[:, lanes], g[:, lanes]
        queries, grads = halves(query), halves(grad)
        keys, values = halves(k[:, lanes]), halves(v[:, lanes])
        sum_q = sum_k = sum_v = None
        for side in range(2):
            head = 2 * pair + side
            scores = jnp.where(valid_near, dot(keys[side], query, NT), -jnp.inf)
            probs = jnp.exp(scores - across[head : head + 1, :])
            grad_probs = dot(values[side], grad, NT)
            grad_scores = probs * (grad_probs - across[SECOND + head : SECOND + head + 1, :])
            grad_scores = grad_scores.astype(BF)
            part_k = dot(grad_scores, queries[side])
            part_v = dot(probs.astype(BF), grads[side])
            part_q = dot(grad_scores, keys[side], TN)
            if side == 0:
                sum_q, sum_k, sum_v = part_q, part_k, part_v
            else:
                sum_q, sum_k, sum_v = sum_q + part_q, sum_k + part_k, sum_v + part_v
        dk[:, lanes] = sum_k
        dv[:, lanes] = sum_v
        dq[:, lanes] = (SCALE * (sum_q + spread(z, offs_ref, pair, dq_sel[:, lanes]))).astype(BF)


def key_grads_kernel(
    z, offs_ref, pad_ref, sel, mid_0, mid_1, far_0, far_1, stats_0, stats_1, dk_near, dv_near, dk, dv
):
    own = lax.axis_index("ctx")
    limit = z.rows * z.devs - pad_ref[0] - own * z.rows
    parts = level_parts(z)
    refs = ((mid_0, mid_1), (far_0, far_1))
    stat_refs = (stats_0, stats_1)
    first_part = (2, 0)
    tail = jnp.zeros((z.sel - parts[1][1], PAIR), F32)
    probs, grad_scores = {}, {}
    for level, (start, stop) in enumerate(parts):
        across = jnp.transpose(jnp.concatenate([ref[level * 4 * z.mid : (level + 1) * 4 * z.mid, :] for ref in stat_refs], axis=0))
        entry = iota((stop - start, 1), 0) + start
        for pair in range(z.pairs):
            keys = sel[start:stop, part_lanes(z, 0, pair)]
            values = sel[start:stop, part_lanes(z, 1, pair)]
            queries = halves(of_level(level, refs, part_lanes(z, first_part[level], pair)))
            grads = halves(of_level(level, refs, part_lanes(z, first_part[level] + 1, pair)))
            for side in range(2):
                head = 2 * pair + side
                at = chosen_row(z, entry, offs_ref[0, head], offs_ref[1, head])
                valid = (at >= 0) & (at < limit)
                scores = jnp.where(valid, dot(keys, queries[side], NT), -jnp.inf)
                exps = jnp.exp(scores - across[head : head + 1, :])
                grad_probs = dot(values, grads[side], NT)
                grad_probs = grad_probs - across[SECOND + head : SECOND + head + 1, :]
                probs[level, head] = exps.astype(BF)
                grad_scores[level, head] = (exps * grad_probs).astype(BF)
    sums_k, sums_v = {}, {}
    for pair in range(z.pairs):
        both_k, both_v = [], []
        for level in range(2):
            queries = halves(of_level(level, refs, part_lanes(z, first_part[level], pair)))
            grads = halves(of_level(level, refs, part_lanes(z, first_part[level] + 1, pair)))
            low, high = 2 * pair, 2 * pair + 1
            both_k.append(
                dot(grad_scores[level, low], queries[0]) + dot(grad_scores[level, high], queries[1])
            )
            both_v.append(dot(probs[level, low], grads[0]) + dot(probs[level, high], grads[1]))
        sums_k[pair] = jnp.concatenate(both_k + [tail], axis=0)
        sums_v[pair] = jnp.concatenate(both_v + [tail], axis=0)
    for pair in range(z.pairs):
        lanes = slice(pair * PAIR, (pair + 1) * PAIR)
        both = jnp.concatenate([sums_k[pair], sums_v[pair]], axis=1)
        moved = spread(z, offs_ref, pair, both)
        dk[:, lanes] = (dk_near[:, lanes] + moved[:, :PAIR]).astype(BF)
        dv[:, lanes] = (dv_near[:, lanes] + moved[:, PAIR:]).astype(BF)


def early_weights_kernel(
    z, turned, turned_other, attn, attn_other, dq, dq_other, cot, cot_other, out
):
    width = z.width
    out[:, :width] = (dot(attn[...], cot[...]) + dot(attn_other[...], cot_other[...])).astype(BF)
    out[:, width:] = (dot(turned[...], dq[...]) + dot(turned_other[...], dq_other[...])).astype(BF)


def late_weights_kernel(z, turned, turned_other, dk, dv, dk_other, dv_other, out):
    width = z.width
    out[:, :width] = (dot(turned[...], dk[...]) + dot(turned_other[...], dk_other[...])).astype(BF)
    out[:, width:] = (dot(turned[...], dv[...]) + dot(turned_other[...], dv_other[...])).astype(BF)


def tiles_kernel(z, dq, dk, dv, w_qkv, out):
    width = z.width
    out[...] = (
        dot(dq[...], w_qkv[:, :width], NT)
        + dot(dk[...], w_qkv[:, width : 2 * width], NT)
        + dot(dv[...], w_qkv[:, 2 * width :], NT)
    ).astype(BF)


def call(kernel, outs, flops, scratch=(), smem=0, spaces=None, vmem=VMEM_BYTES):
    def run(*args):
        moved = sum(int(np.prod(a.shape)) * a.dtype.itemsize for a in args)
        moved += sum(int(np.prod(s)) * jnp.dtype(t).itemsize for s, t in outs)
        specs = [
            pl.BlockSpec(memory_space=spaces or (pltpu.SMEM if i < smem else pltpu.VMEM))
            for i in range(len(args))
        ]
        return pl.pallas_call(
            kernel,
            out_shape=tuple(jax.ShapeDtypeStruct(s, t) for s, t in outs),
            in_specs=specs,
            out_specs=tuple(pl.BlockSpec(memory_space=pltpu.VMEM) for _ in outs),
            scratch_shapes=list(scratch),
            compiler_params=pltpu.CompilerParams(vmem_limit_bytes=vmem),
            cost_estimate=pl.CostEstimate(
                flops=int(flops), bytes_accessed=int(moved), transcendentals=0
            ),
        )(*args)

    return run


def swap(value, mask, dev_count):
    return lax.ppermute(value, "ctx", [(d, d ^ mask) for d in range(dev_count)])


def upper_steps(dev_count):
    steps, base = [], GROUP
    while base < dev_count:
        count = 4 if base * 4 <= dev_count else 2
        steps.append((base, count))
        base *= count
    return steps


PLANE = (2, 4)


def tied(parts, first):
    return list(lax.optimization_barrier((*parts, *first))[: len(parts)]) if first else list(parts)


def plane_parts(value, dev_count, first=()):
    base, count = PLANE
    return tied(
        [value] + [swap(value, base * i, dev_count) for i in range(1, count)], first
    )


def doubled(value, masks, dev_count, first=()):
    for i, mask in enumerate(masks):
        parts = tied([value, swap(value, mask, dev_count)], first if i == 0 else ())
        value = jnp.concatenate(parts, axis=0)
    return value


def halved(value, masks, dev_count):
    for i, mask in enumerate(masks):
        size = value.shape[0] // 2
        total = value[:size].astype(F32) + swap(value[size:], mask, dev_count).astype(F32)
        value = total if i == len(masks) - 1 else total.astype(BF)
    return value


def reduce_step(value, step, dev_count, dtype, first=()):
    base, count = step
    size = value.shape[0] // count
    parts = [value[:size]] + [
        swap(value[i * size : (i + 1) * size], base * i, dev_count) for i in range(1, count)
    ]
    return sum(part.astype(F32) for part in tied(parts, first)).astype(dtype)


def reduce_all(value, steps, dev_count):
    for i, step in enumerate(steps):
        value = reduce_step(value, step, dev_count, F32 if i == len(steps) - 1 else BF)
    return value


def strip_order(z, own):
    core, plane, upper, row = np.meshgrid(
        np.arange(2), np.arange(4), np.arange(z.upper), np.arange(z.strip), indexing="ij"
    )
    mask = (core + 2 * plane + GROUP * upper).reshape(-1, 1).astype(np.int32)
    return (own ^ mask) * z.strip + row.reshape(-1, 1).astype(np.int32)


def after(value, *others):
    return lax.optimization_barrier((value, *others))[0]


def per_device(tiles, w_qkv, w_out, cotangent, offsets, pad_count):
    n = lax.axis_size("ctx")
    z = Sizes(tiles.shape[0], tiles.shape[1], n)
    own = lax.axis_index("ctx")
    rows, width = z.rows, z.width
    order = strip_order(z, own)
    base_flops = 2 * rows * rows * width

    q, k, v, g, sel, far = call(
        functools.partial(project_kernel, z),
        [((rows, width), BF)] * 4 + [((z.sel, 4 * width), BF), ((z.far, 4 * width), BF)],
        2 * rows * width * 4 * width,
        scratch=[
            pltpu.SMEM(offsets.shape, jnp.int32),
            pltpu.VMEM(tiles.shape, BF),
            pltpu.VMEM(w_qkv.shape, BF),
            pltpu.VMEM(cotangent.shape, BF),
            pltpu.VMEM(w_out.shape, BF),
            pltpu.SemaphoreType.DMA((4 * LOAD_CUTS + 3,)),
        ],
        spaces=pltpu.HBM,
        vmem=61 * 1024 * 1024,
    )(offsets, tiles, w_qkv, cotangent, w_out)

    masks = [mask for mask in (2**i for i in range(30)) if GROUP <= mask < n]
    far_up = doubled(far, masks, n)
    mid_parts = plane_parts(sel[: z.mid], n)
    mixed, near_stats, turned, turned_out = call(
        functools.partial(near_kernel, z),
        [
            ((rows, width), F32),
            ((rows, LANES), F32),
            ((z.half, rows), BF),
            ((z.half, rows), BF),
        ],
        8 * base_flops,
        smem=1,
    )(pad_count, after(q, far_up), k, v, g, tiles, order)
    mid_0 = jnp.concatenate(mid_parts, axis=0)
    mid_1 = swap(mid_0, 1, n)
    far_parts = plane_parts(far_up, n, (near_stats,))
    far_0 = jnp.concatenate([part[:, : 2 * width] for part in far_parts], axis=0)
    far_1 = swap(far_0, 1, n)
    far_qg_0 = jnp.concatenate([part[:, 2 * width :] for part in far_parts], axis=0)
    far_qg_1 = swap(far_qg_0, 1, n)

    stats, picked, raw, held = call(
        functools.partial(join_kernel, z),
        [((rows, LANES), F32), ((z.sel, LANES), F32), ((z.sel, LANES), F32), ((z.sel, width), F32)],
        3 * base_flops,
        smem=2,
    )(offsets, pad_count, sel, mid_0, mid_1, far_0, far_1, near_stats)

    out_rows, attn_turned, attn_turned_out = call(
        functools.partial(output_kernel, z),
        [((rows, width), BF), ((z.half, rows), BF), ((z.half, rows), BF)],
        6 * rows * width * width,
        scratch=[pltpu.VMEM((rows, width), BF)],
        smem=1,
    )(offsets, near_stats, stats, picked, raw, mixed, held, tiles, w_out, order)
    attn_other = swap(attn_turned_out, 1, n)
    turned_other = swap(after(turned_out, picked), 1, n)
    cot_other = swap(after(cotangent, picked), 1, n)

    dq, dk_near, dv_near = call(
        functools.partial(near_grads_kernel, z),
        [((rows, width), BF), ((rows, width), F32), ((rows, width), F32)],
        8 * base_flops,
        scratch=[pltpu.VMEM((z.sel, width), F32)],
        smem=2,
    )(offsets, pad_count, q, k, v, g, stats, sel, mid_0, mid_1, far_0, far_1, picked)
    dq_other = swap(dq, 1, n)

    stats_up = doubled(picked[z.mid : z.mid + z.far], masks, n, (out_rows,))
    stats_plane = [doubled(part, (2, 4), n) for part in (jnp.concatenate([picked[: z.mid], stats_up], axis=1),)]
    stats_0 = jnp.concatenate([stats_plane[0][:, :LANES], stats_plane[0][:, LANES:]], axis=0)
    stats_1 = swap(stats_0, 1, n)

    (early_half,) = call(
        functools.partial(early_weights_kernel, z),
        [((z.half, 2 * width), BF)],
        4 * rows * width * width,
    )(turned, turned_other, attn_turned, attn_other, dq, dq_other, cotangent, cot_other)

    dk, dv = call(
        functools.partial(key_grads_kernel, z),
        [((rows, width), BF), ((rows, width), BF)],
        3 * base_flops,
        smem=2,
    )(
        offsets, pad_count, sel, mid_0, mid_1, far_qg_0, far_qg_1, stats_0, stats_1,
        after(dk_near, early_half), dv_near,
    )
    dk_other = swap(dk, 1, n)
    dv_other = swap(dv, 1, n)
    (late_half,) = call(
        functools.partial(late_weights_kernel, z),
        [((z.half, 2 * width), BF)],
        4 * rows * width * width,
    )(turned, turned_other, dk, dv, dk_other, dv_other)
    (grad_tiles,) = call(
        functools.partial(tiles_kernel, z), [((rows, width), BF)], 6 * rows * width * width
    )(after(dq, late_half), dk, dv, w_qkv)
    late = reduce_step(late_half, PLANE, n, BF)
    early = reduce_step(early_half, PLANE, n, BF, (late_half,))
    early = halved(early, masks[::-1], n)
    late = reduce_all(late, upper_steps(n)[::-1], n)
    grad_wqkv = jnp.concatenate([early[:, width:], late], axis=1)
    return out_rows, grad_tiles, grad_wqkv, early[:, :width]


def solution(mesh):
    return jax.shard_map(
        per_device,
        mesh=mesh,
        in_specs=(P("ctx", None), P(), P(), P("ctx", None), P(), P()),
        out_specs=(P("ctx", None), P("ctx", None), P("ctx", None), P("ctx", None)),
        check_vma=False,
    )
```

time: 132 us -> 110 us (0.83)
  starting transfers between devices: 47.8 us -> 36.5 us
  Pallas kernels: 29.8 us -> 23.4 us
  local copies, waits for them, and re-layouts: 6.9 us -> 3.67 us
  waiting for transfers between devices: 42.9 us -> 41.5 us
    ppermute x46 -> x33, starting transfers between devices: 47.8 us -> 36.5 us  [swap(): return lax.ppermute(value, 'ctx', [(d, d ^ mask) for d in range(dev_count)])]
    pallas_call x9, Pallas kernels: 29.8 us -> 23.4 us  [run(): pl.pallas_call(kernel, out_shape=tuple((jax.ShapeDtypeStruct(s, t) for s,...]
    unnamed x35 -> x26, local copies, waits for them, and re-layouts: 6.04 us -> 1.7 us
    concatenate x4 -> x10, other arithmetic: 0.77 us -> 2.6 us  [the longest x1 0.98 us: per_device(): mid_0 = jnp.concatenate(mid_parts, axis=0)]
    ppermute x46 -> x33, waiting for transfers between devices: 42.9 us -> 41.5 us  [swap(): return lax.ppermute(value, 'ctx', [(d, d ^ mask) for d in range(dev_count)])]
  transfers between devices with their start and end apart: 46 -> 33, of which waited for: 20 -> 17; matrix products, arithmetic and copies ran while one was open for 2% -> 4% of each run, Pallas kernels for 20% -> 12%
where the time goes in v3:
time: 110 us
  waiting for transfers between devices  41.5 us (38%)
  starting transfers between devices  36.5 us (33%)
  Pallas kernels  23.4 us (21%)
  local copies, waits for them, and re-layouts  3.67 us (3%)
  other arithmetic  3.03 us (3%)
  between operations  1.67 us (2%)
    ppermute x33, waiting for transfers between devices, swap(): return lax.ppermute(value, 'ctx', [(d, d ^ mask) for d in range(dev_count)])  41.5 us
    ppermute x33, starting transfers between devices, swap(): return lax.ppermute(value, 'ctx', [(d, d ^ mask) for d in range(dev_count)])  36.5 us
    pallas_call x9, Pallas kernels, run(): pl.pallas_call(kernel, out_shape=tuple((jax.ShapeDtypeStruct(s, t) for s,...  23.4 us
  transfers between devices with their start and end apart: 33, of which 17 were waited for; matrix products, arithmetic and copies ran while one was open for 4% of the time, Pallas kernels for 12%

profile of v3, /device:TPU:0, one launch (start us, length us, event | category | flops | bytes accessed | tf_op | source)
XLA Modules:
  0.0 109.8 jit_solution(5672765003962303132)
XLA Ops:
  0.7 5.3 %shard_map.111 = (bf16[256,768]{1,0:T(8,128)(2,1)}, bf16[256,768]{1,0:T(8,128)(2,1)}, bf16[256,768]{1,0:T(8,128)(2,1)}, bf16[256,768]{1,0:T(8,128)(2,1)}, bf16[6...) custom-call(s32[2,12]{1,0:T(2,128)} %offs_ref.7, bf16[256,768]{1,0:T(8,128)(2,1)} %tiles.3, bf16[768,2304]{1,0:T(8,128)(2,1)} %w_qkv.1, ...), custom_call_target="tpu_custom_call" | custom-call | flops 1207959552 | bytes 7520352 | tf_op jit(solution)/shard_map/pallas_call | solution.py:510
  6.0 1.1 slice.93
  7.1 4.0 %collective-permute-start.4 = (bf16[32,3072]{1,0:T(8,128)(2,1)S(1)}, bf16[32,3072]{1,0:T(8,128)(2,1)S(1)}, u32[]{:S(2)}, u32[]{:S(2)}) collective-permute-start(bf16[32,3072]{1,0:T(8,128)(2,1)S(1)} %slice.93), channel_id=1, source_target_pairs={{0,6},{1,7},{2,4},{3,5},{4,2},{5,3},{6,0},{7,1},{8,14},{9,15},{10,... | collective-permute-start | bytes 589832 | tf_op jit(solution)/shard_map/ppermute | solution.py:526
  11.7 2.0 %collective-permute-start = (bf16[8,3072]{1,0:T(8,128)(2,1)}, bf16[8,3072]{1,0:T(8,128)(2,1)}, u32[]{:S(2)}, u32[]{:S(2)}) collective-permute-start(bf16[8,3072]{1,0:T(8,128)(2,1)} %get-tuple-element.42), channel_id=1, source_target_pairs={{0,8},{1,9},{2,10},{3,11},{4,12},{5,13},{6,14},{7,15},{8,0},{9,1},... | collective-permute-start | bytes 147464 | tf_op jit(solution)/shard_map/ppermute | solution.py:526
  13.7 0.8 constant_dynamic-update-slice_fusion.2
  15.2 0.9 collective-permute-done
  16.1 0.8 pad_maximum_fusion.6
  16.9 3.0 %collective-permute-start.1 = (bf16[16,3072]{1,0:T(8,128)(2,1)S(1)}, bf16[16,3072]{1,0:T(8,128)(2,1)S(1)}, u32[]{:S(2)}, u32[]{:S(2)}) collective-permute-start(bf16[16,3072]{1,0:T(8,128)(2,1)S(1)} %pad_maximum_fusion.6), channel_id=1, source_target_pairs={{0,16},{1,17},{2,18},{3,19},{4,20},{5,21},{6,22},{7,23},{8,24},{9,... | collective-permute-start | bytes 294920 | tf_op jit(solution)/shard_map/ppermute | solution.py:526
  20.0 0.8 constant_dynamic-update-slice_fusion.1
  20.8 1.8 %collective-permute-done.1 = bf16[16,3072]{1,0:T(8,128)(2,1)S(1)} collective-permute-done((bf16[16,3072]{1,0:T(8,128)(2,1)S(1)}, bf16[16,3072]{1,0:T(8,128)(2,1)S(1)}, u32[]{:S(2)}, u32[]{:S(2)}) %collective-permute-start.1) | collective-permute-done | bytes 98336 | tf_op jit(solution)/shard_map/ppermute | solution.py:526
  22.6 1.9 %collective-permute-start.6 = (bf16[32,3072]{1,0:T(8,128)(2,1)S(1)}, bf16[32,3072]{1,0:T(8,128)(2,1)S(1)}, u32[]{:S(2)}, u32[]{:S(2)}) collective-permute-start(bf16[32,3072]{1,0:T(8,128)(2,1)S(1)} %constant_dynamic-update-slice_fusion), channel_id=1, source_target_pairs={{0,2},{1,3},{2,0},{3,1},{4,6},{5,7},{6,4},{7,5},{8,10},{9,11},{10,... | collective-permute-start | bytes 589832 | tf_op jit(solution)/shard_map/ppermute | solution.py:526
  24.5 1.5 %collective-permute-start.7 = (bf16[32,3072]{1,0:T(8,128)(2,1)S(1)}, bf16[32,3072]{1,0:T(8,128)(2,1)S(1)}, u32[]{:S(2)}, u32[]{:S(2)}) collective-permute-start(bf16[32,3072]{1,0:T(8,128)(2,1)S(1)} %constant_dynamic-update-slice_fusion), channel_id=1, source_target_pairs={{0,4},{1,5},{2,6},{3,7},{4,0},{5,1},{6,2},{7,3},{8,12},{9,13},{10,... | collective-permute-start | bytes 589832 | tf_op jit(solution)/shard_map/ppermute | solution.py:526
  26.0 2.3 %shard_map.112 = (f32[256,768]{1,0:T(8,128)S(1)}, f32[256,128]{1,0:T(8,128)S(1)}, bf16[384,256]{1,0:T(8,128)(2,1)S(1)}, bf16[384,256]{1,0:T(8,128)(2,1)S(1)}) custom-call(s32[1]{0:T(128)S(6)} %copy.15.pad_ref, bf16[256,768]{1,0:T(8,128)(2,1)S(1)} %copy-done.5, bf16[256,768]{1,0:T(8,128)(2,1)S(1)} %copy-done.6, bf16[256,768]{1,0:T(8,128)(2,1)S(1)} %copy-done.7, ...), custom_call_target="tpu_custom_call" | custom-call | flops 805306368 | bytes 3279876 | tf_op jit(solution)/shard_map/pallas_call | solution.py:510
  28.5 1.0 pad_maximum_fusion.mid_0
  29.6 2.6 %collective-permute-done.7 = bf16[32,3072]{1,0:T(8,128)(2,1)S(1)} collective-permute-done((bf16[32,3072]{1,0:T(8,128)(2,1)S(1)}, bf16[32,3072]{1,0:T(8,128)(2,1)S(1)}, u32[]{:S(2)}, u32[]{:S(2)}) %collective-permute-start.7) | collective-permute-done | bytes 196640 | tf_op jit(solution)/shard_map/ppermute | solution.py:526
  32.3 2.7 %collective-permute-done.8 = bf16[32,3072]{1,0:T(8,128)(2,1)S(1)} collective-permute-done((bf16[32,3072]{1,0:T(8,128)(2,1)S(1)}, bf16[32,3072]{1,0:T(8,128)(2,1)S(1)}, u32[]{:S(2)}, u32[]{:S(2)}) %collective-permute-start.8) | collective-permute-done | bytes 196640 | tf_op jit(solution)/shard_map/ppermute | solution.py:526
  35.1 1.7 %collective-permute-done.9.far_1 = bf16[128,1536]{1,0:T(8,128)(2,1)S(1)} collective-permute-done((bf16[128,1536]{1,0:T(8,128)(2,1)S(1)}, bf16[128,1536]{1,0:T(8,128)(2,1)S(1)}, u32[]{:S(2)}, u32[]{:S(2)}) %collective-permute-start.9) | collective-permute-done | bytes 393248 | tf_op jit(solution)/shard_map/ppermute | solution.py:526
  36.9 2.3 %shard_map.113 = (f32[256,128]{1,0:T(8,128)S(1)}, f32[64,128]{1,0:T(8,128)S(1)}, f32[64,128]{1,0:T(8,128)S(1)}, f32[64,768]{1,0:T(8,128)S(1)}) custom-call(s32[2,12]{1,0:T(2,128)S(1)} %copy-done.9, s32[1]{0:T(128)S(6)} %copy.15.pad_ref, bf16[64,3072]{1,0:T(8,128)(2,1)S(1)} %copy-done.1, bf16[128,3072]{1,0:T(8,128)(2,1)S(1)} %pad_maximum_fusion.mid_0, ...), custom_call_target="tpu_custom_call" | custom-call | flops 301989888 | bytes 3276900 | tf_op jit(solution)/shard_map/pallas_call | solution.py:510
  39.2 1.7 %collective-permute-start.12 = (f32[8,128]{1,0:T(8,128)S(1)}, f32[8,128]{1,0:T(8,128)S(1)}, u32[]{:S(2)}, u32[]{:S(2)}) collective-permute-start(f32[8,128]{1,0:T(8,128)S(1)} %slice.103), channel_id=1, source_target_pairs={{0,8},{1,9},{2,10},{3,11},{4,12},{5,13},{6,14},{7,15},{8,0},{9,1},... | collective-permute-start | bytes 12296 | tf_op jit(solution)/shard_map/ppermute | solution.py:526
  40.9 2.5 %shard_map.114 = (bf16[256,768]{1,0:T(8,128)(2,1)}, bf16[384,256]{1,0:T(8,128)(2,1)S(1)}, bf16[384,256]{1,0:T(8,128)(2,1)S(1)}) custom-call(s32[2,12]{1,0:T(2,128)S(1)} %copy-done.9, f32[256,128]{1,0:T(8,128)S(1)} %get-tuple-element.47.near_stats, f32[256,128]{1,0:T(8,128)S(1)} %get-tuple-element.53.stats, f32[64,128]{1,0:T(8,128)S(1)} %get-tuple-element.54.picked, ...), custom_call_target="tpu_custom_call" | custom-call | flops 905969664 | bytes 3673184 | tf_op jit(solution)/shard_map/pallas_call | solution.py:510
  43.4 3.4 %collective-permute-start.13 = (f32[16,128]{1,0:T(8,128)S(1)}, f32[16,128]{1,0:T(8,128)S(1)}, u32[]{:S(2)}, u32[]{:S(2)}) collective-permute-start(f32[16,128]{1,0:T(8,128)S(1)} %pad_maximum_fusion.8), channel_id=1, source_target_pairs={{0,16},{1,17},{2,18},{3,19},{4,20},{5,21},{6,22},{7,23},{8,24},{9,... | collective-permute-start | bytes 24584 | tf_op jit(solution)/shard_map/ppermute | solution.py:526
  46.8 1.6 %collective-permute-done.13 = f32[16,128]{1,0:T(8,128)S(1)} collective-permute-done((f32[16,128]{1,0:T(8,128)S(1)}, f32[16,128]{1,0:T(8,128)S(1)}, u32[]{:S(2)}, u32[]{:S(2)}) %collective-permute-start.13) | collective-permute-done | bytes 8224 | tf_op jit(solution)/shard_map/ppermute | solution.py:526
  49.7 2.7 %collective-permute-done.14 = f32[32,256]{1,0:T(8,128)S(1)} collective-permute-done((f32[32,256]{1,0:T(8,128)S(1)}, f32[32,256]{1,0:T(8,128)S(1)}, u32[]{:S(2)}, u32[]{:S(2)}) %collective-permute-start.14) | collective-permute-done | bytes 32800 | tf_op jit(solution)/shard_map/ppermute | solution.py:526
  53.0 5.3 %shard_map.115 = (bf16[256,768]{1,0:T(8,128)(2,1)S(1)}, f32[256,768]{1,0:T(8,128)S(1)}, f32[256,768]{1,0:T(8,128)S(1)}) custom-call(s32[2,12]{1,0:T(2,128)S(1)} %copy-done.9, s32[1]{0:T(128)S(6)} %copy.15.pad_ref, bf16[256,768]{1,0:T(8,128)(2,1)S(1)} %copy-done.5, bf16[256,768]{1,0:T(8,128)(2,1)S(1)} %copy-done.6, bf16[256,768]{1,0:T(8,128)(2,1)S(1)} %copy-done.7, ...), custom_call_target="tpu_custom_call" | custom-call | flops 805306368 | bytes 6455396 | tf_op jit(solution)/shard_map/pallas_call | solution.py:510
  59.0 1.0 collective-permute-done.18.dq_other
  60.6 0.8 shard_map.116
  61.4 2.3 %shard_map.117 = (bf16[256,768]{1,0:T(8,128)(2,1)S(1)}, bf16[256,768]{1,0:T(8,128)(2,1)S(1)}) custom-call(s32[2,12]{1,0:T(2,128)S(1)} %copy-done.9, s32[1]{0:T(128)S(6)} %copy.15.pad_ref, bf16[64,3072]{1,0:T(8,128)(2,1)S(1)} %copy-done.1, bf16[128,3072]{1,0:T(8,128)(2,1)S(1)} %pad_maximum_fusion.mid_0, bf16[128,3072]{1,0:T(8,128)(2,1)S(1)} %collective-permute-done.5.mid_1, ...), custom_call_target="tpu_custom_call" | custom-call | flops 301989888 | bytes 5374052 | tf_op jit(solution)/shard_map/pallas_call | solution.py:510
  64.4 0.6 collective-permute-start.22
  65.0 1.5 %collective-permute-start.23 = (bf16[96,1536]{1,0:T(8,128)(2,1)S(1)}, bf16[96,1536]{1,0:T(8,128)(2,1)S(1)}, u32[]{:S(2)}, u32[]{:S(2)}) collective-permute-start(bf16[96,1536]{1,0:T(8,128)(2,1)S(1)} %get-tuple-element.79), channel_id=1, source_target_pairs={{0,4},{1,5},{2,6},{3,7},{4,0},{5,1},{6,2},{7,3},{8,12},{9,13},{10,... | collective-permute-start | bytes 884744 | tf_op jit(solution)/shard_map/ppermute | solution.py:526
  66.5 1.4 %collective-permute-start.24 = (bf16[96,1536]{1,0:T(8,128)(2,1)S(1)}, bf16[96,1536]{1,0:T(8,128)(2,1)S(1)}, u32[]{:S(2)}, u32[]{:S(2)}) collective-permute-start(bf16[96,1536]{1,0:T(8,128)(2,1)S(1)} %get-tuple-element.78), channel_id=1, source_target_pairs={{0,6},{1,7},{2,4},{3,5},{4,2},{5,3},{6,0},{7,1},{8,14},{9,15},{10,... | collective-permute-start | bytes 884744 | tf_op jit(solution)/shard_map/ppermute | solution.py:526
  67.9 0.8 shard_map.118
  68.7 5.6 %collective-permute-done.22 = bf16[96,1536]{1,0:T(8,128)(2,1)S(1)} collective-permute-done((bf16[96,1536]{1,0:T(8,128)(2,1)S(1)}, bf16[96,1536]{1,0:T(8,128)(2,1)S(1)}, u32[]{:S(2)}, u32[]{:S(2)}) %collective-permute-start.22) | collective-permute-done | bytes 294944 | tf_op jit(solution)/shard_map/ppermute | solution.py:526
  74.3 4.8 %collective-permute-done.23 = bf16[96,1536]{1,0:T(8,128)(2,1)S(1)} collective-permute-done((bf16[96,1536]{1,0:T(8,128)(2,1)S(1)}, bf16[96,1536]{1,0:T(8,128)(2,1)S(1)}, u32[]{:S(2)}, u32[]{:S(2)}) %collective-permute-start.23) | collective-permute-done | bytes 294944 | tf_op jit(solution)/shard_map/ppermute | solution.py:526
  79.1 1.6 %collective-permute-done.24 = bf16[96,1536]{1,0:T(8,128)(2,1)S(1)} collective-permute-done((bf16[96,1536]{1,0:T(8,128)(2,1)S(1)}, bf16[96,1536]{1,0:T(8,128)(2,1)S(1)}, u32[]{:S(2)}, u32[]{:S(2)}) %collective-permute-start.24) | collective-permute-done | bytes 294944 | tf_op jit(solution)/shard_map/ppermute | solution.py:526
  80.9 3.0 %collective-permute-start.25 = (bf16[48,1536]{1,0:T(8,128)(2,1)S(1)}, bf16[48,1536]{1,0:T(8,128)(2,1)S(1)}, u32[]{:S(2)}, u32[]{:S(2)}) collective-permute-start(bf16[48,1536]{1,0:T(8,128)(2,1)S(1)} %slice.131), channel_id=1, source_target_pairs={{0,16},{1,17},{2,18},{3,19},{4,20},{5,21},{6,22},{7,23},{8,24},{9,... | collective-permute-start | bytes 442376 | tf_op jit(solution)/shard_map/ppermute | solution.py:526
  84.0 1.8 %collective-permute-start.29 = (bf16[96,1536]{1,0:T(8,128)(2,1)S(1)}, bf16[96,1536]{1,0:T(8,128)(2,1)S(1)}, u32[]{:S(2)}, u32[]{:S(2)}) collective-permute-start(bf16[96,1536]{1,0:T(8,128)(2,1)S(1)} %get-tuple-element.83), channel_id=1, source_target_pairs={{0,6},{1,7},{2,4},{3,5},{4,2},{5,3},{6,0},{7,1},{8,14},{9,15},{10,... | collective-permute-start | bytes 884744 | tf_op jit(solution)/shard_map/ppermute | solution.py:526
  86.3 1.2 %collective-permute-start.27 = (bf16[96,1536]{1,0:T(8,128)(2,1)S(1)}, bf16[96,1536]{1,0:T(8,128)(2,1)S(1)}, u32[]{:S(2)}, u32[]{:S(2)}) collective-permute-start(bf16[96,1536]{1,0:T(8,128)(2,1)S(1)} %get-tuple-element.82), channel_id=1, source_target_pairs={{0,2},{1,3},{2,0},{3,1},{4,6},{5,7},{6,4},{7,5},{8,10},{9,11},{10,... | collective-permute-start | bytes 884744 | tf_op jit(solution)/shard_map/ppermute | solution.py:526
  87.5 2.9 %collective-permute-done.25 = bf16[48,1536]{1,0:T(8,128)(2,1)S(1)} collective-permute-done((bf16[48,1536]{1,0:T(8,128)(2,1)S(1)}, bf16[48,1536]{1,0:T(8,128)(2,1)S(1)}, u32[]{:S(2)}, u32[]{:S(2)}) %collective-permute-start.25) | collective-permute-done | bytes 147488 | tf_op jit(solution)/shard_map/ppermute | solution.py:526
  90.9 1.9 %shard_map.119 = bf16[256,768]{1,0:T(8,128)(2,1)} custom-call(bf16[256,768]{1,0:T(8,128)(2,1)S(1)} %get-tuple-element.73.dq, bf16[256,768]{1,0:T(8,128)(2,1)S(1)} %get-tuple-element.71.dk, bf16[256,768]{1,0:T(8,128)(2,1)S(1)} %get-tuple-element.72.dv, bf16[768,2304]{1,0:T(8,128)(2,1)S(1)} %copy-done), custom_call_target="tpu_custom_call" | custom-call | flops 905969664 | bytes 5111808 | tf_op jit(solution)/shard_map/pallas_call | solution.py:510
  92.7 2.1 %collective-permute-done.26 = bf16[24,1536]{1,0:T(8,128)(2,1)S(1)} collective-permute-done((bf16[24,1536]{1,0:T(8,128)(2,1)S(1)}, bf16[24,1536]{1,0:T(8,128)(2,1)S(1)}, u32[]{:S(2)}, u32[]{:S(2)}) %collective-permute-start.26) | collective-permute-done | bytes 73760 | tf_op jit(solution)/shard_map/ppermute | solution.py:526
  94.9 4.3 %collective-permute-done.28 = bf16[96,1536]{1,0:T(8,128)(2,1)S(1)} collective-permute-done((bf16[96,1536]{1,0:T(8,128)(2,1)S(1)}, bf16[96,1536]{1,0:T(8,128)(2,1)S(1)}, u32[]{:S(2)}, u32[]{:S(2)}) %collective-permute-start.28) | collective-permute-done | bytes 294944 | tf_op jit(solution)/shard_map/ppermute | solution.py:526
  99.4 0.9 collective-permute-start.32
  100.3 1.7 %collective-permute-start.31 = (bf16[24,1536]{1,0:T(8,128)(2,1)S(1)}, bf16[24,1536]{1,0:T(8,128)(2,1)S(1)}, u32[]{:S(2)}, u32[]{:S(2)}) collective-permute-start(bf16[24,1536]{1,0:T(8,128)(2,1)S(1)} %get-tuple-element.87), channel_id=1, source_target_pairs={{0,16},{1,17},{2,18},{3,19},{4,20},{5,21},{6,22},{7,23},{8,24},{9,... | collective-permute-start | bytes 221192 | tf_op jit(solution)/shard_map/ppermute | solution.py:526
  102.0 1.8 %collective-permute-start.30 = (bf16[24,1536]{1,0:T(8,128)(2,1)S(1)}, bf16[24,1536]{1,0:T(8,128)(2,1)S(1)}, u32[]{:S(2)}, u32[]{:S(2)}) collective-permute-start(bf16[24,1536]{1,0:T(8,128)(2,1)S(1)} %get-tuple-element.85), channel_id=1, source_target_pairs={{0,8},{1,9},{2,10},{3,11},{4,12},{5,13},{6,14},{7,15},{8,0},{9,1},... | collective-permute-start | bytes 221192 | tf_op jit(solution)/shard_map/ppermute | solution.py:526
  103.9 0.6 fusion.7
  104.5 1.9 %collective-permute-done.32 = bf16[24,1536]{1,0:T(8,128)(2,1)S(1)} collective-permute-done((bf16[24,1536]{1,0:T(8,128)(2,1)S(1)}, bf16[24,1536]{1,0:T(8,128)(2,1)S(1)}, u32[]{:S(2)}, u32[]{:S(2)}) %collective-permute-start.32) | collective-permute-done | bytes 73760 | tf_op jit(solution)/shard_map/ppermute | solution.py:526
  106.4 2.6 %collective-permute-done.31 = bf16[24,1536]{1,0:T(8,128)(2,1)S(1)} collective-permute-done((bf16[24,1536]{1,0:T(8,128)(2,1)S(1)}, bf16[24,1536]{1,0:T(8,128)(2,1)S(1)}, u32[]{:S(2)}, u32[]{:S(2)}) %collective-permute-start.31) | collective-permute-done | bytes 73760 | tf_op jit(solution)/shard_map/ppermute | solution.py:526
  109.1 0.7 pad_maximum_fusion.3
  (82 shorter events, 6.4 us)
Async XLA Ops:
  0.6 13.9 %copy-start.10 = (s32[768,1]{1,0:T(8,128)S(1)}, s32[768,1]{1,0:T(8,128)}, u32[]{:S(2)}) copy-start(s32[768,1]{1,0:T(8,128)} %constant.11.clone) | copy-start | bytes 9220
  0.6 13.9 %copy-start.11 = (s32[768,1]{1,0:T(8,128)S(1)}, s32[768,1]{1,0:T(8,128)}, u32[]{:S(2)}) copy-start(s32[768,1]{1,0:T(8,128)} %constant.10.clone) | copy-start | bytes 9220
  6.0 20.0 %copy-start.4 = (bf16[256,768]{1,0:T(8,128)(2,1)S(1)}, bf16[256,768]{1,0:T(8,128)(2,1)}, u32[]{:S(2)}) copy-start(bf16[256,768]{1,0:T(8,128)(2,1)} %tiles.3) | copy-start | bytes 1179652
  6.0 20.0 %copy-start.5 = (bf16[256,768]{1,0:T(8,128)(2,1)S(1)}, bf16[256,768]{1,0:T(8,128)(2,1)}, u32[]{:S(2)}) copy-start(bf16[256,768]{1,0:T(8,128)(2,1)} %get-tuple-element.43.q) | copy-start | bytes 1179652
  6.0 20.0 %copy-start.6 = (bf16[256,768]{1,0:T(8,128)(2,1)S(1)}, bf16[256,768]{1,0:T(8,128)(2,1)}, u32[]{:S(2)}) copy-start(bf16[256,768]{1,0:T(8,128)(2,1)} %get-tuple-element.44.k) | copy-start | bytes 1179652
  6.0 20.0 %copy-start.7 = (bf16[256,768]{1,0:T(8,128)(2,1)S(1)}, bf16[256,768]{1,0:T(8,128)(2,1)}, u32[]{:S(2)}) copy-start(bf16[256,768]{1,0:T(8,128)(2,1)} %get-tuple-element.45.v) | copy-start | bytes 1179652
  6.0 20.0 %copy-start.8 = (bf16[256,768]{1,0:T(8,128)(2,1)S(1)}, bf16[256,768]{1,0:T(8,128)(2,1)}, u32[]{:S(2)}) copy-start(bf16[256,768]{1,0:T(8,128)(2,1)} %get-tuple-element.46.g) | copy-start | bytes 1179652
  7.1 21.2 %collective-permute-start.4 = (bf16[32,3072]{1,0:T(8,128)(2,1)S(1)}, bf16[32,3072]{1,0:T(8,128)(2,1)S(1)}, u32[]{:S(2)}, u32[]{:S(2)}) collective-permute-start(bf16[32,3072]{1,0:T(8,128)(2,1)S(1)} %slice.93), channel_id=1, source_target_pairs={{0,6},{1,7},{2,4},{3,5},{4,2},{5,3},{6,0},{7,1},{8,14},{9,15},{10,... | collective-permute-start | bytes 589832 | tf_op jit(solution)/shard_map/ppermute | solution.py:526
  11.1 17.5 %collective-permute-start.3 = (bf16[32,3072]{1,0:T(8,128)(2,1)S(1)}, bf16[32,3072]{1,0:T(8,128)(2,1)S(1)}, u32[]{:S(2)}, u32[]{:S(2)}) collective-permute-start(bf16[32,3072]{1,0:T(8,128)(2,1)S(1)} %slice.93), channel_id=1, source_target_pairs={{0,4},{1,5},{2,6},{3,7},{4,0},{5,1},{6,2},{7,3},{8,12},{9,13},{10,... | collective-permute-start | bytes 589832 | tf_op jit(solution)/shard_map/ppermute | solution.py:526
  11.6 17.0 %collective-permute-start.2 = (bf16[32,3072]{1,0:T(8,128)(2,1)S(1)}, bf16[32,3072]{1,0:T(8,128)(2,1)}, u32[]{:S(2)}, u32[]{:S(2)}) collective-permute-start(bf16[32,3072]{1,0:T(8,128)(2,1)S(1)} %slice.93), channel_id=1, source_target_pairs={{0,2},{1,3},{2,0},{3,1},{4,6},{5,7},{6,4},{7,5},{8,10},{9,11},{10,... | collective-permute-start | bytes 589832 | tf_op jit(solution)/shard_map/ppermute | solution.py:526
  11.7 4.4 %collective-permute-start = (bf16[8,3072]{1,0:T(8,128)(2,1)}, bf16[8,3072]{1,0:T(8,128)(2,1)}, u32[]{:S(2)}, u32[]{:S(2)}) collective-permute-start(bf16[8,3072]{1,0:T(8,128)(2,1)} %get-tuple-element.42), channel_id=1, source_target_pairs={{0,8},{1,9},{2,10},{3,11},{4,12},{5,13},{6,14},{7,15},{8,0},{9,1},... | collective-permute-start | bytes 147464 | tf_op jit(solution)/shard_map/ppermute | solution.py:526
  16.9 5.6 %collective-permute-start.1 = (bf16[16,3072]{1,0:T(8,128)(2,1)S(1)}, bf16[16,3072]{1,0:T(8,128)(2,1)S(1)}, u32[]{:S(2)}, u32[]{:S(2)}) collective-permute-start(bf16[16,3072]{1,0:T(8,128)(2,1)S(1)} %pad_maximum_fusion.6), channel_id=1, source_target_pairs={{0,16},{1,17},{2,18},{3,19},{4,20},{5,21},{6,22},{7,23},{8,24},{9,... | collective-permute-start | bytes 294920 | tf_op jit(solution)/shard_map/ppermute | solution.py:526
  22.6 7.0 %collective-permute-start.6 = (bf16[32,3072]{1,0:T(8,128)(2,1)S(1)}, bf16[32,3072]{1,0:T(8,128)(2,1)S(1)}, u32[]{:S(2)}, u32[]{:S(2)}) collective-permute-start(bf16[32,3072]{1,0:T(8,128)(2,1)S(1)} %constant_dynamic-update-slice_fusion), channel_id=1, source_target_pairs={{0,2},{1,3},{2,0},{3,1},{4,6},{5,7},{6,4},{7,5},{8,10},{9,11},{10,... | collective-permute-start | bytes 589832 | tf_op jit(solution)/shard_map/ppermute | solution.py:526
  24.5 7.8 %collective-permute-start.7 = (bf16[32,3072]{1,0:T(8,128)(2,1)S(1)}, bf16[32,3072]{1,0:T(8,128)(2,1)S(1)}, u32[]{:S(2)}, u32[]{:S(2)}) collective-permute-start(bf16[32,3072]{1,0:T(8,128)(2,1)S(1)} %constant_dynamic-update-slice_fusion), channel_id=1, source_target_pairs={{0,4},{1,5},{2,6},{3,7},{4,0},{5,1},{6,2},{7,3},{8,12},{9,13},{10,... | collective-permute-start | bytes 589832 | tf_op jit(solution)/shard_map/ppermute | solution.py:526
  28.3 6.6 %collective-permute-start.8 = (bf16[32,3072]{1,0:T(8,128)(2,1)S(1)}, bf16[32,3072]{1,0:T(8,128)(2,1)S(1)}, u32[]{:S(2)}, u32[]{:S(2)}) collective-permute-start(bf16[32,3072]{1,0:T(8,128)(2,1)S(1)} %constant_dynamic-update-slice_fusion), channel_id=1, source_target_pairs={{0,6},{1,7},{2,4},{3,5},{4,2},{5,3},{6,0},{7,1},{8,14},{9,15},{10,... | collective-permute-start | bytes 589832 | tf_op jit(solution)/shard_map/ppermute | solution.py:526
  29.5 7.3 %copy-start.1 = (bf16[64,3072]{1,0:T(8,128)(2,1)S(1)}, bf16[64,3072]{1,0:T(8,128)(2,1)}, u32[]{:S(2)}) copy-start(bf16[64,3072]{1,0:T(8,128)(2,1)} %get-tuple-element.48.sel) | copy-start | bytes 1179652
  29.5 7.3 %copy-start.9 = (s32[2,12]{1,0:T(2,128)S(1)}, s32[2,12]{1,0:T(2,128)}, u32[]{:S(2)}) copy-start(s32[2,12]{1,0:T(2,128)} %offs_ref.7) | copy-start | bytes 292
  29.5 7.3 %collective-permute-start.5 = (bf16[128,3072]{1,0:T(8,128)(2,1)S(1)}, bf16[128,3072]{1,0:T(8,128)(2,1)S(1)}, u32[]{:S(2)}, u32[]{:S(2)}) collective-permute-start(bf16[128,3072]{1,0:T(8,128)(2,1)S(1)} %pad_maximum_fusion.mid_0), channel_id=1, source_target_pairs={{0,1},{1,0},{2,3},{3,2},{4,5},{5,4},{6,7},{7,6},{8,9},{9,8},{10,11... | collective-permute-start | bytes 2359304 | tf_op jit(solution)/shard_map/ppermute | solution.py:526
  35.0 5.9 %copy-start.3 = (bf16[768,768]{1,0:T(8,128)(2,1)S(1)}, bf16[768,768]{1,0:T(8,128)(2,1)}, u32[]{:S(2)}) copy-start(bf16[768,768]{1,0:T(8,128)(2,1)} %w_out.1) | copy-start | bytes 3538948
  35.1 1.8 %collective-permute-start.9 = (bf16[128,1536]{1,0:T(8,128)(2,1)S(1)}, bf16[128,1536]{1,0:T(8,128)(2,1)S(1)}, u32[]{:S(2)}, u32[]{:S(2)}) collective-permute-start(bf16[128,1536]{1,0:T(8,128)(2,1)S(1)} %pad_maximum_fusion.1.far_0), channel_id=1, source_target_pairs={{0,1},{1,0},{2,3},{3,2},{4,5},{5,4},{6,7},{7,6},{8,9},{9,8},{10,11... | collective-permute-start | bytes 1179656 | tf_op jit(solution)/shard_map/ppermute | solution.py:526
  39.2 4.3 %collective-permute-start.12 = (f32[8,128]{1,0:T(8,128)S(1)}, f32[8,128]{1,0:T(8,128)S(1)}, u32[]{:S(2)}, u32[]{:S(2)}) collective-permute-start(f32[8,128]{1,0:T(8,128)S(1)} %slice.103), channel_id=1, source_target_pairs={{0,8},{1,9},{2,10},{3,11},{4,12},{5,13},{6,14},{7,15},{8,0},{9,1},... | collective-permute-start | bytes 12296 | tf_op jit(solution)/shard_map/ppermute | solution.py:526
  43.4 5.0 %collective-permute-start.13 = (f32[16,128]{1,0:T(8,128)S(1)}, f32[16,128]{1,0:T(8,128)S(1)}, u32[]{:S(2)}, u32[]{:S(2)}) collective-permute-start(f32[16,128]{1,0:T(8,128)S(1)} %pad_maximum_fusion.8), channel_id=1, source_target_pairs={{0,16},{1,17},{2,18},{3,19},{4,20},{5,21},{6,22},{7,23},{8,24},{9,... | collective-permute-start | bytes 24584 | tf_op jit(solution)/shard_map/ppermute | solution.py:526
  48.5 3.9 %collective-permute-start.14 = (f32[32,256]{1,0:T(8,128)S(1)}, f32[32,256]{1,0:T(8,128)S(1)}, u32[]{:S(2)}, u32[]{:S(2)}) collective-permute-start(f32[32,256]{1,0:T(8,128)S(1)} %maximum_maximum_fusion), channel_id=1, source_target_pairs={{0,2},{1,3},{2,0},{3,1},{4,6},{5,7},{6,4},{7,5},{8,10},{9,11},{10,... | collective-permute-start | bytes 98312 | tf_op jit(solution)/shard_map/ppermute | solution.py:526
  49.0 12.3 %collective-permute-start.11 = (bf16[128,1536]{1,0:T(8,128)(2,1)S(1)}, bf16[128,1536]{1,0:T(8,128)(2,1)S(1)}, u32[]{:S(2)}, u32[]{:S(2)}) collective-permute-start(bf16[128,1536]{1,0:T(8,128)(2,1)S(1)} %pad_maximum_fusion.2.far_0), channel_id=1, source_target_pairs={{0,1},{1,0},{2,3},{3,2},{4,5},{5,4},{6,7},{7,6},{8,9},{9,8},{10,11... | collective-permute-start | bytes 1179656 | tf_op jit(solution)/shard_map/ppermute | solution.py:526
  49.1 9.7 %collective-permute-start.10 = (bf16[384,256]{1,0:T(8,128)(2,1)S(1)}, bf16[384,256]{1,0:T(8,128)(2,1)S(1)}, u32[]{:S(2)}, u32[]{:S(2)}) collective-permute-start(bf16[384,256]{1,0:T(8,128)(2,1)S(1)} %get-tuple-element.62), channel_id=1, source_target_pairs={{0,1},{1,0},{2,3},{3,2},{4,5},{5,4},{6,7},{7,6},{8,9},{9,8},{10,11... | collective-permute-start | bytes 589832 | tf_op jit(solution)/shard_map/ppermute | solution.py:526
  49.6 9.4 %collective-permute-start.17 = (bf16[384,256]{1,0:T(8,128)(2,1)S(1)}, bf16[384,256]{1,0:T(8,128)(2,1)S(1)}, u32[]{:S(2)}, u32[]{:S(2)}) collective-permute-start(bf16[384,256]{1,0:T(8,128)(2,1)S(1)} %get-tuple-element.67), channel_id=1, source_target_pairs={{0,1},{1,0},{2,3},{3,2},{4,5},{5,4},{6,7},{7,6},{8,9},{9,8},{10,11... | collective-permute-start | bytes 589832 | tf_op jit(solution)/shard_map/ppermute | solution.py:526
  52.4 5.9 %copy-start.2 = (bf16[256,768]{1,0:T(8,128)(2,1)S(1)}, bf16[256,768]{1,0:T(8,128)(2,1)}, u32[]{:S(2)}) copy-start(bf16[256,768]{1,0:T(8,128)(2,1)} %cot.1) | copy-start | bytes 1179652
  52.4 5.9 %collective-permute-start.15 = (f32[64,256]{1,0:T(8,128)S(1)}, f32[64,256]{1,0:T(8,128)S(1)}, u32[]{:S(2)}, u32[]{:S(2)}) collective-permute-start(f32[64,256]{1,0:T(8,128)S(1)} %pad_maximum_fusion.7), channel_id=1, source_target_pairs={{0,4},{1,5},{2,6},{3,7},{4,0},{5,1},{6,2},{7,3},{8,12},{9,13},{10,... | collective-permute-start | bytes 196616 | tf_op jit(solution)/shard_map/ppermute | solution.py:526
  58.2 1.8 %collective-permute-start.18 = (bf16[256,768]{1,0:T(8,128)(2,1)S(1)}, bf16[256,768]{1,0:T(8,128)(2,1)S(1)}, u32[]{:S(2)}, u32[]{:S(2)}) collective-permute-start(bf16[256,768]{1,0:T(8,128)(2,1)S(1)} %get-tuple-element.73.dq), channel_id=1, source_target_pairs={{0,1},{1,0},{2,3},{3,2},{4,5},{5,4},{6,7},{7,6},{8,9},{9,8},{10,11... | collective-permute-start | bytes 1179656 | tf_op jit(solution)/shard_map/ppermute | solution.py:526
  58.3 2.3 %collective-permute-start.19 = (bf16[256,768]{1,0:T(8,128)(2,1)S(1)}, bf16[256,768]{1,0:T(8,128)(2,1)S(1)}, u32[]{:S(2)}, u32[]{:S(2)}) collective-permute-start(bf16[256,768]{1,0:T(8,128)(2,1)S(1)} %copy-done.2), channel_id=1, source_target_pairs={{0,1},{1,0},{2,3},{3,2},{4,5},{5,4},{6,7},{7,6},{8,9},{9,8},{10,11... | collective-permute-start | bytes 1179656 | tf_op jit(solution)/shard_map/ppermute | solution.py:526
  58.9 2.5 %collective-permute-start.16 = (f32[256,128]{1,0:T(8,128)S(1)}, f32[256,128]{1,0:T(8,128)S(1)}, u32[]{:S(2)}, u32[]{:S(2)}) collective-permute-start(f32[256,128]{1,0:T(8,128)S(1)} %pad_maximum_fusion.5.stats_0), channel_id=1, source_target_pairs={{0,1},{1,0},{2,3},{3,2},{4,5},{5,4},{6,7},{7,6},{8,9},{9,8},{10,11... | collective-permute-start | bytes 393224 | tf_op jit(solution)/shard_map/ppermute | solution.py:526
  63.7 4.2 %collective-permute-start.20 = (bf16[256,768]{1,0:T(8,128)(2,1)S(1)}, bf16[256,768]{1,0:T(8,128)(2,1)S(1)}, u32[]{:S(2)}, u32[]{:S(2)}) collective-permute-start(bf16[256,768]{1,0:T(8,128)(2,1)S(1)} %get-tuple-element.71.dk), channel_id=1, source_target_pairs={{0,1},{1,0},{2,3},{3,2},{4,5},{5,4},{6,7},{7,6},{8,9},{9,8},{10,11... | collective-permute-start | bytes 1179656 | tf_op jit(solution)/shard_map/ppermute | solution.py:526
  63.9 4.0 %collective-permute-start.21 = (bf16[256,768]{1,0:T(8,128)(2,1)S(1)}, bf16[256,768]{1,0:T(8,128)(2,1)S(1)}, u32[]{:S(2)}, u32[]{:S(2)}) collective-permute-start(bf16[256,768]{1,0:T(8,128)(2,1)S(1)} %get-tuple-element.72.dv), channel_id=1, source_target_pairs={{0,1},{1,0},{2,3},{3,2},{4,5},{5,4},{6,7},{7,6},{8,9},{9,8},{10,11... | collective-permute-start | bytes 1179656 | tf_op jit(solution)/shard_map/ppermute | solution.py:526
  64.4 9.9 %collective-permute-start.22 = (bf16[96,1536]{1,0:T(8,128)(2,1)S(1)}, bf16[96,1536]{1,0:T(8,128)(2,1)S(1)}, u32[]{:S(2)}, u32[]{:S(2)}) collective-permute-start(bf16[96,1536]{1,0:T(8,128)(2,1)S(1)} %get-tuple-element.80), channel_id=1, source_target_pairs={{0,2},{1,3},{2,0},{3,1},{4,6},{5,7},{6,4},{7,5},{8,10},{9,11},{10,... | collective-permute-start | bytes 884744 | tf_op jit(solution)/shard_map/ppermute | solution.py:526
  65.0 14.2 %collective-permute-start.23 = (bf16[96,1536]{1,0:T(8,128)(2,1)S(1)}, bf16[96,1536]{1,0:T(8,128)(2,1)S(1)}, u32[]{:S(2)}, u32[]{:S(2)}) collective-permute-start(bf16[96,1536]{1,0:T(8,128)(2,1)S(1)} %get-tuple-element.79), channel_id=1, source_target_pairs={{0,4},{1,5},{2,6},{3,7},{4,0},{5,1},{6,2},{7,3},{8,12},{9,13},{10,... | collective-permute-start | bytes 884744 | tf_op jit(solution)/shard_map/ppermute | solution.py:526
  66.5 14.3 %collective-permute-start.24 = (bf16[96,1536]{1,0:T(8,128)(2,1)S(1)}, bf16[96,1536]{1,0:T(8,128)(2,1)S(1)}, u32[]{:S(2)}, u32[]{:S(2)}) collective-permute-start(bf16[96,1536]{1,0:T(8,128)(2,1)S(1)} %get-tuple-element.78), channel_id=1, source_target_pairs={{0,6},{1,7},{2,4},{3,5},{4,2},{5,3},{6,0},{7,1},{8,14},{9,15},{10,... | collective-permute-start | bytes 884744 | tf_op jit(solution)/shard_map/ppermute | solution.py:526
  80.7 10.1 %copy-start = (bf16[768,2304]{1,0:T(8,128)(2,1)S(1)}, bf16[768,2304]{1,0:T(8,128)(2,1)}, u32[]{:S(2)}) copy-start(bf16[768,2304]{1,0:T(8,128)(2,1)} %w_qkv.1) | copy-start | bytes 10616836
  80.9 9.5 %collective-permute-start.25 = (bf16[48,1536]{1,0:T(8,128)(2,1)S(1)}, bf16[48,1536]{1,0:T(8,128)(2,1)S(1)}, u32[]{:S(2)}, u32[]{:S(2)}) collective-permute-start(bf16[48,1536]{1,0:T(8,128)(2,1)S(1)} %slice.131), channel_id=1, source_target_pairs={{0,16},{1,17},{2,18},{3,19},{4,20},{5,21},{6,22},{7,23},{8,24},{9,... | collective-permute-start | bytes 442376 | tf_op jit(solution)/shard_map/ppermute | solution.py:526
  84.0 10.9 %collective-permute-start.29 = (bf16[96,1536]{1,0:T(8,128)(2,1)S(1)}, bf16[96,1536]{1,0:T(8,128)(2,1)S(1)}, u32[]{:S(2)}, u32[]{:S(2)}) collective-permute-start(bf16[96,1536]{1,0:T(8,128)(2,1)S(1)} %get-tuple-element.83), channel_id=1, source_target_pairs={{0,6},{1,7},{2,4},{3,5},{4,2},{5,3},{6,0},{7,1},{8,14},{9,15},{10,... | collective-permute-start | bytes 884744 | tf_op jit(solution)/shard_map/ppermute | solution.py:526
  85.8 13.4 %collective-permute-start.28 = (bf16[96,1536]{1,0:T(8,128)(2,1)S(1)}, bf16[96,1536]{1,0:T(8,128)(2,1)S(1)}, u32[]{:S(2)}, u32[]{:S(2)}) collective-permute-start(bf16[96,1536]{1,0:T(8,128)(2,1)S(1)} %get-tuple-element.84), channel_id=1, source_target_pairs={{0,4},{1,5},{2,6},{3,7},{4,0},{5,1},{6,2},{7,3},{8,12},{9,13},{10,... | collective-permute-start | bytes 884744 | tf_op jit(solution)/shard_map/ppermute | solution.py:526
  86.3 12.9 %collective-permute-start.27 = (bf16[96,1536]{1,0:T(8,128)(2,1)S(1)}, bf16[96,1536]{1,0:T(8,128)(2,1)S(1)}, u32[]{:S(2)}, u32[]{:S(2)}) collective-permute-start(bf16[96,1536]{1,0:T(8,128)(2,1)S(1)} %get-tuple-element.82), channel_id=1, source_target_pairs={{0,2},{1,3},{2,0},{3,1},{4,6},{5,7},{6,4},{7,5},{8,10},{9,11},{10,... | collective-permute-start | bytes 884744 | tf_op jit(solution)/shard_map/ppermute | solution.py:526
  90.5 4.4 %collective-permute-start.26 = (bf16[24,1536]{1,0:T(8,128)(2,1)S(1)}, bf16[24,1536]{1,0:T(8,128)(2,1)S(1)}, u32[]{:S(2)}, u32[]{:S(2)}) collective-permute-start(bf16[24,1536]{1,0:T(8,128)(2,1)S(1)} %slice.133), channel_id=1, source_target_pairs={{0,8},{1,9},{2,10},{3,11},{4,12},{5,13},{6,14},{7,15},{8,0},{9,1},... | collective-permute-start | bytes 221192 | tf_op jit(solution)/shard_map/ppermute | solution.py:526
  99.4 7.0 %collective-permute-start.32 = (bf16[24,1536]{1,0:T(8,128)(2,1)S(1)}, bf16[24,1536]{1,0:T(8,128)(2,1)S(1)}, u32[]{:S(2)}, u32[]{:S(2)}) collective-permute-start(bf16[24,1536]{1,0:T(8,128)(2,1)S(1)} %get-tuple-element.86), channel_id=1, source_target_pairs={{0,24},{1,25},{2,26},{3,27},{4,28},{5,29},{6,30},{7,31},{8,16},{9,... | collective-permute-start | bytes 221192 | tf_op jit(solution)/shard_map/ppermute | solution.py:526
  100.3 8.8 %collective-permute-start.31 = (bf16[24,1536]{1,0:T(8,128)(2,1)S(1)}, bf16[24,1536]{1,0:T(8,128)(2,1)S(1)}, u32[]{:S(2)}, u32[]{:S(2)}) collective-permute-start(bf16[24,1536]{1,0:T(8,128)(2,1)S(1)} %get-tuple-element.87), channel_id=1, source_target_pairs={{0,16},{1,17},{2,18},{3,19},{4,20},{5,21},{6,22},{7,23},{8,24},{9,... | collective-permute-start | bytes 221192 | tf_op jit(solution)/shard_map/ppermute | solution.py:526
  102.0 7.0 %collective-permute-start.30 = (bf16[24,1536]{1,0:T(8,128)(2,1)S(1)}, bf16[24,1536]{1,0:T(8,128)(2,1)S(1)}, u32[]{:S(2)}, u32[]{:S(2)}) collective-permute-start(bf16[24,1536]{1,0:T(8,128)(2,1)S(1)} %get-tuple-element.85), channel_id=1, source_target_pairs={{0,8},{1,9},{2,10},{3,11},{4,12},{5,13},{6,14},{7,15},{8,0},{9,1},... | collective-permute-start | bytes 221192 | tf_op jit(solution)/shard_map/ppermute | solution.py:526

commit v4 on v3

--- a/solution.py
+++ b/solution.py
@@ -22,6 +22,7 @@
 LARGE = 1e30
 LOAD_CUTS = 4
 VMEM_BYTES = 40 * 1024 * 1024
+PROJECT_VMEM_BYTES = 57 * 1024 * 1024
 
 
 def dot(a, b, dims=NN):
@@ -141,7 +142,7 @@
 
 
 def project_kernel(
-    z, offs_hbm, tiles_hbm, w_qkv_hbm, cot_hbm, w_out_hbm, q, k, v, g, sel, far,
+    z, offs_hbm, tiles_hbm, w_qkv_hbm, cot_hbm, w_out_hbm, q, k, v, g, sel, mid, far,
     offs_ref, tiles, w_qkv, cot, w_out, sems,
 ):
     width = z.width
@@ -211,10 +212,13 @@
         for part in range(4):
             to = slice(part * width + pair * PAIR, part * width + (pair + 1) * PAIR)
             sel[:, to] = picked[:, part * PAIR : (part + 1) * PAIR]
+            mid[:, to] = picked[: z.mid, part * PAIR : (part + 1) * PAIR]
             far[:, to] = far_part[:, part * PAIR : (part + 1) * PAIR]
 
 
-def near_kernel(z, pad_ref, q, k, v, g, tiles, order, mixed, stats, turned, turned_out):
+def near_kernel(
+    z, pad_ref, q, k, v, g, tiles, order, order_q, mixed, stats, turned, turned_out
+):
     own = lax.axis_index("ctx")
     limit = z.rows * z.devs - pad_ref[0] - own * z.rows
     valid = iota((1, z.rows), 1) < limit
@@ -240,10 +244,12 @@
             both = jnp.where(lane == SECOND + head, meets, both)
         mixed[:, lanes] = total
     stats[...] = both
-    for part, target in enumerate((turned, turned_out)):
-        source = order[part * z.half : (part + 1) * z.half, :]
-        place = (iota((z.half, z.width), 1) == source).astype(F32).astype(BF)
-        target[...] = dot(place, tiles[...], NT).astype(BF)
+    for which, source_rows in enumerate((order, order_q)):
+        for part, target in enumerate((turned, turned_out)):
+            source = source_rows[part * z.half : (part + 1) * z.half, :]
+            place = (iota((z.half, z.width), 1) == source).astype(F32).astype(BF)
+            result = dot(place, tiles[...], NT).astype(BF)
+            target[which * z.half : (which + 1) * z.half, :] = result
 
 
 def of_level(level, refs, lanes):
@@ -476,18 +482,16 @@
         dv[:, lanes] = (dv_near[:, lanes] + moved[:, PAIR:]).astype(BF)
 
 
-def early_weights_kernel(
-    z, turned, turned_other, attn, attn_other, dq, dq_other, cot, cot_other, out
-):
-    width = z.width
-    out[:, :width] = (dot(attn[...], cot[...]) + dot(attn_other[...], cot_other[...])).astype(BF)
-    out[:, width:] = (dot(turned[...], dq[...]) + dot(turned_other[...], dq_other[...])).astype(BF)
+def weights_kernel(start, left, left_other, right, right_other, out):
+    rows = slice(start, start + out.shape[0])
+    out[...] = (dot(left[rows, :], right[...]) + dot(left_other[rows, :], right_other[...])).astype(BF)
 
 
 def late_weights_kernel(z, turned, turned_other, dk, dv, dk_other, dv_other, out):
     width = z.width
-    out[:, :width] = (dot(turned[...], dk[...]) + dot(turned_other[...], dk_other[...])).astype(BF)
-    out[:, width:] = (dot(turned[...], dv[...]) + dot(turned_other[...], dv_other[...])).astype(BF)
+    left, other = turned[: z.half, :], turned_other[: z.half, :]
+    out[:, :width] = (dot(left, dk[...]) + dot(other, dk_other[...])).astype(BF)
+    out[:, width:] = (dot(left, dv[...]) + dot(other, dv_other[...])).astype(BF)
 
 
 def tiles_kernel(z, dq, dk, dv, w_qkv, out):
@@ -542,8 +546,8 @@
     return list(lax.optimization_barrier((*parts, *first))[: len(parts)]) if first else list(parts)
 
 
-def plane_parts(value, dev_count, first=()):
-    base, count = PLANE
+def step_parts(value, step, dev_count, first=()):
+    base, count = step
     return tied(
         [value] + [swap(value, base * i, dev_count) for i in range(1, count)], first
     )
@@ -551,16 +555,18 @@
 
 def doubled(value, masks, dev_count, first=()):
     for i, mask in enumerate(masks):
-        parts = tied([value, swap(value, mask, dev_count)], first if i == 0 else ())
+        parts = tied([value, swap(value, mask, dev_count)], first if i == len(masks) - 1 else ())
         value = jnp.concatenate(parts, axis=0)
     return value
 
 
-def halved(value, masks, dev_count):
+def halved(value, masks, dev_count, firsts=()):
     for i, mask in enumerate(masks):
         size = value.shape[0] // 2
-        total = value[:size].astype(F32) + swap(value[size:], mask, dev_count).astype(F32)
-        value = total if i == len(masks) - 1 else total.astype(BF)
+        first = firsts[i] if i < len(firsts) else ()
+        parts = tied([value[:size], swap(value[size:], mask, dev_count)], first)
+        value = parts[0].astype(F32) + parts[1].astype(F32)
+        value = value if i == len(masks) - 1 else value.astype(BF)
     return value
 
 
@@ -579,12 +585,10 @@
     return value
 
 
-def strip_order(z, own):
-    core, plane, upper, row = np.meshgrid(
-        np.arange(2), np.arange(4), np.arange(z.upper), np.arange(z.strip), indexing="ij"
-    )
-    mask = (core + 2 * plane + GROUP * upper).reshape(-1, 1).astype(np.int32)
-    return (own ^ mask) * z.strip + row.reshape(-1, 1).astype(np.int32)
+def strip_order(z, own, masks):
+    digits = np.meshgrid(*[np.arange(2) for _ in masks], np.arange(z.strip), indexing="ij")
+    moved = sum(digit * mask for digit, mask in zip(digits, masks)).reshape(-1, 1)
+    return (own ^ moved.astype(np.int32)) * z.strip + digits[-1].reshape(-1, 1).astype(np.int32)
 
 
 def after(value, *others):
@@ -596,12 +600,15 @@
     z = Sizes(tiles.shape[0], tiles.shape[1], n)
     own = lax.axis_index("ctx")
     rows, width = z.rows, z.width
-    order = strip_order(z, own)
+    masks = [mask for mask in (2**i for i in range(30)) if GROUP <= mask < n]
+    order = strip_order(z, own, [1, 4, 2] + masks[::-1])
+    order_q = strip_order(z, own, [1] + masks + [2, 4])
+    order_out = strip_order(z, own, [1, 2, 4] + masks)
     base_flops = 2 * rows * rows * width
 
-    q, k, v, g, sel, far = call(
+    q, k, v, g, sel, mid, far = call(
         functools.partial(project_kernel, z),
-        [((rows, width), BF)] * 4 + [((z.sel, 4 * width), BF), ((z.far, 4 * width), BF)],
+        [((rows, width), BF)] * 4 + [((count, 4 * width), BF) for count in (z.sel, z.mid, z.far)],
         2 * rows * width * 4 * width,
         scratch=[
             pltpu.SMEM(offsets.shape, jnp.int32),
@@ -612,26 +619,27 @@
             pltpu.SemaphoreType.DMA((4 * LOAD_CUTS + 3,)),
         ],
         spaces=pltpu.HBM,
-        vmem=61 * 1024 * 1024,
+        vmem=PROJECT_VMEM_BYTES,
     )(offsets, tiles, w_qkv, cotangent, w_out)
 
-    masks = [mask for mask in (2**i for i in range(30)) if GROUP <= mask < n]
-    far_up = doubled(far, masks, n)
-    mid_parts = plane_parts(sel[: z.mid], n)
+    far_up = far
+    for step in upper_steps(n):
+        far_up = jnp.concatenate(step_parts(far_up, step, n), axis=0)
+    mid_parts = step_parts(mid, PLANE, n)
     mixed, near_stats, turned, turned_out = call(
         functools.partial(near_kernel, z),
         [
             ((rows, width), F32),
             ((rows, LANES), F32),
-            ((z.half, rows), BF),
-            ((z.half, rows), BF),
+            ((width, rows), BF),
+            ((width, rows), BF),
         ],
         8 * base_flops,
         smem=1,
-    )(pad_count, after(q, far_up), k, v, g, tiles, order)
+    )(pad_count, after(q, far_up), k, v, g, tiles, order, order_q)
     mid_0 = jnp.concatenate(mid_parts, axis=0)
     mid_1 = swap(mid_0, 1, n)
-    far_parts = plane_parts(far_up, n, (near_stats,))
+    far_parts = step_parts(far_up, PLANE, n, (near_stats,))
     far_0 = jnp.concatenate([part[:, : 2 * width] for part in far_parts], axis=0)
     far_1 = swap(far_0, 1, n)
     far_qg_0 = jnp.concatenate([part[:, 2 * width :] for part in far_parts], axis=0)
@@ -650,10 +658,20 @@
         6 * rows * width * width,
         scratch=[pltpu.VMEM((rows, width), BF)],
         smem=1,
-    )(offsets, near_stats, stats, picked, raw, mixed, held, tiles, w_out, order)
+    )(offsets, near_stats, stats, picked, raw, mixed, held, tiles, w_out, order_out)
     attn_other = swap(attn_turned_out, 1, n)
     turned_other = swap(after(turned_out, picked), 1, n)
     cot_other = swap(after(cotangent, picked), 1, n)
+
+    stats_up = picked[z.mid : z.mid + z.far]
+    for i, step in enumerate(upper_steps(n)):
+        parts = step_parts(stats_up, step, n, (out_rows,) if i == 0 else ())
+        stats_up = jnp.concatenate(parts, axis=0)
+    def weights(start, *args):
+        kernel = functools.partial(weights_kernel, start)
+        return call(kernel, [((z.half, width), BF)], 4 * rows * width * width)(*args)[0]
+
+    wout_half = weights(0, attn_turned, attn_other, cotangent, after(cot_other, stats_up))
 
     dq, dk_near, dv_near = call(
         functools.partial(near_grads_kernel, z),
@@ -661,19 +679,14 @@
         8 * base_flops,
         scratch=[pltpu.VMEM((z.sel, width), F32)],
         smem=2,
-    )(offsets, pad_count, q, k, v, g, stats, sel, mid_0, mid_1, far_0, far_1, picked)
+    )(
+        offsets, pad_count, after(q, wout_half), k, v, g, stats, sel, mid_0, mid_1, far_0, far_1, picked
+    )
     dq_other = swap(dq, 1, n)
-
-    stats_up = doubled(picked[z.mid : z.mid + z.far], masks, n, (out_rows,))
-    stats_plane = [doubled(part, (2, 4), n) for part in (jnp.concatenate([picked[: z.mid], stats_up], axis=1),)]
-    stats_0 = jnp.concatenate([stats_plane[0][:, :LANES], stats_plane[0][:, LANES:]], axis=0)
+    stats_plane = doubled(jnp.concatenate([picked[: z.mid], stats_up], axis=1), (2, 4), n, (dk_near,))
+    stats_0 = jnp.concatenate([stats_plane[:, :LANES], stats_plane[:, LANES:]], axis=0)
     stats_1 = swap(stats_0, 1, n)
-
-    (early_half,) = call(
-        functools.partial(early_weights_kernel, z),
-        [((z.half, 2 * width), BF)],
-        4 * rows * width * width,
-    )(turned, turned_other, attn_turned, attn_other, dq, dq_other, cotangent, cot_other)
+    early_half = weights(z.half, turned, turned_other, dq, dq_other)
 
     dk, dv = call(
         functools.partial(key_grads_kernel, z),
@@ -695,11 +708,11 @@
         functools.partial(tiles_kernel, z), [((rows, width), BF)], 6 * rows * width * width
     )(after(dq, late_half), dk, dv, w_qkv)
     late = reduce_step(late_half, PLANE, n, BF)
-    early = reduce_step(early_half, PLANE, n, BF, (late_half,))
-    early = halved(early, masks[::-1], n)
+    early = halved(early_half, masks + [2, 4], n, ((grad_tiles,),))
+    grad_wout = halved(wout_half, [2, 4] + masks, n, ((dq,), (dk,), (grad_tiles,)))
     late = reduce_all(late, upper_steps(n)[::-1], n)
-    grad_wqkv = jnp.concatenate([early[:, width:], late], axis=1)
-    return out_rows, grad_tiles, grad_wqkv, early[:, :width]
+    grad_wqkv = jnp.concatenate([early, late], axis=1)
+    return out_rows, grad_tiles, grad_wqkv, grad_wout
 
 
 def solution(mesh):

time: 110 us -> 104 us (0.945)
  waiting for transfers between devices: 41.5 us -> 35.7 us
  starting transfers between devices: 36.5 us -> 37.7 us
  local copies, waits for them, and re-layouts: 3.67 us -> 2.47 us
    ppermute x33 -> x38, waiting for transfers between devices: 41.5 us -> 35.7 us  [swap(): return lax.ppermute(value, 'ctx', [(d, d ^ mask) for d in range(dev_count)])]
    slice x6 -> x10, local copies, waits for them, and re-layouts: 1.75 us -> 0.15 us  [the longest x8 0.14 us: halved(): parts = tied([value[:size], swap(value[size:], mask, dev_count)], first)]
    ppermute x33 -> x38, starting transfers between devices: 36.5 us -> 37.7 us  [swap(): return lax.ppermute(value, 'ctx', [(d, d ^ mask) for d in range(dev_count)])]
    pallas_call x9 -> x10, Pallas kernels: 23.4 us -> 23.9 us  [run(): pl.pallas_call(kernel, out_shape=tuple((jax.ShapeDtypeStruct(s, t) for s,...]
  transfers between devices with their start and end apart: 33 -> 38, of which waited for: 17 -> 15; matrix products, arithmetic and copies ran while one was open for 4% -> 3% of each run, Pallas kernels for 12% -> 16%
where the time goes in v4:
time: 104 us
  starting transfers between devices  37.7 us (36%)
  waiting for transfers between devices  35.7 us (34%)
  Pallas kernels  23.9 us (23%)
  local copies, waits for them, and re-layouts  2.47 us (2%)
  other arithmetic  2.02 us (2%)
  between operations  2 us (2%)
    ppermute x38, starting transfers between devices, swap(): return lax.ppermute(value, 'ctx', [(d, d ^ mask) for d in range(dev_count)])  37.7 us
    ppermute x38, waiting for transfers between devices, swap(): return lax.ppermute(value, 'ctx', [(d, d ^ mask) for d in range(dev_count)])  35.7 us
    pallas_call x10, Pallas kernels, run(): pl.pallas_call(kernel, out_shape=tuple((jax.ShapeDtypeStruct(s, t) for s,...  23.9 us
    unnamed x40, local copies, waits for them, and re-layouts  2.15 us
  transfers between devices with their start and end apart: 38, of which 15 were waited for; matrix products, arithmetic and copies ran while one was open for 3% of the time, Pallas kernels for 16%

profile of v4, /device:TPU:0, one launch (start us, length us, event | category | flops | bytes accessed | tf_op | source)
XLA Modules:
  0.0 103.9 jit_solution(12074073253806858096)
XLA Ops:
  0.7 5.4 %shard_map.147 = (bf16[256,768]{1,0:T(8,128)(2,1)}, bf16[256,768]{1,0:T(8,128)(2,1)}, bf16[256,768]{1,0:T(8,128)(2,1)}, bf16[256,768]{1,0:T(8,128)(2,1)}, bf16[6...) custom-call(s32[2,12]{1,0:T(2,128)} %offs_ref.7, bf16[256,768]{1,0:T(8,128)(2,1)} %tiles.3, ...), custom_call_target="tpu_custom_call" | custom-call | flops 1207959552 | bytes 7716960 | tf_op jit(solution)/shard_map/pallas_call | solution.py:514
  6.1 3.1 %collective-permute-start = (bf16[8,3072]{1,0:T(8,128)(2,1)}, bf16[8,3072]{1,0:T(8,128)(2,1)S(1)}, u32[]{:S(2)}, u32[]{:S(2)}) collective-permute-start(bf16[8,3072]{1,0:T(8,128)(2,1)} %get-tuple-element.53), channel_id=1, source_target_pairs={{0,8},{1,9},{2,10},{3,11},{4,12},{5,13},{6,14},{7,15},{8,0},{9,1},... | collective-permute-start | bytes 147464 | tf_op jit(solution)/shard_map/ppermute | solution.py:530
  9.2 2.6 %collective-permute-start.1 = (bf16[8,3072]{1,0:T(8,128)(2,1)}, bf16[8,3072]{1,0:T(8,128)(2,1)S(1)}, u32[]{:S(2)}, u32[]{:S(2)}) collective-permute-start(bf16[8,3072]{1,0:T(8,128)(2,1)} %get-tuple-element.53), channel_id=1, source_target_pairs={{0,16},{1,17},{2,18},{3,19},{4,20},{5,21},{6,22},{7,23},{8,24},{9,... | collective-permute-start | bytes 147464 | tf_op jit(solution)/shard_map/ppermute | solution.py:530
  11.8 1.7 %collective-permute-start.3 = (bf16[32,3072]{1,0:T(8,128)(2,1)}, bf16[32,3072]{1,0:T(8,128)(2,1)S(1)}, u32[]{:S(2)}, u32[]{:S(2)}) collective-permute-start(bf16[32,3072]{1,0:T(8,128)(2,1)} %get-tuple-element.60), channel_id=1, source_target_pairs={{0,2},{1,3},{2,0},{3,1},{4,6},{5,7},{6,4},{7,5},{8,10},{9,11},{10,... | collective-permute-start | bytes 589832 | tf_op jit(solution)/shard_map/ppermute | solution.py:530
  13.5 1.5 %collective-permute-start.4 = (bf16[32,3072]{1,0:T(8,128)(2,1)}, bf16[32,3072]{1,0:T(8,128)(2,1)S(1)}, u32[]{:S(2)}, u32[]{:S(2)}) collective-permute-start(bf16[32,3072]{1,0:T(8,128)(2,1)} %get-tuple-element.60), channel_id=1, source_target_pairs={{0,4},{1,5},{2,6},{3,7},{4,0},{5,1},{6,2},{7,3},{8,12},{9,13},{10,... | collective-permute-start | bytes 589832 | tf_op jit(solution)/shard_map/ppermute | solution.py:530
  15.0 0.8 constant_dynamic-update-slice_fusion.3
  15.8 0.9 constant_dynamic-update-slice_fusion.7
  18.2 1.8 %collective-permute-start.7 = (bf16[32,3072]{1,0:T(8,128)(2,1)S(1)}, bf16[32,3072]{1,0:T(8,128)(2,1)S(1)}, u32[]{:S(2)}, u32[]{:S(2)}) collective-permute-start(bf16[32,3072]{1,0:T(8,128)(2,1)S(1)} %constant_dynamic-update-slice_fusion), channel_id=1, source_target_pairs={{0,2},{1,3},{2,0},{3,1},{4,6},{5,7},{6,4},{7,5},{8,10},{9,11},{10,... | collective-permute-start | bytes 589832 | tf_op jit(solution)/shard_map/ppermute | solution.py:530
  19.9 1.5 %collective-permute-start.8 = (bf16[32,3072]{1,0:T(8,128)(2,1)S(1)}, bf16[32,3072]{1,0:T(8,128)(2,1)S(1)}, u32[]{:S(2)}, u32[]{:S(2)}) collective-permute-start(bf16[32,3072]{1,0:T(8,128)(2,1)S(1)} %constant_dynamic-update-slice_fusion), channel_id=1, source_target_pairs={{0,4},{1,5},{2,6},{3,7},{4,0},{5,1},{6,2},{7,3},{8,12},{9,13},{10,... | collective-permute-start | bytes 589832 | tf_op jit(solution)/shard_map/ppermute | solution.py:530
  21.5 2.5 %shard_map.148 = (f32[256,768]{1,0:T(8,128)S(1)}, f32[256,128]{1,0:T(8,128)S(1)}, bf16[768,256]{1,0:T(8,128)(2,1)S(1)}, bf16[768,256]{1,0:T(8,128)(2,1)S(1)}) custom-call(s32[1]{0:T(128)S(6)} %copy.29.pad_ref, bf16[256,768]{1,0:T(8,128)(2,1)S(1)} %copy-done.5, bf16[256,768]{1,0:T(8,128)(2,1)S(1)} %copy-done.6, bf16[256,768]{1,0:T(8,128)(2,1)S(1)} %copy-done.7, ...), custom_call_target="tpu_custom_call" | custom-call | flops 805306368 | bytes 3676164 | tf_op jit(solution)/shard_map/pallas_call | solution.py:514
  24.4 2.3 %collective-permute-done.5 = bf16[32,3072]{1,0:T(8,128)(2,1)S(1)} collective-permute-done((bf16[32,3072]{1,0:T(8,128)(2,1)S(1)}, bf16[32,3072]{1,0:T(8,128)(2,1)S(1)}, u32[]{:S(2)}, u32[]{:S(2)}) %collective-permute-start.5) | collective-permute-done | bytes 196640 | tf_op jit(solution)/shard_map/ppermute | solution.py:530
  26.8 2.7 %collective-permute-done.7 = bf16[32,3072]{1,0:T(8,128)(2,1)S(1)} collective-permute-done((bf16[32,3072]{1,0:T(8,128)(2,1)S(1)}, bf16[32,3072]{1,0:T(8,128)(2,1)S(1)}, u32[]{:S(2)}, u32[]{:S(2)}) %collective-permute-start.7) | collective-permute-done | bytes 196640 | tf_op jit(solution)/shard_map/ppermute | solution.py:530
  29.5 1.6 %collective-permute-done.8 = bf16[32,3072]{1,0:T(8,128)(2,1)S(1)} collective-permute-done((bf16[32,3072]{1,0:T(8,128)(2,1)S(1)}, bf16[32,3072]{1,0:T(8,128)(2,1)S(1)}, u32[]{:S(2)}, u32[]{:S(2)}) %collective-permute-start.8) | collective-permute-done | bytes 196640 | tf_op jit(solution)/shard_map/ppermute | solution.py:530
  31.1 1.4 %collective-permute-done.9 = bf16[32,3072]{1,0:T(8,128)(2,1)S(1)} collective-permute-done((bf16[32,3072]{1,0:T(8,128)(2,1)S(1)}, bf16[32,3072]{1,0:T(8,128)(2,1)S(1)}, u32[]{:S(2)}, u32[]{:S(2)}) %collective-permute-start.9) | collective-permute-done | bytes 196640 | tf_op jit(solution)/shard_map/ppermute | solution.py:530
  32.7 1.7 %collective-permute-done.10.far_1 = bf16[128,1536]{1,0:T(8,128)(2,1)S(1)} collective-permute-done((bf16[128,1536]{1,0:T(8,128)(2,1)S(1)}, bf16[128,1536]{1,0:T(8,128)(2,1)S(1)}, u32[]{:S(2)}, u32[]{:S(2)}) %collective-permute-start.10) | collective-permute-done | bytes 393248 | tf_op jit(solution)/shard_map/ppermute | solution.py:530
  34.4 2.3 %shard_map.149 = (f32[256,128]{1,0:T(8,128)S(1)}, f32[64,128]{1,0:T(8,128)S(1)}, f32[64,128]{1,0:T(8,128)S(1)}, f32[64,768]{1,0:T(8,128)S(1)}) custom-call(s32[2,12]{1,0:T(2,128)S(1)} %copy-done.9, s32[1]{0:T(128)S(6)} %copy.29.pad_ref, bf16[64,3072]{1,0:T(8,128)(2,1)S(1)} %copy-done.1, bf16[128,3072]{1,0:T(8,128)(2,1)S(1)} %constant_dynamic-update-slice_fusion.4.mid_0, ...), custom_call_target="tpu_custom_call" | custom-call | flops 301989888 | bytes 3276900 | tf_op jit(solution)/shard_map/pallas_call | solution.py:514
  36.7 0.7 collective-permute-start.13
  37.4 3.5 %collective-permute-start.14 = (f32[8,128]{1,0:T(8,128)S(1)}, f32[8,128]{1,0:T(8,128)S(1)}, u32[]{:S(2)}, u32[]{:S(2)}) collective-permute-start(f32[8,128]{1,0:T(8,128)S(1)} %slice.112), channel_id=1, source_target_pairs={{0,16},{1,17},{2,18},{3,19},{4,20},{5,21},{6,22},{7,23},{8,24},{9,... | collective-permute-start | bytes 12296 | tf_op jit(solution)/shard_map/ppermute | solution.py:530
  41.2 2.5 %shard_map.150 = (bf16[256,768]{1,0:T(8,128)(2,1)}, bf16[384,256]{1,0:T(8,128)(2,1)S(1)}, bf16[384,256]{1,0:T(8,128)(2,1)S(1)}) custom-call(s32[2,12]{1,0:T(2,128)S(1)} %copy-done.9, f32[256,128]{1,0:T(8,128)S(1)} %get-tuple-element.58.near_stats, f32[256,128]{1,0:T(8,128)S(1)} %get-tuple-element.65.stats, f32[64,128]{1,0:T(8,128)S(1)} %get-tuple-element.66.picked, ...), custom_call_target="tpu_custom_call" | custom-call | flops 905969664 | bytes 3673184 | tf_op jit(solution)/shard_map/pallas_call | solution.py:514
  44.2 2.1 %collective-permute-done.15 = f32[8,128]{1,0:T(8,128)S(1)} collective-permute-done((f32[8,128]{1,0:T(8,128)S(1)}, f32[8,128]{1,0:T(8,128)S(1)}, u32[]{:S(2)}, u32[]{:S(2)}) %collective-permute-start.15) | collective-permute-done | bytes 4128 | tf_op jit(solution)/shard_map/ppermute | solution.py:530
  46.3 0.8 collective-permute-start.18
  47.7 2.6 %collective-permute-done.18 = f32[32,256]{1,0:T(8,128)S(1)} collective-permute-done((f32[32,256]{1,0:T(8,128)S(1)}, f32[32,256]{1,0:T(8,128)S(1)}, u32[]{:S(2)}, u32[]{:S(2)}) %collective-permute-start.18) | collective-permute-done | bytes 32800 | tf_op jit(solution)/shard_map/ppermute | solution.py:530
  50.3 1.1 %collective-permute-start.19 = (f32[64,256]{1,0:T(8,128)S(1)}, f32[64,256]{1,0:T(8,128)S(1)}, u32[]{:S(2)}, u32[]{:S(2)}) collective-permute-start(f32[64,256]{1,0:T(8,128)S(1)} %pad_maximum_fusion.4), channel_id=1, source_target_pairs={{0,4},{1,5},{2,6},{3,7},{4,0},{5,1},{6,2},{7,3},{8,12},{9,13},{10,... | collective-permute-start | bytes 196616 | tf_op jit(solution)/shard_map/ppermute | solution.py:530
  52.0 0.6 collective-permute-start.34
  52.5 5.3 %shard_map.152 = (bf16[256,768]{1,0:T(8,128)(2,1)S(1)}, f32[256,768]{1,0:T(8,128)S(1)}, f32[256,768]{1,0:T(8,128)S(1)}) custom-call(s32[2,12]{1,0:T(2,128)S(1)} %copy-done.9, s32[1]{0:T(128)S(6)} %copy.29.pad_ref, bf16[256,768]{1,0:T(8,128)(2,1)S(1)} %copy-done.5, bf16[256,768]{1,0:T(8,128)(2,1)S(1)} %copy-done.6, bf16[256,768]{1,0:T(8,128)(2,1)S(1)} %copy-done.7, ...), custom_call_target="tpu_custom_call" | custom-call | flops 805306368 | bytes 6455396 | tf_op jit(solution)/shard_map/pallas_call | solution.py:514
  58.8 1.0 collective-permute-start.35
  60.3 2.3 %shard_map.154 = (bf16[256,768]{1,0:T(8,128)(2,1)S(1)}, bf16[256,768]{1,0:T(8,128)(2,1)S(1)}) custom-call(s32[2,12]{1,0:T(2,128)S(1)} %copy-done.9, s32[1]{0:T(128)S(6)} %copy.29.pad_ref, bf16[64,3072]{1,0:T(8,128)(2,1)S(1)} %copy-done.1, bf16[128,3072]{1,0:T(8,128)(2,1)S(1)} %constant_dynamic-update-slice_fusion.4.mid_0, ...), custom_call_target="tpu_custom_call" | custom-call | flops 301989888 | bytes 5374052 | tf_op jit(solution)/shard_map/pallas_call | solution.py:514
  63.4 1.2 %collective-permute-done.35 = bf16[96,768]{1,0:T(8,128)(2,1)S(1)} collective-permute-done((bf16[96,768]{1,0:T(8,128)(2,1)S(1)}, bf16[96,768]{1,0:T(8,128)(2,1)S(1)}, u32[]{:S(2)}, u32[]{:S(2)}) %collective-permute-start.35) | collective-permute-done | bytes 147488 | tf_op jit(solution)/shard_map/ppermute | solution.py:530
  64.6 0.9 collective-permute-start.36
  65.5 0.8 shard_map.155
  66.6 1.9 %shard_map.156 = bf16[256,768]{1,0:T(8,128)(2,1)} custom-call(bf16[256,768]{1,0:T(8,128)(2,1)S(1)} %get-tuple-element.91.right.dq, bf16[256,768]{1,0:T(8,128)(2,1)S(1)} %get-tuple-element.89.dk, bf16[256,768]{1,0:T(8,128)(2,1)S(1)} %get-tuple-element.90.dv, bf16[768,2304]{1,0:T(8,128)(2,1)S(1)} %copy-done), custom_call_target="tpu_custom_call" | custom-call | flops 905969664 | bytes 5111808 | tf_op jit(solution)/shard_map/pallas_call | solution.py:514
  68.4 5.5 %collective-permute-done.36 = bf16[48,768]{1,0:T(8,128)(2,1)S(1)} collective-permute-done((bf16[48,768]{1,0:T(8,128)(2,1)S(1)}, bf16[48,768]{1,0:T(8,128)(2,1)S(1)}, u32[]{:S(2)}, u32[]{:S(2)}) %collective-permute-start.36) | collective-permute-done | bytes 73760 | tf_op jit(solution)/shard_map/ppermute | solution.py:530
  74.1 1.2 %collective-permute-start.25 = (bf16[96,768]{1,0:T(8,128)(2,1)S(1)}, bf16[96,768]{1,0:T(8,128)(2,1)S(1)}, u32[]{:S(2)}, u32[]{:S(2)}) collective-permute-start(bf16[96,768]{1,0:T(8,128)(2,1)S(1)} %slice.149), channel_id=1, source_target_pairs={{0,16},{1,17},{2,18},{3,19},{4,20},{5,21},{6,22},{7,23},{8,24},{9,... | collective-permute-start | bytes 442376 | tf_op jit(solution)/shard_map/ppermute | solution.py:530
  75.3 1.9 %collective-permute-start.37 = (bf16[24,768]{1,0:T(8,128)(2,1)S(1)}, bf16[24,768]{1,0:T(8,128)(2,1)S(1)}, u32[]{:S(2)}, u32[]{:S(2)}) collective-permute-start(bf16[24,768]{1,0:T(8,128)(2,1)S(1)} %slice.169), channel_id=1, source_target_pairs={{0,16},{1,17},{2,18},{3,19},{4,20},{5,21},{6,22},{7,23},{8,24},{9,... | collective-permute-start | bytes 110600 | tf_op jit(solution)/shard_map/ppermute | solution.py:530
  77.2 1.3 %collective-permute-start.28 = (bf16[96,1536]{1,0:T(8,128)(2,1)S(1)}, bf16[96,1536]{1,0:T(8,128)(2,1)S(1)}, u32[]{:S(2)}, u32[]{:S(2)}) collective-permute-start(bf16[96,1536]{1,0:T(8,128)(2,1)S(1)} %get-tuple-element.100), channel_id=1, source_target_pairs={{0,2},{1,3},{2,0},{3,1},{4,6},{5,7},{6,4},{7,5},{8,10},{9,11},{10,... | collective-permute-start | bytes 884744 | tf_op jit(solution)/shard_map/ppermute | solution.py:530
  78.5 1.1 %collective-permute-start.29 = (bf16[96,1536]{1,0:T(8,128)(2,1)S(1)}, bf16[96,1536]{1,0:T(8,128)(2,1)S(1)}, u32[]{:S(2)}, u32[]{:S(2)}) collective-permute-start(bf16[96,1536]{1,0:T(8,128)(2,1)S(1)} %get-tuple-element.102), channel_id=1, source_target_pairs={{0,4},{1,5},{2,6},{3,7},{4,0},{5,1},{6,2},{7,3},{8,12},{9,13},{10,... | collective-permute-start | bytes 884744 | tf_op jit(solution)/shard_map/ppermute | solution.py:530
  79.6 1.1 %collective-permute-start.30 = (bf16[96,1536]{1,0:T(8,128)(2,1)S(1)}, bf16[96,1536]{1,0:T(8,128)(2,1)S(1)}, u32[]{:S(2)}, u32[]{:S(2)}) collective-permute-start(bf16[96,1536]{1,0:T(8,128)(2,1)S(1)} %get-tuple-element.101), channel_id=1, source_target_pairs={{0,6},{1,7},{2,4},{3,5},{4,2},{5,3},{6,0},{7,1},{8,14},{9,15},{10,... | collective-permute-start | bytes 884744 | tf_op jit(solution)/shard_map/ppermute | solution.py:530
  80.7 3.5 %collective-permute-done.25 = bf16[96,768]{1,0:T(8,128)(2,1)S(1)} collective-permute-done((bf16[96,768]{1,0:T(8,128)(2,1)S(1)}, bf16[96,768]{1,0:T(8,128)(2,1)S(1)}, u32[]{:S(2)}, u32[]{:S(2)}) %collective-permute-start.25) | collective-permute-done | bytes 147488 | tf_op jit(solution)/shard_map/ppermute | solution.py:530
  84.2 1.4 %collective-permute-start.26 = (bf16[48,768]{1,0:T(8,128)(2,1)S(1)}, bf16[48,768]{1,0:T(8,128)(2,1)S(1)}, u32[]{:S(2)}, u32[]{:S(2)}) collective-permute-start(bf16[48,768]{1,0:T(8,128)(2,1)S(1)} %slice.151), channel_id=1, source_target_pairs={{0,2},{1,3},{2,0},{3,1},{4,6},{5,7},{6,4},{7,5},{8,10},{9,11},{10,... | collective-permute-start | bytes 221192 | tf_op jit(solution)/shard_map/ppermute | solution.py:530
  85.6 0.6 convert_add_fusion.1
  86.3 6.4 %collective-permute-done.26 = bf16[48,768]{1,0:T(8,128)(2,1)S(1)} collective-permute-done((bf16[48,768]{1,0:T(8,128)(2,1)S(1)}, bf16[48,768]{1,0:T(8,128)(2,1)S(1)}, u32[]{:S(2)}, u32[]{:S(2)}) %collective-permute-start.26) | collective-permute-done | bytes 73760 | tf_op jit(solution)/shard_map/ppermute | solution.py:530
  92.8 1.2 %collective-permute-start.27 = (bf16[24,768]{1,0:T(8,128)(2,1)S(1)}, bf16[24,768]{1,0:T(8,128)(2,1)S(1)}, u32[]{:S(2)}, u32[]{:S(2)}) collective-permute-start(bf16[24,768]{1,0:T(8,128)(2,1)S(1)} %slice.153), channel_id=1, source_target_pairs={{0,4},{1,5},{2,6},{3,7},{4,0},{5,1},{6,2},{7,3},{8,12},{9,13},{10,... | collective-permute-start | bytes 110600 | tf_op jit(solution)/shard_map/ppermute | solution.py:530
  94.1 0.7 collective-permute-start.31
  94.8 2.2 %collective-permute-start.32 = (bf16[24,1536]{1,0:T(8,128)(2,1)S(1)}, bf16[24,1536]{1,0:T(8,128)(2,1)S(1)}, u32[]{:S(2)}, u32[]{:S(2)}) collective-permute-start(bf16[24,1536]{1,0:T(8,128)(2,1)S(1)} %get-tuple-element.114), channel_id=1, source_target_pairs={{0,16},{1,17},{2,18},{3,19},{4,20},{5,21},{6,22},{7,23},{8,24},{9,... | collective-permute-start | bytes 221192 | tf_op jit(solution)/shard_map/ppermute | solution.py:530
  97.0 1.6 %collective-permute-start.33 = (bf16[24,1536]{1,0:T(8,128)(2,1)S(1)}, bf16[24,1536]{1,0:T(8,128)(2,1)S(1)}, u32[]{:S(2)}, u32[]{:S(2)}) collective-permute-start(bf16[24,1536]{1,0:T(8,128)(2,1)S(1)} %get-tuple-element.113), channel_id=1, source_target_pairs={{0,24},{1,25},{2,26},{3,27},{4,28},{5,29},{6,30},{7,31},{8,16},{9,... | collective-permute-start | bytes 221192 | tf_op jit(solution)/shard_map/ppermute | solution.py:530
  99.1 2.0 %collective-permute-done.32 = bf16[24,1536]{1,0:T(8,128)(2,1)S(1)} collective-permute-done((bf16[24,1536]{1,0:T(8,128)(2,1)S(1)}, bf16[24,1536]{1,0:T(8,128)(2,1)S(1)}, u32[]{:S(2)}, u32[]{:S(2)}) %collective-permute-start.32) | collective-permute-done | bytes 73760 | tf_op jit(solution)/shard_map/ppermute | solution.py:530
  101.0 2.1 %collective-permute-done.33 = bf16[24,1536]{1,0:T(8,128)(2,1)S(1)} collective-permute-done((bf16[24,1536]{1,0:T(8,128)(2,1)S(1)}, bf16[24,1536]{1,0:T(8,128)(2,1)S(1)}, u32[]{:S(2)}, u32[]{:S(2)}) %collective-permute-start.33) | collective-permute-done | bytes 73760 | tf_op jit(solution)/shard_map/ppermute | solution.py:530
  103.2 0.7 pad_maximum_fusion.2
  (114 shorter events, 6.5 us)
Async XLA Ops:
  0.6 16.1 %copy-start.10 = (s32[768,1]{1,0:T(8,128)S(1)}, s32[768,1]{1,0:T(8,128)}, u32[]{:S(2)}) copy-start(s32[768,1]{1,0:T(8,128)} %constant.14.clone) | copy-start | bytes 9220
  0.6 16.1 %copy-start.11 = (s32[768,1]{1,0:T(8,128)S(1)}, s32[768,1]{1,0:T(8,128)}, u32[]{:S(2)}) copy-start(s32[768,1]{1,0:T(8,128)} %constant.15.clone) | copy-start | bytes 9220
  0.7 16.1 %copy-start.12 = (s32[768,1]{1,0:T(8,128)S(1)}, s32[768,1]{1,0:T(8,128)}, u32[]{:S(2)}) copy-start(s32[768,1]{1,0:T(8,128)} %constant.16.clone) | copy-start | bytes 9220
  0.7 16.1 %copy-start.13 = (s32[768,1]{1,0:T(8,128)S(1)}, s32[768,1]{1,0:T(8,128)}, u32[]{:S(2)}) copy-start(s32[768,1]{1,0:T(8,128)} %constant.17.clone) | copy-start | bytes 9220
  6.1 11.7 %collective-permute-start = (bf16[8,3072]{1,0:T(8,128)(2,1)}, bf16[8,3072]{1,0:T(8,128)(2,1)S(1)}, u32[]{:S(2)}, u32[]{:S(2)}) collective-permute-start(bf16[8,3072]{1,0:T(8,128)(2,1)} %get-tuple-element.53), channel_id=1, source_target_pairs={{0,8},{1,9},{2,10},{3,11},{4,12},{5,13},{6,14},{7,15},{8,0},{9,1},... | collective-permute-start | bytes 147464 | tf_op jit(solution)/shard_map/ppermute | solution.py:530
  9.2 8.9 %collective-permute-start.1 = (bf16[8,3072]{1,0:T(8,128)(2,1)}, bf16[8,3072]{1,0:T(8,128)(2,1)S(1)}, u32[]{:S(2)}, u32[]{:S(2)}) collective-permute-start(bf16[8,3072]{1,0:T(8,128)(2,1)} %get-tuple-element.53), channel_id=1, source_target_pairs={{0,16},{1,17},{2,18},{3,19},{4,20},{5,21},{6,22},{7,23},{8,24},{9,... | collective-permute-start | bytes 147464 | tf_op jit(solution)/shard_map/ppermute | solution.py:530
  11.8 6.4 %collective-permute-start.2 = (bf16[8,3072]{1,0:T(8,128)(2,1)}, bf16[8,3072]{1,0:T(8,128)(2,1)S(1)}, u32[]{:S(2)}, u32[]{:S(2)}) collective-permute-start(bf16[8,3072]{1,0:T(8,128)(2,1)} %get-tuple-element.53), channel_id=1, source_target_pairs={{0,24},{1,25},{2,26},{3,27},{4,28},{5,29},{6,30},{7,31},{8,16},{9,... | collective-permute-start | bytes 147464 | tf_op jit(solution)/shard_map/ppermute | solution.py:530
  11.8 12.2 %collective-permute-start.3 = (bf16[32,3072]{1,0:T(8,128)(2,1)}, bf16[32,3072]{1,0:T(8,128)(2,1)S(1)}, u32[]{:S(2)}, u32[]{:S(2)}) collective-permute-start(bf16[32,3072]{1,0:T(8,128)(2,1)} %get-tuple-element.60), channel_id=1, source_target_pairs={{0,2},{1,3},{2,0},{3,1},{4,6},{5,7},{6,4},{7,5},{8,10},{9,11},{10,... | collective-permute-start | bytes 589832 | tf_op jit(solution)/shard_map/ppermute | solution.py:530
  13.5 10.9 %collective-permute-start.4 = (bf16[32,3072]{1,0:T(8,128)(2,1)}, bf16[32,3072]{1,0:T(8,128)(2,1)S(1)}, u32[]{:S(2)}, u32[]{:S(2)}) collective-permute-start(bf16[32,3072]{1,0:T(8,128)(2,1)} %get-tuple-element.60), channel_id=1, source_target_pairs={{0,4},{1,5},{2,6},{3,7},{4,0},{5,1},{6,2},{7,3},{8,12},{9,13},{10,... | collective-permute-start | bytes 589832 | tf_op jit(solution)/shard_map/ppermute | solution.py:530
  16.8 4.6 %copy-start.3 = (bf16[256,768]{1,0:T(8,128)(2,1)S(1)}, bf16[256,768]{1,0:T(8,128)(2,1)}, u32[]{:S(2)}) copy-start(bf16[256,768]{1,0:T(8,128)(2,1)} %tiles.3) | copy-start | bytes 1179652
  16.8 4.6 %copy-start.5 = (bf16[256,768]{1,0:T(8,128)(2,1)S(1)}, bf16[256,768]{1,0:T(8,128)(2,1)}, u32[]{:S(2)}) copy-start(bf16[256,768]{1,0:T(8,128)(2,1)} %get-tuple-element.79.q) | copy-start | bytes 1179652
  16.8 4.6 %copy-start.6 = (bf16[256,768]{1,0:T(8,128)(2,1)S(1)}, bf16[256,768]{1,0:T(8,128)(2,1)}, u32[]{:S(2)}) copy-start(bf16[256,768]{1,0:T(8,128)(2,1)} %get-tuple-element.55.k) | copy-start | bytes 1179652
  16.9 4.6 %copy-start.7 = (bf16[256,768]{1,0:T(8,128)(2,1)S(1)}, bf16[256,768]{1,0:T(8,128)(2,1)}, u32[]{:S(2)}) copy-start(bf16[256,768]{1,0:T(8,128)(2,1)} %get-tuple-element.56.v) | copy-start | bytes 1179652
  17.8 8.9 %collective-permute-start.5 = (bf16[32,3072]{1,0:T(8,128)(2,1)S(1)}, bf16[32,3072]{1,0:T(8,128)(2,1)S(1)}, u32[]{:S(2)}, u32[]{:S(2)}) collective-permute-start(bf16[32,3072]{1,0:T(8,128)(2,1)S(1)} %copy-done.14), channel_id=1, source_target_pairs={{0,6},{1,7},{2,4},{3,5},{4,2},{5,3},{6,0},{7,1},{8,14},{9,15},{10,... | collective-permute-start | bytes 589832 | tf_op jit(solution)/shard_map/ppermute | solution.py:530
  18.2 11.3 %collective-permute-start.7 = (bf16[32,3072]{1,0:T(8,128)(2,1)S(1)}, bf16[32,3072]{1,0:T(8,128)(2,1)S(1)}, u32[]{:S(2)}, u32[]{:S(2)}) collective-permute-start(bf16[32,3072]{1,0:T(8,128)(2,1)S(1)} %constant_dynamic-update-slice_fusion), channel_id=1, source_target_pairs={{0,2},{1,3},{2,0},{3,1},{4,6},{5,7},{6,4},{7,5},{8,10},{9,11},{10,... | collective-permute-start | bytes 589832 | tf_op jit(solution)/shard_map/ppermute | solution.py:530
  19.9 11.1 %collective-permute-start.8 = (bf16[32,3072]{1,0:T(8,128)(2,1)S(1)}, bf16[32,3072]{1,0:T(8,128)(2,1)S(1)}, u32[]{:S(2)}, u32[]{:S(2)}) collective-permute-start(bf16[32,3072]{1,0:T(8,128)(2,1)S(1)} %constant_dynamic-update-slice_fusion), channel_id=1, source_target_pairs={{0,4},{1,5},{2,6},{3,7},{4,0},{5,1},{6,2},{7,3},{8,12},{9,13},{10,... | collective-permute-start | bytes 589832 | tf_op jit(solution)/shard_map/ppermute | solution.py:530
  24.0 8.5 %collective-permute-start.9 = (bf16[32,3072]{1,0:T(8,128)(2,1)S(1)}, bf16[32,3072]{1,0:T(8,128)(2,1)S(1)}, u32[]{:S(2)}, u32[]{:S(2)}) collective-permute-start(bf16[32,3072]{1,0:T(8,128)(2,1)S(1)} %constant_dynamic-update-slice_fusion), channel_id=1, source_target_pairs={{0,6},{1,7},{2,4},{3,5},{4,2},{5,3},{6,0},{7,1},{8,14},{9,15},{10,... | collective-permute-start | bytes 589832 | tf_op jit(solution)/shard_map/ppermute | solution.py:530
  26.7 7.7 %collective-permute-start.6 = (bf16[128,3072]{1,0:T(8,128)(2,1)S(1)}, bf16[128,3072]{1,0:T(8,128)(2,1)S(1)}, u32[]{:S(2)}, u32[]{:S(2)}) collective-permute-start(bf16[128,3072]{1,0:T(8,128)(2,1)S(1)} %constant_dynamic-update-slice_fusion.4.mid_0), channel_id=1, source_target_pairs={{0,1},{1,0},{2,3},{3,2},{4,5},{5,4},{6,7},{7,6},{8,9},{9,8},{10,11... | collective-permute-start | bytes 2359304 | tf_op jit(solution)/shard_map/ppermute | solution.py:530
  32.6 1.8 %collective-permute-start.10 = (bf16[128,1536]{1,0:T(8,128)(2,1)S(1)}, bf16[128,1536]{1,0:T(8,128)(2,1)S(1)}, u32[]{:S(2)}, u32[]{:S(2)}) collective-permute-start(bf16[128,1536]{1,0:T(8,128)(2,1)S(1)} %pad_maximum_fusion.far_0), channel_id=1, source_target_pairs={{0,1},{1,0},{2,3},{3,2},{4,5},{5,4},{6,7},{7,6},{8,9},{9,8},{10,11... | collective-permute-start | bytes 1179656 | tf_op jit(solution)/shard_map/ppermute | solution.py:530
  34.4 6.8 %copy-start.4 = (bf16[256,768]{1,0:T(8,128)(2,1)S(1)}, bf16[256,768]{1,0:T(8,128)(2,1)}, u32[]{:S(2)}) copy-start(bf16[256,768]{1,0:T(8,128)(2,1)} %right.1) | copy-start | bytes 1179652
  34.4 6.8 %copy-start.2 = (bf16[768,768]{1,0:T(8,128)(2,1)S(1)}, bf16[768,768]{1,0:T(8,128)(2,1)}, u32[]{:S(2)}) copy-start(bf16[768,768]{1,0:T(8,128)(2,1)} %w_out.1) | copy-start | bytes 3538948
  36.7 7.5 %collective-permute-start.13 = (f32[8,128]{1,0:T(8,128)S(1)}, f32[8,128]{1,0:T(8,128)S(1)}, u32[]{:S(2)}, u32[]{:S(2)}) collective-permute-start(f32[8,128]{1,0:T(8,128)S(1)} %slice.112), channel_id=1, source_target_pairs={{0,8},{1,9},{2,10},{3,11},{4,12},{5,13},{6,14},{7,15},{8,0},{9,1},... | collective-permute-start | bytes 12296 | tf_op jit(solution)/shard_map/ppermute | solution.py:530
  37.4 6.8 %collective-permute-start.14 = (f32[8,128]{1,0:T(8,128)S(1)}, f32[8,128]{1,0:T(8,128)S(1)}, u32[]{:S(2)}, u32[]{:S(2)}) collective-permute-start(f32[8,128]{1,0:T(8,128)S(1)} %slice.112), channel_id=1, source_target_pairs={{0,16},{1,17},{2,18},{3,19},{4,20},{5,21},{6,22},{7,23},{8,24},{9,... | collective-permute-start | bytes 12296 | tf_op jit(solution)/shard_map/ppermute | solution.py:530
  40.9 5.4 %collective-permute-start.15 = (f32[8,128]{1,0:T(8,128)S(1)}, f32[8,128]{1,0:T(8,128)S(1)}, u32[]{:S(2)}, u32[]{:S(2)}) collective-permute-start(f32[8,128]{1,0:T(8,128)S(1)} %slice.112), channel_id=1, source_target_pairs={{0,24},{1,25},{2,26},{3,27},{4,28},{5,29},{6,30},{7,31},{8,16},{9,... | collective-permute-start | bytes 12296 | tf_op jit(solution)/shard_map/ppermute | solution.py:530
  41.2 10.2 %collective-permute-start.12 = (bf16[256,768]{1,0:T(8,128)(2,1)S(1)}, bf16[256,768]{1,0:T(8,128)(2,1)S(1)}, u32[]{:S(2)}, u32[]{:S(2)}) collective-permute-start(bf16[256,768]{1,0:T(8,128)(2,1)S(1)} %copy-done.4), channel_id=1, source_target_pairs={{0,1},{1,0},{2,3},{3,2},{4,5},{5,4},{6,7},{7,6},{8,9},{9,8},{10,11... | collective-permute-start | bytes 1179656 | tf_op jit(solution)/shard_map/ppermute | solution.py:530
  43.7 7.7 %collective-permute-start.11 = (bf16[384,256]{1,0:T(8,128)(2,1)S(1)}, bf16[384,256]{1,0:T(8,128)(2,1)S(1)}, u32[]{:S(2)}, u32[]{:S(2)}) collective-permute-start(bf16[384,256]{1,0:T(8,128)(2,1)S(1)} %get-tuple-element.72), channel_id=1, source_target_pairs={{0,1},{1,0},{2,3},{3,2},{4,5},{5,4},{6,7},{7,6},{8,9},{9,8},{10,11... | collective-permute-start | bytes 589832 | tf_op jit(solution)/shard_map/ppermute | solution.py:530
  46.3 4.0 %collective-permute-start.18 = (f32[32,256]{1,0:T(8,128)S(1)}, f32[32,256]{1,0:T(8,128)S(1)}, u32[]{:S(2)}, u32[]{:S(2)}) collective-permute-start(f32[32,256]{1,0:T(8,128)S(1)} %pad_maximum_fusion.5), channel_id=1, source_target_pairs={{0,2},{1,3},{2,0},{3,1},{4,6},{5,7},{6,4},{7,5},{8,10},{9,11},{10,... | collective-permute-start | bytes 98312 | tf_op jit(solution)/shard_map/ppermute | solution.py:530
  47.1 13.2 %collective-permute-start.17 = (bf16[128,1536]{1,0:T(8,128)(2,1)S(1)}, bf16[128,1536]{1,0:T(8,128)(2,1)S(1)}, u32[]{:S(2)}, u32[]{:S(2)}) collective-permute-start(bf16[128,1536]{1,0:T(8,128)(2,1)S(1)} %pad_maximum_fusion.1.far_0), channel_id=1, source_target_pairs={{0,1},{1,0},{2,3},{3,2},{4,5},{5,4},{6,7},{7,6},{8,9},{9,8},{10,11... | collective-permute-start | bytes 1179656 | tf_op jit(solution)/shard_map/ppermute | solution.py:530
  47.2 12.6 %collective-permute-start.16 = (bf16[768,256]{1,0:T(8,128)(2,1)S(1)}, bf16[768,256]{1,0:T(8,128)(2,1)S(1)}, u32[]{:S(2)}, u32[]{:S(2)}) collective-permute-start(bf16[768,256]{1,0:T(8,128)(2,1)S(1)} %get-tuple-element.83), channel_id=1, source_target_pairs={{0,1},{1,0},{2,3},{3,2},{4,5},{5,4},{6,7},{7,6},{8,9},{9,8},{10,11... | collective-permute-start | bytes 1179656 | tf_op jit(solution)/shard_map/ppermute | solution.py:530
  50.3 7.6 %collective-permute-start.19 = (f32[64,256]{1,0:T(8,128)S(1)}, f32[64,256]{1,0:T(8,128)S(1)}, u32[]{:S(2)}, u32[]{:S(2)}) collective-permute-start(f32[64,256]{1,0:T(8,128)S(1)} %pad_maximum_fusion.4), channel_id=1, source_target_pairs={{0,4},{1,5},{2,6},{3,7},{4,0},{5,1},{6,2},{7,3},{8,12},{9,13},{10,... | collective-permute-start | bytes 196616 | tf_op jit(solution)/shard_map/ppermute | solution.py:530
  52.0 6.8 %collective-permute-start.34 = (bf16[192,768]{1,0:T(8,128)(2,1)S(1)}, bf16[192,768]{1,0:T(8,128)(2,1)S(1)}, u32[]{:S(2)}, u32[]{:S(2)}) collective-permute-start(bf16[192,768]{1,0:T(8,128)(2,1)S(1)} %get-tuple-element.103), channel_id=1, source_target_pairs={{0,2},{1,3},{2,0},{3,1},{4,6},{5,7},{6,4},{7,5},{8,10},{9,11},{10,... | collective-permute-start | bytes 884744 | tf_op jit(solution)/shard_map/ppermute | solution.py:530
  57.9 2.0 %collective-permute-start.21 = (bf16[256,768]{1,0:T(8,128)(2,1)S(1)}, bf16[256,768]{1,0:T(8,128)(2,1)S(1)}, u32[]{:S(2)}, u32[]{:S(2)}) collective-permute-start(bf16[256,768]{1,0:T(8,128)(2,1)S(1)} %get-tuple-element.91.right.dq), channel_id=1, source_target_pairs={{0,1},{1,0},{2,3},{3,2},{4,5},{5,4},{6,7},{7,6},{8,9},{9,8},{10,11... | collective-permute-start | bytes 1179656 | tf_op jit(solution)/shard_map/ppermute | solution.py:530
  58.0 2.3 %collective-permute-start.20 = (f32[256,128]{1,0:T(8,128)S(1)}, f32[256,128]{1,0:T(8,128)S(1)}, u32[]{:S(2)}, u32[]{:S(2)}) collective-permute-start(f32[256,128]{1,0:T(8,128)S(1)} %pad_maximum_fusion.3.stats_0), channel_id=1, source_target_pairs={{0,1},{1,0},{2,3},{3,2},{4,5},{5,4},{6,7},{7,6},{8,9},{9,8},{10,11... | collective-permute-start | bytes 393224 | tf_op jit(solution)/shard_map/ppermute | solution.py:530
  58.8 5.7 %collective-permute-start.35 = (bf16[96,768]{1,0:T(8,128)(2,1)S(1)}, bf16[96,768]{1,0:T(8,128)(2,1)S(1)}, u32[]{:S(2)}, u32[]{:S(2)}) collective-permute-start(bf16[96,768]{1,0:T(8,128)(2,1)S(1)} %get-tuple-element.110), channel_id=1, source_target_pairs={{0,4},{1,5},{2,6},{3,7},{4,0},{5,1},{6,2},{7,3},{8,12},{9,13},{10,... | collective-permute-start | bytes 442376 | tf_op jit(solution)/shard_map/ppermute | solution.py:530
  62.7 2.9 %collective-permute-start.22 = (bf16[256,768]{1,0:T(8,128)(2,1)S(1)}, bf16[256,768]{1,0:T(8,128)(2,1)S(1)}, u32[]{:S(2)}, u32[]{:S(2)}) collective-permute-start(bf16[256,768]{1,0:T(8,128)(2,1)S(1)} %get-tuple-element.89.dk), channel_id=1, source_target_pairs={{0,1},{1,0},{2,3},{3,2},{4,5},{5,4},{6,7},{7,6},{8,9},{9,8},{10,11... | collective-permute-start | bytes 1179656 | tf_op jit(solution)/shard_map/ppermute | solution.py:530
  62.7 2.8 %collective-permute-start.23 = (bf16[256,768]{1,0:T(8,128)(2,1)S(1)}, bf16[256,768]{1,0:T(8,128)(2,1)S(1)}, u32[]{:S(2)}, u32[]{:S(2)}) collective-permute-start(bf16[256,768]{1,0:T(8,128)(2,1)S(1)} %get-tuple-element.90.dv), channel_id=1, source_target_pairs={{0,1},{1,0},{2,3},{3,2},{4,5},{5,4},{6,7},{7,6},{8,9},{9,8},{10,11... | collective-permute-start | bytes 1179656 | tf_op jit(solution)/shard_map/ppermute | solution.py:530
  63.3 10.7 %collective-permute-start.24 = (bf16[192,768]{1,0:T(8,128)(2,1)S(1)}, bf16[192,768]{1,0:T(8,128)(2,1)S(1)}, u32[]{:S(2)}, u32[]{:S(2)}) collective-permute-start(bf16[192,768]{1,0:T(8,128)(2,1)S(1)} %get-tuple-element.105), channel_id=1, source_target_pairs={{0,8},{1,9},{2,10},{3,11},{4,12},{5,13},{6,14},{7,15},{8,0},{9,1},... | collective-permute-start | bytes 884744 | tf_op jit(solution)/shard_map/ppermute | solution.py:530
  64.6 9.3 %collective-permute-start.36 = (bf16[48,768]{1,0:T(8,128)(2,1)S(1)}, bf16[48,768]{1,0:T(8,128)(2,1)S(1)}, u32[]{:S(2)}, u32[]{:S(2)}) collective-permute-start(bf16[48,768]{1,0:T(8,128)(2,1)S(1)} %get-tuple-element.123), channel_id=1, source_target_pairs={{0,8},{1,9},{2,10},{3,11},{4,12},{5,13},{6,14},{7,15},{8,0},{9,1},... | collective-permute-start | bytes 221192 | tf_op jit(solution)/shard_map/ppermute | solution.py:530
  74.1 10.0 %collective-permute-start.25 = (bf16[96,768]{1,0:T(8,128)(2,1)S(1)}, bf16[96,768]{1,0:T(8,128)(2,1)S(1)}, u32[]{:S(2)}, u32[]{:S(2)}) collective-permute-start(bf16[96,768]{1,0:T(8,128)(2,1)S(1)} %slice.149), channel_id=1, source_target_pairs={{0,16},{1,17},{2,18},{3,19},{4,20},{5,21},{6,22},{7,23},{8,24},{9,... | collective-permute-start | bytes 442376 | tf_op jit(solution)/shard_map/ppermute | solution.py:530
  75.3 10.3 %collective-permute-start.37 = (bf16[24,768]{1,0:T(8,128)(2,1)S(1)}, bf16[24,768]{1,0:T(8,128)(2,1)S(1)}, u32[]{:S(2)}, u32[]{:S(2)}) collective-permute-start(bf16[24,768]{1,0:T(8,128)(2,1)S(1)} %slice.169), channel_id=1, source_target_pairs={{0,16},{1,17},{2,18},{3,19},{4,20},{5,21},{6,22},{7,23},{8,24},{9,... | collective-permute-start | bytes 110600 | tf_op jit(solution)/shard_map/ppermute | solution.py:530
  77.2 16.7 %collective-permute-start.28 = (bf16[96,1536]{1,0:T(8,128)(2,1)S(1)}, bf16[96,1536]{1,0:T(8,128)(2,1)S(1)}, u32[]{:S(2)}, u32[]{:S(2)}) collective-permute-start(bf16[96,1536]{1,0:T(8,128)(2,1)S(1)} %get-tuple-element.100), channel_id=1, source_target_pairs={{0,2},{1,3},{2,0},{3,1},{4,6},{5,7},{6,4},{7,5},{8,10},{9,11},{10,... | collective-permute-start | bytes 884744 | tf_op jit(solution)/shard_map/ppermute | solution.py:530
  78.5 15.4 %collective-permute-start.29 = (bf16[96,1536]{1,0:T(8,128)(2,1)S(1)}, bf16[96,1536]{1,0:T(8,128)(2,1)S(1)}, u32[]{:S(2)}, u32[]{:S(2)}) collective-permute-start(bf16[96,1536]{1,0:T(8,128)(2,1)S(1)} %get-tuple-element.102), channel_id=1, source_target_pairs={{0,4},{1,5},{2,6},{3,7},{4,0},{5,1},{6,2},{7,3},{8,12},{9,13},{10,... | collective-permute-start | bytes 884744 | tf_op jit(solution)/shard_map/ppermute | solution.py:530
  79.6 14.3 %collective-permute-start.30 = (bf16[96,1536]{1,0:T(8,128)(2,1)S(1)}, bf16[96,1536]{1,0:T(8,128)(2,1)S(1)}, u32[]{:S(2)}, u32[]{:S(2)}) collective-permute-start(bf16[96,1536]{1,0:T(8,128)(2,1)S(1)} %get-tuple-element.101), channel_id=1, source_target_pairs={{0,6},{1,7},{2,4},{3,5},{4,2},{5,3},{6,0},{7,1},{8,14},{9,15},{10,... | collective-permute-start | bytes 884744 | tf_op jit(solution)/shard_map/ppermute | solution.py:530
  84.2 8.5 %collective-permute-start.26 = (bf16[48,768]{1,0:T(8,128)(2,1)S(1)}, bf16[48,768]{1,0:T(8,128)(2,1)S(1)}, u32[]{:S(2)}, u32[]{:S(2)}) collective-permute-start(bf16[48,768]{1,0:T(8,128)(2,1)S(1)} %slice.151), channel_id=1, source_target_pairs={{0,2},{1,3},{2,0},{3,1},{4,6},{5,7},{6,4},{7,5},{8,10},{9,11},{10,... | collective-permute-start | bytes 221192 | tf_op jit(solution)/shard_map/ppermute | solution.py:530
  92.8 5.8 %collective-permute-start.27 = (bf16[24,768]{1,0:T(8,128)(2,1)S(1)}, bf16[24,768]{1,0:T(8,128)(2,1)S(1)}, u32[]{:S(2)}, u32[]{:S(2)}) collective-permute-start(bf16[24,768]{1,0:T(8,128)(2,1)S(1)} %slice.153), channel_id=1, source_target_pairs={{0,4},{1,5},{2,6},{3,7},{4,0},{5,1},{6,2},{7,3},{8,12},{9,13},{10,... | collective-permute-start | bytes 110600 | tf_op jit(solution)/shard_map/ppermute | solution.py:530
  94.1 4.9 %collective-permute-start.31 = (bf16[24,1536]{1,0:T(8,128)(2,1)S(1)}, bf16[24,1536]{1,0:T(8,128)(2,1)S(1)}, u32[]{:S(2)}, u32[]{:S(2)}) collective-permute-start(bf16[24,1536]{1,0:T(8,128)(2,1)S(1)} %get-tuple-element.112), channel_id=1, source_target_pairs={{0,8},{1,9},{2,10},{3,11},{4,12},{5,13},{6,14},{7,15},{8,0},{9,1},... | collective-permute-start | bytes 221192 | tf_op jit(solution)/shard_map/ppermute | solution.py:530
  94.8 6.2 %collective-permute-start.32 = (bf16[24,1536]{1,0:T(8,128)(2,1)S(1)}, bf16[24,1536]{1,0:T(8,128)(2,1)S(1)}, u32[]{:S(2)}, u32[]{:S(2)}) collective-permute-start(bf16[24,1536]{1,0:T(8,128)(2,1)S(1)} %get-tuple-element.114), channel_id=1, source_target_pairs={{0,16},{1,17},{2,18},{3,19},{4,20},{5,21},{6,22},{7,23},{8,24},{9,... | collective-permute-start | bytes 221192 | tf_op jit(solution)/shard_map/ppermute | solution.py:530
  97.0 6.2 %collective-permute-start.33 = (bf16[24,1536]{1,0:T(8,128)(2,1)S(1)}, bf16[24,1536]{1,0:T(8,128)(2,1)S(1)}, u32[]{:S(2)}, u32[]{:S(2)}) collective-permute-start(bf16[24,1536]{1,0:T(8,128)(2,1)S(1)} %get-tuple-element.113), channel_id=1, source_target_pairs={{0,24},{1,25},{2,26},{3,27},{4,28},{5,29},{6,30},{7,31},{8,16},{9,... | collective-permute-start | bytes 221192 | tf_op jit(solution)/shard_map/ppermute | solution.py:530
  (5 other events, 11.4 us)

commit v5 on v4

--- a/solution.py
+++ b/solution.py
@@ -142,8 +142,9 @@
 
 
 def project_kernel(
-    z, offs_hbm, tiles_hbm, w_qkv_hbm, cot_hbm, w_out_hbm, q, k, v, g, sel, mid, far,
-    offs_ref, tiles, w_qkv, cot, w_out, sems,
+    z, offs_hbm, tiles_hbm, w_qkv_hbm, cot_hbm, w_out_hbm,
+    q_hbm, k_hbm, v_hbm, g_hbm, sel, mid_kv, mid_qg, far,
+    offs_ref, tiles, w_qkv, cot, w_out, q, k, v, g, sems, out_sems,
 ):
     width = z.width
     step = width // LOAD_CUTS
@@ -182,15 +183,26 @@
         for copy in copies[group]:
             copy.wait()
 
+    leaving = []
+
+    def leave(source, target):
+        copy = pltpu.make_async_copy(source, target, out_sems.at[len(leaving)])
+        copy.start()
+        leaving.append(copy)
+
     arrived(0)
     own = tiles[...]
     k[...] = dot(own, w_qkv[:, width : 2 * width]).astype(BF)
+    leave(k, k_hbm)
     arrived(1)
     v[...] = dot(own, w_qkv[:, 2 * width :]).astype(BF)
+    leave(v, v_hbm)
     arrived(2)
     q[...] = dot(own, w_qkv[:, :width]).astype(BF) * jnp.asarray(SCALE, BF)
+    leave(q, q_hbm)
     arrived(3)
     g[...] = dot(cot[...], w_out[...], NT).astype(BF)
+    leave(g, g_hbm)
     arrived(4)
     entry = iota((2 * z.sel, z.rows), 0)
     column = iota((2 * z.sel, z.rows), 1)
@@ -212,8 +224,12 @@
         for part in range(4):
             to = slice(part * width + pair * PAIR, part * width + (pair + 1) * PAIR)
             sel[:, to] = picked[:, part * PAIR : (part + 1) * PAIR]
-            mid[:, to] = picked[: z.mid, part * PAIR : (part + 1) * PAIR]
+            near_to = slice(to.start % (2 * width), to.start % (2 * width) + PAIR)
+            mid = mid_kv if part < 2 else mid_qg
+            mid[:, near_to] = picked[: z.mid, part * PAIR : (part + 1) * PAIR]
             far[:, to] = far_part[:, part * PAIR : (part + 1) * PAIR]
+    for copy in leaving:
+        copy.wait()
 
 
 def near_kernel(
@@ -378,11 +394,7 @@
         target[...] = dot(place, attn[...], NT).astype(BF)
 
 
-def near_grads_kernel(
-    z, offs_ref, pad_ref, q, k, v, g, stats, sel, mid_0, mid_1, far_0, far_1, picked,
-    dq, dk, dv, dq_sel,
-):
-    own = lax.axis_index("ctx")
+def own_grads_kernel(z, offs_ref, pad_ref, sel, mid_0, mid_1, far_0, far_1, picked, dq_sel):
     limit = z.rows * z.devs - pad_ref[0]
     refs = ((mid_0, mid_1), (far_0, far_1))
     scores, spots = own_scores(z, limit, offs_ref, sel, refs)
@@ -405,6 +417,11 @@
             at, to = spot_of(spots, level, 2 * pair + 1)
             sums.append(low + dot(grad_scores[at:to], keys[1]))
         dq_sel[:, pair * PAIR : (pair + 1) * PAIR] = jnp.concatenate(sums + [tail], axis=0)
+
+
+def near_grads_kernel(z, offs_ref, pad_ref, q, k, v, g, stats, dq_sel, dq, dk, dv):
+    own = lax.axis_index("ctx")
+    limit = z.rows * z.devs - pad_ref[0]
     valid_near = iota((z.rows, 1), 0) < limit - own * z.rows
     across = jnp.transpose(stats[...])
     for pair in range(z.pairs):
@@ -433,14 +450,17 @@
 
 
 def key_grads_kernel(
-    z, offs_ref, pad_ref, sel, mid_0, mid_1, far_0, far_1, stats_0, stats_1, dk_near, dv_near, dk, dv
+    z, offs_ref, pad_ref, sel, qg_0, qg_1, stats_0, stats_1, dk_near, dv_near, dk, dv
 ):
     own = lax.axis_index("ctx")
     limit = z.rows * z.devs - pad_ref[0] - own * z.rows
     parts = level_parts(z)
-    refs = ((mid_0, mid_1), (far_0, far_1))
     stat_refs = (stats_0, stats_1)
-    first_part = (2, 0)
+
+    def rows_of(level, lanes):
+        cuts = [slice(p * z.sel + level * z.mid, p * z.sel + (level + 1) * z.mid) for p in range(4)]
+        return jnp.concatenate([ref[cut, lanes] for ref in (qg_0, qg_1) for cut in cuts], axis=0)
+
     tail = jnp.zeros((z.sel - parts[1][1], PAIR), F32)
     probs, grad_scores = {}, {}
     for level, (start, stop) in enumerate(parts):
@@ -449,8 +469,8 @@
         for pair in range(z.pairs):
             keys = sel[start:stop, part_lanes(z, 0, pair)]
             values = sel[start:stop, part_lanes(z, 1, pair)]
-            queries = halves(of_level(level, refs, part_lanes(z, first_part[level], pair)))
-            grads = halves(of_level(level, refs, part_lanes(z, first_part[level] + 1, pair)))
+            queries = halves(rows_of(level, part_lanes(z, 0, pair)))
+            grads = halves(rows_of(level, part_lanes(z, 1, pair)))
             for side in range(2):
                 head = 2 * pair + side
                 at = chosen_row(z, entry, offs_ref[0, head], offs_ref[1, head])
@@ -465,8 +485,8 @@
     for pair in range(z.pairs):
         both_k, both_v = [], []
         for level in range(2):
-            queries = halves(of_level(level, refs, part_lanes(z, first_part[level], pair)))
-            grads = halves(of_level(level, refs, part_lanes(z, first_part[level] + 1, pair)))
+            queries = halves(rows_of(level, part_lanes(z, 0, pair)))
+            grads = halves(rows_of(level, part_lanes(z, 1, pair)))
             low, high = 2 * pair, 2 * pair + 1
             both_k.append(
                 dot(grad_scores[level, low], queries[0]) + dot(grad_scores[level, high], queries[1])
@@ -503,7 +523,7 @@
     ).astype(BF)
 
 
-def call(kernel, outs, flops, scratch=(), smem=0, spaces=None, vmem=VMEM_BYTES):
+def call(kernel, outs, flops, scratch=(), smem=0, spaces=None, vmem=VMEM_BYTES, hbm_outs=0):
     def run(*args):
         moved = sum(int(np.prod(a.shape)) * a.dtype.itemsize for a in args)
         moved += sum(int(np.prod(s)) * jnp.dtype(t).itemsize for s, t in outs)
@@ -515,7 +535,10 @@
             kernel,
             out_shape=tuple(jax.ShapeDtypeStruct(s, t) for s, t in outs),
             in_specs=specs,
-            out_specs=tuple(pl.BlockSpec(memory_space=pltpu.VMEM) for _ in outs),
+            out_specs=tuple(
+                pl.BlockSpec(memory_space=pltpu.HBM if i < hbm_outs else pltpu.VMEM)
+                for i in range(len(outs))
+            ),
             scratch_shapes=list(scratch),
             compiler_params=pltpu.CompilerParams(vmem_limit_bytes=vmem),
             cost_estimate=pl.CostEstimate(
@@ -548,14 +571,24 @@
 
 def step_parts(value, step, dev_count, first=()):
     base, count = step
-    return tied(
-        [value] + [swap(value, base * i, dev_count) for i in range(1, count)], first
-    )
-
-
-def doubled(value, masks, dev_count, first=()):
+    return tied([value] + [swap(value, base * i, dev_count) for i in range(1, count)], first)
+
+
+def block_parts(value, step, dev_count):
+    base, count = step
+    size = value.shape[0] // count
+    return [value[:size]] + [
+        swap(value[i * size : (i + 1) * size], base * i, dev_count) for i in range(1, count)
+    ]
+
+
+def sum_parts(parts, dtype):
+    return sum(part.astype(F32) for part in parts).astype(dtype)
+
+
+def doubled(value, masks, dev_count, firsts=()):
     for i, mask in enumerate(masks):
-        parts = tied([value, swap(value, mask, dev_count)], first if i == len(masks) - 1 else ())
+        parts = tied([value, swap(value, mask, dev_count)], firsts[i] if i < len(firsts) else ())
         value = jnp.concatenate(parts, axis=0)
     return value
 
@@ -570,18 +603,9 @@
     return value
 
 
-def reduce_step(value, step, dev_count, dtype, first=()):
-    base, count = step
-    size = value.shape[0] // count
-    parts = [value[:size]] + [
-        swap(value[i * size : (i + 1) * size], base * i, dev_count) for i in range(1, count)
-    ]
-    return sum(part.astype(F32) for part in tied(parts, first)).astype(dtype)
-
-
 def reduce_all(value, steps, dev_count):
     for i, step in enumerate(steps):
-        value = reduce_step(value, step, dev_count, F32 if i == len(steps) - 1 else BF)
+        value = sum_parts(block_parts(value, step, dev_count), F32 if i == len(steps) - 1 else BF)
     return value
 
 
@@ -606,9 +630,12 @@
     order_out = strip_order(z, own, [1, 2, 4] + masks)
     base_flops = 2 * rows * rows * width
 
-    q, k, v, g, sel, mid, far = call(
+    q, k, v, g, sel, mid_kv, mid_qg, far = call(
         functools.partial(project_kernel, z),
-        [((rows, width), BF)] * 4 + [((count, 4 * width), BF) for count in (z.sel, z.mid, z.far)],
+        [((rows, width), BF)] * 4
+        + [((z.sel, 4 * width), BF)]
+        + [((z.mid, 2 * width), BF)] * 2
+        + [((z.far, 4 * width), BF)],
         2 * rows * width * 4 * width,
         scratch=[
             pltpu.SMEM(offsets.shape, jnp.int32),
@@ -616,8 +643,10 @@
             pltpu.VMEM(w_qkv.shape, BF),
             pltpu.VMEM(cotangent.shape, BF),
             pltpu.VMEM(w_out.shape, BF),
-            pltpu.SemaphoreType.DMA((4 * LOAD_CUTS + 3,)),
-        ],
+        ]
+        + [pltpu.VMEM((rows, width), BF)] * 4
+        + [pltpu.SemaphoreType.DMA((4 * LOAD_CUTS + 3,)), pltpu.SemaphoreType.DMA((4,))],
+        hbm_outs=4,
         spaces=pltpu.HBM,
         vmem=PROJECT_VMEM_BYTES,
     )(offsets, tiles, w_qkv, cotangent, w_out)
@@ -625,7 +654,7 @@
     far_up = far
     for step in upper_steps(n):
         far_up = jnp.concatenate(step_parts(far_up, step, n), axis=0)
-    mid_parts = step_parts(mid, PLANE, n)
+    mid_parts = step_parts(mid_kv, PLANE, n)
     mixed, near_stats, turned, turned_out = call(
         functools.partial(near_kernel, z),
         [
@@ -639,11 +668,12 @@
     )(pad_count, after(q, far_up), k, v, g, tiles, order, order_q)
     mid_0 = jnp.concatenate(mid_parts, axis=0)
     mid_1 = swap(mid_0, 1, n)
-    far_parts = step_parts(far_up, PLANE, n, (near_stats,))
-    far_0 = jnp.concatenate([part[:, : 2 * width] for part in far_parts], axis=0)
+    far_0 = jnp.concatenate(
+        step_parts(far_up[:, : 2 * width], PLANE, n, (near_stats,)), axis=0
+    )
     far_1 = swap(far_0, 1, n)
-    far_qg_0 = jnp.concatenate([part[:, 2 * width :] for part in far_parts], axis=0)
-    far_qg_1 = swap(far_qg_0, 1, n)
+    qg = jnp.concatenate([mid_qg, far_up[:, 2 * width :]], axis=0)
+    qg_parts = step_parts(after(qg, far_0), PLANE, n)
 
     stats, picked, raw, held = call(
         functools.partial(join_kernel, z),
@@ -660,9 +690,17 @@
         smem=1,
     )(offsets, near_stats, stats, picked, raw, mixed, held, tiles, w_out, order_out)
     attn_other = swap(attn_turned_out, 1, n)
+    (dq_sel,) = call(
+        functools.partial(own_grads_kernel, z),
+        [((z.sel, width), F32)],
+        2 * base_flops,
+        smem=2,
+    )(offsets, pad_count, sel, mid_0, mid_1, far_0, far_1, after(picked, attn_turned))
     turned_other = swap(after(turned_out, picked), 1, n)
     cot_other = swap(after(cotangent, picked), 1, n)
 
+    qg_0 = jnp.concatenate(tied(qg_parts, (out_rows,)), axis=0)
+    qg_1 = swap(qg_0, 1, n)
     stats_up = picked[z.mid : z.mid + z.far]
     for i, step in enumerate(upper_steps(n)):
         parts = step_parts(stats_up, step, n, (out_rows,) if i == 0 else ())
@@ -677,13 +715,10 @@
         functools.partial(near_grads_kernel, z),
         [((rows, width), BF), ((rows, width), F32), ((rows, width), F32)],
         8 * base_flops,
-        scratch=[pltpu.VMEM((z.sel, width), F32)],
         smem=2,
-    )(
-        offsets, pad_count, after(q, wout_half), k, v, g, stats, sel, mid_0, mid_1, far_0, far_1, picked
-    )
+    )(offsets, pad_count, after(q, wout_half), k, v, g, stats, dq_sel)
     dq_other = swap(dq, 1, n)
-    stats_plane = doubled(jnp.concatenate([picked[: z.mid], stats_up], axis=1), (2, 4), n, (dk_near,))
+    stats_plane = doubled(jnp.concatenate([picked[: z.mid], stats_up], axis=1), (2, 4), n, ((dq_sel,), (dk_near,)))
     stats_0 = jnp.concatenate([stats_plane[:, :LANES], stats_plane[:, LANES:]], axis=0)
     stats_1 = swap(stats_0, 1, n)
     early_half = weights(z.half, turned, turned_other, dq, dq_other)
@@ -694,7 +729,7 @@
         3 * base_flops,
         smem=2,
     )(
-        offsets, pad_count, sel, mid_0, mid_1, far_qg_0, far_qg_1, stats_0, stats_1,
+        offsets, pad_count, sel, qg_0, qg_1, stats_0, stats_1,
         after(dk_near, early_half), dv_near,
     )
     dk_other = swap(dk, 1, n)
@@ -707,10 +742,10 @@
     (grad_tiles,) = call(
         functools.partial(tiles_kernel, z), [((rows, width), BF)], 6 * rows * width * width
     )(after(dq, late_half), dk, dv, w_qkv)
-    late = reduce_step(late_half, PLANE, n, BF)
-    early = halved(early_half, masks + [2, 4], n, ((grad_tiles,),))
-    grad_wout = halved(wout_half, [2, 4] + masks, n, ((dq,), (dk,), (grad_tiles,)))
-    late = reduce_all(late, upper_steps(n)[::-1], n)
+    late_parts = block_parts(late_half, PLANE, n)
+    early = halved(early_half, masks + [2, 4], n, ((late_parts[1],),))
+    grad_wout = halved(wout_half, [2, 4] + masks, n, ((dq,), (dk,), (late_parts[1],)))
+    late = reduce_all(sum_parts(late_parts, BF), upper_steps(n)[::-1], n)
     grad_wqkv = jnp.concatenate([early, late], axis=1)
     return out_rows, grad_tiles, grad_wqkv, grad_wout
 

time: 104 us -> 99.3 us (0.955)
  waiting for transfers between devices: 35.7 us -> 29.3 us
  starting transfers between devices: 37.7 us -> 39.1 us
    ppermute x38 -> x41, waiting for transfers between devices: 35.7 us -> 29.3 us  [swap(): return lax.ppermute(value, 'ctx', [(d, d ^ mask) for d in range(dev_count)])]
    ppermute x38 -> x41, starting transfers between devices: 37.7 us -> 39.1 us  [swap(): return lax.ppermute(value, 'ctx', [(d, d ^ mask) for d in range(dev_count)])]
    pallas_call x10 -> x11, Pallas kernels: 23.9 us -> 24.8 us  [run(): pl.pallas_call(kernel, out_shape=tuple((jax.ShapeDtypeStruct(s, t) for s,...]
    unnamed x40 -> x49, local copies, waits for them, and re-layouts: 2.15 us -> 1.7 us
  transfers between devices with their start and end apart: 38 -> 41, of which waited for: 15 -> 13; matrix products, arithmetic and copies ran while one was open for 3% -> 2% of each run, Pallas kernels for 16% -> 19%
where the time goes in v5:
time: 99.3 us; the launch traced here: 99.1 us
  starting transfers between devices  39.1 us (39%)
  waiting for transfers between devices  29.3 us (30%)
  Pallas kernels  24.8 us (25%)
  local copies, waits for them, and re-layouts  2 us (2%)
  other arithmetic  1.97 us (2%)
  between operations  1.95 us (2%)
    ppermute x41, starting transfers between devices, swap(): return lax.ppermute(value, 'ctx', [(d, d ^ mask) for d in range(dev_count)])  39.1 us
    ppermute x41, waiting for transfers between devices, swap(): return lax.ppermute(value, 'ctx', [(d, d ^ mask) for d in range(dev_count)])  29.3 us
    pallas_call x11, Pallas kernels, run(): pl.pallas_call(kernel, out_shape=tuple((jax.ShapeDtypeStruct(s, t) for s,...  24.8 us
  transfers between devices with their start and end apart: 41, of which 13 were waited for; matrix products, arithmetic and copies ran while one was open for 2% of the time, Pallas kernels for 19%

profile of v5, /device:TPU:0, one launch (start us, length us, event | category | flops | bytes accessed | tf_op | source)
XLA Modules:
  0.0 99.1 jit_solution(10059003180637448967)
XLA Ops:
  0.7 5.6 %shard_map.147 = (bf16[256,768]{1,0:T(8,128)(2,1)}, bf16[256,768]{1,0:T(8,128)(2,1)}, bf16[256,768]{1,0:T(8,128)(2,1)}, bf16[256,768]{1,0:T(8,128)(2,1)}, bf16[6...) custom-call(s32[2,12]{1,0:T(2,128)} %offs_ref.9, ...), custom_call_target="tpu_custom_call" | custom-call | flops 1207959552 | bytes 7716960 | tf_op jit(solution)/shard_map/pallas_call | solution.py:534
  6.2 3.1 %collective-permute-start = (bf16[8,3072]{1,0:T(8,128)(2,1)}, bf16[8,3072]{1,0:T(8,128)(2,1)S(1)}, u32[]{:S(2)}, u32[]{:S(2)}) collective-permute-start(bf16[8,3072]{1,0:T(8,128)(2,1)} %get-tuple-element.62), channel_id=1, source_target_pairs={{0,8},{1,9},{2,10},{3,11},{4,12},{5,13},{6,14},{7,15},{8,0},{9,1},... | collective-permute-start | bytes 147464 | tf_op jit(solution)/shard_map/ppermute | solution.py:553
  9.3 2.6 %collective-permute-start.1 = (bf16[8,3072]{1,0:T(8,128)(2,1)}, bf16[8,3072]{1,0:T(8,128)(2,1)S(1)}, u32[]{:S(2)}, u32[]{:S(2)}) collective-permute-start(bf16[8,3072]{1,0:T(8,128)(2,1)} %get-tuple-element.62), channel_id=1, source_target_pairs={{0,16},{1,17},{2,18},{3,19},{4,20},{5,21},{6,22},{7,23},{8,24},{9,... | collective-permute-start | bytes 147464 | tf_op jit(solution)/shard_map/ppermute | solution.py:553
  11.9 1.7 %collective-permute-start.3 = (bf16[32,1536]{1,0:T(8,128)(2,1)}, bf16[32,1536]{1,0:T(8,128)(2,1)S(1)}, u32[]{:S(2)}, u32[]{:S(2)}) collective-permute-start(bf16[32,1536]{1,0:T(8,128)(2,1)} %get-tuple-element.69), channel_id=1, source_target_pairs={{0,2},{1,3},{2,0},{3,1},{4,6},{5,7},{6,4},{7,5},{8,10},{9,11},{10,... | collective-permute-start | bytes 294920 | tf_op jit(solution)/shard_map/ppermute | solution.py:553
  13.6 1.5 %collective-permute-start.4 = (bf16[32,1536]{1,0:T(8,128)(2,1)}, bf16[32,1536]{1,0:T(8,128)(2,1)S(1)}, u32[]{:S(2)}, u32[]{:S(2)}) collective-permute-start(bf16[32,1536]{1,0:T(8,128)(2,1)} %get-tuple-element.69), channel_id=1, source_target_pairs={{0,4},{1,5},{2,6},{3,7},{4,0},{5,1},{6,2},{7,3},{8,12},{9,13},{10,... | collective-permute-start | bytes 294920 | tf_op jit(solution)/shard_map/ppermute | solution.py:553
  15.2 0.8 constant_dynamic-update-slice_fusion.3
  16.2 0.7 copy-done.14
  18.1 1.7 %collective-permute-start.7 = (bf16[32,1536]{1,0:T(8,128)(2,1)S(1)}, bf16[32,1536]{1,0:T(8,128)(2,1)S(1)}, u32[]{:S(2)}, u32[]{:S(2)}) collective-permute-start(bf16[32,1536]{1,0:T(8,128)(2,1)S(1)} %get-tuple-element.70), channel_id=1, source_target_pairs={{0,2},{1,3},{2,0},{3,1},{4,6},{5,7},{6,4},{7,5},{8,10},{9,11},{10,... | collective-permute-start | bytes 294920 | tf_op jit(solution)/shard_map/ppermute | solution.py:553
  19.7 1.5 %collective-permute-start.8 = (bf16[32,1536]{1,0:T(8,128)(2,1)S(1)}, bf16[32,1536]{1,0:T(8,128)(2,1)S(1)}, u32[]{:S(2)}, u32[]{:S(2)}) collective-permute-start(bf16[32,1536]{1,0:T(8,128)(2,1)S(1)} %get-tuple-element.70), channel_id=1, source_target_pairs={{0,4},{1,5},{2,6},{3,7},{4,0},{5,1},{6,2},{7,3},{8,12},{9,13},{10,... | collective-permute-start | bytes 294920 | tf_op jit(solution)/shard_map/ppermute | solution.py:553
  21.3 2.5 %shard_map.148 = (f32[256,768]{1,0:T(8,128)S(1)}, f32[256,128]{1,0:T(8,128)S(1)}, bf16[768,256]{1,0:T(8,128)(2,1)S(1)}, bf16[768,256]{1,0:T(8,128)(2,1)S(1)}) custom-call(s32[1]{0:T(128)S(6)} %copy.36.pad_ref, bf16[256,768]{1,0:T(8,128)(2,1)S(1)} %copy-done.6, bf16[256,768]{1,0:T(8,128)(2,1)S(1)} %copy-done.7, bf16[256,768]{1,0:T(8,128)(2,1)S(1)} %copy-done.8, ...), custom_call_target="tpu_custom_call" | custom-call | flops 805306368 | bytes 3676164 | tf_op jit(solution)/shard_map/pallas_call | solution.py:534
  24.5 5.0 %collective-permute-done.9 = bf16[32,1536]{1,0:T(8,128)(2,1)S(1)} collective-permute-done((bf16[32,1536]{1,0:T(8,128)(2,1)S(1)}, bf16[32,1536]{1,0:T(8,128)(2,1)S(1)}, u32[]{:S(2)}, u32[]{:S(2)}) %collective-permute-start.9) | collective-permute-done | bytes 98336 | tf_op jit(solution)/shard_map/ppermute | solution.py:553
  29.6 0.6 collective-permute-start.17
  30.6 2.6 %collective-permute-start.19 = (bf16[64,1536]{1,0:T(8,128)(2,1)S(1)}, bf16[64,1536]{1,0:T(8,128)(2,1)S(1)}, u32[]{:S(2)}, u32[]{:S(2)}) collective-permute-start(bf16[64,1536]{1,0:T(8,128)(2,1)S(1)} %pad_maximum_fusion.1), channel_id=1, source_target_pairs={{0,6},{1,7},{2,4},{3,5},{4,2},{5,3},{6,0},{7,1},{8,14},{9,15},{10,... | collective-permute-start | bytes 589832 | tf_op jit(solution)/shard_map/ppermute | solution.py:553
  33.2 2.3 %shard_map.149 = (f32[256,128]{1,0:T(8,128)S(1)}, f32[64,128]{1,0:T(8,128)S(1)}, f32[64,128]{1,0:T(8,128)S(1)}, f32[64,768]{1,0:T(8,128)S(1)}) custom-call(s32[2,12]{1,0:T(2,128)S(1)} %copy-done.5, s32[1]{0:T(128)S(6)} %copy.36.pad_ref, bf16[64,3072]{1,0:T(8,128)(2,1)S(1)} %copy-done.1, bf16[128,1536]{1,0:T(8,128)(2,1)S(1)} %constant_dynamic-update-slice_fusion.4.mid_0, ...), custom_call_target="tpu_custom_call" | custom-call | flops 301989888 | bytes 2490468 | tf_op jit(solution)/shard_map/pallas_call | solution.py:534
  35.5 0.7 collective-permute-start.13
  36.2 3.5 %collective-permute-start.14 = (f32[8,128]{1,0:T(8,128)S(1)}, f32[8,128]{1,0:T(8,128)S(1)}, u32[]{:S(2)}, u32[]{:S(2)}) collective-permute-start(f32[8,128]{1,0:T(8,128)S(1)} %slice.91), channel_id=1, source_target_pairs={{0,16},{1,17},{2,18},{3,19},{4,20},{5,21},{6,22},{7,23},{8,24},{9,... | collective-permute-start | bytes 12296 | tf_op jit(solution)/shard_map/ppermute | solution.py:553
  39.7 2.5 %shard_map.150 = (bf16[256,768]{1,0:T(8,128)(2,1)}, bf16[384,256]{1,0:T(8,128)(2,1)S(1)}, bf16[384,256]{1,0:T(8,128)(2,1)S(1)}) custom-call(s32[2,12]{1,0:T(2,128)S(1)} %copy-done.5, f32[256,128]{1,0:T(8,128)S(1)} %get-tuple-element.67.near_stats, f32[256,128]{1,0:T(8,128)S(1)} %get-tuple-element.74.stats, f32[64,128]{1,0:T(8,128)S(1)} %get-tuple-element.89.picked, ...), custom_call_target="tpu_custom_call" | custom-call | flops 905969664 | bytes 3673184 | tf_op jit(solution)/shard_map/pallas_call | solution.py:534
  43.2 4.4 %collective-permute-done.15 = f32[8,128]{1,0:T(8,128)S(1)} collective-permute-done((f32[8,128]{1,0:T(8,128)S(1)}, f32[8,128]{1,0:T(8,128)S(1)}, u32[]{:S(2)}, u32[]{:S(2)}) %collective-permute-start.15) | collective-permute-done | bytes 4128 | tf_op jit(solution)/shard_map/ppermute | solution.py:553
  47.7 0.6 collective-permute-start.21
  48.4 1.9 %shard_map.152.dq_sel = f32[64,768]{1,0:T(8,128)S(1)} custom-call(s32[2,12]{1,0:T(2,128)S(1)} %copy-done.5, s32[1]{0:T(128)S(6)} %copy.36.pad_ref, bf16[64,3072]{1,0:T(8,128)(2,1)S(1)} %copy-done.1, bf16[128,1536]{1,0:T(8,128)(2,1)S(1)} %constant_dynamic-update-slice_fusion.4.mid_0, bf16[128,1536]{1,0:T(8,128)(2,1)S(1)} %collective-permute-done.6.mid_1, ...), custom_call_target="tpu_custom_call" | custom-call | flops 201326592 | bytes 2195556 | tf_op jit(solution)/shard_map/pallas_call | solution.py:534
  50.2 1.4 %collective-permute-done.21 = f32[32,256]{1,0:T(8,128)S(1)} collective-permute-done((f32[32,256]{1,0:T(8,128)S(1)}, f32[32,256]{1,0:T(8,128)S(1)}, u32[]{:S(2)}, u32[]{:S(2)}) %collective-permute-start.21) | collective-permute-done | bytes 32800 | tf_op jit(solution)/shard_map/ppermute | solution.py:553
  51.7 0.6 collective-permute-start.22
  52.8 0.6 collective-permute-start.37
  53.4 4.1 %shard_map.153 = (bf16[256,768]{1,0:T(8,128)(2,1)S(1)}, f32[256,768]{1,0:T(8,128)S(1)}, f32[256,768]{1,0:T(8,128)S(1)}) custom-call(s32[2,12]{1,0:T(2,128)S(1)} %copy-done.5, s32[1]{0:T(128)S(6)} %copy.36.pad_ref, bf16[256,768]{1,0:T(8,128)(2,1)S(1)} %copy-done.6, bf16[256,768]{1,0:T(8,128)(2,1)S(1)} %copy-done.7, bf16[256,768]{1,0:T(8,128)(2,1)S(1)} %copy-done.8, ...), custom_call_target="tpu_custom_call" | custom-call | flops 805306368 | bytes 3866724 | tf_op jit(solution)/shard_map/pallas_call | solution.py:534
  57.6 0.5 collective-permute-start.23
  58.2 2.4 %collective-permute-done.37 = bf16[192,768]{1,0:T(8,128)(2,1)S(1)} collective-permute-done((bf16[192,768]{1,0:T(8,128)(2,1)S(1)}, bf16[192,768]{1,0:T(8,128)(2,1)S(1)}, u32[]{:S(2)}, u32[]{:S(2)}) %collective-permute-start.37) | collective-permute-done | bytes 294944 | tf_op jit(solution)/shard_map/ppermute | solution.py:553
  60.7 1.6 %collective-permute-start.38 = (bf16[96,768]{1,0:T(8,128)(2,1)S(1)}, bf16[96,768]{1,0:T(8,128)(2,1)S(1)}, u32[]{:S(2)}, u32[]{:S(2)}) collective-permute-start(bf16[96,768]{1,0:T(8,128)(2,1)S(1)} %get-tuple-element.128), channel_id=1, source_target_pairs={{0,4},{1,5},{2,6},{3,7},{4,0},{5,1},{6,2},{7,3},{8,12},{9,13},{10,... | collective-permute-start | bytes 442376 | tf_op jit(solution)/shard_map/ppermute | solution.py:553
  62.8 2.4 %shard_map.155 = (bf16[256,768]{1,0:T(8,128)(2,1)S(1)}, bf16[256,768]{1,0:T(8,128)(2,1)S(1)}) custom-call(s32[2,12]{1,0:T(2,128)S(1)} %copy-done.5, s32[1]{0:T(128)S(6)} %copy.36.pad_ref, bf16[64,3072]{1,0:T(8,128)(2,1)S(1)} %copy-done.1, bf16[256,1536]{1,0:T(8,128)(2,1)S(1)} %constant_dynamic-update-slice_fusion.16.qg_0, ...), custom_call_target="tpu_custom_call" | custom-call | flops 301989888 | bytes 4587620 | tf_op jit(solution)/shard_map/pallas_call | solution.py:534
  65.9 1.0 %collective-permute-done.25.dk_other = bf16[256,768]{1,0:T(8,128)(2,1)S(1)} collective-permute-done((bf16[256,768]{1,0:T(8,128)(2,1)S(1)}, bf16[256,768]{1,0:T(8,128)(2,1)S(1)}, u32[]{:S(2)}, u32[]{:S(2)}) %collective-permute-start.25) | collective-permute-done | bytes 393248 | tf_op jit(solution)/shard_map/ppermute | solution.py:553
  66.9 0.6 collective-permute-done.26.dv_other
  67.5 0.8 shard_map.156
  68.4 1.5 %collective-permute-start.28 = (bf16[96,1536]{1,0:T(8,128)(2,1)S(1)}, bf16[96,1536]{1,0:T(8,128)(2,1)S(1)}, u32[]{:S(2)}, u32[]{:S(2)}) collective-permute-start(bf16[96,1536]{1,0:T(8,128)(2,1)S(1)} %get-tuple-element.118), channel_id=1, source_target_pairs={{0,2},{1,3},{2,0},{3,1},{4,6},{5,7},{6,4},{7,5},{8,10},{9,11},{10,... | collective-permute-start | bytes 884744 | tf_op jit(solution)/shard_map/ppermute | solution.py:553
  69.9 0.5 collective-permute-start.39
  70.4 0.5 collective-permute-start.32
  71.0 1.5 %collective-permute-start.33 = (bf16[96,1536]{1,0:T(8,128)(2,1)S(1)}, bf16[96,1536]{1,0:T(8,128)(2,1)S(1)}, u32[]{:S(2)}, u32[]{:S(2)}) collective-permute-start(bf16[96,1536]{1,0:T(8,128)(2,1)S(1)} %get-tuple-element.119), channel_id=1, source_target_pairs={{0,6},{1,7},{2,4},{3,5},{4,2},{5,3},{6,0},{7,1},{8,14},{9,15},{10,... | collective-permute-start | bytes 884744 | tf_op jit(solution)/shard_map/ppermute | solution.py:553
  72.4 1.9 %shard_map.157 = bf16[256,768]{1,0:T(8,128)(2,1)} custom-call(bf16[256,768]{1,0:T(8,128)(2,1)S(1)} %get-tuple-element.109.right.dq, bf16[256,768]{1,0:T(8,128)(2,1)S(1)} %get-tuple-element.107.dk, bf16[256,768]{1,0:T(8,128)(2,1)S(1)} %get-tuple-element.108.dv, bf16[768,2304]{1,0:T(8,128)(2,1)S(1)} %copy-done), custom_call_target="tpu_custom_call" | custom-call | flops 905969664 | bytes 5111808 | tf_op jit(solution)/shard_map/pallas_call | solution.py:534
  74.3 2.1 %collective-permute-done.39 = bf16[48,768]{1,0:T(8,128)(2,1)S(1)} collective-permute-done((bf16[48,768]{1,0:T(8,128)(2,1)S(1)}, bf16[48,768]{1,0:T(8,128)(2,1)S(1)}, u32[]{:S(2)}, u32[]{:S(2)}) %collective-permute-start.39) | collective-permute-done | bytes 73760 | tf_op jit(solution)/shard_map/ppermute | solution.py:553
  76.4 1.9 %collective-permute-done.28 = bf16[96,1536]{1,0:T(8,128)(2,1)S(1)} collective-permute-done((bf16[96,1536]{1,0:T(8,128)(2,1)S(1)}, bf16[96,1536]{1,0:T(8,128)(2,1)S(1)}, u32[]{:S(2)}, u32[]{:S(2)}) %collective-permute-start.28) | collective-permute-done | bytes 294944 | tf_op jit(solution)/shard_map/ppermute | solution.py:553
  78.5 3.0 %collective-permute-start.29 = (bf16[96,768]{1,0:T(8,128)(2,1)S(1)}, bf16[96,768]{1,0:T(8,128)(2,1)S(1)}, u32[]{:S(2)}, u32[]{:S(2)}) collective-permute-start(bf16[96,768]{1,0:T(8,128)(2,1)S(1)} %slice.128), channel_id=1, source_target_pairs={{0,16},{1,17},{2,18},{3,19},{4,20},{5,21},{6,22},{7,23},{8,24},{9,... | collective-permute-start | bytes 442376 | tf_op jit(solution)/shard_map/ppermute | solution.py:553
  81.5 3.7 %collective-permute-done.32 = bf16[96,1536]{1,0:T(8,128)(2,1)S(1)} collective-permute-done((bf16[96,1536]{1,0:T(8,128)(2,1)S(1)}, bf16[96,1536]{1,0:T(8,128)(2,1)S(1)}, u32[]{:S(2)}, u32[]{:S(2)}) %collective-permute-start.32) | collective-permute-done | bytes 294944 | tf_op jit(solution)/shard_map/ppermute | solution.py:553
  85.3 1.7 %collective-permute-start.34 = (bf16[24,1536]{1,0:T(8,128)(2,1)S(1)}, bf16[24,1536]{1,0:T(8,128)(2,1)S(1)}, u32[]{:S(2)}, u32[]{:S(2)}) collective-permute-start(bf16[24,1536]{1,0:T(8,128)(2,1)S(1)} %get-tuple-element.130), channel_id=1, source_target_pairs={{0,8},{1,9},{2,10},{3,11},{4,12},{5,13},{6,14},{7,15},{8,0},{9,1},... | collective-permute-start | bytes 221192 | tf_op jit(solution)/shard_map/ppermute | solution.py:553
  87.1 2.7 %collective-permute-start.36 = (bf16[24,1536]{1,0:T(8,128)(2,1)S(1)}, bf16[24,1536]{1,0:T(8,128)(2,1)S(1)}, u32[]{:S(2)}, u32[]{:S(2)}) collective-permute-start(bf16[24,1536]{1,0:T(8,128)(2,1)S(1)} %get-tuple-element.131), channel_id=1, source_target_pairs={{0,24},{1,25},{2,26},{3,27},{4,28},{5,29},{6,30},{7,31},{8,16},{9,... | collective-permute-start | bytes 221192 | tf_op jit(solution)/shard_map/ppermute | solution.py:553
  89.9 0.6 collective-permute-start.30
  90.5 0.6 convert_add_fusion.1
  91.1 3.2 %collective-permute-done.30 = bf16[48,768]{1,0:T(8,128)(2,1)S(1)} collective-permute-done((bf16[48,768]{1,0:T(8,128)(2,1)S(1)}, bf16[48,768]{1,0:T(8,128)(2,1)S(1)}, u32[]{:S(2)}, u32[]{:S(2)}) %collective-permute-start.30) | collective-permute-done | bytes 73760 | tf_op jit(solution)/shard_map/ppermute | solution.py:553
  94.3 0.6 collective-permute-start.31
  95.0 3.4 %collective-permute-done.31 = bf16[24,768]{1,0:T(8,128)(2,1)S(1)} collective-permute-done((bf16[24,768]{1,0:T(8,128)(2,1)S(1)}, bf16[24,768]{1,0:T(8,128)(2,1)S(1)}, u32[]{:S(2)}, u32[]{:S(2)}) %collective-permute-start.31) | collective-permute-done | bytes 36896 | tf_op jit(solution)/shard_map/ppermute | solution.py:553
  98.4 0.7 pad_maximum_fusion
  (130 shorter events, 5.4 us)
Async XLA Ops:
  0.6 15.3 %copy-start.10 = (s32[768,1]{1,0:T(8,128)S(1)}, s32[768,1]{1,0:T(8,128)}, u32[]{:S(2)}) copy-start(s32[768,1]{1,0:T(8,128)} %constant.14.clone) | copy-start | bytes 9220
  0.6 15.3 %copy-start.11 = (s32[768,1]{1,0:T(8,128)S(1)}, s32[768,1]{1,0:T(8,128)}, u32[]{:S(2)}) copy-start(s32[768,1]{1,0:T(8,128)} %constant.15.clone) | copy-start | bytes 9220
  0.7 15.3 %copy-start.12 = (s32[768,1]{1,0:T(8,128)S(1)}, s32[768,1]{1,0:T(8,128)}, u32[]{:S(2)}) copy-start(s32[768,1]{1,0:T(8,128)} %constant.16.clone) | copy-start | bytes 9220
  0.7 15.3 %copy-start.13 = (s32[768,1]{1,0:T(8,128)S(1)}, s32[768,1]{1,0:T(8,128)}, u32[]{:S(2)}) copy-start(s32[768,1]{1,0:T(8,128)} %constant.17.clone) | copy-start | bytes 9220
  6.2 11.3 %collective-permute-start = (bf16[8,3072]{1,0:T(8,128)(2,1)}, bf16[8,3072]{1,0:T(8,128)(2,1)S(1)}, u32[]{:S(2)}, u32[]{:S(2)}) collective-permute-start(bf16[8,3072]{1,0:T(8,128)(2,1)} %get-tuple-element.62), channel_id=1, source_target_pairs={{0,8},{1,9},{2,10},{3,11},{4,12},{5,13},{6,14},{7,15},{8,0},{9,1},... | collective-permute-start | bytes 147464 | tf_op jit(solution)/shard_map/ppermute | solution.py:553
  9.3 8.6 %collective-permute-start.1 = (bf16[8,3072]{1,0:T(8,128)(2,1)}, bf16[8,3072]{1,0:T(8,128)(2,1)S(1)}, u32[]{:S(2)}, u32[]{:S(2)}) collective-permute-start(bf16[8,3072]{1,0:T(8,128)(2,1)} %get-tuple-element.62), channel_id=1, source_target_pairs={{0,16},{1,17},{2,18},{3,19},{4,20},{5,21},{6,22},{7,23},{8,24},{9,... | collective-permute-start | bytes 147464 | tf_op jit(solution)/shard_map/ppermute | solution.py:553
  11.9 6.1 %collective-permute-start.2 = (bf16[8,3072]{1,0:T(8,128)(2,1)}, bf16[8,3072]{1,0:T(8,128)(2,1)S(1)}, u32[]{:S(2)}, u32[]{:S(2)}) collective-permute-start(bf16[8,3072]{1,0:T(8,128)(2,1)} %get-tuple-element.62), channel_id=1, source_target_pairs={{0,24},{1,25},{2,26},{3,27},{4,28},{5,29},{6,30},{7,31},{8,16},{9,... | collective-permute-start | bytes 147464 | tf_op jit(solution)/shard_map/ppermute | solution.py:553
  11.9 11.9 %collective-permute-start.3 = (bf16[32,1536]{1,0:T(8,128)(2,1)}, bf16[32,1536]{1,0:T(8,128)(2,1)S(1)}, u32[]{:S(2)}, u32[]{:S(2)}) collective-permute-start(bf16[32,1536]{1,0:T(8,128)(2,1)} %get-tuple-element.69), channel_id=1, source_target_pairs={{0,2},{1,3},{2,0},{3,1},{4,6},{5,7},{6,4},{7,5},{8,10},{9,11},{10,... | collective-permute-start | bytes 294920 | tf_op jit(solution)/shard_map/ppermute | solution.py:553
  13.6 10.6 %collective-permute-start.4 = (bf16[32,1536]{1,0:T(8,128)(2,1)}, bf16[32,1536]{1,0:T(8,128)(2,1)S(1)}, u32[]{:S(2)}, u32[]{:S(2)}) collective-permute-start(bf16[32,1536]{1,0:T(8,128)(2,1)} %get-tuple-element.69), channel_id=1, source_target_pairs={{0,4},{1,5},{2,6},{3,7},{4,0},{5,1},{6,2},{7,3},{8,12},{9,13},{10,... | collective-permute-start | bytes 294920 | tf_op jit(solution)/shard_map/ppermute | solution.py:553
  17.6 6.8 %collective-permute-start.5 = (bf16[32,1536]{1,0:T(8,128)(2,1)S(1)}, bf16[32,1536]{1,0:T(8,128)(2,1)S(1)}, u32[]{:S(2)}, u32[]{:S(2)}) collective-permute-start(bf16[32,1536]{1,0:T(8,128)(2,1)S(1)} %copy-done.14), channel_id=1, source_target_pairs={{0,6},{1,7},{2,4},{3,5},{4,2},{5,3},{6,0},{7,1},{8,14},{9,15},{10,... | collective-permute-start | bytes 294920 | tf_op jit(solution)/shard_map/ppermute | solution.py:553
  18.1 6.4 %collective-permute-start.7 = (bf16[32,1536]{1,0:T(8,128)(2,1)S(1)}, bf16[32,1536]{1,0:T(8,128)(2,1)S(1)}, u32[]{:S(2)}, u32[]{:S(2)}) collective-permute-start(bf16[32,1536]{1,0:T(8,128)(2,1)S(1)} %get-tuple-element.70), channel_id=1, source_target_pairs={{0,2},{1,3},{2,0},{3,1},{4,6},{5,7},{6,4},{7,5},{8,10},{9,11},{10,... | collective-permute-start | bytes 294920 | tf_op jit(solution)/shard_map/ppermute | solution.py:553
  19.7 4.7 %collective-permute-start.8 = (bf16[32,1536]{1,0:T(8,128)(2,1)S(1)}, bf16[32,1536]{1,0:T(8,128)(2,1)S(1)}, u32[]{:S(2)}, u32[]{:S(2)}) collective-permute-start(bf16[32,1536]{1,0:T(8,128)(2,1)S(1)} %get-tuple-element.70), channel_id=1, source_target_pairs={{0,4},{1,5},{2,6},{3,7},{4,0},{5,1},{6,2},{7,3},{8,12},{9,13},{10,... | collective-permute-start | bytes 294920 | tf_op jit(solution)/shard_map/ppermute | solution.py:553
  23.8 9.4 %copy-start.1 = (bf16[64,3072]{1,0:T(8,128)(2,1)S(1)}, bf16[64,3072]{1,0:T(8,128)(2,1)}, u32[]{:S(2)}) copy-start(bf16[64,3072]{1,0:T(8,128)(2,1)} %get-tuple-element.68.sel) | copy-start | bytes 1179652
  23.8 9.4 %copy-start.5 = (s32[2,12]{1,0:T(2,128)S(1)}, s32[2,12]{1,0:T(2,128)}, u32[]{:S(2)}) copy-start(s32[2,12]{1,0:T(2,128)} %offs_ref.9) | copy-start | bytes 292
  23.8 5.6 %collective-permute-start.9 = (bf16[32,1536]{1,0:T(8,128)(2,1)S(1)}, bf16[32,1536]{1,0:T(8,128)(2,1)S(1)}, u32[]{:S(2)}, u32[]{:S(2)}) collective-permute-start(bf16[32,1536]{1,0:T(8,128)(2,1)S(1)} %get-tuple-element.70), channel_id=1, source_target_pairs={{0,6},{1,7},{2,4},{3,5},{4,2},{5,3},{6,0},{7,1},{8,14},{9,15},{10,... | collective-permute-start | bytes 294920 | tf_op jit(solution)/shard_map/ppermute | solution.py:553
  24.3 8.8 %collective-permute-start.6 = (bf16[128,1536]{1,0:T(8,128)(2,1)S(1)}, bf16[128,1536]{1,0:T(8,128)(2,1)S(1)}, u32[]{:S(2)}, u32[]{:S(2)}) collective-permute-start(bf16[128,1536]{1,0:T(8,128)(2,1)S(1)} %constant_dynamic-update-slice_fusion.4.mid_0), channel_id=1, source_target_pairs={{0,1},{1,0},{2,3},{3,2},{4,5},{5,4},{6,7},{7,6},{8,9},{9,8},{10,11... | collective-permute-start | bytes 1179656 | tf_op jit(solution)/shard_map/ppermute | solution.py:553
  29.5 3.7 %collective-permute-start.10 = (bf16[128,1536]{1,0:T(8,128)(2,1)S(1)}, bf16[128,1536]{1,0:T(8,128)(2,1)S(1)}, u32[]{:S(2)}, u32[]{:S(2)}) collective-permute-start(bf16[128,1536]{1,0:T(8,128)(2,1)S(1)} %constant_dynamic-update-slice_fusion.8.far_0), channel_id=1, source_target_pairs={{0,1},{1,0},{2,3},{3,2},{4,5},{5,4},{6,7},{7,6},{8,9},{9,8},{10,11... | collective-permute-start | bytes 1179656 | tf_op jit(solution)/shard_map/ppermute | solution.py:553
  29.6 10.1 %copy-start.2 = (bf16[768,768]{1,0:T(8,128)(2,1)S(1)}, bf16[768,768]{1,0:T(8,128)(2,1)}, u32[]{:S(2)}) copy-start(bf16[768,768]{1,0:T(8,128)(2,1)} %w_out.1) | copy-start | bytes 3538948
  29.6 12.6 %collective-permute-start.17 = (bf16[64,1536]{1,0:T(8,128)(2,1)S(1)}, bf16[64,1536]{1,0:T(8,128)(2,1)S(1)}, u32[]{:S(2)}, u32[]{:S(2)}) collective-permute-start(bf16[64,1536]{1,0:T(8,128)(2,1)S(1)} %pad_maximum_fusion.1), channel_id=1, source_target_pairs={{0,2},{1,3},{2,0},{3,1},{4,6},{5,7},{6,4},{7,5},{8,10},{9,11},{10,... | collective-permute-start | bytes 589832 | tf_op jit(solution)/shard_map/ppermute | solution.py:553
  30.2 12.3 %collective-permute-start.18 = (bf16[64,1536]{1,0:T(8,128)(2,1)S(1)}, bf16[64,1536]{1,0:T(8,128)(2,1)S(1)}, u32[]{:S(2)}, u32[]{:S(2)}) collective-permute-start(bf16[64,1536]{1,0:T(8,128)(2,1)S(1)} %pad_maximum_fusion.1), channel_id=1, source_target_pairs={{0,4},{1,5},{2,6},{3,7},{4,0},{5,1},{6,2},{7,3},{8,12},{9,13},{10,... | collective-permute-start | bytes 589832 | tf_op jit(solution)/shard_map/ppermute | solution.py:553
  30.6 11.9 %collective-permute-start.19 = (bf16[64,1536]{1,0:T(8,128)(2,1)S(1)}, bf16[64,1536]{1,0:T(8,128)(2,1)S(1)}, u32[]{:S(2)}, u32[]{:S(2)}) collective-permute-start(bf16[64,1536]{1,0:T(8,128)(2,1)S(1)} %pad_maximum_fusion.1), channel_id=1, source_target_pairs={{0,6},{1,7},{2,4},{3,5},{4,2},{5,3},{6,0},{7,1},{8,14},{9,15},{10,... | collective-permute-start | bytes 589832 | tf_op jit(solution)/shard_map/ppermute | solution.py:553
  35.5 7.6 %collective-permute-start.13 = (f32[8,128]{1,0:T(8,128)S(1)}, f32[8,128]{1,0:T(8,128)S(1)}, u32[]{:S(2)}, u32[]{:S(2)}) collective-permute-start(f32[8,128]{1,0:T(8,128)S(1)} %slice.91), channel_id=1, source_target_pairs={{0,8},{1,9},{2,10},{3,11},{4,12},{5,13},{6,14},{7,15},{8,0},{9,1},... | collective-permute-start | bytes 12296 | tf_op jit(solution)/shard_map/ppermute | solution.py:553
  36.2 7.0 %collective-permute-start.14 = (f32[8,128]{1,0:T(8,128)S(1)}, f32[8,128]{1,0:T(8,128)S(1)}, u32[]{:S(2)}, u32[]{:S(2)}) collective-permute-start(f32[8,128]{1,0:T(8,128)S(1)} %slice.91), channel_id=1, source_target_pairs={{0,16},{1,17},{2,18},{3,19},{4,20},{5,21},{6,22},{7,23},{8,24},{9,... | collective-permute-start | bytes 12296 | tf_op jit(solution)/shard_map/ppermute | solution.py:553
  42.2 5.4 %collective-permute-start.15 = (f32[8,128]{1,0:T(8,128)S(1)}, f32[8,128]{1,0:T(8,128)S(1)}, u32[]{:S(2)}, u32[]{:S(2)}) collective-permute-start(f32[8,128]{1,0:T(8,128)S(1)} %slice.91), channel_id=1, source_target_pairs={{0,24},{1,25},{2,26},{3,27},{4,28},{5,29},{6,30},{7,31},{8,16},{9,... | collective-permute-start | bytes 12296 | tf_op jit(solution)/shard_map/ppermute | solution.py:553
  42.5 9.8 %collective-permute-start.12 = (bf16[256,768]{1,0:T(8,128)(2,1)S(1)}, bf16[256,768]{1,0:T(8,128)(2,1)S(1)}, u32[]{:S(2)}, u32[]{:S(2)}) collective-permute-start(bf16[256,768]{1,0:T(8,128)(2,1)S(1)} %copy-done.4), channel_id=1, source_target_pairs={{0,1},{1,0},{2,3},{3,2},{4,5},{5,4},{6,7},{7,6},{8,9},{9,8},{10,11... | collective-permute-start | bytes 1179656 | tf_op jit(solution)/shard_map/ppermute | solution.py:553
  42.5 9.8 %collective-permute-start.11 = (bf16[384,256]{1,0:T(8,128)(2,1)S(1)}, bf16[384,256]{1,0:T(8,128)(2,1)S(1)}, u32[]{:S(2)}, u32[]{:S(2)}) collective-permute-start(bf16[384,256]{1,0:T(8,128)(2,1)S(1)} %get-tuple-element.81), channel_id=1, source_target_pairs={{0,1},{1,0},{2,3},{3,2},{4,5},{5,4},{6,7},{7,6},{8,9},{9,8},{10,11... | collective-permute-start | bytes 589832 | tf_op jit(solution)/shard_map/ppermute | solution.py:553
  43.1 19.2 %collective-permute-start.16 = (bf16[768,256]{1,0:T(8,128)(2,1)S(1)}, bf16[768,256]{1,0:T(8,128)(2,1)S(1)}, u32[]{:S(2)}, u32[]{:S(2)}) collective-permute-start(bf16[768,256]{1,0:T(8,128)(2,1)S(1)} %get-tuple-element.93), channel_id=1, source_target_pairs={{0,1},{1,0},{2,3},{3,2},{4,5},{5,4},{6,7},{7,6},{8,9},{9,8},{10,11... | collective-permute-start | bytes 1179656 | tf_op jit(solution)/shard_map/ppermute | solution.py:553
  47.7 4.0 %collective-permute-start.21 = (f32[32,256]{1,0:T(8,128)S(1)}, f32[32,256]{1,0:T(8,128)S(1)}, u32[]{:S(2)}, u32[]{:S(2)}) collective-permute-start(f32[32,256]{1,0:T(8,128)S(1)} %pad_maximum_fusion.3), channel_id=1, source_target_pairs={{0,2},{1,3},{2,0},{3,1},{4,6},{5,7},{6,4},{7,5},{8,10},{9,11},{10,... | collective-permute-start | bytes 98312 | tf_op jit(solution)/shard_map/ppermute | solution.py:553
  48.3 14.5 %collective-permute-start.20 = (bf16[256,1536]{1,0:T(8,128)(2,1)S(1)}, bf16[256,1536]{1,0:T(8,128)(2,1)S(1)}, u32[]{:S(2)}, u32[]{:S(2)}) collective-permute-start(bf16[256,1536]{1,0:T(8,128)(2,1)S(1)} %constant_dynamic-update-slice_fusion.16.qg_0), channel_id=1, source_target_pairs={{0,1},{1,0},{2,3},{3,2},{4,5},{5,4},{6,7},{7,6},{8,9},{9,8},{10,11... | collective-permute-start | bytes 2359304 | tf_op jit(solution)/shard_map/ppermute | solution.py:553
  51.7 5.9 %collective-permute-start.22 = (f32[64,256]{1,0:T(8,128)S(1)}, f32[64,256]{1,0:T(8,128)S(1)}, u32[]{:S(2)}, u32[]{:S(2)}) collective-permute-start(f32[64,256]{1,0:T(8,128)S(1)} %constant_dynamic-update-slice_fusion.20), channel_id=1, source_target_pairs={{0,4},{1,5},{2,6},{3,7},{4,0},{5,1},{6,2},{7,3},{8,12},{9,13},{10,... | collective-permute-start | bytes 196616 | tf_op jit(solution)/shard_map/ppermute | solution.py:553
  52.8 7.8 %collective-permute-start.37 = (bf16[192,768]{1,0:T(8,128)(2,1)S(1)}, bf16[192,768]{1,0:T(8,128)(2,1)S(1)}, u32[]{:S(2)}, u32[]{:S(2)}) collective-permute-start(bf16[192,768]{1,0:T(8,128)(2,1)S(1)} %get-tuple-element.121), channel_id=1, source_target_pairs={{0,2},{1,3},{2,0},{3,1},{4,6},{5,7},{6,4},{7,5},{8,10},{9,11},{10,... | collective-permute-start | bytes 884744 | tf_op jit(solution)/shard_map/ppermute | solution.py:553
  57.5 4.8 %collective-permute-start.24 = (bf16[256,768]{1,0:T(8,128)(2,1)S(1)}, bf16[256,768]{1,0:T(8,128)(2,1)S(1)}, u32[]{:S(2)}, u32[]{:S(2)}) collective-permute-start(bf16[256,768]{1,0:T(8,128)(2,1)S(1)} %get-tuple-element.109.right.dq), channel_id=1, source_target_pairs={{0,1},{1,0},{2,3},{3,2},{4,5},{5,4},{6,7},{7,6},{8,9},{9,8},{10,11... | collective-permute-start | bytes 1179656 | tf_op jit(solution)/shard_map/ppermute | solution.py:553
  57.6 5.2 %collective-permute-start.23 = (f32[256,128]{1,0:T(8,128)S(1)}, f32[256,128]{1,0:T(8,128)S(1)}, u32[]{:S(2)}, u32[]{:S(2)}) collective-permute-start(f32[256,128]{1,0:T(8,128)S(1)} %pad_maximum_fusion.2.stats_0), channel_id=1, source_target_pairs={{0,1},{1,0},{2,3},{3,2},{4,5},{5,4},{6,7},{7,6},{8,9},{9,8},{10,11... | collective-permute-start | bytes 393224 | tf_op jit(solution)/shard_map/ppermute | solution.py:553
  60.7 5.2 %collective-permute-start.38 = (bf16[96,768]{1,0:T(8,128)(2,1)S(1)}, bf16[96,768]{1,0:T(8,128)(2,1)S(1)}, u32[]{:S(2)}, u32[]{:S(2)}) collective-permute-start(bf16[96,768]{1,0:T(8,128)(2,1)S(1)} %get-tuple-element.128), channel_id=1, source_target_pairs={{0,4},{1,5},{2,6},{3,7},{4,0},{5,1},{6,2},{7,3},{8,12},{9,13},{10,... | collective-permute-start | bytes 442376 | tf_op jit(solution)/shard_map/ppermute | solution.py:553
  65.2 1.8 %collective-permute-start.25 = (bf16[256,768]{1,0:T(8,128)(2,1)S(1)}, bf16[256,768]{1,0:T(8,128)(2,1)S(1)}, u32[]{:S(2)}, u32[]{:S(2)}) collective-permute-start(bf16[256,768]{1,0:T(8,128)(2,1)S(1)} %get-tuple-element.107.dk), channel_id=1, source_target_pairs={{0,1},{1,0},{2,3},{3,2},{4,5},{5,4},{6,7},{7,6},{8,9},{9,8},{10,11... | collective-permute-start | bytes 1179656 | tf_op jit(solution)/shard_map/ppermute | solution.py:553
  65.2 2.3 %collective-permute-start.26 = (bf16[256,768]{1,0:T(8,128)(2,1)S(1)}, bf16[256,768]{1,0:T(8,128)(2,1)S(1)}, u32[]{:S(2)}, u32[]{:S(2)}) collective-permute-start(bf16[256,768]{1,0:T(8,128)(2,1)S(1)} %get-tuple-element.108.dv), channel_id=1, source_target_pairs={{0,1},{1,0},{2,3},{3,2},{4,5},{5,4},{6,7},{7,6},{8,9},{9,8},{10,11... | collective-permute-start | bytes 1179656 | tf_op jit(solution)/shard_map/ppermute | solution.py:553
  65.8 12.6 %collective-permute-start.27 = (bf16[192,768]{1,0:T(8,128)(2,1)S(1)}, bf16[192,768]{1,0:T(8,128)(2,1)S(1)}, u32[]{:S(2)}, u32[]{:S(2)}) collective-permute-start(bf16[192,768]{1,0:T(8,128)(2,1)S(1)} %get-tuple-element.123), channel_id=1, source_target_pairs={{0,8},{1,9},{2,10},{3,11},{4,12},{5,13},{6,14},{7,15},{8,0},{9,1},... | collective-permute-start | bytes 884744 | tf_op jit(solution)/shard_map/ppermute | solution.py:553
  68.4 9.9 %collective-permute-start.28 = (bf16[96,1536]{1,0:T(8,128)(2,1)S(1)}, bf16[96,1536]{1,0:T(8,128)(2,1)S(1)}, u32[]{:S(2)}, u32[]{:S(2)}) collective-permute-start(bf16[96,1536]{1,0:T(8,128)(2,1)S(1)} %get-tuple-element.118), channel_id=1, source_target_pairs={{0,2},{1,3},{2,0},{3,1},{4,6},{5,7},{6,4},{7,5},{8,10},{9,11},{10,... | collective-permute-start | bytes 884744 | tf_op jit(solution)/shard_map/ppermute | solution.py:553
  69.9 6.5 %collective-permute-start.39 = (bf16[48,768]{1,0:T(8,128)(2,1)S(1)}, bf16[48,768]{1,0:T(8,128)(2,1)S(1)}, u32[]{:S(2)}, u32[]{:S(2)}) collective-permute-start(bf16[48,768]{1,0:T(8,128)(2,1)S(1)} %get-tuple-element.135), channel_id=1, source_target_pairs={{0,8},{1,9},{2,10},{3,11},{4,12},{5,13},{6,14},{7,15},{8,0},{9,1},... | collective-permute-start | bytes 221192 | tf_op jit(solution)/shard_map/ppermute | solution.py:553
  70.4 14.7 %collective-permute-start.32 = (bf16[96,1536]{1,0:T(8,128)(2,1)S(1)}, bf16[96,1536]{1,0:T(8,128)(2,1)S(1)}, u32[]{:S(2)}, u32[]{:S(2)}) collective-permute-start(bf16[96,1536]{1,0:T(8,128)(2,1)S(1)} %get-tuple-element.120), channel_id=1, source_target_pairs={{0,4},{1,5},{2,6},{3,7},{4,0},{5,1},{6,2},{7,3},{8,12},{9,13},{10,... | collective-permute-start | bytes 884744 | tf_op jit(solution)/shard_map/ppermute | solution.py:553
  71.0 14.2 %collective-permute-start.33 = (bf16[96,1536]{1,0:T(8,128)(2,1)S(1)}, bf16[96,1536]{1,0:T(8,128)(2,1)S(1)}, u32[]{:S(2)}, u32[]{:S(2)}) collective-permute-start(bf16[96,1536]{1,0:T(8,128)(2,1)S(1)} %get-tuple-element.119), channel_id=1, source_target_pairs={{0,6},{1,7},{2,4},{3,5},{4,2},{5,3},{6,0},{7,1},{8,14},{9,15},{10,... | collective-permute-start | bytes 884744 | tf_op jit(solution)/shard_map/ppermute | solution.py:553
  78.3 12.1 %collective-permute-start.40 = (bf16[24,768]{1,0:T(8,128)(2,1)S(1)}, bf16[24,768]{1,0:T(8,128)(2,1)S(1)}, u32[]{:S(2)}, u32[]{:S(2)}) collective-permute-start(bf16[24,768]{1,0:T(8,128)(2,1)S(1)} %slice.147), channel_id=1, source_target_pairs={{0,16},{1,17},{2,18},{3,19},{4,20},{5,21},{6,22},{7,23},{8,24},{9,... | collective-permute-start | bytes 110600 | tf_op jit(solution)/shard_map/ppermute | solution.py:553
  78.5 11.3 %collective-permute-start.29 = (bf16[96,768]{1,0:T(8,128)(2,1)S(1)}, bf16[96,768]{1,0:T(8,128)(2,1)S(1)}, u32[]{:S(2)}, u32[]{:S(2)}) collective-permute-start(bf16[96,768]{1,0:T(8,128)(2,1)S(1)} %slice.128), channel_id=1, source_target_pairs={{0,16},{1,17},{2,18},{3,19},{4,20},{5,21},{6,22},{7,23},{8,24},{9,... | collective-permute-start | bytes 442376 | tf_op jit(solution)/shard_map/ppermute | solution.py:553
  85.3 9.6 %collective-permute-start.34 = (bf16[24,1536]{1,0:T(8,128)(2,1)S(1)}, bf16[24,1536]{1,0:T(8,128)(2,1)S(1)}, u32[]{:S(2)}, u32[]{:S(2)}) collective-permute-start(bf16[24,1536]{1,0:T(8,128)(2,1)S(1)} %get-tuple-element.130), channel_id=1, source_target_pairs={{0,8},{1,9},{2,10},{3,11},{4,12},{5,13},{6,14},{7,15},{8,0},{9,1},... | collective-permute-start | bytes 221192 | tf_op jit(solution)/shard_map/ppermute | solution.py:553
  87.1 7.8 %collective-permute-start.35 = (bf16[24,1536]{1,0:T(8,128)(2,1)S(1)}, bf16[24,1536]{1,0:T(8,128)(2,1)S(1)}, u32[]{:S(2)}, u32[]{:S(2)}) collective-permute-start(bf16[24,1536]{1,0:T(8,128)(2,1)S(1)} %get-tuple-element.132), channel_id=1, source_target_pairs={{0,16},{1,17},{2,18},{3,19},{4,20},{5,21},{6,22},{7,23},{8,24},{9,... | collective-permute-start | bytes 221192 | tf_op jit(solution)/shard_map/ppermute | solution.py:553
  87.1 7.8 %collective-permute-start.36 = (bf16[24,1536]{1,0:T(8,128)(2,1)S(1)}, bf16[24,1536]{1,0:T(8,128)(2,1)S(1)}, u32[]{:S(2)}, u32[]{:S(2)}) collective-permute-start(bf16[24,1536]{1,0:T(8,128)(2,1)S(1)} %get-tuple-element.131), channel_id=1, source_target_pairs={{0,24},{1,25},{2,26},{3,27},{4,28},{5,29},{6,30},{7,31},{8,16},{9,... | collective-permute-start | bytes 221192 | tf_op jit(solution)/shard_map/ppermute | solution.py:553
  89.9 4.4 %collective-permute-start.30 = (bf16[48,768]{1,0:T(8,128)(2,1)S(1)}, bf16[48,768]{1,0:T(8,128)(2,1)S(1)}, u32[]{:S(2)}, u32[]{:S(2)}) collective-permute-start(bf16[48,768]{1,0:T(8,128)(2,1)S(1)} %slice.130), channel_id=1, source_target_pairs={{0,2},{1,3},{2,0},{3,1},{4,6},{5,7},{6,4},{7,5},{8,10},{9,11},{10,... | collective-permute-start | bytes 221192 | tf_op jit(solution)/shard_map/ppermute | solution.py:553
  94.3 4.0 %collective-permute-start.31 = (bf16[24,768]{1,0:T(8,128)(2,1)S(1)}, bf16[24,768]{1,0:T(8,128)(2,1)S(1)}, u32[]{:S(2)}, u32[]{:S(2)}) collective-permute-start(bf16[24,768]{1,0:T(8,128)(2,1)S(1)} %slice.132), channel_id=1, source_target_pairs={{0,4},{1,5},{2,6},{3,7},{4,0},{5,1},{6,2},{7,3},{8,12},{9,13},{10,... | collective-permute-start | bytes 110600 | tf_op jit(solution)/shard_map/ppermute | solution.py:553
  (9 other events, 40.5 us)

commit v6 on v5

--- a/solution.py
+++ b/solution.py
@@ -20,6 +20,7 @@
 NN = (((1,), (0,)), ((), ()))
 TN = (((0,), (0,)), ((), ()))
 LARGE = 1e30
+COST = 0.05
 LOAD_CUTS = 4
 VMEM_BYTES = 40 * 1024 * 1024
 PROJECT_VMEM_BYTES = 57 * 1024 * 1024
@@ -507,11 +508,13 @@
     out[...] = (dot(left[rows, :], right[...]) + dot(left_other[rows, :], right_other[...])).astype(BF)
 
 
-def late_weights_kernel(z, turned, turned_other, dk, dv, dk_other, dv_other, out):
-    width = z.width
+def late_weights_kernel(z, turned, turned_other, dk, dv, dk_other, dv_other, *blocks):
     left, other = turned[: z.half, :], turned_other[: z.half, :]
-    out[:, :width] = (dot(left, dk[...]) + dot(other, dk_other[...])).astype(BF)
-    out[:, width:] = (dot(left, dv[...]) + dot(other, dv_other[...])).astype(BF)
+    size = z.half // len(blocks)
+    for part, (own, far) in enumerate(((dk, dk_other), (dv, dv_other))):
+        result = (dot(left, own[...]) + dot(other, far[...])).astype(BF)
+        for i, block in enumerate(blocks):
+            block[part * size : (part + 1) * size, :] = result[i * size : (i + 1) * size]
 
 
 def tiles_kernel(z, dq, dk, dv, w_qkv, out):
@@ -542,7 +545,7 @@
             scratch_shapes=list(scratch),
             compiler_params=pltpu.CompilerParams(vmem_limit_bytes=vmem),
             cost_estimate=pl.CostEstimate(
-                flops=int(flops), bytes_accessed=int(moved), transcendentals=0
+                flops=int(flops * COST), bytes_accessed=int(moved * COST), transcendentals=0
             ),
         )(*args)
 
@@ -574,14 +577,6 @@
     return tied([value] + [swap(value, base * i, dev_count) for i in range(1, count)], first)
 
 
-def block_parts(value, step, dev_count):
-    base, count = step
-    size = value.shape[0] // count
-    return [value[:size]] + [
-        swap(value[i * size : (i + 1) * size], base * i, dev_count) for i in range(1, count)
-    ]
-
-
 def sum_parts(parts, dtype):
     return sum(part.astype(F32) for part in parts).astype(dtype)
 
@@ -593,19 +588,11 @@
     return value
 
 
-def halved(value, masks, dev_count, firsts=()):
-    for i, mask in enumerate(masks):
+def halved(value, masks, dev_count, firsts, dtype):
+    for mask, first in zip(masks, firsts):
         size = value.shape[0] // 2
-        first = firsts[i] if i < len(firsts) else ()
         parts = tied([value[:size], swap(value[size:], mask, dev_count)], first)
-        value = parts[0].astype(F32) + parts[1].astype(F32)
-        value = value if i == len(masks) - 1 else value.astype(BF)
-    return value
-
-
-def reduce_all(value, steps, dev_count):
-    for i, step in enumerate(steps):
-        value = sum_parts(block_parts(value, step, dev_count), F32 if i == len(steps) - 1 else BF)
+        value = sum_parts(parts, dtype)
     return value
 
 
@@ -626,9 +613,13 @@
     rows, width = z.rows, z.width
     masks = [mask for mask in (2**i for i in range(30)) if GROUP <= mask < n]
     order = strip_order(z, own, [1, 4, 2] + masks[::-1])
-    order_q = strip_order(z, own, [1] + masks + [2, 4])
-    order_out = strip_order(z, own, [1, 2, 4] + masks)
+    order_q = strip_order(z, own, [1] + masks[:-1] + [4, 2] + masks[-1:])
+    order_out = strip_order(z, own, [1, 2, 4] + masks[::-1])
     base_flops = 2 * rows * rows * width
+
+    def weights(start, *args):
+        kernel = functools.partial(weights_kernel, start)
+        return call(kernel, [((z.half, width), BF)], 4 * rows * width * width)(*args)[0]
 
     q, k, v, g, sel, mid_kv, mid_qg, far = call(
         functools.partial(project_kernel, z),
@@ -665,11 +656,11 @@
         ],
         8 * base_flops,
         smem=1,
-    )(pad_count, after(q, far_up), k, v, g, tiles, order, order_q)
+    )(pad_count, after(q, far_up, *mid_parts[1:3]), k, v, g, tiles, order, order_q)
     mid_0 = jnp.concatenate(mid_parts, axis=0)
     mid_1 = swap(mid_0, 1, n)
     far_0 = jnp.concatenate(
-        step_parts(far_up[:, : 2 * width], PLANE, n, (near_stats,)), axis=0
+        step_parts(after(far_up[:, : 2 * width], *mid_parts[1:3]), PLANE, n, (near_stats,)), axis=0
     )
     far_1 = swap(far_0, 1, n)
     qg = jnp.concatenate([mid_qg, far_up[:, 2 * width :]], axis=0)
@@ -682,46 +673,45 @@
         smem=2,
     )(offsets, pad_count, sel, mid_0, mid_1, far_0, far_1, near_stats)
 
+    (dq_sel,) = call(
+        functools.partial(own_grads_kernel, z),
+        [((z.sel, width), F32)],
+        2 * base_flops,
+        smem=2,
+    )(offsets, pad_count, sel, mid_0, mid_1, far_0, far_1, picked)
+    stats_up = doubled(picked[z.mid : z.mid + z.far], masks[:1], n, ((dq_sel,),))
+    dq, dk_near, dv_near = call(
+        functools.partial(near_grads_kernel, z),
+        [((rows, width), BF), ((rows, width), F32), ((rows, width), F32)],
+        8 * base_flops,
+        smem=2,
+    )(offsets, pad_count, after(q, stats_up), k, v, g, stats, dq_sel)
+    turned_other = swap(after(turned_out, dk_near), 1, n)
+    cot_other = swap(after(cotangent, dk_near), 1, n)
+    dq_other = swap(dq, 1, n)
+
+    qg_0 = jnp.concatenate(tied(qg_parts, (dk_near,)), axis=0)
+    qg_1 = swap(qg_0, 1, n)
+    stats_up = doubled(stats_up, masks[1:], n, ((dk_near,),))
     out_rows, attn_turned, attn_turned_out = call(
         functools.partial(output_kernel, z),
         [((rows, width), BF), ((z.half, rows), BF), ((z.half, rows), BF)],
         6 * rows * width * width,
         scratch=[pltpu.VMEM((rows, width), BF)],
         smem=1,
-    )(offsets, near_stats, stats, picked, raw, mixed, held, tiles, w_out, order_out)
+    )(offsets, near_stats, stats, after(picked, stats_up), raw, mixed, held, tiles, w_out, order_out)
     attn_other = swap(attn_turned_out, 1, n)
-    (dq_sel,) = call(
-        functools.partial(own_grads_kernel, z),
-        [((z.sel, width), F32)],
-        2 * base_flops,
-        smem=2,
-    )(offsets, pad_count, sel, mid_0, mid_1, far_0, far_1, after(picked, attn_turned))
-    turned_other = swap(after(turned_out, picked), 1, n)
-    cot_other = swap(after(cotangent, picked), 1, n)
-
-    qg_0 = jnp.concatenate(tied(qg_parts, (out_rows,)), axis=0)
-    qg_1 = swap(qg_0, 1, n)
-    stats_up = picked[z.mid : z.mid + z.far]
-    for i, step in enumerate(upper_steps(n)):
-        parts = step_parts(stats_up, step, n, (out_rows,) if i == 0 else ())
-        stats_up = jnp.concatenate(parts, axis=0)
-    def weights(start, *args):
-        kernel = functools.partial(weights_kernel, start)
-        return call(kernel, [((z.half, width), BF)], 4 * rows * width * width)(*args)[0]
-
-    wout_half = weights(0, attn_turned, attn_other, cotangent, after(cot_other, stats_up))
-
-    dq, dk_near, dv_near = call(
-        functools.partial(near_grads_kernel, z),
-        [((rows, width), BF), ((rows, width), F32), ((rows, width), F32)],
-        8 * base_flops,
-        smem=2,
-    )(offsets, pad_count, after(q, wout_half), k, v, g, stats, dq_sel)
-    dq_other = swap(dq, 1, n)
-    stats_plane = doubled(jnp.concatenate([picked[: z.mid], stats_up], axis=1), (2, 4), n, ((dq_sel,), (dk_near,)))
+    wout_half = weights(0, attn_turned, attn_other, cotangent, cot_other)
+
+    early_half = weights(z.half, turned, turned_other, dq, dq_other)
+    stats_plane = doubled(
+        jnp.concatenate([picked[: z.mid], stats_up], axis=1),
+        (2, 4),
+        n,
+        ((out_rows,), (wout_half, early_half)),
+    )
     stats_0 = jnp.concatenate([stats_plane[:, :LANES], stats_plane[:, LANES:]], axis=0)
     stats_1 = swap(stats_0, 1, n)
-    early_half = weights(z.half, turned, turned_other, dq, dq_other)
 
     dk, dv = call(
         functools.partial(key_grads_kernel, z),
@@ -734,19 +724,51 @@
     )
     dk_other = swap(dk, 1, n)
     dv_other = swap(dv, 1, n)
-    (late_half,) = call(
+    count = PLANE[1]
+    block = z.half // count
+    late = call(
         functools.partial(late_weights_kernel, z),
-        [((z.half, 2 * width), BF)],
+        [((2 * block, width), BF)] * count,
         4 * rows * width * width,
     )(turned, turned_other, dk, dv, dk_other, dv_other)
     (grad_tiles,) = call(
         functools.partial(tiles_kernel, z), [((rows, width), BF)], 6 * rows * width * width
-    )(after(dq, late_half), dk, dv, w_qkv)
-    late_parts = block_parts(late_half, PLANE, n)
-    early = halved(early_half, masks + [2, 4], n, ((late_parts[1],),))
-    grad_wout = halved(wout_half, [2, 4] + masks, n, ((dq,), (dk,), (late_parts[1],)))
-    late = reduce_all(sum_parts(late_parts, BF), upper_steps(n)[::-1], n)
-    grad_wqkv = jnp.concatenate([early, late], axis=1)
+    )(after(dq, late[0]), dk, dv, w_qkv)
+
+    wout = halved(wout_half, [2], n, ((dk,),), BF)
+    wq = halved(early_half, masks[:-1], n, ((dk,),) * len(masks[:-1]), BF)
+    sums = [[late[0][:block]], [late[0][block:]], [wout[:block]], [wq[: wq.shape[0] // count]]]
+    for i in range(1, count):
+        parts = [late[i], wq[i * wq.shape[0] // count : (i + 1) * wq.shape[0] // count]]
+        if PLANE[0] * i == 4:
+            parts.append(wout[block:])
+        got = swap(jnp.concatenate(parts, axis=0), PLANE[0] * i, n)
+        sums[0].append(got[:block])
+        sums[1].append(got[block : 2 * block])
+        rest = 2 * block + parts[1].shape[0]
+        sums[3].append(got[2 * block : rest])
+        if PLANE[0] * i == 4:
+            sums[2].append(got[rest:])
+    steps = upper_steps(n)[::-1]
+    for at, (base, count) in enumerate(steps):
+        held = [sum_parts(parts, BF) for parts in sums]
+        size = held[0].shape[0] // count
+        last = at == len(steps) - 1
+        sums = [[array[:size]] for array in held[:3]] + [held[3:]]
+        meets_top = held[3].shape[0] > z.strip
+        if meets_top:
+            sums[3] = [held[3][: z.strip]]
+        for i in range(1, count):
+            parts = [array[i * size : (i + 1) * size] for array in held[:3]]
+            if meets_top and base * i == masks[-1]:
+                parts.append(held[3][z.strip :])
+            got = swap(jnp.concatenate(parts, axis=0), base * i, n)
+            for k in range(3):
+                sums[k].append(got[k * size : (k + 1) * size])
+            if len(parts) == 4:
+                sums[3].append(got[3 * size :])
+    grad_k, grad_v, grad_wout, grad_q = [sum_parts(parts, F32) for parts in sums]
+    grad_wqkv = jnp.concatenate([grad_q, grad_k, grad_v], axis=1)
     return out_rows, grad_tiles, grad_wqkv, grad_wout
 
 

time: 99.3 us -> 108 us (1.088)
  local copies, waits for them, and re-layouts: 2 us -> 9.75 us
  waiting for transfers between devices: 29.3 us -> 34.7 us
  starting transfers between devices: 39.1 us -> 34.2 us
    unnamed x49 -> x46, local copies, waits for them, and re-layouts: 1.7 us -> 7.17 us
    ppermute x41 -> x34, waiting for transfers between devices: 29.3 us -> 34.7 us  [swap(): return lax.ppermute(value, 'ctx', [(d, d ^ mask) for d in range(dev_count)])]
    ppermute x41 -> x34, starting transfers between devices: 39.1 us -> 34.2 us  [swap(): return lax.ppermute(value, 'ctx', [(d, d ^ mask) for d in range(dev_count)])]
    concatenate x1, local copies, waits for them, and re-layouts: 0.01 us -> 1.42 us  [per_device(): far_up = jnp.concatenate(step_parts(far_up, step, n), axis=0)]
  transfers between devices with their start and end apart: 41 -> 34, of which waited for: 13 -> 11; matrix products, arithmetic and copies ran while one was open for 2% -> 9% of each run, Pallas kernels for 19% -> 15%
where the time goes in v6:
time: 108 us; the launch traced here: 107 us
  waiting for transfers between devices  34.7 us (32%)
  starting transfers between devices  34.2 us (32%)
  Pallas kernels  24.7 us (23%)
  local copies, waits for them, and re-layouts  9.75 us (9%)
  other arithmetic  2.04 us (2%)
  between operations  1.92 us (2%)
    ppermute x34, waiting for transfers between devices, swap(): return lax.ppermute(value, 'ctx', [(d, d ^ mask) for d in range(dev_count)])  34.7 us
    ppermute x34, starting transfers between devices, swap(): return lax.ppermute(value, 'ctx', [(d, d ^ mask) for d in range(dev_count)])  34.2 us
    pallas_call x11, Pallas kernels, run(): pl.pallas_call(kernel, out_shape=tuple((jax.ShapeDtypeStruct(s, t) for s,...  24.7 us
    unnamed x46, local copies, waits for them, and re-layouts  7.17 us
  transfers between devices with their start and end apart: 34, of which 11 were waited for; matrix products, arithmetic and copies ran while one was open for 9% of the time, Pallas kernels for 15%

profile of v6, /device:TPU:0, one launch (start us, length us, event | category | flops | bytes accessed | tf_op | source)
XLA Modules:
  0.0 107.3 jit_solution(17819709270849195819)
XLA Ops:
  0.7 5.6 %shard_map.147 = (bf16[256,768]{1,0:T(8,128)(2,1)}, bf16[256,768]{1,0:T(8,128)(2,1)}, bf16[256,768]{1,0:T(8,128)(2,1)}, bf16[256,768]{1,0:T(8,128)(2,1)}, bf16[6...) custom-call(s32[2,12]{1,0:T(2,128)} %offs_ref.9, ...), custom_call_target="tpu_custom_call" | custom-call | flops 60397976 | bytes 385848 | tf_op jit(solution)/shard_map/pallas_call | solution.py:537
  6.3 3.1 %collective-permute-start = (bf16[8,3072]{1,0:T(8,128)(2,1)}, bf16[8,3072]{1,0:T(8,128)(2,1)}, u32[]{:S(2)}, u32[]{:S(2)}) collective-permute-start(bf16[8,3072]{1,0:T(8,128)(2,1)} %get-tuple-element.62), channel_id=1, source_target_pairs={{0,8},{1,9},{2,10},{3,11},{4,12},{5,13},{6,14},{7,15},{8,0},{9,1},... | collective-permute-start | bytes 147464 | tf_op jit(solution)/shard_map/ppermute | solution.py:556
  9.4 2.6 %collective-permute-start.1 = (bf16[8,3072]{1,0:T(8,128)(2,1)}, bf16[8,3072]{1,0:T(8,128)(2,1)}, u32[]{:S(2)}, u32[]{:S(2)}) collective-permute-start(bf16[8,3072]{1,0:T(8,128)(2,1)} %get-tuple-element.62), channel_id=1, source_target_pairs={{0,16},{1,17},{2,18},{3,19},{4,20},{5,21},{6,22},{7,23},{8,24},{9,... | collective-permute-start | bytes 147464 | tf_op jit(solution)/shard_map/ppermute | solution.py:556
  12.0 1.7 %collective-permute-start.3 = (bf16[32,1536]{1,0:T(8,128)(2,1)}, bf16[32,1536]{1,0:T(8,128)(2,1)}, u32[]{:S(2)}, u32[]{:S(2)}) collective-permute-start(bf16[32,1536]{1,0:T(8,128)(2,1)} %get-tuple-element.63), channel_id=1, source_target_pairs={{0,2},{1,3},{2,0},{3,1},{4,6},{5,7},{6,4},{7,5},{8,10},{9,11},{10,... | collective-permute-start | bytes 294920 | tf_op jit(solution)/shard_map/ppermute | solution.py:556
  13.7 1.5 %collective-permute-start.4 = (bf16[32,1536]{1,0:T(8,128)(2,1)}, bf16[32,1536]{1,0:T(8,128)(2,1)}, u32[]{:S(2)}, u32[]{:S(2)}) collective-permute-start(bf16[32,1536]{1,0:T(8,128)(2,1)} %get-tuple-element.63), channel_id=1, source_target_pairs={{0,4},{1,5},{2,6},{3,7},{4,0},{5,1},{6,2},{7,3},{8,12},{9,13},{10,... | collective-permute-start | bytes 294920 | tf_op jit(solution)/shard_map/ppermute | solution.py:556
  15.2 1.4 %constant_dynamic-update-slice_fusion.3 = bf16[32,3072]{1,0:T(8,128)(2,1)} fusion(bf16[8,3072]{1,0:T(8,128)(2,1)} %get-tuple-element.62), kind=kLoop, calls=%fused_computation.25 | loop fusion | bytes 98304
  16.8 0.9 constant_dynamic-update-slice_fusion.7
  18.8 1.4 %constant_dynamic-update-slice_fusion.2 = bf16[32,3072]{1,0:T(8,128)(2,1)} fusion(bf16[32,3072]{1,0:T(8,128)(2,1)} %constant_dynamic-update-slice_fusion.3, bf16[8,3072]{1,0:T(8,128)(2,1)} %collective-permute-done), kind=kLoop, calls=%fused_computation.24 | loop fusion | bytes 98304
  20.2 1.4 %constant_dynamic-update-slice_fusion.1 = bf16[32,3072]{1,0:T(8,128)(2,1)} fusion(bf16[32,3072]{1,0:T(8,128)(2,1)} %constant_dynamic-update-slice_fusion.2, bf16[8,3072]{1,0:T(8,128)(2,1)} %collective-permute-done.1), kind=kLoop, calls=%fused_computation.23 | loop fusion | bytes 98304
  21.6 1.4 %constant_dynamic-update-slice_fusion = bf16[32,3072]{1,0:T(8,128)(2,1)} fusion(bf16[32,3072]{1,0:T(8,128)(2,1)} %constant_dynamic-update-slice_fusion.1, bf16[8,3072]{1,0:T(8,128)(2,1)} %collective-permute-done.2), kind=kLoop, calls=%fused_computation.22 | loop fusion | bytes 98304 | tf_op jit(solution)/shard_map/concatenate | solution.py:647
  23.0 1.0 fusion.3
  24.0 1.8 %collective-permute-start.7 = (bf16[32,1536]{1,0:T(8,128)(2,1)S(1)}, bf16[32,1536]{1,0:T(8,128)(2,1)S(1)}, u32[]{:S(2)}, u32[]{:S(2)}) collective-permute-start(bf16[32,1536]{1,0:T(8,128)(2,1)S(1)} %get-tuple-element.71), channel_id=1, source_target_pairs={{0,2},{1,3},{2,0},{3,1},{4,6},{5,7},{6,4},{7,5},{8,10},{9,11},{10,... | collective-permute-start | bytes 294920 | tf_op jit(solution)/shard_map/ppermute | solution.py:556
  25.8 1.5 %collective-permute-start.8 = (bf16[32,1536]{1,0:T(8,128)(2,1)S(1)}, bf16[32,1536]{1,0:T(8,128)(2,1)S(1)}, u32[]{:S(2)}, u32[]{:S(2)}) collective-permute-start(bf16[32,1536]{1,0:T(8,128)(2,1)S(1)} %get-tuple-element.71), channel_id=1, source_target_pairs={{0,4},{1,5},{2,6},{3,7},{4,0},{5,1},{6,2},{7,3},{8,12},{9,13},{10,... | collective-permute-start | bytes 294920 | tf_op jit(solution)/shard_map/ppermute | solution.py:556
  27.6 0.9 constant_dynamic-update-slice_fusion.6
  28.5 0.9 constant_dynamic-update-slice_fusion.5
  29.5 2.5 %shard_map.148 = (f32[256,768]{1,0:T(8,128)S(1)}, f32[256,128]{1,0:T(8,128)S(1)}, bf16[768,256]{1,0:T(8,128)(2,1)S(1)}, bf16[768,256]{1,0:T(8,128)(2,1)S(1)}) custom-call(s32[1]{0:T(128)S(6)} %copy.35.pad_ref, bf16[256,768]{1,0:T(8,128)(2,1)S(1)} %copy-done.5, bf16[256,768]{1,0:T(8,128)(2,1)S(1)} %copy-done.6, bf16[256,768]{1,0:T(8,128)(2,1)S(1)} %copy-done.7, ...), custom_call_target="tpu_custom_call" | custom-call | flops 40265320 | bytes 183808 | tf_op jit(solution)/shard_map/pallas_call | solution.py:537
  32.0 0.8 collective-permute-done.9
  33.0 1.7 %collective-permute-done.10.far_1 = bf16[128,1536]{1,0:T(8,128)(2,1)S(1)} collective-permute-done((bf16[128,1536]{1,0:T(8,128)(2,1)S(1)}, bf16[128,1536]{1,0:T(8,128)(2,1)S(1)}, u32[]{:S(2)}, u32[]{:S(2)}) %collective-permute-start.10) | collective-permute-done | bytes 393248 | tf_op jit(solution)/shard_map/ppermute | solution.py:556
  34.7 2.3 %shard_map.149 = (f32[256,128]{1,0:T(8,128)S(1)}, f32[64,128]{1,0:T(8,128)S(1)}, f32[64,128]{1,0:T(8,128)S(1)}, f32[64,768]{1,0:T(8,128)S(1)}) custom-call(s32[2,12]{1,0:T(2,128)S(1)} %copy-done.9, s32[1]{0:T(128)S(6)} %copy.35.pad_ref, bf16[64,3072]{1,0:T(8,128)(2,1)S(1)} %copy-done.2, bf16[128,1536]{1,0:T(8,128)(2,1)S(1)} %constant_dynamic-update-slice_fusion.4.mid_0, ...), custom_call_target="tpu_custom_call" | custom-call | flops 15099494 | bytes 124523 | tf_op jit(solution)/shard_map/pallas_call | solution.py:537
  37.0 0.7 collective-permute-start.11
  37.8 1.1 %collective-permute-start.14 = (bf16[64,1536]{1,0:T(8,128)(2,1)S(1)}, bf16[64,1536]{1,0:T(8,128)(2,1)S(1)}, u32[]{:S(2)}, u32[]{:S(2)}) collective-permute-start(bf16[64,1536]{1,0:T(8,128)(2,1)S(1)} %pad_maximum_fusion.4), channel_id=1, source_target_pairs={{0,2},{1,3},{2,0},{3,1},{4,6},{5,7},{6,4},{7,5},{8,10},{9,11},{10,... | collective-permute-start | bytes 589832 | tf_op jit(solution)/shard_map/ppermute | solution.py:556
  38.9 1.5 %collective-permute-start.15 = (bf16[64,1536]{1,0:T(8,128)(2,1)S(1)}, bf16[64,1536]{1,0:T(8,128)(2,1)S(1)}, u32[]{:S(2)}, u32[]{:S(2)}) collective-permute-start(bf16[64,1536]{1,0:T(8,128)(2,1)S(1)} %pad_maximum_fusion.4), channel_id=1, source_target_pairs={{0,4},{1,5},{2,6},{3,7},{4,0},{5,1},{6,2},{7,3},{8,12},{9,13},{10,... | collective-permute-start | bytes 589832 | tf_op jit(solution)/shard_map/ppermute | solution.py:556
  40.4 0.9 collective-permute-start.16
  41.3 1.9 %shard_map.150.dq_sel = f32[64,768]{1,0:T(8,128)S(1)} custom-call(s32[2,12]{1,0:T(2,128)S(1)} %copy-done.9, s32[1]{0:T(128)S(6)} %copy.35.pad_ref, bf16[64,3072]{1,0:T(8,128)(2,1)S(1)} %copy-done.2, bf16[128,1536]{1,0:T(8,128)(2,1)S(1)} %constant_dynamic-update-slice_fusion.4.mid_0, bf16[128,1536]{1,0:T(8,128)(2,1)S(1)} %collective-permute-done.6.mid_1, ...), custom_call_target="tpu_custom_call" | custom-call | flops 10066329 | bytes 109777 | tf_op jit(solution)/shard_map/pallas_call | solution.py:537
  43.2 3.5 %collective-permute-start.12 = (f32[16,128]{1,0:T(8,128)S(1)}, f32[16,128]{1,0:T(8,128)S(1)}, u32[]{:S(2)}, u32[]{:S(2)}) collective-permute-start(f32[16,128]{1,0:T(8,128)S(1)} %constant_dynamic-update-slice_fusion.12), channel_id=1, source_target_pairs={{0,16},{1,17},{2,18},{3,19},{4,20},{5,21},{6,22},{7,23},{8,24},{9,... | collective-permute-start | bytes 24584 | tf_op jit(solution)/shard_map/ppermute | solution.py:556
  46.8 3.9 %shard_map.151 = (bf16[256,768]{1,0:T(8,128)(2,1)S(1)}, f32[256,768]{1,0:T(8,128)S(1)}, f32[256,768]{1,0:T(8,128)S(1)}) custom-call(s32[2,12]{1,0:T(2,128)S(1)} %copy-done.9, s32[1]{0:T(128)S(6)} %copy.35.pad_ref, bf16[256,768]{1,0:T(8,128)(2,1)S(1)} %copy-done.5, bf16[256,768]{1,0:T(8,128)(2,1)S(1)} %copy-done.6, bf16[256,768]{1,0:T(8,128)(2,1)S(1)} %copy-done.7, ...), custom_call_target="tpu_custom_call" | custom-call | flops 40265320 | bytes 193336 | tf_op jit(solution)/shard_map/pallas_call | solution.py:537
  51.4 1.1 %collective-permute-start.18 = (f32[32,256]{1,0:T(8,128)S(1)}, f32[32,256]{1,0:T(8,128)S(1)}, u32[]{:S(2)}, u32[]{:S(2)}) collective-permute-start(f32[32,256]{1,0:T(8,128)S(1)} %pad_maximum_fusion.9), channel_id=1, source_target_pairs={{0,2},{1,3},{2,0},{3,1},{4,6},{5,7},{6,4},{7,5},{8,10},{9,11},{10,... | collective-permute-start | bytes 98312 | tf_op jit(solution)/shard_map/ppermute | solution.py:556
  52.8 2.7 %shard_map.152 = (bf16[256,768]{1,0:T(8,128)(2,1)}, bf16[384,256]{1,0:T(8,128)(2,1)S(1)}, bf16[384,256]{1,0:T(8,128)(2,1)S(1)}) custom-call(s32[2,12]{1,0:T(2,128)S(1)} %copy-done.9, f32[256,128]{1,0:T(8,128)S(1)} %get-tuple-element.68.near_stats, f32[256,128]{1,0:T(8,128)S(1)} %get-tuple-element.75.stats, f32[64,128]{1,0:T(8,128)S(1)} %get-tuple-element.83.picked, ...), custom_call_target="tpu_custom_call" | custom-call | flops 45298484 | bytes 183659 | tf_op jit(solution)/shard_map/pallas_call | solution.py:537
  55.8 1.6 %collective-permute-start.19 = (f32[64,256]{1,0:T(8,128)S(1)}, f32[64,256]{1,0:T(8,128)S(1)}, u32[]{:S(2)}, u32[]{:S(2)}) collective-permute-start(f32[64,256]{1,0:T(8,128)S(1)} %constant_dynamic-update-slice_fusion.20), channel_id=1, source_target_pairs={{0,4},{1,5},{2,6},{3,7},{4,0},{5,1},{6,2},{7,3},{8,12},{9,13},{10,... | collective-permute-start | bytes 196616 | tf_op jit(solution)/shard_map/ppermute | solution.py:556
  58.5 1.7 %collective-permute-done.19 = f32[64,256]{1,0:T(8,128)S(1)} collective-permute-done((f32[64,256]{1,0:T(8,128)S(1)}, f32[64,256]{1,0:T(8,128)S(1)}, u32[]{:S(2)}, u32[]{:S(2)}) %collective-permute-start.19) | collective-permute-done | bytes 65568 | tf_op jit(solution)/shard_map/ppermute | solution.py:556
  60.2 1.0 collective-permute-start.28
  61.3 1.3 %collective-permute-done.23.stats_1 = f32[256,128]{1,0:T(8,128)S(1)} collective-permute-done((f32[256,128]{1,0:T(8,128)S(1)}, f32[256,128]{1,0:T(8,128)S(1)}, u32[]{:S(2)}, u32[]{:S(2)}) %collective-permute-start.23) | collective-permute-done | bytes 131104 | tf_op jit(solution)/shard_map/ppermute | solution.py:556
  62.6 2.4 %shard_map.155 = (bf16[256,768]{1,0:T(8,128)(2,1)S(1)}, bf16[256,768]{1,0:T(8,128)(2,1)S(1)}) custom-call(s32[2,12]{1,0:T(2,128)S(1)} %copy-done.9, s32[1]{0:T(128)S(6)} %copy.35.pad_ref, bf16[64,3072]{1,0:T(8,128)(2,1)S(1)} %copy-done.2, bf16[256,1536]{1,0:T(8,128)(2,1)S(1)} %constant_dynamic-update-slice_fusion.16.qg_0, ...), custom_call_target="tpu_custom_call" | custom-call | flops 15099494 | bytes 229381 | tf_op jit(solution)/shard_map/pallas_call | solution.py:537
  65.2 2.9 %collective-permute-done.26 = bf16[192,768]{1,0:T(8,128)(2,1)S(1)} collective-permute-done((bf16[192,768]{1,0:T(8,128)(2,1)S(1)}, bf16[192,768]{1,0:T(8,128)(2,1)S(1)}, u32[]{:S(2)}, u32[]{:S(2)}) %collective-permute-start.26) | collective-permute-done | bytes 294944 | tf_op jit(solution)/shard_map/ppermute | solution.py:556
  68.3 1.5 %collective-permute-done.25.dv_other = bf16[256,768]{1,0:T(8,128)(2,1)S(1)} collective-permute-done((bf16[256,768]{1,0:T(8,128)(2,1)S(1)}, bf16[256,768]{1,0:T(8,128)(2,1)S(1)}, u32[]{:S(2)}, u32[]{:S(2)}) %collective-permute-start.25) | collective-permute-done | bytes 393248 | tf_op jit(solution)/shard_map/ppermute | solution.py:556
  69.8 0.8 shard_map.156
  70.7 1.6 %collective-permute-start.29 = (bf16[336,768]{1,0:T(8,128)(2,1)S(1)}, bf16[336,768]{1,0:T(8,128)(2,1)S(1)}, u32[]{:S(2)}, u32[]{:S(2)}) collective-permute-start(bf16[336,768]{1,0:T(8,128)(2,1)S(1)} %pad_maximum_fusion), channel_id=1, source_target_pairs={{0,4},{1,5},{2,6},{3,7},{4,0},{5,1},{6,2},{7,3},{8,12},{9,13},{10,... | collective-permute-start | bytes 1548296 | tf_op jit(solution)/shard_map/ppermute | solution.py:556
  72.3 1.7 %collective-permute-start.27 = (bf16[240,768]{1,0:T(8,128)(2,1)S(1)}, bf16[240,768]{1,0:T(8,128)(2,1)S(1)}, u32[]{:S(2)}, u32[]{:S(2)}) collective-permute-start(bf16[240,768]{1,0:T(8,128)(2,1)S(1)} %pad_maximum_fusion.1), channel_id=1, source_target_pairs={{0,2},{1,3},{2,0},{3,1},{4,6},{5,7},{6,4},{7,5},{8,10},{9,11},{10,... | collective-permute-start | bytes 1105928 | tf_op jit(solution)/shard_map/ppermute | solution.py:556
  74.4 9.4 %collective-permute-done.27 = bf16[240,768]{1,0:T(8,128)(2,1)S(1)} collective-permute-done((bf16[240,768]{1,0:T(8,128)(2,1)S(1)}, bf16[240,768]{1,0:T(8,128)(2,1)S(1)}, u32[]{:S(2)}, u32[]{:S(2)}) %collective-permute-start.27) | collective-permute-done | bytes 368672 | tf_op jit(solution)/shard_map/ppermute | solution.py:556
  83.8 6.8 %collective-permute-done.30 = bf16[240,768]{1,0:T(8,128)(2,1)S(1)} collective-permute-done((bf16[240,768]{1,0:T(8,128)(2,1)S(1)}, bf16[240,768]{1,0:T(8,128)(2,1)S(1)}, u32[]{:S(2)}, u32[]{:S(2)}) %collective-permute-start.30) | collective-permute-done | bytes 368672 | tf_op jit(solution)/shard_map/ppermute | solution.py:556
  90.6 1.8 %collective-permute-done.29 = bf16[336,768]{1,0:T(8,128)(2,1)S(1)} collective-permute-done((bf16[336,768]{1,0:T(8,128)(2,1)S(1)}, bf16[336,768]{1,0:T(8,128)(2,1)S(1)}, u32[]{:S(2)}, u32[]{:S(2)}) %collective-permute-start.29) | collective-permute-done | bytes 516128 | tf_op jit(solution)/shard_map/ppermute | solution.py:556
  93.1 2.3 %collective-permute-start.31 = (bf16[96,768]{1,0:T(8,128)(2,1)S(1)}, bf16[96,768]{1,0:T(8,128)(2,1)S(1)}, u32[]{:S(2)}, u32[]{:S(2)}) collective-permute-start(bf16[96,768]{1,0:T(8,128)(2,1)S(1)} %pad_maximum_fusion.5), channel_id=1, source_target_pairs={{0,16},{1,17},{2,18},{3,19},{4,20},{5,21},{6,22},{7,23},{8,24},{9,... | collective-permute-start | bytes 442376 | tf_op jit(solution)/shard_map/ppermute | solution.py:556
  95.4 2.0 %collective-permute-start.33 = (bf16[72,768]{1,0:T(8,128)(2,1)S(1)}, bf16[72,768]{1,0:T(8,128)(2,1)S(1)}, u32[]{:S(2)}, u32[]{:S(2)}) collective-permute-start(bf16[72,768]{1,0:T(8,128)(2,1)S(1)} %pad_maximum_fusion.8), channel_id=1, source_target_pairs={{0,24},{1,25},{2,26},{3,27},{4,28},{5,29},{6,30},{7,31},{8,16},{9,... | collective-permute-start | bytes 331784 | tf_op jit(solution)/shard_map/ppermute | solution.py:556
  97.3 1.9 %shard_map.157 = bf16[256,768]{1,0:T(8,128)(2,1)} custom-call(bf16[256,768]{1,0:T(8,128)(2,1)S(1)} %get-tuple-element.110.right.dq, bf16[256,768]{1,0:T(8,128)(2,1)S(1)} %get-tuple-element.107.dk, bf16[256,768]{1,0:T(8,128)(2,1)S(1)} %get-tuple-element.108.dv, bf16[768,2304]{1,0:T(8,128)(2,1)S(1)} %copy-done), custom_call_target="tpu_custom_call" | custom-call | flops 45298484 | bytes 255590 | tf_op jit(solution)/shard_map/pallas_call | solution.py:537
  99.2 5.3 %collective-permute-done.33 = bf16[72,768]{1,0:T(8,128)(2,1)S(1)} collective-permute-done((bf16[72,768]{1,0:T(8,128)(2,1)S(1)}, bf16[72,768]{1,0:T(8,128)(2,1)S(1)}, u32[]{:S(2)}, u32[]{:S(2)}) %collective-permute-start.33) | collective-permute-done | bytes 110624 | tf_op jit(solution)/shard_map/ppermute | solution.py:556
  104.5 1.4 %collective-permute-done.31 = bf16[96,768]{1,0:T(8,128)(2,1)S(1)} collective-permute-done((bf16[96,768]{1,0:T(8,128)(2,1)S(1)}, bf16[96,768]{1,0:T(8,128)(2,1)S(1)}, u32[]{:S(2)}, u32[]{:S(2)}) %collective-permute-start.31) | collective-permute-done | bytes 147488 | tf_op jit(solution)/shard_map/ppermute | solution.py:556
  105.9 0.7 convert_add_fusion
  106.6 0.7 pad_maximum_fusion.3
  (112 shorter events, 5.1 us)
Async XLA Ops:
  0.6 16.0 %copy-start.10 = (s32[768,1]{1,0:T(8,128)S(1)}, s32[768,1]{1,0:T(8,128)}, u32[]{:S(2)}) copy-start(s32[768,1]{1,0:T(8,128)} %constant.14.clone) | copy-start | bytes 9220
  0.6 16.0 %copy-start.11 = (s32[768,1]{1,0:T(8,128)S(1)}, s32[768,1]{1,0:T(8,128)}, u32[]{:S(2)}) copy-start(s32[768,1]{1,0:T(8,128)} %constant.15.clone) | copy-start | bytes 9220
  0.7 16.0 %copy-start.12 = (s32[768,1]{1,0:T(8,128)S(1)}, s32[768,1]{1,0:T(8,128)}, u32[]{:S(2)}) copy-start(s32[768,1]{1,0:T(8,128)} %constant.16.clone) | copy-start | bytes 9220
  0.7 16.0 %copy-start.13 = (s32[768,1]{1,0:T(8,128)S(1)}, s32[768,1]{1,0:T(8,128)}, u32[]{:S(2)}) copy-start(s32[768,1]{1,0:T(8,128)} %constant.17.clone) | copy-start | bytes 9220
  6.3 23.2 %copy-start.3 = (bf16[256,768]{1,0:T(8,128)(2,1)S(1)}, bf16[256,768]{1,0:T(8,128)(2,1)}, u32[]{:S(2)}) copy-start(bf16[256,768]{1,0:T(8,128)(2,1)} %tiles.3) | copy-start | bytes 1179652
  6.3 23.2 %copy-start.5 = (bf16[256,768]{1,0:T(8,128)(2,1)S(1)}, bf16[256,768]{1,0:T(8,128)(2,1)}, u32[]{:S(2)}) copy-start(bf16[256,768]{1,0:T(8,128)(2,1)} %get-tuple-element.79.q) | copy-start | bytes 1179652
  6.3 23.2 %copy-start.6 = (bf16[256,768]{1,0:T(8,128)(2,1)S(1)}, bf16[256,768]{1,0:T(8,128)(2,1)}, u32[]{:S(2)}) copy-start(bf16[256,768]{1,0:T(8,128)(2,1)} %get-tuple-element.65.k) | copy-start | bytes 1179652
  6.3 23.2 %copy-start.7 = (bf16[256,768]{1,0:T(8,128)(2,1)S(1)}, bf16[256,768]{1,0:T(8,128)(2,1)}, u32[]{:S(2)}) copy-start(bf16[256,768]{1,0:T(8,128)(2,1)} %get-tuple-element.66.v) | copy-start | bytes 1179652
  6.3 23.2 %copy-start.8 = (bf16[256,768]{1,0:T(8,128)(2,1)S(1)}, bf16[256,768]{1,0:T(8,128)(2,1)}, u32[]{:S(2)}) copy-start(bf16[256,768]{1,0:T(8,128)(2,1)} %get-tuple-element.67.g) | copy-start | bytes 1179652
  6.3 12.1 %collective-permute-start = (bf16[8,3072]{1,0:T(8,128)(2,1)}, bf16[8,3072]{1,0:T(8,128)(2,1)}, u32[]{:S(2)}, u32[]{:S(2)}) collective-permute-start(bf16[8,3072]{1,0:T(8,128)(2,1)} %get-tuple-element.62), channel_id=1, source_target_pairs={{0,8},{1,9},{2,10},{3,11},{4,12},{5,13},{6,14},{7,15},{8,0},{9,1},... | collective-permute-start | bytes 147464 | tf_op jit(solution)/shard_map/ppermute | solution.py:556
  9.4 10.8 %collective-permute-start.1 = (bf16[8,3072]{1,0:T(8,128)(2,1)}, bf16[8,3072]{1,0:T(8,128)(2,1)}, u32[]{:S(2)}, u32[]{:S(2)}) collective-permute-start(bf16[8,3072]{1,0:T(8,128)(2,1)} %get-tuple-element.62), channel_id=1, source_target_pairs={{0,16},{1,17},{2,18},{3,19},{4,20},{5,21},{6,22},{7,23},{8,24},{9,... | collective-permute-start | bytes 147464 | tf_op jit(solution)/shard_map/ppermute | solution.py:556
  12.0 9.6 %collective-permute-start.2 = (bf16[8,3072]{1,0:T(8,128)(2,1)}, bf16[8,3072]{1,0:T(8,128)(2,1)}, u32[]{:S(2)}, u32[]{:S(2)}) collective-permute-start(bf16[8,3072]{1,0:T(8,128)(2,1)} %get-tuple-element.62), channel_id=1, source_target_pairs={{0,24},{1,25},{2,26},{3,27},{4,28},{5,29},{6,30},{7,31},{8,16},{9,... | collective-permute-start | bytes 147464 | tf_op jit(solution)/shard_map/ppermute | solution.py:556
  12.0 12.0 %collective-permute-start.3 = (bf16[32,1536]{1,0:T(8,128)(2,1)}, bf16[32,1536]{1,0:T(8,128)(2,1)}, u32[]{:S(2)}, u32[]{:S(2)}) collective-permute-start(bf16[32,1536]{1,0:T(8,128)(2,1)} %get-tuple-element.63), channel_id=1, source_target_pairs={{0,2},{1,3},{2,0},{3,1},{4,6},{5,7},{6,4},{7,5},{8,10},{9,11},{10,... | collective-permute-start | bytes 294920 | tf_op jit(solution)/shard_map/ppermute | solution.py:556
  13.7 10.3 %collective-permute-start.4 = (bf16[32,1536]{1,0:T(8,128)(2,1)}, bf16[32,1536]{1,0:T(8,128)(2,1)}, u32[]{:S(2)}, u32[]{:S(2)}) collective-permute-start(bf16[32,1536]{1,0:T(8,128)(2,1)} %get-tuple-element.63), channel_id=1, source_target_pairs={{0,4},{1,5},{2,6},{3,7},{4,0},{5,1},{6,2},{7,3},{8,12},{9,13},{10,... | collective-permute-start | bytes 294920 | tf_op jit(solution)/shard_map/ppermute | solution.py:556
  16.7 18.0 %copy-start.2 = (bf16[64,3072]{1,0:T(8,128)(2,1)S(1)}, bf16[64,3072]{1,0:T(8,128)(2,1)}, u32[]{:S(2)}) copy-start(bf16[64,3072]{1,0:T(8,128)(2,1)} %get-tuple-element.69.sel) | copy-start | bytes 1179652
  16.7 18.0 %copy-start.9 = (s32[2,12]{1,0:T(2,128)S(1)}, s32[2,12]{1,0:T(2,128)}, u32[]{:S(2)}) copy-start(s32[2,12]{1,0:T(2,128)} %offs_ref.9) | copy-start | bytes 292
  16.8 20.9 %copy-start.14 = (bf16[32,1536]{1,0:T(8,128)(2,1)S(1)}, bf16[32,1536]{1,0:T(8,128)(2,1)}, u32[]{:S(2)}) copy-start(bf16[32,1536]{1,0:T(8,128)(2,1)} %get-tuple-element.92) | copy-start | bytes 294916
  18.4 10.9 %collective-permute-start.5 = (bf16[32,1536]{1,0:T(8,128)(2,1)}, bf16[32,1536]{1,0:T(8,128)(2,1)S(1)}, u32[]{:S(2)}, u32[]{:S(2)}) collective-permute-start(bf16[32,1536]{1,0:T(8,128)(2,1)} %get-tuple-element.63), channel_id=1, source_target_pairs={{0,6},{1,7},{2,4},{3,5},{4,2},{5,3},{6,0},{7,1},{8,14},{9,15},{10,... | collective-permute-start | bytes 294920 | tf_op jit(solution)/shard_map/ppermute | solution.py:556
  24.0 8.0 %collective-permute-start.7 = (bf16[32,1536]{1,0:T(8,128)(2,1)S(1)}, bf16[32,1536]{1,0:T(8,128)(2,1)S(1)}, u32[]{:S(2)}, u32[]{:S(2)}) collective-permute-start(bf16[32,1536]{1,0:T(8,128)(2,1)S(1)} %get-tuple-element.71), channel_id=1, source_target_pairs={{0,2},{1,3},{2,0},{3,1},{4,6},{5,7},{6,4},{7,5},{8,10},{9,11},{10,... | collective-permute-start | bytes 294920 | tf_op jit(solution)/shard_map/ppermute | solution.py:556
  25.8 6.2 %collective-permute-start.8 = (bf16[32,1536]{1,0:T(8,128)(2,1)S(1)}, bf16[32,1536]{1,0:T(8,128)(2,1)S(1)}, u32[]{:S(2)}, u32[]{:S(2)}) collective-permute-start(bf16[32,1536]{1,0:T(8,128)(2,1)S(1)} %get-tuple-element.71), channel_id=1, source_target_pairs={{0,4},{1,5},{2,6},{3,7},{4,0},{5,1},{6,2},{7,3},{8,12},{9,13},{10,... | collective-permute-start | bytes 294920 | tf_op jit(solution)/shard_map/ppermute | solution.py:556
  27.3 5.5 %collective-permute-start.9 = (bf16[32,1536]{1,0:T(8,128)(2,1)S(1)}, bf16[32,1536]{1,0:T(8,128)(2,1)S(1)}, u32[]{:S(2)}, u32[]{:S(2)}) collective-permute-start(bf16[32,1536]{1,0:T(8,128)(2,1)S(1)} %get-tuple-element.71), channel_id=1, source_target_pairs={{0,6},{1,7},{2,4},{3,5},{4,2},{5,3},{6,0},{7,1},{8,14},{9,15},{10,... | collective-permute-start | bytes 294920 | tf_op jit(solution)/shard_map/ppermute | solution.py:556
  29.4 3.6 %collective-permute-start.6 = (bf16[128,1536]{1,0:T(8,128)(2,1)S(1)}, bf16[128,1536]{1,0:T(8,128)(2,1)S(1)}, u32[]{:S(2)}, u32[]{:S(2)}) collective-permute-start(bf16[128,1536]{1,0:T(8,128)(2,1)S(1)} %constant_dynamic-update-slice_fusion.4.mid_0), channel_id=1, source_target_pairs={{0,1},{1,0},{2,3},{3,2},{4,5},{5,4},{6,7},{7,6},{8,9},{9,8},{10,11... | collective-permute-start | bytes 1179656 | tf_op jit(solution)/shard_map/ppermute | solution.py:556
  32.9 18.4 %copy-start.4 = (bf16[256,768]{1,0:T(8,128)(2,1)S(1)}, bf16[256,768]{1,0:T(8,128)(2,1)}, u32[]{:S(2)}) copy-start(bf16[256,768]{1,0:T(8,128)(2,1)} %right.1) | copy-start | bytes 1179652
  32.9 1.8 %collective-permute-start.10 = (bf16[128,1536]{1,0:T(8,128)(2,1)S(1)}, bf16[128,1536]{1,0:T(8,128)(2,1)S(1)}, u32[]{:S(2)}, u32[]{:S(2)}) collective-permute-start(bf16[128,1536]{1,0:T(8,128)(2,1)S(1)} %constant_dynamic-update-slice_fusion.8.far_0), channel_id=1, source_target_pairs={{0,1},{1,0},{2,3},{3,2},{4,5},{5,4},{6,7},{7,6},{8,9},{9,8},{10,11... | collective-permute-start | bytes 1179656 | tf_op jit(solution)/shard_map/ppermute | solution.py:556
  37.0 6.2 %collective-permute-start.11 = (f32[8,128]{1,0:T(8,128)S(1)}, f32[8,128]{1,0:T(8,128)S(1)}, u32[]{:S(2)}, u32[]{:S(2)}) collective-permute-start(f32[8,128]{1,0:T(8,128)S(1)} %slice.157), channel_id=1, source_target_pairs={{0,8},{1,9},{2,10},{3,11},{4,12},{5,13},{6,14},{7,15},{8,0},{9,1},... | collective-permute-start | bytes 12296 | tf_op jit(solution)/shard_map/ppermute | solution.py:556
  37.8 13.0 %collective-permute-start.14 = (bf16[64,1536]{1,0:T(8,128)(2,1)S(1)}, bf16[64,1536]{1,0:T(8,128)(2,1)S(1)}, u32[]{:S(2)}, u32[]{:S(2)}) collective-permute-start(bf16[64,1536]{1,0:T(8,128)(2,1)S(1)} %pad_maximum_fusion.4), channel_id=1, source_target_pairs={{0,2},{1,3},{2,0},{3,1},{4,6},{5,7},{6,4},{7,5},{8,10},{9,11},{10,... | collective-permute-start | bytes 589832 | tf_op jit(solution)/shard_map/ppermute | solution.py:556
  38.9 12.3 %collective-permute-start.15 = (bf16[64,1536]{1,0:T(8,128)(2,1)S(1)}, bf16[64,1536]{1,0:T(8,128)(2,1)S(1)}, u32[]{:S(2)}, u32[]{:S(2)}) collective-permute-start(bf16[64,1536]{1,0:T(8,128)(2,1)S(1)} %pad_maximum_fusion.4), channel_id=1, source_target_pairs={{0,4},{1,5},{2,6},{3,7},{4,0},{5,1},{6,2},{7,3},{8,12},{9,13},{10,... | collective-permute-start | bytes 589832 | tf_op jit(solution)/shard_map/ppermute | solution.py:556
  40.4 10.9 %collective-permute-start.16 = (bf16[64,1536]{1,0:T(8,128)(2,1)S(1)}, bf16[64,1536]{1,0:T(8,128)(2,1)S(1)}, u32[]{:S(2)}, u32[]{:S(2)}) collective-permute-start(bf16[64,1536]{1,0:T(8,128)(2,1)S(1)} %pad_maximum_fusion.4), channel_id=1, source_target_pairs={{0,6},{1,7},{2,4},{3,5},{4,2},{5,3},{6,0},{7,1},{8,14},{9,15},{10,... | collective-permute-start | bytes 589832 | tf_op jit(solution)/shard_map/ppermute | solution.py:556
  43.2 8.2 %collective-permute-start.12 = (f32[16,128]{1,0:T(8,128)S(1)}, f32[16,128]{1,0:T(8,128)S(1)}, u32[]{:S(2)}, u32[]{:S(2)}) collective-permute-start(f32[16,128]{1,0:T(8,128)S(1)} %constant_dynamic-update-slice_fusion.12), channel_id=1, source_target_pairs={{0,16},{1,17},{2,18},{3,19},{4,20},{5,21},{6,22},{7,23},{8,24},{9,... | collective-permute-start | bytes 24584 | tf_op jit(solution)/shard_map/ppermute | solution.py:556
  50.6 5.2 %collective-permute-start.13 = (bf16[768,256]{1,0:T(8,128)(2,1)S(1)}, bf16[768,256]{1,0:T(8,128)(2,1)S(1)}, u32[]{:S(2)}, u32[]{:S(2)}) collective-permute-start(bf16[768,256]{1,0:T(8,128)(2,1)S(1)} %get-tuple-element.91), channel_id=1, source_target_pairs={{0,1},{1,0},{2,3},{3,2},{4,5},{5,4},{6,7},{7,6},{8,9},{9,8},{10,11... | collective-permute-start | bytes 1179656 | tf_op jit(solution)/shard_map/ppermute | solution.py:556
  50.7 6.7 %collective-permute-start.22 = (bf16[256,768]{1,0:T(8,128)(2,1)S(1)}, bf16[256,768]{1,0:T(8,128)(2,1)S(1)}, u32[]{:S(2)}, u32[]{:S(2)}) collective-permute-start(bf16[256,768]{1,0:T(8,128)(2,1)S(1)} %get-tuple-element.110.right.dq), channel_id=1, source_target_pairs={{0,1},{1,0},{2,3},{3,2},{4,5},{5,4},{6,7},{7,6},{8,9},{9,8},{10,11... | collective-permute-start | bytes 1179656 | tf_op jit(solution)/shard_map/ppermute | solution.py:556
  51.2 6.7 %collective-permute-start.21 = (bf16[256,768]{1,0:T(8,128)(2,1)S(1)}, bf16[256,768]{1,0:T(8,128)(2,1)S(1)}, u32[]{:S(2)}, u32[]{:S(2)}) collective-permute-start(bf16[256,768]{1,0:T(8,128)(2,1)S(1)} %copy-done.4), channel_id=1, source_target_pairs={{0,1},{1,0},{2,3},{3,2},{4,5},{5,4},{6,7},{7,6},{8,9},{9,8},{10,11... | collective-permute-start | bytes 1179656 | tf_op jit(solution)/shard_map/ppermute | solution.py:556
  51.4 4.1 %collective-permute-start.18 = (f32[32,256]{1,0:T(8,128)S(1)}, f32[32,256]{1,0:T(8,128)S(1)}, u32[]{:S(2)}, u32[]{:S(2)}) collective-permute-start(f32[32,256]{1,0:T(8,128)S(1)} %pad_maximum_fusion.9), channel_id=1, source_target_pairs={{0,2},{1,3},{2,0},{3,1},{4,6},{5,7},{6,4},{7,5},{8,10},{9,11},{10,... | collective-permute-start | bytes 98312 | tf_op jit(solution)/shard_map/ppermute | solution.py:556
  52.6 10.1 %collective-permute-start.17 = (bf16[256,1536]{1,0:T(8,128)(2,1)S(1)}, bf16[256,1536]{1,0:T(8,128)(2,1)S(1)}, u32[]{:S(2)}, u32[]{:S(2)}) collective-permute-start(bf16[256,1536]{1,0:T(8,128)(2,1)S(1)} %constant_dynamic-update-slice_fusion.16.qg_0), channel_id=1, source_target_pairs={{0,1},{1,0},{2,3},{3,2},{4,5},{5,4},{6,7},{7,6},{8,9},{9,8},{10,11... | collective-permute-start | bytes 2359304 | tf_op jit(solution)/shard_map/ppermute | solution.py:556
  55.5 2.5 %collective-permute-start.20 = (bf16[384,256]{1,0:T(8,128)(2,1)S(1)}, bf16[384,256]{1,0:T(8,128)(2,1)S(1)}, u32[]{:S(2)}, u32[]{:S(2)}) collective-permute-start(bf16[384,256]{1,0:T(8,128)(2,1)S(1)} %get-tuple-element.101), channel_id=1, source_target_pairs={{0,1},{1,0},{2,3},{3,2},{4,5},{5,4},{6,7},{7,6},{8,9},{9,8},{10,11... | collective-permute-start | bytes 589832 | tf_op jit(solution)/shard_map/ppermute | solution.py:556
  55.8 4.3 %collective-permute-start.19 = (f32[64,256]{1,0:T(8,128)S(1)}, f32[64,256]{1,0:T(8,128)S(1)}, u32[]{:S(2)}, u32[]{:S(2)}) collective-permute-start(f32[64,256]{1,0:T(8,128)S(1)} %constant_dynamic-update-slice_fusion.20), channel_id=1, source_target_pairs={{0,4},{1,5},{2,6},{3,7},{4,0},{5,1},{6,2},{7,3},{8,12},{9,13},{10,... | collective-permute-start | bytes 196616 | tf_op jit(solution)/shard_map/ppermute | solution.py:556
  60.2 7.9 %collective-permute-start.26 = (bf16[192,768]{1,0:T(8,128)(2,1)S(1)}, bf16[192,768]{1,0:T(8,128)(2,1)S(1)}, u32[]{:S(2)}, u32[]{:S(2)}) collective-permute-start(bf16[192,768]{1,0:T(8,128)(2,1)S(1)} %get-tuple-element.120), channel_id=1, source_target_pairs={{0,8},{1,9},{2,10},{3,11},{4,12},{5,13},{6,14},{7,15},{8,0},{9,1},... | collective-permute-start | bytes 884744 | tf_op jit(solution)/shard_map/ppermute | solution.py:556
  60.2 7.9 %collective-permute-start.28 = (bf16[192,768]{1,0:T(8,128)(2,1)S(1)}, bf16[192,768]{1,0:T(8,128)(2,1)S(1)}, u32[]{:S(2)}, u32[]{:S(2)}) collective-permute-start(bf16[192,768]{1,0:T(8,128)(2,1)S(1)} %get-tuple-element.122), channel_id=1, source_target_pairs={{0,2},{1,3},{2,0},{3,1},{4,6},{5,7},{6,4},{7,5},{8,10},{9,11},{10,... | collective-permute-start | bytes 884744 | tf_op jit(solution)/shard_map/ppermute | solution.py:556
  61.2 1.4 %collective-permute-start.23 = (f32[256,128]{1,0:T(8,128)S(1)}, f32[256,128]{1,0:T(8,128)S(1)}, u32[]{:S(2)}, u32[]{:S(2)}) collective-permute-start(f32[256,128]{1,0:T(8,128)S(1)} %pad_maximum_fusion.6.stats_0), channel_id=1, source_target_pairs={{0,1},{1,0},{2,3},{3,2},{4,5},{5,4},{6,7},{7,6},{8,9},{9,8},{10,11... | collective-permute-start | bytes 393224 | tf_op jit(solution)/shard_map/ppermute | solution.py:556
  65.0 3.3 %collective-permute-start.24 = (bf16[256,768]{1,0:T(8,128)(2,1)S(1)}, bf16[256,768]{1,0:T(8,128)(2,1)S(1)}, u32[]{:S(2)}, u32[]{:S(2)}) collective-permute-start(bf16[256,768]{1,0:T(8,128)(2,1)S(1)} %get-tuple-element.107.dk), channel_id=1, source_target_pairs={{0,1},{1,0},{2,3},{3,2},{4,5},{5,4},{6,7},{7,6},{8,9},{9,8},{10,11... | collective-permute-start | bytes 1179656 | tf_op jit(solution)/shard_map/ppermute | solution.py:556
  68.1 1.7 %collective-permute-start.25 = (bf16[256,768]{1,0:T(8,128)(2,1)S(1)}, bf16[256,768]{1,0:T(8,128)(2,1)S(1)}, u32[]{:S(2)}, u32[]{:S(2)}) collective-permute-start(bf16[256,768]{1,0:T(8,128)(2,1)S(1)} %get-tuple-element.108.dv), channel_id=1, source_target_pairs={{0,1},{1,0},{2,3},{3,2},{4,5},{5,4},{6,7},{7,6},{8,9},{9,8},{10,11... | collective-permute-start | bytes 1179656 | tf_op jit(solution)/shard_map/ppermute | solution.py:556
  70.6 26.7 %copy-start = (bf16[768,2304]{1,0:T(8,128)(2,1)S(1)}, bf16[768,2304]{1,0:T(8,128)(2,1)}, u32[]{:S(2)}) copy-start(bf16[768,2304]{1,0:T(8,128)(2,1)} %w_qkv.1) | copy-start | bytes 10616836
  70.7 21.8 %collective-permute-start.29 = (bf16[336,768]{1,0:T(8,128)(2,1)S(1)}, bf16[336,768]{1,0:T(8,128)(2,1)S(1)}, u32[]{:S(2)}, u32[]{:S(2)}) collective-permute-start(bf16[336,768]{1,0:T(8,128)(2,1)S(1)} %pad_maximum_fusion), channel_id=1, source_target_pairs={{0,4},{1,5},{2,6},{3,7},{4,0},{5,1},{6,2},{7,3},{8,12},{9,13},{10,... | collective-permute-start | bytes 1548296 | tf_op jit(solution)/shard_map/ppermute | solution.py:556
  72.3 11.5 %collective-permute-start.27 = (bf16[240,768]{1,0:T(8,128)(2,1)S(1)}, bf16[240,768]{1,0:T(8,128)(2,1)S(1)}, u32[]{:S(2)}, u32[]{:S(2)}) collective-permute-start(bf16[240,768]{1,0:T(8,128)(2,1)S(1)} %pad_maximum_fusion.1), channel_id=1, source_target_pairs={{0,2},{1,3},{2,0},{3,1},{4,6},{5,7},{6,4},{7,5},{8,10},{9,11},{10,... | collective-permute-start | bytes 1105928 | tf_op jit(solution)/shard_map/ppermute | solution.py:556
  73.9 16.7 %collective-permute-start.30 = (bf16[240,768]{1,0:T(8,128)(2,1)S(1)}, bf16[240,768]{1,0:T(8,128)(2,1)S(1)}, u32[]{:S(2)}, u32[]{:S(2)}) collective-permute-start(bf16[240,768]{1,0:T(8,128)(2,1)S(1)} %pad_maximum_fusion.2), channel_id=1, source_target_pairs={{0,6},{1,7},{2,4},{3,5},{4,2},{5,3},{6,0},{7,1},{8,14},{9,15},{10,... | collective-permute-start | bytes 1105928 | tf_op jit(solution)/shard_map/ppermute | solution.py:556
  92.7 6.5 %collective-permute-start.32 = (bf16[72,768]{1,0:T(8,128)(2,1)S(1)}, bf16[72,768]{1,0:T(8,128)(2,1)S(1)}, u32[]{:S(2)}, u32[]{:S(2)}) collective-permute-start(bf16[72,768]{1,0:T(8,128)(2,1)S(1)} %pad_maximum_fusion.7), channel_id=1, source_target_pairs={{0,8},{1,9},{2,10},{3,11},{4,12},{5,13},{6,14},{7,15},{8,0},{9,1},... | collective-permute-start | bytes 331784 | tf_op jit(solution)/shard_map/ppermute | solution.py:556
  93.1 12.8 %collective-permute-start.31 = (bf16[96,768]{1,0:T(8,128)(2,1)S(1)}, bf16[96,768]{1,0:T(8,128)(2,1)S(1)}, u32[]{:S(2)}, u32[]{:S(2)}) collective-permute-start(bf16[96,768]{1,0:T(8,128)(2,1)S(1)} %pad_maximum_fusion.5), channel_id=1, source_target_pairs={{0,16},{1,17},{2,18},{3,19},{4,20},{5,21},{6,22},{7,23},{8,24},{9,... | collective-permute-start | bytes 442376 | tf_op jit(solution)/shard_map/ppermute | solution.py:556
  95.4 9.1 %collective-permute-start.33 = (bf16[72,768]{1,0:T(8,128)(2,1)S(1)}, bf16[72,768]{1,0:T(8,128)(2,1)S(1)}, u32[]{:S(2)}, u32[]{:S(2)}) collective-permute-start(bf16[72,768]{1,0:T(8,128)(2,1)S(1)} %pad_maximum_fusion.8), channel_id=1, source_target_pairs={{0,24},{1,25},{2,26},{3,27},{4,28},{5,29},{6,30},{7,31},{8,16},{9,... | collective-permute-start | bytes 331784 | tf_op jit(solution)/shard_map/ppermute | solution.py:556
  (1 other events, 15.8 us)

commit v7 on v5

--- a/solution.py
+++ b/solution.py
@@ -20,6 +20,7 @@
 NN = (((1,), (0,)), ((), ()))
 TN = (((0,), (0,)), ((), ()))
 LARGE = 1e30
+LOW_COST = 0.05
 LOAD_CUTS = 4
 VMEM_BYTES = 40 * 1024 * 1024
 PROJECT_VMEM_BYTES = 57 * 1024 * 1024
@@ -523,7 +524,7 @@
     ).astype(BF)
 
 
-def call(kernel, outs, flops, scratch=(), smem=0, spaces=None, vmem=VMEM_BYTES, hbm_outs=0):
+def call(kernel, outs, flops, scratch=(), smem=0, spaces=None, vmem=VMEM_BYTES, hbm_outs=0, cost=1.0):
     def run(*args):
         moved = sum(int(np.prod(a.shape)) * a.dtype.itemsize for a in args)
         moved += sum(int(np.prod(s)) * jnp.dtype(t).itemsize for s, t in outs)
@@ -542,7 +543,7 @@
             scratch_shapes=list(scratch),
             compiler_params=pltpu.CompilerParams(vmem_limit_bytes=vmem),
             cost_estimate=pl.CostEstimate(
-                flops=int(flops), bytes_accessed=int(moved), transcendentals=0
+                flops=int(flops * cost), bytes_accessed=int(moved * cost), transcendentals=0
             ),
         )(*args)
 
@@ -629,6 +630,10 @@
     order_q = strip_order(z, own, [1] + masks + [2, 4])
     order_out = strip_order(z, own, [1, 2, 4] + masks)
     base_flops = 2 * rows * rows * width
+
+    def weights(start, *args):
+        kernel = functools.partial(weights_kernel, start)
+        return call(kernel, [((z.half, width), BF)], 4 * rows * width * width)(*args)[0]
 
     q, k, v, g, sel, mid_kv, mid_qg, far = call(
         functools.partial(project_kernel, z),
@@ -651,9 +656,12 @@
         vmem=PROJECT_VMEM_BYTES,
     )(offsets, tiles, w_qkv, cotangent, w_out)
 
+    steps = upper_steps(n)
     far_up = far
-    for step in upper_steps(n):
+    for step in steps[:-1]:
         far_up = jnp.concatenate(step_parts(far_up, step, n), axis=0)
+    far_up = step_parts(far_up, steps[-1], n)
+    far_kv = jnp.concatenate([part[:, : 2 * width] for part in far_up], axis=0)
     mid_parts = step_parts(mid_kv, PLANE, n)
     mixed, near_stats, turned, turned_out = call(
         functools.partial(near_kernel, z),
@@ -665,16 +673,13 @@
         ],
         8 * base_flops,
         smem=1,
-    )(pad_count, after(q, far_up), k, v, g, tiles, order, order_q)
+    )(pad_count, after(q, far_kv, *mid_parts[1:3]), k, v, g, tiles, order, order_q)
     mid_0 = jnp.concatenate(mid_parts, axis=0)
     mid_1 = swap(mid_0, 1, n)
     far_0 = jnp.concatenate(
-        step_parts(far_up[:, : 2 * width], PLANE, n, (near_stats,)), axis=0
+        step_parts(after(far_kv, *mid_parts[1:3]), PLANE, n, (near_stats,)), axis=0
     )
     far_1 = swap(far_0, 1, n)
-    qg = jnp.concatenate([mid_qg, far_up[:, 2 * width :]], axis=0)
-    qg_parts = step_parts(after(qg, far_0), PLANE, n)
-
     stats, picked, raw, held = call(
         functools.partial(join_kernel, z),
         [((rows, LANES), F32), ((z.sel, LANES), F32), ((z.sel, LANES), F32), ((z.sel, width), F32)],
@@ -682,52 +687,59 @@
         smem=2,
     )(offsets, pad_count, sel, mid_0, mid_1, far_0, far_1, near_stats)
 
+    (dq_sel,) = call(
+        functools.partial(own_grads_kernel, z),
+        [((z.sel, width), F32)],
+        2 * base_flops,
+        smem=2,
+    )(offsets, pad_count, sel, mid_0, mid_1, far_0, far_1, picked)
+    qg_mid, *qg_far = tied([mid_qg] + far_up, (dq_sel,))
+    qg = jnp.concatenate([qg_mid] + [part[:, 2 * width :] for part in qg_far], axis=0)
+    qg_parts = step_parts(qg, PLANE, n)
+    cot_other = swap(after(cotangent, picked), 1, n)
+    stats_up = doubled(picked[z.mid : z.mid + z.far], masks[:1], n, ((dq_sel,),))
     out_rows, attn_turned, attn_turned_out = call(
         functools.partial(output_kernel, z),
         [((rows, width), BF), ((z.half, rows), BF), ((z.half, rows), BF)],
         6 * rows * width * width,
         scratch=[pltpu.VMEM((rows, width), BF)],
         smem=1,
-    )(offsets, near_stats, stats, picked, raw, mixed, held, tiles, w_out, order_out)
+    )(offsets, near_stats, stats, after(picked, stats_up), raw, mixed, held, tiles, w_out, order_out)
     attn_other = swap(attn_turned_out, 1, n)
-    (dq_sel,) = call(
-        functools.partial(own_grads_kernel, z),
-        [((z.sel, width), F32)],
-        2 * base_flops,
-        smem=2,
-    )(offsets, pad_count, sel, mid_0, mid_1, far_0, far_1, after(picked, attn_turned))
-    turned_other = swap(after(turned_out, picked), 1, n)
-    cot_other = swap(after(cotangent, picked), 1, n)
-
-    qg_0 = jnp.concatenate(tied(qg_parts, (out_rows,)), axis=0)
+    stats_up = doubled(stats_up, masks[1:], n, ((out_rows,),))
+    wout_half = weights(0, attn_turned, attn_other, cotangent, after(cot_other, stats_up))
+    turned_other = swap(after(turned_out, wout_half), 1, n)
+    qg_0 = jnp.concatenate(tied(qg_parts, (wout_half,)), axis=0)
     qg_1 = swap(qg_0, 1, n)
-    stats_up = picked[z.mid : z.mid + z.far]
-    for i, step in enumerate(upper_steps(n)):
-        parts = step_parts(stats_up, step, n, (out_rows,) if i == 0 else ())
-        stats_up = jnp.concatenate(parts, axis=0)
-    def weights(start, *args):
-        kernel = functools.partial(weights_kernel, start)
-        return call(kernel, [((z.half, width), BF)], 4 * rows * width * width)(*args)[0]
-
-    wout_half = weights(0, attn_turned, attn_other, cotangent, after(cot_other, stats_up))
-
+
+    stats_far = stats_up
+    stats_up = jnp.concatenate([picked[: z.mid], stats_far], axis=1)
+    stats_up = doubled(stats_up, (4,), n, ((wout_half,),))
     dq, dk_near, dv_near = call(
         functools.partial(near_grads_kernel, z),
         [((rows, width), BF), ((rows, width), F32), ((rows, width), F32)],
         8 * base_flops,
         smem=2,
-    )(offsets, pad_count, after(q, wout_half), k, v, g, stats, dq_sel)
+    )(offsets, pad_count, after(q, stats_up), k, v, g, stats, dq_sel)
     dq_other = swap(dq, 1, n)
-    stats_plane = doubled(jnp.concatenate([picked[: z.mid], stats_up], axis=1), (2, 4), n, ((dq_sel,), (dk_near,)))
-    stats_0 = jnp.concatenate([stats_plane[:, :LANES], stats_plane[:, LANES:]], axis=0)
+    stats_up = doubled(stats_up, (2,), n, ((dk_near,),))
+    early_half = weights(z.half, turned, turned_other, dq, dq_other)
+    stats_0 = jnp.concatenate(
+        [
+            stats_up[at * z.mid : (at + 1) * z.mid, level * LANES : (level + 1) * LANES]
+            for level in range(2)
+            for at in (0, 2, 1, 3)
+        ],
+        axis=0,
+    )
     stats_1 = swap(stats_0, 1, n)
-    early_half = weights(z.half, turned, turned_other, dq, dq_other)
 
     dk, dv = call(
         functools.partial(key_grads_kernel, z),
         [((rows, width), BF), ((rows, width), BF)],
         3 * base_flops,
         smem=2,
+        cost=LOW_COST,
     )(
         offsets, pad_count, sel, qg_0, qg_1, stats_0, stats_1,
         after(dk_near, early_half), dv_near,
@@ -738,13 +750,17 @@
         functools.partial(late_weights_kernel, z),
         [((z.half, 2 * width), BF)],
         4 * rows * width * width,
+        cost=LOW_COST,
     )(turned, turned_other, dk, dv, dk_other, dv_other)
     (grad_tiles,) = call(
-        functools.partial(tiles_kernel, z), [((rows, width), BF)], 6 * rows * width * width
+        functools.partial(tiles_kernel, z),
+        [((rows, width), BF)],
+        6 * rows * width * width,
+        cost=LOW_COST,
     )(after(dq, late_half), dk, dv, w_qkv)
     late_parts = block_parts(late_half, PLANE, n)
-    early = halved(early_half, masks + [2, 4], n, ((late_parts[1],),))
-    grad_wout = halved(wout_half, [2, 4] + masks, n, ((dq,), (dk,), (late_parts[1],)))
+    early = halved(early_half, masks + [2, 4], n, ((dk_other,), (late_parts[1],)))
+    grad_wout = halved(wout_half, [2, 4] + masks, n, ((dk_near,), (late_parts[1],)))
     late = reduce_all(sum_parts(late_parts, BF), upper_steps(n)[::-1], n)
     grad_wqkv = jnp.concatenate([early, late], axis=1)
     return out_rows, grad_tiles, grad_wqkv, grad_wout

time: 99.3 us -> 98.9 us (level)
  starting transfers between devices: 39.1 us -> 40.9 us
  waiting for transfers between devices: 29.3 us -> 27.9 us
    ppermute x41 -> x40, starting transfers between devices: 39.1 us -> 40.9 us  [swap(): return lax.ppermute(value, 'ctx', [(d, d ^ mask) for d in range(dev_count)])]
    ppermute x41 -> x40, waiting for transfers between devices: 29.3 us -> 27.9 us  [swap(): return lax.ppermute(value, 'ctx', [(d, d ^ mask) for d in range(dev_count)])]
  transfers between devices with their start and end apart: 41 -> 40, of which waited for: 13 -> 14; matrix products, arithmetic and copies ran while one was open for 2% -> 2% of each run, Pallas kernels for 19% -> 15%
where the time goes in v7:
time: 98.9 us; the launch traced here: 98.8 us
  starting transfers between devices  40.9 us (41%)
  waiting for transfers between devices  27.9 us (28%)
  Pallas kernels  24.7 us (25%)
  between operations  2.1 us (2%)
  other arithmetic  1.94 us (2%)
  local copies, waits for them, and re-layouts  1.25 us (1%)
    ppermute x40, starting transfers between devices, swap(): return lax.ppermute(value, 'ctx', [(d, d ^ mask) for d in range(dev_count)])  40.9 us
    ppermute x40, waiting for transfers between devices, swap(): return lax.ppermute(value, 'ctx', [(d, d ^ mask) for d in range(dev_count)])  27.9 us
    pallas_call x11, Pallas kernels, run(): pl.pallas_call(kernel, out_shape=tuple((jax.ShapeDtypeStruct(s, t) for s,...  24.7 us
  transfers between devices with their start and end apart: 40, of which 14 were waited for; matrix products, arithmetic and copies ran while one was open for 2% of the time, Pallas kernels for 15%

profile of v7, /device:TPU:0, one launch (start us, length us, event | category | flops | bytes accessed | tf_op | source)
XLA Modules:
  0.0 98.8 jit_solution(12948749280299874431)
XLA Ops:
  0.7 5.6 %shard_map.147 = (bf16[256,768]{1,0:T(8,128)(2,1)}, bf16[256,768]{1,0:T(8,128)(2,1)}, bf16[256,768]{1,0:T(8,128)(2,1)}, bf16[256,768]{1,0:T(8,128)(2,1)}, bf16[6...) custom-call(s32[2,12]{1,0:T(2,128)} %offs_ref.9, ...), custom_call_target="tpu_custom_call" | custom-call | flops 1207959552 | bytes 7716960 | tf_op jit(solution)/shard_map/pallas_call | solution.py:535
  6.2 3.1 %collective-permute-start = (bf16[8,3072]{1,0:T(8,128)(2,1)}, bf16[8,3072]{1,0:T(8,128)(2,1)S(1)}, u32[]{:S(2)}, u32[]{:S(2)}) collective-permute-start(bf16[8,3072]{1,0:T(8,128)(2,1)} %get-tuple-element.104), channel_id=1, source_target_pairs={{0,8},{1,9},{2,10},{3,11},{4,12},{5,13},{6,14},{7,15},{8,0},{9,1},... | collective-permute-start | bytes 147464 | tf_op jit(solution)/shard_map/ppermute | solution.py:554
  9.3 2.6 %collective-permute-start.1 = (bf16[8,3072]{1,0:T(8,128)(2,1)}, bf16[8,3072]{1,0:T(8,128)(2,1)S(1)}, u32[]{:S(2)}, u32[]{:S(2)}) collective-permute-start(bf16[8,3072]{1,0:T(8,128)(2,1)} %get-tuple-element.104), channel_id=1, source_target_pairs={{0,16},{1,17},{2,18},{3,19},{4,20},{5,21},{6,22},{7,23},{8,24},{9,... | collective-permute-start | bytes 147464 | tf_op jit(solution)/shard_map/ppermute | solution.py:554
  11.9 1.7 %collective-permute-start.3 = (bf16[32,1536]{1,0:T(8,128)(2,1)}, bf16[32,1536]{1,0:T(8,128)(2,1)S(1)}, u32[]{:S(2)}, u32[]{:S(2)}) collective-permute-start(bf16[32,1536]{1,0:T(8,128)(2,1)} %get-tuple-element.68), channel_id=1, source_target_pairs={{0,2},{1,3},{2,0},{3,1},{4,6},{5,7},{6,4},{7,5},{8,10},{9,11},{10,... | collective-permute-start | bytes 294920 | tf_op jit(solution)/shard_map/ppermute | solution.py:554
  13.6 1.5 %collective-permute-start.4 = (bf16[32,1536]{1,0:T(8,128)(2,1)}, bf16[32,1536]{1,0:T(8,128)(2,1)S(1)}, u32[]{:S(2)}, u32[]{:S(2)}) collective-permute-start(bf16[32,1536]{1,0:T(8,128)(2,1)} %get-tuple-element.68), channel_id=1, source_target_pairs={{0,4},{1,5},{2,6},{3,7},{4,0},{5,1},{6,2},{7,3},{8,12},{9,13},{10,... | collective-permute-start | bytes 294920 | tf_op jit(solution)/shard_map/ppermute | solution.py:554
  15.4 0.7 copy-done.15
  17.2 0.8 collective-permute-done.2
  18.1 0.6 collective-permute-done.4
  18.7 0.9 collective-permute-start.7
  19.6 2.0 %collective-permute-start.8 = (bf16[32,1536]{1,0:T(8,128)(2,1)S(1)}, bf16[32,1536]{1,0:T(8,128)(2,1)S(1)}, u32[]{:S(2)}, u32[]{:S(2)}) collective-permute-start(bf16[32,1536]{1,0:T(8,128)(2,1)S(1)} %pad_maximum_fusion.1), channel_id=1, source_target_pairs={{0,4},{1,5},{2,6},{3,7},{4,0},{5,1},{6,2},{7,3},{8,12},{9,13},{10,... | collective-permute-start | bytes 294920 | tf_op jit(solution)/shard_map/ppermute | solution.py:554
  21.6 0.9 collective-permute-start.9
  22.8 2.5 %shard_map.148 = (f32[256,768]{1,0:T(8,128)S(1)}, f32[256,128]{1,0:T(8,128)S(1)}, bf16[768,256]{1,0:T(8,128)(2,1)S(1)}, bf16[768,256]{1,0:T(8,128)(2,1)S(1)}) custom-call(s32[1]{0:T(128)S(6)} %copy.42.pad_ref, bf16[256,768]{1,0:T(8,128)(2,1)S(1)} %copy-done.6, bf16[256,768]{1,0:T(8,128)(2,1)S(1)} %copy-done.7, bf16[256,768]{1,0:T(8,128)(2,1)S(1)} %copy-done.8, ...), custom_call_target="tpu_custom_call" | custom-call | flops 805306368 | bytes 3676164 | tf_op jit(solution)/shard_map/pallas_call | solution.py:535
  25.3 1.7 %collective-permute-done.9 = bf16[32,1536]{1,0:T(8,128)(2,1)S(1)} collective-permute-done((bf16[32,1536]{1,0:T(8,128)(2,1)S(1)}, bf16[32,1536]{1,0:T(8,128)(2,1)S(1)}, u32[]{:S(2)}, u32[]{:S(2)}) %collective-permute-start.9) | collective-permute-done | bytes 98336 | tf_op jit(solution)/shard_map/ppermute | solution.py:554
  27.2 1.7 %collective-permute-done.10.far_1 = bf16[128,1536]{1,0:T(8,128)(2,1)S(1)} collective-permute-done((bf16[128,1536]{1,0:T(8,128)(2,1)S(1)}, bf16[128,1536]{1,0:T(8,128)(2,1)S(1)}, u32[]{:S(2)}, u32[]{:S(2)}) %collective-permute-start.10) | collective-permute-done | bytes 393248 | tf_op jit(solution)/shard_map/ppermute | solution.py:554
  28.9 2.3 %shard_map.149 = (f32[256,128]{1,0:T(8,128)S(1)}, f32[64,128]{1,0:T(8,128)S(1)}, f32[64,128]{1,0:T(8,128)S(1)}, f32[64,768]{1,0:T(8,128)S(1)}) custom-call(s32[2,12]{1,0:T(2,128)S(1)} %copy-done.5, s32[1]{0:T(128)S(6)} %copy.42.pad_ref, bf16[64,3072]{1,0:T(8,128)(2,1)S(1)} %copy-done.1, bf16[128,1536]{1,0:T(8,128)(2,1)S(1)} %constant_dynamic-update-slice_fusion.mid_0, ...), custom_call_target="tpu_custom_call" | custom-call | flops 301989888 | bytes 2490468 | tf_op jit(solution)/shard_map/pallas_call | solution.py:535
  31.3 0.7 collective-permute-start.11
  32.0 1.8 %shard_map.150.dq_sel = f32[64,768]{1,0:T(8,128)S(1)} custom-call(s32[2,12]{1,0:T(2,128)S(1)} %copy-done.5, s32[1]{0:T(128)S(6)} %copy.42.pad_ref, bf16[64,3072]{1,0:T(8,128)(2,1)S(1)} %copy-done.1, bf16[128,1536]{1,0:T(8,128)(2,1)S(1)} %constant_dynamic-update-slice_fusion.mid_0, bf16[128,1536]{1,0:T(8,128)(2,1)S(1)} %collective-permute-done.6.mid_1, ...), custom_call_target="tpu_custom_call" | custom-call | flops 201326592 | bytes 2195556 | tf_op jit(solution)/shard_map/pallas_call | solution.py:535
  34.0 1.6 %collective-permute-start.17 = (bf16[64,1536]{1,0:T(8,128)(2,1)S(1)}, bf16[64,1536]{1,0:T(8,128)(2,1)S(1)}, u32[]{:S(2)}, u32[]{:S(2)}) collective-permute-start(bf16[64,1536]{1,0:T(8,128)(2,1)S(1)} %constant_dynamic-update-slice_fusion.14), channel_id=1, source_target_pairs={{0,2},{1,3},{2,0},{3,1},{4,6},{5,7},{6,4},{7,5},{8,10},{9,11},{10,... | collective-permute-start | bytes 589832 | tf_op jit(solution)/shard_map/ppermute | solution.py:554
  35.7 1.8 %collective-permute-start.19 = (bf16[64,1536]{1,0:T(8,128)(2,1)S(1)}, bf16[64,1536]{1,0:T(8,128)(2,1)S(1)}, u32[]{:S(2)}, u32[]{:S(2)}) collective-permute-start(bf16[64,1536]{1,0:T(8,128)(2,1)S(1)} %constant_dynamic-update-slice_fusion.14), channel_id=1, source_target_pairs={{0,6},{1,7},{2,4},{3,5},{4,2},{5,3},{6,0},{7,1},{8,14},{9,15},{10,... | collective-permute-start | bytes 589832 | tf_op jit(solution)/shard_map/ppermute | solution.py:554
  37.5 3.6 %collective-permute-start.12 = (f32[16,128]{1,0:T(8,128)S(1)}, f32[16,128]{1,0:T(8,128)S(1)}, u32[]{:S(2)}, u32[]{:S(2)}) collective-permute-start(f32[16,128]{1,0:T(8,128)S(1)} %constant_dynamic-update-slice_fusion.8), channel_id=1, source_target_pairs={{0,16},{1,17},{2,18},{3,19},{4,20},{5,21},{6,22},{7,23},{8,24},{9,... | collective-permute-start | bytes 24584 | tf_op jit(solution)/shard_map/ppermute | solution.py:554
  41.1 2.5 %shard_map.151 = (bf16[256,768]{1,0:T(8,128)(2,1)}, bf16[384,256]{1,0:T(8,128)(2,1)S(1)}, bf16[384,256]{1,0:T(8,128)(2,1)S(1)}) custom-call(s32[2,12]{1,0:T(2,128)S(1)} %copy-done.5, f32[256,128]{1,0:T(8,128)S(1)} %get-tuple-element.73.near_stats, f32[256,128]{1,0:T(8,128)S(1)} %get-tuple-element.80.stats, f32[64,128]{1,0:T(8,128)S(1)} %get-tuple-element.84.picked, ...), custom_call_target="tpu_custom_call" | custom-call | flops 905969664 | bytes 3673184 | tf_op jit(solution)/shard_map/pallas_call | solution.py:535
  44.2 0.9 collective-permute-done.14.left_other
  45.6 2.2 %collective-permute-done.13 = f32[32,256]{1,0:T(8,128)S(1)} collective-permute-done((f32[32,256]{1,0:T(8,128)S(1)}, f32[32,256]{1,0:T(8,128)S(1)}, u32[]{:S(2)}, u32[]{:S(2)}) %collective-permute-start.13) | collective-permute-done | bytes 32800 | tf_op jit(solution)/shard_map/ppermute | solution.py:554
  47.8 1.6 %collective-permute-start.21 = (f32[64,256]{1,0:T(8,128)S(1)}, f32[64,256]{1,0:T(8,128)S(1)}, u32[]{:S(2)}, u32[]{:S(2)}) collective-permute-start(f32[64,256]{1,0:T(8,128)S(1)} %constant_dynamic-update-slice_fusion.12), channel_id=1, source_target_pairs={{0,2},{1,3},{2,0},{3,1},{4,6},{5,7},{6,4},{7,5},{8,10},{9,11},{10,... | collective-permute-start | bytes 196616 | tf_op jit(solution)/shard_map/ppermute | solution.py:554
  49.4 0.5 collective-permute-start.36
  49.9 4.1 %shard_map.153 = (bf16[256,768]{1,0:T(8,128)(2,1)S(1)}, f32[256,768]{1,0:T(8,128)S(1)}, f32[256,768]{1,0:T(8,128)S(1)}) custom-call(s32[2,12]{1,0:T(2,128)S(1)} %copy-done.5, s32[1]{0:T(128)S(6)} %copy.42.pad_ref, bf16[256,768]{1,0:T(8,128)(2,1)S(1)} %copy-done.6, bf16[256,768]{1,0:T(8,128)(2,1)S(1)} %copy-done.7, bf16[256,768]{1,0:T(8,128)(2,1)S(1)} %copy-done.8, ...), custom_call_target="tpu_custom_call" | custom-call | flops 805306368 | bytes 3866724 | tf_op jit(solution)/shard_map/pallas_call | solution.py:535
  54.1 0.5 collective-permute-start.23
  54.9 0.5 collective-permute-start.22
  55.4 2.6 %collective-permute-done.36 = bf16[192,768]{1,0:T(8,128)(2,1)S(1)} collective-permute-done((bf16[192,768]{1,0:T(8,128)(2,1)S(1)}, bf16[192,768]{1,0:T(8,128)(2,1)S(1)}, u32[]{:S(2)}, u32[]{:S(2)}) %collective-permute-start.36) | collective-permute-done | bytes 294944 | tf_op jit(solution)/shard_map/ppermute | solution.py:554
  58.5 2.4 %shard_map.155 = (bf16[256,768]{1,0:T(8,128)(2,1)S(1)}, bf16[256,768]{1,0:T(8,128)(2,1)S(1)}) custom-call(s32[2,12]{1,0:T(2,128)S(1)} %copy-done.5, s32[1]{0:T(128)S(6)} %copy.42.pad_ref, bf16[64,3072]{1,0:T(8,128)(2,1)S(1)} %copy-done.1, bf16[256,1536]{1,0:T(8,128)(2,1)S(1)} %constant_dynamic-update-slice_fusion.19.qg_0, ...), custom_call_target="tpu_custom_call" | custom-call | flops 15099494 | bytes 229381 | tf_op jit(solution)/shard_map/pallas_call | solution.py:535
  61.0 0.5 collective-permute-start.25
  61.9 1.0 %collective-permute-start.26 = (bf16[192,768]{1,0:T(8,128)(2,1)S(1)}, bf16[192,768]{1,0:T(8,128)(2,1)S(1)}, u32[]{:S(2)}, u32[]{:S(2)}) collective-permute-start(bf16[192,768]{1,0:T(8,128)(2,1)S(1)} %get-tuple-element.133), channel_id=1, source_target_pairs={{0,8},{1,9},{2,10},{3,11},{4,12},{5,13},{6,14},{7,15},{8,0},{9,1},... | collective-permute-start | bytes 884744 | tf_op jit(solution)/shard_map/ppermute | solution.py:554
  63.2 0.8 shard_map.156
  64.1 1.0 %collective-permute-start.28 = (bf16[96,1536]{1,0:T(8,128)(2,1)S(1)}, bf16[96,1536]{1,0:T(8,128)(2,1)S(1)}, u32[]{:S(2)}, u32[]{:S(2)}) collective-permute-start(bf16[96,1536]{1,0:T(8,128)(2,1)S(1)} %get-tuple-element.128), channel_id=1, source_target_pairs={{0,2},{1,3},{2,0},{3,1},{4,6},{5,7},{6,4},{7,5},{8,10},{9,11},{10,... | collective-permute-start | bytes 884744 | tf_op jit(solution)/shard_map/ppermute | solution.py:554
  65.1 5.5 %collective-permute-done.26 = bf16[192,768]{1,0:T(8,128)(2,1)S(1)} collective-permute-done((bf16[192,768]{1,0:T(8,128)(2,1)S(1)}, bf16[192,768]{1,0:T(8,128)(2,1)S(1)}, u32[]{:S(2)}, u32[]{:S(2)}) %collective-permute-start.26) | collective-permute-done | bytes 294944 | tf_op jit(solution)/shard_map/ppermute | solution.py:554
  70.8 3.1 %collective-permute-start.27 = (bf16[96,768]{1,0:T(8,128)(2,1)S(1)}, bf16[96,768]{1,0:T(8,128)(2,1)S(1)}, u32[]{:S(2)}, u32[]{:S(2)}) collective-permute-start(bf16[96,768]{1,0:T(8,128)(2,1)S(1)} %get-tuple-element.140), channel_id=1, source_target_pairs={{0,16},{1,17},{2,18},{3,19},{4,20},{5,21},{6,22},{7,23},{8,24},{9,... | collective-permute-start | bytes 442376 | tf_op jit(solution)/shard_map/ppermute | solution.py:554
  73.9 0.9 collective-permute-start.31
  74.8 1.8 %collective-permute-start.32 = (bf16[96,1536]{1,0:T(8,128)(2,1)S(1)}, bf16[96,1536]{1,0:T(8,128)(2,1)S(1)}, u32[]{:S(2)}, u32[]{:S(2)}) collective-permute-start(bf16[96,1536]{1,0:T(8,128)(2,1)S(1)} %get-tuple-element.129), channel_id=1, source_target_pairs={{0,6},{1,7},{2,4},{3,5},{4,2},{5,3},{6,0},{7,1},{8,14},{9,15},{10,... | collective-permute-start | bytes 884744 | tf_op jit(solution)/shard_map/ppermute | solution.py:554
  76.6 1.9 %shard_map.157 = bf16[256,768]{1,0:T(8,128)(2,1)} custom-call(bf16[256,768]{1,0:T(8,128)(2,1)S(1)} %get-tuple-element.119.right.dq, bf16[256,768]{1,0:T(8,128)(2,1)S(1)} %get-tuple-element.117.dk, bf16[256,768]{1,0:T(8,128)(2,1)S(1)} %get-tuple-element.118.dv, bf16[768,2304]{1,0:T(8,128)(2,1)S(1)} %copy-done), custom_call_target="tpu_custom_call" | custom-call | flops 45298484 | bytes 255590 | tf_op jit(solution)/shard_map/pallas_call | solution.py:535
  78.9 1.1 %collective-permute-done.27 = bf16[96,768]{1,0:T(8,128)(2,1)S(1)} collective-permute-done((bf16[96,768]{1,0:T(8,128)(2,1)S(1)}, bf16[96,768]{1,0:T(8,128)(2,1)S(1)}, u32[]{:S(2)}, u32[]{:S(2)}) %collective-permute-start.27) | collective-permute-done | bytes 147488 | tf_op jit(solution)/shard_map/ppermute | solution.py:554
  80.0 1.4 %collective-permute-start.29 = (bf16[48,768]{1,0:T(8,128)(2,1)S(1)}, bf16[48,768]{1,0:T(8,128)(2,1)S(1)}, u32[]{:S(2)}, u32[]{:S(2)}) collective-permute-start(bf16[48,768]{1,0:T(8,128)(2,1)S(1)} %slice.177), channel_id=1, source_target_pairs={{0,2},{1,3},{2,0},{3,1},{4,6},{5,7},{6,4},{7,5},{8,10},{9,11},{10,... | collective-permute-start | bytes 221192 | tf_op jit(solution)/shard_map/ppermute | solution.py:554
  81.4 6.4 %collective-permute-done.31 = bf16[96,1536]{1,0:T(8,128)(2,1)S(1)} collective-permute-done((bf16[96,1536]{1,0:T(8,128)(2,1)S(1)}, bf16[96,1536]{1,0:T(8,128)(2,1)S(1)}, u32[]{:S(2)}, u32[]{:S(2)}) %collective-permute-start.31) | collective-permute-done | bytes 294944 | tf_op jit(solution)/shard_map/ppermute | solution.py:554
  88.3 0.5 collective-permute-start.34
  88.8 3.6 %collective-permute-start.35 = (bf16[24,1536]{1,0:T(8,128)(2,1)S(1)}, bf16[24,1536]{1,0:T(8,128)(2,1)S(1)}, u32[]{:S(2)}, u32[]{:S(2)}) collective-permute-start(bf16[24,1536]{1,0:T(8,128)(2,1)S(1)} %get-tuple-element.143), channel_id=1, source_target_pairs={{0,24},{1,25},{2,26},{3,27},{4,28},{5,29},{6,30},{7,31},{8,16},{9,... | collective-permute-start | bytes 221192 | tf_op jit(solution)/shard_map/ppermute | solution.py:554
  92.5 1.0 collective-permute-start.30
  93.5 3.4 %collective-permute-done.34 = bf16[24,1536]{1,0:T(8,128)(2,1)S(1)} collective-permute-done((bf16[24,1536]{1,0:T(8,128)(2,1)S(1)}, bf16[24,1536]{1,0:T(8,128)(2,1)S(1)}, u32[]{:S(2)}, u32[]{:S(2)}) %collective-permute-start.34) | collective-permute-done | bytes 73760 | tf_op jit(solution)/shard_map/ppermute | solution.py:554
  97.0 0.7 pad_maximum_fusion
  98.1 0.6 convert_add_fusion.1
  (138 shorter events, 5.6 us)
Async XLA Ops:
  0.6 14.5 %copy-start.10 = (s32[768,1]{1,0:T(8,128)S(1)}, s32[768,1]{1,0:T(8,128)}, u32[]{:S(2)}) copy-start(s32[768,1]{1,0:T(8,128)} %constant.14.clone) | copy-start | bytes 9220
  0.6 14.5 %copy-start.11 = (s32[768,1]{1,0:T(8,128)S(1)}, s32[768,1]{1,0:T(8,128)}, u32[]{:S(2)}) copy-start(s32[768,1]{1,0:T(8,128)} %constant.15.clone) | copy-start | bytes 9220
  0.7 14.5 %copy-start.12 = (s32[768,1]{1,0:T(8,128)S(1)}, s32[768,1]{1,0:T(8,128)}, u32[]{:S(2)}) copy-start(s32[768,1]{1,0:T(8,128)} %constant.16.clone) | copy-start | bytes 9220
  0.7 14.5 %copy-start.13 = (s32[768,1]{1,0:T(8,128)S(1)}, s32[768,1]{1,0:T(8,128)}, u32[]{:S(2)}) copy-start(s32[768,1]{1,0:T(8,128)} %constant.17.clone) | copy-start | bytes 9220
  6.2 10.6 %collective-permute-start = (bf16[8,3072]{1,0:T(8,128)(2,1)}, bf16[8,3072]{1,0:T(8,128)(2,1)S(1)}, u32[]{:S(2)}, u32[]{:S(2)}) collective-permute-start(bf16[8,3072]{1,0:T(8,128)(2,1)} %get-tuple-element.104), channel_id=1, source_target_pairs={{0,8},{1,9},{2,10},{3,11},{4,12},{5,13},{6,14},{7,15},{8,0},{9,1},... | collective-permute-start | bytes 147464 | tf_op jit(solution)/shard_map/ppermute | solution.py:554
  9.3 7.9 %collective-permute-start.1 = (bf16[8,3072]{1,0:T(8,128)(2,1)}, bf16[8,3072]{1,0:T(8,128)(2,1)S(1)}, u32[]{:S(2)}, u32[]{:S(2)}) collective-permute-start(bf16[8,3072]{1,0:T(8,128)(2,1)} %get-tuple-element.104), channel_id=1, source_target_pairs={{0,16},{1,17},{2,18},{3,19},{4,20},{5,21},{6,22},{7,23},{8,24},{9,... | collective-permute-start | bytes 147464 | tf_op jit(solution)/shard_map/ppermute | solution.py:554
  11.9 6.1 %collective-permute-start.2 = (bf16[8,3072]{1,0:T(8,128)(2,1)}, bf16[8,3072]{1,0:T(8,128)(2,1)S(1)}, u32[]{:S(2)}, u32[]{:S(2)}) collective-permute-start(bf16[8,3072]{1,0:T(8,128)(2,1)} %get-tuple-element.104), channel_id=1, source_target_pairs={{0,24},{1,25},{2,26},{3,27},{4,28},{5,29},{6,30},{7,31},{8,16},{9,... | collective-permute-start | bytes 147464 | tf_op jit(solution)/shard_map/ppermute | solution.py:554
  11.9 6.1 %collective-permute-start.3 = (bf16[32,1536]{1,0:T(8,128)(2,1)}, bf16[32,1536]{1,0:T(8,128)(2,1)S(1)}, u32[]{:S(2)}, u32[]{:S(2)}) collective-permute-start(bf16[32,1536]{1,0:T(8,128)(2,1)} %get-tuple-element.68), channel_id=1, source_target_pairs={{0,2},{1,3},{2,0},{3,1},{4,6},{5,7},{6,4},{7,5},{8,10},{9,11},{10,... | collective-permute-start | bytes 294920 | tf_op jit(solution)/shard_map/ppermute | solution.py:554
  13.6 5.1 %collective-permute-start.4 = (bf16[32,1536]{1,0:T(8,128)(2,1)}, bf16[32,1536]{1,0:T(8,128)(2,1)S(1)}, u32[]{:S(2)}, u32[]{:S(2)}) collective-permute-start(bf16[32,1536]{1,0:T(8,128)(2,1)} %get-tuple-element.68), channel_id=1, source_target_pairs={{0,4},{1,5},{2,6},{3,7},{4,0},{5,1},{6,2},{7,3},{8,12},{9,13},{10,... | collective-permute-start | bytes 294920 | tf_op jit(solution)/shard_map/ppermute | solution.py:554
  15.2 7.5 %copy-start.8 = (bf16[256,768]{1,0:T(8,128)(2,1)S(1)}, bf16[256,768]{1,0:T(8,128)(2,1)}, u32[]{:S(2)}) copy-start(bf16[256,768]{1,0:T(8,128)(2,1)} %get-tuple-element.71.v) | copy-start | bytes 1179652
  15.2 7.5 %copy-start.9 = (bf16[256,768]{1,0:T(8,128)(2,1)S(1)}, bf16[256,768]{1,0:T(8,128)(2,1)}, u32[]{:S(2)}) copy-start(bf16[256,768]{1,0:T(8,128)(2,1)} %get-tuple-element.72.g) | copy-start | bytes 1179652
  16.9 5.7 %collective-permute-start.5 = (bf16[32,1536]{1,0:T(8,128)(2,1)S(1)}, bf16[32,1536]{1,0:T(8,128)(2,1)S(1)}, u32[]{:S(2)}, u32[]{:S(2)}) collective-permute-start(bf16[32,1536]{1,0:T(8,128)(2,1)S(1)} %copy-done.15), channel_id=1, source_target_pairs={{0,6},{1,7},{2,4},{3,5},{4,2},{5,3},{6,0},{7,1},{8,14},{9,15},{10,... | collective-permute-start | bytes 294920 | tf_op jit(solution)/shard_map/ppermute | solution.py:554
  18.7 6.6 %collective-permute-start.7 = (bf16[32,1536]{1,0:T(8,128)(2,1)S(1)}, bf16[32,1536]{1,0:T(8,128)(2,1)S(1)}, u32[]{:S(2)}, u32[]{:S(2)}) collective-permute-start(bf16[32,1536]{1,0:T(8,128)(2,1)S(1)} %pad_maximum_fusion.1), channel_id=1, source_target_pairs={{0,2},{1,3},{2,0},{3,1},{4,6},{5,7},{6,4},{7,5},{8,10},{9,11},{10,... | collective-permute-start | bytes 294920 | tf_op jit(solution)/shard_map/ppermute | solution.py:554
  19.6 5.7 %collective-permute-start.8 = (bf16[32,1536]{1,0:T(8,128)(2,1)S(1)}, bf16[32,1536]{1,0:T(8,128)(2,1)S(1)}, u32[]{:S(2)}, u32[]{:S(2)}) collective-permute-start(bf16[32,1536]{1,0:T(8,128)(2,1)S(1)} %pad_maximum_fusion.1), channel_id=1, source_target_pairs={{0,4},{1,5},{2,6},{3,7},{4,0},{5,1},{6,2},{7,3},{8,12},{9,13},{10,... | collective-permute-start | bytes 294920 | tf_op jit(solution)/shard_map/ppermute | solution.py:554
  21.6 5.5 %collective-permute-start.9 = (bf16[32,1536]{1,0:T(8,128)(2,1)S(1)}, bf16[32,1536]{1,0:T(8,128)(2,1)S(1)}, u32[]{:S(2)}, u32[]{:S(2)}) collective-permute-start(bf16[32,1536]{1,0:T(8,128)(2,1)S(1)} %pad_maximum_fusion.1), channel_id=1, source_target_pairs={{0,6},{1,7},{2,4},{3,5},{4,2},{5,3},{6,0},{7,1},{8,14},{9,15},{10,... | collective-permute-start | bytes 294920 | tf_op jit(solution)/shard_map/ppermute | solution.py:554
  22.6 4.6 %collective-permute-start.6 = (bf16[128,1536]{1,0:T(8,128)(2,1)S(1)}, bf16[128,1536]{1,0:T(8,128)(2,1)S(1)}, u32[]{:S(2)}, u32[]{:S(2)}) collective-permute-start(bf16[128,1536]{1,0:T(8,128)(2,1)S(1)} %constant_dynamic-update-slice_fusion.mid_0), channel_id=1, source_target_pairs={{0,1},{1,0},{2,3},{3,2},{4,5},{5,4},{6,7},{7,6},{8,9},{9,8},{10,11... | collective-permute-start | bytes 1179656 | tf_op jit(solution)/shard_map/ppermute | solution.py:554
  27.2 1.8 %collective-permute-start.10 = (bf16[128,1536]{1,0:T(8,128)(2,1)S(1)}, bf16[128,1536]{1,0:T(8,128)(2,1)S(1)}, u32[]{:S(2)}, u32[]{:S(2)}) collective-permute-start(bf16[128,1536]{1,0:T(8,128)(2,1)S(1)} %constant_dynamic-update-slice_fusion.4.far_0), channel_id=1, source_target_pairs={{0,1},{1,0},{2,3},{3,2},{4,5},{5,4},{6,7},{7,6},{8,9},{9,8},{10,11... | collective-permute-start | bytes 1179656 | tf_op jit(solution)/shard_map/ppermute | solution.py:554
  31.3 9.9 %copy-start.2 = (bf16[768,768]{1,0:T(8,128)(2,1)S(1)}, bf16[768,768]{1,0:T(8,128)(2,1)}, u32[]{:S(2)}) copy-start(bf16[768,768]{1,0:T(8,128)(2,1)} %w_out.1) | copy-start | bytes 3538948
  31.3 6.2 %collective-permute-start.11 = (f32[8,128]{1,0:T(8,128)S(1)}, f32[8,128]{1,0:T(8,128)S(1)}, u32[]{:S(2)}, u32[]{:S(2)}) collective-permute-start(f32[8,128]{1,0:T(8,128)S(1)} %slice.130), channel_id=1, source_target_pairs={{0,8},{1,9},{2,10},{3,11},{4,12},{5,13},{6,14},{7,15},{8,0},{9,1},... | collective-permute-start | bytes 12296 | tf_op jit(solution)/shard_map/ppermute | solution.py:554
  34.0 20.0 %collective-permute-start.17 = (bf16[64,1536]{1,0:T(8,128)(2,1)S(1)}, bf16[64,1536]{1,0:T(8,128)(2,1)S(1)}, u32[]{:S(2)}, u32[]{:S(2)}) collective-permute-start(bf16[64,1536]{1,0:T(8,128)(2,1)S(1)} %constant_dynamic-update-slice_fusion.14), channel_id=1, source_target_pairs={{0,2},{1,3},{2,0},{3,1},{4,6},{5,7},{6,4},{7,5},{8,10},{9,11},{10,... | collective-permute-start | bytes 589832 | tf_op jit(solution)/shard_map/ppermute | solution.py:554
  35.5 18.5 %collective-permute-start.18 = (bf16[64,1536]{1,0:T(8,128)(2,1)S(1)}, bf16[64,1536]{1,0:T(8,128)(2,1)S(1)}, u32[]{:S(2)}, u32[]{:S(2)}) collective-permute-start(bf16[64,1536]{1,0:T(8,128)(2,1)S(1)} %constant_dynamic-update-slice_fusion.14), channel_id=1, source_target_pairs={{0,4},{1,5},{2,6},{3,7},{4,0},{5,1},{6,2},{7,3},{8,12},{9,13},{10,... | collective-permute-start | bytes 589832 | tf_op jit(solution)/shard_map/ppermute | solution.py:554
  35.7 18.9 %collective-permute-start.19 = (bf16[64,1536]{1,0:T(8,128)(2,1)S(1)}, bf16[64,1536]{1,0:T(8,128)(2,1)S(1)}, u32[]{:S(2)}, u32[]{:S(2)}) collective-permute-start(bf16[64,1536]{1,0:T(8,128)(2,1)S(1)} %constant_dynamic-update-slice_fusion.14), channel_id=1, source_target_pairs={{0,6},{1,7},{2,4},{3,5},{4,2},{5,3},{6,0},{7,1},{8,14},{9,15},{10,... | collective-permute-start | bytes 589832 | tf_op jit(solution)/shard_map/ppermute | solution.py:554
  37.5 6.3 %collective-permute-start.15 = (bf16[256,768]{1,0:T(8,128)(2,1)S(1)}, bf16[256,768]{1,0:T(8,128)(2,1)S(1)}, u32[]{:S(2)}, u32[]{:S(2)}) collective-permute-start(bf16[256,768]{1,0:T(8,128)(2,1)S(1)} %copy-done.4), channel_id=1, source_target_pairs={{0,1},{1,0},{2,3},{3,2},{4,5},{5,4},{6,7},{7,6},{8,9},{9,8},{10,11... | collective-permute-start | bytes 1179656 | tf_op jit(solution)/shard_map/ppermute | solution.py:554
  37.5 6.1 %collective-permute-start.12 = (f32[16,128]{1,0:T(8,128)S(1)}, f32[16,128]{1,0:T(8,128)S(1)}, u32[]{:S(2)}, u32[]{:S(2)}) collective-permute-start(f32[16,128]{1,0:T(8,128)S(1)} %constant_dynamic-update-slice_fusion.8), channel_id=1, source_target_pairs={{0,16},{1,17},{2,18},{3,19},{4,20},{5,21},{6,22},{7,23},{8,24},{9,... | collective-permute-start | bytes 24584 | tf_op jit(solution)/shard_map/ppermute | solution.py:554
  43.6 1.4 %collective-permute-start.14 = (bf16[384,256]{1,0:T(8,128)(2,1)S(1)}, bf16[384,256]{1,0:T(8,128)(2,1)S(1)}, u32[]{:S(2)}, u32[]{:S(2)}) collective-permute-start(bf16[384,256]{1,0:T(8,128)(2,1)S(1)} %get-tuple-element.92), channel_id=1, source_target_pairs={{0,1},{1,0},{2,3},{3,2},{4,5},{5,4},{6,7},{7,6},{8,9},{9,8},{10,11... | collective-permute-start | bytes 589832 | tf_op jit(solution)/shard_map/ppermute | solution.py:554
  43.8 4.0 %collective-permute-start.13 = (f32[32,256]{1,0:T(8,128)S(1)}, f32[32,256]{1,0:T(8,128)S(1)}, u32[]{:S(2)}, u32[]{:S(2)}) collective-permute-start(f32[32,256]{1,0:T(8,128)S(1)} %pad_maximum_fusion.2), channel_id=1, source_target_pairs={{0,4},{1,5},{2,6},{3,7},{4,0},{5,1},{6,2},{7,3},{8,12},{9,13},{10,... | collective-permute-start | bytes 98312 | tf_op jit(solution)/shard_map/ppermute | solution.py:554
  47.8 7.0 %collective-permute-start.21 = (f32[64,256]{1,0:T(8,128)S(1)}, f32[64,256]{1,0:T(8,128)S(1)}, u32[]{:S(2)}, u32[]{:S(2)}) collective-permute-start(f32[64,256]{1,0:T(8,128)S(1)} %constant_dynamic-update-slice_fusion.12), channel_id=1, source_target_pairs={{0,2},{1,3},{2,0},{3,1},{4,6},{5,7},{6,4},{7,5},{8,10},{9,11},{10,... | collective-permute-start | bytes 196616 | tf_op jit(solution)/shard_map/ppermute | solution.py:554
  49.4 8.6 %collective-permute-start.36 = (bf16[192,768]{1,0:T(8,128)(2,1)S(1)}, bf16[192,768]{1,0:T(8,128)(2,1)S(1)}, u32[]{:S(2)}, u32[]{:S(2)}) collective-permute-start(bf16[192,768]{1,0:T(8,128)(2,1)S(1)} %get-tuple-element.131), channel_id=1, source_target_pairs={{0,2},{1,3},{2,0},{3,1},{4,6},{5,7},{6,4},{7,5},{8,10},{9,11},{10,... | collective-permute-start | bytes 884744 | tf_op jit(solution)/shard_map/ppermute | solution.py:554
  54.0 4.0 %collective-permute-start.16 = (bf16[768,256]{1,0:T(8,128)(2,1)S(1)}, bf16[768,256]{1,0:T(8,128)(2,1)S(1)}, u32[]{:S(2)}, u32[]{:S(2)}) collective-permute-start(bf16[768,256]{1,0:T(8,128)(2,1)S(1)} %get-tuple-element.101), channel_id=1, source_target_pairs={{0,1},{1,0},{2,3},{3,2},{4,5},{5,4},{6,7},{7,6},{8,9},{9,8},{10,11... | collective-permute-start | bytes 1179656 | tf_op jit(solution)/shard_map/ppermute | solution.py:554
  54.1 3.9 %collective-permute-start.23 = (bf16[256,768]{1,0:T(8,128)(2,1)S(1)}, bf16[256,768]{1,0:T(8,128)(2,1)S(1)}, u32[]{:S(2)}, u32[]{:S(2)}) collective-permute-start(bf16[256,768]{1,0:T(8,128)(2,1)S(1)} %get-tuple-element.119.right.dq), channel_id=1, source_target_pairs={{0,1},{1,0},{2,3},{3,2},{4,5},{5,4},{6,7},{7,6},{8,9},{9,8},{10,11... | collective-permute-start | bytes 1179656 | tf_op jit(solution)/shard_map/ppermute | solution.py:554
  54.6 3.9 %collective-permute-start.20 = (bf16[256,1536]{1,0:T(8,128)(2,1)S(1)}, bf16[256,1536]{1,0:T(8,128)(2,1)S(1)}, u32[]{:S(2)}, u32[]{:S(2)}) collective-permute-start(bf16[256,1536]{1,0:T(8,128)(2,1)S(1)} %constant_dynamic-update-slice_fusion.19.qg_0), channel_id=1, source_target_pairs={{0,1},{1,0},{2,3},{3,2},{4,5},{5,4},{6,7},{7,6},{8,9},{9,8},{10,11... | collective-permute-start | bytes 2359304 | tf_op jit(solution)/shard_map/ppermute | solution.py:554
  54.9 3.6 %collective-permute-start.22 = (f32[256,128]{1,0:T(8,128)S(1)}, f32[256,128]{1,0:T(8,128)S(1)}, u32[]{:S(2)}, u32[]{:S(2)}) collective-permute-start(f32[256,128]{1,0:T(8,128)S(1)} %constant_dynamic-update-slice_fusion.23.stats_0), channel_id=1, source_target_pairs={{0,1},{1,0},{2,3},{3,2},{4,5},{5,4},{6,7},{7,6},{8,9},{9,8},{10,11... | collective-permute-start | bytes 393224 | tf_op jit(solution)/shard_map/ppermute | solution.py:554
  60.9 2.0 %collective-permute-start.24 = (bf16[256,768]{1,0:T(8,128)(2,1)S(1)}, bf16[256,768]{1,0:T(8,128)(2,1)S(1)}, u32[]{:S(2)}, u32[]{:S(2)}) collective-permute-start(bf16[256,768]{1,0:T(8,128)(2,1)S(1)} %get-tuple-element.117.dk), channel_id=1, source_target_pairs={{0,1},{1,0},{2,3},{3,2},{4,5},{5,4},{6,7},{7,6},{8,9},{9,8},{10,11... | collective-permute-start | bytes 1179656 | tf_op jit(solution)/shard_map/ppermute | solution.py:554
  61.0 2.3 %collective-permute-start.25 = (bf16[256,768]{1,0:T(8,128)(2,1)S(1)}, bf16[256,768]{1,0:T(8,128)(2,1)S(1)}, u32[]{:S(2)}, u32[]{:S(2)}) collective-permute-start(bf16[256,768]{1,0:T(8,128)(2,1)S(1)} %get-tuple-element.118.dv), channel_id=1, source_target_pairs={{0,1},{1,0},{2,3},{3,2},{4,5},{5,4},{6,7},{7,6},{8,9},{9,8},{10,11... | collective-permute-start | bytes 1179656 | tf_op jit(solution)/shard_map/ppermute | solution.py:554
  61.5 17.0 %collective-permute-start.37 = (bf16[96,768]{1,0:T(8,128)(2,1)S(1)}, bf16[96,768]{1,0:T(8,128)(2,1)S(1)}, u32[]{:S(2)}, u32[]{:S(2)}) collective-permute-start(bf16[96,768]{1,0:T(8,128)(2,1)S(1)} %get-tuple-element.138), channel_id=1, source_target_pairs={{0,4},{1,5},{2,6},{3,7},{4,0},{5,1},{6,2},{7,3},{8,12},{9,13},{10,... | collective-permute-start | bytes 442376 | tf_op jit(solution)/shard_map/ppermute | solution.py:554
  61.9 8.8 %collective-permute-start.26 = (bf16[192,768]{1,0:T(8,128)(2,1)S(1)}, bf16[192,768]{1,0:T(8,128)(2,1)S(1)}, u32[]{:S(2)}, u32[]{:S(2)}) collective-permute-start(bf16[192,768]{1,0:T(8,128)(2,1)S(1)} %get-tuple-element.133), channel_id=1, source_target_pairs={{0,8},{1,9},{2,10},{3,11},{4,12},{5,13},{6,14},{7,15},{8,0},{9,1},... | collective-permute-start | bytes 884744 | tf_op jit(solution)/shard_map/ppermute | solution.py:554
  63.2 13.4 %copy-start = (bf16[768,2304]{1,0:T(8,128)(2,1)S(1)}, bf16[768,2304]{1,0:T(8,128)(2,1)}, u32[]{:S(2)}) copy-start(bf16[768,2304]{1,0:T(8,128)(2,1)} %w_qkv.1) | copy-start | bytes 10616836
  64.1 14.4 %collective-permute-start.28 = (bf16[96,1536]{1,0:T(8,128)(2,1)S(1)}, bf16[96,1536]{1,0:T(8,128)(2,1)S(1)}, u32[]{:S(2)}, u32[]{:S(2)}) collective-permute-start(bf16[96,1536]{1,0:T(8,128)(2,1)S(1)} %get-tuple-element.128), channel_id=1, source_target_pairs={{0,2},{1,3},{2,0},{3,1},{4,6},{5,7},{6,4},{7,5},{8,10},{9,11},{10,... | collective-permute-start | bytes 884744 | tf_op jit(solution)/shard_map/ppermute | solution.py:554
  70.8 9.2 %collective-permute-start.27 = (bf16[96,768]{1,0:T(8,128)(2,1)S(1)}, bf16[96,768]{1,0:T(8,128)(2,1)S(1)}, u32[]{:S(2)}, u32[]{:S(2)}) collective-permute-start(bf16[96,768]{1,0:T(8,128)(2,1)S(1)} %get-tuple-element.140), channel_id=1, source_target_pairs={{0,16},{1,17},{2,18},{3,19},{4,20},{5,21},{6,22},{7,23},{8,24},{9,... | collective-permute-start | bytes 442376 | tf_op jit(solution)/shard_map/ppermute | solution.py:554
  73.9 13.9 %collective-permute-start.31 = (bf16[96,1536]{1,0:T(8,128)(2,1)S(1)}, bf16[96,1536]{1,0:T(8,128)(2,1)S(1)}, u32[]{:S(2)}, u32[]{:S(2)}) collective-permute-start(bf16[96,1536]{1,0:T(8,128)(2,1)S(1)} %get-tuple-element.130), channel_id=1, source_target_pairs={{0,4},{1,5},{2,6},{3,7},{4,0},{5,1},{6,2},{7,3},{8,12},{9,13},{10,... | collective-permute-start | bytes 884744 | tf_op jit(solution)/shard_map/ppermute | solution.py:554
  74.8 13.0 %collective-permute-start.32 = (bf16[96,1536]{1,0:T(8,128)(2,1)S(1)}, bf16[96,1536]{1,0:T(8,128)(2,1)S(1)}, u32[]{:S(2)}, u32[]{:S(2)}) collective-permute-start(bf16[96,1536]{1,0:T(8,128)(2,1)S(1)} %get-tuple-element.129), channel_id=1, source_target_pairs={{0,6},{1,7},{2,4},{3,5},{4,2},{5,3},{6,0},{7,1},{8,14},{9,15},{10,... | collective-permute-start | bytes 884744 | tf_op jit(solution)/shard_map/ppermute | solution.py:554
  78.5 13.8 %collective-permute-start.38 = (bf16[48,768]{1,0:T(8,128)(2,1)S(1)}, bf16[48,768]{1,0:T(8,128)(2,1)S(1)}, u32[]{:S(2)}, u32[]{:S(2)}) collective-permute-start(bf16[48,768]{1,0:T(8,128)(2,1)S(1)} %slice.192), channel_id=1, source_target_pairs={{0,8},{1,9},{2,10},{3,11},{4,12},{5,13},{6,14},{7,15},{8,0},{9,1},... | collective-permute-start | bytes 221192 | tf_op jit(solution)/shard_map/ppermute | solution.py:554
  80.0 12.5 %collective-permute-start.29 = (bf16[48,768]{1,0:T(8,128)(2,1)S(1)}, bf16[48,768]{1,0:T(8,128)(2,1)S(1)}, u32[]{:S(2)}, u32[]{:S(2)}) collective-permute-start(bf16[48,768]{1,0:T(8,128)(2,1)S(1)} %slice.177), channel_id=1, source_target_pairs={{0,2},{1,3},{2,0},{3,1},{4,6},{5,7},{6,4},{7,5},{8,10},{9,11},{10,... | collective-permute-start | bytes 221192 | tf_op jit(solution)/shard_map/ppermute | solution.py:554
  87.9 5.6 %collective-permute-start.33 = (bf16[24,1536]{1,0:T(8,128)(2,1)S(1)}, bf16[24,1536]{1,0:T(8,128)(2,1)S(1)}, u32[]{:S(2)}, u32[]{:S(2)}) collective-permute-start(bf16[24,1536]{1,0:T(8,128)(2,1)S(1)} %get-tuple-element.142), channel_id=1, source_target_pairs={{0,8},{1,9},{2,10},{3,11},{4,12},{5,13},{6,14},{7,15},{8,0},{9,1},... | collective-permute-start | bytes 221192 | tf_op jit(solution)/shard_map/ppermute | solution.py:554
  88.3 8.6 %collective-permute-start.34 = (bf16[24,1536]{1,0:T(8,128)(2,1)S(1)}, bf16[24,1536]{1,0:T(8,128)(2,1)S(1)}, u32[]{:S(2)}, u32[]{:S(2)}) collective-permute-start(bf16[24,1536]{1,0:T(8,128)(2,1)S(1)} %get-tuple-element.144), channel_id=1, source_target_pairs={{0,16},{1,17},{2,18},{3,19},{4,20},{5,21},{6,22},{7,23},{8,24},{9,... | collective-permute-start | bytes 221192 | tf_op jit(solution)/shard_map/ppermute | solution.py:554
  88.8 8.2 %collective-permute-start.35 = (bf16[24,1536]{1,0:T(8,128)(2,1)S(1)}, bf16[24,1536]{1,0:T(8,128)(2,1)S(1)}, u32[]{:S(2)}, u32[]{:S(2)}) collective-permute-start(bf16[24,1536]{1,0:T(8,128)(2,1)S(1)} %get-tuple-element.143), channel_id=1, source_target_pairs={{0,24},{1,25},{2,26},{3,27},{4,28},{5,29},{6,30},{7,31},{8,16},{9,... | collective-permute-start | bytes 221192 | tf_op jit(solution)/shard_map/ppermute | solution.py:554
  92.4 5.7 %collective-permute-start.39 = (bf16[24,768]{1,0:T(8,128)(2,1)S(1)}, bf16[24,768]{1,0:T(8,128)(2,1)S(1)}, u32[]{:S(2)}, u32[]{:S(2)}) collective-permute-start(bf16[24,768]{1,0:T(8,128)(2,1)S(1)} %slice.194), channel_id=1, source_target_pairs={{0,16},{1,17},{2,18},{3,19},{4,20},{5,21},{6,22},{7,23},{8,24},{9,... | collective-permute-start | bytes 110600 | tf_op jit(solution)/shard_map/ppermute | solution.py:554
  92.5 4.4 %collective-permute-start.30 = (bf16[24,768]{1,0:T(8,128)(2,1)S(1)}, bf16[24,768]{1,0:T(8,128)(2,1)S(1)}, u32[]{:S(2)}, u32[]{:S(2)}) collective-permute-start(bf16[24,768]{1,0:T(8,128)(2,1)S(1)} %slice.179), channel_id=1, source_target_pairs={{0,4},{1,5},{2,6},{3,7},{4,0},{5,1},{6,2},{7,3},{8,12},{9,13},{10,... | collective-permute-start | bytes 110600 | tf_op jit(solution)/shard_map/ppermute | solution.py:554
  (9 other events, 43.1 us)

commit v8 on v7

--- a/solution.py
+++ b/solution.py
@@ -759,8 +759,8 @@
         cost=LOW_COST,
     )(after(dq, late_half), dk, dv, w_qkv)
     late_parts = block_parts(late_half, PLANE, n)
-    early = halved(early_half, masks + [2, 4], n, ((dk_other,), (late_parts[1],)))
-    grad_wout = halved(wout_half, [2, 4] + masks, n, ((dk_near,), (late_parts[1],)))
+    early = halved(early_half, masks + [2, 4], n, ((late_parts[1],),))
+    grad_wout = halved(wout_half, [2, 4] + masks, n, ((dk,), (late_parts[1],)))
     late = reduce_all(sum_parts(late_parts, BF), upper_steps(n)[::-1], n)
     grad_wqkv = jnp.concatenate([early, late], axis=1)
     return out_rows, grad_tiles, grad_wqkv, grad_wout

time: 98.9 us -> 101 us (1.021)
  starting transfers between devices: 40.9 us -> 42.1 us
    ppermute x40, starting transfers between devices: 40.9 us -> 42.1 us  [swap(): return lax.ppermute(value, 'ctx', [(d, d ^ mask) for d in range(dev_count)])]
  transfers between devices with their start and end apart: 40 -> 40, of which waited for: 14 -> 15; matrix products, arithmetic and copies ran while one was open for 2% -> 2% of each run, Pallas kernels for 15% -> 15%
where the time goes in v8:
time: 101 us
  starting transfers between devices  42.1 us (42%)
  waiting for transfers between devices  28.6 us (28%)
  Pallas kernels  24.8 us (25%)
  between operations  2.07 us (2%)
  other arithmetic  1.94 us (2%)
  local copies, waits for them, and re-layouts  1.25 us (1%)
    ppermute x40, starting transfers between devices, swap(): return lax.ppermute(value, 'ctx', [(d, d ^ mask) for d in range(dev_count)])  42.1 us
    ppermute x40, waiting for transfers between devices, swap(): return lax.ppermute(value, 'ctx', [(d, d ^ mask) for d in range(dev_count)])  28.6 us
    pallas_call x11, Pallas kernels, run(): pl.pallas_call(kernel, out_shape=tuple((jax.ShapeDtypeStruct(s, t) for s,...  24.8 us
  transfers between devices with their start and end apart: 40, of which 15 were waited for; matrix products, arithmetic and copies ran while one was open for 2% of the time, Pallas kernels for 15%

profile of v8, /device:TPU:0, one launch (start us, length us, event | category | flops | bytes accessed | tf_op | source)
XLA Modules:
  0.0 100.8 jit_solution(1562283443367876789)
XLA Ops:
  0.7 5.6 %shard_map.147 = (bf16[256,768]{1,0:T(8,128)(2,1)}, bf16[256,768]{1,0:T(8,128)(2,1)}, bf16[256,768]{1,0:T(8,128)(2,1)}, bf16[256,768]{1,0:T(8,128)(2,1)}, bf16[6...) custom-call(s32[2,12]{1,0:T(2,128)} %offs_ref.9, ...), custom_call_target="tpu_custom_call" | custom-call | flops 1207959552 | bytes 7716960 | tf_op jit(solution)/shard_map/pallas_call | solution.py:535
  6.3 5.1 %collective-permute-start.2 = (bf16[8,3072]{1,0:T(8,128)(2,1)}, bf16[8,3072]{1,0:T(8,128)(2,1)S(1)}, u32[]{:S(2)}, u32[]{:S(2)}) collective-permute-start(bf16[8,3072]{1,0:T(8,128)(2,1)} %get-tuple-element.102), channel_id=1, source_target_pairs={{0,24},{1,25},{2,26},{3,27},{4,28},{5,29},{6,30},{7,31},{8,16},{9,... | collective-permute-start | bytes 147464 | tf_op jit(solution)/shard_map/ppermute | solution.py:554
  11.4 0.6 collective-permute-start
  12.0 2.6 %collective-permute-start.5 = (bf16[32,1536]{1,0:T(8,128)(2,1)}, bf16[32,1536]{1,0:T(8,128)(2,1)S(1)}, u32[]{:S(2)}, u32[]{:S(2)}) collective-permute-start(bf16[32,1536]{1,0:T(8,128)(2,1)} %get-tuple-element.66), channel_id=1, source_target_pairs={{0,6},{1,7},{2,4},{3,5},{4,2},{5,3},{6,0},{7,1},{8,14},{9,15},{10,... | collective-permute-start | bytes 294920 | tf_op jit(solution)/shard_map/ppermute | solution.py:554
  14.6 0.5 collective-permute-start.4
  15.3 0.7 copy-done.15
  17.3 2.1 %collective-permute-done.4 = bf16[32,1536]{1,0:T(8,128)(2,1)S(1)} collective-permute-done((bf16[32,1536]{1,0:T(8,128)(2,1)}, bf16[32,1536]{1,0:T(8,128)(2,1)S(1)}, u32[]{:S(2)}, u32[]{:S(2)}) %collective-permute-start.4) | collective-permute-done | bytes 98336 | tf_op jit(solution)/shard_map/ppermute | solution.py:554
  19.4 2.1 %collective-permute-done.3 = bf16[32,1536]{1,0:T(8,128)(2,1)S(1)} collective-permute-done((bf16[32,1536]{1,0:T(8,128)(2,1)S(1)}, bf16[32,1536]{1,0:T(8,128)(2,1)S(1)}, u32[]{:S(2)}, u32[]{:S(2)}) %collective-permute-start.3) | collective-permute-done | bytes 98336 | tf_op jit(solution)/shard_map/ppermute | solution.py:554
  21.5 1.5 %collective-permute-start.9 = (bf16[32,1536]{1,0:T(8,128)(2,1)S(1)}, bf16[32,1536]{1,0:T(8,128)(2,1)S(1)}, u32[]{:S(2)}, u32[]{:S(2)}) collective-permute-start(bf16[32,1536]{1,0:T(8,128)(2,1)S(1)} %pad_maximum_fusion.1), channel_id=1, source_target_pairs={{0,6},{1,7},{2,4},{3,5},{4,2},{5,3},{6,0},{7,1},{8,14},{9,15},{10,... | collective-permute-start | bytes 294920 | tf_op jit(solution)/shard_map/ppermute | solution.py:554
  23.4 1.6 %collective-permute-start.7 = (bf16[32,1536]{1,0:T(8,128)(2,1)S(1)}, bf16[32,1536]{1,0:T(8,128)(2,1)S(1)}, u32[]{:S(2)}, u32[]{:S(2)}) collective-permute-start(bf16[32,1536]{1,0:T(8,128)(2,1)S(1)} %pad_maximum_fusion.1), channel_id=1, source_target_pairs={{0,2},{1,3},{2,0},{3,1},{4,6},{5,7},{6,4},{7,5},{8,10},{9,11},{10,... | collective-permute-start | bytes 294920 | tf_op jit(solution)/shard_map/ppermute | solution.py:554
  25.2 2.5 %shard_map.148 = (f32[256,768]{1,0:T(8,128)S(1)}, f32[256,128]{1,0:T(8,128)S(1)}, bf16[768,256]{1,0:T(8,128)(2,1)S(1)}, bf16[768,256]{1,0:T(8,128)(2,1)S(1)}) custom-call(s32[1]{0:T(128)S(6)} %copy.42.pad_ref, bf16[256,768]{1,0:T(8,128)(2,1)S(1)} %copy-done.6, bf16[256,768]{1,0:T(8,128)(2,1)S(1)} %copy-done.7, bf16[256,768]{1,0:T(8,128)(2,1)S(1)} %copy-done.8, ...), custom_call_target="tpu_custom_call" | custom-call | flops 805306368 | bytes 3676164 | tf_op jit(solution)/shard_map/pallas_call | solution.py:535
  28.4 1.6 %collective-permute-done.10.far_1 = bf16[128,1536]{1,0:T(8,128)(2,1)S(1)} collective-permute-done((bf16[128,1536]{1,0:T(8,128)(2,1)S(1)}, bf16[128,1536]{1,0:T(8,128)(2,1)S(1)}, u32[]{:S(2)}, u32[]{:S(2)}) %collective-permute-start.10) | collective-permute-done | bytes 393248 | tf_op jit(solution)/shard_map/ppermute | solution.py:554
  30.0 2.3 %shard_map.149 = (f32[256,128]{1,0:T(8,128)S(1)}, f32[64,128]{1,0:T(8,128)S(1)}, f32[64,128]{1,0:T(8,128)S(1)}, f32[64,768]{1,0:T(8,128)S(1)}) custom-call(s32[2,12]{1,0:T(2,128)S(1)} %copy-done.5, s32[1]{0:T(128)S(6)} %copy.42.pad_ref, bf16[64,3072]{1,0:T(8,128)(2,1)S(1)} %copy-done.1, bf16[128,1536]{1,0:T(8,128)(2,1)S(1)} %constant_dynamic-update-slice_fusion.mid_0, ...), custom_call_target="tpu_custom_call" | custom-call | flops 301989888 | bytes 2490468 | tf_op jit(solution)/shard_map/pallas_call | solution.py:535
  32.4 1.9 %shard_map.150.dq_sel = f32[64,768]{1,0:T(8,128)S(1)} custom-call(s32[2,12]{1,0:T(2,128)S(1)} %copy-done.5, s32[1]{0:T(128)S(6)} %copy.42.pad_ref, bf16[64,3072]{1,0:T(8,128)(2,1)S(1)} %copy-done.1, bf16[128,1536]{1,0:T(8,128)(2,1)S(1)} %constant_dynamic-update-slice_fusion.mid_0, bf16[128,1536]{1,0:T(8,128)(2,1)S(1)} %collective-permute-done.6.mid_1, ...), custom_call_target="tpu_custom_call" | custom-call | flops 201326592 | bytes 2195556 | tf_op jit(solution)/shard_map/pallas_call | solution.py:535
  34.2 1.3 %collective-permute-start.11 = (f32[8,128]{1,0:T(8,128)S(1)}, f32[8,128]{1,0:T(8,128)S(1)}, u32[]{:S(2)}, u32[]{:S(2)}) collective-permute-start(f32[8,128]{1,0:T(8,128)S(1)} %slice.130), channel_id=1, source_target_pairs={{0,8},{1,9},{2,10},{3,11},{4,12},{5,13},{6,14},{7,15},{8,0},{9,1},... | collective-permute-start | bytes 12296 | tf_op jit(solution)/shard_map/ppermute | solution.py:554
  35.6 2.5 %collective-permute-start.19 = (bf16[64,1536]{1,0:T(8,128)(2,1)S(1)}, bf16[64,1536]{1,0:T(8,128)(2,1)S(1)}, u32[]{:S(2)}, u32[]{:S(2)}) collective-permute-start(bf16[64,1536]{1,0:T(8,128)(2,1)S(1)} %constant_dynamic-update-slice_fusion.14), channel_id=1, source_target_pairs={{0,6},{1,7},{2,4},{3,5},{4,2},{5,3},{6,0},{7,1},{8,14},{9,15},{10,... | collective-permute-start | bytes 589832 | tf_op jit(solution)/shard_map/ppermute | solution.py:554
  38.1 0.5 collective-permute-start.18
  38.6 0.6 collective-permute-start.17
  39.2 3.0 %collective-permute-start.12 = (f32[16,128]{1,0:T(8,128)S(1)}, f32[16,128]{1,0:T(8,128)S(1)}, u32[]{:S(2)}, u32[]{:S(2)}) collective-permute-start(f32[16,128]{1,0:T(8,128)S(1)} %constant_dynamic-update-slice_fusion.8), channel_id=1, source_target_pairs={{0,16},{1,17},{2,18},{3,19},{4,20},{5,21},{6,22},{7,23},{8,24},{9,... | collective-permute-start | bytes 24584 | tf_op jit(solution)/shard_map/ppermute | solution.py:554
  42.2 2.5 %shard_map.151 = (bf16[256,768]{1,0:T(8,128)(2,1)}, bf16[384,256]{1,0:T(8,128)(2,1)S(1)}, bf16[384,256]{1,0:T(8,128)(2,1)S(1)}) custom-call(s32[2,12]{1,0:T(2,128)S(1)} %copy-done.5, f32[256,128]{1,0:T(8,128)S(1)} %get-tuple-element.71.near_stats, f32[256,128]{1,0:T(8,128)S(1)} %get-tuple-element.78.stats, f32[64,128]{1,0:T(8,128)S(1)} %get-tuple-element.82.picked, ...), custom_call_target="tpu_custom_call" | custom-call | flops 905969664 | bytes 3673184 | tf_op jit(solution)/shard_map/pallas_call | solution.py:535
  44.9 1.5 %collective-permute-start.13 = (f32[32,256]{1,0:T(8,128)S(1)}, f32[32,256]{1,0:T(8,128)S(1)}, u32[]{:S(2)}, u32[]{:S(2)}) collective-permute-start(f32[32,256]{1,0:T(8,128)S(1)} %pad_maximum_fusion.2), channel_id=1, source_target_pairs={{0,4},{1,5},{2,6},{3,7},{4,0},{5,1},{6,2},{7,3},{8,12},{9,13},{10,... | collective-permute-start | bytes 98312 | tf_op jit(solution)/shard_map/ppermute | solution.py:554
  46.9 2.0 %collective-permute-done.13 = f32[32,256]{1,0:T(8,128)S(1)} collective-permute-done((f32[32,256]{1,0:T(8,128)S(1)}, f32[32,256]{1,0:T(8,128)S(1)}, u32[]{:S(2)}, u32[]{:S(2)}) %collective-permute-start.13) | collective-permute-done | bytes 32800 | tf_op jit(solution)/shard_map/ppermute | solution.py:554
  48.9 1.5 %collective-permute-start.21 = (f32[64,256]{1,0:T(8,128)S(1)}, f32[64,256]{1,0:T(8,128)S(1)}, u32[]{:S(2)}, u32[]{:S(2)}) collective-permute-start(f32[64,256]{1,0:T(8,128)S(1)} %constant_dynamic-update-slice_fusion.12), channel_id=1, source_target_pairs={{0,2},{1,3},{2,0},{3,1},{4,6},{5,7},{6,4},{7,5},{8,10},{9,11},{10,... | collective-permute-start | bytes 196616 | tf_op jit(solution)/shard_map/ppermute | solution.py:554
  50.5 4.1 %shard_map.153 = (bf16[256,768]{1,0:T(8,128)(2,1)S(1)}, f32[256,768]{1,0:T(8,128)S(1)}, f32[256,768]{1,0:T(8,128)S(1)}) custom-call(s32[2,12]{1,0:T(2,128)S(1)} %copy-done.5, s32[1]{0:T(128)S(6)} %copy.42.pad_ref, bf16[256,768]{1,0:T(8,128)(2,1)S(1)} %copy-done.6, bf16[256,768]{1,0:T(8,128)(2,1)S(1)} %copy-done.7, bf16[256,768]{1,0:T(8,128)(2,1)S(1)} %copy-done.8, ...), custom_call_target="tpu_custom_call" | custom-call | flops 805306368 | bytes 3866724 | tf_op jit(solution)/shard_map/pallas_call | solution.py:535
  55.1 0.7 collective-permute-start.36
  56.0 0.5 collective-permute-start.22
  57.4 1.0 %collective-permute-done.22.stats_1 = f32[256,128]{1,0:T(8,128)S(1)} collective-permute-done((f32[256,128]{1,0:T(8,128)S(1)}, f32[256,128]{1,0:T(8,128)S(1)}, u32[]{:S(2)}, u32[]{:S(2)}) %collective-permute-start.22) | collective-permute-done | bytes 131104 | tf_op jit(solution)/shard_map/ppermute | solution.py:554
  58.4 2.4 %shard_map.155 = (bf16[256,768]{1,0:T(8,128)(2,1)S(1)}, bf16[256,768]{1,0:T(8,128)(2,1)S(1)}) custom-call(s32[2,12]{1,0:T(2,128)S(1)} %copy-done.5, s32[1]{0:T(128)S(6)} %copy.42.pad_ref, bf16[64,3072]{1,0:T(8,128)(2,1)S(1)} %copy-done.1, bf16[256,1536]{1,0:T(8,128)(2,1)S(1)} %constant_dynamic-update-slice_fusion.19.qg_0, ...), custom_call_target="tpu_custom_call" | custom-call | flops 15099494 | bytes 229381 | tf_op jit(solution)/shard_map/pallas_call | solution.py:535
  60.9 3.2 %collective-permute-done.36 = bf16[192,768]{1,0:T(8,128)(2,1)S(1)} collective-permute-done((bf16[192,768]{1,0:T(8,128)(2,1)S(1)}, bf16[192,768]{1,0:T(8,128)(2,1)S(1)}, u32[]{:S(2)}, u32[]{:S(2)}) %collective-permute-start.36) | collective-permute-done | bytes 294944 | tf_op jit(solution)/shard_map/ppermute | solution.py:554
  64.3 1.6 %collective-permute-start.37 = (bf16[96,768]{1,0:T(8,128)(2,1)S(1)}, bf16[96,768]{1,0:T(8,128)(2,1)S(1)}, u32[]{:S(2)}, u32[]{:S(2)}) collective-permute-start(bf16[96,768]{1,0:T(8,128)(2,1)S(1)} %get-tuple-element.134), channel_id=1, source_target_pairs={{0,4},{1,5},{2,6},{3,7},{4,0},{5,1},{6,2},{7,3},{8,12},{9,13},{10,... | collective-permute-start | bytes 442376 | tf_op jit(solution)/shard_map/ppermute | solution.py:554
  65.9 0.8 shard_map.156
  66.8 0.7 collective-permute-start.27
  67.6 2.4 %collective-permute-start.32 = (bf16[96,1536]{1,0:T(8,128)(2,1)S(1)}, bf16[96,1536]{1,0:T(8,128)(2,1)S(1)}, u32[]{:S(2)}, u32[]{:S(2)}) collective-permute-start(bf16[96,1536]{1,0:T(8,128)(2,1)S(1)} %get-tuple-element.125), channel_id=1, source_target_pairs={{0,6},{1,7},{2,4},{3,5},{4,2},{5,3},{6,0},{7,1},{8,14},{9,15},{10,... | collective-permute-start | bytes 884744 | tf_op jit(solution)/shard_map/ppermute | solution.py:554
  70.0 0.5 collective-permute-start.31
  70.5 1.9 %shard_map.157 = bf16[256,768]{1,0:T(8,128)(2,1)} custom-call(bf16[256,768]{1,0:T(8,128)(2,1)S(1)} %get-tuple-element.117.right.dq, bf16[256,768]{1,0:T(8,128)(2,1)S(1)} %get-tuple-element.115.dk, bf16[256,768]{1,0:T(8,128)(2,1)S(1)} %get-tuple-element.116.dv, bf16[768,2304]{1,0:T(8,128)(2,1)S(1)} %copy-done), custom_call_target="tpu_custom_call" | custom-call | flops 45298484 | bytes 255590 | tf_op jit(solution)/shard_map/pallas_call | solution.py:535
  72.4 4.3 %collective-permute-done.27 = bf16[96,1536]{1,0:T(8,128)(2,1)S(1)} collective-permute-done((bf16[96,1536]{1,0:T(8,128)(2,1)S(1)}, bf16[96,1536]{1,0:T(8,128)(2,1)S(1)}, u32[]{:S(2)}, u32[]{:S(2)}) %collective-permute-start.27) | collective-permute-done | bytes 294944 | tf_op jit(solution)/shard_map/ppermute | solution.py:554
  77.0 2.5 %collective-permute-start.28 = (bf16[96,768]{1,0:T(8,128)(2,1)S(1)}, bf16[96,768]{1,0:T(8,128)(2,1)S(1)}, u32[]{:S(2)}, u32[]{:S(2)}) collective-permute-start(bf16[96,768]{1,0:T(8,128)(2,1)S(1)} %slice.175), channel_id=1, source_target_pairs={{0,16},{1,17},{2,18},{3,19},{4,20},{5,21},{6,22},{7,23},{8,24},{9,... | collective-permute-start | bytes 442376 | tf_op jit(solution)/shard_map/ppermute | solution.py:554
  79.5 3.8 %collective-permute-done.32 = bf16[96,1536]{1,0:T(8,128)(2,1)S(1)} collective-permute-done((bf16[96,1536]{1,0:T(8,128)(2,1)S(1)}, bf16[96,1536]{1,0:T(8,128)(2,1)S(1)}, u32[]{:S(2)}, u32[]{:S(2)}) %collective-permute-start.32) | collective-permute-done | bytes 294944 | tf_op jit(solution)/shard_map/ppermute | solution.py:554
  83.3 1.5 %collective-permute-done.31 = bf16[96,1536]{1,0:T(8,128)(2,1)S(1)} collective-permute-done((bf16[96,1536]{1,0:T(8,128)(2,1)S(1)}, bf16[96,1536]{1,0:T(8,128)(2,1)S(1)}, u32[]{:S(2)}, u32[]{:S(2)}) %collective-permute-start.31) | collective-permute-done | bytes 294944 | tf_op jit(solution)/shard_map/ppermute | solution.py:554
  85.0 1.7 %collective-permute-start.33 = (bf16[24,1536]{1,0:T(8,128)(2,1)S(1)}, bf16[24,1536]{1,0:T(8,128)(2,1)S(1)}, u32[]{:S(2)}, u32[]{:S(2)}) collective-permute-start(bf16[24,1536]{1,0:T(8,128)(2,1)S(1)} %get-tuple-element.136), channel_id=1, source_target_pairs={{0,8},{1,9},{2,10},{3,11},{4,12},{5,13},{6,14},{7,15},{8,0},{9,1},... | collective-permute-start | bytes 221192 | tf_op jit(solution)/shard_map/ppermute | solution.py:554
  86.7 1.7 %collective-permute-start.35 = (bf16[24,1536]{1,0:T(8,128)(2,1)S(1)}, bf16[24,1536]{1,0:T(8,128)(2,1)S(1)}, u32[]{:S(2)}, u32[]{:S(2)}) collective-permute-start(bf16[24,1536]{1,0:T(8,128)(2,1)S(1)} %get-tuple-element.137), channel_id=1, source_target_pairs={{0,24},{1,25},{2,26},{3,27},{4,28},{5,29},{6,30},{7,31},{8,16},{9,... | collective-permute-start | bytes 221192 | tf_op jit(solution)/shard_map/ppermute | solution.py:554
  88.6 2.8 %collective-permute-start.39 = (bf16[24,768]{1,0:T(8,128)(2,1)S(1)}, bf16[24,768]{1,0:T(8,128)(2,1)S(1)}, u32[]{:S(2)}, u32[]{:S(2)}) collective-permute-start(bf16[24,768]{1,0:T(8,128)(2,1)S(1)} %slice.194), channel_id=1, source_target_pairs={{0,16},{1,17},{2,18},{3,19},{4,20},{5,21},{6,22},{7,23},{8,24},{9,... | collective-permute-start | bytes 110600 | tf_op jit(solution)/shard_map/ppermute | solution.py:554
  91.5 0.9 collective-permute-start.29
  92.9 3.1 %collective-permute-done.34 = bf16[24,1536]{1,0:T(8,128)(2,1)S(1)} collective-permute-done((bf16[24,1536]{1,0:T(8,128)(2,1)S(1)}, bf16[24,1536]{1,0:T(8,128)(2,1)S(1)}, u32[]{:S(2)}, u32[]{:S(2)}) %collective-permute-start.34) | collective-permute-done | bytes 73760 | tf_op jit(solution)/shard_map/ppermute | solution.py:554
  96.0 0.8 collective-permute-start.30
  96.8 0.6 convert_add_fusion.1
  97.5 2.6 %collective-permute-done.30 = bf16[24,768]{1,0:T(8,128)(2,1)S(1)} collective-permute-done((bf16[24,768]{1,0:T(8,128)(2,1)S(1)}, bf16[24,768]{1,0:T(8,128)(2,1)S(1)}, u32[]{:S(2)}, u32[]{:S(2)}) %collective-permute-start.30) | collective-permute-done | bytes 36896 | tf_op jit(solution)/shard_map/ppermute | solution.py:554
  100.1 0.7 pad_maximum_fusion
  (138 shorter events, 5.9 us)
Async XLA Ops:
  0.6 14.5 %copy-start.10 = (s32[768,1]{1,0:T(8,128)S(1)}, s32[768,1]{1,0:T(8,128)}, u32[]{:S(2)}) copy-start(s32[768,1]{1,0:T(8,128)} %constant.17.clone) | copy-start | bytes 9220
  0.6 14.5 %copy-start.11 = (s32[768,1]{1,0:T(8,128)S(1)}, s32[768,1]{1,0:T(8,128)}, u32[]{:S(2)}) copy-start(s32[768,1]{1,0:T(8,128)} %constant.16.clone) | copy-start | bytes 9220
  0.7 14.5 %copy-start.12 = (s32[768,1]{1,0:T(8,128)S(1)}, s32[768,1]{1,0:T(8,128)}, u32[]{:S(2)}) copy-start(s32[768,1]{1,0:T(8,128)} %constant.15.clone) | copy-start | bytes 9220
  0.7 14.5 %copy-start.13 = (s32[768,1]{1,0:T(8,128)S(1)}, s32[768,1]{1,0:T(8,128)}, u32[]{:S(2)}) copy-start(s32[768,1]{1,0:T(8,128)} %constant.14.clone) | copy-start | bytes 9220
  6.3 10.6 %collective-permute-start.2 = (bf16[8,3072]{1,0:T(8,128)(2,1)}, bf16[8,3072]{1,0:T(8,128)(2,1)S(1)}, u32[]{:S(2)}, u32[]{:S(2)}) collective-permute-start(bf16[8,3072]{1,0:T(8,128)(2,1)} %get-tuple-element.102), channel_id=1, source_target_pairs={{0,24},{1,25},{2,26},{3,27},{4,28},{5,29},{6,30},{7,31},{8,16},{9,... | collective-permute-start | bytes 147464 | tf_op jit(solution)/shard_map/ppermute | solution.py:554
  11.4 5.9 %collective-permute-start.1 = (bf16[8,3072]{1,0:T(8,128)(2,1)}, bf16[8,3072]{1,0:T(8,128)(2,1)S(1)}, u32[]{:S(2)}, u32[]{:S(2)}) collective-permute-start(bf16[8,3072]{1,0:T(8,128)(2,1)} %get-tuple-element.102), channel_id=1, source_target_pairs={{0,16},{1,17},{2,18},{3,19},{4,20},{5,21},{6,22},{7,23},{8,24},{9,... | collective-permute-start | bytes 147464 | tf_op jit(solution)/shard_map/ppermute | solution.py:554
  11.4 5.9 %collective-permute-start = (bf16[8,3072]{1,0:T(8,128)(2,1)}, bf16[8,3072]{1,0:T(8,128)(2,1)S(1)}, u32[]{:S(2)}, u32[]{:S(2)}) collective-permute-start(bf16[8,3072]{1,0:T(8,128)(2,1)} %get-tuple-element.102), channel_id=1, source_target_pairs={{0,8},{1,9},{2,10},{3,11},{4,12},{5,13},{6,14},{7,15},{8,0},{9,1},... | collective-permute-start | bytes 147464 | tf_op jit(solution)/shard_map/ppermute | solution.py:554
  12.0 13.0 %collective-permute-start.5 = (bf16[32,1536]{1,0:T(8,128)(2,1)}, bf16[32,1536]{1,0:T(8,128)(2,1)S(1)}, u32[]{:S(2)}, u32[]{:S(2)}) collective-permute-start(bf16[32,1536]{1,0:T(8,128)(2,1)} %get-tuple-element.66), channel_id=1, source_target_pairs={{0,6},{1,7},{2,4},{3,5},{4,2},{5,3},{6,0},{7,1},{8,14},{9,15},{10,... | collective-permute-start | bytes 294920 | tf_op jit(solution)/shard_map/ppermute | solution.py:554
  14.6 4.8 %collective-permute-start.4 = (bf16[32,1536]{1,0:T(8,128)(2,1)}, bf16[32,1536]{1,0:T(8,128)(2,1)S(1)}, u32[]{:S(2)}, u32[]{:S(2)}) collective-permute-start(bf16[32,1536]{1,0:T(8,128)(2,1)} %get-tuple-element.66), channel_id=1, source_target_pairs={{0,4},{1,5},{2,6},{3,7},{4,0},{5,1},{6,2},{7,3},{8,12},{9,13},{10,... | collective-permute-start | bytes 294920 | tf_op jit(solution)/shard_map/ppermute | solution.py:554
  15.2 10.0 %copy-start.8 = (bf16[256,768]{1,0:T(8,128)(2,1)S(1)}, bf16[256,768]{1,0:T(8,128)(2,1)}, u32[]{:S(2)}) copy-start(bf16[256,768]{1,0:T(8,128)(2,1)} %get-tuple-element.69.v) | copy-start | bytes 1179652
  15.2 10.0 %copy-start.9 = (bf16[256,768]{1,0:T(8,128)(2,1)S(1)}, bf16[256,768]{1,0:T(8,128)(2,1)}, u32[]{:S(2)}) copy-start(bf16[256,768]{1,0:T(8,128)(2,1)} %get-tuple-element.70.g) | copy-start | bytes 1179652
  16.0 9.1 %copy-start.7 = (bf16[256,768]{1,0:T(8,128)(2,1)S(1)}, bf16[256,768]{1,0:T(8,128)(2,1)}, u32[]{:S(2)}) copy-start(bf16[256,768]{1,0:T(8,128)(2,1)} %get-tuple-element.68.k) | copy-start | bytes 1179652
  16.8 4.7 %collective-permute-start.3 = (bf16[32,1536]{1,0:T(8,128)(2,1)S(1)}, bf16[32,1536]{1,0:T(8,128)(2,1)S(1)}, u32[]{:S(2)}, u32[]{:S(2)}) collective-permute-start(bf16[32,1536]{1,0:T(8,128)(2,1)S(1)} %copy-done.15), channel_id=1, source_target_pairs={{0,2},{1,3},{2,0},{3,1},{4,6},{5,7},{6,4},{7,5},{8,10},{9,11},{10,... | collective-permute-start | bytes 294920 | tf_op jit(solution)/shard_map/ppermute | solution.py:554
  21.5 6.2 %collective-permute-start.9 = (bf16[32,1536]{1,0:T(8,128)(2,1)S(1)}, bf16[32,1536]{1,0:T(8,128)(2,1)S(1)}, u32[]{:S(2)}, u32[]{:S(2)}) collective-permute-start(bf16[32,1536]{1,0:T(8,128)(2,1)S(1)} %pad_maximum_fusion.1), channel_id=1, source_target_pairs={{0,6},{1,7},{2,4},{3,5},{4,2},{5,3},{6,0},{7,1},{8,14},{9,15},{10,... | collective-permute-start | bytes 294920 | tf_op jit(solution)/shard_map/ppermute | solution.py:554
  23.0 5.1 %collective-permute-start.8 = (bf16[32,1536]{1,0:T(8,128)(2,1)S(1)}, bf16[32,1536]{1,0:T(8,128)(2,1)S(1)}, u32[]{:S(2)}, u32[]{:S(2)}) collective-permute-start(bf16[32,1536]{1,0:T(8,128)(2,1)S(1)} %pad_maximum_fusion.1), channel_id=1, source_target_pairs={{0,4},{1,5},{2,6},{3,7},{4,0},{5,1},{6,2},{7,3},{8,12},{9,13},{10,... | collective-permute-start | bytes 294920 | tf_op jit(solution)/shard_map/ppermute | solution.py:554
  23.4 4.8 %collective-permute-start.7 = (bf16[32,1536]{1,0:T(8,128)(2,1)S(1)}, bf16[32,1536]{1,0:T(8,128)(2,1)S(1)}, u32[]{:S(2)}, u32[]{:S(2)}) collective-permute-start(bf16[32,1536]{1,0:T(8,128)(2,1)S(1)} %pad_maximum_fusion.1), channel_id=1, source_target_pairs={{0,2},{1,3},{2,0},{3,1},{4,6},{5,7},{6,4},{7,5},{8,10},{9,11},{10,... | collective-permute-start | bytes 294920 | tf_op jit(solution)/shard_map/ppermute | solution.py:554
  25.0 3.3 %collective-permute-start.6 = (bf16[128,1536]{1,0:T(8,128)(2,1)S(1)}, bf16[128,1536]{1,0:T(8,128)(2,1)S(1)}, u32[]{:S(2)}, u32[]{:S(2)}) collective-permute-start(bf16[128,1536]{1,0:T(8,128)(2,1)S(1)} %constant_dynamic-update-slice_fusion.mid_0), channel_id=1, source_target_pairs={{0,1},{1,0},{2,3},{3,2},{4,5},{5,4},{6,7},{7,6},{8,9},{9,8},{10,11... | collective-permute-start | bytes 1179656 | tf_op jit(solution)/shard_map/ppermute | solution.py:554
  28.2 1.8 %collective-permute-start.10 = (bf16[128,1536]{1,0:T(8,128)(2,1)S(1)}, bf16[128,1536]{1,0:T(8,128)(2,1)S(1)}, u32[]{:S(2)}, u32[]{:S(2)}) collective-permute-start(bf16[128,1536]{1,0:T(8,128)(2,1)S(1)} %constant_dynamic-update-slice_fusion.4.far_0), channel_id=1, source_target_pairs={{0,1},{1,0},{2,3},{3,2},{4,5},{5,4},{6,7},{7,6},{8,9},{9,8},{10,11... | collective-permute-start | bytes 1179656 | tf_op jit(solution)/shard_map/ppermute | solution.py:554
  32.3 9.8 %copy-start.2 = (bf16[768,768]{1,0:T(8,128)(2,1)S(1)}, bf16[768,768]{1,0:T(8,128)(2,1)}, u32[]{:S(2)}) copy-start(bf16[768,768]{1,0:T(8,128)(2,1)} %w_out.1) | copy-start | bytes 3538948
  34.2 5.0 %collective-permute-start.11 = (f32[8,128]{1,0:T(8,128)S(1)}, f32[8,128]{1,0:T(8,128)S(1)}, u32[]{:S(2)}, u32[]{:S(2)}) collective-permute-start(f32[8,128]{1,0:T(8,128)S(1)} %slice.130), channel_id=1, source_target_pairs={{0,8},{1,9},{2,10},{3,11},{4,12},{5,13},{6,14},{7,15},{8,0},{9,1},... | collective-permute-start | bytes 12296 | tf_op jit(solution)/shard_map/ppermute | solution.py:554
  35.6 14.8 %collective-permute-start.19 = (bf16[64,1536]{1,0:T(8,128)(2,1)S(1)}, bf16[64,1536]{1,0:T(8,128)(2,1)S(1)}, u32[]{:S(2)}, u32[]{:S(2)}) collective-permute-start(bf16[64,1536]{1,0:T(8,128)(2,1)S(1)} %constant_dynamic-update-slice_fusion.14), channel_id=1, source_target_pairs={{0,6},{1,7},{2,4},{3,5},{4,2},{5,3},{6,0},{7,1},{8,14},{9,15},{10,... | collective-permute-start | bytes 589832 | tf_op jit(solution)/shard_map/ppermute | solution.py:554
  38.1 12.4 %collective-permute-start.18 = (bf16[64,1536]{1,0:T(8,128)(2,1)S(1)}, bf16[64,1536]{1,0:T(8,128)(2,1)S(1)}, u32[]{:S(2)}, u32[]{:S(2)}) collective-permute-start(bf16[64,1536]{1,0:T(8,128)(2,1)S(1)} %constant_dynamic-update-slice_fusion.14), channel_id=1, source_target_pairs={{0,4},{1,5},{2,6},{3,7},{4,0},{5,1},{6,2},{7,3},{8,12},{9,13},{10,... | collective-permute-start | bytes 589832 | tf_op jit(solution)/shard_map/ppermute | solution.py:554
  38.6 11.9 %collective-permute-start.17 = (bf16[64,1536]{1,0:T(8,128)(2,1)S(1)}, bf16[64,1536]{1,0:T(8,128)(2,1)S(1)}, u32[]{:S(2)}, u32[]{:S(2)}) collective-permute-start(bf16[64,1536]{1,0:T(8,128)(2,1)S(1)} %constant_dynamic-update-slice_fusion.14), channel_id=1, source_target_pairs={{0,2},{1,3},{2,0},{3,1},{4,6},{5,7},{6,4},{7,5},{8,10},{9,11},{10,... | collective-permute-start | bytes 589832 | tf_op jit(solution)/shard_map/ppermute | solution.py:554
  39.2 5.7 %collective-permute-start.15 = (bf16[256,768]{1,0:T(8,128)(2,1)S(1)}, bf16[256,768]{1,0:T(8,128)(2,1)S(1)}, u32[]{:S(2)}, u32[]{:S(2)}) collective-permute-start(bf16[256,768]{1,0:T(8,128)(2,1)S(1)} %copy-done.4), channel_id=1, source_target_pairs={{0,1},{1,0},{2,3},{3,2},{4,5},{5,4},{6,7},{7,6},{8,9},{9,8},{10,11... | collective-permute-start | bytes 1179656 | tf_op jit(solution)/shard_map/ppermute | solution.py:554
  39.2 5.5 %collective-permute-start.12 = (f32[16,128]{1,0:T(8,128)S(1)}, f32[16,128]{1,0:T(8,128)S(1)}, u32[]{:S(2)}, u32[]{:S(2)}) collective-permute-start(f32[16,128]{1,0:T(8,128)S(1)} %constant_dynamic-update-slice_fusion.8), channel_id=1, source_target_pairs={{0,16},{1,17},{2,18},{3,19},{4,20},{5,21},{6,22},{7,23},{8,24},{9,... | collective-permute-start | bytes 24584 | tf_op jit(solution)/shard_map/ppermute | solution.py:554
  44.7 1.7 %collective-permute-start.14 = (bf16[384,256]{1,0:T(8,128)(2,1)S(1)}, bf16[384,256]{1,0:T(8,128)(2,1)S(1)}, u32[]{:S(2)}, u32[]{:S(2)}) collective-permute-start(bf16[384,256]{1,0:T(8,128)(2,1)S(1)} %get-tuple-element.90), channel_id=1, source_target_pairs={{0,1},{1,0},{2,3},{3,2},{4,5},{5,4},{6,7},{7,6},{8,9},{9,8},{10,11... | collective-permute-start | bytes 589832 | tf_op jit(solution)/shard_map/ppermute | solution.py:554
  44.9 4.0 %collective-permute-start.13 = (f32[32,256]{1,0:T(8,128)S(1)}, f32[32,256]{1,0:T(8,128)S(1)}, u32[]{:S(2)}, u32[]{:S(2)}) collective-permute-start(f32[32,256]{1,0:T(8,128)S(1)} %pad_maximum_fusion.2), channel_id=1, source_target_pairs={{0,4},{1,5},{2,6},{3,7},{4,0},{5,1},{6,2},{7,3},{8,12},{9,13},{10,... | collective-permute-start | bytes 98312 | tf_op jit(solution)/shard_map/ppermute | solution.py:554
  48.9 7.0 %collective-permute-start.21 = (f32[64,256]{1,0:T(8,128)S(1)}, f32[64,256]{1,0:T(8,128)S(1)}, u32[]{:S(2)}, u32[]{:S(2)}) collective-permute-start(f32[64,256]{1,0:T(8,128)S(1)} %constant_dynamic-update-slice_fusion.12), channel_id=1, source_target_pairs={{0,2},{1,3},{2,0},{3,1},{4,6},{5,7},{6,4},{7,5},{8,10},{9,11},{10,... | collective-permute-start | bytes 196616 | tf_op jit(solution)/shard_map/ppermute | solution.py:554
  54.5 2.0 %collective-permute-start.23 = (bf16[256,768]{1,0:T(8,128)(2,1)S(1)}, bf16[256,768]{1,0:T(8,128)(2,1)S(1)}, u32[]{:S(2)}, u32[]{:S(2)}) collective-permute-start(bf16[256,768]{1,0:T(8,128)(2,1)S(1)} %get-tuple-element.117.right.dq), channel_id=1, source_target_pairs={{0,1},{1,0},{2,3},{3,2},{4,5},{5,4},{6,7},{7,6},{8,9},{9,8},{10,11... | collective-permute-start | bytes 1179656 | tf_op jit(solution)/shard_map/ppermute | solution.py:554
  54.6 2.3 %collective-permute-start.16 = (bf16[768,256]{1,0:T(8,128)(2,1)S(1)}, bf16[768,256]{1,0:T(8,128)(2,1)S(1)}, u32[]{:S(2)}, u32[]{:S(2)}) collective-permute-start(bf16[768,256]{1,0:T(8,128)(2,1)S(1)} %get-tuple-element.99), channel_id=1, source_target_pairs={{0,1},{1,0},{2,3},{3,2},{4,5},{5,4},{6,7},{7,6},{8,9},{9,8},{10,11... | collective-permute-start | bytes 1179656 | tf_op jit(solution)/shard_map/ppermute | solution.py:554
  55.1 9.1 %collective-permute-start.36 = (bf16[192,768]{1,0:T(8,128)(2,1)S(1)}, bf16[192,768]{1,0:T(8,128)(2,1)S(1)}, u32[]{:S(2)}, u32[]{:S(2)}) collective-permute-start(bf16[192,768]{1,0:T(8,128)(2,1)S(1)} %get-tuple-element.127), channel_id=1, source_target_pairs={{0,2},{1,3},{2,0},{3,1},{4,6},{5,7},{6,4},{7,5},{8,10},{9,11},{10,... | collective-permute-start | bytes 884744 | tf_op jit(solution)/shard_map/ppermute | solution.py:554
  55.8 2.5 %collective-permute-start.20 = (bf16[256,1536]{1,0:T(8,128)(2,1)S(1)}, bf16[256,1536]{1,0:T(8,128)(2,1)S(1)}, u32[]{:S(2)}, u32[]{:S(2)}) collective-permute-start(bf16[256,1536]{1,0:T(8,128)(2,1)S(1)} %constant_dynamic-update-slice_fusion.19.qg_0), channel_id=1, source_target_pairs={{0,1},{1,0},{2,3},{3,2},{4,5},{5,4},{6,7},{7,6},{8,9},{9,8},{10,11... | collective-permute-start | bytes 2359304 | tf_op jit(solution)/shard_map/ppermute | solution.py:554
  56.0 2.4 %collective-permute-start.22 = (f32[256,128]{1,0:T(8,128)S(1)}, f32[256,128]{1,0:T(8,128)S(1)}, u32[]{:S(2)}, u32[]{:S(2)}) collective-permute-start(f32[256,128]{1,0:T(8,128)S(1)} %constant_dynamic-update-slice_fusion.23.stats_0), channel_id=1, source_target_pairs={{0,1},{1,0},{2,3},{3,2},{4,5},{5,4},{6,7},{7,6},{8,9},{9,8},{10,11... | collective-permute-start | bytes 393224 | tf_op jit(solution)/shard_map/ppermute | solution.py:554
  60.7 5.2 %collective-permute-start.24 = (bf16[256,768]{1,0:T(8,128)(2,1)S(1)}, bf16[256,768]{1,0:T(8,128)(2,1)S(1)}, u32[]{:S(2)}, u32[]{:S(2)}) collective-permute-start(bf16[256,768]{1,0:T(8,128)(2,1)S(1)} %get-tuple-element.115.dk), channel_id=1, source_target_pairs={{0,1},{1,0},{2,3},{3,2},{4,5},{5,4},{6,7},{7,6},{8,9},{9,8},{10,11... | collective-permute-start | bytes 1179656 | tf_op jit(solution)/shard_map/ppermute | solution.py:554
  64.2 1.7 %collective-permute-start.25 = (bf16[256,768]{1,0:T(8,128)(2,1)S(1)}, bf16[256,768]{1,0:T(8,128)(2,1)S(1)}, u32[]{:S(2)}, u32[]{:S(2)}) collective-permute-start(bf16[256,768]{1,0:T(8,128)(2,1)S(1)} %get-tuple-element.116.dv), channel_id=1, source_target_pairs={{0,1},{1,0},{2,3},{3,2},{4,5},{5,4},{6,7},{7,6},{8,9},{9,8},{10,11... | collective-permute-start | bytes 1179656 | tf_op jit(solution)/shard_map/ppermute | solution.py:554
  64.3 8.1 %collective-permute-start.37 = (bf16[96,768]{1,0:T(8,128)(2,1)S(1)}, bf16[96,768]{1,0:T(8,128)(2,1)S(1)}, u32[]{:S(2)}, u32[]{:S(2)}) collective-permute-start(bf16[96,768]{1,0:T(8,128)(2,1)S(1)} %get-tuple-element.134), channel_id=1, source_target_pairs={{0,4},{1,5},{2,6},{3,7},{4,0},{5,1},{6,2},{7,3},{8,12},{9,13},{10,... | collective-permute-start | bytes 442376 | tf_op jit(solution)/shard_map/ppermute | solution.py:554
  66.8 9.9 %collective-permute-start.27 = (bf16[96,1536]{1,0:T(8,128)(2,1)S(1)}, bf16[96,1536]{1,0:T(8,128)(2,1)S(1)}, u32[]{:S(2)}, u32[]{:S(2)}) collective-permute-start(bf16[96,1536]{1,0:T(8,128)(2,1)S(1)} %get-tuple-element.124), channel_id=1, source_target_pairs={{0,2},{1,3},{2,0},{3,1},{4,6},{5,7},{6,4},{7,5},{8,10},{9,11},{10,... | collective-permute-start | bytes 884744 | tf_op jit(solution)/shard_map/ppermute | solution.py:554
  67.5 9.3 %collective-permute-start.26 = (bf16[192,768]{1,0:T(8,128)(2,1)S(1)}, bf16[192,768]{1,0:T(8,128)(2,1)S(1)}, u32[]{:S(2)}, u32[]{:S(2)}) collective-permute-start(bf16[192,768]{1,0:T(8,128)(2,1)S(1)} %get-tuple-element.129), channel_id=1, source_target_pairs={{0,8},{1,9},{2,10},{3,11},{4,12},{5,13},{6,14},{7,15},{8,0},{9,1},... | collective-permute-start | bytes 884744 | tf_op jit(solution)/shard_map/ppermute | solution.py:554
  67.6 15.7 %collective-permute-start.32 = (bf16[96,1536]{1,0:T(8,128)(2,1)S(1)}, bf16[96,1536]{1,0:T(8,128)(2,1)S(1)}, u32[]{:S(2)}, u32[]{:S(2)}) collective-permute-start(bf16[96,1536]{1,0:T(8,128)(2,1)S(1)} %get-tuple-element.125), channel_id=1, source_target_pairs={{0,6},{1,7},{2,4},{3,5},{4,2},{5,3},{6,0},{7,1},{8,14},{9,15},{10,... | collective-permute-start | bytes 884744 | tf_op jit(solution)/shard_map/ppermute | solution.py:554
  70.0 14.8 %collective-permute-start.31 = (bf16[96,1536]{1,0:T(8,128)(2,1)S(1)}, bf16[96,1536]{1,0:T(8,128)(2,1)S(1)}, u32[]{:S(2)}, u32[]{:S(2)}) collective-permute-start(bf16[96,1536]{1,0:T(8,128)(2,1)S(1)} %get-tuple-element.126), channel_id=1, source_target_pairs={{0,4},{1,5},{2,6},{3,7},{4,0},{5,1},{6,2},{7,3},{8,12},{9,13},{10,... | collective-permute-start | bytes 884744 | tf_op jit(solution)/shard_map/ppermute | solution.py:554
  76.7 11.8 %collective-permute-start.38 = (bf16[48,768]{1,0:T(8,128)(2,1)S(1)}, bf16[48,768]{1,0:T(8,128)(2,1)S(1)}, u32[]{:S(2)}, u32[]{:S(2)}) collective-permute-start(bf16[48,768]{1,0:T(8,128)(2,1)S(1)} %slice.192), channel_id=1, source_target_pairs={{0,8},{1,9},{2,10},{3,11},{4,12},{5,13},{6,14},{7,15},{8,0},{9,1},... | collective-permute-start | bytes 221192 | tf_op jit(solution)/shard_map/ppermute | solution.py:554
  77.0 14.4 %collective-permute-start.28 = (bf16[96,768]{1,0:T(8,128)(2,1)S(1)}, bf16[96,768]{1,0:T(8,128)(2,1)S(1)}, u32[]{:S(2)}, u32[]{:S(2)}) collective-permute-start(bf16[96,768]{1,0:T(8,128)(2,1)S(1)} %slice.175), channel_id=1, source_target_pairs={{0,16},{1,17},{2,18},{3,19},{4,20},{5,21},{6,22},{7,23},{8,24},{9,... | collective-permute-start | bytes 442376 | tf_op jit(solution)/shard_map/ppermute | solution.py:554
  85.0 7.4 %collective-permute-start.33 = (bf16[24,1536]{1,0:T(8,128)(2,1)S(1)}, bf16[24,1536]{1,0:T(8,128)(2,1)S(1)}, u32[]{:S(2)}, u32[]{:S(2)}) collective-permute-start(bf16[24,1536]{1,0:T(8,128)(2,1)S(1)} %get-tuple-element.136), channel_id=1, source_target_pairs={{0,8},{1,9},{2,10},{3,11},{4,12},{5,13},{6,14},{7,15},{8,0},{9,1},... | collective-permute-start | bytes 221192 | tf_op jit(solution)/shard_map/ppermute | solution.py:554
  86.7 6.2 %collective-permute-start.35 = (bf16[24,1536]{1,0:T(8,128)(2,1)S(1)}, bf16[24,1536]{1,0:T(8,128)(2,1)S(1)}, u32[]{:S(2)}, u32[]{:S(2)}) collective-permute-start(bf16[24,1536]{1,0:T(8,128)(2,1)S(1)} %get-tuple-element.137), channel_id=1, source_target_pairs={{0,24},{1,25},{2,26},{3,27},{4,28},{5,29},{6,30},{7,31},{8,16},{9,... | collective-permute-start | bytes 221192 | tf_op jit(solution)/shard_map/ppermute | solution.py:554
  88.4 7.6 %collective-permute-start.34 = (bf16[24,1536]{1,0:T(8,128)(2,1)S(1)}, bf16[24,1536]{1,0:T(8,128)(2,1)S(1)}, u32[]{:S(2)}, u32[]{:S(2)}) collective-permute-start(bf16[24,1536]{1,0:T(8,128)(2,1)S(1)} %get-tuple-element.138), channel_id=1, source_target_pairs={{0,16},{1,17},{2,18},{3,19},{4,20},{5,21},{6,22},{7,23},{8,24},{9,... | collective-permute-start | bytes 221192 | tf_op jit(solution)/shard_map/ppermute | solution.py:554
  88.6 8.2 %collective-permute-start.39 = (bf16[24,768]{1,0:T(8,128)(2,1)S(1)}, bf16[24,768]{1,0:T(8,128)(2,1)S(1)}, u32[]{:S(2)}, u32[]{:S(2)}) collective-permute-start(bf16[24,768]{1,0:T(8,128)(2,1)S(1)} %slice.194), channel_id=1, source_target_pairs={{0,16},{1,17},{2,18},{3,19},{4,20},{5,21},{6,22},{7,23},{8,24},{9,... | collective-permute-start | bytes 110600 | tf_op jit(solution)/shard_map/ppermute | solution.py:554
  91.5 4.5 %collective-permute-start.29 = (bf16[48,768]{1,0:T(8,128)(2,1)S(1)}, bf16[48,768]{1,0:T(8,128)(2,1)S(1)}, u32[]{:S(2)}, u32[]{:S(2)}) collective-permute-start(bf16[48,768]{1,0:T(8,128)(2,1)S(1)} %slice.177), channel_id=1, source_target_pairs={{0,2},{1,3},{2,0},{3,1},{4,6},{5,7},{6,4},{7,5},{8,10},{9,11},{10,... | collective-permute-start | bytes 221192 | tf_op jit(solution)/shard_map/ppermute | solution.py:554
  96.0 4.0 %collective-permute-start.30 = (bf16[24,768]{1,0:T(8,128)(2,1)S(1)}, bf16[24,768]{1,0:T(8,128)(2,1)S(1)}, u32[]{:S(2)}, u32[]{:S(2)}) collective-permute-start(bf16[24,768]{1,0:T(8,128)(2,1)S(1)} %slice.179), channel_id=1, source_target_pairs={{0,4},{1,5},{2,6},{3,7},{4,0},{5,1},{6,2},{7,3},{8,12},{9,13},{10,... | collective-permute-start | bytes 110600 | tf_op jit(solution)/shard_map/ppermute | solution.py:554
  (9 other events, 44.4 us)

commit v9 on v8

--- a/solution.py
+++ b/solution.py
@@ -760,7 +760,7 @@
     )(after(dq, late_half), dk, dv, w_qkv)
     late_parts = block_parts(late_half, PLANE, n)
     early = halved(early_half, masks + [2, 4], n, ((late_parts[1],),))
-    grad_wout = halved(wout_half, [2, 4] + masks, n, ((dk,), (late_parts[1],)))
+    grad_wout = halved(wout_half, [2, 4] + masks, n, ((dk_near,), (late_parts[1],)))
     late = reduce_all(sum_parts(late_parts, BF), upper_steps(n)[::-1], n)
     grad_wqkv = jnp.concatenate([early, late], axis=1)
     return out_rows, grad_tiles, grad_wqkv, grad_wout

time: 101 us -> 95.9 us (0.950)
  waiting for transfers between devices: 28.6 us -> 25.4 us
  starting transfers between devices: 42.1 us -> 40.3 us
    ppermute x40, waiting for transfers between devices: 28.6 us -> 25.4 us  [swap(): return lax.ppermute(value, 'ctx', [(d, d ^ mask) for d in range(dev_count)])]
    ppermute x40, starting transfers between devices: 42.1 us -> 40.3 us  [swap(): return lax.ppermute(value, 'ctx', [(d, d ^ mask) for d in range(dev_count)])]
  transfers between devices with their start and end apart: 40 -> 40, of which waited for: 15 -> 16; matrix products, arithmetic and copies ran while one was open for 2% -> 2% of each run, Pallas kernels for 15% -> 15%
where the time goes in v9:
time: 95.9 us; the launch traced here: 95.7 us
  starting transfers between devices  40.3 us (42%)
  waiting for transfers between devices  25.4 us (26%)
  Pallas kernels  24.8 us (26%)
  between operations  2.06 us (2%)
  other arithmetic  1.93 us (2%)
  local copies, waits for them, and re-layouts  1.25 us (1%)
    ppermute x40, starting transfers between devices, swap(): return lax.ppermute(value, 'ctx', [(d, d ^ mask) for d in range(dev_count)])  40.3 us
    ppermute x40, waiting for transfers between devices, swap(): return lax.ppermute(value, 'ctx', [(d, d ^ mask) for d in range(dev_count)])  25.4 us
    pallas_call x11, Pallas kernels, run(): pl.pallas_call(kernel, out_shape=tuple((jax.ShapeDtypeStruct(s, t) for s,...  24.8 us
  transfers between devices with their start and end apart: 40, of which 16 were waited for; matrix products, arithmetic and copies ran while one was open for 2% of the time, Pallas kernels for 15%

profile of v9, /device:TPU:0, one launch (start us, length us, event | category | flops | bytes accessed | tf_op | source)
XLA Modules:
  0.0 95.7 jit_solution(9810213341670014686)
XLA Ops:
  0.7 5.6 %shard_map.147 = (bf16[256,768]{1,0:T(8,128)(2,1)}, bf16[256,768]{1,0:T(8,128)(2,1)}, bf16[256,768]{1,0:T(8,128)(2,1)}, bf16[256,768]{1,0:T(8,128)(2,1)}, bf16[6...) custom-call(s32[2,12]{1,0:T(2,128)} %offs_ref.9, ...), custom_call_target="tpu_custom_call" | custom-call | flops 1207959552 | bytes 7716960 | tf_op jit(solution)/shard_map/pallas_call | solution.py:535
  6.3 3.1 %collective-permute-start = (bf16[8,3072]{1,0:T(8,128)(2,1)}, bf16[8,3072]{1,0:T(8,128)(2,1)S(1)}, u32[]{:S(2)}, u32[]{:S(2)}) collective-permute-start(bf16[8,3072]{1,0:T(8,128)(2,1)} %get-tuple-element.102), channel_id=1, source_target_pairs={{0,8},{1,9},{2,10},{3,11},{4,12},{5,13},{6,14},{7,15},{8,0},{9,1},... | collective-permute-start | bytes 147464 | tf_op jit(solution)/shard_map/ppermute | solution.py:554
  9.3 2.6 %collective-permute-start.1 = (bf16[8,3072]{1,0:T(8,128)(2,1)}, bf16[8,3072]{1,0:T(8,128)(2,1)S(1)}, u32[]{:S(2)}, u32[]{:S(2)}) collective-permute-start(bf16[8,3072]{1,0:T(8,128)(2,1)} %get-tuple-element.102), channel_id=1, source_target_pairs={{0,16},{1,17},{2,18},{3,19},{4,20},{5,21},{6,22},{7,23},{8,24},{9,... | collective-permute-start | bytes 147464 | tf_op jit(solution)/shard_map/ppermute | solution.py:554
  11.9 1.7 %collective-permute-start.3 = (bf16[32,1536]{1,0:T(8,128)(2,1)}, bf16[32,1536]{1,0:T(8,128)(2,1)S(1)}, u32[]{:S(2)}, u32[]{:S(2)}) collective-permute-start(bf16[32,1536]{1,0:T(8,128)(2,1)} %get-tuple-element.66), channel_id=1, source_target_pairs={{0,2},{1,3},{2,0},{3,1},{4,6},{5,7},{6,4},{7,5},{8,10},{9,11},{10,... | collective-permute-start | bytes 294920 | tf_op jit(solution)/shard_map/ppermute | solution.py:554
  13.7 1.5 %collective-permute-start.4 = (bf16[32,1536]{1,0:T(8,128)(2,1)}, bf16[32,1536]{1,0:T(8,128)(2,1)S(1)}, u32[]{:S(2)}, u32[]{:S(2)}) collective-permute-start(bf16[32,1536]{1,0:T(8,128)(2,1)} %get-tuple-element.66), channel_id=1, source_target_pairs={{0,4},{1,5},{2,6},{3,7},{4,0},{5,1},{6,2},{7,3},{8,12},{9,13},{10,... | collective-permute-start | bytes 294920 | tf_op jit(solution)/shard_map/ppermute | solution.py:554
  15.4 0.7 copy-done.15
  17.2 0.8 collective-permute-done.2
  18.1 0.6 collective-permute-done.4
  18.7 0.9 collective-permute-start.7
  19.6 2.0 %collective-permute-start.8 = (bf16[32,1536]{1,0:T(8,128)(2,1)S(1)}, bf16[32,1536]{1,0:T(8,128)(2,1)S(1)}, u32[]{:S(2)}, u32[]{:S(2)}) collective-permute-start(bf16[32,1536]{1,0:T(8,128)(2,1)S(1)} %pad_maximum_fusion.1), channel_id=1, source_target_pairs={{0,4},{1,5},{2,6},{3,7},{4,0},{5,1},{6,2},{7,3},{8,12},{9,13},{10,... | collective-permute-start | bytes 294920 | tf_op jit(solution)/shard_map/ppermute | solution.py:554
  21.6 0.9 collective-permute-start.9
  22.8 2.5 %shard_map.148 = (f32[256,768]{1,0:T(8,128)S(1)}, f32[256,128]{1,0:T(8,128)S(1)}, bf16[768,256]{1,0:T(8,128)(2,1)S(1)}, bf16[768,256]{1,0:T(8,128)(2,1)S(1)}) custom-call(s32[1]{0:T(128)S(6)} %copy.42.pad_ref, bf16[256,768]{1,0:T(8,128)(2,1)S(1)} %copy-done.6, bf16[256,768]{1,0:T(8,128)(2,1)S(1)} %copy-done.7, bf16[256,768]{1,0:T(8,128)(2,1)S(1)} %copy-done.8, ...), custom_call_target="tpu_custom_call" | custom-call | flops 805306368 | bytes 3676164 | tf_op jit(solution)/shard_map/pallas_call | solution.py:535
  25.4 1.7 %collective-permute-done.9 = bf16[32,1536]{1,0:T(8,128)(2,1)S(1)} collective-permute-done((bf16[32,1536]{1,0:T(8,128)(2,1)S(1)}, bf16[32,1536]{1,0:T(8,128)(2,1)S(1)}, u32[]{:S(2)}, u32[]{:S(2)}) %collective-permute-start.9) | collective-permute-done | bytes 98336 | tf_op jit(solution)/shard_map/ppermute | solution.py:554
  27.2 1.7 %collective-permute-done.10.far_1 = bf16[128,1536]{1,0:T(8,128)(2,1)S(1)} collective-permute-done((bf16[128,1536]{1,0:T(8,128)(2,1)S(1)}, bf16[128,1536]{1,0:T(8,128)(2,1)S(1)}, u32[]{:S(2)}, u32[]{:S(2)}) %collective-permute-start.10) | collective-permute-done | bytes 393248 | tf_op jit(solution)/shard_map/ppermute | solution.py:554
  29.0 2.3 %shard_map.149 = (f32[256,128]{1,0:T(8,128)S(1)}, f32[64,128]{1,0:T(8,128)S(1)}, f32[64,128]{1,0:T(8,128)S(1)}, f32[64,768]{1,0:T(8,128)S(1)}) custom-call(s32[2,12]{1,0:T(2,128)S(1)} %copy-done.5, s32[1]{0:T(128)S(6)} %copy.42.pad_ref, bf16[64,3072]{1,0:T(8,128)(2,1)S(1)} %copy-done.1, bf16[128,1536]{1,0:T(8,128)(2,1)S(1)} %constant_dynamic-update-slice_fusion.mid_0, ...), custom_call_target="tpu_custom_call" | custom-call | flops 301989888 | bytes 2490468 | tf_op jit(solution)/shard_map/pallas_call | solution.py:535
  31.3 0.7 collective-permute-start.11
  32.0 1.8 %shard_map.150.dq_sel = f32[64,768]{1,0:T(8,128)S(1)} custom-call(s32[2,12]{1,0:T(2,128)S(1)} %copy-done.5, s32[1]{0:T(128)S(6)} %copy.42.pad_ref, bf16[64,3072]{1,0:T(8,128)(2,1)S(1)} %copy-done.1, bf16[128,1536]{1,0:T(8,128)(2,1)S(1)} %constant_dynamic-update-slice_fusion.mid_0, bf16[128,1536]{1,0:T(8,128)(2,1)S(1)} %collective-permute-done.6.mid_1, ...), custom_call_target="tpu_custom_call" | custom-call | flops 201326592 | bytes 2195556 | tf_op jit(solution)/shard_map/pallas_call | solution.py:535
  34.0 1.6 %collective-permute-start.17 = (bf16[64,1536]{1,0:T(8,128)(2,1)S(1)}, bf16[64,1536]{1,0:T(8,128)(2,1)S(1)}, u32[]{:S(2)}, u32[]{:S(2)}) collective-permute-start(bf16[64,1536]{1,0:T(8,128)(2,1)S(1)} %constant_dynamic-update-slice_fusion.14), channel_id=1, source_target_pairs={{0,2},{1,3},{2,0},{3,1},{4,6},{5,7},{6,4},{7,5},{8,10},{9,11},{10,... | collective-permute-start | bytes 589832 | tf_op jit(solution)/shard_map/ppermute | solution.py:554
  35.7 1.8 %collective-permute-start.19 = (bf16[64,1536]{1,0:T(8,128)(2,1)S(1)}, bf16[64,1536]{1,0:T(8,128)(2,1)S(1)}, u32[]{:S(2)}, u32[]{:S(2)}) collective-permute-start(bf16[64,1536]{1,0:T(8,128)(2,1)S(1)} %constant_dynamic-update-slice_fusion.14), channel_id=1, source_target_pairs={{0,6},{1,7},{2,4},{3,5},{4,2},{5,3},{6,0},{7,1},{8,14},{9,15},{10,... | collective-permute-start | bytes 589832 | tf_op jit(solution)/shard_map/ppermute | solution.py:554
  37.5 3.6 %collective-permute-start.12 = (f32[16,128]{1,0:T(8,128)S(1)}, f32[16,128]{1,0:T(8,128)S(1)}, u32[]{:S(2)}, u32[]{:S(2)}) collective-permute-start(f32[16,128]{1,0:T(8,128)S(1)} %constant_dynamic-update-slice_fusion.8), channel_id=1, source_target_pairs={{0,16},{1,17},{2,18},{3,19},{4,20},{5,21},{6,22},{7,23},{8,24},{9,... | collective-permute-start | bytes 24584 | tf_op jit(solution)/shard_map/ppermute | solution.py:554
  41.1 2.5 %shard_map.151 = (bf16[256,768]{1,0:T(8,128)(2,1)}, bf16[384,256]{1,0:T(8,128)(2,1)S(1)}, bf16[384,256]{1,0:T(8,128)(2,1)S(1)}) custom-call(s32[2,12]{1,0:T(2,128)S(1)} %copy-done.5, f32[256,128]{1,0:T(8,128)S(1)} %get-tuple-element.71.near_stats, f32[256,128]{1,0:T(8,128)S(1)} %get-tuple-element.78.stats, f32[64,128]{1,0:T(8,128)S(1)} %get-tuple-element.82.picked, ...), custom_call_target="tpu_custom_call" | custom-call | flops 905969664 | bytes 3673184 | tf_op jit(solution)/shard_map/pallas_call | solution.py:535
  44.2 0.9 collective-permute-done.14.left_other
  45.6 2.2 %collective-permute-done.13 = f32[32,256]{1,0:T(8,128)S(1)} collective-permute-done((f32[32,256]{1,0:T(8,128)S(1)}, f32[32,256]{1,0:T(8,128)S(1)}, u32[]{:S(2)}, u32[]{:S(2)}) %collective-permute-start.13) | collective-permute-done | bytes 32800 | tf_op jit(solution)/shard_map/ppermute | solution.py:554
  47.8 1.5 %collective-permute-start.21 = (f32[64,256]{1,0:T(8,128)S(1)}, f32[64,256]{1,0:T(8,128)S(1)}, u32[]{:S(2)}, u32[]{:S(2)}) collective-permute-start(f32[64,256]{1,0:T(8,128)S(1)} %constant_dynamic-update-slice_fusion.12), channel_id=1, source_target_pairs={{0,2},{1,3},{2,0},{3,1},{4,6},{5,7},{6,4},{7,5},{8,10},{9,11},{10,... | collective-permute-start | bytes 196616 | tf_op jit(solution)/shard_map/ppermute | solution.py:554
  49.4 0.6 collective-permute-start.36
  49.9 4.1 %shard_map.153 = (bf16[256,768]{1,0:T(8,128)(2,1)S(1)}, f32[256,768]{1,0:T(8,128)S(1)}, f32[256,768]{1,0:T(8,128)S(1)}) custom-call(s32[2,12]{1,0:T(2,128)S(1)} %copy-done.5, s32[1]{0:T(128)S(6)} %copy.42.pad_ref, bf16[256,768]{1,0:T(8,128)(2,1)S(1)} %copy-done.6, bf16[256,768]{1,0:T(8,128)(2,1)S(1)} %copy-done.7, bf16[256,768]{1,0:T(8,128)(2,1)S(1)} %copy-done.8, ...), custom_call_target="tpu_custom_call" | custom-call | flops 805306368 | bytes 3866724 | tf_op jit(solution)/shard_map/pallas_call | solution.py:535
  55.4 2.5 %collective-permute-done.36 = bf16[192,768]{1,0:T(8,128)(2,1)S(1)} collective-permute-done((bf16[192,768]{1,0:T(8,128)(2,1)S(1)}, bf16[192,768]{1,0:T(8,128)(2,1)S(1)}, u32[]{:S(2)}, u32[]{:S(2)}) %collective-permute-start.36) | collective-permute-done | bytes 294944 | tf_op jit(solution)/shard_map/ppermute | solution.py:554
  58.4 2.4 %shard_map.155 = (bf16[256,768]{1,0:T(8,128)(2,1)S(1)}, bf16[256,768]{1,0:T(8,128)(2,1)S(1)}) custom-call(s32[2,12]{1,0:T(2,128)S(1)} %copy-done.5, s32[1]{0:T(128)S(6)} %copy.42.pad_ref, bf16[64,3072]{1,0:T(8,128)(2,1)S(1)} %copy-done.1, bf16[256,1536]{1,0:T(8,128)(2,1)S(1)} %constant_dynamic-update-slice_fusion.19.qg_0, ...), custom_call_target="tpu_custom_call" | custom-call | flops 15099494 | bytes 229381 | tf_op jit(solution)/shard_map/pallas_call | solution.py:535
  61.8 0.8 collective-permute-done.24.dk_other
  62.6 0.6 collective-permute-done.25.dv_other
  63.2 0.8 shard_map.156
  64.0 1.0 %collective-permute-start.27 = (bf16[96,1536]{1,0:T(8,128)(2,1)S(1)}, bf16[96,1536]{1,0:T(8,128)(2,1)S(1)}, u32[]{:S(2)}, u32[]{:S(2)}) collective-permute-start(bf16[96,1536]{1,0:T(8,128)(2,1)S(1)} %get-tuple-element.124), channel_id=1, source_target_pairs={{0,2},{1,3},{2,0},{3,1},{4,6},{5,7},{6,4},{7,5},{8,10},{9,11},{10,... | collective-permute-start | bytes 884744 | tf_op jit(solution)/shard_map/ppermute | solution.py:554
  65.4 1.2 %collective-permute-start.31 = (bf16[96,1536]{1,0:T(8,128)(2,1)S(1)}, bf16[96,1536]{1,0:T(8,128)(2,1)S(1)}, u32[]{:S(2)}, u32[]{:S(2)}) collective-permute-start(bf16[96,1536]{1,0:T(8,128)(2,1)S(1)} %get-tuple-element.126), channel_id=1, source_target_pairs={{0,4},{1,5},{2,6},{3,7},{4,0},{5,1},{6,2},{7,3},{8,12},{9,13},{10,... | collective-permute-start | bytes 884744 | tf_op jit(solution)/shard_map/ppermute | solution.py:554
  66.6 1.2 %collective-permute-start.32 = (bf16[96,1536]{1,0:T(8,128)(2,1)S(1)}, bf16[96,1536]{1,0:T(8,128)(2,1)S(1)}, u32[]{:S(2)}, u32[]{:S(2)}) collective-permute-start(bf16[96,1536]{1,0:T(8,128)(2,1)S(1)} %get-tuple-element.125), channel_id=1, source_target_pairs={{0,6},{1,7},{2,4},{3,5},{4,2},{5,3},{6,0},{7,1},{8,14},{9,15},{10,... | collective-permute-start | bytes 884744 | tf_op jit(solution)/shard_map/ppermute | solution.py:554
  67.9 1.9 %shard_map.157 = bf16[256,768]{1,0:T(8,128)(2,1)} custom-call(bf16[256,768]{1,0:T(8,128)(2,1)S(1)} %get-tuple-element.117.right.dq, bf16[256,768]{1,0:T(8,128)(2,1)S(1)} %get-tuple-element.115.dk, bf16[256,768]{1,0:T(8,128)(2,1)S(1)} %get-tuple-element.116.dv, bf16[768,2304]{1,0:T(8,128)(2,1)S(1)} %copy-done), custom_call_target="tpu_custom_call" | custom-call | flops 45298484 | bytes 255590 | tf_op jit(solution)/shard_map/pallas_call | solution.py:535
  69.7 4.2 %collective-permute-done.27 = bf16[96,1536]{1,0:T(8,128)(2,1)S(1)} collective-permute-done((bf16[96,1536]{1,0:T(8,128)(2,1)S(1)}, bf16[96,1536]{1,0:T(8,128)(2,1)S(1)}, u32[]{:S(2)}, u32[]{:S(2)}) %collective-permute-start.27) | collective-permute-done | bytes 294944 | tf_op jit(solution)/shard_map/ppermute | solution.py:554
  74.3 2.1 %collective-permute-start.28 = (bf16[96,768]{1,0:T(8,128)(2,1)S(1)}, bf16[96,768]{1,0:T(8,128)(2,1)S(1)}, u32[]{:S(2)}, u32[]{:S(2)}) collective-permute-start(bf16[96,768]{1,0:T(8,128)(2,1)S(1)} %slice.175), channel_id=1, source_target_pairs={{0,16},{1,17},{2,18},{3,19},{4,20},{5,21},{6,22},{7,23},{8,24},{9,... | collective-permute-start | bytes 442376 | tf_op jit(solution)/shard_map/ppermute | solution.py:554
  76.4 3.9 %collective-permute-done.31 = bf16[96,1536]{1,0:T(8,128)(2,1)S(1)} collective-permute-done((bf16[96,1536]{1,0:T(8,128)(2,1)S(1)}, bf16[96,1536]{1,0:T(8,128)(2,1)S(1)}, u32[]{:S(2)}, u32[]{:S(2)}) %collective-permute-start.31) | collective-permute-done | bytes 294944 | tf_op jit(solution)/shard_map/ppermute | solution.py:554
  80.5 1.7 %collective-permute-start.33 = (bf16[24,1536]{1,0:T(8,128)(2,1)S(1)}, bf16[24,1536]{1,0:T(8,128)(2,1)S(1)}, u32[]{:S(2)}, u32[]{:S(2)}) collective-permute-start(bf16[24,1536]{1,0:T(8,128)(2,1)S(1)} %get-tuple-element.136), channel_id=1, source_target_pairs={{0,8},{1,9},{2,10},{3,11},{4,12},{5,13},{6,14},{7,15},{8,0},{9,1},... | collective-permute-start | bytes 221192 | tf_op jit(solution)/shard_map/ppermute | solution.py:554
  82.2 2.3 %collective-permute-start.34 = (bf16[24,1536]{1,0:T(8,128)(2,1)S(1)}, bf16[24,1536]{1,0:T(8,128)(2,1)S(1)}, u32[]{:S(2)}, u32[]{:S(2)}) collective-permute-start(bf16[24,1536]{1,0:T(8,128)(2,1)S(1)} %get-tuple-element.138), channel_id=1, source_target_pairs={{0,16},{1,17},{2,18},{3,19},{4,20},{5,21},{6,22},{7,23},{8,24},{9,... | collective-permute-start | bytes 221192 | tf_op jit(solution)/shard_map/ppermute | solution.py:554
  85.0 1.5 %collective-permute-start.39 = (bf16[24,768]{1,0:T(8,128)(2,1)S(1)}, bf16[24,768]{1,0:T(8,128)(2,1)S(1)}, u32[]{:S(2)}, u32[]{:S(2)}) collective-permute-start(bf16[24,768]{1,0:T(8,128)(2,1)S(1)} %slice.194), channel_id=1, source_target_pairs={{0,16},{1,17},{2,18},{3,19},{4,20},{5,21},{6,22},{7,23},{8,24},{9,... | collective-permute-start | bytes 110600 | tf_op jit(solution)/shard_map/ppermute | solution.py:554
  86.5 1.0 %collective-permute-start.29 = (bf16[48,768]{1,0:T(8,128)(2,1)S(1)}, bf16[48,768]{1,0:T(8,128)(2,1)S(1)}, u32[]{:S(2)}, u32[]{:S(2)}) collective-permute-start(bf16[48,768]{1,0:T(8,128)(2,1)S(1)} %slice.177), channel_id=1, source_target_pairs={{0,2},{1,3},{2,0},{3,1},{4,6},{5,7},{6,4},{7,5},{8,10},{9,11},{10,... | collective-permute-start | bytes 221192 | tf_op jit(solution)/shard_map/ppermute | solution.py:554
  87.6 2.1 %collective-permute-done.34 = bf16[24,1536]{1,0:T(8,128)(2,1)S(1)} collective-permute-done((bf16[24,1536]{1,0:T(8,128)(2,1)S(1)}, bf16[24,1536]{1,0:T(8,128)(2,1)S(1)}, u32[]{:S(2)}, u32[]{:S(2)}) %collective-permute-start.34) | collective-permute-done | bytes 73760 | tf_op jit(solution)/shard_map/ppermute | solution.py:554
  89.6 1.1 %collective-permute-done.35 = bf16[24,1536]{1,0:T(8,128)(2,1)S(1)} collective-permute-done((bf16[24,1536]{1,0:T(8,128)(2,1)S(1)}, bf16[24,1536]{1,0:T(8,128)(2,1)S(1)}, u32[]{:S(2)}, u32[]{:S(2)}) %collective-permute-start.35) | collective-permute-done | bytes 73760 | tf_op jit(solution)/shard_map/ppermute | solution.py:554
  91.0 1.4 %collective-permute-start.30 = (bf16[24,768]{1,0:T(8,128)(2,1)S(1)}, bf16[24,768]{1,0:T(8,128)(2,1)S(1)}, u32[]{:S(2)}, u32[]{:S(2)}) collective-permute-start(bf16[24,768]{1,0:T(8,128)(2,1)S(1)} %slice.179), channel_id=1, source_target_pairs={{0,4},{1,5},{2,6},{3,7},{4,0},{5,1},{6,2},{7,3},{8,12},{9,13},{10,... | collective-permute-start | bytes 110600 | tf_op jit(solution)/shard_map/ppermute | solution.py:554
  92.4 0.6 convert_add_fusion.1
  93.0 2.0 %collective-permute-done.30 = bf16[24,768]{1,0:T(8,128)(2,1)S(1)} collective-permute-done((bf16[24,768]{1,0:T(8,128)(2,1)S(1)}, bf16[24,768]{1,0:T(8,128)(2,1)S(1)}, u32[]{:S(2)}, u32[]{:S(2)}) %collective-permute-start.30) | collective-permute-done | bytes 36896 | tf_op jit(solution)/shard_map/ppermute | solution.py:554
  95.0 0.7 pad_maximum_fusion
  (138 shorter events, 6.6 us)
Async XLA Ops:
  0.6 14.5 %copy-start.10 = (s32[768,1]{1,0:T(8,128)S(1)}, s32[768,1]{1,0:T(8,128)}, u32[]{:S(2)}) copy-start(s32[768,1]{1,0:T(8,128)} %constant.14.clone) | copy-start | bytes 9220
  0.6 14.5 %copy-start.11 = (s32[768,1]{1,0:T(8,128)S(1)}, s32[768,1]{1,0:T(8,128)}, u32[]{:S(2)}) copy-start(s32[768,1]{1,0:T(8,128)} %constant.15.clone) | copy-start | bytes 9220
  0.7 14.5 %copy-start.12 = (s32[768,1]{1,0:T(8,128)S(1)}, s32[768,1]{1,0:T(8,128)}, u32[]{:S(2)}) copy-start(s32[768,1]{1,0:T(8,128)} %constant.16.clone) | copy-start | bytes 9220
  0.7 14.5 %copy-start.13 = (s32[768,1]{1,0:T(8,128)S(1)}, s32[768,1]{1,0:T(8,128)}, u32[]{:S(2)}) copy-start(s32[768,1]{1,0:T(8,128)} %constant.17.clone) | copy-start | bytes 9220
  6.3 10.6 %collective-permute-start = (bf16[8,3072]{1,0:T(8,128)(2,1)}, bf16[8,3072]{1,0:T(8,128)(2,1)S(1)}, u32[]{:S(2)}, u32[]{:S(2)}) collective-permute-start(bf16[8,3072]{1,0:T(8,128)(2,1)} %get-tuple-element.102), channel_id=1, source_target_pairs={{0,8},{1,9},{2,10},{3,11},{4,12},{5,13},{6,14},{7,15},{8,0},{9,1},... | collective-permute-start | bytes 147464 | tf_op jit(solution)/shard_map/ppermute | solution.py:554
  9.3 7.9 %collective-permute-start.1 = (bf16[8,3072]{1,0:T(8,128)(2,1)}, bf16[8,3072]{1,0:T(8,128)(2,1)S(1)}, u32[]{:S(2)}, u32[]{:S(2)}) collective-permute-start(bf16[8,3072]{1,0:T(8,128)(2,1)} %get-tuple-element.102), channel_id=1, source_target_pairs={{0,16},{1,17},{2,18},{3,19},{4,20},{5,21},{6,22},{7,23},{8,24},{9,... | collective-permute-start | bytes 147464 | tf_op jit(solution)/shard_map/ppermute | solution.py:554
  11.9 6.1 %collective-permute-start.2 = (bf16[8,3072]{1,0:T(8,128)(2,1)}, bf16[8,3072]{1,0:T(8,128)(2,1)S(1)}, u32[]{:S(2)}, u32[]{:S(2)}) collective-permute-start(bf16[8,3072]{1,0:T(8,128)(2,1)} %get-tuple-element.102), channel_id=1, source_target_pairs={{0,24},{1,25},{2,26},{3,27},{4,28},{5,29},{6,30},{7,31},{8,16},{9,... | collective-permute-start | bytes 147464 | tf_op jit(solution)/shard_map/ppermute | solution.py:554
  11.9 6.1 %collective-permute-start.3 = (bf16[32,1536]{1,0:T(8,128)(2,1)}, bf16[32,1536]{1,0:T(8,128)(2,1)S(1)}, u32[]{:S(2)}, u32[]{:S(2)}) collective-permute-start(bf16[32,1536]{1,0:T(8,128)(2,1)} %get-tuple-element.66), channel_id=1, source_target_pairs={{0,2},{1,3},{2,0},{3,1},{4,6},{5,7},{6,4},{7,5},{8,10},{9,11},{10,... | collective-permute-start | bytes 294920 | tf_op jit(solution)/shard_map/ppermute | solution.py:554
  13.7 5.1 %collective-permute-start.4 = (bf16[32,1536]{1,0:T(8,128)(2,1)}, bf16[32,1536]{1,0:T(8,128)(2,1)S(1)}, u32[]{:S(2)}, u32[]{:S(2)}) collective-permute-start(bf16[32,1536]{1,0:T(8,128)(2,1)} %get-tuple-element.66), channel_id=1, source_target_pairs={{0,4},{1,5},{2,6},{3,7},{4,0},{5,1},{6,2},{7,3},{8,12},{9,13},{10,... | collective-permute-start | bytes 294920 | tf_op jit(solution)/shard_map/ppermute | solution.py:554
  15.2 7.5 %copy-start.8 = (bf16[256,768]{1,0:T(8,128)(2,1)S(1)}, bf16[256,768]{1,0:T(8,128)(2,1)}, u32[]{:S(2)}) copy-start(bf16[256,768]{1,0:T(8,128)(2,1)} %get-tuple-element.69.v) | copy-start | bytes 1179652
  15.2 7.5 %copy-start.9 = (bf16[256,768]{1,0:T(8,128)(2,1)S(1)}, bf16[256,768]{1,0:T(8,128)(2,1)}, u32[]{:S(2)}) copy-start(bf16[256,768]{1,0:T(8,128)(2,1)} %get-tuple-element.70.g) | copy-start | bytes 1179652
  16.1 6.7 %copy-start.7 = (bf16[256,768]{1,0:T(8,128)(2,1)S(1)}, bf16[256,768]{1,0:T(8,128)(2,1)}, u32[]{:S(2)}) copy-start(bf16[256,768]{1,0:T(8,128)(2,1)} %get-tuple-element.68.k) | copy-start | bytes 1179652
  16.9 5.7 %collective-permute-start.5 = (bf16[32,1536]{1,0:T(8,128)(2,1)S(1)}, bf16[32,1536]{1,0:T(8,128)(2,1)S(1)}, u32[]{:S(2)}, u32[]{:S(2)}) collective-permute-start(bf16[32,1536]{1,0:T(8,128)(2,1)S(1)} %copy-done.15), channel_id=1, source_target_pairs={{0,6},{1,7},{2,4},{3,5},{4,2},{5,3},{6,0},{7,1},{8,14},{9,15},{10,... | collective-permute-start | bytes 294920 | tf_op jit(solution)/shard_map/ppermute | solution.py:554
  18.7 6.6 %collective-permute-start.7 = (bf16[32,1536]{1,0:T(8,128)(2,1)S(1)}, bf16[32,1536]{1,0:T(8,128)(2,1)S(1)}, u32[]{:S(2)}, u32[]{:S(2)}) collective-permute-start(bf16[32,1536]{1,0:T(8,128)(2,1)S(1)} %pad_maximum_fusion.1), channel_id=1, source_target_pairs={{0,2},{1,3},{2,0},{3,1},{4,6},{5,7},{6,4},{7,5},{8,10},{9,11},{10,... | collective-permute-start | bytes 294920 | tf_op jit(solution)/shard_map/ppermute | solution.py:554
  19.6 5.7 %collective-permute-start.8 = (bf16[32,1536]{1,0:T(8,128)(2,1)S(1)}, bf16[32,1536]{1,0:T(8,128)(2,1)S(1)}, u32[]{:S(2)}, u32[]{:S(2)}) collective-permute-start(bf16[32,1536]{1,0:T(8,128)(2,1)S(1)} %pad_maximum_fusion.1), channel_id=1, source_target_pairs={{0,4},{1,5},{2,6},{3,7},{4,0},{5,1},{6,2},{7,3},{8,12},{9,13},{10,... | collective-permute-start | bytes 294920 | tf_op jit(solution)/shard_map/ppermute | solution.py:554
  21.6 5.5 %collective-permute-start.9 = (bf16[32,1536]{1,0:T(8,128)(2,1)S(1)}, bf16[32,1536]{1,0:T(8,128)(2,1)S(1)}, u32[]{:S(2)}, u32[]{:S(2)}) collective-permute-start(bf16[32,1536]{1,0:T(8,128)(2,1)S(1)} %pad_maximum_fusion.1), channel_id=1, source_target_pairs={{0,6},{1,7},{2,4},{3,5},{4,2},{5,3},{6,0},{7,1},{8,14},{9,15},{10,... | collective-permute-start | bytes 294920 | tf_op jit(solution)/shard_map/ppermute | solution.py:554
  22.6 4.6 %collective-permute-start.6 = (bf16[128,1536]{1,0:T(8,128)(2,1)S(1)}, bf16[128,1536]{1,0:T(8,128)(2,1)S(1)}, u32[]{:S(2)}, u32[]{:S(2)}) collective-permute-start(bf16[128,1536]{1,0:T(8,128)(2,1)S(1)} %constant_dynamic-update-slice_fusion.mid_0), channel_id=1, source_target_pairs={{0,1},{1,0},{2,3},{3,2},{4,5},{5,4},{6,7},{7,6},{8,9},{9,8},{10,11... | collective-permute-start | bytes 1179656 | tf_op jit(solution)/shard_map/ppermute | solution.py:554
  27.2 1.8 %collective-permute-start.10 = (bf16[128,1536]{1,0:T(8,128)(2,1)S(1)}, bf16[128,1536]{1,0:T(8,128)(2,1)S(1)}, u32[]{:S(2)}, u32[]{:S(2)}) collective-permute-start(bf16[128,1536]{1,0:T(8,128)(2,1)S(1)} %constant_dynamic-update-slice_fusion.4.far_0), channel_id=1, source_target_pairs={{0,1},{1,0},{2,3},{3,2},{4,5},{5,4},{6,7},{7,6},{8,9},{9,8},{10,11... | collective-permute-start | bytes 1179656 | tf_op jit(solution)/shard_map/ppermute | solution.py:554
  31.3 9.9 %copy-start.2 = (bf16[768,768]{1,0:T(8,128)(2,1)S(1)}, bf16[768,768]{1,0:T(8,128)(2,1)}, u32[]{:S(2)}) copy-start(bf16[768,768]{1,0:T(8,128)(2,1)} %w_out.1) | copy-start | bytes 3538948
  31.3 6.2 %collective-permute-start.11 = (f32[8,128]{1,0:T(8,128)S(1)}, f32[8,128]{1,0:T(8,128)S(1)}, u32[]{:S(2)}, u32[]{:S(2)}) collective-permute-start(f32[8,128]{1,0:T(8,128)S(1)} %slice.130), channel_id=1, source_target_pairs={{0,8},{1,9},{2,10},{3,11},{4,12},{5,13},{6,14},{7,15},{8,0},{9,1},... | collective-permute-start | bytes 12296 | tf_op jit(solution)/shard_map/ppermute | solution.py:554
  34.0 20.0 %collective-permute-start.17 = (bf16[64,1536]{1,0:T(8,128)(2,1)S(1)}, bf16[64,1536]{1,0:T(8,128)(2,1)S(1)}, u32[]{:S(2)}, u32[]{:S(2)}) collective-permute-start(bf16[64,1536]{1,0:T(8,128)(2,1)S(1)} %constant_dynamic-update-slice_fusion.14), channel_id=1, source_target_pairs={{0,2},{1,3},{2,0},{3,1},{4,6},{5,7},{6,4},{7,5},{8,10},{9,11},{10,... | collective-permute-start | bytes 589832 | tf_op jit(solution)/shard_map/ppermute | solution.py:554
  35.5 18.5 %collective-permute-start.18 = (bf16[64,1536]{1,0:T(8,128)(2,1)S(1)}, bf16[64,1536]{1,0:T(8,128)(2,1)S(1)}, u32[]{:S(2)}, u32[]{:S(2)}) collective-permute-start(bf16[64,1536]{1,0:T(8,128)(2,1)S(1)} %constant_dynamic-update-slice_fusion.14), channel_id=1, source_target_pairs={{0,4},{1,5},{2,6},{3,7},{4,0},{5,1},{6,2},{7,3},{8,12},{9,13},{10,... | collective-permute-start | bytes 589832 | tf_op jit(solution)/shard_map/ppermute | solution.py:554
  35.7 18.9 %collective-permute-start.19 = (bf16[64,1536]{1,0:T(8,128)(2,1)S(1)}, bf16[64,1536]{1,0:T(8,128)(2,1)S(1)}, u32[]{:S(2)}, u32[]{:S(2)}) collective-permute-start(bf16[64,1536]{1,0:T(8,128)(2,1)S(1)} %constant_dynamic-update-slice_fusion.14), channel_id=1, source_target_pairs={{0,6},{1,7},{2,4},{3,5},{4,2},{5,3},{6,0},{7,1},{8,14},{9,15},{10,... | collective-permute-start | bytes 589832 | tf_op jit(solution)/shard_map/ppermute | solution.py:554
  37.5 6.3 %collective-permute-start.15 = (bf16[256,768]{1,0:T(8,128)(2,1)S(1)}, bf16[256,768]{1,0:T(8,128)(2,1)S(1)}, u32[]{:S(2)}, u32[]{:S(2)}) collective-permute-start(bf16[256,768]{1,0:T(8,128)(2,1)S(1)} %copy-done.4), channel_id=1, source_target_pairs={{0,1},{1,0},{2,3},{3,2},{4,5},{5,4},{6,7},{7,6},{8,9},{9,8},{10,11... | collective-permute-start | bytes 1179656 | tf_op jit(solution)/shard_map/ppermute | solution.py:554
  37.5 6.1 %collective-permute-start.12 = (f32[16,128]{1,0:T(8,128)S(1)}, f32[16,128]{1,0:T(8,128)S(1)}, u32[]{:S(2)}, u32[]{:S(2)}) collective-permute-start(f32[16,128]{1,0:T(8,128)S(1)} %constant_dynamic-update-slice_fusion.8), channel_id=1, source_target_pairs={{0,16},{1,17},{2,18},{3,19},{4,20},{5,21},{6,22},{7,23},{8,24},{9,... | collective-permute-start | bytes 24584 | tf_op jit(solution)/shard_map/ppermute | solution.py:554
  43.7 1.4 %collective-permute-start.14 = (bf16[384,256]{1,0:T(8,128)(2,1)S(1)}, bf16[384,256]{1,0:T(8,128)(2,1)S(1)}, u32[]{:S(2)}, u32[]{:S(2)}) collective-permute-start(bf16[384,256]{1,0:T(8,128)(2,1)S(1)} %get-tuple-element.90), channel_id=1, source_target_pairs={{0,1},{1,0},{2,3},{3,2},{4,5},{5,4},{6,7},{7,6},{8,9},{9,8},{10,11... | collective-permute-start | bytes 589832 | tf_op jit(solution)/shard_map/ppermute | solution.py:554
  43.8 4.0 %collective-permute-start.13 = (f32[32,256]{1,0:T(8,128)S(1)}, f32[32,256]{1,0:T(8,128)S(1)}, u32[]{:S(2)}, u32[]{:S(2)}) collective-permute-start(f32[32,256]{1,0:T(8,128)S(1)} %pad_maximum_fusion.2), channel_id=1, source_target_pairs={{0,4},{1,5},{2,6},{3,7},{4,0},{5,1},{6,2},{7,3},{8,12},{9,13},{10,... | collective-permute-start | bytes 98312 | tf_op jit(solution)/shard_map/ppermute | solution.py:554
  47.8 7.0 %collective-permute-start.21 = (f32[64,256]{1,0:T(8,128)S(1)}, f32[64,256]{1,0:T(8,128)S(1)}, u32[]{:S(2)}, u32[]{:S(2)}) collective-permute-start(f32[64,256]{1,0:T(8,128)S(1)} %constant_dynamic-update-slice_fusion.12), channel_id=1, source_target_pairs={{0,2},{1,3},{2,0},{3,1},{4,6},{5,7},{6,4},{7,5},{8,10},{9,11},{10,... | collective-permute-start | bytes 196616 | tf_op jit(solution)/shard_map/ppermute | solution.py:554
  49.4 8.6 %collective-permute-start.36 = (bf16[192,768]{1,0:T(8,128)(2,1)S(1)}, bf16[192,768]{1,0:T(8,128)(2,1)S(1)}, u32[]{:S(2)}, u32[]{:S(2)}) collective-permute-start(bf16[192,768]{1,0:T(8,128)(2,1)S(1)} %get-tuple-element.127), channel_id=1, source_target_pairs={{0,2},{1,3},{2,0},{3,1},{4,6},{5,7},{6,4},{7,5},{8,10},{9,11},{10,... | collective-permute-start | bytes 884744 | tf_op jit(solution)/shard_map/ppermute | solution.py:554
  54.0 3.9 %collective-permute-start.16 = (bf16[768,256]{1,0:T(8,128)(2,1)S(1)}, bf16[768,256]{1,0:T(8,128)(2,1)S(1)}, u32[]{:S(2)}, u32[]{:S(2)}) collective-permute-start(bf16[768,256]{1,0:T(8,128)(2,1)S(1)} %get-tuple-element.99), channel_id=1, source_target_pairs={{0,1},{1,0},{2,3},{3,2},{4,5},{5,4},{6,7},{7,6},{8,9},{9,8},{10,11... | collective-permute-start | bytes 1179656 | tf_op jit(solution)/shard_map/ppermute | solution.py:554
  54.1 3.9 %collective-permute-start.23 = (bf16[256,768]{1,0:T(8,128)(2,1)S(1)}, bf16[256,768]{1,0:T(8,128)(2,1)S(1)}, u32[]{:S(2)}, u32[]{:S(2)}) collective-permute-start(bf16[256,768]{1,0:T(8,128)(2,1)S(1)} %get-tuple-element.117.right.dq), channel_id=1, source_target_pairs={{0,1},{1,0},{2,3},{3,2},{4,5},{5,4},{6,7},{7,6},{8,9},{9,8},{10,11... | collective-permute-start | bytes 1179656 | tf_op jit(solution)/shard_map/ppermute | solution.py:554
  54.7 3.8 %collective-permute-start.20 = (bf16[256,1536]{1,0:T(8,128)(2,1)S(1)}, bf16[256,1536]{1,0:T(8,128)(2,1)S(1)}, u32[]{:S(2)}, u32[]{:S(2)}) collective-permute-start(bf16[256,1536]{1,0:T(8,128)(2,1)S(1)} %constant_dynamic-update-slice_fusion.19.qg_0), channel_id=1, source_target_pairs={{0,1},{1,0},{2,3},{3,2},{4,5},{5,4},{6,7},{7,6},{8,9},{9,8},{10,11... | collective-permute-start | bytes 2359304 | tf_op jit(solution)/shard_map/ppermute | solution.py:554
  54.9 3.5 %collective-permute-start.22 = (f32[256,128]{1,0:T(8,128)S(1)}, f32[256,128]{1,0:T(8,128)S(1)}, u32[]{:S(2)}, u32[]{:S(2)}) collective-permute-start(f32[256,128]{1,0:T(8,128)S(1)} %constant_dynamic-update-slice_fusion.23.stats_0), channel_id=1, source_target_pairs={{0,1},{1,0},{2,3},{3,2},{4,5},{5,4},{6,7},{7,6},{8,9},{9,8},{10,11... | collective-permute-start | bytes 393224 | tf_op jit(solution)/shard_map/ppermute | solution.py:554
  60.8 1.8 %collective-permute-start.24 = (bf16[256,768]{1,0:T(8,128)(2,1)S(1)}, bf16[256,768]{1,0:T(8,128)(2,1)S(1)}, u32[]{:S(2)}, u32[]{:S(2)}) collective-permute-start(bf16[256,768]{1,0:T(8,128)(2,1)S(1)} %get-tuple-element.115.dk), channel_id=1, source_target_pairs={{0,1},{1,0},{2,3},{3,2},{4,5},{5,4},{6,7},{7,6},{8,9},{9,8},{10,11... | collective-permute-start | bytes 1179656 | tf_op jit(solution)/shard_map/ppermute | solution.py:554
  60.9 2.3 %collective-permute-start.25 = (bf16[256,768]{1,0:T(8,128)(2,1)S(1)}, bf16[256,768]{1,0:T(8,128)(2,1)S(1)}, u32[]{:S(2)}, u32[]{:S(2)}) collective-permute-start(bf16[256,768]{1,0:T(8,128)(2,1)S(1)} %get-tuple-element.116.dv), channel_id=1, source_target_pairs={{0,1},{1,0},{2,3},{3,2},{4,5},{5,4},{6,7},{7,6},{8,9},{9,8},{10,11... | collective-permute-start | bytes 1179656 | tf_op jit(solution)/shard_map/ppermute | solution.py:554
  61.5 8.3 %collective-permute-start.37 = (bf16[96,768]{1,0:T(8,128)(2,1)S(1)}, bf16[96,768]{1,0:T(8,128)(2,1)S(1)}, u32[]{:S(2)}, u32[]{:S(2)}) collective-permute-start(bf16[96,768]{1,0:T(8,128)(2,1)S(1)} %get-tuple-element.134), channel_id=1, source_target_pairs={{0,4},{1,5},{2,6},{3,7},{4,0},{5,1},{6,2},{7,3},{8,12},{9,13},{10,... | collective-permute-start | bytes 442376 | tf_op jit(solution)/shard_map/ppermute | solution.py:554
  64.0 9.9 %collective-permute-start.27 = (bf16[96,1536]{1,0:T(8,128)(2,1)S(1)}, bf16[96,1536]{1,0:T(8,128)(2,1)S(1)}, u32[]{:S(2)}, u32[]{:S(2)}) collective-permute-start(bf16[96,1536]{1,0:T(8,128)(2,1)S(1)} %get-tuple-element.124), channel_id=1, source_target_pairs={{0,2},{1,3},{2,0},{3,1},{4,6},{5,7},{6,4},{7,5},{8,10},{9,11},{10,... | collective-permute-start | bytes 884744 | tf_op jit(solution)/shard_map/ppermute | solution.py:554
  65.1 9.2 %collective-permute-start.26 = (bf16[192,768]{1,0:T(8,128)(2,1)S(1)}, bf16[192,768]{1,0:T(8,128)(2,1)S(1)}, u32[]{:S(2)}, u32[]{:S(2)}) collective-permute-start(bf16[192,768]{1,0:T(8,128)(2,1)S(1)} %get-tuple-element.129), channel_id=1, source_target_pairs={{0,8},{1,9},{2,10},{3,11},{4,12},{5,13},{6,14},{7,15},{8,0},{9,1},... | collective-permute-start | bytes 884744 | tf_op jit(solution)/shard_map/ppermute | solution.py:554
  65.4 14.9 %collective-permute-start.31 = (bf16[96,1536]{1,0:T(8,128)(2,1)S(1)}, bf16[96,1536]{1,0:T(8,128)(2,1)S(1)}, u32[]{:S(2)}, u32[]{:S(2)}) collective-permute-start(bf16[96,1536]{1,0:T(8,128)(2,1)S(1)} %get-tuple-element.126), channel_id=1, source_target_pairs={{0,4},{1,5},{2,6},{3,7},{4,0},{5,1},{6,2},{7,3},{8,12},{9,13},{10,... | collective-permute-start | bytes 884744 | tf_op jit(solution)/shard_map/ppermute | solution.py:554
  66.6 13.7 %collective-permute-start.32 = (bf16[96,1536]{1,0:T(8,128)(2,1)S(1)}, bf16[96,1536]{1,0:T(8,128)(2,1)S(1)}, u32[]{:S(2)}, u32[]{:S(2)}) collective-permute-start(bf16[96,1536]{1,0:T(8,128)(2,1)S(1)} %get-tuple-element.125), channel_id=1, source_target_pairs={{0,6},{1,7},{2,4},{3,5},{4,2},{5,3},{6,0},{7,1},{8,14},{9,15},{10,... | collective-permute-start | bytes 884744 | tf_op jit(solution)/shard_map/ppermute | solution.py:554
  74.0 11.0 %collective-permute-start.38 = (bf16[48,768]{1,0:T(8,128)(2,1)S(1)}, bf16[48,768]{1,0:T(8,128)(2,1)S(1)}, u32[]{:S(2)}, u32[]{:S(2)}) collective-permute-start(bf16[48,768]{1,0:T(8,128)(2,1)S(1)} %slice.192), channel_id=1, source_target_pairs={{0,8},{1,9},{2,10},{3,11},{4,12},{5,13},{6,14},{7,15},{8,0},{9,1},... | collective-permute-start | bytes 221192 | tf_op jit(solution)/shard_map/ppermute | solution.py:554
  74.3 12.1 %collective-permute-start.28 = (bf16[96,768]{1,0:T(8,128)(2,1)S(1)}, bf16[96,768]{1,0:T(8,128)(2,1)S(1)}, u32[]{:S(2)}, u32[]{:S(2)}) collective-permute-start(bf16[96,768]{1,0:T(8,128)(2,1)S(1)} %slice.175), channel_id=1, source_target_pairs={{0,16},{1,17},{2,18},{3,19},{4,20},{5,21},{6,22},{7,23},{8,24},{9,... | collective-permute-start | bytes 442376 | tf_op jit(solution)/shard_map/ppermute | solution.py:554
  80.5 7.1 %collective-permute-start.33 = (bf16[24,1536]{1,0:T(8,128)(2,1)S(1)}, bf16[24,1536]{1,0:T(8,128)(2,1)S(1)}, u32[]{:S(2)}, u32[]{:S(2)}) collective-permute-start(bf16[24,1536]{1,0:T(8,128)(2,1)S(1)} %get-tuple-element.136), channel_id=1, source_target_pairs={{0,8},{1,9},{2,10},{3,11},{4,12},{5,13},{6,14},{7,15},{8,0},{9,1},... | collective-permute-start | bytes 221192 | tf_op jit(solution)/shard_map/ppermute | solution.py:554
  82.2 7.4 %collective-permute-start.34 = (bf16[24,1536]{1,0:T(8,128)(2,1)S(1)}, bf16[24,1536]{1,0:T(8,128)(2,1)S(1)}, u32[]{:S(2)}, u32[]{:S(2)}) collective-permute-start(bf16[24,1536]{1,0:T(8,128)(2,1)S(1)} %get-tuple-element.138), channel_id=1, source_target_pairs={{0,16},{1,17},{2,18},{3,19},{4,20},{5,21},{6,22},{7,23},{8,24},{9,... | collective-permute-start | bytes 221192 | tf_op jit(solution)/shard_map/ppermute | solution.py:554
  84.5 6.3 %collective-permute-start.35 = (bf16[24,1536]{1,0:T(8,128)(2,1)S(1)}, bf16[24,1536]{1,0:T(8,128)(2,1)S(1)}, u32[]{:S(2)}, u32[]{:S(2)}) collective-permute-start(bf16[24,1536]{1,0:T(8,128)(2,1)S(1)} %get-tuple-element.137), channel_id=1, source_target_pairs={{0,24},{1,25},{2,26},{3,27},{4,28},{5,29},{6,30},{7,31},{8,16},{9,... | collective-permute-start | bytes 221192 | tf_op jit(solution)/shard_map/ppermute | solution.py:554
  85.0 7.4 %collective-permute-start.39 = (bf16[24,768]{1,0:T(8,128)(2,1)S(1)}, bf16[24,768]{1,0:T(8,128)(2,1)S(1)}, u32[]{:S(2)}, u32[]{:S(2)}) collective-permute-start(bf16[24,768]{1,0:T(8,128)(2,1)S(1)} %slice.194), channel_id=1, source_target_pairs={{0,16},{1,17},{2,18},{3,19},{4,20},{5,21},{6,22},{7,23},{8,24},{9,... | collective-permute-start | bytes 110600 | tf_op jit(solution)/shard_map/ppermute | solution.py:554
  86.5 4.4 %collective-permute-start.29 = (bf16[48,768]{1,0:T(8,128)(2,1)S(1)}, bf16[48,768]{1,0:T(8,128)(2,1)S(1)}, u32[]{:S(2)}, u32[]{:S(2)}) collective-permute-start(bf16[48,768]{1,0:T(8,128)(2,1)S(1)} %slice.177), channel_id=1, source_target_pairs={{0,2},{1,3},{2,0},{3,1},{4,6},{5,7},{6,4},{7,5},{8,10},{9,11},{10,... | collective-permute-start | bytes 221192 | tf_op jit(solution)/shard_map/ppermute | solution.py:554
  91.0 4.0 %collective-permute-start.30 = (bf16[24,768]{1,0:T(8,128)(2,1)S(1)}, bf16[24,768]{1,0:T(8,128)(2,1)S(1)}, u32[]{:S(2)}, u32[]{:S(2)}) collective-permute-start(bf16[24,768]{1,0:T(8,128)(2,1)S(1)} %slice.179), channel_id=1, source_target_pairs={{0,4},{1,5},{2,6},{3,7},{4,0},{5,1},{6,2},{7,3},{8,12},{9,13},{10,... | collective-permute-start | bytes 110600 | tf_op jit(solution)/shard_map/ppermute | solution.py:554
  (9 other events, 41.1 us)

commit v10 on v9

--- a/solution.py
+++ b/solution.py
@@ -760,8 +760,10 @@
     )(after(dq, late_half), dk, dv, w_qkv)
     late_parts = block_parts(late_half, PLANE, n)
     early = halved(early_half, masks + [2, 4], n, ((late_parts[1],),))
-    grad_wout = halved(wout_half, [2, 4] + masks, n, ((dk_near,), (late_parts[1],)))
-    late = reduce_all(sum_parts(late_parts, BF), upper_steps(n)[::-1], n)
+    wout = halved(wout_half, [2, 4] + masks[:-1], n, ((dk_near,), (late_parts[1],))).astype(BF)
+    late = sum_parts(tied(late_parts, (wout,)), BF)
+    grad_wout = halved(wout, masks[-1:], n)
+    late = reduce_all(late, upper_steps(n)[::-1], n)
     grad_wqkv = jnp.concatenate([early, late], axis=1)
     return out_rows, grad_tiles, grad_wqkv, grad_wout
 

time: 95.9 us -> 95.2 us (level)
  waiting for transfers between devices: 25.4 us -> 23.6 us
  starting transfers between devices: 40.3 us -> 41.3 us
    ppermute x40, waiting for transfers between devices: 25.4 us -> 23.6 us  [swap(): return lax.ppermute(value, 'ctx', [(d, d ^ mask) for d in range(dev_count)])]
    ppermute x40, starting transfers between devices: 40.3 us -> 41.3 us  [swap(): return lax.ppermute(value, 'ctx', [(d, d ^ mask) for d in range(dev_count)])]
  transfers between devices with their start and end apart: 40 -> 40, of which waited for: 16 -> 14; matrix products, arithmetic and copies ran while one was open for 2% -> 2% of each run, Pallas kernels for 15% -> 15%
where the time goes in v10:
time: 95.2 us; the launch traced here: 95 us
  starting transfers between devices  41.3 us (43%)
  Pallas kernels  24.8 us (26%)
  waiting for transfers between devices  23.6 us (25%)
  between operations  2.08 us (2%)
  other arithmetic  1.94 us (2%)
  local copies, waits for them, and re-layouts  1.27 us (1%)
    ppermute x40, starting transfers between devices, swap(): return lax.ppermute(value, 'ctx', [(d, d ^ mask) for d in range(dev_count)])  41.3 us
    pallas_call x11, Pallas kernels, run(): pl.pallas_call(kernel, out_shape=tuple((jax.ShapeDtypeStruct(s, t) for s,...  24.8 us
    ppermute x40, waiting for transfers between devices, swap(): return lax.ppermute(value, 'ctx', [(d, d ^ mask) for d in range(dev_count)])  23.6 us
  transfers between devices with their start and end apart: 40, of which 14 were waited for; matrix products, arithmetic and copies ran while one was open for 2% of the time, Pallas kernels for 15%

profile of v10, /device:TPU:0, one launch (start us, length us, event | category | flops | bytes accessed | tf_op | source)
XLA Modules:
  0.0 95.0 jit_solution(12327120705528308117)
XLA Ops:
  0.7 5.6 %shard_map.147 = (bf16[256,768]{1,0:T(8,128)(2,1)}, bf16[256,768]{1,0:T(8,128)(2,1)}, bf16[256,768]{1,0:T(8,128)(2,1)}, bf16[256,768]{1,0:T(8,128)(2,1)}, bf16[6...) custom-call(s32[2,12]{1,0:T(2,128)} %offs_ref.9, ...), custom_call_target="tpu_custom_call" | custom-call | flops 1207959552 | bytes 7716960 | tf_op jit(solution)/shard_map/pallas_call | solution.py:535
  6.3 3.1 %collective-permute-start = (bf16[8,3072]{1,0:T(8,128)(2,1)}, bf16[8,3072]{1,0:T(8,128)(2,1)S(1)}, u32[]{:S(2)}, u32[]{:S(2)}) collective-permute-start(bf16[8,3072]{1,0:T(8,128)(2,1)} %get-tuple-element.106), channel_id=1, source_target_pairs={{0,8},{1,9},{2,10},{3,11},{4,12},{5,13},{6,14},{7,15},{8,0},{9,1},... | collective-permute-start | bytes 147464 | tf_op jit(solution)/shard_map/ppermute | solution.py:554
  9.3 2.6 %collective-permute-start.1 = (bf16[8,3072]{1,0:T(8,128)(2,1)}, bf16[8,3072]{1,0:T(8,128)(2,1)S(1)}, u32[]{:S(2)}, u32[]{:S(2)}) collective-permute-start(bf16[8,3072]{1,0:T(8,128)(2,1)} %get-tuple-element.106), channel_id=1, source_target_pairs={{0,16},{1,17},{2,18},{3,19},{4,20},{5,21},{6,22},{7,23},{8,24},{9,... | collective-permute-start | bytes 147464 | tf_op jit(solution)/shard_map/ppermute | solution.py:554
  11.9 1.7 %collective-permute-start.3 = (bf16[32,1536]{1,0:T(8,128)(2,1)}, bf16[32,1536]{1,0:T(8,128)(2,1)S(1)}, u32[]{:S(2)}, u32[]{:S(2)}) collective-permute-start(bf16[32,1536]{1,0:T(8,128)(2,1)} %get-tuple-element.70), channel_id=1, source_target_pairs={{0,2},{1,3},{2,0},{3,1},{4,6},{5,7},{6,4},{7,5},{8,10},{9,11},{10,... | collective-permute-start | bytes 294920 | tf_op jit(solution)/shard_map/ppermute | solution.py:554
  13.7 1.5 %collective-permute-start.4 = (bf16[32,1536]{1,0:T(8,128)(2,1)}, bf16[32,1536]{1,0:T(8,128)(2,1)S(1)}, u32[]{:S(2)}, u32[]{:S(2)}) collective-permute-start(bf16[32,1536]{1,0:T(8,128)(2,1)} %get-tuple-element.70), channel_id=1, source_target_pairs={{0,4},{1,5},{2,6},{3,7},{4,0},{5,1},{6,2},{7,3},{8,12},{9,13},{10,... | collective-permute-start | bytes 294920 | tf_op jit(solution)/shard_map/ppermute | solution.py:554
  15.4 0.7 copy-done.15
  17.2 0.8 collective-permute-done.2
  18.1 0.6 collective-permute-done.4
  18.7 0.9 collective-permute-start.7
  19.6 2.0 %collective-permute-start.8 = (bf16[32,1536]{1,0:T(8,128)(2,1)S(1)}, bf16[32,1536]{1,0:T(8,128)(2,1)S(1)}, u32[]{:S(2)}, u32[]{:S(2)}) collective-permute-start(bf16[32,1536]{1,0:T(8,128)(2,1)S(1)} %pad_maximum_fusion.1), channel_id=1, source_target_pairs={{0,4},{1,5},{2,6},{3,7},{4,0},{5,1},{6,2},{7,3},{8,12},{9,13},{10,... | collective-permute-start | bytes 294920 | tf_op jit(solution)/shard_map/ppermute | solution.py:554
  21.6 0.9 collective-permute-start.9
  22.8 2.6 %shard_map.148 = (f32[256,768]{1,0:T(8,128)S(1)}, f32[256,128]{1,0:T(8,128)S(1)}, bf16[768,256]{1,0:T(8,128)(2,1)S(1)}, bf16[768,256]{1,0:T(8,128)(2,1)S(1)}) custom-call(s32[1]{0:T(128)S(6)} %copy.42.pad_ref, bf16[256,768]{1,0:T(8,128)(2,1)S(1)} %copy-done.6, bf16[256,768]{1,0:T(8,128)(2,1)S(1)} %copy-done.7, bf16[256,768]{1,0:T(8,128)(2,1)S(1)} %copy-done.8, ...), custom_call_target="tpu_custom_call" | custom-call | flops 805306368 | bytes 3676164 | tf_op jit(solution)/shard_map/pallas_call | solution.py:535
  25.4 1.7 %collective-permute-done.9 = bf16[32,1536]{1,0:T(8,128)(2,1)S(1)} collective-permute-done((bf16[32,1536]{1,0:T(8,128)(2,1)S(1)}, bf16[32,1536]{1,0:T(8,128)(2,1)S(1)}, u32[]{:S(2)}, u32[]{:S(2)}) %collective-permute-start.9) | collective-permute-done | bytes 98336 | tf_op jit(solution)/shard_map/ppermute | solution.py:554
  27.2 1.7 %collective-permute-done.10.far_1 = bf16[128,1536]{1,0:T(8,128)(2,1)S(1)} collective-permute-done((bf16[128,1536]{1,0:T(8,128)(2,1)S(1)}, bf16[128,1536]{1,0:T(8,128)(2,1)S(1)}, u32[]{:S(2)}, u32[]{:S(2)}) %collective-permute-start.10) | collective-permute-done | bytes 393248 | tf_op jit(solution)/shard_map/ppermute | solution.py:554
  29.0 2.3 %shard_map.149 = (f32[256,128]{1,0:T(8,128)S(1)}, f32[64,128]{1,0:T(8,128)S(1)}, f32[64,128]{1,0:T(8,128)S(1)}, f32[64,768]{1,0:T(8,128)S(1)}) custom-call(s32[2,12]{1,0:T(2,128)S(1)} %copy-done.5, s32[1]{0:T(128)S(6)} %copy.42.pad_ref, bf16[64,3072]{1,0:T(8,128)(2,1)S(1)} %copy-done.1, bf16[128,1536]{1,0:T(8,128)(2,1)S(1)} %constant_dynamic-update-slice_fusion.mid_0, ...), custom_call_target="tpu_custom_call" | custom-call | flops 301989888 | bytes 2490468 | tf_op jit(solution)/shard_map/pallas_call | solution.py:535
  31.3 0.7 collective-permute-start.11
  32.0 1.8 %shard_map.150.dq_sel = f32[64,768]{1,0:T(8,128)S(1)} custom-call(s32[2,12]{1,0:T(2,128)S(1)} %copy-done.5, s32[1]{0:T(128)S(6)} %copy.42.pad_ref, bf16[64,3072]{1,0:T(8,128)(2,1)S(1)} %copy-done.1, bf16[128,1536]{1,0:T(8,128)(2,1)S(1)} %constant_dynamic-update-slice_fusion.mid_0, bf16[128,1536]{1,0:T(8,128)(2,1)S(1)} %collective-permute-done.6.mid_1, ...), custom_call_target="tpu_custom_call" | custom-call | flops 201326592 | bytes 2195556 | tf_op jit(solution)/shard_map/pallas_call | solution.py:535
  34.0 1.6 %collective-permute-start.17 = (bf16[64,1536]{1,0:T(8,128)(2,1)S(1)}, bf16[64,1536]{1,0:T(8,128)(2,1)S(1)}, u32[]{:S(2)}, u32[]{:S(2)}) collective-permute-start(bf16[64,1536]{1,0:T(8,128)(2,1)S(1)} %constant_dynamic-update-slice_fusion.14), channel_id=1, source_target_pairs={{0,2},{1,3},{2,0},{3,1},{4,6},{5,7},{6,4},{7,5},{8,10},{9,11},{10,... | collective-permute-start | bytes 589832 | tf_op jit(solution)/shard_map/ppermute | solution.py:554
  35.7 1.8 %collective-permute-start.19 = (bf16[64,1536]{1,0:T(8,128)(2,1)S(1)}, bf16[64,1536]{1,0:T(8,128)(2,1)S(1)}, u32[]{:S(2)}, u32[]{:S(2)}) collective-permute-start(bf16[64,1536]{1,0:T(8,128)(2,1)S(1)} %constant_dynamic-update-slice_fusion.14), channel_id=1, source_target_pairs={{0,6},{1,7},{2,4},{3,5},{4,2},{5,3},{6,0},{7,1},{8,14},{9,15},{10,... | collective-permute-start | bytes 589832 | tf_op jit(solution)/shard_map/ppermute | solution.py:554
  37.5 3.6 %collective-permute-start.12 = (f32[16,128]{1,0:T(8,128)S(1)}, f32[16,128]{1,0:T(8,128)S(1)}, u32[]{:S(2)}, u32[]{:S(2)}) collective-permute-start(f32[16,128]{1,0:T(8,128)S(1)} %constant_dynamic-update-slice_fusion.8), channel_id=1, source_target_pairs={{0,16},{1,17},{2,18},{3,19},{4,20},{5,21},{6,22},{7,23},{8,24},{9,... | collective-permute-start | bytes 24584 | tf_op jit(solution)/shard_map/ppermute | solution.py:554
  41.1 2.5 %shard_map.151 = (bf16[256,768]{1,0:T(8,128)(2,1)}, bf16[384,256]{1,0:T(8,128)(2,1)S(1)}, bf16[384,256]{1,0:T(8,128)(2,1)S(1)}) custom-call(s32[2,12]{1,0:T(2,128)S(1)} %copy-done.5, f32[256,128]{1,0:T(8,128)S(1)} %get-tuple-element.75.near_stats, f32[256,128]{1,0:T(8,128)S(1)} %get-tuple-element.82.stats, f32[64,128]{1,0:T(8,128)S(1)} %get-tuple-element.86.picked, ...), custom_call_target="tpu_custom_call" | custom-call | flops 905969664 | bytes 3673184 | tf_op jit(solution)/shard_map/pallas_call | solution.py:535
  44.2 0.9 collective-permute-done.14.left_other
  45.6 2.2 %collective-permute-done.13 = f32[32,256]{1,0:T(8,128)S(1)} collective-permute-done((f32[32,256]{1,0:T(8,128)S(1)}, f32[32,256]{1,0:T(8,128)S(1)}, u32[]{:S(2)}, u32[]{:S(2)}) %collective-permute-start.13) | collective-permute-done | bytes 32800 | tf_op jit(solution)/shard_map/ppermute | solution.py:554
  47.8 1.6 %collective-permute-start.21 = (f32[64,256]{1,0:T(8,128)S(1)}, f32[64,256]{1,0:T(8,128)S(1)}, u32[]{:S(2)}, u32[]{:S(2)}) collective-permute-start(f32[64,256]{1,0:T(8,128)S(1)} %constant_dynamic-update-slice_fusion.12), channel_id=1, source_target_pairs={{0,2},{1,3},{2,0},{3,1},{4,6},{5,7},{6,4},{7,5},{8,10},{9,11},{10,... | collective-permute-start | bytes 196616 | tf_op jit(solution)/shard_map/ppermute | solution.py:554
  49.4 0.5 collective-permute-start.33
  49.9 4.1 %shard_map.153 = (bf16[256,768]{1,0:T(8,128)(2,1)S(1)}, f32[256,768]{1,0:T(8,128)S(1)}, f32[256,768]{1,0:T(8,128)S(1)}) custom-call(s32[2,12]{1,0:T(2,128)S(1)} %copy-done.5, s32[1]{0:T(128)S(6)} %copy.42.pad_ref, bf16[256,768]{1,0:T(8,128)(2,1)S(1)} %copy-done.6, bf16[256,768]{1,0:T(8,128)(2,1)S(1)} %copy-done.7, bf16[256,768]{1,0:T(8,128)(2,1)S(1)} %copy-done.8, ...), custom_call_target="tpu_custom_call" | custom-call | flops 805306368 | bytes 3866724 | tf_op jit(solution)/shard_map/pallas_call | solution.py:535
  55.4 2.6 %collective-permute-done.33 = bf16[192,768]{1,0:T(8,128)(2,1)S(1)} collective-permute-done((bf16[192,768]{1,0:T(8,128)(2,1)S(1)}, bf16[192,768]{1,0:T(8,128)(2,1)S(1)}, u32[]{:S(2)}, u32[]{:S(2)}) %collective-permute-start.33) | collective-permute-done | bytes 294944 | tf_op jit(solution)/shard_map/ppermute | solution.py:554
  58.4 2.4 %shard_map.155 = (bf16[256,768]{1,0:T(8,128)(2,1)S(1)}, bf16[256,768]{1,0:T(8,128)(2,1)S(1)}) custom-call(s32[2,12]{1,0:T(2,128)S(1)} %copy-done.5, s32[1]{0:T(128)S(6)} %copy.42.pad_ref, bf16[64,3072]{1,0:T(8,128)(2,1)S(1)} %copy-done.1, bf16[256,1536]{1,0:T(8,128)(2,1)S(1)} %constant_dynamic-update-slice_fusion.19.qg_0, ...), custom_call_target="tpu_custom_call" | custom-call | flops 15099494 | bytes 229381 | tf_op jit(solution)/shard_map/pallas_call | solution.py:535
  61.8 0.8 collective-permute-done.24.dk_other
  62.6 0.6 collective-permute-done.25.dv_other
  63.1 0.8 shard_map.156
  64.0 1.0 %collective-permute-start.27 = (bf16[96,1536]{1,0:T(8,128)(2,1)S(1)}, bf16[96,1536]{1,0:T(8,128)(2,1)S(1)}, u32[]{:S(2)}, u32[]{:S(2)}) collective-permute-start(bf16[96,1536]{1,0:T(8,128)(2,1)S(1)} %get-tuple-element.135), channel_id=1, source_target_pairs={{0,2},{1,3},{2,0},{3,1},{4,6},{5,7},{6,4},{7,5},{8,10},{9,11},{10,... | collective-permute-start | bytes 884744 | tf_op jit(solution)/shard_map/ppermute | solution.py:554
  65.4 1.2 %collective-permute-start.31 = (bf16[96,1536]{1,0:T(8,128)(2,1)S(1)}, bf16[96,1536]{1,0:T(8,128)(2,1)S(1)}, u32[]{:S(2)}, u32[]{:S(2)}) collective-permute-start(bf16[96,1536]{1,0:T(8,128)(2,1)S(1)} %get-tuple-element.133), channel_id=1, source_target_pairs={{0,4},{1,5},{2,6},{3,7},{4,0},{5,1},{6,2},{7,3},{8,12},{9,13},{10,... | collective-permute-start | bytes 884744 | tf_op jit(solution)/shard_map/ppermute | solution.py:554
  66.7 1.2 %collective-permute-start.32 = (bf16[96,1536]{1,0:T(8,128)(2,1)S(1)}, bf16[96,1536]{1,0:T(8,128)(2,1)S(1)}, u32[]{:S(2)}, u32[]{:S(2)}) collective-permute-start(bf16[96,1536]{1,0:T(8,128)(2,1)S(1)} %get-tuple-element.132), channel_id=1, source_target_pairs={{0,6},{1,7},{2,4},{3,5},{4,2},{5,3},{6,0},{7,1},{8,14},{9,15},{10,... | collective-permute-start | bytes 884744 | tf_op jit(solution)/shard_map/ppermute | solution.py:554
  67.9 1.9 %shard_map.157 = bf16[256,768]{1,0:T(8,128)(2,1)} custom-call(bf16[256,768]{1,0:T(8,128)(2,1)S(1)} %get-tuple-element.121.right.dq, bf16[256,768]{1,0:T(8,128)(2,1)S(1)} %get-tuple-element.119.dk, bf16[256,768]{1,0:T(8,128)(2,1)S(1)} %get-tuple-element.120.dv, bf16[768,2304]{1,0:T(8,128)(2,1)S(1)} %copy-done), custom_call_target="tpu_custom_call" | custom-call | flops 45298484 | bytes 255590 | tf_op jit(solution)/shard_map/pallas_call | solution.py:535
  69.8 4.2 %collective-permute-done.27 = bf16[96,1536]{1,0:T(8,128)(2,1)S(1)} collective-permute-done((bf16[96,1536]{1,0:T(8,128)(2,1)S(1)}, bf16[96,1536]{1,0:T(8,128)(2,1)S(1)}, u32[]{:S(2)}, u32[]{:S(2)}) %collective-permute-start.27) | collective-permute-done | bytes 294944 | tf_op jit(solution)/shard_map/ppermute | solution.py:554
  74.4 2.1 %collective-permute-start.28 = (bf16[96,768]{1,0:T(8,128)(2,1)S(1)}, bf16[96,768]{1,0:T(8,128)(2,1)S(1)}, u32[]{:S(2)}, u32[]{:S(2)}) collective-permute-start(bf16[96,768]{1,0:T(8,128)(2,1)S(1)} %slice.175), channel_id=1, source_target_pairs={{0,16},{1,17},{2,18},{3,19},{4,20},{5,21},{6,22},{7,23},{8,24},{9,... | collective-permute-start | bytes 442376 | tf_op jit(solution)/shard_map/ppermute | solution.py:554
  76.5 2.0 %collective-permute-done.35 = bf16[48,768]{1,0:T(8,128)(2,1)S(1)} collective-permute-done((bf16[48,768]{1,0:T(8,128)(2,1)S(1)}, bf16[48,768]{1,0:T(8,128)(2,1)S(1)}, u32[]{:S(2)}, u32[]{:S(2)}) %collective-permute-start.35) | collective-permute-done | bytes 73760 | tf_op jit(solution)/shard_map/ppermute | solution.py:554
  78.5 2.6 %collective-permute-start.39 = (bf16[24,768]{1,0:T(8,128)(2,1)S(1)}, bf16[24,768]{1,0:T(8,128)(2,1)S(1)}, u32[]{:S(2)}, u32[]{:S(2)}) collective-permute-start(bf16[24,768]{1,0:T(8,128)(2,1)S(1)} %slice.194), channel_id=1, source_target_pairs={{0,16},{1,17},{2,18},{3,19},{4,20},{5,21},{6,22},{7,23},{8,24},{9,... | collective-permute-start | bytes 110600 | tf_op jit(solution)/shard_map/ppermute | solution.py:554
  81.3 0.9 collective-permute-start.36
  82.2 2.3 %collective-permute-start.37 = (bf16[24,1536]{1,0:T(8,128)(2,1)S(1)}, bf16[24,1536]{1,0:T(8,128)(2,1)S(1)}, u32[]{:S(2)}, u32[]{:S(2)}) collective-permute-start(bf16[24,1536]{1,0:T(8,128)(2,1)S(1)} %get-tuple-element.145), channel_id=1, source_target_pairs={{0,16},{1,17},{2,18},{3,19},{4,20},{5,21},{6,22},{7,23},{8,24},{9,... | collective-permute-start | bytes 221192 | tf_op jit(solution)/shard_map/ppermute | solution.py:554
  84.5 1.2 %collective-permute-start.38 = (bf16[24,1536]{1,0:T(8,128)(2,1)S(1)}, bf16[24,1536]{1,0:T(8,128)(2,1)S(1)}, u32[]{:S(2)}, u32[]{:S(2)}) collective-permute-start(bf16[24,1536]{1,0:T(8,128)(2,1)S(1)} %get-tuple-element.144), channel_id=1, source_target_pairs={{0,24},{1,25},{2,26},{3,27},{4,28},{5,29},{6,30},{7,31},{8,16},{9,... | collective-permute-start | bytes 221192 | tf_op jit(solution)/shard_map/ppermute | solution.py:554
  85.8 1.1 %collective-permute-start.29 = (bf16[48,768]{1,0:T(8,128)(2,1)S(1)}, bf16[48,768]{1,0:T(8,128)(2,1)S(1)}, u32[]{:S(2)}, u32[]{:S(2)}) collective-permute-start(bf16[48,768]{1,0:T(8,128)(2,1)S(1)} %slice.177), channel_id=1, source_target_pairs={{0,2},{1,3},{2,0},{3,1},{4,6},{5,7},{6,4},{7,5},{8,10},{9,11},{10,... | collective-permute-start | bytes 221192 | tf_op jit(solution)/shard_map/ppermute | solution.py:554
  86.9 0.6 convert_add_fusion.1
  87.6 2.7 %collective-permute-done.29 = bf16[48,768]{1,0:T(8,128)(2,1)S(1)} collective-permute-done((bf16[48,768]{1,0:T(8,128)(2,1)S(1)}, bf16[48,768]{1,0:T(8,128)(2,1)S(1)}, u32[]{:S(2)}, u32[]{:S(2)}) %collective-permute-start.29) | collective-permute-done | bytes 73760 | tf_op jit(solution)/shard_map/ppermute | solution.py:554
  90.3 1.2 %collective-permute-start.30 = (bf16[24,768]{1,0:T(8,128)(2,1)S(1)}, bf16[24,768]{1,0:T(8,128)(2,1)S(1)}, u32[]{:S(2)}, u32[]{:S(2)}) collective-permute-start(bf16[24,768]{1,0:T(8,128)(2,1)S(1)} %slice.179), channel_id=1, source_target_pairs={{0,4},{1,5},{2,6},{3,7},{4,0},{5,1},{6,2},{7,3},{8,12},{9,13},{10,... | collective-permute-start | bytes 110600 | tf_op jit(solution)/shard_map/ppermute | solution.py:554
  91.5 2.8 %collective-permute-done.30 = bf16[24,768]{1,0:T(8,128)(2,1)S(1)} collective-permute-done((bf16[24,768]{1,0:T(8,128)(2,1)S(1)}, bf16[24,768]{1,0:T(8,128)(2,1)S(1)}, u32[]{:S(2)}, u32[]{:S(2)}) %collective-permute-start.30) | collective-permute-done | bytes 36896 | tf_op jit(solution)/shard_map/ppermute | solution.py:554
  94.3 0.7 pad_maximum_fusion
  (138 shorter events, 6.1 us)
Async XLA Ops:
  0.6 14.5 %copy-start.10 = (s32[768,1]{1,0:T(8,128)S(1)}, s32[768,1]{1,0:T(8,128)}, u32[]{:S(2)}) copy-start(s32[768,1]{1,0:T(8,128)} %constant.14.clone) | copy-start | bytes 9220
  0.6 14.5 %copy-start.11 = (s32[768,1]{1,0:T(8,128)S(1)}, s32[768,1]{1,0:T(8,128)}, u32[]{:S(2)}) copy-start(s32[768,1]{1,0:T(8,128)} %constant.15.clone) | copy-start | bytes 9220
  0.7 14.5 %copy-start.12 = (s32[768,1]{1,0:T(8,128)S(1)}, s32[768,1]{1,0:T(8,128)}, u32[]{:S(2)}) copy-start(s32[768,1]{1,0:T(8,128)} %constant.16.clone) | copy-start | bytes 9220
  0.7 14.5 %copy-start.13 = (s32[768,1]{1,0:T(8,128)S(1)}, s32[768,1]{1,0:T(8,128)}, u32[]{:S(2)}) copy-start(s32[768,1]{1,0:T(8,128)} %constant.17.clone) | copy-start | bytes 9220
  6.3 10.6 %collective-permute-start = (bf16[8,3072]{1,0:T(8,128)(2,1)}, bf16[8,3072]{1,0:T(8,128)(2,1)S(1)}, u32[]{:S(2)}, u32[]{:S(2)}) collective-permute-start(bf16[8,3072]{1,0:T(8,128)(2,1)} %get-tuple-element.106), channel_id=1, source_target_pairs={{0,8},{1,9},{2,10},{3,11},{4,12},{5,13},{6,14},{7,15},{8,0},{9,1},... | collective-permute-start | bytes 147464 | tf_op jit(solution)/shard_map/ppermute | solution.py:554
  9.3 7.9 %collective-permute-start.1 = (bf16[8,3072]{1,0:T(8,128)(2,1)}, bf16[8,3072]{1,0:T(8,128)(2,1)S(1)}, u32[]{:S(2)}, u32[]{:S(2)}) collective-permute-start(bf16[8,3072]{1,0:T(8,128)(2,1)} %get-tuple-element.106), channel_id=1, source_target_pairs={{0,16},{1,17},{2,18},{3,19},{4,20},{5,21},{6,22},{7,23},{8,24},{9,... | collective-permute-start | bytes 147464 | tf_op jit(solution)/shard_map/ppermute | solution.py:554
  11.9 6.1 %collective-permute-start.2 = (bf16[8,3072]{1,0:T(8,128)(2,1)}, bf16[8,3072]{1,0:T(8,128)(2,1)S(1)}, u32[]{:S(2)}, u32[]{:S(2)}) collective-permute-start(bf16[8,3072]{1,0:T(8,128)(2,1)} %get-tuple-element.106), channel_id=1, source_target_pairs={{0,24},{1,25},{2,26},{3,27},{4,28},{5,29},{6,30},{7,31},{8,16},{9,... | collective-permute-start | bytes 147464 | tf_op jit(solution)/shard_map/ppermute | solution.py:554
  11.9 6.1 %collective-permute-start.3 = (bf16[32,1536]{1,0:T(8,128)(2,1)}, bf16[32,1536]{1,0:T(8,128)(2,1)S(1)}, u32[]{:S(2)}, u32[]{:S(2)}) collective-permute-start(bf16[32,1536]{1,0:T(8,128)(2,1)} %get-tuple-element.70), channel_id=1, source_target_pairs={{0,2},{1,3},{2,0},{3,1},{4,6},{5,7},{6,4},{7,5},{8,10},{9,11},{10,... | collective-permute-start | bytes 294920 | tf_op jit(solution)/shard_map/ppermute | solution.py:554
  13.7 5.1 %collective-permute-start.4 = (bf16[32,1536]{1,0:T(8,128)(2,1)}, bf16[32,1536]{1,0:T(8,128)(2,1)S(1)}, u32[]{:S(2)}, u32[]{:S(2)}) collective-permute-start(bf16[32,1536]{1,0:T(8,128)(2,1)} %get-tuple-element.70), channel_id=1, source_target_pairs={{0,4},{1,5},{2,6},{3,7},{4,0},{5,1},{6,2},{7,3},{8,12},{9,13},{10,... | collective-permute-start | bytes 294920 | tf_op jit(solution)/shard_map/ppermute | solution.py:554
  15.2 7.5 %copy-start.8 = (bf16[256,768]{1,0:T(8,128)(2,1)S(1)}, bf16[256,768]{1,0:T(8,128)(2,1)}, u32[]{:S(2)}) copy-start(bf16[256,768]{1,0:T(8,128)(2,1)} %get-tuple-element.73.v) | copy-start | bytes 1179652
  15.2 7.5 %copy-start.9 = (bf16[256,768]{1,0:T(8,128)(2,1)S(1)}, bf16[256,768]{1,0:T(8,128)(2,1)}, u32[]{:S(2)}) copy-start(bf16[256,768]{1,0:T(8,128)(2,1)} %get-tuple-element.74.g) | copy-start | bytes 1179652
  16.1 6.7 %copy-start.7 = (bf16[256,768]{1,0:T(8,128)(2,1)S(1)}, bf16[256,768]{1,0:T(8,128)(2,1)}, u32[]{:S(2)}) copy-start(bf16[256,768]{1,0:T(8,128)(2,1)} %get-tuple-element.72.k) | copy-start | bytes 1179652
  16.9 5.7 %collective-permute-start.5 = (bf16[32,1536]{1,0:T(8,128)(2,1)S(1)}, bf16[32,1536]{1,0:T(8,128)(2,1)S(1)}, u32[]{:S(2)}, u32[]{:S(2)}) collective-permute-start(bf16[32,1536]{1,0:T(8,128)(2,1)S(1)} %copy-done.15), channel_id=1, source_target_pairs={{0,6},{1,7},{2,4},{3,5},{4,2},{5,3},{6,0},{7,1},{8,14},{9,15},{10,... | collective-permute-start | bytes 294920 | tf_op jit(solution)/shard_map/ppermute | solution.py:554
  18.7 6.6 %collective-permute-start.7 = (bf16[32,1536]{1,0:T(8,128)(2,1)S(1)}, bf16[32,1536]{1,0:T(8,128)(2,1)S(1)}, u32[]{:S(2)}, u32[]{:S(2)}) collective-permute-start(bf16[32,1536]{1,0:T(8,128)(2,1)S(1)} %pad_maximum_fusion.1), channel_id=1, source_target_pairs={{0,2},{1,3},{2,0},{3,1},{4,6},{5,7},{6,4},{7,5},{8,10},{9,11},{10,... | collective-permute-start | bytes 294920 | tf_op jit(solution)/shard_map/ppermute | solution.py:554
  19.6 5.7 %collective-permute-start.8 = (bf16[32,1536]{1,0:T(8,128)(2,1)S(1)}, bf16[32,1536]{1,0:T(8,128)(2,1)S(1)}, u32[]{:S(2)}, u32[]{:S(2)}) collective-permute-start(bf16[32,1536]{1,0:T(8,128)(2,1)S(1)} %pad_maximum_fusion.1), channel_id=1, source_target_pairs={{0,4},{1,5},{2,6},{3,7},{4,0},{5,1},{6,2},{7,3},{8,12},{9,13},{10,... | collective-permute-start | bytes 294920 | tf_op jit(solution)/shard_map/ppermute | solution.py:554
  21.6 5.5 %collective-permute-start.9 = (bf16[32,1536]{1,0:T(8,128)(2,1)S(1)}, bf16[32,1536]{1,0:T(8,128)(2,1)S(1)}, u32[]{:S(2)}, u32[]{:S(2)}) collective-permute-start(bf16[32,1536]{1,0:T(8,128)(2,1)S(1)} %pad_maximum_fusion.1), channel_id=1, source_target_pairs={{0,6},{1,7},{2,4},{3,5},{4,2},{5,3},{6,0},{7,1},{8,14},{9,15},{10,... | collective-permute-start | bytes 294920 | tf_op jit(solution)/shard_map/ppermute | solution.py:554
  22.6 4.6 %collective-permute-start.6 = (bf16[128,1536]{1,0:T(8,128)(2,1)S(1)}, bf16[128,1536]{1,0:T(8,128)(2,1)S(1)}, u32[]{:S(2)}, u32[]{:S(2)}) collective-permute-start(bf16[128,1536]{1,0:T(8,128)(2,1)S(1)} %constant_dynamic-update-slice_fusion.mid_0), channel_id=1, source_target_pairs={{0,1},{1,0},{2,3},{3,2},{4,5},{5,4},{6,7},{7,6},{8,9},{9,8},{10,11... | collective-permute-start | bytes 1179656 | tf_op jit(solution)/shard_map/ppermute | solution.py:554
  27.2 1.8 %collective-permute-start.10 = (bf16[128,1536]{1,0:T(8,128)(2,1)S(1)}, bf16[128,1536]{1,0:T(8,128)(2,1)S(1)}, u32[]{:S(2)}, u32[]{:S(2)}) collective-permute-start(bf16[128,1536]{1,0:T(8,128)(2,1)S(1)} %constant_dynamic-update-slice_fusion.4.far_0), channel_id=1, source_target_pairs={{0,1},{1,0},{2,3},{3,2},{4,5},{5,4},{6,7},{7,6},{8,9},{9,8},{10,11... | collective-permute-start | bytes 1179656 | tf_op jit(solution)/shard_map/ppermute | solution.py:554
  31.3 9.9 %copy-start.2 = (bf16[768,768]{1,0:T(8,128)(2,1)S(1)}, bf16[768,768]{1,0:T(8,128)(2,1)}, u32[]{:S(2)}) copy-start(bf16[768,768]{1,0:T(8,128)(2,1)} %w_out.1) | copy-start | bytes 3538948
  31.3 6.2 %collective-permute-start.11 = (f32[8,128]{1,0:T(8,128)S(1)}, f32[8,128]{1,0:T(8,128)S(1)}, u32[]{:S(2)}, u32[]{:S(2)}) collective-permute-start(f32[8,128]{1,0:T(8,128)S(1)} %slice.130), channel_id=1, source_target_pairs={{0,8},{1,9},{2,10},{3,11},{4,12},{5,13},{6,14},{7,15},{8,0},{9,1},... | collective-permute-start | bytes 12296 | tf_op jit(solution)/shard_map/ppermute | solution.py:554
  34.0 20.0 %collective-permute-start.17 = (bf16[64,1536]{1,0:T(8,128)(2,1)S(1)}, bf16[64,1536]{1,0:T(8,128)(2,1)S(1)}, u32[]{:S(2)}, u32[]{:S(2)}) collective-permute-start(bf16[64,1536]{1,0:T(8,128)(2,1)S(1)} %constant_dynamic-update-slice_fusion.14), channel_id=1, source_target_pairs={{0,2},{1,3},{2,0},{3,1},{4,6},{5,7},{6,4},{7,5},{8,10},{9,11},{10,... | collective-permute-start | bytes 589832 | tf_op jit(solution)/shard_map/ppermute | solution.py:554
  35.5 18.5 %collective-permute-start.18 = (bf16[64,1536]{1,0:T(8,128)(2,1)S(1)}, bf16[64,1536]{1,0:T(8,128)(2,1)S(1)}, u32[]{:S(2)}, u32[]{:S(2)}) collective-permute-start(bf16[64,1536]{1,0:T(8,128)(2,1)S(1)} %constant_dynamic-update-slice_fusion.14), channel_id=1, source_target_pairs={{0,4},{1,5},{2,6},{3,7},{4,0},{5,1},{6,2},{7,3},{8,12},{9,13},{10,... | collective-permute-start | bytes 589832 | tf_op jit(solution)/shard_map/ppermute | solution.py:554
  35.7 18.9 %collective-permute-start.19 = (bf16[64,1536]{1,0:T(8,128)(2,1)S(1)}, bf16[64,1536]{1,0:T(8,128)(2,1)S(1)}, u32[]{:S(2)}, u32[]{:S(2)}) collective-permute-start(bf16[64,1536]{1,0:T(8,128)(2,1)S(1)} %constant_dynamic-update-slice_fusion.14), channel_id=1, source_target_pairs={{0,6},{1,7},{2,4},{3,5},{4,2},{5,3},{6,0},{7,1},{8,14},{9,15},{10,... | collective-permute-start | bytes 589832 | tf_op jit(solution)/shard_map/ppermute | solution.py:554
  37.5 6.3 %collective-permute-start.15 = (bf16[256,768]{1,0:T(8,128)(2,1)S(1)}, bf16[256,768]{1,0:T(8,128)(2,1)S(1)}, u32[]{:S(2)}, u32[]{:S(2)}) collective-permute-start(bf16[256,768]{1,0:T(8,128)(2,1)S(1)} %copy-done.4), channel_id=1, source_target_pairs={{0,1},{1,0},{2,3},{3,2},{4,5},{5,4},{6,7},{7,6},{8,9},{9,8},{10,11... | collective-permute-start | bytes 1179656 | tf_op jit(solution)/shard_map/ppermute | solution.py:554
  37.5 6.1 %collective-permute-start.12 = (f32[16,128]{1,0:T(8,128)S(1)}, f32[16,128]{1,0:T(8,128)S(1)}, u32[]{:S(2)}, u32[]{:S(2)}) collective-permute-start(f32[16,128]{1,0:T(8,128)S(1)} %constant_dynamic-update-slice_fusion.8), channel_id=1, source_target_pairs={{0,16},{1,17},{2,18},{3,19},{4,20},{5,21},{6,22},{7,23},{8,24},{9,... | collective-permute-start | bytes 24584 | tf_op jit(solution)/shard_map/ppermute | solution.py:554
  43.6 1.4 %collective-permute-start.14 = (bf16[384,256]{1,0:T(8,128)(2,1)S(1)}, bf16[384,256]{1,0:T(8,128)(2,1)S(1)}, u32[]{:S(2)}, u32[]{:S(2)}) collective-permute-start(bf16[384,256]{1,0:T(8,128)(2,1)S(1)} %get-tuple-element.94), channel_id=1, source_target_pairs={{0,1},{1,0},{2,3},{3,2},{4,5},{5,4},{6,7},{7,6},{8,9},{9,8},{10,11... | collective-permute-start | bytes 589832 | tf_op jit(solution)/shard_map/ppermute | solution.py:554
  43.8 4.0 %collective-permute-start.13 = (f32[32,256]{1,0:T(8,128)S(1)}, f32[32,256]{1,0:T(8,128)S(1)}, u32[]{:S(2)}, u32[]{:S(2)}) collective-permute-start(f32[32,256]{1,0:T(8,128)S(1)} %pad_maximum_fusion.2), channel_id=1, source_target_pairs={{0,4},{1,5},{2,6},{3,7},{4,0},{5,1},{6,2},{7,3},{8,12},{9,13},{10,... | collective-permute-start | bytes 98312 | tf_op jit(solution)/shard_map/ppermute | solution.py:554
  47.8 7.0 %collective-permute-start.21 = (f32[64,256]{1,0:T(8,128)S(1)}, f32[64,256]{1,0:T(8,128)S(1)}, u32[]{:S(2)}, u32[]{:S(2)}) collective-permute-start(f32[64,256]{1,0:T(8,128)S(1)} %constant_dynamic-update-slice_fusion.12), channel_id=1, source_target_pairs={{0,2},{1,3},{2,0},{3,1},{4,6},{5,7},{6,4},{7,5},{8,10},{9,11},{10,... | collective-permute-start | bytes 196616 | tf_op jit(solution)/shard_map/ppermute | solution.py:554
  49.4 8.6 %collective-permute-start.33 = (bf16[192,768]{1,0:T(8,128)(2,1)S(1)}, bf16[192,768]{1,0:T(8,128)(2,1)S(1)}, u32[]{:S(2)}, u32[]{:S(2)}) collective-permute-start(bf16[192,768]{1,0:T(8,128)(2,1)S(1)} %get-tuple-element.138), channel_id=1, source_target_pairs={{0,2},{1,3},{2,0},{3,1},{4,6},{5,7},{6,4},{7,5},{8,10},{9,11},{10,... | collective-permute-start | bytes 884744 | tf_op jit(solution)/shard_map/ppermute | solution.py:554
  54.0 4.0 %collective-permute-start.16 = (bf16[768,256]{1,0:T(8,128)(2,1)S(1)}, bf16[768,256]{1,0:T(8,128)(2,1)S(1)}, u32[]{:S(2)}, u32[]{:S(2)}) collective-permute-start(bf16[768,256]{1,0:T(8,128)(2,1)S(1)} %get-tuple-element.103), channel_id=1, source_target_pairs={{0,1},{1,0},{2,3},{3,2},{4,5},{5,4},{6,7},{7,6},{8,9},{9,8},{10,11... | collective-permute-start | bytes 1179656 | tf_op jit(solution)/shard_map/ppermute | solution.py:554
  54.1 3.9 %collective-permute-start.23 = (bf16[256,768]{1,0:T(8,128)(2,1)S(1)}, bf16[256,768]{1,0:T(8,128)(2,1)S(1)}, u32[]{:S(2)}, u32[]{:S(2)}) collective-permute-start(bf16[256,768]{1,0:T(8,128)(2,1)S(1)} %get-tuple-element.121.right.dq), channel_id=1, source_target_pairs={{0,1},{1,0},{2,3},{3,2},{4,5},{5,4},{6,7},{7,6},{8,9},{9,8},{10,11... | collective-permute-start | bytes 1179656 | tf_op jit(solution)/shard_map/ppermute | solution.py:554
  54.6 3.8 %collective-permute-start.20 = (bf16[256,1536]{1,0:T(8,128)(2,1)S(1)}, bf16[256,1536]{1,0:T(8,128)(2,1)S(1)}, u32[]{:S(2)}, u32[]{:S(2)}) collective-permute-start(bf16[256,1536]{1,0:T(8,128)(2,1)S(1)} %constant_dynamic-update-slice_fusion.19.qg_0), channel_id=1, source_target_pairs={{0,1},{1,0},{2,3},{3,2},{4,5},{5,4},{6,7},{7,6},{8,9},{9,8},{10,11... | collective-permute-start | bytes 2359304 | tf_op jit(solution)/shard_map/ppermute | solution.py:554
  54.9 3.5 %collective-permute-start.22 = (f32[256,128]{1,0:T(8,128)S(1)}, f32[256,128]{1,0:T(8,128)S(1)}, u32[]{:S(2)}, u32[]{:S(2)}) collective-permute-start(f32[256,128]{1,0:T(8,128)S(1)} %constant_dynamic-update-slice_fusion.23.stats_0), channel_id=1, source_target_pairs={{0,1},{1,0},{2,3},{3,2},{4,5},{5,4},{6,7},{7,6},{8,9},{9,8},{10,11... | collective-permute-start | bytes 393224 | tf_op jit(solution)/shard_map/ppermute | solution.py:554
  60.8 1.8 %collective-permute-start.24 = (bf16[256,768]{1,0:T(8,128)(2,1)S(1)}, bf16[256,768]{1,0:T(8,128)(2,1)S(1)}, u32[]{:S(2)}, u32[]{:S(2)}) collective-permute-start(bf16[256,768]{1,0:T(8,128)(2,1)S(1)} %get-tuple-element.119.dk), channel_id=1, source_target_pairs={{0,1},{1,0},{2,3},{3,2},{4,5},{5,4},{6,7},{7,6},{8,9},{9,8},{10,11... | collective-permute-start | bytes 1179656 | tf_op jit(solution)/shard_map/ppermute | solution.py:554
  60.9 2.3 %collective-permute-start.25 = (bf16[256,768]{1,0:T(8,128)(2,1)S(1)}, bf16[256,768]{1,0:T(8,128)(2,1)S(1)}, u32[]{:S(2)}, u32[]{:S(2)}) collective-permute-start(bf16[256,768]{1,0:T(8,128)(2,1)S(1)} %get-tuple-element.120.dv), channel_id=1, source_target_pairs={{0,1},{1,0},{2,3},{3,2},{4,5},{5,4},{6,7},{7,6},{8,9},{9,8},{10,11... | collective-permute-start | bytes 1179656 | tf_op jit(solution)/shard_map/ppermute | solution.py:554
  61.5 8.3 %collective-permute-start.34 = (bf16[96,768]{1,0:T(8,128)(2,1)S(1)}, bf16[96,768]{1,0:T(8,128)(2,1)S(1)}, u32[]{:S(2)}, u32[]{:S(2)}) collective-permute-start(bf16[96,768]{1,0:T(8,128)(2,1)S(1)} %get-tuple-element.146), channel_id=1, source_target_pairs={{0,4},{1,5},{2,6},{3,7},{4,0},{5,1},{6,2},{7,3},{8,12},{9,13},{10,... | collective-permute-start | bytes 442376 | tf_op jit(solution)/shard_map/ppermute | solution.py:554
  64.0 9.9 %collective-permute-start.27 = (bf16[96,1536]{1,0:T(8,128)(2,1)S(1)}, bf16[96,1536]{1,0:T(8,128)(2,1)S(1)}, u32[]{:S(2)}, u32[]{:S(2)}) collective-permute-start(bf16[96,1536]{1,0:T(8,128)(2,1)S(1)} %get-tuple-element.135), channel_id=1, source_target_pairs={{0,2},{1,3},{2,0},{3,1},{4,6},{5,7},{6,4},{7,5},{8,10},{9,11},{10,... | collective-permute-start | bytes 884744 | tf_op jit(solution)/shard_map/ppermute | solution.py:554
  65.1 9.2 %collective-permute-start.26 = (bf16[192,768]{1,0:T(8,128)(2,1)S(1)}, bf16[192,768]{1,0:T(8,128)(2,1)S(1)}, u32[]{:S(2)}, u32[]{:S(2)}) collective-permute-start(bf16[192,768]{1,0:T(8,128)(2,1)S(1)} %get-tuple-element.136), channel_id=1, source_target_pairs={{0,8},{1,9},{2,10},{3,11},{4,12},{5,13},{6,14},{7,15},{8,0},{9,1},... | collective-permute-start | bytes 884744 | tf_op jit(solution)/shard_map/ppermute | solution.py:554
  65.4 15.7 %collective-permute-start.31 = (bf16[96,1536]{1,0:T(8,128)(2,1)S(1)}, bf16[96,1536]{1,0:T(8,128)(2,1)S(1)}, u32[]{:S(2)}, u32[]{:S(2)}) collective-permute-start(bf16[96,1536]{1,0:T(8,128)(2,1)S(1)} %get-tuple-element.133), channel_id=1, source_target_pairs={{0,4},{1,5},{2,6},{3,7},{4,0},{5,1},{6,2},{7,3},{8,12},{9,13},{10,... | collective-permute-start | bytes 884744 | tf_op jit(solution)/shard_map/ppermute | solution.py:554
  66.7 14.5 %collective-permute-start.32 = (bf16[96,1536]{1,0:T(8,128)(2,1)S(1)}, bf16[96,1536]{1,0:T(8,128)(2,1)S(1)}, u32[]{:S(2)}, u32[]{:S(2)}) collective-permute-start(bf16[96,1536]{1,0:T(8,128)(2,1)S(1)} %get-tuple-element.132), channel_id=1, source_target_pairs={{0,6},{1,7},{2,4},{3,5},{4,2},{5,3},{6,0},{7,1},{8,14},{9,15},{10,... | collective-permute-start | bytes 884744 | tf_op jit(solution)/shard_map/ppermute | solution.py:554
  74.0 4.5 %collective-permute-start.35 = (bf16[48,768]{1,0:T(8,128)(2,1)S(1)}, bf16[48,768]{1,0:T(8,128)(2,1)S(1)}, u32[]{:S(2)}, u32[]{:S(2)}) collective-permute-start(bf16[48,768]{1,0:T(8,128)(2,1)S(1)} %slice.188), channel_id=1, source_target_pairs={{0,8},{1,9},{2,10},{3,11},{4,12},{5,13},{6,14},{7,15},{8,0},{9,1},... | collective-permute-start | bytes 221192 | tf_op jit(solution)/shard_map/ppermute | solution.py:554
  74.4 11.4 %collective-permute-start.28 = (bf16[96,768]{1,0:T(8,128)(2,1)S(1)}, bf16[96,768]{1,0:T(8,128)(2,1)S(1)}, u32[]{:S(2)}, u32[]{:S(2)}) collective-permute-start(bf16[96,768]{1,0:T(8,128)(2,1)S(1)} %slice.175), channel_id=1, source_target_pairs={{0,16},{1,17},{2,18},{3,19},{4,20},{5,21},{6,22},{7,23},{8,24},{9,... | collective-permute-start | bytes 442376 | tf_op jit(solution)/shard_map/ppermute | solution.py:554
  78.5 8.4 %collective-permute-start.39 = (bf16[24,768]{1,0:T(8,128)(2,1)S(1)}, bf16[24,768]{1,0:T(8,128)(2,1)S(1)}, u32[]{:S(2)}, u32[]{:S(2)}) collective-permute-start(bf16[24,768]{1,0:T(8,128)(2,1)S(1)} %slice.194), channel_id=1, source_target_pairs={{0,16},{1,17},{2,18},{3,19},{4,20},{5,21},{6,22},{7,23},{8,24},{9,... | collective-permute-start | bytes 110600 | tf_op jit(solution)/shard_map/ppermute | solution.py:554
  81.3 10.2 %collective-permute-start.36 = (bf16[24,1536]{1,0:T(8,128)(2,1)S(1)}, bf16[24,1536]{1,0:T(8,128)(2,1)S(1)}, u32[]{:S(2)}, u32[]{:S(2)}) collective-permute-start(bf16[24,1536]{1,0:T(8,128)(2,1)S(1)} %get-tuple-element.143), channel_id=1, source_target_pairs={{0,8},{1,9},{2,10},{3,11},{4,12},{5,13},{6,14},{7,15},{8,0},{9,1},... | collective-permute-start | bytes 221192 | tf_op jit(solution)/shard_map/ppermute | solution.py:554
  82.2 9.2 %collective-permute-start.37 = (bf16[24,1536]{1,0:T(8,128)(2,1)S(1)}, bf16[24,1536]{1,0:T(8,128)(2,1)S(1)}, u32[]{:S(2)}, u32[]{:S(2)}) collective-permute-start(bf16[24,1536]{1,0:T(8,128)(2,1)S(1)} %get-tuple-element.145), channel_id=1, source_target_pairs={{0,16},{1,17},{2,18},{3,19},{4,20},{5,21},{6,22},{7,23},{8,24},{9,... | collective-permute-start | bytes 221192 | tf_op jit(solution)/shard_map/ppermute | solution.py:554
  84.5 6.9 %collective-permute-start.38 = (bf16[24,1536]{1,0:T(8,128)(2,1)S(1)}, bf16[24,1536]{1,0:T(8,128)(2,1)S(1)}, u32[]{:S(2)}, u32[]{:S(2)}) collective-permute-start(bf16[24,1536]{1,0:T(8,128)(2,1)S(1)} %get-tuple-element.144), channel_id=1, source_target_pairs={{0,24},{1,25},{2,26},{3,27},{4,28},{5,29},{6,30},{7,31},{8,16},{9,... | collective-permute-start | bytes 221192 | tf_op jit(solution)/shard_map/ppermute | solution.py:554
  85.8 4.4 %collective-permute-start.29 = (bf16[48,768]{1,0:T(8,128)(2,1)S(1)}, bf16[48,768]{1,0:T(8,128)(2,1)S(1)}, u32[]{:S(2)}, u32[]{:S(2)}) collective-permute-start(bf16[48,768]{1,0:T(8,128)(2,1)S(1)} %slice.177), channel_id=1, source_target_pairs={{0,2},{1,3},{2,0},{3,1},{4,6},{5,7},{6,4},{7,5},{8,10},{9,11},{10,... | collective-permute-start | bytes 221192 | tf_op jit(solution)/shard_map/ppermute | solution.py:554
  90.3 4.0 %collective-permute-start.30 = (bf16[24,768]{1,0:T(8,128)(2,1)S(1)}, bf16[24,768]{1,0:T(8,128)(2,1)S(1)}, u32[]{:S(2)}, u32[]{:S(2)}) collective-permute-start(bf16[24,768]{1,0:T(8,128)(2,1)S(1)} %slice.179), channel_id=1, source_target_pairs={{0,4},{1,5},{2,6},{3,7},{4,0},{5,1},{6,2},{7,3},{8,12},{9,13},{10,... | collective-permute-start | bytes 110600 | tf_op jit(solution)/shard_map/ppermute | solution.py:554
  (9 other events, 40.4 us)

commit v11 on v10

--- a/solution.py
+++ b/solution.py
@@ -21,7 +21,7 @@
 TN = (((0,), (0,)), ((), ()))
 LARGE = 1e30
 LOW_COST = 0.05
-LOAD_CUTS = 4
+LOAD_CUTS = 8
 VMEM_BYTES = 40 * 1024 * 1024
 PROJECT_VMEM_BYTES = 57 * 1024 * 1024
 
@@ -572,7 +572,9 @@
 
 def step_parts(value, step, dev_count, first=()):
     base, count = step
-    return tied([value] + [swap(value, base * i, dev_count) for i in range(1, count)], first)
+    order = sorted(range(1, count), key=lambda i: i != 2)
+    moved = {i: swap(value, base * i, dev_count) for i in order}
+    return tied([value] + [moved[i] for i in range(1, count)], first)
 
 
 def block_parts(value, step, dev_count):

time: 95.2 us -> 95.3 us (level)
  no operation moved by 1% of the time
where the time goes in v11:
time: 95.3 us; the launch traced here: 95.2 us
  starting transfers between devices  41.3 us (43%)
  Pallas kernels  25 us (26%)
  waiting for transfers between devices  23.6 us (25%)
  between operations  2.08 us (2%)
  other arithmetic  1.94 us (2%)
  local copies, waits for them, and re-layouts  1.27 us (1%)
    ppermute x40, starting transfers between devices, swap(): return lax.ppermute(value, 'ctx', [(d, d ^ mask) for d in range(dev_count)])  41.3 us
    pallas_call x11, Pallas kernels, run(): pl.pallas_call(kernel, out_shape=tuple((jax.ShapeDtypeStruct(s, t) for s,...  25 us
    ppermute x40, waiting for transfers between devices, swap(): return lax.ppermute(value, 'ctx', [(d, d ^ mask) for d in range(dev_count)])  23.6 us
  transfers between devices with their start and end apart: 40, of which 14 were waited for; matrix products, arithmetic and copies ran while one was open for 2% of the time, Pallas kernels for 15%

profile of v11, /device:TPU:0, one launch (start us, length us, event | category | flops | bytes accessed | tf_op | source)
XLA Modules:
  0.0 95.2 jit_solution(2256593593768031197)
XLA Ops:
  0.7 5.8 %shard_map.147 = (bf16[256,768]{1,0:T(8,128)(2,1)}, bf16[256,768]{1,0:T(8,128)(2,1)}, bf16[256,768]{1,0:T(8,128)(2,1)}, bf16[256,768]{1,0:T(8,128)(2,1)}, bf16[6...) custom-call(s32[2,12]{1,0:T(2,128)} %offs_ref.9, ...), custom_call_target="tpu_custom_call" | custom-call | flops 1207959552 | bytes 7716960 | tf_op jit(solution)/shard_map/pallas_call | solution.py:535
  6.4 3.1 %collective-permute-start = (bf16[8,3072]{1,0:T(8,128)(2,1)}, bf16[8,3072]{1,0:T(8,128)(2,1)S(1)}, u32[]{:S(2)}, u32[]{:S(2)}) collective-permute-start(bf16[8,3072]{1,0:T(8,128)(2,1)} %get-tuple-element.106), channel_id=1, source_target_pairs={{0,8},{1,9},{2,10},{3,11},{4,12},{5,13},{6,14},{7,15},{8,0},{9,1},... | collective-permute-start | bytes 147464 | tf_op jit(solution)/shard_map/ppermute | solution.py:554
  9.5 2.6 %collective-permute-start.1 = (bf16[8,3072]{1,0:T(8,128)(2,1)}, bf16[8,3072]{1,0:T(8,128)(2,1)S(1)}, u32[]{:S(2)}, u32[]{:S(2)}) collective-permute-start(bf16[8,3072]{1,0:T(8,128)(2,1)} %get-tuple-element.106), channel_id=1, source_target_pairs={{0,16},{1,17},{2,18},{3,19},{4,20},{5,21},{6,22},{7,23},{8,24},{9,... | collective-permute-start | bytes 147464 | tf_op jit(solution)/shard_map/ppermute | solution.py:554
  12.1 1.7 %collective-permute-start.3 = (bf16[32,1536]{1,0:T(8,128)(2,1)}, bf16[32,1536]{1,0:T(8,128)(2,1)S(1)}, u32[]{:S(2)}, u32[]{:S(2)}) collective-permute-start(bf16[32,1536]{1,0:T(8,128)(2,1)} %get-tuple-element.70), channel_id=1, source_target_pairs={{0,2},{1,3},{2,0},{3,1},{4,6},{5,7},{6,4},{7,5},{8,10},{9,11},{10,... | collective-permute-start | bytes 294920 | tf_op jit(solution)/shard_map/ppermute | solution.py:554
  13.8 1.5 %collective-permute-start.4 = (bf16[32,1536]{1,0:T(8,128)(2,1)}, bf16[32,1536]{1,0:T(8,128)(2,1)S(1)}, u32[]{:S(2)}, u32[]{:S(2)}) collective-permute-start(bf16[32,1536]{1,0:T(8,128)(2,1)} %get-tuple-element.70), channel_id=1, source_target_pairs={{0,4},{1,5},{2,6},{3,7},{4,0},{5,1},{6,2},{7,3},{8,12},{9,13},{10,... | collective-permute-start | bytes 294920 | tf_op jit(solution)/shard_map/ppermute | solution.py:554
  15.5 0.7 copy-done.15
  17.4 0.8 collective-permute-done.2
  18.2 0.7 collective-permute-done.4
  18.9 0.9 collective-permute-start.7
  19.8 2.0 %collective-permute-start.8 = (bf16[32,1536]{1,0:T(8,128)(2,1)S(1)}, bf16[32,1536]{1,0:T(8,128)(2,1)S(1)}, u32[]{:S(2)}, u32[]{:S(2)}) collective-permute-start(bf16[32,1536]{1,0:T(8,128)(2,1)S(1)} %pad_maximum_fusion.1), channel_id=1, source_target_pairs={{0,4},{1,5},{2,6},{3,7},{4,0},{5,1},{6,2},{7,3},{8,12},{9,13},{10,... | collective-permute-start | bytes 294920 | tf_op jit(solution)/shard_map/ppermute | solution.py:554
  21.8 0.9 collective-permute-start.9
  23.0 2.6 %shard_map.148 = (f32[256,768]{1,0:T(8,128)S(1)}, f32[256,128]{1,0:T(8,128)S(1)}, bf16[768,256]{1,0:T(8,128)(2,1)S(1)}, bf16[768,256]{1,0:T(8,128)(2,1)S(1)}) custom-call(s32[1]{0:T(128)S(6)} %copy.42.pad_ref, bf16[256,768]{1,0:T(8,128)(2,1)S(1)} %copy-done.6, bf16[256,768]{1,0:T(8,128)(2,1)S(1)} %copy-done.7, bf16[256,768]{1,0:T(8,128)(2,1)S(1)} %copy-done.8, ...), custom_call_target="tpu_custom_call" | custom-call | flops 805306368 | bytes 3676164 | tf_op jit(solution)/shard_map/pallas_call | solution.py:535
  25.6 1.7 %collective-permute-done.9 = bf16[32,1536]{1,0:T(8,128)(2,1)S(1)} collective-permute-done((bf16[32,1536]{1,0:T(8,128)(2,1)S(1)}, bf16[32,1536]{1,0:T(8,128)(2,1)S(1)}, u32[]{:S(2)}, u32[]{:S(2)}) %collective-permute-start.9) | collective-permute-done | bytes 98336 | tf_op jit(solution)/shard_map/ppermute | solution.py:554
  27.4 1.7 %collective-permute-done.10.far_1 = bf16[128,1536]{1,0:T(8,128)(2,1)S(1)} collective-permute-done((bf16[128,1536]{1,0:T(8,128)(2,1)S(1)}, bf16[128,1536]{1,0:T(8,128)(2,1)S(1)}, u32[]{:S(2)}, u32[]{:S(2)}) %collective-permute-start.10) | collective-permute-done | bytes 393248 | tf_op jit(solution)/shard_map/ppermute | solution.py:554
  29.1 2.3 %shard_map.149 = (f32[256,128]{1,0:T(8,128)S(1)}, f32[64,128]{1,0:T(8,128)S(1)}, f32[64,128]{1,0:T(8,128)S(1)}, f32[64,768]{1,0:T(8,128)S(1)}) custom-call(s32[2,12]{1,0:T(2,128)S(1)} %copy-done.5, s32[1]{0:T(128)S(6)} %copy.42.pad_ref, bf16[64,3072]{1,0:T(8,128)(2,1)S(1)} %copy-done.1, bf16[128,1536]{1,0:T(8,128)(2,1)S(1)} %constant_dynamic-update-slice_fusion.mid_0, ...), custom_call_target="tpu_custom_call" | custom-call | flops 301989888 | bytes 2490468 | tf_op jit(solution)/shard_map/pallas_call | solution.py:535
  31.5 0.7 collective-permute-start.11
  32.2 1.9 %shard_map.150.dq_sel = f32[64,768]{1,0:T(8,128)S(1)} custom-call(s32[2,12]{1,0:T(2,128)S(1)} %copy-done.5, s32[1]{0:T(128)S(6)} %copy.42.pad_ref, bf16[64,3072]{1,0:T(8,128)(2,1)S(1)} %copy-done.1, bf16[128,1536]{1,0:T(8,128)(2,1)S(1)} %constant_dynamic-update-slice_fusion.mid_0, bf16[128,1536]{1,0:T(8,128)(2,1)S(1)} %collective-permute-done.6.mid_1, ...), custom_call_target="tpu_custom_call" | custom-call | flops 201326592 | bytes 2195556 | tf_op jit(solution)/shard_map/pallas_call | solution.py:535
  34.1 1.6 %collective-permute-start.17 = (bf16[64,1536]{1,0:T(8,128)(2,1)S(1)}, bf16[64,1536]{1,0:T(8,128)(2,1)S(1)}, u32[]{:S(2)}, u32[]{:S(2)}) collective-permute-start(bf16[64,1536]{1,0:T(8,128)(2,1)S(1)} %constant_dynamic-update-slice_fusion.14), channel_id=1, source_target_pairs={{0,2},{1,3},{2,0},{3,1},{4,6},{5,7},{6,4},{7,5},{8,10},{9,11},{10,... | collective-permute-start | bytes 589832 | tf_op jit(solution)/shard_map/ppermute | solution.py:554
  35.9 1.8 %collective-permute-start.19 = (bf16[64,1536]{1,0:T(8,128)(2,1)S(1)}, bf16[64,1536]{1,0:T(8,128)(2,1)S(1)}, u32[]{:S(2)}, u32[]{:S(2)}) collective-permute-start(bf16[64,1536]{1,0:T(8,128)(2,1)S(1)} %constant_dynamic-update-slice_fusion.14), channel_id=1, source_target_pairs={{0,6},{1,7},{2,4},{3,5},{4,2},{5,3},{6,0},{7,1},{8,14},{9,15},{10,... | collective-permute-start | bytes 589832 | tf_op jit(solution)/shard_map/ppermute | solution.py:554
  37.7 3.6 %collective-permute-start.12 = (f32[16,128]{1,0:T(8,128)S(1)}, f32[16,128]{1,0:T(8,128)S(1)}, u32[]{:S(2)}, u32[]{:S(2)}) collective-permute-start(f32[16,128]{1,0:T(8,128)S(1)} %constant_dynamic-update-slice_fusion.8), channel_id=1, source_target_pairs={{0,16},{1,17},{2,18},{3,19},{4,20},{5,21},{6,22},{7,23},{8,24},{9,... | collective-permute-start | bytes 24584 | tf_op jit(solution)/shard_map/ppermute | solution.py:554
  41.3 2.5 %shard_map.151 = (bf16[256,768]{1,0:T(8,128)(2,1)}, bf16[384,256]{1,0:T(8,128)(2,1)S(1)}, bf16[384,256]{1,0:T(8,128)(2,1)S(1)}) custom-call(s32[2,12]{1,0:T(2,128)S(1)} %copy-done.5, f32[256,128]{1,0:T(8,128)S(1)} %get-tuple-element.75.near_stats, f32[256,128]{1,0:T(8,128)S(1)} %get-tuple-element.82.stats, f32[64,128]{1,0:T(8,128)S(1)} %get-tuple-element.86.picked, ...), custom_call_target="tpu_custom_call" | custom-call | flops 905969664 | bytes 3673184 | tf_op jit(solution)/shard_map/pallas_call | solution.py:535
  44.4 0.9 collective-permute-done.14.left_other
  45.8 2.2 %collective-permute-done.13 = f32[32,256]{1,0:T(8,128)S(1)} collective-permute-done((f32[32,256]{1,0:T(8,128)S(1)}, f32[32,256]{1,0:T(8,128)S(1)}, u32[]{:S(2)}, u32[]{:S(2)}) %collective-permute-start.13) | collective-permute-done | bytes 32800 | tf_op jit(solution)/shard_map/ppermute | solution.py:554
  48.0 1.6 %collective-permute-start.21 = (f32[64,256]{1,0:T(8,128)S(1)}, f32[64,256]{1,0:T(8,128)S(1)}, u32[]{:S(2)}, u32[]{:S(2)}) collective-permute-start(f32[64,256]{1,0:T(8,128)S(1)} %constant_dynamic-update-slice_fusion.12), channel_id=1, source_target_pairs={{0,2},{1,3},{2,0},{3,1},{4,6},{5,7},{6,4},{7,5},{8,10},{9,11},{10,... | collective-permute-start | bytes 196616 | tf_op jit(solution)/shard_map/ppermute | solution.py:554
  49.5 0.5 collective-permute-start.33
  50.1 4.1 %shard_map.153 = (bf16[256,768]{1,0:T(8,128)(2,1)S(1)}, f32[256,768]{1,0:T(8,128)S(1)}, f32[256,768]{1,0:T(8,128)S(1)}) custom-call(s32[2,12]{1,0:T(2,128)S(1)} %copy-done.5, s32[1]{0:T(128)S(6)} %copy.42.pad_ref, bf16[256,768]{1,0:T(8,128)(2,1)S(1)} %copy-done.6, bf16[256,768]{1,0:T(8,128)(2,1)S(1)} %copy-done.7, bf16[256,768]{1,0:T(8,128)(2,1)S(1)} %copy-done.8, ...), custom_call_target="tpu_custom_call" | custom-call | flops 805306368 | bytes 3866724 | tf_op jit(solution)/shard_map/pallas_call | solution.py:535
  55.6 2.5 %collective-permute-done.33 = bf16[192,768]{1,0:T(8,128)(2,1)S(1)} collective-permute-done((bf16[192,768]{1,0:T(8,128)(2,1)S(1)}, bf16[192,768]{1,0:T(8,128)(2,1)S(1)}, u32[]{:S(2)}, u32[]{:S(2)}) %collective-permute-start.33) | collective-permute-done | bytes 294944 | tf_op jit(solution)/shard_map/ppermute | solution.py:554
  58.6 2.4 %shard_map.155 = (bf16[256,768]{1,0:T(8,128)(2,1)S(1)}, bf16[256,768]{1,0:T(8,128)(2,1)S(1)}) custom-call(s32[2,12]{1,0:T(2,128)S(1)} %copy-done.5, s32[1]{0:T(128)S(6)} %copy.42.pad_ref, bf16[64,3072]{1,0:T(8,128)(2,1)S(1)} %copy-done.1, bf16[256,1536]{1,0:T(8,128)(2,1)S(1)} %constant_dynamic-update-slice_fusion.19.qg_0, ...), custom_call_target="tpu_custom_call" | custom-call | flops 15099494 | bytes 229381 | tf_op jit(solution)/shard_map/pallas_call | solution.py:535
  62.0 0.8 collective-permute-done.24.dk_other
  62.8 0.6 collective-permute-done.25.dv_other
  63.3 0.8 shard_map.156
  64.2 1.0 %collective-permute-start.27 = (bf16[96,1536]{1,0:T(8,128)(2,1)S(1)}, bf16[96,1536]{1,0:T(8,128)(2,1)S(1)}, u32[]{:S(2)}, u32[]{:S(2)}) collective-permute-start(bf16[96,1536]{1,0:T(8,128)(2,1)S(1)} %get-tuple-element.135), channel_id=1, source_target_pairs={{0,2},{1,3},{2,0},{3,1},{4,6},{5,7},{6,4},{7,5},{8,10},{9,11},{10,... | collective-permute-start | bytes 884744 | tf_op jit(solution)/shard_map/ppermute | solution.py:554
  65.6 1.2 %collective-permute-start.31 = (bf16[96,1536]{1,0:T(8,128)(2,1)S(1)}, bf16[96,1536]{1,0:T(8,128)(2,1)S(1)}, u32[]{:S(2)}, u32[]{:S(2)}) collective-permute-start(bf16[96,1536]{1,0:T(8,128)(2,1)S(1)} %get-tuple-element.133), channel_id=1, source_target_pairs={{0,4},{1,5},{2,6},{3,7},{4,0},{5,1},{6,2},{7,3},{8,12},{9,13},{10,... | collective-permute-start | bytes 884744 | tf_op jit(solution)/shard_map/ppermute | solution.py:554
  66.8 1.2 %collective-permute-start.32 = (bf16[96,1536]{1,0:T(8,128)(2,1)S(1)}, bf16[96,1536]{1,0:T(8,128)(2,1)S(1)}, u32[]{:S(2)}, u32[]{:S(2)}) collective-permute-start(bf16[96,1536]{1,0:T(8,128)(2,1)S(1)} %get-tuple-element.132), channel_id=1, source_target_pairs={{0,6},{1,7},{2,4},{3,5},{4,2},{5,3},{6,0},{7,1},{8,14},{9,15},{10,... | collective-permute-start | bytes 884744 | tf_op jit(solution)/shard_map/ppermute | solution.py:554
  68.1 1.9 %shard_map.157 = bf16[256,768]{1,0:T(8,128)(2,1)} custom-call(bf16[256,768]{1,0:T(8,128)(2,1)S(1)} %get-tuple-element.121.right.dq, bf16[256,768]{1,0:T(8,128)(2,1)S(1)} %get-tuple-element.119.dk, bf16[256,768]{1,0:T(8,128)(2,1)S(1)} %get-tuple-element.120.dv, bf16[768,2304]{1,0:T(8,128)(2,1)S(1)} %copy-done), custom_call_target="tpu_custom_call" | custom-call | flops 45298484 | bytes 255590 | tf_op jit(solution)/shard_map/pallas_call | solution.py:535
  69.9 4.2 %collective-permute-done.27 = bf16[96,1536]{1,0:T(8,128)(2,1)S(1)} collective-permute-done((bf16[96,1536]{1,0:T(8,128)(2,1)S(1)}, bf16[96,1536]{1,0:T(8,128)(2,1)S(1)}, u32[]{:S(2)}, u32[]{:S(2)}) %collective-permute-start.27) | collective-permute-done | bytes 294944 | tf_op jit(solution)/shard_map/ppermute | solution.py:554
  74.5 2.1 %collective-permute-start.28 = (bf16[96,768]{1,0:T(8,128)(2,1)S(1)}, bf16[96,768]{1,0:T(8,128)(2,1)S(1)}, u32[]{:S(2)}, u32[]{:S(2)}) collective-permute-start(bf16[96,768]{1,0:T(8,128)(2,1)S(1)} %slice.175), channel_id=1, source_target_pairs={{0,16},{1,17},{2,18},{3,19},{4,20},{5,21},{6,22},{7,23},{8,24},{9,... | collective-permute-start | bytes 442376 | tf_op jit(solution)/shard_map/ppermute | solution.py:554
  76.6 2.0 %collective-permute-done.35 = bf16[48,768]{1,0:T(8,128)(2,1)S(1)} collective-permute-done((bf16[48,768]{1,0:T(8,128)(2,1)S(1)}, bf16[48,768]{1,0:T(8,128)(2,1)S(1)}, u32[]{:S(2)}, u32[]{:S(2)}) %collective-permute-start.35) | collective-permute-done | bytes 73760 | tf_op jit(solution)/shard_map/ppermute | solution.py:554
  78.7 2.6 %collective-permute-start.39 = (bf16[24,768]{1,0:T(8,128)(2,1)S(1)}, bf16[24,768]{1,0:T(8,128)(2,1)S(1)}, u32[]{:S(2)}, u32[]{:S(2)}) collective-permute-start(bf16[24,768]{1,0:T(8,128)(2,1)S(1)} %slice.194), channel_id=1, source_target_pairs={{0,16},{1,17},{2,18},{3,19},{4,20},{5,21},{6,22},{7,23},{8,24},{9,... | collective-permute-start | bytes 110600 | tf_op jit(solution)/shard_map/ppermute | solution.py:554
  81.5 0.9 collective-permute-start.36
  82.4 2.3 %collective-permute-start.37 = (bf16[24,1536]{1,0:T(8,128)(2,1)S(1)}, bf16[24,1536]{1,0:T(8,128)(2,1)S(1)}, u32[]{:S(2)}, u32[]{:S(2)}) collective-permute-start(bf16[24,1536]{1,0:T(8,128)(2,1)S(1)} %get-tuple-element.145), channel_id=1, source_target_pairs={{0,16},{1,17},{2,18},{3,19},{4,20},{5,21},{6,22},{7,23},{8,24},{9,... | collective-permute-start | bytes 221192 | tf_op jit(solution)/shard_map/ppermute | solution.py:554
  84.7 1.2 %collective-permute-start.38 = (bf16[24,1536]{1,0:T(8,128)(2,1)S(1)}, bf16[24,1536]{1,0:T(8,128)(2,1)S(1)}, u32[]{:S(2)}, u32[]{:S(2)}) collective-permute-start(bf16[24,1536]{1,0:T(8,128)(2,1)S(1)} %get-tuple-element.144), channel_id=1, source_target_pairs={{0,24},{1,25},{2,26},{3,27},{4,28},{5,29},{6,30},{7,31},{8,16},{9,... | collective-permute-start | bytes 221192 | tf_op jit(solution)/shard_map/ppermute | solution.py:554
  86.0 1.1 %collective-permute-start.29 = (bf16[48,768]{1,0:T(8,128)(2,1)S(1)}, bf16[48,768]{1,0:T(8,128)(2,1)S(1)}, u32[]{:S(2)}, u32[]{:S(2)}) collective-permute-start(bf16[48,768]{1,0:T(8,128)(2,1)S(1)} %slice.177), channel_id=1, source_target_pairs={{0,2},{1,3},{2,0},{3,1},{4,6},{5,7},{6,4},{7,5},{8,10},{9,11},{10,... | collective-permute-start | bytes 221192 | tf_op jit(solution)/shard_map/ppermute | solution.py:554
  87.1 0.6 convert_add_fusion.1
  87.8 2.7 %collective-permute-done.29 = bf16[48,768]{1,0:T(8,128)(2,1)S(1)} collective-permute-done((bf16[48,768]{1,0:T(8,128)(2,1)S(1)}, bf16[48,768]{1,0:T(8,128)(2,1)S(1)}, u32[]{:S(2)}, u32[]{:S(2)}) %collective-permute-start.29) | collective-permute-done | bytes 73760 | tf_op jit(solution)/shard_map/ppermute | solution.py:554
  90.5 1.2 %collective-permute-start.30 = (bf16[24,768]{1,0:T(8,128)(2,1)S(1)}, bf16[24,768]{1,0:T(8,128)(2,1)S(1)}, u32[]{:S(2)}, u32[]{:S(2)}) collective-permute-start(bf16[24,768]{1,0:T(8,128)(2,1)S(1)} %slice.179), channel_id=1, source_target_pairs={{0,4},{1,5},{2,6},{3,7},{4,0},{5,1},{6,2},{7,3},{8,12},{9,13},{10,... | collective-permute-start | bytes 110600 | tf_op jit(solution)/shard_map/ppermute | solution.py:554
  91.7 2.8 %collective-permute-done.30 = bf16[24,768]{1,0:T(8,128)(2,1)S(1)} collective-permute-done((bf16[24,768]{1,0:T(8,128)(2,1)S(1)}, bf16[24,768]{1,0:T(8,128)(2,1)S(1)}, u32[]{:S(2)}, u32[]{:S(2)}) %collective-permute-start.30) | collective-permute-done | bytes 36896 | tf_op jit(solution)/shard_map/ppermute | solution.py:554
  94.5 0.7 pad_maximum_fusion
  (138 shorter events, 6.1 us)
Async XLA Ops:
  0.6 14.7 %copy-start.10 = (s32[768,1]{1,0:T(8,128)S(1)}, s32[768,1]{1,0:T(8,128)}, u32[]{:S(2)}) copy-start(s32[768,1]{1,0:T(8,128)} %constant.14.clone) | copy-start | bytes 9220
  0.6 14.7 %copy-start.11 = (s32[768,1]{1,0:T(8,128)S(1)}, s32[768,1]{1,0:T(8,128)}, u32[]{:S(2)}) copy-start(s32[768,1]{1,0:T(8,128)} %constant.15.clone) | copy-start | bytes 9220
  0.7 14.7 %copy-start.12 = (s32[768,1]{1,0:T(8,128)S(1)}, s32[768,1]{1,0:T(8,128)}, u32[]{:S(2)}) copy-start(s32[768,1]{1,0:T(8,128)} %constant.16.clone) | copy-start | bytes 9220
  0.7 14.7 %copy-start.13 = (s32[768,1]{1,0:T(8,128)S(1)}, s32[768,1]{1,0:T(8,128)}, u32[]{:S(2)}) copy-start(s32[768,1]{1,0:T(8,128)} %constant.17.clone) | copy-start | bytes 9220
  6.4 10.6 %collective-permute-start = (bf16[8,3072]{1,0:T(8,128)(2,1)}, bf16[8,3072]{1,0:T(8,128)(2,1)S(1)}, u32[]{:S(2)}, u32[]{:S(2)}) collective-permute-start(bf16[8,3072]{1,0:T(8,128)(2,1)} %get-tuple-element.106), channel_id=1, source_target_pairs={{0,8},{1,9},{2,10},{3,11},{4,12},{5,13},{6,14},{7,15},{8,0},{9,1},... | collective-permute-start | bytes 147464 | tf_op jit(solution)/shard_map/ppermute | solution.py:554
  9.5 7.9 %collective-permute-start.1 = (bf16[8,3072]{1,0:T(8,128)(2,1)}, bf16[8,3072]{1,0:T(8,128)(2,1)S(1)}, u32[]{:S(2)}, u32[]{:S(2)}) collective-permute-start(bf16[8,3072]{1,0:T(8,128)(2,1)} %get-tuple-element.106), channel_id=1, source_target_pairs={{0,16},{1,17},{2,18},{3,19},{4,20},{5,21},{6,22},{7,23},{8,24},{9,... | collective-permute-start | bytes 147464 | tf_op jit(solution)/shard_map/ppermute | solution.py:554
  12.1 6.1 %collective-permute-start.2 = (bf16[8,3072]{1,0:T(8,128)(2,1)}, bf16[8,3072]{1,0:T(8,128)(2,1)S(1)}, u32[]{:S(2)}, u32[]{:S(2)}) collective-permute-start(bf16[8,3072]{1,0:T(8,128)(2,1)} %get-tuple-element.106), channel_id=1, source_target_pairs={{0,24},{1,25},{2,26},{3,27},{4,28},{5,29},{6,30},{7,31},{8,16},{9,... | collective-permute-start | bytes 147464 | tf_op jit(solution)/shard_map/ppermute | solution.py:554
  12.1 6.1 %collective-permute-start.3 = (bf16[32,1536]{1,0:T(8,128)(2,1)}, bf16[32,1536]{1,0:T(8,128)(2,1)S(1)}, u32[]{:S(2)}, u32[]{:S(2)}) collective-permute-start(bf16[32,1536]{1,0:T(8,128)(2,1)} %get-tuple-element.70), channel_id=1, source_target_pairs={{0,2},{1,3},{2,0},{3,1},{4,6},{5,7},{6,4},{7,5},{8,10},{9,11},{10,... | collective-permute-start | bytes 294920 | tf_op jit(solution)/shard_map/ppermute | solution.py:554
  13.8 5.1 %collective-permute-start.4 = (bf16[32,1536]{1,0:T(8,128)(2,1)}, bf16[32,1536]{1,0:T(8,128)(2,1)S(1)}, u32[]{:S(2)}, u32[]{:S(2)}) collective-permute-start(bf16[32,1536]{1,0:T(8,128)(2,1)} %get-tuple-element.70), channel_id=1, source_target_pairs={{0,4},{1,5},{2,6},{3,7},{4,0},{5,1},{6,2},{7,3},{8,12},{9,13},{10,... | collective-permute-start | bytes 294920 | tf_op jit(solution)/shard_map/ppermute | solution.py:554
  15.4 7.5 %copy-start.8 = (bf16[256,768]{1,0:T(8,128)(2,1)S(1)}, bf16[256,768]{1,0:T(8,128)(2,1)}, u32[]{:S(2)}) copy-start(bf16[256,768]{1,0:T(8,128)(2,1)} %get-tuple-element.73.v) | copy-start | bytes 1179652
  15.4 7.5 %copy-start.9 = (bf16[256,768]{1,0:T(8,128)(2,1)S(1)}, bf16[256,768]{1,0:T(8,128)(2,1)}, u32[]{:S(2)}) copy-start(bf16[256,768]{1,0:T(8,128)(2,1)} %get-tuple-element.74.g) | copy-start | bytes 1179652
  16.3 6.7 %copy-start.7 = (bf16[256,768]{1,0:T(8,128)(2,1)S(1)}, bf16[256,768]{1,0:T(8,128)(2,1)}, u32[]{:S(2)}) copy-start(bf16[256,768]{1,0:T(8,128)(2,1)} %get-tuple-element.72.k) | copy-start | bytes 1179652
  17.1 5.8 %collective-permute-start.5 = (bf16[32,1536]{1,0:T(8,128)(2,1)S(1)}, bf16[32,1536]{1,0:T(8,128)(2,1)S(1)}, u32[]{:S(2)}, u32[]{:S(2)}) collective-permute-start(bf16[32,1536]{1,0:T(8,128)(2,1)S(1)} %copy-done.15), channel_id=1, source_target_pairs={{0,6},{1,7},{2,4},{3,5},{4,2},{5,3},{6,0},{7,1},{8,14},{9,15},{10,... | collective-permute-start | bytes 294920 | tf_op jit(solution)/shard_map/ppermute | solution.py:554
  18.9 6.7 %collective-permute-start.7 = (bf16[32,1536]{1,0:T(8,128)(2,1)S(1)}, bf16[32,1536]{1,0:T(8,128)(2,1)S(1)}, u32[]{:S(2)}, u32[]{:S(2)}) collective-permute-start(bf16[32,1536]{1,0:T(8,128)(2,1)S(1)} %pad_maximum_fusion.1), channel_id=1, source_target_pairs={{0,2},{1,3},{2,0},{3,1},{4,6},{5,7},{6,4},{7,5},{8,10},{9,11},{10,... | collective-permute-start | bytes 294920 | tf_op jit(solution)/shard_map/ppermute | solution.py:554
  19.8 5.8 %collective-permute-start.8 = (bf16[32,1536]{1,0:T(8,128)(2,1)S(1)}, bf16[32,1536]{1,0:T(8,128)(2,1)S(1)}, u32[]{:S(2)}, u32[]{:S(2)}) collective-permute-start(bf16[32,1536]{1,0:T(8,128)(2,1)S(1)} %pad_maximum_fusion.1), channel_id=1, source_target_pairs={{0,4},{1,5},{2,6},{3,7},{4,0},{5,1},{6,2},{7,3},{8,12},{9,13},{10,... | collective-permute-start | bytes 294920 | tf_op jit(solution)/shard_map/ppermute | solution.py:554
  21.8 5.5 %collective-permute-start.9 = (bf16[32,1536]{1,0:T(8,128)(2,1)S(1)}, bf16[32,1536]{1,0:T(8,128)(2,1)S(1)}, u32[]{:S(2)}, u32[]{:S(2)}) collective-permute-start(bf16[32,1536]{1,0:T(8,128)(2,1)S(1)} %pad_maximum_fusion.1), channel_id=1, source_target_pairs={{0,6},{1,7},{2,4},{3,5},{4,2},{5,3},{6,0},{7,1},{8,14},{9,15},{10,... | collective-permute-start | bytes 294920 | tf_op jit(solution)/shard_map/ppermute | solution.py:554
  22.8 4.6 %collective-permute-start.6 = (bf16[128,1536]{1,0:T(8,128)(2,1)S(1)}, bf16[128,1536]{1,0:T(8,128)(2,1)S(1)}, u32[]{:S(2)}, u32[]{:S(2)}) collective-permute-start(bf16[128,1536]{1,0:T(8,128)(2,1)S(1)} %constant_dynamic-update-slice_fusion.mid_0), channel_id=1, source_target_pairs={{0,1},{1,0},{2,3},{3,2},{4,5},{5,4},{6,7},{7,6},{8,9},{9,8},{10,11... | collective-permute-start | bytes 1179656 | tf_op jit(solution)/shard_map/ppermute | solution.py:554
  27.3 1.8 %collective-permute-start.10 = (bf16[128,1536]{1,0:T(8,128)(2,1)S(1)}, bf16[128,1536]{1,0:T(8,128)(2,1)S(1)}, u32[]{:S(2)}, u32[]{:S(2)}) collective-permute-start(bf16[128,1536]{1,0:T(8,128)(2,1)S(1)} %constant_dynamic-update-slice_fusion.4.far_0), channel_id=1, source_target_pairs={{0,1},{1,0},{2,3},{3,2},{4,5},{5,4},{6,7},{7,6},{8,9},{9,8},{10,11... | collective-permute-start | bytes 1179656 | tf_op jit(solution)/shard_map/ppermute | solution.py:554
  31.5 9.8 %copy-start.2 = (bf16[768,768]{1,0:T(8,128)(2,1)S(1)}, bf16[768,768]{1,0:T(8,128)(2,1)}, u32[]{:S(2)}) copy-start(bf16[768,768]{1,0:T(8,128)(2,1)} %w_out.1) | copy-start | bytes 3538948
  31.5 6.2 %collective-permute-start.11 = (f32[8,128]{1,0:T(8,128)S(1)}, f32[8,128]{1,0:T(8,128)S(1)}, u32[]{:S(2)}, u32[]{:S(2)}) collective-permute-start(f32[8,128]{1,0:T(8,128)S(1)} %slice.130), channel_id=1, source_target_pairs={{0,8},{1,9},{2,10},{3,11},{4,12},{5,13},{6,14},{7,15},{8,0},{9,1},... | collective-permute-start | bytes 12296 | tf_op jit(solution)/shard_map/ppermute | solution.py:554
  34.1 20.0 %collective-permute-start.17 = (bf16[64,1536]{1,0:T(8,128)(2,1)S(1)}, bf16[64,1536]{1,0:T(8,128)(2,1)S(1)}, u32[]{:S(2)}, u32[]{:S(2)}) collective-permute-start(bf16[64,1536]{1,0:T(8,128)(2,1)S(1)} %constant_dynamic-update-slice_fusion.14), channel_id=1, source_target_pairs={{0,2},{1,3},{2,0},{3,1},{4,6},{5,7},{6,4},{7,5},{8,10},{9,11},{10,... | collective-permute-start | bytes 589832 | tf_op jit(solution)/shard_map/ppermute | solution.py:554
  35.7 18.5 %collective-permute-start.18 = (bf16[64,1536]{1,0:T(8,128)(2,1)S(1)}, bf16[64,1536]{1,0:T(8,128)(2,1)S(1)}, u32[]{:S(2)}, u32[]{:S(2)}) collective-permute-start(bf16[64,1536]{1,0:T(8,128)(2,1)S(1)} %constant_dynamic-update-slice_fusion.14), channel_id=1, source_target_pairs={{0,4},{1,5},{2,6},{3,7},{4,0},{5,1},{6,2},{7,3},{8,12},{9,13},{10,... | collective-permute-start | bytes 589832 | tf_op jit(solution)/shard_map/ppermute | solution.py:554
  35.9 18.9 %collective-permute-start.19 = (bf16[64,1536]{1,0:T(8,128)(2,1)S(1)}, bf16[64,1536]{1,0:T(8,128)(2,1)S(1)}, u32[]{:S(2)}, u32[]{:S(2)}) collective-permute-start(bf16[64,1536]{1,0:T(8,128)(2,1)S(1)} %constant_dynamic-update-slice_fusion.14), channel_id=1, source_target_pairs={{0,6},{1,7},{2,4},{3,5},{4,2},{5,3},{6,0},{7,1},{8,14},{9,15},{10,... | collective-permute-start | bytes 589832 | tf_op jit(solution)/shard_map/ppermute | solution.py:554
  37.7 6.3 %collective-permute-start.15 = (bf16[256,768]{1,0:T(8,128)(2,1)S(1)}, bf16[256,768]{1,0:T(8,128)(2,1)S(1)}, u32[]{:S(2)}, u32[]{:S(2)}) collective-permute-start(bf16[256,768]{1,0:T(8,128)(2,1)S(1)} %copy-done.4), channel_id=1, source_target_pairs={{0,1},{1,0},{2,3},{3,2},{4,5},{5,4},{6,7},{7,6},{8,9},{9,8},{10,11... | collective-permute-start | bytes 1179656 | tf_op jit(solution)/shard_map/ppermute | solution.py:554
  37.7 6.1 %collective-permute-start.12 = (f32[16,128]{1,0:T(8,128)S(1)}, f32[16,128]{1,0:T(8,128)S(1)}, u32[]{:S(2)}, u32[]{:S(2)}) collective-permute-start(f32[16,128]{1,0:T(8,128)S(1)} %constant_dynamic-update-slice_fusion.8), channel_id=1, source_target_pairs={{0,16},{1,17},{2,18},{3,19},{4,20},{5,21},{6,22},{7,23},{8,24},{9,... | collective-permute-start | bytes 24584 | tf_op jit(solution)/shard_map/ppermute | solution.py:554
  43.8 1.4 %collective-permute-start.14 = (bf16[384,256]{1,0:T(8,128)(2,1)S(1)}, bf16[384,256]{1,0:T(8,128)(2,1)S(1)}, u32[]{:S(2)}, u32[]{:S(2)}) collective-permute-start(bf16[384,256]{1,0:T(8,128)(2,1)S(1)} %get-tuple-element.94), channel_id=1, source_target_pairs={{0,1},{1,0},{2,3},{3,2},{4,5},{5,4},{6,7},{7,6},{8,9},{9,8},{10,11... | collective-permute-start | bytes 589832 | tf_op jit(solution)/shard_map/ppermute | solution.py:554
  44.0 4.0 %collective-permute-start.13 = (f32[32,256]{1,0:T(8,128)S(1)}, f32[32,256]{1,0:T(8,128)S(1)}, u32[]{:S(2)}, u32[]{:S(2)}) collective-permute-start(f32[32,256]{1,0:T(8,128)S(1)} %pad_maximum_fusion.2), channel_id=1, source_target_pairs={{0,4},{1,5},{2,6},{3,7},{4,0},{5,1},{6,2},{7,3},{8,12},{9,13},{10,... | collective-permute-start | bytes 98312 | tf_op jit(solution)/shard_map/ppermute | solution.py:554
  48.0 7.0 %collective-permute-start.21 = (f32[64,256]{1,0:T(8,128)S(1)}, f32[64,256]{1,0:T(8,128)S(1)}, u32[]{:S(2)}, u32[]{:S(2)}) collective-permute-start(f32[64,256]{1,0:T(8,128)S(1)} %constant_dynamic-update-slice_fusion.12), channel_id=1, source_target_pairs={{0,2},{1,3},{2,0},{3,1},{4,6},{5,7},{6,4},{7,5},{8,10},{9,11},{10,... | collective-permute-start | bytes 196616 | tf_op jit(solution)/shard_map/ppermute | solution.py:554
  49.5 8.6 %collective-permute-start.33 = (bf16[192,768]{1,0:T(8,128)(2,1)S(1)}, bf16[192,768]{1,0:T(8,128)(2,1)S(1)}, u32[]{:S(2)}, u32[]{:S(2)}) collective-permute-start(bf16[192,768]{1,0:T(8,128)(2,1)S(1)} %get-tuple-element.138), channel_id=1, source_target_pairs={{0,2},{1,3},{2,0},{3,1},{4,6},{5,7},{6,4},{7,5},{8,10},{9,11},{10,... | collective-permute-start | bytes 884744 | tf_op jit(solution)/shard_map/ppermute | solution.py:554
  54.2 3.9 %collective-permute-start.16 = (bf16[768,256]{1,0:T(8,128)(2,1)S(1)}, bf16[768,256]{1,0:T(8,128)(2,1)S(1)}, u32[]{:S(2)}, u32[]{:S(2)}) collective-permute-start(bf16[768,256]{1,0:T(8,128)(2,1)S(1)} %get-tuple-element.103), channel_id=1, source_target_pairs={{0,1},{1,0},{2,3},{3,2},{4,5},{5,4},{6,7},{7,6},{8,9},{9,8},{10,11... | collective-permute-start | bytes 1179656 | tf_op jit(solution)/shard_map/ppermute | solution.py:554
  54.3 3.8 %collective-permute-start.23 = (bf16[256,768]{1,0:T(8,128)(2,1)S(1)}, bf16[256,768]{1,0:T(8,128)(2,1)S(1)}, u32[]{:S(2)}, u32[]{:S(2)}) collective-permute-start(bf16[256,768]{1,0:T(8,128)(2,1)S(1)} %get-tuple-element.121.right.dq), channel_id=1, source_target_pairs={{0,1},{1,0},{2,3},{3,2},{4,5},{5,4},{6,7},{7,6},{8,9},{9,8},{10,11... | collective-permute-start | bytes 1179656 | tf_op jit(solution)/shard_map/ppermute | solution.py:554
  54.8 3.8 %collective-permute-start.20 = (bf16[256,1536]{1,0:T(8,128)(2,1)S(1)}, bf16[256,1536]{1,0:T(8,128)(2,1)S(1)}, u32[]{:S(2)}, u32[]{:S(2)}) collective-permute-start(bf16[256,1536]{1,0:T(8,128)(2,1)S(1)} %constant_dynamic-update-slice_fusion.19.qg_0), channel_id=1, source_target_pairs={{0,1},{1,0},{2,3},{3,2},{4,5},{5,4},{6,7},{7,6},{8,9},{9,8},{10,11... | collective-permute-start | bytes 2359304 | tf_op jit(solution)/shard_map/ppermute | solution.py:554
  55.1 3.5 %collective-permute-start.22 = (f32[256,128]{1,0:T(8,128)S(1)}, f32[256,128]{1,0:T(8,128)S(1)}, u32[]{:S(2)}, u32[]{:S(2)}) collective-permute-start(f32[256,128]{1,0:T(8,128)S(1)} %constant_dynamic-update-slice_fusion.23.stats_0), channel_id=1, source_target_pairs={{0,1},{1,0},{2,3},{3,2},{4,5},{5,4},{6,7},{7,6},{8,9},{9,8},{10,11... | collective-permute-start | bytes 393224 | tf_op jit(solution)/shard_map/ppermute | solution.py:554
  61.0 1.8 %collective-permute-start.24 = (bf16[256,768]{1,0:T(8,128)(2,1)S(1)}, bf16[256,768]{1,0:T(8,128)(2,1)S(1)}, u32[]{:S(2)}, u32[]{:S(2)}) collective-permute-start(bf16[256,768]{1,0:T(8,128)(2,1)S(1)} %get-tuple-element.119.dk), channel_id=1, source_target_pairs={{0,1},{1,0},{2,3},{3,2},{4,5},{5,4},{6,7},{7,6},{8,9},{9,8},{10,11... | collective-permute-start | bytes 1179656 | tf_op jit(solution)/shard_map/ppermute | solution.py:554
  61.0 2.3 %collective-permute-start.25 = (bf16[256,768]{1,0:T(8,128)(2,1)S(1)}, bf16[256,768]{1,0:T(8,128)(2,1)S(1)}, u32[]{:S(2)}, u32[]{:S(2)}) collective-permute-start(bf16[256,768]{1,0:T(8,128)(2,1)S(1)} %get-tuple-element.120.dv), channel_id=1, source_target_pairs={{0,1},{1,0},{2,3},{3,2},{4,5},{5,4},{6,7},{7,6},{8,9},{9,8},{10,11... | collective-permute-start | bytes 1179656 | tf_op jit(solution)/shard_map/ppermute | solution.py:554
  61.6 8.3 %collective-permute-start.34 = (bf16[96,768]{1,0:T(8,128)(2,1)S(1)}, bf16[96,768]{1,0:T(8,128)(2,1)S(1)}, u32[]{:S(2)}, u32[]{:S(2)}) collective-permute-start(bf16[96,768]{1,0:T(8,128)(2,1)S(1)} %get-tuple-element.146), channel_id=1, source_target_pairs={{0,4},{1,5},{2,6},{3,7},{4,0},{5,1},{6,2},{7,3},{8,12},{9,13},{10,... | collective-permute-start | bytes 442376 | tf_op jit(solution)/shard_map/ppermute | solution.py:554
  64.2 9.9 %collective-permute-start.27 = (bf16[96,1536]{1,0:T(8,128)(2,1)S(1)}, bf16[96,1536]{1,0:T(8,128)(2,1)S(1)}, u32[]{:S(2)}, u32[]{:S(2)}) collective-permute-start(bf16[96,1536]{1,0:T(8,128)(2,1)S(1)} %get-tuple-element.135), channel_id=1, source_target_pairs={{0,2},{1,3},{2,0},{3,1},{4,6},{5,7},{6,4},{7,5},{8,10},{9,11},{10,... | collective-permute-start | bytes 884744 | tf_op jit(solution)/shard_map/ppermute | solution.py:554
  65.3 9.2 %collective-permute-start.26 = (bf16[192,768]{1,0:T(8,128)(2,1)S(1)}, bf16[192,768]{1,0:T(8,128)(2,1)S(1)}, u32[]{:S(2)}, u32[]{:S(2)}) collective-permute-start(bf16[192,768]{1,0:T(8,128)(2,1)S(1)} %get-tuple-element.136), channel_id=1, source_target_pairs={{0,8},{1,9},{2,10},{3,11},{4,12},{5,13},{6,14},{7,15},{8,0},{9,1},... | collective-permute-start | bytes 884744 | tf_op jit(solution)/shard_map/ppermute | solution.py:554
  65.6 15.7 %collective-permute-start.31 = (bf16[96,1536]{1,0:T(8,128)(2,1)S(1)}, bf16[96,1536]{1,0:T(8,128)(2,1)S(1)}, u32[]{:S(2)}, u32[]{:S(2)}) collective-permute-start(bf16[96,1536]{1,0:T(8,128)(2,1)S(1)} %get-tuple-element.133), channel_id=1, source_target_pairs={{0,4},{1,5},{2,6},{3,7},{4,0},{5,1},{6,2},{7,3},{8,12},{9,13},{10,... | collective-permute-start | bytes 884744 | tf_op jit(solution)/shard_map/ppermute | solution.py:554
  66.8 14.5 %collective-permute-start.32 = (bf16[96,1536]{1,0:T(8,128)(2,1)S(1)}, bf16[96,1536]{1,0:T(8,128)(2,1)S(1)}, u32[]{:S(2)}, u32[]{:S(2)}) collective-permute-start(bf16[96,1536]{1,0:T(8,128)(2,1)S(1)} %get-tuple-element.132), channel_id=1, source_target_pairs={{0,6},{1,7},{2,4},{3,5},{4,2},{5,3},{6,0},{7,1},{8,14},{9,15},{10,... | collective-permute-start | bytes 884744 | tf_op jit(solution)/shard_map/ppermute | solution.py:554
  74.2 4.5 %collective-permute-start.35 = (bf16[48,768]{1,0:T(8,128)(2,1)S(1)}, bf16[48,768]{1,0:T(8,128)(2,1)S(1)}, u32[]{:S(2)}, u32[]{:S(2)}) collective-permute-start(bf16[48,768]{1,0:T(8,128)(2,1)S(1)} %slice.188), channel_id=1, source_target_pairs={{0,8},{1,9},{2,10},{3,11},{4,12},{5,13},{6,14},{7,15},{8,0},{9,1},... | collective-permute-start | bytes 221192 | tf_op jit(solution)/shard_map/ppermute | solution.py:554
  74.5 11.4 %collective-permute-start.28 = (bf16[96,768]{1,0:T(8,128)(2,1)S(1)}, bf16[96,768]{1,0:T(8,128)(2,1)S(1)}, u32[]{:S(2)}, u32[]{:S(2)}) collective-permute-start(bf16[96,768]{1,0:T(8,128)(2,1)S(1)} %slice.175), channel_id=1, source_target_pairs={{0,16},{1,17},{2,18},{3,19},{4,20},{5,21},{6,22},{7,23},{8,24},{9,... | collective-permute-start | bytes 442376 | tf_op jit(solution)/shard_map/ppermute | solution.py:554
  78.7 8.4 %collective-permute-start.39 = (bf16[24,768]{1,0:T(8,128)(2,1)S(1)}, bf16[24,768]{1,0:T(8,128)(2,1)S(1)}, u32[]{:S(2)}, u32[]{:S(2)}) collective-permute-start(bf16[24,768]{1,0:T(8,128)(2,1)S(1)} %slice.194), channel_id=1, source_target_pairs={{0,16},{1,17},{2,18},{3,19},{4,20},{5,21},{6,22},{7,23},{8,24},{9,... | collective-permute-start | bytes 110600 | tf_op jit(solution)/shard_map/ppermute | solution.py:554
  81.5 10.2 %collective-permute-start.36 = (bf16[24,1536]{1,0:T(8,128)(2,1)S(1)}, bf16[24,1536]{1,0:T(8,128)(2,1)S(1)}, u32[]{:S(2)}, u32[]{:S(2)}) collective-permute-start(bf16[24,1536]{1,0:T(8,128)(2,1)S(1)} %get-tuple-element.143), channel_id=1, source_target_pairs={{0,8},{1,9},{2,10},{3,11},{4,12},{5,13},{6,14},{7,15},{8,0},{9,1},... | collective-permute-start | bytes 221192 | tf_op jit(solution)/shard_map/ppermute | solution.py:554
  82.4 9.2 %collective-permute-start.37 = (bf16[24,1536]{1,0:T(8,128)(2,1)S(1)}, bf16[24,1536]{1,0:T(8,128)(2,1)S(1)}, u32[]{:S(2)}, u32[]{:S(2)}) collective-permute-start(bf16[24,1536]{1,0:T(8,128)(2,1)S(1)} %get-tuple-element.145), channel_id=1, source_target_pairs={{0,16},{1,17},{2,18},{3,19},{4,20},{5,21},{6,22},{7,23},{8,24},{9,... | collective-permute-start | bytes 221192 | tf_op jit(solution)/shard_map/ppermute | solution.py:554
  84.7 7.0 %collective-permute-start.38 = (bf16[24,1536]{1,0:T(8,128)(2,1)S(1)}, bf16[24,1536]{1,0:T(8,128)(2,1)S(1)}, u32[]{:S(2)}, u32[]{:S(2)}) collective-permute-start(bf16[24,1536]{1,0:T(8,128)(2,1)S(1)} %get-tuple-element.144), channel_id=1, source_target_pairs={{0,24},{1,25},{2,26},{3,27},{4,28},{5,29},{6,30},{7,31},{8,16},{9,... | collective-permute-start | bytes 221192 | tf_op jit(solution)/shard_map/ppermute | solution.py:554
  86.0 4.4 %collective-permute-start.29 = (bf16[48,768]{1,0:T(8,128)(2,1)S(1)}, bf16[48,768]{1,0:T(8,128)(2,1)S(1)}, u32[]{:S(2)}, u32[]{:S(2)}) collective-permute-start(bf16[48,768]{1,0:T(8,128)(2,1)S(1)} %slice.177), channel_id=1, source_target_pairs={{0,2},{1,3},{2,0},{3,1},{4,6},{5,7},{6,4},{7,5},{8,10},{9,11},{10,... | collective-permute-start | bytes 221192 | tf_op jit(solution)/shard_map/ppermute | solution.py:554
  90.5 4.0 %collective-permute-start.30 = (bf16[24,768]{1,0:T(8,128)(2,1)S(1)}, bf16[24,768]{1,0:T(8,128)(2,1)S(1)}, u32[]{:S(2)}, u32[]{:S(2)}) collective-permute-start(bf16[24,768]{1,0:T(8,128)(2,1)S(1)} %slice.179), channel_id=1, source_target_pairs={{0,4},{1,5},{2,6},{3,7},{4,0},{5,1},{6,2},{7,3},{8,12},{9,13},{10,... | collective-permute-start | bytes 110600 | tf_op jit(solution)/shard_map/ppermute | solution.py:554
  (9 other events, 40.4 us)

commit v12 on v10

--- a/solution.py
+++ b/solution.py
@@ -627,7 +627,7 @@
     rows, width = z.rows, z.width
     masks = [mask for mask in (2**i for i in range(30)) if GROUP <= mask < n]
     order = strip_order(z, own, [1, 4, 2] + masks[::-1])
-    order_q = strip_order(z, own, [1] + masks + [2, 4])
+    order_q = strip_order(z, own, [1] + masks[:-1] + [4, 2] + masks[-1:])
     order_out = strip_order(z, own, [1, 2, 4] + masks)
     base_flops = 2 * rows * rows * width
 
@@ -759,7 +759,9 @@
         cost=LOW_COST,
     )(after(dq, late_half), dk, dv, w_qkv)
     late_parts = block_parts(late_half, PLANE, n)
-    early = halved(early_half, masks + [2, 4], n, ((late_parts[1],),))
+    early = halved(early_half, masks[:-1], n, ((late_parts[1],),)).astype(BF)
+    early = sum_parts(block_parts(early, PLANE, n), BF)
+    early = halved(early, masks[-1:], n)
     wout = halved(wout_half, [2, 4] + masks[:-1], n, ((dk_near,), (late_parts[1],))).astype(BF)
     late = sum_parts(tied(late_parts, (wout,)), BF)
     grad_wout = halved(wout, masks[-1:], n)

time: 95.2 us -> 95.8 us (level)
    ppermute x40 -> x41, waiting for transfers between devices: 23.6 us -> 24.1 us  [swap(): return lax.ppermute(value, 'ctx', [(d, d ^ mask) for d in range(dev_count)])]
    ppermute x40 -> x41, starting transfers between devices: 41.3 us -> 41.6 us  [swap(): return lax.ppermute(value, 'ctx', [(d, d ^ mask) for d in range(dev_count)])]
  transfers between devices with their start and end apart: 40 -> 41, of which waited for: 14 -> 15; matrix products, arithmetic and copies ran while one was open for 2% -> 2% of each run, Pallas kernels for 15% -> 15%
where the time goes in v12:
time: 95.8 us; the launch traced here: 95.7 us
  starting transfers between devices  41.6 us (43%)
  Pallas kernels  24.8 us (26%)
  waiting for transfers between devices  24.1 us (25%)
  between operations  2.06 us (2%)
  other arithmetic  1.92 us (2%)
  local copies, waits for them, and re-layouts  1.27 us (1%)
    ppermute x41, starting transfers between devices, swap(): return lax.ppermute(value, 'ctx', [(d, d ^ mask) for d in range(dev_count)])  41.6 us
    pallas_call x11, Pallas kernels, run(): pl.pallas_call(kernel, out_shape=tuple((jax.ShapeDtypeStruct(s, t) for s,...  24.8 us
    ppermute x41, waiting for transfers between devices, swap(): return lax.ppermute(value, 'ctx', [(d, d ^ mask) for d in range(dev_count)])  24.1 us
  transfers between devices with their start and end apart: 41, of which 15 were waited for; matrix products, arithmetic and copies ran while one was open for 2% of the time, Pallas kernels for 15%

profile of v12, /device:TPU:0, one launch (start us, length us, event | category | flops | bytes accessed | tf_op | source)
XLA Modules:
  0.0 95.7 jit_solution(2888174854328798534)
XLA Ops:
  0.7 5.6 %shard_map.147 = (bf16[256,768]{1,0:T(8,128)(2,1)}, bf16[256,768]{1,0:T(8,128)(2,1)}, bf16[256,768]{1,0:T(8,128)(2,1)}, bf16[256,768]{1,0:T(8,128)(2,1)}, bf16[6...) custom-call(s32[2,12]{1,0:T(2,128)} %offs_ref.9, ...), custom_call_target="tpu_custom_call" | custom-call | flops 1207959552 | bytes 7716960 | tf_op jit(solution)/shard_map/pallas_call | solution.py:535
  6.3 3.1 %collective-permute-start = (bf16[8,3072]{1,0:T(8,128)(2,1)}, bf16[8,3072]{1,0:T(8,128)(2,1)S(1)}, u32[]{:S(2)}, u32[]{:S(2)}) collective-permute-start(bf16[8,3072]{1,0:T(8,128)(2,1)} %get-tuple-element.106), channel_id=1, source_target_pairs={{0,8},{1,9},{2,10},{3,11},{4,12},{5,13},{6,14},{7,15},{8,0},{9,1},... | collective-permute-start | bytes 147464 | tf_op jit(solution)/shard_map/ppermute | solution.py:554
  9.3 2.6 %collective-permute-start.1 = (bf16[8,3072]{1,0:T(8,128)(2,1)}, bf16[8,3072]{1,0:T(8,128)(2,1)S(1)}, u32[]{:S(2)}, u32[]{:S(2)}) collective-permute-start(bf16[8,3072]{1,0:T(8,128)(2,1)} %get-tuple-element.106), channel_id=1, source_target_pairs={{0,16},{1,17},{2,18},{3,19},{4,20},{5,21},{6,22},{7,23},{8,24},{9,... | collective-permute-start | bytes 147464 | tf_op jit(solution)/shard_map/ppermute | solution.py:554
  11.9 1.7 %collective-permute-start.3 = (bf16[32,1536]{1,0:T(8,128)(2,1)}, bf16[32,1536]{1,0:T(8,128)(2,1)S(1)}, u32[]{:S(2)}, u32[]{:S(2)}) collective-permute-start(bf16[32,1536]{1,0:T(8,128)(2,1)} %get-tuple-element.70), channel_id=1, source_target_pairs={{0,2},{1,3},{2,0},{3,1},{4,6},{5,7},{6,4},{7,5},{8,10},{9,11},{10,... | collective-permute-start | bytes 294920 | tf_op jit(solution)/shard_map/ppermute | solution.py:554
  13.7 1.5 %collective-permute-start.4 = (bf16[32,1536]{1,0:T(8,128)(2,1)}, bf16[32,1536]{1,0:T(8,128)(2,1)S(1)}, u32[]{:S(2)}, u32[]{:S(2)}) collective-permute-start(bf16[32,1536]{1,0:T(8,128)(2,1)} %get-tuple-element.70), channel_id=1, source_target_pairs={{0,4},{1,5},{2,6},{3,7},{4,0},{5,1},{6,2},{7,3},{8,12},{9,13},{10,... | collective-permute-start | bytes 294920 | tf_op jit(solution)/shard_map/ppermute | solution.py:554
  15.4 0.7 copy-done.15
  17.2 0.8 collective-permute-done.2
  18.1 0.6 collective-permute-done.4
  18.7 0.9 collective-permute-start.7
  19.6 2.0 %collective-permute-start.8 = (bf16[32,1536]{1,0:T(8,128)(2,1)S(1)}, bf16[32,1536]{1,0:T(8,128)(2,1)S(1)}, u32[]{:S(2)}, u32[]{:S(2)}) collective-permute-start(bf16[32,1536]{1,0:T(8,128)(2,1)S(1)} %pad_maximum_fusion.1), channel_id=1, source_target_pairs={{0,4},{1,5},{2,6},{3,7},{4,0},{5,1},{6,2},{7,3},{8,12},{9,13},{10,... | collective-permute-start | bytes 294920 | tf_op jit(solution)/shard_map/ppermute | solution.py:554
  21.6 0.9 collective-permute-start.9
  22.8 2.6 %shard_map.148 = (f32[256,768]{1,0:T(8,128)S(1)}, f32[256,128]{1,0:T(8,128)S(1)}, bf16[768,256]{1,0:T(8,128)(2,1)S(1)}, bf16[768,256]{1,0:T(8,128)(2,1)S(1)}) custom-call(s32[1]{0:T(128)S(6)} %copy.42.pad_ref, bf16[256,768]{1,0:T(8,128)(2,1)S(1)} %copy-done.6, bf16[256,768]{1,0:T(8,128)(2,1)S(1)} %copy-done.7, bf16[256,768]{1,0:T(8,128)(2,1)S(1)} %copy-done.8, ...), custom_call_target="tpu_custom_call" | custom-call | flops 805306368 | bytes 3676164 | tf_op jit(solution)/shard_map/pallas_call | solution.py:535
  25.4 1.7 %collective-permute-done.9 = bf16[32,1536]{1,0:T(8,128)(2,1)S(1)} collective-permute-done((bf16[32,1536]{1,0:T(8,128)(2,1)S(1)}, bf16[32,1536]{1,0:T(8,128)(2,1)S(1)}, u32[]{:S(2)}, u32[]{:S(2)}) %collective-permute-start.9) | collective-permute-done | bytes 98336 | tf_op jit(solution)/shard_map/ppermute | solution.py:554
  27.2 1.7 %collective-permute-done.10.far_1 = bf16[128,1536]{1,0:T(8,128)(2,1)S(1)} collective-permute-done((bf16[128,1536]{1,0:T(8,128)(2,1)S(1)}, bf16[128,1536]{1,0:T(8,128)(2,1)S(1)}, u32[]{:S(2)}, u32[]{:S(2)}) %collective-permute-start.10) | collective-permute-done | bytes 393248 | tf_op jit(solution)/shard_map/ppermute | solution.py:554
  29.0 2.3 %shard_map.149 = (f32[256,128]{1,0:T(8,128)S(1)}, f32[64,128]{1,0:T(8,128)S(1)}, f32[64,128]{1,0:T(8,128)S(1)}, f32[64,768]{1,0:T(8,128)S(1)}) custom-call(s32[2,12]{1,0:T(2,128)S(1)} %copy-done.5, s32[1]{0:T(128)S(6)} %copy.42.pad_ref, bf16[64,3072]{1,0:T(8,128)(2,1)S(1)} %copy-done.1, bf16[128,1536]{1,0:T(8,128)(2,1)S(1)} %constant_dynamic-update-slice_fusion.mid_0, ...), custom_call_target="tpu_custom_call" | custom-call | flops 301989888 | bytes 2490468 | tf_op jit(solution)/shard_map/pallas_call | solution.py:535
  31.3 0.7 collective-permute-start.11
  32.0 1.8 %shard_map.150.dq_sel = f32[64,768]{1,0:T(8,128)S(1)} custom-call(s32[2,12]{1,0:T(2,128)S(1)} %copy-done.5, s32[1]{0:T(128)S(6)} %copy.42.pad_ref, bf16[64,3072]{1,0:T(8,128)(2,1)S(1)} %copy-done.1, bf16[128,1536]{1,0:T(8,128)(2,1)S(1)} %constant_dynamic-update-slice_fusion.mid_0, bf16[128,1536]{1,0:T(8,128)(2,1)S(1)} %collective-permute-done.6.mid_1, ...), custom_call_target="tpu_custom_call" | custom-call | flops 201326592 | bytes 2195556 | tf_op jit(solution)/shard_map/pallas_call | solution.py:535
  34.0 1.6 %collective-permute-start.17 = (bf16[64,1536]{1,0:T(8,128)(2,1)S(1)}, bf16[64,1536]{1,0:T(8,128)(2,1)S(1)}, u32[]{:S(2)}, u32[]{:S(2)}) collective-permute-start(bf16[64,1536]{1,0:T(8,128)(2,1)S(1)} %constant_dynamic-update-slice_fusion.14), channel_id=1, source_target_pairs={{0,2},{1,3},{2,0},{3,1},{4,6},{5,7},{6,4},{7,5},{8,10},{9,11},{10,... | collective-permute-start | bytes 589832 | tf_op jit(solution)/shard_map/ppermute | solution.py:554
  35.7 1.8 %collective-permute-start.19 = (bf16[64,1536]{1,0:T(8,128)(2,1)S(1)}, bf16[64,1536]{1,0:T(8,128)(2,1)S(1)}, u32[]{:S(2)}, u32[]{:S(2)}) collective-permute-start(bf16[64,1536]{1,0:T(8,128)(2,1)S(1)} %constant_dynamic-update-slice_fusion.14), channel_id=1, source_target_pairs={{0,6},{1,7},{2,4},{3,5},{4,2},{5,3},{6,0},{7,1},{8,14},{9,15},{10,... | collective-permute-start | bytes 589832 | tf_op jit(solution)/shard_map/ppermute | solution.py:554
  37.5 3.6 %collective-permute-start.12 = (f32[16,128]{1,0:T(8,128)S(1)}, f32[16,128]{1,0:T(8,128)S(1)}, u32[]{:S(2)}, u32[]{:S(2)}) collective-permute-start(f32[16,128]{1,0:T(8,128)S(1)} %constant_dynamic-update-slice_fusion.8), channel_id=1, source_target_pairs={{0,16},{1,17},{2,18},{3,19},{4,20},{5,21},{6,22},{7,23},{8,24},{9,... | collective-permute-start | bytes 24584 | tf_op jit(solution)/shard_map/ppermute | solution.py:554
  41.1 2.5 %shard_map.151 = (bf16[256,768]{1,0:T(8,128)(2,1)}, bf16[384,256]{1,0:T(8,128)(2,1)S(1)}, bf16[384,256]{1,0:T(8,128)(2,1)S(1)}) custom-call(s32[2,12]{1,0:T(2,128)S(1)} %copy-done.5, f32[256,128]{1,0:T(8,128)S(1)} %get-tuple-element.75.near_stats, f32[256,128]{1,0:T(8,128)S(1)} %get-tuple-element.82.stats, f32[64,128]{1,0:T(8,128)S(1)} %get-tuple-element.86.picked, ...), custom_call_target="tpu_custom_call" | custom-call | flops 905969664 | bytes 3673184 | tf_op jit(solution)/shard_map/pallas_call | solution.py:535
  44.2 0.9 collective-permute-done.14.left_other
  45.6 2.2 %collective-permute-done.13 = f32[32,256]{1,0:T(8,128)S(1)} collective-permute-done((f32[32,256]{1,0:T(8,128)S(1)}, f32[32,256]{1,0:T(8,128)S(1)}, u32[]{:S(2)}, u32[]{:S(2)}) %collective-permute-start.13) | collective-permute-done | bytes 32800 | tf_op jit(solution)/shard_map/ppermute | solution.py:554
  47.8 1.6 %collective-permute-start.21 = (f32[64,256]{1,0:T(8,128)S(1)}, f32[64,256]{1,0:T(8,128)S(1)}, u32[]{:S(2)}, u32[]{:S(2)}) collective-permute-start(f32[64,256]{1,0:T(8,128)S(1)} %constant_dynamic-update-slice_fusion.12), channel_id=1, source_target_pairs={{0,2},{1,3},{2,0},{3,1},{4,6},{5,7},{6,4},{7,5},{8,10},{9,11},{10,... | collective-permute-start | bytes 196616 | tf_op jit(solution)/shard_map/ppermute | solution.py:554
  49.9 4.1 %shard_map.153 = (bf16[256,768]{1,0:T(8,128)(2,1)S(1)}, f32[256,768]{1,0:T(8,128)S(1)}, f32[256,768]{1,0:T(8,128)S(1)}) custom-call(s32[2,12]{1,0:T(2,128)S(1)} %copy-done.5, s32[1]{0:T(128)S(6)} %copy.42.pad_ref, bf16[256,768]{1,0:T(8,128)(2,1)S(1)} %copy-done.6, bf16[256,768]{1,0:T(8,128)(2,1)S(1)} %copy-done.7, bf16[256,768]{1,0:T(8,128)(2,1)S(1)} %copy-done.8, ...), custom_call_target="tpu_custom_call" | custom-call | flops 805306368 | bytes 3866724 | tf_op jit(solution)/shard_map/pallas_call | solution.py:535
  55.4 2.6 %collective-permute-done.34 = bf16[192,768]{1,0:T(8,128)(2,1)S(1)} collective-permute-done((bf16[192,768]{1,0:T(8,128)(2,1)S(1)}, bf16[192,768]{1,0:T(8,128)(2,1)S(1)}, u32[]{:S(2)}, u32[]{:S(2)}) %collective-permute-start.34) | collective-permute-done | bytes 294944 | tf_op jit(solution)/shard_map/ppermute | solution.py:554
  58.4 2.4 %shard_map.155 = (bf16[256,768]{1,0:T(8,128)(2,1)S(1)}, bf16[256,768]{1,0:T(8,128)(2,1)S(1)}) custom-call(s32[2,12]{1,0:T(2,128)S(1)} %copy-done.5, s32[1]{0:T(128)S(6)} %copy.42.pad_ref, bf16[64,3072]{1,0:T(8,128)(2,1)S(1)} %copy-done.1, bf16[256,1536]{1,0:T(8,128)(2,1)S(1)} %constant_dynamic-update-slice_fusion.19.qg_0, ...), custom_call_target="tpu_custom_call" | custom-call | flops 15099494 | bytes 229381 | tf_op jit(solution)/shard_map/pallas_call | solution.py:535
  61.8 0.8 collective-permute-done.24.dk_other
  62.6 0.6 collective-permute-done.25.dv_other
  63.1 0.8 shard_map.156
  64.0 1.0 %collective-permute-start.27 = (bf16[96,1536]{1,0:T(8,128)(2,1)S(1)}, bf16[96,1536]{1,0:T(8,128)(2,1)S(1)}, u32[]{:S(2)}, u32[]{:S(2)}) collective-permute-start(bf16[96,1536]{1,0:T(8,128)(2,1)S(1)} %get-tuple-element.135), channel_id=1, source_target_pairs={{0,2},{1,3},{2,0},{3,1},{4,6},{5,7},{6,4},{7,5},{8,10},{9,11},{10,... | collective-permute-start | bytes 884744 | tf_op jit(solution)/shard_map/ppermute | solution.py:554
  65.4 1.2 %collective-permute-start.32 = (bf16[96,1536]{1,0:T(8,128)(2,1)S(1)}, bf16[96,1536]{1,0:T(8,128)(2,1)S(1)}, u32[]{:S(2)}, u32[]{:S(2)}) collective-permute-start(bf16[96,1536]{1,0:T(8,128)(2,1)S(1)} %get-tuple-element.133), channel_id=1, source_target_pairs={{0,4},{1,5},{2,6},{3,7},{4,0},{5,1},{6,2},{7,3},{8,12},{9,13},{10,... | collective-permute-start | bytes 884744 | tf_op jit(solution)/shard_map/ppermute | solution.py:554
  66.7 1.2 %collective-permute-start.33 = (bf16[96,1536]{1,0:T(8,128)(2,1)S(1)}, bf16[96,1536]{1,0:T(8,128)(2,1)S(1)}, u32[]{:S(2)}, u32[]{:S(2)}) collective-permute-start(bf16[96,1536]{1,0:T(8,128)(2,1)S(1)} %get-tuple-element.132), channel_id=1, source_target_pairs={{0,6},{1,7},{2,4},{3,5},{4,2},{5,3},{6,0},{7,1},{8,14},{9,15},{10,... | collective-permute-start | bytes 884744 | tf_op jit(solution)/shard_map/ppermute | solution.py:554
  67.9 1.9 %shard_map.157 = bf16[256,768]{1,0:T(8,128)(2,1)} custom-call(bf16[256,768]{1,0:T(8,128)(2,1)S(1)} %get-tuple-element.121.right.dq, bf16[256,768]{1,0:T(8,128)(2,1)S(1)} %get-tuple-element.119.dk, bf16[256,768]{1,0:T(8,128)(2,1)S(1)} %get-tuple-element.120.dv, bf16[768,2304]{1,0:T(8,128)(2,1)S(1)} %copy-done), custom_call_target="tpu_custom_call" | custom-call | flops 45298484 | bytes 255590 | tf_op jit(solution)/shard_map/pallas_call | solution.py:535
  69.8 4.2 %collective-permute-done.27 = bf16[96,1536]{1,0:T(8,128)(2,1)S(1)} collective-permute-done((bf16[96,1536]{1,0:T(8,128)(2,1)S(1)}, bf16[96,1536]{1,0:T(8,128)(2,1)S(1)}, u32[]{:S(2)}, u32[]{:S(2)}) %collective-permute-start.27) | collective-permute-done | bytes 294944 | tf_op jit(solution)/shard_map/ppermute | solution.py:554
  74.4 1.1 %collective-permute-start.28 = (bf16[48,768]{1,0:T(8,128)(2,1)S(1)}, bf16[48,768]{1,0:T(8,128)(2,1)S(1)}, u32[]{:S(2)}, u32[]{:S(2)}) collective-permute-start(bf16[48,768]{1,0:T(8,128)(2,1)S(1)} %get-tuple-element.143), channel_id=1, source_target_pairs={{0,2},{1,3},{2,0},{3,1},{4,6},{5,7},{6,4},{7,5},{8,10},{9,11},{10,... | collective-permute-start | bytes 221192 | tf_op jit(solution)/shard_map/ppermute | solution.py:554
  75.5 1.2 %collective-permute-start.29 = (bf16[48,768]{1,0:T(8,128)(2,1)S(1)}, bf16[48,768]{1,0:T(8,128)(2,1)S(1)}, u32[]{:S(2)}, u32[]{:S(2)}) collective-permute-start(bf16[48,768]{1,0:T(8,128)(2,1)S(1)} %get-tuple-element.145), channel_id=1, source_target_pairs={{0,4},{1,5},{2,6},{3,7},{4,0},{5,1},{6,2},{7,3},{8,12},{9,13},{10,... | collective-permute-start | bytes 221192 | tf_op jit(solution)/shard_map/ppermute | solution.py:554
  76.7 1.7 %collective-permute-done.36 = bf16[48,768]{1,0:T(8,128)(2,1)S(1)} collective-permute-done((bf16[48,768]{1,0:T(8,128)(2,1)S(1)}, bf16[48,768]{1,0:T(8,128)(2,1)S(1)}, u32[]{:S(2)}, u32[]{:S(2)}) %collective-permute-start.36) | collective-permute-done | bytes 73760 | tf_op jit(solution)/shard_map/ppermute | solution.py:554
  78.4 0.8 collective-permute-start.30
  79.3 2.6 %collective-permute-done.28 = bf16[48,768]{1,0:T(8,128)(2,1)S(1)} collective-permute-done((bf16[48,768]{1,0:T(8,128)(2,1)S(1)}, bf16[48,768]{1,0:T(8,128)(2,1)S(1)}, u32[]{:S(2)}, u32[]{:S(2)}) %collective-permute-start.28) | collective-permute-done | bytes 73760 | tf_op jit(solution)/shard_map/ppermute | solution.py:554
  81.9 2.2 %collective-permute-start.40 = (bf16[24,768]{1,0:T(8,128)(2,1)S(1)}, bf16[24,768]{1,0:T(8,128)(2,1)S(1)}, u32[]{:S(2)}, u32[]{:S(2)}) collective-permute-start(bf16[24,768]{1,0:T(8,128)(2,1)S(1)} %slice.194), channel_id=1, source_target_pairs={{0,16},{1,17},{2,18},{3,19},{4,20},{5,21},{6,22},{7,23},{8,24},{9,... | collective-permute-start | bytes 110600 | tf_op jit(solution)/shard_map/ppermute | solution.py:554
  84.1 1.9 %collective-permute-start.31 = (bf16[24,768]{1,0:T(8,128)(2,1)S(1)}, bf16[24,768]{1,0:T(8,128)(2,1)S(1)}, u32[]{:S(2)}, u32[]{:S(2)}) collective-permute-start(bf16[24,768]{1,0:T(8,128)(2,1)S(1)} %slice.179), channel_id=1, source_target_pairs={{0,16},{1,17},{2,18},{3,19},{4,20},{5,21},{6,22},{7,23},{8,24},{9,... | collective-permute-start | bytes 110600 | tf_op jit(solution)/shard_map/ppermute | solution.py:554
  86.2 1.6 %collective-permute-start.37 = (bf16[24,1536]{1,0:T(8,128)(2,1)S(1)}, bf16[24,1536]{1,0:T(8,128)(2,1)S(1)}, u32[]{:S(2)}, u32[]{:S(2)}) collective-permute-start(bf16[24,1536]{1,0:T(8,128)(2,1)S(1)} %get-tuple-element.146), channel_id=1, source_target_pairs={{0,8},{1,9},{2,10},{3,11},{4,12},{5,13},{6,14},{7,15},{8,0},{9,1},... | collective-permute-start | bytes 221192 | tf_op jit(solution)/shard_map/ppermute | solution.py:554
  87.8 0.6 collective-permute-start.38
  88.5 2.2 %collective-permute-start.39 = (bf16[24,1536]{1,0:T(8,128)(2,1)S(1)}, bf16[24,1536]{1,0:T(8,128)(2,1)S(1)}, u32[]{:S(2)}, u32[]{:S(2)}) collective-permute-start(bf16[24,1536]{1,0:T(8,128)(2,1)S(1)} %get-tuple-element.147), channel_id=1, source_target_pairs={{0,24},{1,25},{2,26},{3,27},{4,28},{5,29},{6,30},{7,31},{8,16},{9,... | collective-permute-start | bytes 221192 | tf_op jit(solution)/shard_map/ppermute | solution.py:554
  90.6 0.6 convert_add_fusion.1
  91.7 3.2 %collective-permute-done.38 = bf16[24,1536]{1,0:T(8,128)(2,1)S(1)} collective-permute-done((bf16[24,1536]{1,0:T(8,128)(2,1)S(1)}, bf16[24,1536]{1,0:T(8,128)(2,1)S(1)}, u32[]{:S(2)}, u32[]{:S(2)}) %collective-permute-start.38) | collective-permute-done | bytes 73760 | tf_op jit(solution)/shard_map/ppermute | solution.py:554
  95.0 0.7 pad_maximum_fusion
  (138 shorter events, 7.1 us)
Async XLA Ops:
  0.6 14.5 %copy-start.10 = (s32[768,1]{1,0:T(8,128)S(1)}, s32[768,1]{1,0:T(8,128)}, u32[]{:S(2)}) copy-start(s32[768,1]{1,0:T(8,128)} %constant.14.clone) | copy-start | bytes 9220
  0.6 14.5 %copy-start.11 = (s32[768,1]{1,0:T(8,128)S(1)}, s32[768,1]{1,0:T(8,128)}, u32[]{:S(2)}) copy-start(s32[768,1]{1,0:T(8,128)} %constant.15.clone) | copy-start | bytes 9220
  0.7 14.5 %copy-start.12 = (s32[768,1]{1,0:T(8,128)S(1)}, s32[768,1]{1,0:T(8,128)}, u32[]{:S(2)}) copy-start(s32[768,1]{1,0:T(8,128)} %constant.16.clone) | copy-start | bytes 9220
  0.7 14.5 %copy-start.13 = (s32[768,1]{1,0:T(8,128)S(1)}, s32[768,1]{1,0:T(8,128)}, u32[]{:S(2)}) copy-start(s32[768,1]{1,0:T(8,128)} %constant.17.clone) | copy-start | bytes 9220
  6.3 10.6 %collective-permute-start = (bf16[8,3072]{1,0:T(8,128)(2,1)}, bf16[8,3072]{1,0:T(8,128)(2,1)S(1)}, u32[]{:S(2)}, u32[]{:S(2)}) collective-permute-start(bf16[8,3072]{1,0:T(8,128)(2,1)} %get-tuple-element.106), channel_id=1, source_target_pairs={{0,8},{1,9},{2,10},{3,11},{4,12},{5,13},{6,14},{7,15},{8,0},{9,1},... | collective-permute-start | bytes 147464 | tf_op jit(solution)/shard_map/ppermute | solution.py:554
  9.3 7.9 %collective-permute-start.1 = (bf16[8,3072]{1,0:T(8,128)(2,1)}, bf16[8,3072]{1,0:T(8,128)(2,1)S(1)}, u32[]{:S(2)}, u32[]{:S(2)}) collective-permute-start(bf16[8,3072]{1,0:T(8,128)(2,1)} %get-tuple-element.106), channel_id=1, source_target_pairs={{0,16},{1,17},{2,18},{3,19},{4,20},{5,21},{6,22},{7,23},{8,24},{9,... | collective-permute-start | bytes 147464 | tf_op jit(solution)/shard_map/ppermute | solution.py:554
  11.9 6.1 %collective-permute-start.2 = (bf16[8,3072]{1,0:T(8,128)(2,1)}, bf16[8,3072]{1,0:T(8,128)(2,1)S(1)}, u32[]{:S(2)}, u32[]{:S(2)}) collective-permute-start(bf16[8,3072]{1,0:T(8,128)(2,1)} %get-tuple-element.106), channel_id=1, source_target_pairs={{0,24},{1,25},{2,26},{3,27},{4,28},{5,29},{6,30},{7,31},{8,16},{9,... | collective-permute-start | bytes 147464 | tf_op jit(solution)/shard_map/ppermute | solution.py:554
  11.9 6.1 %collective-permute-start.3 = (bf16[32,1536]{1,0:T(8,128)(2,1)}, bf16[32,1536]{1,0:T(8,128)(2,1)S(1)}, u32[]{:S(2)}, u32[]{:S(2)}) collective-permute-start(bf16[32,1536]{1,0:T(8,128)(2,1)} %get-tuple-element.70), channel_id=1, source_target_pairs={{0,2},{1,3},{2,0},{3,1},{4,6},{5,7},{6,4},{7,5},{8,10},{9,11},{10,... | collective-permute-start | bytes 294920 | tf_op jit(solution)/shard_map/ppermute | solution.py:554
  13.7 5.1 %collective-permute-start.4 = (bf16[32,1536]{1,0:T(8,128)(2,1)}, bf16[32,1536]{1,0:T(8,128)(2,1)S(1)}, u32[]{:S(2)}, u32[]{:S(2)}) collective-permute-start(bf16[32,1536]{1,0:T(8,128)(2,1)} %get-tuple-element.70), channel_id=1, source_target_pairs={{0,4},{1,5},{2,6},{3,7},{4,0},{5,1},{6,2},{7,3},{8,12},{9,13},{10,... | collective-permute-start | bytes 294920 | tf_op jit(solution)/shard_map/ppermute | solution.py:554
  15.2 7.5 %copy-start.8 = (bf16[256,768]{1,0:T(8,128)(2,1)S(1)}, bf16[256,768]{1,0:T(8,128)(2,1)}, u32[]{:S(2)}) copy-start(bf16[256,768]{1,0:T(8,128)(2,1)} %get-tuple-element.73.v) | copy-start | bytes 1179652
  15.2 7.5 %copy-start.9 = (bf16[256,768]{1,0:T(8,128)(2,1)S(1)}, bf16[256,768]{1,0:T(8,128)(2,1)}, u32[]{:S(2)}) copy-start(bf16[256,768]{1,0:T(8,128)(2,1)} %get-tuple-element.74.g) | copy-start | bytes 1179652
  16.9 5.7 %collective-permute-start.5 = (bf16[32,1536]{1,0:T(8,128)(2,1)S(1)}, bf16[32,1536]{1,0:T(8,128)(2,1)S(1)}, u32[]{:S(2)}, u32[]{:S(2)}) collective-permute-start(bf16[32,1536]{1,0:T(8,128)(2,1)S(1)} %copy-done.15), channel_id=1, source_target_pairs={{0,6},{1,7},{2,4},{3,5},{4,2},{5,3},{6,0},{7,1},{8,14},{9,15},{10,... | collective-permute-start | bytes 294920 | tf_op jit(solution)/shard_map/ppermute | solution.py:554
  18.7 6.6 %collective-permute-start.7 = (bf16[32,1536]{1,0:T(8,128)(2,1)S(1)}, bf16[32,1536]{1,0:T(8,128)(2,1)S(1)}, u32[]{:S(2)}, u32[]{:S(2)}) collective-permute-start(bf16[32,1536]{1,0:T(8,128)(2,1)S(1)} %pad_maximum_fusion.1), channel_id=1, source_target_pairs={{0,2},{1,3},{2,0},{3,1},{4,6},{5,7},{6,4},{7,5},{8,10},{9,11},{10,... | collective-permute-start | bytes 294920 | tf_op jit(solution)/shard_map/ppermute | solution.py:554
  19.6 5.7 %collective-permute-start.8 = (bf16[32,1536]{1,0:T(8,128)(2,1)S(1)}, bf16[32,1536]{1,0:T(8,128)(2,1)S(1)}, u32[]{:S(2)}, u32[]{:S(2)}) collective-permute-start(bf16[32,1536]{1,0:T(8,128)(2,1)S(1)} %pad_maximum_fusion.1), channel_id=1, source_target_pairs={{0,4},{1,5},{2,6},{3,7},{4,0},{5,1},{6,2},{7,3},{8,12},{9,13},{10,... | collective-permute-start | bytes 294920 | tf_op jit(solution)/shard_map/ppermute | solution.py:554
  21.6 5.5 %collective-permute-start.9 = (bf16[32,1536]{1,0:T(8,128)(2,1)S(1)}, bf16[32,1536]{1,0:T(8,128)(2,1)S(1)}, u32[]{:S(2)}, u32[]{:S(2)}) collective-permute-start(bf16[32,1536]{1,0:T(8,128)(2,1)S(1)} %pad_maximum_fusion.1), channel_id=1, source_target_pairs={{0,6},{1,7},{2,4},{3,5},{4,2},{5,3},{6,0},{7,1},{8,14},{9,15},{10,... | collective-permute-start | bytes 294920 | tf_op jit(solution)/shard_map/ppermute | solution.py:554
  22.6 4.6 %collective-permute-start.6 = (bf16[128,1536]{1,0:T(8,128)(2,1)S(1)}, bf16[128,1536]{1,0:T(8,128)(2,1)S(1)}, u32[]{:S(2)}, u32[]{:S(2)}) collective-permute-start(bf16[128,1536]{1,0:T(8,128)(2,1)S(1)} %constant_dynamic-update-slice_fusion.mid_0), channel_id=1, source_target_pairs={{0,1},{1,0},{2,3},{3,2},{4,5},{5,4},{6,7},{7,6},{8,9},{9,8},{10,11... | collective-permute-start | bytes 1179656 | tf_op jit(solution)/shard_map/ppermute | solution.py:554
  27.2 1.8 %collective-permute-start.10 = (bf16[128,1536]{1,0:T(8,128)(2,1)S(1)}, bf16[128,1536]{1,0:T(8,128)(2,1)S(1)}, u32[]{:S(2)}, u32[]{:S(2)}) collective-permute-start(bf16[128,1536]{1,0:T(8,128)(2,1)S(1)} %constant_dynamic-update-slice_fusion.4.far_0), channel_id=1, source_target_pairs={{0,1},{1,0},{2,3},{3,2},{4,5},{5,4},{6,7},{7,6},{8,9},{9,8},{10,11... | collective-permute-start | bytes 1179656 | tf_op jit(solution)/shard_map/ppermute | solution.py:554
  31.3 9.9 %copy-start.2 = (bf16[768,768]{1,0:T(8,128)(2,1)S(1)}, bf16[768,768]{1,0:T(8,128)(2,1)}, u32[]{:S(2)}) copy-start(bf16[768,768]{1,0:T(8,128)(2,1)} %w_out.1) | copy-start | bytes 3538948
  31.3 6.2 %collective-permute-start.11 = (f32[8,128]{1,0:T(8,128)S(1)}, f32[8,128]{1,0:T(8,128)S(1)}, u32[]{:S(2)}, u32[]{:S(2)}) collective-permute-start(f32[8,128]{1,0:T(8,128)S(1)} %slice.130), channel_id=1, source_target_pairs={{0,8},{1,9},{2,10},{3,11},{4,12},{5,13},{6,14},{7,15},{8,0},{9,1},... | collective-permute-start | bytes 12296 | tf_op jit(solution)/shard_map/ppermute | solution.py:554
  34.0 20.0 %collective-permute-start.17 = (bf16[64,1536]{1,0:T(8,128)(2,1)S(1)}, bf16[64,1536]{1,0:T(8,128)(2,1)S(1)}, u32[]{:S(2)}, u32[]{:S(2)}) collective-permute-start(bf16[64,1536]{1,0:T(8,128)(2,1)S(1)} %constant_dynamic-update-slice_fusion.14), channel_id=1, source_target_pairs={{0,2},{1,3},{2,0},{3,1},{4,6},{5,7},{6,4},{7,5},{8,10},{9,11},{10,... | collective-permute-start | bytes 589832 | tf_op jit(solution)/shard_map/ppermute | solution.py:554
  35.5 18.5 %collective-permute-start.18 = (bf16[64,1536]{1,0:T(8,128)(2,1)S(1)}, bf16[64,1536]{1,0:T(8,128)(2,1)S(1)}, u32[]{:S(2)}, u32[]{:S(2)}) collective-permute-start(bf16[64,1536]{1,0:T(8,128)(2,1)S(1)} %constant_dynamic-update-slice_fusion.14), channel_id=1, source_target_pairs={{0,4},{1,5},{2,6},{3,7},{4,0},{5,1},{6,2},{7,3},{8,12},{9,13},{10,... | collective-permute-start | bytes 589832 | tf_op jit(solution)/shard_map/ppermute | solution.py:554
  35.7 18.9 %collective-permute-start.19 = (bf16[64,1536]{1,0:T(8,128)(2,1)S(1)}, bf16[64,1536]{1,0:T(8,128)(2,1)S(1)}, u32[]{:S(2)}, u32[]{:S(2)}) collective-permute-start(bf16[64,1536]{1,0:T(8,128)(2,1)S(1)} %constant_dynamic-update-slice_fusion.14), channel_id=1, source_target_pairs={{0,6},{1,7},{2,4},{3,5},{4,2},{5,3},{6,0},{7,1},{8,14},{9,15},{10,... | collective-permute-start | bytes 589832 | tf_op jit(solution)/shard_map/ppermute | solution.py:554
  37.5 6.3 %collective-permute-start.15 = (bf16[256,768]{1,0:T(8,128)(2,1)S(1)}, bf16[256,768]{1,0:T(8,128)(2,1)S(1)}, u32[]{:S(2)}, u32[]{:S(2)}) collective-permute-start(bf16[256,768]{1,0:T(8,128)(2,1)S(1)} %copy-done.4), channel_id=1, source_target_pairs={{0,1},{1,0},{2,3},{3,2},{4,5},{5,4},{6,7},{7,6},{8,9},{9,8},{10,11... | collective-permute-start | bytes 1179656 | tf_op jit(solution)/shard_map/ppermute | solution.py:554
  37.5 6.1 %collective-permute-start.12 = (f32[16,128]{1,0:T(8,128)S(1)}, f32[16,128]{1,0:T(8,128)S(1)}, u32[]{:S(2)}, u32[]{:S(2)}) collective-permute-start(f32[16,128]{1,0:T(8,128)S(1)} %constant_dynamic-update-slice_fusion.8), channel_id=1, source_target_pairs={{0,16},{1,17},{2,18},{3,19},{4,20},{5,21},{6,22},{7,23},{8,24},{9,... | collective-permute-start | bytes 24584 | tf_op jit(solution)/shard_map/ppermute | solution.py:554
  43.6 1.4 %collective-permute-start.14 = (bf16[384,256]{1,0:T(8,128)(2,1)S(1)}, bf16[384,256]{1,0:T(8,128)(2,1)S(1)}, u32[]{:S(2)}, u32[]{:S(2)}) collective-permute-start(bf16[384,256]{1,0:T(8,128)(2,1)S(1)} %get-tuple-element.94), channel_id=1, source_target_pairs={{0,1},{1,0},{2,3},{3,2},{4,5},{5,4},{6,7},{7,6},{8,9},{9,8},{10,11... | collective-permute-start | bytes 589832 | tf_op jit(solution)/shard_map/ppermute | solution.py:554
  43.8 4.0 %collective-permute-start.13 = (f32[32,256]{1,0:T(8,128)S(1)}, f32[32,256]{1,0:T(8,128)S(1)}, u32[]{:S(2)}, u32[]{:S(2)}) collective-permute-start(f32[32,256]{1,0:T(8,128)S(1)} %pad_maximum_fusion.2), channel_id=1, source_target_pairs={{0,4},{1,5},{2,6},{3,7},{4,0},{5,1},{6,2},{7,3},{8,12},{9,13},{10,... | collective-permute-start | bytes 98312 | tf_op jit(solution)/shard_map/ppermute | solution.py:554
  47.8 7.0 %collective-permute-start.21 = (f32[64,256]{1,0:T(8,128)S(1)}, f32[64,256]{1,0:T(8,128)S(1)}, u32[]{:S(2)}, u32[]{:S(2)}) collective-permute-start(f32[64,256]{1,0:T(8,128)S(1)} %constant_dynamic-update-slice_fusion.12), channel_id=1, source_target_pairs={{0,2},{1,3},{2,0},{3,1},{4,6},{5,7},{6,4},{7,5},{8,10},{9,11},{10,... | collective-permute-start | bytes 196616 | tf_op jit(solution)/shard_map/ppermute | solution.py:554
  49.4 8.6 %collective-permute-start.34 = (bf16[192,768]{1,0:T(8,128)(2,1)S(1)}, bf16[192,768]{1,0:T(8,128)(2,1)S(1)}, u32[]{:S(2)}, u32[]{:S(2)}) collective-permute-start(bf16[192,768]{1,0:T(8,128)(2,1)S(1)} %get-tuple-element.138), channel_id=1, source_target_pairs={{0,2},{1,3},{2,0},{3,1},{4,6},{5,7},{6,4},{7,5},{8,10},{9,11},{10,... | collective-permute-start | bytes 884744 | tf_op jit(solution)/shard_map/ppermute | solution.py:554
  54.0 4.0 %collective-permute-start.16 = (bf16[768,256]{1,0:T(8,128)(2,1)S(1)}, bf16[768,256]{1,0:T(8,128)(2,1)S(1)}, u32[]{:S(2)}, u32[]{:S(2)}) collective-permute-start(bf16[768,256]{1,0:T(8,128)(2,1)S(1)} %get-tuple-element.103), channel_id=1, source_target_pairs={{0,1},{1,0},{2,3},{3,2},{4,5},{5,4},{6,7},{7,6},{8,9},{9,8},{10,11... | collective-permute-start | bytes 1179656 | tf_op jit(solution)/shard_map/ppermute | solution.py:554
  54.1 3.9 %collective-permute-start.23 = (bf16[256,768]{1,0:T(8,128)(2,1)S(1)}, bf16[256,768]{1,0:T(8,128)(2,1)S(1)}, u32[]{:S(2)}, u32[]{:S(2)}) collective-permute-start(bf16[256,768]{1,0:T(8,128)(2,1)S(1)} %get-tuple-element.121.right.dq), channel_id=1, source_target_pairs={{0,1},{1,0},{2,3},{3,2},{4,5},{5,4},{6,7},{7,6},{8,9},{9,8},{10,11... | collective-permute-start | bytes 1179656 | tf_op jit(solution)/shard_map/ppermute | solution.py:554
  54.6 3.8 %collective-permute-start.20 = (bf16[256,1536]{1,0:T(8,128)(2,1)S(1)}, bf16[256,1536]{1,0:T(8,128)(2,1)S(1)}, u32[]{:S(2)}, u32[]{:S(2)}) collective-permute-start(bf16[256,1536]{1,0:T(8,128)(2,1)S(1)} %constant_dynamic-update-slice_fusion.19.qg_0), channel_id=1, source_target_pairs={{0,1},{1,0},{2,3},{3,2},{4,5},{5,4},{6,7},{7,6},{8,9},{9,8},{10,11... | collective-permute-start | bytes 2359304 | tf_op jit(solution)/shard_map/ppermute | solution.py:554
  54.9 3.5 %collective-permute-start.22 = (f32[256,128]{1,0:T(8,128)S(1)}, f32[256,128]{1,0:T(8,128)S(1)}, u32[]{:S(2)}, u32[]{:S(2)}) collective-permute-start(f32[256,128]{1,0:T(8,128)S(1)} %constant_dynamic-update-slice_fusion.23.stats_0), channel_id=1, source_target_pairs={{0,1},{1,0},{2,3},{3,2},{4,5},{5,4},{6,7},{7,6},{8,9},{9,8},{10,11... | collective-permute-start | bytes 393224 | tf_op jit(solution)/shard_map/ppermute | solution.py:554
  60.8 1.8 %collective-permute-start.24 = (bf16[256,768]{1,0:T(8,128)(2,1)S(1)}, bf16[256,768]{1,0:T(8,128)(2,1)S(1)}, u32[]{:S(2)}, u32[]{:S(2)}) collective-permute-start(bf16[256,768]{1,0:T(8,128)(2,1)S(1)} %get-tuple-element.119.dk), channel_id=1, source_target_pairs={{0,1},{1,0},{2,3},{3,2},{4,5},{5,4},{6,7},{7,6},{8,9},{9,8},{10,11... | collective-permute-start | bytes 1179656 | tf_op jit(solution)/shard_map/ppermute | solution.py:554
  60.9 2.3 %collective-permute-start.25 = (bf16[256,768]{1,0:T(8,128)(2,1)S(1)}, bf16[256,768]{1,0:T(8,128)(2,1)S(1)}, u32[]{:S(2)}, u32[]{:S(2)}) collective-permute-start(bf16[256,768]{1,0:T(8,128)(2,1)S(1)} %get-tuple-element.120.dv), channel_id=1, source_target_pairs={{0,1},{1,0},{2,3},{3,2},{4,5},{5,4},{6,7},{7,6},{8,9},{9,8},{10,11... | collective-permute-start | bytes 1179656 | tf_op jit(solution)/shard_map/ppermute | solution.py:554
  61.5 8.3 %collective-permute-start.35 = (bf16[96,768]{1,0:T(8,128)(2,1)S(1)}, bf16[96,768]{1,0:T(8,128)(2,1)S(1)}, u32[]{:S(2)}, u32[]{:S(2)}) collective-permute-start(bf16[96,768]{1,0:T(8,128)(2,1)S(1)} %get-tuple-element.149), channel_id=1, source_target_pairs={{0,4},{1,5},{2,6},{3,7},{4,0},{5,1},{6,2},{7,3},{8,12},{9,13},{10,... | collective-permute-start | bytes 442376 | tf_op jit(solution)/shard_map/ppermute | solution.py:554
  64.0 9.9 %collective-permute-start.27 = (bf16[96,1536]{1,0:T(8,128)(2,1)S(1)}, bf16[96,1536]{1,0:T(8,128)(2,1)S(1)}, u32[]{:S(2)}, u32[]{:S(2)}) collective-permute-start(bf16[96,1536]{1,0:T(8,128)(2,1)S(1)} %get-tuple-element.135), channel_id=1, source_target_pairs={{0,2},{1,3},{2,0},{3,1},{4,6},{5,7},{6,4},{7,5},{8,10},{9,11},{10,... | collective-permute-start | bytes 884744 | tf_op jit(solution)/shard_map/ppermute | solution.py:554
  65.1 9.2 %collective-permute-start.26 = (bf16[192,768]{1,0:T(8,128)(2,1)S(1)}, bf16[192,768]{1,0:T(8,128)(2,1)S(1)}, u32[]{:S(2)}, u32[]{:S(2)}) collective-permute-start(bf16[192,768]{1,0:T(8,128)(2,1)S(1)} %get-tuple-element.136), channel_id=1, source_target_pairs={{0,8},{1,9},{2,10},{3,11},{4,12},{5,13},{6,14},{7,15},{8,0},{9,1},... | collective-permute-start | bytes 884744 | tf_op jit(solution)/shard_map/ppermute | solution.py:554
  65.4 20.6 %collective-permute-start.32 = (bf16[96,1536]{1,0:T(8,128)(2,1)S(1)}, bf16[96,1536]{1,0:T(8,128)(2,1)S(1)}, u32[]{:S(2)}, u32[]{:S(2)}) collective-permute-start(bf16[96,1536]{1,0:T(8,128)(2,1)S(1)} %get-tuple-element.133), channel_id=1, source_target_pairs={{0,4},{1,5},{2,6},{3,7},{4,0},{5,1},{6,2},{7,3},{8,12},{9,13},{10,... | collective-permute-start | bytes 884744 | tf_op jit(solution)/shard_map/ppermute | solution.py:554
  66.7 19.3 %collective-permute-start.33 = (bf16[96,1536]{1,0:T(8,128)(2,1)S(1)}, bf16[96,1536]{1,0:T(8,128)(2,1)S(1)}, u32[]{:S(2)}, u32[]{:S(2)}) collective-permute-start(bf16[96,1536]{1,0:T(8,128)(2,1)S(1)} %get-tuple-element.132), channel_id=1, source_target_pairs={{0,6},{1,7},{2,4},{3,5},{4,2},{5,3},{6,0},{7,1},{8,14},{9,15},{10,... | collective-permute-start | bytes 884744 | tf_op jit(solution)/shard_map/ppermute | solution.py:554
  74.0 4.4 %collective-permute-start.36 = (bf16[48,768]{1,0:T(8,128)(2,1)S(1)}, bf16[48,768]{1,0:T(8,128)(2,1)S(1)}, u32[]{:S(2)}, u32[]{:S(2)}) collective-permute-start(bf16[48,768]{1,0:T(8,128)(2,1)S(1)} %slice.188), channel_id=1, source_target_pairs={{0,8},{1,9},{2,10},{3,11},{4,12},{5,13},{6,14},{7,15},{8,0},{9,1},... | collective-permute-start | bytes 221192 | tf_op jit(solution)/shard_map/ppermute | solution.py:554
  74.4 7.5 %collective-permute-start.28 = (bf16[48,768]{1,0:T(8,128)(2,1)S(1)}, bf16[48,768]{1,0:T(8,128)(2,1)S(1)}, u32[]{:S(2)}, u32[]{:S(2)}) collective-permute-start(bf16[48,768]{1,0:T(8,128)(2,1)S(1)} %get-tuple-element.143), channel_id=1, source_target_pairs={{0,2},{1,3},{2,0},{3,1},{4,6},{5,7},{6,4},{7,5},{8,10},{9,11},{10,... | collective-permute-start | bytes 221192 | tf_op jit(solution)/shard_map/ppermute | solution.py:554
  75.5 8.6 %collective-permute-start.29 = (bf16[48,768]{1,0:T(8,128)(2,1)S(1)}, bf16[48,768]{1,0:T(8,128)(2,1)S(1)}, u32[]{:S(2)}, u32[]{:S(2)}) collective-permute-start(bf16[48,768]{1,0:T(8,128)(2,1)S(1)} %get-tuple-element.145), channel_id=1, source_target_pairs={{0,4},{1,5},{2,6},{3,7},{4,0},{5,1},{6,2},{7,3},{8,12},{9,13},{10,... | collective-permute-start | bytes 221192 | tf_op jit(solution)/shard_map/ppermute | solution.py:554
  78.4 5.7 %collective-permute-start.30 = (bf16[48,768]{1,0:T(8,128)(2,1)S(1)}, bf16[48,768]{1,0:T(8,128)(2,1)S(1)}, u32[]{:S(2)}, u32[]{:S(2)}) collective-permute-start(bf16[48,768]{1,0:T(8,128)(2,1)S(1)} %get-tuple-element.144), channel_id=1, source_target_pairs={{0,6},{1,7},{2,4},{3,5},{4,2},{5,3},{6,0},{7,1},{8,14},{9,15},{10,... | collective-permute-start | bytes 221192 | tf_op jit(solution)/shard_map/ppermute | solution.py:554
  81.9 8.8 %collective-permute-start.40 = (bf16[24,768]{1,0:T(8,128)(2,1)S(1)}, bf16[24,768]{1,0:T(8,128)(2,1)S(1)}, u32[]{:S(2)}, u32[]{:S(2)}) collective-permute-start(bf16[24,768]{1,0:T(8,128)(2,1)S(1)} %slice.194), channel_id=1, source_target_pairs={{0,16},{1,17},{2,18},{3,19},{4,20},{5,21},{6,22},{7,23},{8,24},{9,... | collective-permute-start | bytes 110600 | tf_op jit(solution)/shard_map/ppermute | solution.py:554
  84.1 7.1 %collective-permute-start.31 = (bf16[24,768]{1,0:T(8,128)(2,1)S(1)}, bf16[24,768]{1,0:T(8,128)(2,1)S(1)}, u32[]{:S(2)}, u32[]{:S(2)}) collective-permute-start(bf16[24,768]{1,0:T(8,128)(2,1)S(1)} %slice.179), channel_id=1, source_target_pairs={{0,16},{1,17},{2,18},{3,19},{4,20},{5,21},{6,22},{7,23},{8,24},{9,... | collective-permute-start | bytes 110600 | tf_op jit(solution)/shard_map/ppermute | solution.py:554
  86.2 5.5 %collective-permute-start.37 = (bf16[24,1536]{1,0:T(8,128)(2,1)S(1)}, bf16[24,1536]{1,0:T(8,128)(2,1)S(1)}, u32[]{:S(2)}, u32[]{:S(2)}) collective-permute-start(bf16[24,1536]{1,0:T(8,128)(2,1)S(1)} %get-tuple-element.146), channel_id=1, source_target_pairs={{0,8},{1,9},{2,10},{3,11},{4,12},{5,13},{6,14},{7,15},{8,0},{9,1},... | collective-permute-start | bytes 221192 | tf_op jit(solution)/shard_map/ppermute | solution.py:554
  87.8 7.1 %collective-permute-start.38 = (bf16[24,1536]{1,0:T(8,128)(2,1)S(1)}, bf16[24,1536]{1,0:T(8,128)(2,1)S(1)}, u32[]{:S(2)}, u32[]{:S(2)}) collective-permute-start(bf16[24,1536]{1,0:T(8,128)(2,1)S(1)} %get-tuple-element.148), channel_id=1, source_target_pairs={{0,16},{1,17},{2,18},{3,19},{4,20},{5,21},{6,22},{7,23},{8,24},{9,... | collective-permute-start | bytes 221192 | tf_op jit(solution)/shard_map/ppermute | solution.py:554
  88.5 6.5 %collective-permute-start.39 = (bf16[24,1536]{1,0:T(8,128)(2,1)S(1)}, bf16[24,1536]{1,0:T(8,128)(2,1)S(1)}, u32[]{:S(2)}, u32[]{:S(2)}) collective-permute-start(bf16[24,1536]{1,0:T(8,128)(2,1)S(1)} %get-tuple-element.147), channel_id=1, source_target_pairs={{0,24},{1,25},{2,26},{3,27},{4,28},{5,29},{6,30},{7,31},{8,16},{9,... | collective-permute-start | bytes 221192 | tf_op jit(solution)/shard_map/ppermute | solution.py:554
  (10 other events, 47.0 us)

commit v13 on v12

--- a/solution.py
+++ b/solution.py
@@ -761,10 +761,10 @@
     late_parts = block_parts(late_half, PLANE, n)
     early = halved(early_half, masks[:-1], n, ((late_parts[1],),)).astype(BF)
     early = sum_parts(block_parts(early, PLANE, n), BF)
-    early = halved(early, masks[-1:], n)
     wout = halved(wout_half, [2, 4] + masks[:-1], n, ((dk_near,), (late_parts[1],))).astype(BF)
-    late = sum_parts(tied(late_parts, (wout,)), BF)
-    grad_wout = halved(wout, masks[-1:], n)
+    late = sum_parts(late_parts, BF)
+    early = halved(after(early, late), masks[-1:], n)
+    grad_wout = halved(after(wout, late), masks[-1:], n)
     late = reduce_all(late, upper_steps(n)[::-1], n)
     grad_wqkv = jnp.concatenate([early, late], axis=1)
     return out_rows, grad_tiles, grad_wqkv, grad_wout

time: 95.8 us -> 96.1 us (level)
  waiting for transfers between devices: 24.1 us -> 25.9 us
  starting transfers between devices: 41.6 us -> 40.1 us
    ppermute x41, waiting for transfers between devices: 24.1 us -> 25.9 us  [swap(): return lax.ppermute(value, 'ctx', [(d, d ^ mask) for d in range(dev_count)])]
    ppermute x41, starting transfers between devices: 41.6 us -> 40.1 us  [swap(): return lax.ppermute(value, 'ctx', [(d, d ^ mask) for d in range(dev_count)])]
where the time goes in v13:
time: 96.1 us; the launch traced here: 96 us
  starting transfers between devices  40.1 us (42%)
  waiting for transfers between devices  25.9 us (27%)
  Pallas kernels  24.8 us (26%)
  between operations  2.07 us (2%)
  other arithmetic  1.92 us (2%)
  local copies, waits for them, and re-layouts  1.25 us (1%)
    ppermute x41, starting transfers between devices, swap(): return lax.ppermute(value, 'ctx', [(d, d ^ mask) for d in range(dev_count)])  40.1 us
    ppermute x41, waiting for transfers between devices, swap(): return lax.ppermute(value, 'ctx', [(d, d ^ mask) for d in range(dev_count)])  25.9 us
    pallas_call x11, Pallas kernels, run(): pl.pallas_call(kernel, out_shape=tuple((jax.ShapeDtypeStruct(s, t) for s,...  24.8 us
  transfers between devices with their start and end apart: 41, of which 15 were waited for; matrix products, arithmetic and copies ran while one was open for 2% of the time, Pallas kernels for 15%

profile of v13, /device:TPU:0, one launch (start us, length us, event | category | flops | bytes accessed | tf_op | source)
XLA Modules:
  0.0 96.0 jit_solution(18103060973863636376)
XLA Ops:
  0.7 5.6 %shard_map.147 = (bf16[256,768]{1,0:T(8,128)(2,1)}, bf16[256,768]{1,0:T(8,128)(2,1)}, bf16[256,768]{1,0:T(8,128)(2,1)}, bf16[256,768]{1,0:T(8,128)(2,1)}, bf16[6...) custom-call(s32[2,12]{1,0:T(2,128)} %offs_ref.9, ...), custom_call_target="tpu_custom_call" | custom-call | flops 1207959552 | bytes 7716960 | tf_op jit(solution)/shard_map/pallas_call | solution.py:535
  6.3 3.1 %collective-permute-start = (bf16[8,3072]{1,0:T(8,128)(2,1)}, bf16[8,3072]{1,0:T(8,128)(2,1)S(1)}, u32[]{:S(2)}, u32[]{:S(2)}) collective-permute-start(bf16[8,3072]{1,0:T(8,128)(2,1)} %get-tuple-element.104), channel_id=1, source_target_pairs={{0,8},{1,9},{2,10},{3,11},{4,12},{5,13},{6,14},{7,15},{8,0},{9,1},... | collective-permute-start | bytes 147464 | tf_op jit(solution)/shard_map/ppermute | solution.py:554
  9.3 2.6 %collective-permute-start.1 = (bf16[8,3072]{1,0:T(8,128)(2,1)}, bf16[8,3072]{1,0:T(8,128)(2,1)S(1)}, u32[]{:S(2)}, u32[]{:S(2)}) collective-permute-start(bf16[8,3072]{1,0:T(8,128)(2,1)} %get-tuple-element.104), channel_id=1, source_target_pairs={{0,16},{1,17},{2,18},{3,19},{4,20},{5,21},{6,22},{7,23},{8,24},{9,... | collective-permute-start | bytes 147464 | tf_op jit(solution)/shard_map/ppermute | solution.py:554
  11.9 1.7 %collective-permute-start.3 = (bf16[32,1536]{1,0:T(8,128)(2,1)}, bf16[32,1536]{1,0:T(8,128)(2,1)S(1)}, u32[]{:S(2)}, u32[]{:S(2)}) collective-permute-start(bf16[32,1536]{1,0:T(8,128)(2,1)} %get-tuple-element.68), channel_id=1, source_target_pairs={{0,2},{1,3},{2,0},{3,1},{4,6},{5,7},{6,4},{7,5},{8,10},{9,11},{10,... | collective-permute-start | bytes 294920 | tf_op jit(solution)/shard_map/ppermute | solution.py:554
  13.7 1.5 %collective-permute-start.4 = (bf16[32,1536]{1,0:T(8,128)(2,1)}, bf16[32,1536]{1,0:T(8,128)(2,1)S(1)}, u32[]{:S(2)}, u32[]{:S(2)}) collective-permute-start(bf16[32,1536]{1,0:T(8,128)(2,1)} %get-tuple-element.68), channel_id=1, source_target_pairs={{0,4},{1,5},{2,6},{3,7},{4,0},{5,1},{6,2},{7,3},{8,12},{9,13},{10,... | collective-permute-start | bytes 294920 | tf_op jit(solution)/shard_map/ppermute | solution.py:554
  15.4 0.7 copy-done.15
  17.2 0.8 collective-permute-done.2
  18.1 0.6 collective-permute-done.4
  18.7 0.9 collective-permute-start.7
  19.6 2.0 %collective-permute-start.8 = (bf16[32,1536]{1,0:T(8,128)(2,1)S(1)}, bf16[32,1536]{1,0:T(8,128)(2,1)S(1)}, u32[]{:S(2)}, u32[]{:S(2)}) collective-permute-start(bf16[32,1536]{1,0:T(8,128)(2,1)S(1)} %pad_maximum_fusion.1), channel_id=1, source_target_pairs={{0,4},{1,5},{2,6},{3,7},{4,0},{5,1},{6,2},{7,3},{8,12},{9,13},{10,... | collective-permute-start | bytes 294920 | tf_op jit(solution)/shard_map/ppermute | solution.py:554
  21.6 0.9 collective-permute-start.9
  22.8 2.5 %shard_map.148 = (f32[256,768]{1,0:T(8,128)S(1)}, f32[256,128]{1,0:T(8,128)S(1)}, bf16[768,256]{1,0:T(8,128)(2,1)S(1)}, bf16[768,256]{1,0:T(8,128)(2,1)S(1)}) custom-call(s32[1]{0:T(128)S(6)} %copy.42.pad_ref, bf16[256,768]{1,0:T(8,128)(2,1)S(1)} %copy-done.6, bf16[256,768]{1,0:T(8,128)(2,1)S(1)} %copy-done.7, bf16[256,768]{1,0:T(8,128)(2,1)S(1)} %copy-done.8, ...), custom_call_target="tpu_custom_call" | custom-call | flops 805306368 | bytes 3676164 | tf_op jit(solution)/shard_map/pallas_call | solution.py:535
  25.4 1.7 %collective-permute-done.9 = bf16[32,1536]{1,0:T(8,128)(2,1)S(1)} collective-permute-done((bf16[32,1536]{1,0:T(8,128)(2,1)S(1)}, bf16[32,1536]{1,0:T(8,128)(2,1)S(1)}, u32[]{:S(2)}, u32[]{:S(2)}) %collective-permute-start.9) | collective-permute-done | bytes 98336 | tf_op jit(solution)/shard_map/ppermute | solution.py:554
  27.2 1.7 %collective-permute-done.10.far_1 = bf16[128,1536]{1,0:T(8,128)(2,1)S(1)} collective-permute-done((bf16[128,1536]{1,0:T(8,128)(2,1)S(1)}, bf16[128,1536]{1,0:T(8,128)(2,1)S(1)}, u32[]{:S(2)}, u32[]{:S(2)}) %collective-permute-start.10) | collective-permute-done | bytes 393248 | tf_op jit(solution)/shard_map/ppermute | solution.py:554
  29.0 2.3 %shard_map.149 = (f32[256,128]{1,0:T(8,128)S(1)}, f32[64,128]{1,0:T(8,128)S(1)}, f32[64,128]{1,0:T(8,128)S(1)}, f32[64,768]{1,0:T(8,128)S(1)}) custom-call(s32[2,12]{1,0:T(2,128)S(1)} %copy-done.5, s32[1]{0:T(128)S(6)} %copy.42.pad_ref, bf16[64,3072]{1,0:T(8,128)(2,1)S(1)} %copy-done.1, bf16[128,1536]{1,0:T(8,128)(2,1)S(1)} %constant_dynamic-update-slice_fusion.mid_0, ...), custom_call_target="tpu_custom_call" | custom-call | flops 301989888 | bytes 2490468 | tf_op jit(solution)/shard_map/pallas_call | solution.py:535
  31.3 0.7 collective-permute-start.11
  32.0 1.8 %shard_map.150.dq_sel = f32[64,768]{1,0:T(8,128)S(1)} custom-call(s32[2,12]{1,0:T(2,128)S(1)} %copy-done.5, s32[1]{0:T(128)S(6)} %copy.42.pad_ref, bf16[64,3072]{1,0:T(8,128)(2,1)S(1)} %copy-done.1, bf16[128,1536]{1,0:T(8,128)(2,1)S(1)} %constant_dynamic-update-slice_fusion.mid_0, bf16[128,1536]{1,0:T(8,128)(2,1)S(1)} %collective-permute-done.6.mid_1, ...), custom_call_target="tpu_custom_call" | custom-call | flops 201326592 | bytes 2195556 | tf_op jit(solution)/shard_map/pallas_call | solution.py:535
  34.0 1.6 %collective-permute-start.17 = (bf16[64,1536]{1,0:T(8,128)(2,1)S(1)}, bf16[64,1536]{1,0:T(8,128)(2,1)S(1)}, u32[]{:S(2)}, u32[]{:S(2)}) collective-permute-start(bf16[64,1536]{1,0:T(8,128)(2,1)S(1)} %constant_dynamic-update-slice_fusion.14), channel_id=1, source_target_pairs={{0,2},{1,3},{2,0},{3,1},{4,6},{5,7},{6,4},{7,5},{8,10},{9,11},{10,... | collective-permute-start | bytes 589832 | tf_op jit(solution)/shard_map/ppermute | solution.py:554
  35.7 1.8 %collective-permute-start.19 = (bf16[64,1536]{1,0:T(8,128)(2,1)S(1)}, bf16[64,1536]{1,0:T(8,128)(2,1)S(1)}, u32[]{:S(2)}, u32[]{:S(2)}) collective-permute-start(bf16[64,1536]{1,0:T(8,128)(2,1)S(1)} %constant_dynamic-update-slice_fusion.14), channel_id=1, source_target_pairs={{0,6},{1,7},{2,4},{3,5},{4,2},{5,3},{6,0},{7,1},{8,14},{9,15},{10,... | collective-permute-start | bytes 589832 | tf_op jit(solution)/shard_map/ppermute | solution.py:554
  37.5 3.6 %collective-permute-start.12 = (f32[16,128]{1,0:T(8,128)S(1)}, f32[16,128]{1,0:T(8,128)S(1)}, u32[]{:S(2)}, u32[]{:S(2)}) collective-permute-start(f32[16,128]{1,0:T(8,128)S(1)} %constant_dynamic-update-slice_fusion.8), channel_id=1, source_target_pairs={{0,16},{1,17},{2,18},{3,19},{4,20},{5,21},{6,22},{7,23},{8,24},{9,... | collective-permute-start | bytes 24584 | tf_op jit(solution)/shard_map/ppermute | solution.py:554
  41.1 2.5 %shard_map.151 = (bf16[256,768]{1,0:T(8,128)(2,1)}, bf16[384,256]{1,0:T(8,128)(2,1)S(1)}, bf16[384,256]{1,0:T(8,128)(2,1)S(1)}) custom-call(s32[2,12]{1,0:T(2,128)S(1)} %copy-done.5, f32[256,128]{1,0:T(8,128)S(1)} %get-tuple-element.73.near_stats, f32[256,128]{1,0:T(8,128)S(1)} %get-tuple-element.80.stats, f32[64,128]{1,0:T(8,128)S(1)} %get-tuple-element.84.picked, ...), custom_call_target="tpu_custom_call" | custom-call | flops 905969664 | bytes 3673184 | tf_op jit(solution)/shard_map/pallas_call | solution.py:535
  44.2 0.9 collective-permute-done.14.left_other
  45.6 2.2 %collective-permute-done.13 = f32[32,256]{1,0:T(8,128)S(1)} collective-permute-done((f32[32,256]{1,0:T(8,128)S(1)}, f32[32,256]{1,0:T(8,128)S(1)}, u32[]{:S(2)}, u32[]{:S(2)}) %collective-permute-start.13) | collective-permute-done | bytes 32800 | tf_op jit(solution)/shard_map/ppermute | solution.py:554
  47.8 1.5 %collective-permute-start.21 = (f32[64,256]{1,0:T(8,128)S(1)}, f32[64,256]{1,0:T(8,128)S(1)}, u32[]{:S(2)}, u32[]{:S(2)}) collective-permute-start(f32[64,256]{1,0:T(8,128)S(1)} %constant_dynamic-update-slice_fusion.12), channel_id=1, source_target_pairs={{0,2},{1,3},{2,0},{3,1},{4,6},{5,7},{6,4},{7,5},{8,10},{9,11},{10,... | collective-permute-start | bytes 196616 | tf_op jit(solution)/shard_map/ppermute | solution.py:554
  49.4 0.6 collective-permute-start.37
  49.9 4.1 %shard_map.153 = (bf16[256,768]{1,0:T(8,128)(2,1)S(1)}, f32[256,768]{1,0:T(8,128)S(1)}, f32[256,768]{1,0:T(8,128)S(1)}) custom-call(s32[2,12]{1,0:T(2,128)S(1)} %copy-done.5, s32[1]{0:T(128)S(6)} %copy.42.pad_ref, bf16[256,768]{1,0:T(8,128)(2,1)S(1)} %copy-done.6, bf16[256,768]{1,0:T(8,128)(2,1)S(1)} %copy-done.7, bf16[256,768]{1,0:T(8,128)(2,1)S(1)} %copy-done.8, ...), custom_call_target="tpu_custom_call" | custom-call | flops 805306368 | bytes 3866724 | tf_op jit(solution)/shard_map/pallas_call | solution.py:535
  55.4 2.5 %collective-permute-done.37 = bf16[192,768]{1,0:T(8,128)(2,1)S(1)} collective-permute-done((bf16[192,768]{1,0:T(8,128)(2,1)S(1)}, bf16[192,768]{1,0:T(8,128)(2,1)S(1)}, u32[]{:S(2)}, u32[]{:S(2)}) %collective-permute-start.37) | collective-permute-done | bytes 294944 | tf_op jit(solution)/shard_map/ppermute | solution.py:554
  58.4 2.4 %shard_map.155 = (bf16[256,768]{1,0:T(8,128)(2,1)S(1)}, bf16[256,768]{1,0:T(8,128)(2,1)S(1)}) custom-call(s32[2,12]{1,0:T(2,128)S(1)} %copy-done.5, s32[1]{0:T(128)S(6)} %copy.42.pad_ref, bf16[64,3072]{1,0:T(8,128)(2,1)S(1)} %copy-done.1, bf16[256,1536]{1,0:T(8,128)(2,1)S(1)} %constant_dynamic-update-slice_fusion.19.qg_0, ...), custom_call_target="tpu_custom_call" | custom-call | flops 15099494 | bytes 229381 | tf_op jit(solution)/shard_map/pallas_call | solution.py:535
  61.8 0.8 collective-permute-done.24.dk_other
  62.6 0.6 collective-permute-done.25.dv_other
  63.2 0.8 shard_map.156
  64.0 1.0 %collective-permute-start.27 = (bf16[96,1536]{1,0:T(8,128)(2,1)S(1)}, bf16[96,1536]{1,0:T(8,128)(2,1)S(1)}, u32[]{:S(2)}, u32[]{:S(2)}) collective-permute-start(bf16[96,1536]{1,0:T(8,128)(2,1)S(1)} %get-tuple-element.128), channel_id=1, source_target_pairs={{0,2},{1,3},{2,0},{3,1},{4,6},{5,7},{6,4},{7,5},{8,10},{9,11},{10,... | collective-permute-start | bytes 884744 | tf_op jit(solution)/shard_map/ppermute | solution.py:554
  65.4 1.2 %collective-permute-start.31 = (bf16[96,1536]{1,0:T(8,128)(2,1)S(1)}, bf16[96,1536]{1,0:T(8,128)(2,1)S(1)}, u32[]{:S(2)}, u32[]{:S(2)}) collective-permute-start(bf16[96,1536]{1,0:T(8,128)(2,1)S(1)} %get-tuple-element.130), channel_id=1, source_target_pairs={{0,4},{1,5},{2,6},{3,7},{4,0},{5,1},{6,2},{7,3},{8,12},{9,13},{10,... | collective-permute-start | bytes 884744 | tf_op jit(solution)/shard_map/ppermute | solution.py:554
  66.6 1.2 %collective-permute-start.32 = (bf16[96,1536]{1,0:T(8,128)(2,1)S(1)}, bf16[96,1536]{1,0:T(8,128)(2,1)S(1)}, u32[]{:S(2)}, u32[]{:S(2)}) collective-permute-start(bf16[96,1536]{1,0:T(8,128)(2,1)S(1)} %get-tuple-element.129), channel_id=1, source_target_pairs={{0,6},{1,7},{2,4},{3,5},{4,2},{5,3},{6,0},{7,1},{8,14},{9,15},{10,... | collective-permute-start | bytes 884744 | tf_op jit(solution)/shard_map/ppermute | solution.py:554
  67.9 1.9 %shard_map.157 = bf16[256,768]{1,0:T(8,128)(2,1)} custom-call(bf16[256,768]{1,0:T(8,128)(2,1)S(1)} %get-tuple-element.119.right.dq, bf16[256,768]{1,0:T(8,128)(2,1)S(1)} %get-tuple-element.117.dk, bf16[256,768]{1,0:T(8,128)(2,1)S(1)} %get-tuple-element.118.dv, bf16[768,2304]{1,0:T(8,128)(2,1)S(1)} %copy-done), custom_call_target="tpu_custom_call" | custom-call | flops 45298484 | bytes 255590 | tf_op jit(solution)/shard_map/pallas_call | solution.py:535
  69.7 4.2 %collective-permute-done.27 = bf16[96,1536]{1,0:T(8,128)(2,1)S(1)} collective-permute-done((bf16[96,1536]{1,0:T(8,128)(2,1)S(1)}, bf16[96,1536]{1,0:T(8,128)(2,1)S(1)}, u32[]{:S(2)}, u32[]{:S(2)}) %collective-permute-start.27) | collective-permute-done | bytes 294944 | tf_op jit(solution)/shard_map/ppermute | solution.py:554
  74.4 1.1 %collective-permute-start.28 = (bf16[48,768]{1,0:T(8,128)(2,1)S(1)}, bf16[48,768]{1,0:T(8,128)(2,1)S(1)}, u32[]{:S(2)}, u32[]{:S(2)}) collective-permute-start(bf16[48,768]{1,0:T(8,128)(2,1)S(1)} %get-tuple-element.140), channel_id=1, source_target_pairs={{0,2},{1,3},{2,0},{3,1},{4,6},{5,7},{6,4},{7,5},{8,10},{9,11},{10,... | collective-permute-start | bytes 221192 | tf_op jit(solution)/shard_map/ppermute | solution.py:554
  75.5 1.2 %collective-permute-start.29 = (bf16[48,768]{1,0:T(8,128)(2,1)S(1)}, bf16[48,768]{1,0:T(8,128)(2,1)S(1)}, u32[]{:S(2)}, u32[]{:S(2)}) collective-permute-start(bf16[48,768]{1,0:T(8,128)(2,1)S(1)} %get-tuple-element.142), channel_id=1, source_target_pairs={{0,4},{1,5},{2,6},{3,7},{4,0},{5,1},{6,2},{7,3},{8,12},{9,13},{10,... | collective-permute-start | bytes 221192 | tf_op jit(solution)/shard_map/ppermute | solution.py:554
  76.7 5.2 %collective-permute-done.31 = bf16[96,1536]{1,0:T(8,128)(2,1)S(1)} collective-permute-done((bf16[96,1536]{1,0:T(8,128)(2,1)S(1)}, bf16[96,1536]{1,0:T(8,128)(2,1)S(1)}, u32[]{:S(2)}, u32[]{:S(2)}) %collective-permute-start.31) | collective-permute-done | bytes 294944 | tf_op jit(solution)/shard_map/ppermute | solution.py:554
  82.2 1.6 %collective-permute-start.34 = (bf16[24,1536]{1,0:T(8,128)(2,1)S(1)}, bf16[24,1536]{1,0:T(8,128)(2,1)S(1)}, u32[]{:S(2)}, u32[]{:S(2)}) collective-permute-start(bf16[24,1536]{1,0:T(8,128)(2,1)S(1)} %get-tuple-element.143), channel_id=1, source_target_pairs={{0,8},{1,9},{2,10},{3,11},{4,12},{5,13},{6,14},{7,15},{8,0},{9,1},... | collective-permute-start | bytes 221192 | tf_op jit(solution)/shard_map/ppermute | solution.py:554
  83.8 3.0 %collective-permute-start.35 = (bf16[24,1536]{1,0:T(8,128)(2,1)S(1)}, bf16[24,1536]{1,0:T(8,128)(2,1)S(1)}, u32[]{:S(2)}, u32[]{:S(2)}) collective-permute-start(bf16[24,1536]{1,0:T(8,128)(2,1)S(1)} %get-tuple-element.145), channel_id=1, source_target_pairs={{0,16},{1,17},{2,18},{3,19},{4,20},{5,21},{6,22},{7,23},{8,24},{9,... | collective-permute-start | bytes 221192 | tf_op jit(solution)/shard_map/ppermute | solution.py:554
  87.0 1.5 %collective-permute-start.40 = (bf16[24,768]{1,0:T(8,128)(2,1)S(1)}, bf16[24,768]{1,0:T(8,128)(2,1)S(1)}, u32[]{:S(2)}, u32[]{:S(2)}) collective-permute-start(bf16[24,768]{1,0:T(8,128)(2,1)S(1)} %slice.167), channel_id=1, source_target_pairs={{0,16},{1,17},{2,18},{3,19},{4,20},{5,21},{6,22},{7,23},{8,24},{9,... | collective-permute-start | bytes 110600 | tf_op jit(solution)/shard_map/ppermute | solution.py:554
  88.6 1.5 %collective-permute-start.33 = (bf16[24,768]{1,0:T(8,128)(2,1)S(1)}, bf16[24,768]{1,0:T(8,128)(2,1)S(1)}, u32[]{:S(2)}, u32[]{:S(2)}) collective-permute-start(bf16[24,768]{1,0:T(8,128)(2,1)S(1)} %slice.155), channel_id=1, source_target_pairs={{0,16},{1,17},{2,18},{3,19},{4,20},{5,21},{6,22},{7,23},{8,24},{9,... | collective-permute-start | bytes 110600 | tf_op jit(solution)/shard_map/ppermute | solution.py:554
  90.1 1.8 %collective-permute-done.35 = bf16[24,1536]{1,0:T(8,128)(2,1)S(1)} collective-permute-done((bf16[24,1536]{1,0:T(8,128)(2,1)S(1)}, bf16[24,1536]{1,0:T(8,128)(2,1)S(1)}, u32[]{:S(2)}, u32[]{:S(2)}) %collective-permute-start.35) | collective-permute-done | bytes 73760 | tf_op jit(solution)/shard_map/ppermute | solution.py:554
  91.9 1.3 %collective-permute-done.36 = bf16[24,1536]{1,0:T(8,128)(2,1)S(1)} collective-permute-done((bf16[24,1536]{1,0:T(8,128)(2,1)S(1)}, bf16[24,1536]{1,0:T(8,128)(2,1)S(1)}, u32[]{:S(2)}, u32[]{:S(2)}) %collective-permute-start.36) | collective-permute-done | bytes 73760 | tf_op jit(solution)/shard_map/ppermute | solution.py:554
  93.3 1.4 %collective-permute-done.33 = bf16[24,768]{1,0:T(8,128)(2,1)S(1)} collective-permute-done((bf16[24,768]{1,0:T(8,128)(2,1)S(1)}, bf16[24,768]{1,0:T(8,128)(2,1)S(1)}, u32[]{:S(2)}, u32[]{:S(2)}) %collective-permute-start.33) | collective-permute-done | bytes 36896 | tf_op jit(solution)/shard_map/ppermute | solution.py:554
  94.7 0.7 pad_maximum_fusion
  95.4 0.6 convert_add_fusion.1
  (138 shorter events, 6.2 us)
Async XLA Ops:
  0.6 14.5 %copy-start.10 = (s32[768,1]{1,0:T(8,128)S(1)}, s32[768,1]{1,0:T(8,128)}, u32[]{:S(2)}) copy-start(s32[768,1]{1,0:T(8,128)} %constant.14.clone) | copy-start | bytes 9220
  0.6 14.5 %copy-start.11 = (s32[768,1]{1,0:T(8,128)S(1)}, s32[768,1]{1,0:T(8,128)}, u32[]{:S(2)}) copy-start(s32[768,1]{1,0:T(8,128)} %constant.15.clone) | copy-start | bytes 9220
  0.7 14.5 %copy-start.12 = (s32[768,1]{1,0:T(8,128)S(1)}, s32[768,1]{1,0:T(8,128)}, u32[]{:S(2)}) copy-start(s32[768,1]{1,0:T(8,128)} %constant.16.clone) | copy-start | bytes 9220
  0.7 14.5 %copy-start.13 = (s32[768,1]{1,0:T(8,128)S(1)}, s32[768,1]{1,0:T(8,128)}, u32[]{:S(2)}) copy-start(s32[768,1]{1,0:T(8,128)} %constant.17.clone) | copy-start | bytes 9220
  6.3 10.6 %collective-permute-start = (bf16[8,3072]{1,0:T(8,128)(2,1)}, bf16[8,3072]{1,0:T(8,128)(2,1)S(1)}, u32[]{:S(2)}, u32[]{:S(2)}) collective-permute-start(bf16[8,3072]{1,0:T(8,128)(2,1)} %get-tuple-element.104), channel_id=1, source_target_pairs={{0,8},{1,9},{2,10},{3,11},{4,12},{5,13},{6,14},{7,15},{8,0},{9,1},... | collective-permute-start | bytes 147464 | tf_op jit(solution)/shard_map/ppermute | solution.py:554
  9.3 7.9 %collective-permute-start.1 = (bf16[8,3072]{1,0:T(8,128)(2,1)}, bf16[8,3072]{1,0:T(8,128)(2,1)S(1)}, u32[]{:S(2)}, u32[]{:S(2)}) collective-permute-start(bf16[8,3072]{1,0:T(8,128)(2,1)} %get-tuple-element.104), channel_id=1, source_target_pairs={{0,16},{1,17},{2,18},{3,19},{4,20},{5,21},{6,22},{7,23},{8,24},{9,... | collective-permute-start | bytes 147464 | tf_op jit(solution)/shard_map/ppermute | solution.py:554
  11.9 6.1 %collective-permute-start.2 = (bf16[8,3072]{1,0:T(8,128)(2,1)}, bf16[8,3072]{1,0:T(8,128)(2,1)S(1)}, u32[]{:S(2)}, u32[]{:S(2)}) collective-permute-start(bf16[8,3072]{1,0:T(8,128)(2,1)} %get-tuple-element.104), channel_id=1, source_target_pairs={{0,24},{1,25},{2,26},{3,27},{4,28},{5,29},{6,30},{7,31},{8,16},{9,... | collective-permute-start | bytes 147464 | tf_op jit(solution)/shard_map/ppermute | solution.py:554
  11.9 6.1 %collective-permute-start.3 = (bf16[32,1536]{1,0:T(8,128)(2,1)}, bf16[32,1536]{1,0:T(8,128)(2,1)S(1)}, u32[]{:S(2)}, u32[]{:S(2)}) collective-permute-start(bf16[32,1536]{1,0:T(8,128)(2,1)} %get-tuple-element.68), channel_id=1, source_target_pairs={{0,2},{1,3},{2,0},{3,1},{4,6},{5,7},{6,4},{7,5},{8,10},{9,11},{10,... | collective-permute-start | bytes 294920 | tf_op jit(solution)/shard_map/ppermute | solution.py:554
  13.7 5.1 %collective-permute-start.4 = (bf16[32,1536]{1,0:T(8,128)(2,1)}, bf16[32,1536]{1,0:T(8,128)(2,1)S(1)}, u32[]{:S(2)}, u32[]{:S(2)}) collective-permute-start(bf16[32,1536]{1,0:T(8,128)(2,1)} %get-tuple-element.68), channel_id=1, source_target_pairs={{0,4},{1,5},{2,6},{3,7},{4,0},{5,1},{6,2},{7,3},{8,12},{9,13},{10,... | collective-permute-start | bytes 294920 | tf_op jit(solution)/shard_map/ppermute | solution.py:554
  15.2 7.5 %copy-start.8 = (bf16[256,768]{1,0:T(8,128)(2,1)S(1)}, bf16[256,768]{1,0:T(8,128)(2,1)}, u32[]{:S(2)}) copy-start(bf16[256,768]{1,0:T(8,128)(2,1)} %get-tuple-element.71.v) | copy-start | bytes 1179652
  15.2 7.5 %copy-start.9 = (bf16[256,768]{1,0:T(8,128)(2,1)S(1)}, bf16[256,768]{1,0:T(8,128)(2,1)}, u32[]{:S(2)}) copy-start(bf16[256,768]{1,0:T(8,128)(2,1)} %get-tuple-element.72.g) | copy-start | bytes 1179652
  16.9 5.7 %collective-permute-start.5 = (bf16[32,1536]{1,0:T(8,128)(2,1)S(1)}, bf16[32,1536]{1,0:T(8,128)(2,1)S(1)}, u32[]{:S(2)}, u32[]{:S(2)}) collective-permute-start(bf16[32,1536]{1,0:T(8,128)(2,1)S(1)} %copy-done.15), channel_id=1, source_target_pairs={{0,6},{1,7},{2,4},{3,5},{4,2},{5,3},{6,0},{7,1},{8,14},{9,15},{10,... | collective-permute-start | bytes 294920 | tf_op jit(solution)/shard_map/ppermute | solution.py:554
  18.7 6.6 %collective-permute-start.7 = (bf16[32,1536]{1,0:T(8,128)(2,1)S(1)}, bf16[32,1536]{1,0:T(8,128)(2,1)S(1)}, u32[]{:S(2)}, u32[]{:S(2)}) collective-permute-start(bf16[32,1536]{1,0:T(8,128)(2,1)S(1)} %pad_maximum_fusion.1), channel_id=1, source_target_pairs={{0,2},{1,3},{2,0},{3,1},{4,6},{5,7},{6,4},{7,5},{8,10},{9,11},{10,... | collective-permute-start | bytes 294920 | tf_op jit(solution)/shard_map/ppermute | solution.py:554
  19.6 5.7 %collective-permute-start.8 = (bf16[32,1536]{1,0:T(8,128)(2,1)S(1)}, bf16[32,1536]{1,0:T(8,128)(2,1)S(1)}, u32[]{:S(2)}, u32[]{:S(2)}) collective-permute-start(bf16[32,1536]{1,0:T(8,128)(2,1)S(1)} %pad_maximum_fusion.1), channel_id=1, source_target_pairs={{0,4},{1,5},{2,6},{3,7},{4,0},{5,1},{6,2},{7,3},{8,12},{9,13},{10,... | collective-permute-start | bytes 294920 | tf_op jit(solution)/shard_map/ppermute | solution.py:554
  21.6 5.5 %collective-permute-start.9 = (bf16[32,1536]{1,0:T(8,128)(2,1)S(1)}, bf16[32,1536]{1,0:T(8,128)(2,1)S(1)}, u32[]{:S(2)}, u32[]{:S(2)}) collective-permute-start(bf16[32,1536]{1,0:T(8,128)(2,1)S(1)} %pad_maximum_fusion.1), channel_id=1, source_target_pairs={{0,6},{1,7},{2,4},{3,5},{4,2},{5,3},{6,0},{7,1},{8,14},{9,15},{10,... | collective-permute-start | bytes 294920 | tf_op jit(solution)/shard_map/ppermute | solution.py:554
  22.6 4.6 %collective-permute-start.6 = (bf16[128,1536]{1,0:T(8,128)(2,1)S(1)}, bf16[128,1536]{1,0:T(8,128)(2,1)S(1)}, u32[]{:S(2)}, u32[]{:S(2)}) collective-permute-start(bf16[128,1536]{1,0:T(8,128)(2,1)S(1)} %constant_dynamic-update-slice_fusion.mid_0), channel_id=1, source_target_pairs={{0,1},{1,0},{2,3},{3,2},{4,5},{5,4},{6,7},{7,6},{8,9},{9,8},{10,11... | collective-permute-start | bytes 1179656 | tf_op jit(solution)/shard_map/ppermute | solution.py:554
  27.2 1.8 %collective-permute-start.10 = (bf16[128,1536]{1,0:T(8,128)(2,1)S(1)}, bf16[128,1536]{1,0:T(8,128)(2,1)S(1)}, u32[]{:S(2)}, u32[]{:S(2)}) collective-permute-start(bf16[128,1536]{1,0:T(8,128)(2,1)S(1)} %constant_dynamic-update-slice_fusion.4.far_0), channel_id=1, source_target_pairs={{0,1},{1,0},{2,3},{3,2},{4,5},{5,4},{6,7},{7,6},{8,9},{9,8},{10,11... | collective-permute-start | bytes 1179656 | tf_op jit(solution)/shard_map/ppermute | solution.py:554
  31.3 9.9 %copy-start.2 = (bf16[768,768]{1,0:T(8,128)(2,1)S(1)}, bf16[768,768]{1,0:T(8,128)(2,1)}, u32[]{:S(2)}) copy-start(bf16[768,768]{1,0:T(8,128)(2,1)} %w_out.1) | copy-start | bytes 3538948
  31.3 6.2 %collective-permute-start.11 = (f32[8,128]{1,0:T(8,128)S(1)}, f32[8,128]{1,0:T(8,128)S(1)}, u32[]{:S(2)}, u32[]{:S(2)}) collective-permute-start(f32[8,128]{1,0:T(8,128)S(1)} %slice.130), channel_id=1, source_target_pairs={{0,8},{1,9},{2,10},{3,11},{4,12},{5,13},{6,14},{7,15},{8,0},{9,1},... | collective-permute-start | bytes 12296 | tf_op jit(solution)/shard_map/ppermute | solution.py:554
  34.0 20.0 %collective-permute-start.17 = (bf16[64,1536]{1,0:T(8,128)(2,1)S(1)}, bf16[64,1536]{1,0:T(8,128)(2,1)S(1)}, u32[]{:S(2)}, u32[]{:S(2)}) collective-permute-start(bf16[64,1536]{1,0:T(8,128)(2,1)S(1)} %constant_dynamic-update-slice_fusion.14), channel_id=1, source_target_pairs={{0,2},{1,3},{2,0},{3,1},{4,6},{5,7},{6,4},{7,5},{8,10},{9,11},{10,... | collective-permute-start | bytes 589832 | tf_op jit(solution)/shard_map/ppermute | solution.py:554
  35.5 18.5 %collective-permute-start.18 = (bf16[64,1536]{1,0:T(8,128)(2,1)S(1)}, bf16[64,1536]{1,0:T(8,128)(2,1)S(1)}, u32[]{:S(2)}, u32[]{:S(2)}) collective-permute-start(bf16[64,1536]{1,0:T(8,128)(2,1)S(1)} %constant_dynamic-update-slice_fusion.14), channel_id=1, source_target_pairs={{0,4},{1,5},{2,6},{3,7},{4,0},{5,1},{6,2},{7,3},{8,12},{9,13},{10,... | collective-permute-start | bytes 589832 | tf_op jit(solution)/shard_map/ppermute | solution.py:554
  35.7 18.9 %collective-permute-start.19 = (bf16[64,1536]{1,0:T(8,128)(2,1)S(1)}, bf16[64,1536]{1,0:T(8,128)(2,1)S(1)}, u32[]{:S(2)}, u32[]{:S(2)}) collective-permute-start(bf16[64,1536]{1,0:T(8,128)(2,1)S(1)} %constant_dynamic-update-slice_fusion.14), channel_id=1, source_target_pairs={{0,6},{1,7},{2,4},{3,5},{4,2},{5,3},{6,0},{7,1},{8,14},{9,15},{10,... | collective-permute-start | bytes 589832 | tf_op jit(solution)/shard_map/ppermute | solution.py:554
  37.5 6.3 %collective-permute-start.15 = (bf16[256,768]{1,0:T(8,128)(2,1)S(1)}, bf16[256,768]{1,0:T(8,128)(2,1)S(1)}, u32[]{:S(2)}, u32[]{:S(2)}) collective-permute-start(bf16[256,768]{1,0:T(8,128)(2,1)S(1)} %copy-done.4), channel_id=1, source_target_pairs={{0,1},{1,0},{2,3},{3,2},{4,5},{5,4},{6,7},{7,6},{8,9},{9,8},{10,11... | collective-permute-start | bytes 1179656 | tf_op jit(solution)/shard_map/ppermute | solution.py:554
  37.5 6.1 %collective-permute-start.12 = (f32[16,128]{1,0:T(8,128)S(1)}, f32[16,128]{1,0:T(8,128)S(1)}, u32[]{:S(2)}, u32[]{:S(2)}) collective-permute-start(f32[16,128]{1,0:T(8,128)S(1)} %constant_dynamic-update-slice_fusion.8), channel_id=1, source_target_pairs={{0,16},{1,17},{2,18},{3,19},{4,20},{5,21},{6,22},{7,23},{8,24},{9,... | collective-permute-start | bytes 24584 | tf_op jit(solution)/shard_map/ppermute | solution.py:554
  43.7 1.4 %collective-permute-start.14 = (bf16[384,256]{1,0:T(8,128)(2,1)S(1)}, bf16[384,256]{1,0:T(8,128)(2,1)S(1)}, u32[]{:S(2)}, u32[]{:S(2)}) collective-permute-start(bf16[384,256]{1,0:T(8,128)(2,1)S(1)} %get-tuple-element.92), channel_id=1, source_target_pairs={{0,1},{1,0},{2,3},{3,2},{4,5},{5,4},{6,7},{7,6},{8,9},{9,8},{10,11... | collective-permute-start | bytes 589832 | tf_op jit(solution)/shard_map/ppermute | solution.py:554
  43.8 4.0 %collective-permute-start.13 = (f32[32,256]{1,0:T(8,128)S(1)}, f32[32,256]{1,0:T(8,128)S(1)}, u32[]{:S(2)}, u32[]{:S(2)}) collective-permute-start(f32[32,256]{1,0:T(8,128)S(1)} %pad_maximum_fusion.2), channel_id=1, source_target_pairs={{0,4},{1,5},{2,6},{3,7},{4,0},{5,1},{6,2},{7,3},{8,12},{9,13},{10,... | collective-permute-start | bytes 98312 | tf_op jit(solution)/shard_map/ppermute | solution.py:554
  47.8 7.0 %collective-permute-start.21 = (f32[64,256]{1,0:T(8,128)S(1)}, f32[64,256]{1,0:T(8,128)S(1)}, u32[]{:S(2)}, u32[]{:S(2)}) collective-permute-start(f32[64,256]{1,0:T(8,128)S(1)} %constant_dynamic-update-slice_fusion.12), channel_id=1, source_target_pairs={{0,2},{1,3},{2,0},{3,1},{4,6},{5,7},{6,4},{7,5},{8,10},{9,11},{10,... | collective-permute-start | bytes 196616 | tf_op jit(solution)/shard_map/ppermute | solution.py:554
  49.4 8.6 %collective-permute-start.37 = (bf16[192,768]{1,0:T(8,128)(2,1)S(1)}, bf16[192,768]{1,0:T(8,128)(2,1)S(1)}, u32[]{:S(2)}, u32[]{:S(2)}) collective-permute-start(bf16[192,768]{1,0:T(8,128)(2,1)S(1)} %get-tuple-element.131), channel_id=1, source_target_pairs={{0,2},{1,3},{2,0},{3,1},{4,6},{5,7},{6,4},{7,5},{8,10},{9,11},{10,... | collective-permute-start | bytes 884744 | tf_op jit(solution)/shard_map/ppermute | solution.py:554
  54.0 3.9 %collective-permute-start.16 = (bf16[768,256]{1,0:T(8,128)(2,1)S(1)}, bf16[768,256]{1,0:T(8,128)(2,1)S(1)}, u32[]{:S(2)}, u32[]{:S(2)}) collective-permute-start(bf16[768,256]{1,0:T(8,128)(2,1)S(1)} %get-tuple-element.101), channel_id=1, source_target_pairs={{0,1},{1,0},{2,3},{3,2},{4,5},{5,4},{6,7},{7,6},{8,9},{9,8},{10,11... | collective-permute-start | bytes 1179656 | tf_op jit(solution)/shard_map/ppermute | solution.py:554
  54.1 3.9 %collective-permute-start.23 = (bf16[256,768]{1,0:T(8,128)(2,1)S(1)}, bf16[256,768]{1,0:T(8,128)(2,1)S(1)}, u32[]{:S(2)}, u32[]{:S(2)}) collective-permute-start(bf16[256,768]{1,0:T(8,128)(2,1)S(1)} %get-tuple-element.119.right.dq), channel_id=1, source_target_pairs={{0,1},{1,0},{2,3},{3,2},{4,5},{5,4},{6,7},{7,6},{8,9},{9,8},{10,11... | collective-permute-start | bytes 1179656 | tf_op jit(solution)/shard_map/ppermute | solution.py:554
  54.7 3.8 %collective-permute-start.20 = (bf16[256,1536]{1,0:T(8,128)(2,1)S(1)}, bf16[256,1536]{1,0:T(8,128)(2,1)S(1)}, u32[]{:S(2)}, u32[]{:S(2)}) collective-permute-start(bf16[256,1536]{1,0:T(8,128)(2,1)S(1)} %constant_dynamic-update-slice_fusion.19.qg_0), channel_id=1, source_target_pairs={{0,1},{1,0},{2,3},{3,2},{4,5},{5,4},{6,7},{7,6},{8,9},{9,8},{10,11... | collective-permute-start | bytes 2359304 | tf_op jit(solution)/shard_map/ppermute | solution.py:554
  54.9 3.5 %collective-permute-start.22 = (f32[256,128]{1,0:T(8,128)S(1)}, f32[256,128]{1,0:T(8,128)S(1)}, u32[]{:S(2)}, u32[]{:S(2)}) collective-permute-start(f32[256,128]{1,0:T(8,128)S(1)} %constant_dynamic-update-slice_fusion.23.stats_0), channel_id=1, source_target_pairs={{0,1},{1,0},{2,3},{3,2},{4,5},{5,4},{6,7},{7,6},{8,9},{9,8},{10,11... | collective-permute-start | bytes 393224 | tf_op jit(solution)/shard_map/ppermute | solution.py:554
  60.8 1.8 %collective-permute-start.24 = (bf16[256,768]{1,0:T(8,128)(2,1)S(1)}, bf16[256,768]{1,0:T(8,128)(2,1)S(1)}, u32[]{:S(2)}, u32[]{:S(2)}) collective-permute-start(bf16[256,768]{1,0:T(8,128)(2,1)S(1)} %get-tuple-element.117.dk), channel_id=1, source_target_pairs={{0,1},{1,0},{2,3},{3,2},{4,5},{5,4},{6,7},{7,6},{8,9},{9,8},{10,11... | collective-permute-start | bytes 1179656 | tf_op jit(solution)/shard_map/ppermute | solution.py:554
  60.9 2.3 %collective-permute-start.25 = (bf16[256,768]{1,0:T(8,128)(2,1)S(1)}, bf16[256,768]{1,0:T(8,128)(2,1)S(1)}, u32[]{:S(2)}, u32[]{:S(2)}) collective-permute-start(bf16[256,768]{1,0:T(8,128)(2,1)S(1)} %get-tuple-element.118.dv), channel_id=1, source_target_pairs={{0,1},{1,0},{2,3},{3,2},{4,5},{5,4},{6,7},{7,6},{8,9},{9,8},{10,11... | collective-permute-start | bytes 1179656 | tf_op jit(solution)/shard_map/ppermute | solution.py:554
  61.5 8.3 %collective-permute-start.38 = (bf16[96,768]{1,0:T(8,128)(2,1)S(1)}, bf16[96,768]{1,0:T(8,128)(2,1)S(1)}, u32[]{:S(2)}, u32[]{:S(2)}) collective-permute-start(bf16[96,768]{1,0:T(8,128)(2,1)S(1)} %get-tuple-element.138), channel_id=1, source_target_pairs={{0,4},{1,5},{2,6},{3,7},{4,0},{5,1},{6,2},{7,3},{8,12},{9,13},{10,... | collective-permute-start | bytes 442376 | tf_op jit(solution)/shard_map/ppermute | solution.py:554
  64.0 9.9 %collective-permute-start.27 = (bf16[96,1536]{1,0:T(8,128)(2,1)S(1)}, bf16[96,1536]{1,0:T(8,128)(2,1)S(1)}, u32[]{:S(2)}, u32[]{:S(2)}) collective-permute-start(bf16[96,1536]{1,0:T(8,128)(2,1)S(1)} %get-tuple-element.128), channel_id=1, source_target_pairs={{0,2},{1,3},{2,0},{3,1},{4,6},{5,7},{6,4},{7,5},{8,10},{9,11},{10,... | collective-permute-start | bytes 884744 | tf_op jit(solution)/shard_map/ppermute | solution.py:554
  65.1 9.2 %collective-permute-start.26 = (bf16[192,768]{1,0:T(8,128)(2,1)S(1)}, bf16[192,768]{1,0:T(8,128)(2,1)S(1)}, u32[]{:S(2)}, u32[]{:S(2)}) collective-permute-start(bf16[192,768]{1,0:T(8,128)(2,1)S(1)} %get-tuple-element.133), channel_id=1, source_target_pairs={{0,8},{1,9},{2,10},{3,11},{4,12},{5,13},{6,14},{7,15},{8,0},{9,1},... | collective-permute-start | bytes 884744 | tf_op jit(solution)/shard_map/ppermute | solution.py:554
  65.4 16.5 %collective-permute-start.31 = (bf16[96,1536]{1,0:T(8,128)(2,1)S(1)}, bf16[96,1536]{1,0:T(8,128)(2,1)S(1)}, u32[]{:S(2)}, u32[]{:S(2)}) collective-permute-start(bf16[96,1536]{1,0:T(8,128)(2,1)S(1)} %get-tuple-element.130), channel_id=1, source_target_pairs={{0,4},{1,5},{2,6},{3,7},{4,0},{5,1},{6,2},{7,3},{8,12},{9,13},{10,... | collective-permute-start | bytes 884744 | tf_op jit(solution)/shard_map/ppermute | solution.py:554
  66.6 15.3 %collective-permute-start.32 = (bf16[96,1536]{1,0:T(8,128)(2,1)S(1)}, bf16[96,1536]{1,0:T(8,128)(2,1)S(1)}, u32[]{:S(2)}, u32[]{:S(2)}) collective-permute-start(bf16[96,1536]{1,0:T(8,128)(2,1)S(1)} %get-tuple-element.129), channel_id=1, source_target_pairs={{0,6},{1,7},{2,4},{3,5},{4,2},{5,3},{6,0},{7,1},{8,14},{9,15},{10,... | collective-permute-start | bytes 884744 | tf_op jit(solution)/shard_map/ppermute | solution.py:554
  74.0 9.8 %collective-permute-start.39 = (bf16[48,768]{1,0:T(8,128)(2,1)S(1)}, bf16[48,768]{1,0:T(8,128)(2,1)S(1)}, u32[]{:S(2)}, u32[]{:S(2)}) collective-permute-start(bf16[48,768]{1,0:T(8,128)(2,1)S(1)} %slice.190), channel_id=1, source_target_pairs={{0,8},{1,9},{2,10},{3,11},{4,12},{5,13},{6,14},{7,15},{8,0},{9,1},... | collective-permute-start | bytes 221192 | tf_op jit(solution)/shard_map/ppermute | solution.py:554
  74.4 12.5 %collective-permute-start.28 = (bf16[48,768]{1,0:T(8,128)(2,1)S(1)}, bf16[48,768]{1,0:T(8,128)(2,1)S(1)}, u32[]{:S(2)}, u32[]{:S(2)}) collective-permute-start(bf16[48,768]{1,0:T(8,128)(2,1)S(1)} %get-tuple-element.140), channel_id=1, source_target_pairs={{0,2},{1,3},{2,0},{3,1},{4,6},{5,7},{6,4},{7,5},{8,10},{9,11},{10,... | collective-permute-start | bytes 221192 | tf_op jit(solution)/shard_map/ppermute | solution.py:554
  75.5 11.5 %collective-permute-start.29 = (bf16[48,768]{1,0:T(8,128)(2,1)S(1)}, bf16[48,768]{1,0:T(8,128)(2,1)S(1)}, u32[]{:S(2)}, u32[]{:S(2)}) collective-permute-start(bf16[48,768]{1,0:T(8,128)(2,1)S(1)} %get-tuple-element.142), channel_id=1, source_target_pairs={{0,4},{1,5},{2,6},{3,7},{4,0},{5,1},{6,2},{7,3},{8,12},{9,13},{10,... | collective-permute-start | bytes 221192 | tf_op jit(solution)/shard_map/ppermute | solution.py:554
  81.9 6.6 %collective-permute-start.30 = (bf16[48,768]{1,0:T(8,128)(2,1)S(1)}, bf16[48,768]{1,0:T(8,128)(2,1)S(1)}, u32[]{:S(2)}, u32[]{:S(2)}) collective-permute-start(bf16[48,768]{1,0:T(8,128)(2,1)S(1)} %get-tuple-element.141), channel_id=1, source_target_pairs={{0,6},{1,7},{2,4},{3,5},{4,2},{5,3},{6,0},{7,1},{8,14},{9,15},{10,... | collective-permute-start | bytes 221192 | tf_op jit(solution)/shard_map/ppermute | solution.py:554
  82.2 7.9 %collective-permute-start.34 = (bf16[24,1536]{1,0:T(8,128)(2,1)S(1)}, bf16[24,1536]{1,0:T(8,128)(2,1)S(1)}, u32[]{:S(2)}, u32[]{:S(2)}) collective-permute-start(bf16[24,1536]{1,0:T(8,128)(2,1)S(1)} %get-tuple-element.143), channel_id=1, source_target_pairs={{0,8},{1,9},{2,10},{3,11},{4,12},{5,13},{6,14},{7,15},{8,0},{9,1},... | collective-permute-start | bytes 221192 | tf_op jit(solution)/shard_map/ppermute | solution.py:554
  83.8 8.0 %collective-permute-start.35 = (bf16[24,1536]{1,0:T(8,128)(2,1)S(1)}, bf16[24,1536]{1,0:T(8,128)(2,1)S(1)}, u32[]{:S(2)}, u32[]{:S(2)}) collective-permute-start(bf16[24,1536]{1,0:T(8,128)(2,1)S(1)} %get-tuple-element.145), channel_id=1, source_target_pairs={{0,16},{1,17},{2,18},{3,19},{4,20},{5,21},{6,22},{7,23},{8,24},{9,... | collective-permute-start | bytes 221192 | tf_op jit(solution)/shard_map/ppermute | solution.py:554
  86.9 6.3 %collective-permute-start.36 = (bf16[24,1536]{1,0:T(8,128)(2,1)S(1)}, bf16[24,1536]{1,0:T(8,128)(2,1)S(1)}, u32[]{:S(2)}, u32[]{:S(2)}) collective-permute-start(bf16[24,1536]{1,0:T(8,128)(2,1)S(1)} %get-tuple-element.144), channel_id=1, source_target_pairs={{0,24},{1,25},{2,26},{3,27},{4,28},{5,29},{6,30},{7,31},{8,16},{9,... | collective-permute-start | bytes 221192 | tf_op jit(solution)/shard_map/ppermute | solution.py:554
  87.0 8.4 %collective-permute-start.40 = (bf16[24,768]{1,0:T(8,128)(2,1)S(1)}, bf16[24,768]{1,0:T(8,128)(2,1)S(1)}, u32[]{:S(2)}, u32[]{:S(2)}) collective-permute-start(bf16[24,768]{1,0:T(8,128)(2,1)S(1)} %slice.167), channel_id=1, source_target_pairs={{0,16},{1,17},{2,18},{3,19},{4,20},{5,21},{6,22},{7,23},{8,24},{9,... | collective-permute-start | bytes 110600 | tf_op jit(solution)/shard_map/ppermute | solution.py:554
  88.6 6.1 %collective-permute-start.33 = (bf16[24,768]{1,0:T(8,128)(2,1)S(1)}, bf16[24,768]{1,0:T(8,128)(2,1)S(1)}, u32[]{:S(2)}, u32[]{:S(2)}) collective-permute-start(bf16[24,768]{1,0:T(8,128)(2,1)S(1)} %slice.155), channel_id=1, source_target_pairs={{0,16},{1,17},{2,18},{3,19},{4,20},{5,21},{6,22},{7,23},{8,24},{9,... | collective-permute-start | bytes 110600 | tf_op jit(solution)/shard_map/ppermute | solution.py:554
  (10 other events, 47.8 us)
